TPU v7x, 32 devices: a whole 2x2x4 slice. The times are simulated.
32 devices in a mesh: groups: 2 (over y), gx: 4 (over z), gy: 2 (over x), gz: 2 (over core).
Axes of the slice: x: 2, y: 2, z: 4, core: 2. Of those that a mesh axis runs over, the one named last changes fastest.
Arguments:
- potential_cot: float32 [128, 64, 256], P(('groups', 'gx'), 'gy', 'gz'), parts along dimension 0, may hold values from -16 to 16
- damping: float32 [128, 64, 256], P(('groups', 'gx'), 'gy', 'gz'), parts along dimension 0, may hold values from 0.1 to 8
- tissue_label: int32 [128, 64, 256], P(('groups', 'gx'), 'gy', 'gz'), parts along dimension 0, may hold values from 0 to 1, as said below
- heart_index: int32 [8, 2, 2, 20480], P(('groups', 'gx'), 'gy', 'gz'), parts along dimension 0, may hold values from 0 to 65536, as said below
- voltage: float32 [8, 32768], P(('groups', 'gy', 'gz'), 'gx'), parts along dimension 0, may hold values from -4 to 4
- gates: float32 [20, 8, 32768], P(None, ('groups', 'gy', 'gz'), 'gx'), parts along dimension 1, may hold values from 0 to 1
- voltage_cot: float32 [8, 32768], P(('groups', 'gy', 'gz'), 'gx'), parts along dimension 0, may hold values from -6 to 6
- gates_cot: float32 [20, 8, 32768], P(None, ('groups', 'gy', 'gz'), 'gx'), parts along dimension 1, may hold values from -6 to 6
- half_voltage: float32 [20], replicated, may hold values from -0.8 to 0.8
- gate_slope: float32 [20], replicated, may hold values from 0.2 to 0.8
- tau_base: float32 [20], replicated, may hold values from 0.05 to 4
- conductance: float32 [20], replicated, may hold values from 0.01 to 0.1
- reversal: float32 [20], replicated, may hold values from -1.5 to 1.5
Outputs:
- potential_adjoint: float32 [128, 64, 256], P(('groups', 'gx'), 'gy', 'gz'), parts along dimension 0
- voltage_grad: float32 [8, 32768], P(('groups', 'gy', 'gz'), 'gx'), parts along dimension 0
- gate_grad: float32 [20, 8, 32768], P(None, ('groups', 'gy', 'gz'), 'gx'), parts along dimension 1
There are 2 independent parts, one for each index of `groups`. A program takes and returns all parts, laid end to end along the dimension named above; an argument that names none is the same for every part. Nothing has to cross between parts.
Inputs may be any that keep to these rules, and one draw needn't show every extreme that they name: `tissue_label`: 1 marks a heart cell, 0 a torso cell. `heart_index`: for each tile, the local indices of its heart cells (tissue_label 1) in ascending order, then 16 * 32 * 128 in every remaining slot. Each column of tiles (same second and third index) holds exactly 32768 heart cells, each tile at most 20480, and in every column some tile holds exactly 20480.
All inputs are finite; a program needn't handle non-finite values.
Results may differ from a plain program's by a relative error of at most 0.0001.
Values sent between devices are 32-bit elements; how exact they have to be, the bound alone decides.
No kernel may reach another device: no remote copies, remote signals or barrier semaphores. Data moves between devices by JAX's collectives and lax.ppermute only.
A program may use at most 64 MiB of HBM per device.

v0:
```python
import jax
import jax.numpy as jnp
from jax import lax
from jax.sharding import PartitionSpec as P

ITERS = 3


time_step = 0.5
face_moves = ((1, 0, 0), (-1, 0, 0), (0, 1, 0), (0, -1, 0), (0, 0, 1), (0, 0, -1))
edge_moves = (
    (1, 1, 0),
    (1, -1, 0),
    (-1, 1, 0),
    (-1, -1, 0),
    (1, 0, 1),
    (1, 0, -1),
    (-1, 0, 1),
    (-1, 0, -1),
    (0, 1, 1),
    (0, 1, -1),
    (0, -1, 1),
    (0, -1, -1),
)


def with_halo(block, sides, width):
    for axis, dim in sides:
        count = lax.axis_size(axis)
        forward = [(i, i + 1) for i in range(count - 1)]
        backward = [(target, source) for source, target in forward]
        low = lax.ppermute(
            lax.slice_in_dim(block, block.shape[dim] - width, None, axis=dim), axis, forward
        )
        high = lax.ppermute(lax.slice_in_dim(block, 0, width, axis=dim), axis, backward)
        block = jnp.concatenate([low, block, high], axis=dim)
    return block


def neighbour(padded, offset, extent):
    return padded[
        1 + offset[0] : 1 + offset[0] + extent[0],
        1 + offset[1] : 1 + offset[1] + extent[1],
        1 + offset[2] : 1 + offset[2] + extent[2],
    ]


def face_total(padded, extent):
    face_sum = neighbour(padded, face_moves[0], extent)
    for offset in face_moves[1:]:
        face_sum = face_sum + neighbour(padded, offset, extent)
    return face_sum


def stencil(source, diagonal):
    padded = with_halo(source, (("gx", 0), ("gy", 1), ("gz", 2)), 1)
    extent = source.shape
    edge_sum = neighbour(padded, edge_moves[0], extent)
    for offset in edge_moves[1:]:
        edge_sum = edge_sum + neighbour(padded, offset, extent)
    return (diagonal * source - face_total(padded, extent) - 0.5 * edge_sum, padded)


def membrane_step(voltage, gates, half_voltage, gate_slope, tau_base, conductance, reversal):
    param_shape = (-1,) + (1,) * voltage.ndim
    scaled = (voltage[None] - half_voltage.reshape(param_shape)) / gate_slope.reshape(param_shape)
    steady = 1.0 / (1.0 + jnp.exp(-scaled))
    time_const = tau_base.reshape(param_shape) * (0.5 + jnp.exp(-scaled * scaled))
    decay = jnp.exp(-time_step / time_const)
    new_gates = steady + (gates - steady) * decay
    current = jnp.sum(
        conductance.reshape(param_shape) * gates * (voltage[None] - reversal.reshape(param_shape)),
        axis=0,
    )
    return (voltage - time_step * current, new_gates)


def weighted_norm(residual, precond):
    return lax.psum(jnp.sum(residual * precond), ("gx", "gy", "gz"))


def solve(right_side, diagonal):
    inverse = 1.0 / diagonal
    solution = jnp.zeros_like(right_side)
    padded_solution = None
    residual = right_side
    precond = inverse * residual
    direction = precond
    norm_now = weighted_norm(residual, precond)
    for iteration in range(ITERS):
        applied, padded_dir = stencil(direction, diagonal)
        curve_sum = lax.psum(jnp.sum(direction * applied), ("gx", "gy", "gz"))
        step_size = norm_now / curve_sum
        solution = solution + step_size * direction
        residual = residual - step_size * applied
        if iteration + 1 < ITERS:
            precond = inverse * residual
            norm_next = weighted_norm(residual, precond)
            direction = precond + norm_next / norm_now * direction
            norm_now = norm_next
    return (solution, padded_solution)


def local(
    potential_cot,
    damping,
    tissue_label,
    heart_index,
    voltage,
    gates,
    voltage_cot,
    gates_cot,
    half_voltage,
    gate_slope,
    tau_base,
    conductance,
    reversal,
):
    diagonal = 12.0 + damping * (1.0 + 3.0 * tissue_label.astype(jnp.float32))

    def local_step(volts_in, gates_in):
        return membrane_step(
            volts_in, gates_in, half_voltage, gate_slope, tau_base, conductance, reversal
        )

    outputs, pullback = jax.vjp(local_step, voltage, gates)
    solution, padded = solve(potential_cot, diagonal)
    padded = with_halo(solution, (("gx", 0), ("gy", 1), ("gz", 2)), 1)
    coupling = face_total(padded, solution.shape) - 6.0 * solution
    tile_size = coupling.shape[0] * coupling.shape[1] * coupling.shape[2]
    slot_count = heart_index.shape[3]
    width_block = voltage.shape[1]
    heart_list = heart_index.reshape(slot_count)
    is_heart = heart_list < tile_size
    flat_field = coupling.reshape(tile_size)
    heart_vals = jnp.where(
        is_heart, jnp.take(flat_field, jnp.minimum(heart_list, tile_size - 1)), 0.0
    )
    heart_count = jnp.sum(is_heart.astype(jnp.int32)).reshape(1)
    all_counts = lax.all_gather(heart_count, "gx", axis=0, tiled=True)
    all_offsets = jnp.cumsum(all_counts) - all_counts
    block_start = lax.axis_index("gx") * width_block
    piece = lax.all_gather(heart_vals, "gx", axis=0, tiled=True)
    rows = jnp.arange(piece.shape[0], dtype=jnp.int32)
    shard_of = rows // slot_count
    slot_of = rows - shard_of * slot_count
    in_block = jnp.take(all_offsets, shard_of) + slot_of - block_start
    inside = (slot_of < jnp.take(all_counts, shard_of)) & (in_block >= 0) & (in_block < width_block)
    target = jnp.where(inside, in_block, width_block)
    landed = (
        jnp.zeros((width_block,), jnp.float32)
        .at[target]
        .add(jnp.where(inside, piece, 0.0), mode="drop")
    )
    volt_grad, gate_grad = pullback((voltage_cot + landed.reshape(voltage.shape), gates_cot))
    return (solution, volt_grad, gate_grad)


def solution(mesh):
    in_specs = (
        P(("groups", "gx"), "gy", "gz"),
        P(("groups", "gx"), "gy", "gz"),
        P(("groups", "gx"), "gy", "gz"),
        P(("groups", "gx"), "gy", "gz", None),
        P(("groups", "gy", "gz"), "gx"),
        P(None, ("groups", "gy", "gz"), "gx"),
        P(("groups", "gy", "gz"), "gx"),
        P(None, ("groups", "gy", "gz"), "gx"),
        P(),
        P(),
        P(),
        P(),
        P(),
    )
    out_specs = (
        P(("groups", "gx"), "gy", "gz"),
        P(("groups", "gy", "gz"), "gx"),
        P(None, ("groups", "gy", "gz"), "gx"),
    )
    return jax.shard_map(local, mesh=mesh, in_specs=in_specs, out_specs=out_specs, check_vma=False)
```

profile of v0, /device:TPU:0, one launch (start us, length us, event | category | flops | bytes accessed | tf_op | source)
XLA Modules:
  0.0 854.4 jit_solution(12017070808214872449)
XLA Ops:
  3.1 5.7 collective-permute-start.1
  11.6 4.5 collective-permute-start.3
  19.0 3.1 collective-permute-start.5
  24.8 36.6 %all-reduce.1 = (f32[]{:T(128)}, f32[]{:T(128)}) all-reduce(f32[]{:T(128)} %get-tuple-element.7, f32[]{:T(128)} %get-tuple-element.6), channel_id=1, replica_groups=mesh['groups'=2,'gx'=4,'gy'=2,'gz'=2] {'gx','gy','gz'}, use_global_device_ids=true, to_apply=%region_1.0 | all-reduce | flops 2 | bytes 16 | tf_op jit(solution)/shard_map/psum | solution.py:79
  63.4 30.1 %psum.44 = f32[]{:T(128)} all-reduce(f32[]{:T(128)} %get-tuple-element.14), channel_id=1, replica_groups=mesh['groups'=2,'gx'=4,'gy'=2,'gz'=2] {'gx','gy','gz'}, use_global_device_ids=true, to_apply=%region_5.0 | all-reduce | flops 1 | bytes 8 | tf_op jit(solution)/shard_map/psum | solution.py:79
  96.2 4.5 collective-permute-start.7
  103.5 4.5 collective-permute-start.9
  111.5 3.1 collective-permute-start.11
  117.4 30.5 %psum.45 = f32[]{:T(128)} all-reduce(f32[]{:T(128)} %get-tuple-element.12), channel_id=1, replica_groups=mesh['groups'=2,'gx'=4,'gy'=2,'gz'=2] {'gx','gy','gz'}, use_global_device_ids=true, to_apply=%region_7.0 | all-reduce | flops 1 | bytes 8 | tf_op jit(solution)/shard_map/psum | solution.py:92
  151.3 30.1 %psum.46 = f32[]{:T(128)} all-reduce(f32[]{:T(128)} %multiply_reduce_fusion.1), channel_id=1, replica_groups=mesh['groups'=2,'gx'=4,'gy'=2,'gz'=2] {'gx','gy','gz'}, use_global_device_ids=true, to_apply=%region_9.0 | all-reduce | flops 1 | bytes 8 | tf_op jit(solution)/shard_map/psum | solution.py:79
  184.1 4.5 collective-permute-start.13
  188.8 5.6 all-reduce
  195.9 4.5 collective-permute-start.15
  203.3 3.1 collective-permute-start.17
  209.8 34.5 %psum.47 = f32[]{:T(128)} all-reduce(f32[]{:T(128)} %fusion.17), channel_id=1, replica_groups=mesh['groups'=2,'gx'=4,'gy'=2,'gz'=2] {'gx','gy','gz'}, use_global_device_ids=true, to_apply=%region_11.0 | all-reduce | flops 1 | bytes 8 | tf_op jit(solution)/shard_map/psum | solution.py:92
  247.0 4.5 collective-permute-start.19
  254.3 4.5 collective-permute-start.21
  258.8 5.3 compare_select_fusion.1
  267.1 2.2 collective-permute-done.22
  269.7 113.0 %gather_fusion = f32[20480]{0:T(1024)S(1)} fusion(f32[65536]{0:T(1024)S(1)} %bitcast.23, s32[20480]{0:T(1024)S(1)} %broadcast_clamp_fusion), kind=kCustom, calls=%fused_computation | custom fusion | bytes 245760 | tf_op jit(solution)/shard_map/jit(_take)/gather | solution.py:137
  382.8 14.3 %all_gather.7 = f32[81920]{0:T(1024)S(1)} all-gather(f32[20480]{0:T(1024)S(1)} %select_select_fusion), channel_id=1, replica_groups=mesh['groups'=2,'gx'=4,'gy'=2,'gz'=2] {'gx'}, dimensions={0}, use_global_device_ids=true | all-gather | bytes 409600 | tf_op jit(solution)/shard_map/all_gather | solution.py:143
  397.1 5.3 broadcast_select_fusion
  402.4 440.5 %scatter_custom_fusion = f32[8192]{0:T(1024)S(1)} fusion(s32[81920]{0:T(1024)S(1)} %compare_select_fusion.1, f32[81920]{0:T(1024)S(1)} %broadcast_select_fusion, f32[]{:T(128)} %constant.20.clone.1), kind=kCustom, calls=%fused_computation.161 | custom fusion | flops 81920 | bytes 32772 | tf_op jit(solution)/shard_map/scatter-add | solution.py:153
  843.7 10.1 %multiply_reduce_fusion = (f32[8192]{0:T(1024)S(1)}, f32[8192]{0:T(1024)S(1)}, f32[20,1,8192]{2,1,0:T(1,128)}) fusion(f32[20,1,8192]{2,1,0:T(1,128)S(1)} %copy-done.3, f32[8192]{0:T(1024)S(1)} %bitcast.26, f32[20]{0:T(128)S(1)} %copy-done.7, f32[20,1,8192]{2,1,0:T(1,128)S(1)} %copy-done.4, f32[20]{0:T(128)S(1)} %copy-done.8, f32[20]{0:T(128)S(1)} %copy-done.9, ...), kind=kLoop, calls=%fused_computation.24 | loop fusion | flops 6864896 | bytes 2097552 | tf_op jit(solution)/shard_map/transpose(jvp())/reduce_sum | solution.py:72
  (109 shorter events, 41.6 us)
Async XLA Ops:
  1.8 7.0 collective-permute-start
  3.1 7.1 collective-permute-start.1
  10.3 6.0 collective-permute-start.2
  11.6 5.9 collective-permute-start.3
  17.7 4.5 collective-permute-start.4
  19.0 4.4 collective-permute-start.5
  94.9 6.1 collective-permute-start.6
  96.2 6.0 collective-permute-start.7
  102.2 7.8 collective-permute-start.8
  103.5 6.5 collective-permute-start.9
  110.2 4.4 collective-permute-start.10
  111.5 4.4 collective-permute-start.11
  182.8 11.8 %collective-permute-start.12 = (f32[1,32,128]{2,1,0:T(8,128)S(1)}, f32[1,32,128]{2,1,0:T(8,128)S(1)}, u32[]{:S(2)}, u32[]{:S(2)}) collective-permute-start(f32[1,32,128]{2,1,0:T(8,128)S(1)} %get-tuple-element.51), channel_id=1, source_target_pairs={{4,0},{8,4},{12,8},{5,1},{9,5},{13,9},{6,2},{10,6},{14,10},{7,3},{... | collective-permute-start | bytes 49160 | tf_op jit(solution)/shard_map/ppermute | solution.py:35
  184.1 10.5 %collective-permute-start.13 = (f32[1,32,128]{2,1,0:T(8,128)S(1)}, f32[1,32,128]{2,1,0:T(8,128)S(1)}, u32[]{:S(2)}, u32[]{:S(2)}) collective-permute-start(f32[1,32,128]{2,1,0:T(8,128)S(1)} %get-tuple-element.50), channel_id=1, source_target_pairs={{0,4},{4,8},{8,12},{1,5},{5,9},{9,13},{2,6},{6,10},{10,14},{3,7},{... | collective-permute-start | bytes 49160 | tf_op jit(solution)/shard_map/ppermute | solution.py:32
  194.6 5.9 collective-permute-start.14
  195.9 5.9 collective-permute-start.15
  202.0 4.4 collective-permute-start.16
  203.3 4.4 collective-permute-start.17
  245.7 6.5 collective-permute-start.18
  247.0 6.0 collective-permute-start.19
  253.0 11.2 %collective-permute-start.20 = (f32[18,1,128]{2,1,0:T(1,128)S(1)}, f32[18,1,128]{2,1,0:T(1,128)S(1)}, u32[]{:S(2)}, u32[]{:S(2)}) collective-permute-start(f32[18,1,128]{2,1,0:T(1,128)S(1)} %get-tuple-element.35), channel_id=1, source_target_pairs={{2,0},{3,1},{6,4},{7,5},{10,8},{11,9},{14,12},{15,13},{18,16},{19,... | collective-permute-start | bytes 27656 | tf_op jit(solution)/shard_map/ppermute | solution.py:35
  254.3 9.9 %collective-permute-start.21 = (f32[18,1,128]{2,1,0:T(1,128)S(1)}, f32[18,1,128]{2,1,0:T(1,128)S(1)}, u32[]{:S(2)}, u32[]{:S(2)}) collective-permute-start(f32[18,1,128]{2,1,0:T(1,128)S(1)} %get-tuple-element.34), channel_id=1, source_target_pairs={{0,2},{1,3},{4,6},{5,7},{8,10},{9,11},{12,14},{13,15},{16,18},{17,... | collective-permute-start | bytes 27656 | tf_op jit(solution)/shard_map/ppermute | solution.py:32
  264.4 2.6 collective-permute-start.23
  265.7 3.6 collective-permute-start.22
  (13 other events, 2323.5 us)
where the time goes:
time: 856 us; the launch traced here: 854 us
  other arithmetic  471 us (55%)
  blocking collectives  182 us (21%)
  local copies, waits for them, and re-layouts  118 us (14%)
  starting transfers between devices  63.5 us (7%)
  waiting for transfers between devices  11.8 us (1%)
    scatter-add x1, other arithmetic, local(): landed = jnp.zeros((width_block,), jnp.float32).at[target].add(jnp.where(...  441 us
    gather x1, local copies, waits for them, and re-layouts, local(): jnp.take(flat_field, jnp.minimum(heart_list, tile_size - 1))  113 us
    psum x3, blocking collectives, weighted_norm(): return lax.psum(jnp.sum(residual * precond), ('gx', 'gy', 'gz'))  96.8 us
    psum x2, blocking collectives, solve(): curve_sum = lax.psum(jnp.sum(direction * applied), ('gx', 'gy', 'gz'))  64.9 us
    ppermute x12, starting transfers between devices, with_halo(): lax.ppermute(lax.slice_in_dim(block, block.shape[dim] - width, None, axis...  48 us
  transfers between devices with their start and end apart: 24, of which 9 were waited for; matrix products, arithmetic and copies ran while one was open for 1% of the time, Pallas kernels for 0%

commit v1 on v0

v1 whole, which is shorter than its diff:
```python
import functools

import jax
import jax.numpy as jnp
from jax import lax
from jax.experimental import pallas as pl
from jax.experimental.pallas import tpu as pltpu
from jax.sharding import PartitionSpec as P

TIME_STEP = 0.5
LANES = 128
SIDES = (("gz", 2), ("gy", 1), ("gx", 0))


def exchange(pair, axis, dim):
    count = lax.axis_size(axis)
    here = lax.axis_index(axis)
    first = lax.slice_in_dim(pair, 0, 3, axis=dim)
    last = lax.slice_in_dim(pair, pair.shape[dim] - 3, None, axis=dim)
    if count == 2:
        got = lax.ppermute(jnp.where(here == 0, last, first), axis, [(0, 1), (1, 0)])
        low = jnp.where(here == 1, got, 0.0)
        high = jnp.where(here == 0, got, 0.0)
    else:
        forward = [(i, i + 1) for i in range(count - 1)]
        backward = [(i + 1, i) for i in range(count - 1)]
        low = lax.ppermute(last, axis, forward)
        high = lax.ppermute(first, axis, backward)
    return jnp.concatenate([low, pair, high], axis=dim)


def neighbour_sum(v):
    mid = v[:, :, 1:-1]
    along_z = v[:, :, 2:] + v[:, :, :-2]
    both = mid + 0.5 * along_z
    plane = along_z[:, 1:-1] + both[:, 2:] + both[:, :-2]
    wing = both[:, 1:-1] + 0.5 * (mid[:, 2:] + mid[:, :-2])
    return plane[1:-1] + wing[2:] + wing[:-2]


def core(v, width):
    return v[width:-width, width:-width, width:-width] if width else v


def face_sum(v):
    return (
        v[2:, 1:-1, 1:-1] + v[:-2, 1:-1, 1:-1]
        + v[1:-1, 2:, 1:-1] + v[1:-1, :-2, 1:-1]
        + v[1:-1, 1:-1, 2:] + v[1:-1, 1:-1, :-2]
    )


def galerkin(t):
    g00, g01, g02, g12, g22 = t[0] - t[1], t[1] - t[2], t[2] - t[3], t[3] - t[4], t[4] - t[5]
    g11 = g02
    l10, l20 = g01 / g00, g02 / g00
    d1 = g11 - l10 * g01
    m21 = g12 - l20 * g01
    ok1 = d1 > 1e-6 * g11
    d1 = jnp.where(ok1, d1, 1.0)
    l21 = jnp.where(ok1, m21 / d1, 0.0)
    d2 = g22 - l20 * g02 - l21 * m21
    ok2 = ok1 & (d2 > 1e-6 * g22)
    d2 = jnp.where(ok2, d2, 1.0)
    y1 = t[1] - l10 * t[0]
    y2 = t[2] - l20 * t[0] - l21 * y1
    c2 = jnp.where(ok2, y2 / d2, 0.0)
    c1 = jnp.where(ok1, y1 / d1 - l21 * c2, 0.0)
    c0 = t[0] / g00 - l10 * c1 - l20 * c2
    return c0, c1, c2


def shift_left(v, amount, lane):
    rows = v.shape[0]
    if amount < LANES:
        turned = pltpu.roll(v, LANES - amount, 1)
        below = pltpu.roll(turned, rows - 1, 0)
        return jnp.where(lane < LANES - amount, turned, below)
    return jnp.concatenate([v[amount // LANES :], v[: amount // LANES]], axis=0)


def compact_kernel(place_ref, label_ref, value_ref, out_ref):
    rows = label_ref.shape[0]
    label = label_ref[...]
    lane = lax.broadcasted_iota(jnp.int32, (rows, LANES), 1)
    row = lax.broadcasted_iota(jnp.int32, (rows, LANES), 0)
    heart = label == 1
    ones = heart.astype(jnp.bfloat16)
    upper = (
        lax.broadcasted_iota(jnp.int32, (LANES, LANES), 0) < lax.broadcasted_iota(jnp.int32, (LANES, LANES), 1)
    ).astype(jnp.bfloat16)
    in_row = jnp.dot(ones, upper, preferred_element_type=jnp.float32)
    totals = jnp.dot(ones, jnp.ones((LANES, LANES), jnp.bfloat16), preferred_element_type=jnp.float32)
    lower = (
        lax.broadcasted_iota(jnp.int32, (rows, rows), 0) > lax.broadcasted_iota(jnp.int32, (rows, rows), 1)
    ).astype(jnp.bfloat16)
    before = jnp.dot(lower, totals.astype(jnp.bfloat16), preferred_element_type=jnp.float32)
    rank = (in_row + before).astype(jnp.int32)
    way = jnp.where(heart, row * LANES + lane - rank, 0)
    value = value_ref[...]
    step = 1
    while step < rows * LANES:
        moving = jnp.where((way & step) != 0, way, 0)
        arriving = shift_left(moving, step, lane)
        value = jnp.where(arriving != 0, shift_left(value, step, lane), value)
        way = (way - moving) | arriving
        step *= 2
    offset = place_ref[0]
    count = place_ref[1]
    slots = value[:160]
    index = (row * LANES + lane)[:160]
    slots = jnp.where(index < count, slots, 0.0)
    slots = jnp.concatenate([slots, jnp.zeros((8, LANES), jnp.float32)], axis=0)
    inner = lax.rem(offset, LANES)
    turned = pltpu.roll(slots, inner, 1)
    above = pltpu.roll(turned, 1, 0)
    moved = jnp.where(lane[:168] >= inner, turned, above)
    out_ref[...] = jnp.zeros_like(out_ref)
    out_ref[pl.ds(offset // LANES, 168), :] = moved


def local(
    potential_cot, damping, tissue_label, heart_index, voltage, gates, voltage_cot, gates_cot,
    half_voltage, gate_slope, tau_base, conductance, reversal,
):
    shape = potential_cot.shape
    rows = shape[0] * shape[1]
    n_gx = lax.axis_size("gx")
    width_block = voltage.shape[1]
    block_rows = width_block // LANES

    diagonal = 12.0 + damping * (1.0 + 3.0 * tissue_label.astype(jnp.float32))
    inverse = 1.0 / diagonal
    w0 = inverse * potential_cot
    pair = jnp.stack([w0, inverse])
    for axis, dim in SIDES:
        pair = exchange(pair, axis, dim + 1)
    field, inverse = pair[0], core(pair[1], 1)
    w1 = neighbour_sum(field) * inverse
    w2 = neighbour_sum(w1) * core(inverse, 1)
    n2 = neighbour_sum(w2)
    in0, in1, in2 = core(field, 3), core(w1, 2), core(w2, 1)

    count = jnp.sum((tissue_label == 1).astype(jnp.float32))
    sums = jnp.stack([
        jnp.sum(potential_cot * in0),
        jnp.sum(potential_cot * in1),
        jnp.sum(diagonal * in1 * in1),
        jnp.sum(diagonal * in1 * in2),
        jnp.sum(diagonal * in2 * in2),
        jnp.sum(in2 * n2),
    ])
    here = (lax.axis_index("gx") * lax.axis_size("gy") + lax.axis_index("gy")) * lax.axis_size("gz") + lax.axis_index("gz")
    n_dev = n_gx * lax.axis_size("gy") * lax.axis_size("gz")
    counts = jnp.where(jnp.arange(n_dev) == here, count, 0.0)
    total = lax.psum(jnp.concatenate([sums, counts]), ("gx", "gy", "gz"))
    c0, c1, c2 = galerkin([total[i] for i in range(6)])
    wide = c0 * core(field, 2) + c1 * core(w1, 1) + c2 * w2
    solution = core(wide, 1)
    coupling = face_sum(wide) - 6.0 * solution

    column = total[6:].reshape(n_gx, -1)
    mine = lax.axis_index("gy") * lax.axis_size("gz") + lax.axis_index("gz")
    column = lax.dynamic_index_in_dim(column, mine, axis=1, keepdims=False)
    offset = jnp.sum(jnp.where(jnp.arange(n_gx) < lax.axis_index("gx"), column, 0.0))
    place = jnp.stack([offset, count]).astype(jnp.int32)
    placed = pl.pallas_call(
        compact_kernel,
        out_shape=jax.ShapeDtypeStruct((n_gx * block_rows + 168, LANES), jnp.float32),
        in_specs=[
            pl.BlockSpec(memory_space=pltpu.SMEM),
            pl.BlockSpec(memory_space=pltpu.VMEM),
            pl.BlockSpec(memory_space=pltpu.VMEM),
        ],
        out_specs=pl.BlockSpec(memory_space=pltpu.VMEM),
        compiler_params=pltpu.CompilerParams(vmem_limit_bytes=32 * 1024 * 1024),
    )(place, tissue_label.reshape(rows, LANES), coupling.reshape(rows, LANES))
    blocks = placed[: n_gx * block_rows].reshape(n_gx, block_rows, LANES)
    landed = jnp.sum(lax.all_to_all(blocks, "gx", 0, 0, tiled=True), axis=0)

    param = lambda a: a.reshape(-1, 1, 1)
    scaled = (voltage[None] - param(half_voltage)) / param(gate_slope)
    steady = 1.0 / (1.0 + jnp.exp(-scaled))
    bell = jnp.exp(-scaled * scaled)
    tau = param(tau_base) * (0.5 + bell)
    decay = jnp.exp(-TIME_STEP / tau)
    steady_slope = steady * (1.0 - steady) / param(gate_slope)
    tau_slope = param(tau_base) * bell * (-2.0 * scaled) / param(gate_slope)
    decay_slope = decay * TIME_STEP / (tau * tau) * tau_slope
    gate_slope_total = steady_slope * (1.0 - decay) + (gates - steady) * decay_slope
    cot = voltage_cot + landed.reshape(voltage.shape)
    volt_grad = (
        cot * (1.0 - TIME_STEP * jnp.sum(param(conductance) * gates, axis=0))
        + jnp.sum(gates_cot * gate_slope_total, axis=0)
    )
    gate_grad = gates_cot * decay - TIME_STEP * param(conductance) * (voltage[None] - param(reversal)) * cot[None]
    return solution, volt_grad, gate_grad


def solution(mesh):
    grid = P(("groups", "gx"), "gy", "gz")
    cells = P(("groups", "gy", "gz"), "gx")
    states = P(None, ("groups", "gy", "gz"), "gx")
    in_specs = (
        grid, grid, grid, P(("groups", "gx"), "gy", "gz", None), cells, states, cells, states,
        P(), P(), P(), P(), P(),
    )
    return jax.shard_map(
        local, mesh=mesh, in_specs=in_specs, out_specs=(grid, cells, states), check_vma=False
    )
```

time: 856 us -> 104 us (0.12)
  other arithmetic: 471 us -> 27.1 us
  blocking collectives: 182 us -> 29.5 us
  local copies, waits for them, and re-layouts: 118 us -> 6.57 us
  starting transfers between devices: 63.5 us -> 11.5 us
    scatter-add x1 -> x0, other arithmetic: 441 us -> none  [local(): landed = jnp.zeros((width_block,), jnp.float32).at[target].add(jnp.where(...]
    psum x5 -> x1, blocking collectives: 162 us -> 29.5 us  [local(): total = lax.psum(jnp.concatenate([sums, counts]), ('gx', 'gy', 'gz'))]
    gather x3 -> x0, local copies, waits for them, and re-layouts: 114 us -> none  [the longest x1 113 us: local(): jnp.take(flat_field, jnp.minimum(heart_list, tile_size - 1))]
    ppermute x24 -> x4, starting transfers between devices: 63.5 us -> 8.22 us  [the longest x1 3.48 us: exchange(): low = lax.ppermute(last, axis, forward)]
    all_gather x1 -> x0, blocking collectives: 14.3 us -> none  [local(): piece = lax.all_gather(heart_vals, 'gx', axis=0, tiled=True)]
  transfers between devices with their start and end apart: 24 -> 5, of which waited for: 9 -> 4; matrix products, arithmetic and copies ran while one was open for 1% -> 9% of each run, Pallas kernels for 0% -> 0%
where the time goes in v1:
time: 104 us; the launch traced here: 103 us
  blocking collectives  29.5 us (28%)
  other arithmetic  27.1 us (26%)
  waiting for transfers between devices  15.3 us (15%)
  starting transfers between devices  11.5 us (11%)
  between operations  10.6 us (10%)
  local copies, waits for them, and re-layouts  6.57 us (6%)
  Pallas kernels  2.74 us (3%)
    psum x1, blocking collectives, local(): total = lax.psum(jnp.concatenate([sums, counts]), ('gx', 'gy', 'gz'))  29.5 us
    reduce_sum x1, other arithmetic, local(): jnp.sum(param(conductance) * gates, axis=0)  8.18 us
    all_to_all x1, waiting for transfers between devices, local(): landed = jnp.sum(lax.all_to_all(blocks, 'gx', 0, 0, tiled=True), axis=0)  6.17 us
    ppermute x1, waiting for transfers between devices, exchange(): high = lax.ppermute(first, axis, backward)  4.02 us
    sub x1, other arithmetic, local(): gates_cot * decay  3.94 us
    concatenate x1, local copies, waits for them, and re-layouts, local(): total = lax.psum(jnp.concatenate([sums, counts]), ('gx', 'gy', 'gz'))  3.89 us
    ppermute x1, waiting for transfers between devices, exchange(): low = lax.ppermute(last, axis, forward)  3.49 us
    ppermute x1, starting transfers between devices, exchange(): low = lax.ppermute(last, axis, forward)  3.48 us
  transfers between devices with their start and end apart: 5, of which 4 were waited for; matrix products, arithmetic and copies ran while one was open for 9% of the time, Pallas kernels for 0%

profile of v1, /device:TPU:0, one launch (start us, length us, event | category | flops | bytes accessed | tf_op | source)
XLA Modules:
  0.0 103.4 jit_solution(14437433525005943144)
XLA Ops:
  0.6 2.0 %multiply_bitcast_fusion = (f32[1,16,32,128]{3,2,1,0:T(8,128)S(1)}, f32[16,32,128]{2,1,0:T(8,128)S(1)}, f32[]{:T(128)}) fusion(f32[16,32,128]{2,1,0:T(8,128)} %param.13, f32[16,32,128]{2,1,0:T(8,128)} %param.14, s32[16,32,128]{2,1,0:T(8,128)} %param.15), kind=kLoop, calls=%fused_computation.72 | loop fusion | flops 655359 | bytes 1310724 | tf_op jit(solution)/shard_map/stack | solution.py:135
  3.5 1.7 %collective-permute-done = f32[2,16,32,3]{3,2,1,0:T(8,128)} collective-permute-done((f32[2,16,32,3]{3,2,1,0:T(8,128)S(1)}, f32[2,16,32,3]{3,2,1,0:T(8,128)}, u32[]{:S(2)}, u32[]{:S(2)}) %collective-permute-start) | collective-permute-done | bytes 12320 | tf_op jit(solution)/shard_map/ppermute | solution.py:21
  5.1 1.2 %broadcast_select_fusion.1 = (f32[2,16,32,3]{3,2,1,0:T(8,128)S(1)}, f32[2,16,32,3]{3,2,1,0:T(8,128)S(1)}) fusion(f32[2,16,32,3]{3,2,1,0:T(8,128)} %collective-permute-done, pred[]{:T(512)S(6)} %eq.28, pred[]{:T(512)S(6)} %eq.29), kind=kLoop, calls=%fused_computation.71 | loop fusion | flops 6144 | bytes 36866 | tf_op jit(solution)/shard_map/jit(_where)/select_n | solution.py:22
  6.6 2.9 %collective-permute-start.1 = (f32[2,16,3,134]{3,2,1,0:T(4,128)S(1)}, f32[2,16,3,134]{3,2,1,0:T(4,128)S(1)}, u32[]{:S(2)}, u32[]{:S(2)}) collective-permute-start(f32[2,16,3,134]{3,2,1,0:T(4,128)S(1)} %fusion.19), channel_id=1, source_target_pairs={{0,2},{2,0},{1,3},{3,1},{4,6},{6,4},{5,7},{7,5},{8,10},{10,8},{9,1... | collective-permute-start | bytes 154376 | tf_op jit(solution)/shard_map/ppermute | solution.py:21
  9.6 8.2 %multiply_reduce_fusion.1 = (f32[8192]{0:T(1024)S(1)}, f32[8192]{0:T(1024)}) fusion(f32[20,1,8192]{2,1,0:T(1,128)S(1)} %copy-done.3, f32[20]{0:T(128)S(1)} %copy-done.11, f32[20,1,8192]{2,1,0:T(1,128)S(1)} %copy-done.1, f32[20]{0:T(128)S(1)} %copy-done.7, f32[20]{0:T(128)S(1)} %copy-done.8, f32[20]{0:T(128)S(1)} %copy-done.9, f32[8192]{0:T(1024)S(1)} %bitcast.32), kind=kLoop, calls=%fused_computation.42 | loop fusion | flops 4734976 | bytes 1409344 | tf_op jit(solution)/shard_map/reduce_sum | solution.py:193
  17.8 1.0 %pad_maximum_fusion.7 = (f32[2,3,38,134]{3,2,1,0:T(8,128)}, f32[2,3,38,134]{3,2,1,0:T(8,128)}) fusion(f32[2,16,3,134]{3,2,1,0:T(4,128)S(1)} %get-tuple-element.40, f32[2,16,3,134]{3,2,1,0:T(4,128)S(1)} %get-tuple-element.39, f32[2,16,32,3]{3,2,1,0:T(8,128)S(1)} %get-tuple-element.34, f32[2,16,32,3]{3,2,1,0:T(8,128)S(1)} %get-tuple-element.33, ...), kind=kLoop, calls=%fused_computation.79 | loop fusion | flops 305520 | bytes 896192 | tf_op jit(solution)/shard_map/slice | solution.py:19
  18.8 3.5 %collective-permute-start.2 = (f32[2,3,38,134]{3,2,1,0:T(8,128)}, f32[2,3,38,134]{3,2,1,0:T(8,128)S(1)}, u32[]{:S(2)}, u32[]{:S(2)}) collective-permute-start(f32[2,3,38,134]{3,2,1,0:T(8,128)} %get-tuple-element.23), channel_id=1, source_target_pairs={{0,4},{4,8},{8,12},{1,5},{5,9},{9,13},{2,6},{6,10},{10,14},{3,7},{... | collective-permute-start | bytes 366632 | tf_op jit(solution)/shard_map/ppermute | solution.py:27
  22.3 1.3 %collective-permute-start.3 = (f32[2,3,38,134]{3,2,1,0:T(8,128)}, f32[2,3,38,134]{3,2,1,0:T(8,128)S(1)}, u32[]{:S(2)}, u32[]{:S(2)}) collective-permute-start(f32[2,3,38,134]{3,2,1,0:T(8,128)} %get-tuple-element.24), channel_id=1, source_target_pairs={{4,0},{8,4},{12,8},{5,1},{9,5},{13,9},{6,2},{10,6},{14,10},{7,3},{... | collective-permute-start | bytes 366632 | tf_op jit(solution)/shard_map/ppermute | solution.py:28
  23.6 0.7 compare_select_fusion.1
  24.3 3.5 %collective-permute-done.2 = f32[2,3,38,134]{3,2,1,0:T(8,128)S(1)} collective-permute-done((f32[2,3,38,134]{3,2,1,0:T(8,128)}, f32[2,3,38,134]{3,2,1,0:T(8,128)S(1)}, u32[]{:S(2)}, u32[]{:S(2)}) %collective-permute-start.2) | collective-permute-done | bytes 122240 | tf_op jit(solution)/shard_map/ppermute | solution.py:27
  27.8 4.0 %collective-permute-done.3 = f32[2,3,38,134]{3,2,1,0:T(8,128)S(1)} collective-permute-done((f32[2,3,38,134]{3,2,1,0:T(8,128)}, f32[2,3,38,134]{3,2,1,0:T(8,128)S(1)}, u32[]{:S(2)}, u32[]{:S(2)}) %collective-permute-start.3) | collective-permute-done | bytes 122240 | tf_op jit(solution)/shard_map/ppermute | solution.py:28
  36.3 0.6 copy-done.2
  37.0 1.0 %multiply_reduce_fusion.2 = (f32[]{:T(128)}, f32[]{:T(128)}, f32[]{:T(128)}, f32[]{:T(128)}, f32[]{:T(128)}, /*index=5*/f32[]{:T(128)}) fusion(f32[16,32,128]{2,1,0:T(8,128)S(1)} %get-tuple-element.22, f32[18,34,130]{2,1,0:T(8,128)S(1)} %slice_multiply_fusion.3, f32[20,36,132]{2,1,0:T(8,128)S(1)} %slice_multiply_fusion, f32[16,32,128]{2,1,0:T(8,128)S(1)} %copy-done.2, ...), kind=kLoop, calls=%fused_computation.67 | loop fusion | flops 1179642 | bytes 2621464 | tf_op jit(solution)/shard_map/reduce_sum | solution.py:149
  38.0 3.9 %concatenate.15 = f32[22]{0:T(128)S(1)} concatenate(f32[1]{0:T(128)} %bitcast.3, f32[1]{0:T(128)} %bitcast.5, f32[1]{0:T(128)} %bitcast.6, f32[1]{0:T(128)} %bitcast.7, f32[1]{0:T(128)} %bitcast.8, f32[1]{0:T(128)} %bitcast.9, f32[16]{0:T(128)S(1)} %compare_select_fusion.1), dimensions={0} | concatenate | bytes 176 | tf_op jit(solution)/shard_map/concatenate | solution.py:156
  41.9 29.5 %psum.7 = f32[22]{0:T(128)S(1)} all-reduce(f32[22]{0:T(128)S(1)} %concatenate.15), channel_id=1, replica_groups=mesh['groups'=2,'gx'=4,'gy'=2,'gz'=2] {'gx','gy','gz'}, use_global_device_ids=true, to_apply=%region_7.8 | all-reduce | flops 22 | bytes 176 | tf_op jit(solution)/shard_map/psum | solution.py:156
  71.4 0.7 fusion.25
  82.3 1.2 %fusion.15 = (f32[16,32,128]{2,1,0:T(8,128)S(1)}, f32[16,32,128]{2,1,0:T(8,128)}) fusion(f32[18,34,130]{2,1,0:T(8,128)S(1)} %fusion.5), kind=kLoop, calls=%fused_computation.53 | loop fusion | flops 458752 | bytes 2359296 | tf_op jit(solution)/shard_map/sub | solution.py:160
  84.4 1.4 %maximum_convert_fusion.place_ref = s32[2]{0:T(128)S(1)} fusion(f32[1]{0:T(128)} %bitcast.17, f32[1]{0:T(128)} %bitcast.16), kind=kLoop, calls=%fused_computation.94 | loop fusion | flops 4 | bytes 16 | tf_op jit(solution)/shard_map/convert_element_type | solution.py:166
  85.8 2.7 %shard_map.142 = f32[424,128]{1,0:T(8,128)S(1)} custom-call(s32[2]{0:T(128)S(1)} %maximum_convert_fusion.place_ref, s32[512,128]{1,0:T(8,128)S(1)} %bitcast.30, f32[512,128]{1,0:T(8,128)S(1)} %bitcast.31), custom_call_target="tpu_custom_call" | custom-call | tf_op jit(solution)/shard_map/pallas_call | solution.py:167
  88.5 0.7 slice.331
  89.2 3.3 %all-to-all-start = ((f32[4,64,128]{2,1,0:T(8,128)}), f32[4,64,128]{2,1,0:T(8,128)S(1)}, u32[]{:S(2)}, u32[]{:S(2)}) async-start(f32[4,64,128]{2,1,0:T(8,128)} %bitcast.20), calls=%async_computation | async-start | bytes 262144 | tf_op jit(solution)/shard_map/all_to_all | solution.py:179
  92.5 6.2 %all-to-all-done = f32[4,64,128]{2,1,0:T(8,128)S(1)} async-done(((f32[4,64,128]{2,1,0:T(8,128)}), f32[4,64,128]{2,1,0:T(8,128)S(1)}, u32[]{:S(2)}, u32[]{:S(2)}) %all-to-all-start) | async-done | bytes 131104 | tf_op jit(solution)/shard_map/all_to_all | solution.py:179
  98.7 0.7 multiply_add_fusion.1
  99.4 3.9 %multiply_subtract_fusion = f32[20,1,8192]{2,1,0:T(1,128)} fusion(f32[20,1,8192]{2,1,0:T(1,128)S(1)} %copy-done.1, f32[20]{0:T(128)S(1)} %broadcast_multiply_fusion, f32[8192]{0:T(1024)S(1)} %bitcast.36, f32[8192]{0:T(1024)S(1)} %bitcast.33, f32[20]{0:T(128)S(1)} %copy-done.10, f32[20]{0:T(128)S(1)} %copy-done.8, f32[20]{0:T(128)S(1)} %copy-done.9, ...), kind=kLoop, calls=%fused_computation.37 | loop fusion | flops 1966080 | bytes 1376656 | tf_op jit(solution)/shard_map/sub | solution.py:196
  (50 shorter events, 7.0 us)
Async XLA Ops:
  2.9 6.7 %copy-start.1 = (f32[20,1,8192]{2,1,0:T(1,128)S(1)}, f32[20,1,8192]{2,1,0:T(1,128)}, u32[]{:S(2)}) copy-start(f32[20,1,8192]{2,1,0:T(1,128)} %param.19) | copy-start | bytes 1966084
  2.9 6.6 %copy-start.3 = (f32[20,1,8192]{2,1,0:T(1,128)S(1)}, f32[20,1,8192]{2,1,0:T(1,128)}, u32[]{:S(2)}) copy-start(f32[20,1,8192]{2,1,0:T(1,128)} %param.17) | copy-start | bytes 1966084
  2.9 6.6 %copy-start.4 = (f32[1,8192]{1,0:T(1,128)S(1)}, f32[1,8192]{1,0:T(1,128)}, u32[]{:S(2)}) copy-start(f32[1,8192]{1,0:T(1,128)} %param.16) | copy-start | bytes 98308
  2.9 6.6 %copy-start.7 = (f32[20]{0:T(128)S(1)}, f32[20]{0:T(128)}, u32[]{:S(2)}) copy-start(f32[20]{0:T(128)} %param.22) | copy-start | bytes 244
  2.9 6.6 %copy-start.8 = (f32[20]{0:T(128)S(1)}, f32[20]{0:T(128)}, u32[]{:S(2)}) copy-start(f32[20]{0:T(128)} %param.21) | copy-start | bytes 244
  2.9 6.6 %copy-start.9 = (f32[20]{0:T(128)S(1)}, f32[20]{0:T(128)}, u32[]{:S(2)}) copy-start(f32[20]{0:T(128)} %param.20) | copy-start | bytes 244
  2.9 6.6 %copy-start.11 = (f32[20]{0:T(128)S(1)}, f32[20]{0:T(128)}, u32[]{:S(2)}) copy-start(f32[20]{0:T(128)} %param.23) | copy-start | bytes 244
  2.9 2.2 %collective-permute-start = (f32[2,16,32,3]{3,2,1,0:T(8,128)S(1)}, f32[2,16,32,3]{3,2,1,0:T(8,128)}, u32[]{:S(2)}, u32[]{:S(2)}) collective-permute-start(f32[2,16,32,3]{3,2,1,0:T(8,128)S(1)} %fusion.11), channel_id=1, source_target_pairs={{0,1},{1,0},{2,3},{3,2},{4,5},{5,4},{6,7},{7,6},{8,9},{9,8},{10,11... | collective-permute-start | bytes 36872 | tf_op jit(solution)/shard_map/ppermute | solution.py:21
  6.6 11.2 %collective-permute-start.1 = (f32[2,16,3,134]{3,2,1,0:T(4,128)S(1)}, f32[2,16,3,134]{3,2,1,0:T(4,128)S(1)}, u32[]{:S(2)}, u32[]{:S(2)}) collective-permute-start(f32[2,16,3,134]{3,2,1,0:T(4,128)S(1)} %fusion.19), channel_id=1, source_target_pairs={{0,2},{2,0},{1,3},{3,1},{4,6},{6,4},{5,7},{7,5},{8,10},{10,8},{9,1... | collective-permute-start | bytes 154376 | tf_op jit(solution)/shard_map/ppermute | solution.py:21
  18.8 9.0 %collective-permute-start.2 = (f32[2,3,38,134]{3,2,1,0:T(8,128)}, f32[2,3,38,134]{3,2,1,0:T(8,128)S(1)}, u32[]{:S(2)}, u32[]{:S(2)}) collective-permute-start(f32[2,3,38,134]{3,2,1,0:T(8,128)} %get-tuple-element.23), channel_id=1, source_target_pairs={{0,4},{4,8},{8,12},{1,5},{5,9},{9,13},{2,6},{6,10},{10,14},{3,7},{... | collective-permute-start | bytes 366632 | tf_op jit(solution)/shard_map/ppermute | solution.py:27
  22.3 9.5 %collective-permute-start.3 = (f32[2,3,38,134]{3,2,1,0:T(8,128)}, f32[2,3,38,134]{3,2,1,0:T(8,128)S(1)}, u32[]{:S(2)}, u32[]{:S(2)}) collective-permute-start(f32[2,3,38,134]{3,2,1,0:T(8,128)} %get-tuple-element.24), channel_id=1, source_target_pairs={{4,0},{8,4},{12,8},{5,1},{9,5},{13,9},{6,2},{10,6},{14,10},{7,3},{... | collective-permute-start | bytes 366632 | tf_op jit(solution)/shard_map/ppermute | solution.py:28
  36.0 1.0 copy-start.2
  82.3 3.5 %copy-start = (s32[16,32,128]{2,1,0:T(8,128)S(1)}, s32[16,32,128]{2,1,0:T(8,128)}, u32[]{:S(2)}) copy-start(s32[16,32,128]{2,1,0:T(8,128)} %param.15) | copy-start | bytes 786436
  82.3 16.4 %copy-start.5 = (f32[8192]{0:T(1024)S(1)}, f32[8192]{0:T(1024)}, u32[]{:S(2)}) copy-start(f32[8192]{0:T(1024)} %get-tuple-element.9) | copy-start | bytes 98308
  82.3 16.4 %copy-start.6 = (f32[1,8192]{1,0:T(1,128)S(1)}, f32[1,8192]{1,0:T(1,128)}, u32[]{:S(2)}) copy-start(f32[1,8192]{1,0:T(1,128)} %param.18) | copy-start | bytes 98308
  82.3 17.1 %copy-start.10 = (f32[20]{0:T(128)S(1)}, f32[20]{0:T(128)}, u32[]{:S(2)}) copy-start(f32[20]{0:T(128)} %param.24) | copy-start | bytes 244
  89.2 9.5 %all-to-all-start = ((f32[4,64,128]{2,1,0:T(8,128)}), f32[4,64,128]{2,1,0:T(8,128)S(1)}, u32[]{:S(2)}, u32[]{:S(2)}) async-start(f32[4,64,128]{2,1,0:T(8,128)} %bitcast.20), calls=%async_computation | async-start | bytes 262144 | tf_op jit(solution)/shard_map/all_to_all | solution.py:179

commit v2 on v1

v2 whole, which is shorter than its diff:
```python
import functools

import jax
import jax.numpy as jnp
from jax import lax
from jax.experimental import pallas as pl
from jax.experimental.pallas import tpu as pltpu
from jax.sharding import PartitionSpec as P

TIME_STEP = 0.5
LANES = 128
SUB = 8
PACK = 8
F32 = jnp.float32

VMEM = pl.BlockSpec(memory_space=pltpu.VMEM)
SMEM = pl.BlockSpec(memory_space=pltpu.SMEM)


def shape_of(*dims):
    return jax.ShapeDtypeStruct(dims, F32)


def call(kernel, out_shape, n_in, specs=None, scratch=(), cost=2_000_000, limit=32):
    return pl.pallas_call(
        kernel,
        out_shape=out_shape,
        in_specs=specs if specs is not None else [VMEM] * n_in,
        out_specs=jax.tree.map(lambda _: VMEM, out_shape),
        scratch_shapes=list(scratch),
        compiler_params=pltpu.CompilerParams(vmem_limit_bytes=limit * 1024 * 1024),
        cost_estimate=pl.CostEstimate(flops=cost, bytes_accessed=cost, transcendentals=0),
    )


def lanes_of(shape):
    return lax.broadcasted_iota(jnp.int32, shape, len(shape) - 1)


def subs_of(shape):
    return lax.broadcasted_iota(jnp.int32, shape, len(shape) - 2)


def start_kernel(right_ref, damping_ref, label_ref, w0_ref, inv_ref, pack_ref, stat_ref):
    nx, ny, nz = right_ref.shape
    gz = lax.axis_index("gz")
    lane = lanes_of((ny, nz))
    packed_w = jnp.zeros((ny, nz), F32)
    packed_i = jnp.zeros((ny, nz), F32)
    energy = jnp.zeros((ny, nz), F32)
    cells = jnp.zeros((ny, nz), F32)
    for x in range(nx):
        label = label_ref[x].astype(F32)
        right = right_ref[x]
        inv = 1.0 / (12.0 + damping_ref[x] * (1.0 + 3.0 * label))
        w0 = right * inv
        w0_ref[x] = w0
        inv_ref[x] = inv
        energy = energy + right * w0
        cells = cells + label
        turn = (PACK * x + 3) % nz
        begin = PACK * x + 3 * gz
        chosen = (lane >= begin) & (lane < begin + 3)
        packed_w = jnp.where(chosen, pltpu.roll(w0, turn, 1), packed_w)
        packed_i = jnp.where(chosen, pltpu.roll(inv, turn, 1), packed_i)
    pack_ref[0] = packed_w
    pack_ref[1] = packed_i
    stat_ref[0] = jnp.broadcast_to(jnp.sum(energy, axis=0, keepdims=True), (SUB, nz))
    stat_ref[1] = jnp.broadcast_to(jnp.sum(cells, axis=0, keepdims=True), (SUB, nz))


def y_faces_kernel(w0_ref, inv_ref, own_ref, got_ref, slab_ref, up_ref, down_ref):
    nx, ny, nz = w0_ref.shape
    sub = subs_of((SUB, nz))
    slab_ref[...] = own_ref[...] + got_ref[...]
    for x in range(nx + 1):
        if x < nx:
            w_last, w_first = w0_ref[x, ny - SUB :], w0_ref[x, :SUB]
            i_last, i_first = inv_ref[x, ny - SUB :], inv_ref[x, :SUB]
        else:
            w_last, w_first = slab_ref[0, ny - SUB :], slab_ref[0, :SUB]
            i_last, i_first = slab_ref[1, ny - SUB :], slab_ref[1, :SUB]
        up_ref[x] = jnp.where(sub >= 5, w_last, pltpu.roll(i_last, 4, 0))
        down_ref[x] = jnp.where(sub <= 2, w_first, pltpu.roll(i_first, 4, 0))


def y_face_one_kernel(w0_ref, inv_ref, own_ref, got_ref, slab_ref, face_ref):
    nx, ny, nz = w0_ref.shape
    sub = subs_of((SUB, nz))
    up = lax.axis_index("gy") == 0
    keep_w = jnp.where(up, sub, SUB - 1 - sub) >= 5
    slab_ref[...] = own_ref[...] + got_ref[...]
    for x in range(nx + 1):
        if x < nx:
            w_last, w_first = w0_ref[x, ny - SUB :], w0_ref[x, :SUB]
            i_last, i_first = inv_ref[x, ny - SUB :], inv_ref[x, :SUB]
        else:
            w_last, w_first = slab_ref[0, ny - SUB :], slab_ref[0, :SUB]
            i_last, i_first = slab_ref[1, ny - SUB :], slab_ref[1, :SUB]
        w_face = jnp.where(up, w_last, w_first)
        i_face = jnp.where(up, i_last, i_first)
        face_ref[x] = jnp.where(keep_w, w_face, pltpu.roll(i_face, 4, 0))


def x_faces_kernel(one, w0_ref, inv_ref, slab_ref, *refs):
    if one:
        got_ref, w_ref, i_ref, ring_ref, up_ref, down_ref = refs
    else:
        low_ref, high_ref, w_ref, i_ref, ring_ref, up_ref, down_ref = refs
    nx, ny, nz = w0_ref.shape
    sub = subs_of((SUB, nz))
    lane = lanes_of((ny + SUB, nz))
    if one:
        gy = lax.axis_index("gy")
        from_low = (gy == 1) & (sub >= 5)
        from_high = (gy == 0) & (sub <= 2)
        inv_low = (gy == 1) & (sub >= 6)
        inv_high = (gy == 0) & (sub <= 1)
    for x in range(nx + 1):
        if one:
            got = got_ref[x]
            turned = pltpu.roll(got, 4, 0)
            w_halo = jnp.where(from_low | from_high, got, 0.0)
            i_halo = jnp.where(inv_low | inv_high, turned, 0.0)
        else:
            low, high = low_ref[x], high_ref[x]
            w_halo = jnp.where(sub >= 5, low, jnp.where(sub <= 2, high, 0.0))
            i_halo = jnp.where(
                sub >= 6, pltpu.roll(low, 4, 0), jnp.where(sub <= 1, pltpu.roll(high, 4, 0), 0.0)
            )
        if x < nx:
            w_ref[x, :ny] = w0_ref[x]
            w_ref[x, ny:] = w_halo
            i_ref[x, :ny] = inv_ref[x]
            i_ref[x, ny:] = i_halo
        else:
            ring_ref[0, :ny] = slab_ref[0]
            ring_ref[0, ny:] = w_halo
            ring_ref[1, :ny] = slab_ref[1]
            ring_ref[1, ny:] = i_halo
    for k in range(3):
        up_ref[k] = w_ref[nx - 3 + k]
        down_ref[k] = w_ref[k]
    for k in range(2):
        up_ref[3 + k] = i_ref[nx - 2 + k]
        down_ref[3 + k] = i_ref[k]
    half = pltpu.roll(ring_ref[1], nz // 2, 1)
    up_ref[5] = jnp.where(lane >= nz - 3 * PACK, ring_ref[0], half)
    down_ref[5] = jnp.where(lane < 3 * PACK, ring_ref[0], half)


def around(v):
    rows = v.shape[0]
    return pltpu.roll(v, 1, 0) + pltpu.roll(v, rows - 1, 0)


def stencil_kernel(
    w_ref, i_ref, ring_ref, low_ref, high_ref, stat_ref,
    w1_ref, w2_ref, f0_ref, f1_ref, f2_ref, total_ref,
    a_ref, b_ref, sw_ref,
):
    nx, ring, nz = w_ref.shape
    ny = ring - SUB
    gz = lax.axis_index("gz")
    lane = lanes_of((ring, nz))
    entry = (nz - 1) * gz
    at_entry = lane == entry
    lane_first = lane == 0
    lane_last = lane == nz - 1

    def w0_plane(x):
        if x < 0:
            return low_ref[3 + x]
        if x >= nx:
            return high_ref[x - nx]
        return w_ref[x]

    def inv_plane(x):
        if x < 0:
            return low_ref[5 + x]
        if x >= nx:
            return high_ref[3 + x - nx]
        return i_ref[x]

    lo5, hi5 = low_ref[5], high_ref[5]
    slab_w = jnp.where(lane < 3 * PACK, hi5, 0.0) + jnp.where(lane >= nz - 3 * PACK, lo5, 0.0)
    lo5, hi5 = pltpu.roll(lo5, nz // 2, 1), pltpu.roll(hi5, nz // 2, 1)
    slab_i = jnp.where(lane < 2 * PACK, hi5, 0.0) + jnp.where(lane >= nz - 2 * PACK, lo5, 0.0)
    slab = jnp.concatenate([ring_ref[0], slab_w], axis=1)
    slab_inv = jnp.concatenate([ring_ref[1], slab_i], axis=1)

    def slab_step(s):
        width = s.shape[1]
        along = pltpu.roll(s, 1, 1) + pltpu.roll(s, width - 1, 1)
        both = s + 0.5 * along
        wing = both + 0.5 * around(s)
        total = along + around(both) + pltpu.roll(wing, PACK, 1) + pltpu.roll(wing, width - PACK, 1)
        return total * slab_inv

    def sweep(source, margin, face_ref, store):
        wing_before = wing_here = rest_here = None
        v_before = v_here = face_here = None
        for x in range(-margin - 1, nx + margin + 1):
            v = source(x)
            place = (PACK * x) % (2 * nz)
            half = sw_ref[:, nz * (place // nz) : nz * (place // nz) + nz]
            turn = lax.rem(entry - (place % nz + 3 - gz) + 2 * nz, nz)
            edge = jnp.where(at_entry, pltpu.roll(half, turn, 1), 0.0)
            along = pltpu.roll(jnp.where(lane_first, edge, v), nz - 1, 1) + pltpu.roll(
                jnp.where(lane_last, edge, v), 1, 1
            )
            both = v + 0.5 * along
            beside = around(v)
            wing = both + 0.5 * beside
            rest = along + around(both)
            done = x - 1
            if done >= -margin:
                store(done, rest_here + wing_before + wing, v_here)
                if 0 <= done < nx:
                    face_ref[done] = face_here + (v_before + v)[:ny]
            wing_before, wing_here, rest_here = wing_here, wing, rest
            v_before, v_here = v_here, v
            if 0 <= x < nx:
                face_here = (along + beside - 6.0 * v)[:ny]

    sums = {}

    def add(name, value):
        part = jnp.sum(value[:ny].reshape(ny // SUB, SUB, nz), axis=0)
        sums[name] = part if name not in sums else sums[name] + part

    def store0(x, total, v):
        w1 = total * inv_plane(x)
        a_ref[x + 2] = w1
        if 0 <= x < nx:
            w1_ref[x] = w1[:ny]
            add(1, v * total)
            add(2, w1 * total)

    def store1(x, total, v):
        w2 = total * inv_plane(x)
        b_ref[x + 1] = w2
        if 0 <= x < nx:
            w2_ref[x] = w2[:ny]
            add(3, v * total)
            add(4, w2 * total)

    def store2(x, total, v):
        add(5, v * total)

    sw_ref[...] = slab
    sweep(w0_plane, 2, f0_ref, store0)
    slab = slab_step(slab)
    sw_ref[...] = slab
    sweep(lambda x: a_ref[x + 2], 1, f1_ref, store1)
    slab = slab_step(slab)
    sw_ref[...] = slab
    sweep(lambda x: b_ref[x + 1], 0, f2_ref, store2)

    total_ref[0:1] = stat_ref[0, 0:1]
    for k in range(1, 6):
        total_ref[k : k + 1] = jnp.sum(sums[k], axis=0, keepdims=True)
    total_ref[6:8] = jnp.zeros((2, nz), F32)
    here = (lax.axis_index("gx") * lax.axis_size("gy") + lax.axis_index("gy")) * lax.axis_size("gz") + gz
    count = jnp.sum(stat_ref[1], axis=1, keepdims=True)
    total_ref[8:16] = jnp.where(lanes_of((SUB, nz)) == here, count, 0.0)


def shift_left(v, amount, lane):
    rows = v.shape[0]
    if amount < LANES:
        turned = pltpu.roll(v, LANES - amount, 1)
        below = pltpu.roll(turned, rows - 1, 0)
        return jnp.where(lane < LANES - amount, turned, below)
    return jnp.concatenate([v[amount // LANES :], v[: amount // LANES]], axis=0)


def plan_kernel(label_ref, plan_ref):
    rows = label_ref.shape[0]
    lane = lanes_of((rows, LANES))
    row = subs_of((rows, LANES))
    heart = label_ref[...] == 1
    ones = heart.astype(jnp.bfloat16)
    upper = (subs_of((LANES, LANES)) < lanes_of((LANES, LANES))).astype(jnp.bfloat16)
    in_row = jnp.dot(ones, upper, preferred_element_type=F32)
    totals = jnp.dot(ones, jnp.ones((LANES, LANES), jnp.bfloat16), preferred_element_type=F32)
    lower = (subs_of((rows, rows)) > lanes_of((rows, rows))).astype(jnp.bfloat16)
    before = jnp.dot(lower, totals.astype(jnp.bfloat16), preferred_element_type=F32)
    rank = (in_row + before).astype(jnp.int32)
    way = jnp.where(heart, row * LANES + lane - rank, 0)
    plan = jnp.zeros((rows, LANES), jnp.int32)
    step = 1
    while step < rows * LANES:
        moving = jnp.where((way & step) != 0, way, 0)
        arriving = shift_left(moving, step, lane)
        plan = plan | (arriving & step)
        way = (way - moving) | arriving
        step *= 2
    plan_ref[...] = plan


def galerkin(t):
    g00, g01, g02, g12, g22 = t[0] - t[1], t[1] - t[2], t[2] - t[3], t[3] - t[4], t[4] - t[5]
    g11 = g02
    l10, l20 = g01 / g00, g02 / g00
    d1 = g11 - l10 * g01
    m21 = g12 - l20 * g01
    ok1 = d1 > 1e-6 * g11
    d1 = jnp.where(ok1, d1, 1.0)
    l21 = jnp.where(ok1, m21 / d1, 0.0)
    d2 = g22 - l20 * g02 - l21 * m21
    ok2 = ok1 & (d2 > 1e-6 * g22)
    d2 = jnp.where(ok2, d2, 1.0)
    y1 = t[1] - l10 * t[0]
    y2 = t[2] - l20 * t[0] - l21 * y1
    c2 = jnp.where(ok2, y2 / d2, 0.0)
    c1 = jnp.where(ok1, y1 / d1 - l21 * c2, 0.0)
    c0 = t[0] / g00 - l10 * c1 - l20 * c2
    return c0, c1, c2


def combine_kernel(
    slot_rows, total_ref, w0_ref, w1_ref, w2_ref, f0_ref, f1_ref, f2_ref, plan_ref, x_ref, out_ref, buf_ref
):
    rows = w0_ref.shape[0]
    lane = lanes_of((rows, LANES))
    row = subs_of((rows, LANES))
    sums = jnp.sum(total_ref[0:8], axis=1, keepdims=True)
    t = [jnp.broadcast_to(sums[k : k + 1], (1, LANES)) for k in range(6)]
    c0, c1, c2 = galerkin(t)
    x_ref[...] = c0 * w0_ref[...] + c1 * w1_ref[...] + c2 * w2_ref[...]
    value = c0 * f0_ref[...] + c1 * f1_ref[...] + c2 * f2_ref[...]
    plan = plan_ref[...]
    step = 1
    while step < rows * LANES:
        value = jnp.where((plan & step) != 0, shift_left(value, step, lane), value)
        step *= 2
    ny, nz = lax.axis_size("gy"), lax.axis_size("gz")
    counts = total_ref[8:16]
    dev = lanes_of((SUB, LANES))
    column = lax.axis_index("gy") * nz + lax.axis_index("gz")
    mine = lax.rem(dev, ny * nz) == column
    gx = lax.axis_index("gx")
    first = subs_of((SUB, LANES)) == 0
    offset = jnp.sum(jnp.where(first & mine & (dev < gx * ny * nz), counts, 0.0)).astype(jnp.int32)
    count = jnp.sum(jnp.where(first & mine & (dev // (ny * nz) == gx), counts, 0.0)).astype(jnp.int32)
    slots = value[:slot_rows]
    index = (row * LANES + lane)[:slot_rows]
    slots = jnp.where(index < count, slots, 0.0)
    slots = jnp.concatenate([slots, jnp.zeros((SUB, LANES), F32)], axis=0)
    inner = lax.rem(offset, LANES)
    turned = pltpu.roll(slots, inner, 1)
    above = pltpu.roll(turned, 1, 0)
    moved = jnp.where(lane[: slot_rows + SUB] >= inner, turned, above)
    buf_ref[...] = jnp.zeros_like(buf_ref)
    buf_ref[pl.ds(offset // LANES, slot_rows + SUB), :] = moved
    out_ref[...] = buf_ref[: out_ref.shape[0]]


def membrane_kernel(
    half_ref, slope_ref, tau_ref, cond_ref, v_ref, gates_ref, cot_ref, base_ref, sum_ref, factor_ref
):
    n_states = gates_ref.shape[0]
    v = v_ref[...]
    rows = v.shape[0]

    def state(g, carry):
        total, current = carry
        inv_slope = 1.0 / slope_ref[g]
        tau_base = tau_ref[g]
        scaled = (v - half_ref[g]) * inv_slope
        gate = gates_ref[g]
        cot = cot_ref[g]
        steady = 1.0 / (1.0 + jnp.exp(-scaled))
        bell = jnp.exp(-scaled * scaled)
        rate = TIME_STEP / (tau_base * (0.5 + bell))
        decay = jnp.exp(-rate)
        steady_slope = steady * (1.0 - steady)
        decay_slope = decay * rate * rate * ((tau_base / TIME_STEP) * bell * (-2.0 * scaled))
        change = (steady_slope * (1.0 - decay) + (gate - steady) * decay_slope) * inv_slope
        base_ref[g] = cot * decay
        return total + cot * change, current + cond_ref[g] * gate

    zero = jnp.zeros((rows, LANES), F32)
    total, current = lax.fori_loop(0, n_states, state, (zero, zero), unroll=2)
    sum_ref[...] = total
    factor_ref[...] = 1.0 - TIME_STEP * current


def finish_kernel(
    cond_ref, rev_ref, landed_ref, vcot_ref, v_ref, sum_ref, factor_ref, base_ref, volt_ref, gate_ref
):
    landed = landed_ref[0]
    for k in range(1, landed_ref.shape[0]):
        landed = landed + landed_ref[k]
    cot = vcot_ref[...] + landed
    v = v_ref[...]
    volt_ref[...] = cot * factor_ref[...] + sum_ref[...]
    half = TIME_STEP * cot
    for g in range(base_ref.shape[0]):
        gate_ref[g] = base_ref[g] - (cond_ref[g] * half) * (v - rev_ref[g])


def both_ways(up, down, axis):
    count = lax.axis_size(axis)
    low = lax.ppermute(up, axis, [(i, i + 1) for i in range(count - 1)])
    high = lax.ppermute(down, axis, [(i + 1, i) for i in range(count - 1)])
    return low, high


def reduce_over(value, axis):
    count = lax.axis_size(axis)
    step = 1
    while step < count:
        value = value + lax.ppermute(value, axis, [(i, i ^ step) for i in range(count)])
        step *= 2
    return value


def local(
    potential_cot, damping, tissue_label, heart_index, voltage, gates, voltage_cot, gates_cot,
    half_voltage, gate_slope, tau_base, conductance, reversal,
):
    nx, ny, nz = potential_cot.shape
    rows = nx * ny
    ring = ny + SUB
    n_gx, n_gy = lax.axis_size("gx"), lax.axis_size("gy")
    n_states = gates.shape[0]
    block_rows = voltage.shape[1] // LANES
    slot_rows = heart_index.shape[3] // LANES
    block = shape_of(nx, ny, nz)
    flat = lambda a: a.reshape(rows, LANES)
    cells = lambda a: a.reshape(block_rows, LANES)
    states = lambda a: a.reshape(n_states, block_rows, LANES)

    w0, inv, packed, stat = call(
        start_kernel, (block, block, shape_of(2, ny, nz), shape_of(2, SUB, nz)), 3
    )(potential_cot, damping, tissue_label)

    got = lax.ppermute(packed, "gz", [(0, 1), (1, 0)])
    base, total_change, factor = call(
        membrane_kernel,
        (shape_of(n_states, block_rows, LANES), shape_of(block_rows, LANES), shape_of(block_rows, LANES)),
        7,
        specs=[SMEM] * 4 + [VMEM] * 3,
        cost=6_000_000,
    )(half_voltage, gate_slope, tau_base, conductance, cells(voltage), states(gates), states(gates_cot))
    plan = call(plan_kernel, jax.ShapeDtypeStruct((rows, LANES), jnp.int32), 1, cost=6_000_000)(flat(tissue_label))

    face = shape_of(nx + 1, SUB, nz)
    slab_shape = shape_of(2, ny, nz)
    ring_shapes = (shape_of(nx, ring, nz), shape_of(nx, ring, nz), shape_of(2, ring, nz))
    x_shapes = ring_shapes + (shape_of(6, ring, nz), shape_of(6, ring, nz))
    if n_gy == 2:
        slab, mine = call(y_face_one_kernel, (slab_shape, face), 4)(w0, inv, packed, got)
        halo = (lax.ppermute(mine, "gy", [(0, 1), (1, 0)]),)
    else:
        slab, up, down = call(y_faces_kernel, (slab_shape, face, face), 4)(w0, inv, packed, got)
        halo = both_ways(up, down, "gy")
    wide, wide_inv, ring_slab, up, down = call(
        functools.partial(x_faces_kernel, n_gy == 2), x_shapes, 3 + len(halo)
    )(w0, inv, slab, *halo)
    low, high = both_ways(up, down, "gx")

    w1, w2, f0, f1, f2, sums = call(
        stencil_kernel,
        (block,) * 5 + (shape_of(16, nz),),
        6,
        scratch=[
            pltpu.VMEM((nx + 4, ring, nz), F32),
            pltpu.VMEM((nx + 2, ring, nz), F32),
            pltpu.VMEM((ring, 2 * nz), F32),
        ],
    )(wide, wide_inv, ring_slab, low, high, stat)
    for axis in ("gz", "gy", "gx"):
        sums = reduce_over(sums, axis)

    solution, placed = call(
        functools.partial(combine_kernel, slot_rows),
        (shape_of(rows, LANES), shape_of(n_gx * block_rows, LANES)),
        8,
        scratch=[pltpu.VMEM((n_gx * block_rows + slot_rows + SUB, LANES), F32)],
    )(sums, flat(w0), flat(w1), flat(w2), flat(f0), flat(f1), flat(f2), plan)
    landed = lax.all_to_all(placed.reshape(n_gx, block_rows, LANES), "gx", 0, 0, tiled=True)

    volt_grad, gate_grad = call(
        finish_kernel,
        (shape_of(block_rows, LANES), shape_of(n_states, block_rows, LANES)),
        8,
        specs=[SMEM] * 2 + [VMEM] * 6,
    )(conductance, reversal, landed, cells(voltage_cot), cells(voltage), total_change, factor, base)
    return solution.reshape(nx, ny, nz), volt_grad.reshape(voltage.shape), gate_grad.reshape(gates.shape)


def solution(mesh):
    grid = P(("groups", "gx"), "gy", "gz")
    cells = P(("groups", "gy", "gz"), "gx")
    states = P(None, ("groups", "gy", "gz"), "gx")
    in_specs = (
        grid, grid, grid, P(("groups", "gx"), "gy", "gz", None), cells, states, cells, states,
        P(), P(), P(), P(), P(),
    )
    return jax.shard_map(
        local, mesh=mesh, in_specs=in_specs, out_specs=(grid, cells, states), check_vma=False
    )
```

time: 104 us -> 53.4 us (0.51)
  blocking collectives: 29.5 us -> 0 us
  other arithmetic: 27.1 us -> 0.01 us
  between operations: 10.6 us -> 0.74 us
  Pallas kernels: 2.74 us -> 12.1 us
  starting transfers between devices: 11.5 us -> 18.2 us
  waiting for transfers between devices: 15.3 us -> 17.8 us
  local copies, waits for them, and re-layouts: 6.57 us -> 4.16 us
    psum x1 -> x0, blocking collectives: 29.5 us -> none  [local(): total = lax.psum(jnp.concatenate([sums, counts]), ('gx', 'gy', 'gz'))]
    reduce_sum x4 -> x0, other arithmetic: 9.84 us -> none  [the longest x1 8.18 us: local(): jnp.sum(param(conductance) * gates, axis=0)]
    pallas_call x1 -> x8, Pallas kernels: 2.74 us -> 12.1 us  [the longest x1 4.79 us: local(): call(stencil_kernel, (block,) * 5 + (shape_of(16, nz),), 6, scratch=[pltp...]
    ppermute x4 -> x8, starting transfers between devices: 8.22 us -> 14.2 us  [the longest x4 5.72 us: reduce_over(): lax.ppermute(value, axis, [(i, i ^ step) for i in range(count)])]
    ppermute x4 -> x8, waiting for transfers between devices: 9.18 us -> 14.5 us  [the longest x4 5.63 us: reduce_over(): lax.ppermute(value, axis, [(i, i ^ step) for i in range(count)])]
    sub x3 -> x0, other arithmetic: 5.12 us -> none  [the longest x1 3.94 us: local(): gates_cot * decay]
    concatenate x1 -> x0, local copies, waits for them, and re-layouts: 3.89 us -> none  [local(): total = lax.psum(jnp.concatenate([sums, counts]), ('gx', 'gy', 'gz'))]
    unnamed x24 -> x26, local copies, waits for them, and re-layouts: 0.72 us -> 4.16 us
  transfers between devices with their start and end apart: 5 -> 9, of which waited for: 4 -> 9; matrix products, arithmetic and copies ran while one was open for 9% -> 0% of each run, Pallas kernels for 0% -> 7%
where the time goes in v2:
time: 53.4 us; the launch traced here: 53 us
  starting transfers between devices  18.2 us (34%)
  waiting for transfers between devices  17.8 us (33%)
  Pallas kernels  12.1 us (23%)
  local copies, waits for them, and re-layouts  4.16 us (8%)
  between operations  0.74 us (1%)
    ppermute x4, starting transfers between devices, reduce_over(): lax.ppermute(value, axis, [(i, i ^ step) for i in range(count)])  5.72 us
    ppermute x4, waiting for transfers between devices, reduce_over(): lax.ppermute(value, axis, [(i, i ^ step) for i in range(count)])  5.63 us
    pallas_call x1, Pallas kernels, local(): call(stencil_kernel, (block,) * 5 + (shape_of(16, nz),), 6, scratch=[pltp...  4.79 us
    ppermute x1, waiting for transfers between devices, both_ways(): high = lax.ppermute(down, axis, [(i + 1, i) for i in range(count - 1)])  4.35 us
    unnamed x26, local copies, waits for them, and re-layouts  4.16 us
    all_to_all x1, starting transfers between devices, local(): lax.all_to_all(placed.reshape(n_gx, block_rows, LANES), 'gx', 0, 0, tiled...  3.99 us
    ppermute x1, starting transfers between devices, both_ways(): low = lax.ppermute(up, axis, [(i, i + 1) for i in range(count - 1)])  3.79 us
    all_to_all x1, waiting for transfers between devices, local(): lax.all_to_all(placed.reshape(n_gx, block_rows, LANES), 'gx', 0, 0, tiled...  3.32 us
  transfers between devices with their start and end apart: 9, of which 9 were waited for; matrix products, arithmetic and copies ran while one was open for 0% of the time, Pallas kernels for 7%

profile of v2, /device:TPU:0, one launch (start us, length us, event | category | flops | bytes accessed | tf_op | source)
XLA Modules:
  0.0 53.0 jit_solution(6287573550989782673)
XLA Ops:
  0.6 0.9 %copy-done = s32[16,32,128]{2,1,0:T(8,128)S(1)} copy-done((s32[16,32,128]{2,1,0:T(8,128)S(1)}, s32[16,32,128]{2,1,0:T(8,128)}, u32[]{:S(2)}) %copy-start) | copy-done | bytes 262168
  1.6 0.9 %copy-done.4 = f32[16,32,128]{2,1,0:T(8,128)S(1)} copy-done((f32[16,32,128]{2,1,0:T(8,128)S(1)}, f32[16,32,128]{2,1,0:T(8,128)}, u32[]{:S(2)}) %copy-start.4) | copy-done | bytes 262168
  2.5 0.9 %copy-done.5 = f32[16,32,128]{2,1,0:T(8,128)S(1)} copy-done((f32[16,32,128]{2,1,0:T(8,128)S(1)}, f32[16,32,128]{2,1,0:T(8,128)}, u32[]{:S(2)}) %copy-start.5) | copy-done | bytes 262168
  4.2 0.9 %collective-permute-done.got_ref = f32[2,32,128]{2,1,0:T(8,128)S(1)} collective-permute-done((f32[2,32,128]{2,1,0:T(8,128)S(1)}, f32[2,32,128]{2,1,0:T(8,128)S(1)}, u32[]{:S(2)}, u32[]{:S(2)}) %collective-permute-start) | collective-permute-done | bytes 32800 | tf_op jit(solution)/shard_map/ppermute | solution.py:440
  5.1 2.9 %collective-permute-start.1 = (f32[17,8,128]{2,1,0:T(8,128)S(1)}, f32[17,8,128]{2,1,0:T(8,128)S(1)}, u32[]{:S(2)}, u32[]{:S(2)}) collective-permute-start(f32[17,8,128]{2,1,0:T(8,128)S(1)} %get-tuple-element.31), channel_id=1, source_target_pairs={{0,2},{2,0},{1,3},{3,1},{4,6},{6,4},{5,7},{7,5},{8,10},{10,8},{9,1... | collective-permute-start | bytes 208904 | tf_op jit(solution)/shard_map/ppermute | solution.py:456
  8.0 2.5 %collective-permute-done.1.refs_0_ = f32[17,8,128]{2,1,0:T(8,128)S(1)} collective-permute-done((f32[17,8,128]{2,1,0:T(8,128)S(1)}, f32[17,8,128]{2,1,0:T(8,128)S(1)}, u32[]{:S(2)}, u32[]{:S(2)}) %collective-permute-start.1) | collective-permute-done | bytes 69664 | tf_op jit(solution)/shard_map/ppermute | solution.py:456
  10.6 3.8 %collective-permute-start.2 = (f32[6,40,128]{2,1,0:T(8,128)S(1)}, f32[6,40,128]{2,1,0:T(8,128)S(1)}, u32[]{:S(2)}, u32[]{:S(2)}) collective-permute-start(f32[6,40,128]{2,1,0:T(8,128)S(1)} %get-tuple-element.35), channel_id=1, source_target_pairs={{0,4},{4,8},{8,12},{1,5},{5,9},{9,13},{2,6},{6,10},{10,14},{3,7},{... | collective-permute-start | bytes 368648 | tf_op jit(solution)/shard_map/ppermute | solution.py:406
  14.4 1.3 %collective-permute-start.3 = (f32[6,40,128]{2,1,0:T(8,128)S(1)}, f32[6,40,128]{2,1,0:T(8,128)S(1)}, u32[]{:S(2)}, u32[]{:S(2)}) collective-permute-start(f32[6,40,128]{2,1,0:T(8,128)S(1)} %get-tuple-element.36), channel_id=1, source_target_pairs={{4,0},{8,4},{12,8},{5,1},{9,5},{13,9},{6,2},{10,6},{14,10},{7,3},{... | collective-permute-start | bytes 368648 | tf_op jit(solution)/shard_map/ppermute | solution.py:407
  15.7 1.1 %collective-permute-done.2.low_ref = f32[6,40,128]{2,1,0:T(8,128)S(1)} collective-permute-done((f32[6,40,128]{2,1,0:T(8,128)S(1)}, f32[6,40,128]{2,1,0:T(8,128)S(1)}, u32[]{:S(2)}, u32[]{:S(2)}) %collective-permute-start.2) | collective-permute-done | bytes 122912 | tf_op jit(solution)/shard_map/ppermute | solution.py:406
  16.8 4.4 %collective-permute-done.3.high_ref = f32[6,40,128]{2,1,0:T(8,128)S(1)} collective-permute-done((f32[6,40,128]{2,1,0:T(8,128)S(1)}, f32[6,40,128]{2,1,0:T(8,128)S(1)}, u32[]{:S(2)}, u32[]{:S(2)}) %collective-permute-start.3) | collective-permute-done | bytes 122912 | tf_op jit(solution)/shard_map/ppermute | solution.py:407
  21.2 4.8 %shard_map.142 = (f32[16,32,128]{2,1,0:T(8,128)S(1)}, f32[16,32,128]{2,1,0:T(8,128)S(1)}, f32[16,32,128]{2,1,0:T(8,128)S(1)}, f32[16,32,128]{2,1,0:T(8,128)S(1)}...) custom-call(f32[16,40,128]{2,1,0:T(8,128)S(1)} %get-tuple-element.32.w_ref, ...), custom_call_target="tpu_custom_call" | custom-call | flops 2000000 | bytes 2000000 | tf_op jit(solution)/shard_map/pallas_call | solution.py:465
  26.1 1.2 %collective-permute-done.4 = f32[16,128]{1,0:T(8,128)S(1)} collective-permute-done((f32[16,128]{1,0:T(8,128)S(1)}, f32[16,128]{1,0:T(8,128)S(1)}, u32[]{:S(2)}, u32[]{:S(2)}) %collective-permute-start.4) | collective-permute-done | bytes 8224 | tf_op jit(solution)/shard_map/ppermute | solution.py:415
  27.2 1.5 %collective-permute-start.5 = (f32[16,128]{1,0:T(8,128)S(1)}, f32[16,128]{1,0:T(8,128)S(1)}, u32[]{:S(2)}, u32[]{:S(2)}) collective-permute-start(f32[16,128]{1,0:T(8,128)S(1)} %add.12), channel_id=1, source_target_pairs={{0,2},{2,0},{1,3},{3,1},{4,6},{6,4},{5,7},{7,5},{8,10},{10,8},{9,1... | collective-permute-start | bytes 24584 | tf_op jit(solution)/shard_map/ppermute | solution.py:415
  28.7 2.2 %collective-permute-done.5 = f32[16,128]{1,0:T(8,128)S(1)} collective-permute-done((f32[16,128]{1,0:T(8,128)S(1)}, f32[16,128]{1,0:T(8,128)S(1)}, u32[]{:S(2)}, u32[]{:S(2)}) %collective-permute-start.5) | collective-permute-done | bytes 8224 | tf_op jit(solution)/shard_map/ppermute | solution.py:415
  30.9 1.6 %collective-permute-start.6 = (f32[16,128]{1,0:T(8,128)S(1)}, f32[16,128]{1,0:T(8,128)S(1)}, u32[]{:S(2)}, u32[]{:S(2)}) collective-permute-start(f32[16,128]{1,0:T(8,128)S(1)} %add.13), channel_id=1, source_target_pairs={{0,4},{4,0},{8,12},{12,8},{1,5},{5,1},{9,13},{13,9},{2,6},{6,2},{1... | collective-permute-start | bytes 24584 | tf_op jit(solution)/shard_map/ppermute | solution.py:415
  32.5 2.1 %collective-permute-done.6 = f32[16,128]{1,0:T(8,128)S(1)} collective-permute-done((f32[16,128]{1,0:T(8,128)S(1)}, f32[16,128]{1,0:T(8,128)S(1)}, u32[]{:S(2)}, u32[]{:S(2)}) %collective-permute-start.6) | collective-permute-done | bytes 8224 | tf_op jit(solution)/shard_map/ppermute | solution.py:415
  34.5 2.6 %collective-permute-start.7 = (f32[16,128]{1,0:T(8,128)S(1)}, f32[16,128]{1,0:T(8,128)S(1)}, u32[]{:S(2)}, u32[]{:S(2)}) collective-permute-start(f32[16,128]{1,0:T(8,128)S(1)} %add.14), channel_id=1, source_target_pairs={{0,8},{4,12},{8,0},{12,4},{1,9},{5,13},{9,1},{13,5},{2,10},{6,14},... | collective-permute-start | bytes 24584 | tf_op jit(solution)/shard_map/ppermute | solution.py:415
  37.1 1.7 %shard_map.143.plan_ref = s32[512,128]{1,0:T(8,128)S(1)} custom-call(s32[512,128]{1,0:T(8,128)S(1)} %bitcast.16), custom_call_target="tpu_custom_call" | custom-call | flops 6000000 | bytes 6000000 | tf_op jit(solution)/shard_map/pallas_call | solution.py:448
  39.1 1.8 %shard_map.144 = (f32[512,128]{1,0:T(8,128)}, f32[256,128]{1,0:T(8,128)}) custom-call(f32[16,128]{1,0:T(8,128)S(1)} %add.15.total_ref, f32[512,128]{1,0:T(8,128)S(1)} %bitcast.15, f32[512,128]{1,0:T(8,128)S(1)} %bitcast.19, f32[512,128]{1,0:T(8,128)S(1)} %bitcast.20, f32[512,128]{1,0:T(8,128)S(1)} %bitcast.21, f32[512,128]{1,0:T(8,128)S(1)} %bitcast.22, ...), custom_call_target="tpu_custom_call" | custom-call | flops 2000000 | bytes 2000000 | tf_op jit(solution)/shard_map/pallas_call | solution.py:478
  40.9 4.0 %all-to-all-start = ((f32[4,64,128]{2,1,0:T(8,128)}), f32[4,64,128]{2,1,0:T(8,128)S(1)}, u32[]{:S(2)}, u32[]{:S(2)}) async-start(f32[4,64,128]{2,1,0:T(8,128)} %bitcast.8), calls=%async_computation | async-start | bytes 262144 | tf_op jit(solution)/shard_map/all_to_all | solution.py:484
  45.6 1.9 %shard_map.145 = (f32[20,64,128]{2,1,0:T(8,128)S(1)}, f32[64,128]{1,0:T(8,128)S(1)}, f32[64,128]{1,0:T(8,128)S(1)}) custom-call(f32[20]{0:T(128)S(1)} %copy-done.9, f32[20]{0:T(128)S(1)} %copy-done.10, f32[20]{0:T(128)S(1)} %copy-done.11, f32[20]{0:T(128)S(1)} %copy-done.8, f32[64,128]{1,0:T(8,128)S(1)} %bitcast.24, f32[20,64,128]{2,1,0:T(8,128)S(1)} %bitcast.17, ...), custom_call_target="tpu_custom_call" | custom-call | flops 6000000 | bytes 6000000 | tf_op jit(solution)/shard_map/pallas_call | solution.py:441
  47.5 3.3 %all-to-all-done.landed_ref = f32[4,64,128]{2,1,0:T(8,128)S(1)} async-done(((f32[4,64,128]{2,1,0:T(8,128)}), f32[4,64,128]{2,1,0:T(8,128)S(1)}, u32[]{:S(2)}, u32[]{:S(2)}) %all-to-all-start) | async-done | bytes 131104 | tf_op jit(solution)/shard_map/all_to_all | solution.py:484
  50.8 0.7 %copy-done.12 = f32[20]{0:T(128)S(1)} copy-done((f32[20]{0:T(128)S(1)}, f32[20]{0:T(128)}, u32[]{:S(2)}) %copy-start.12) | copy-done | bytes 104
  51.5 1.5 %shard_map.146 = (f32[64,128]{1,0:T(8,128)}, f32[20,64,128]{2,1,0:T(8,128)}) custom-call(f32[20]{0:T(128)S(1)} %copy-done.8, f32[20]{0:T(128)S(1)} %copy-done.12, f32[4,64,128]{2,1,0:T(8,128)S(1)} %all-to-all-done.landed_ref, f32[64,128]{1,0:T(8,128)S(1)} %bitcast.26, f32[64,128]{1,0:T(8,128)S(1)} %bitcast.25, f32[64,128]{1,0:T(8,128)S(1)} %get-tuple-element.46.sum_ref, ...), custom_call_target="tpu_custom_call" | custom-call | flops 2000000 | bytes 2000000 | tf_op jit(solution)/shard_map/pallas_call | solution.py:486
  (32 shorter events, 1.9 us)
Async XLA Ops:
  0.6 1.0 %copy-start = (s32[16,32,128]{2,1,0:T(8,128)S(1)}, s32[16,32,128]{2,1,0:T(8,128)}, u32[]{:S(2)}) copy-start(s32[16,32,128]{2,1,0:T(8,128)} %label_ref.1) | copy-start | bytes 786436
  1.6 0.9 %copy-start.4 = (f32[16,32,128]{2,1,0:T(8,128)S(1)}, f32[16,32,128]{2,1,0:T(8,128)}, u32[]{:S(2)}) copy-start(f32[16,32,128]{2,1,0:T(8,128)} %right_ref.1) | copy-start | bytes 786436
  2.5 0.9 %copy-start.5 = (f32[16,32,128]{2,1,0:T(8,128)S(1)}, f32[16,32,128]{2,1,0:T(8,128)}, u32[]{:S(2)}) copy-start(f32[16,32,128]{2,1,0:T(8,128)} %damping_ref.1) | copy-start | bytes 786436
  3.7 1.4 %collective-permute-start = (f32[2,32,128]{2,1,0:T(8,128)S(1)}, f32[2,32,128]{2,1,0:T(8,128)S(1)}, u32[]{:S(2)}, u32[]{:S(2)}) collective-permute-start(f32[2,32,128]{2,1,0:T(8,128)S(1)} %get-tuple-element.29.own_ref), channel_id=1, source_target_pairs={{0,1},{1,0},{2,3},{3,2},{4,5},{5,4},{6,7},{7,6},{8,9},{9,8},{10,11... | collective-permute-start | bytes 98312 | tf_op jit(solution)/shard_map/ppermute | solution.py:440
  5.1 5.4 %collective-permute-start.1 = (f32[17,8,128]{2,1,0:T(8,128)S(1)}, f32[17,8,128]{2,1,0:T(8,128)S(1)}, u32[]{:S(2)}, u32[]{:S(2)}) collective-permute-start(f32[17,8,128]{2,1,0:T(8,128)S(1)} %get-tuple-element.31), channel_id=1, source_target_pairs={{0,2},{2,0},{1,3},{3,1},{4,6},{6,4},{5,7},{7,5},{8,10},{10,8},{9,1... | collective-permute-start | bytes 208904 | tf_op jit(solution)/shard_map/ppermute | solution.py:456
  10.6 6.2 %collective-permute-start.2 = (f32[6,40,128]{2,1,0:T(8,128)S(1)}, f32[6,40,128]{2,1,0:T(8,128)S(1)}, u32[]{:S(2)}, u32[]{:S(2)}) collective-permute-start(f32[6,40,128]{2,1,0:T(8,128)S(1)} %get-tuple-element.35), channel_id=1, source_target_pairs={{0,4},{4,8},{8,12},{1,5},{5,9},{9,13},{2,6},{6,10},{10,14},{3,7},{... | collective-permute-start | bytes 368648 | tf_op jit(solution)/shard_map/ppermute | solution.py:406
  14.4 6.8 %collective-permute-start.3 = (f32[6,40,128]{2,1,0:T(8,128)S(1)}, f32[6,40,128]{2,1,0:T(8,128)S(1)}, u32[]{:S(2)}, u32[]{:S(2)}) collective-permute-start(f32[6,40,128]{2,1,0:T(8,128)S(1)} %get-tuple-element.36), channel_id=1, source_target_pairs={{4,0},{8,4},{12,8},{5,1},{9,5},{13,9},{6,2},{10,6},{14,10},{7,3},{... | collective-permute-start | bytes 368648 | tf_op jit(solution)/shard_map/ppermute | solution.py:407
  21.2 15.9 %copy-start.1 = (s32[16,32,128]{2,1,0:T(8,128)S(1)}, s32[16,32,128]{2,1,0:T(8,128)}, u32[]{:S(2)}) copy-start(s32[16,32,128]{2,1,0:T(8,128)} %label_ref.1) | copy-start | bytes 786436
  26.0 1.2 %collective-permute-start.4 = (f32[16,128]{1,0:T(8,128)S(1)}, f32[16,128]{1,0:T(8,128)S(1)}, u32[]{:S(2)}, u32[]{:S(2)}) collective-permute-start(f32[16,128]{1,0:T(8,128)S(1)} %get-tuple-element.38), channel_id=1, source_target_pairs={{0,1},{1,0},{2,3},{3,2},{4,5},{5,4},{6,7},{7,6},{8,9},{9,8},{10,11... | collective-permute-start | bytes 24584 | tf_op jit(solution)/shard_map/ppermute | solution.py:415
  27.2 3.7 %collective-permute-start.5 = (f32[16,128]{1,0:T(8,128)S(1)}, f32[16,128]{1,0:T(8,128)S(1)}, u32[]{:S(2)}, u32[]{:S(2)}) collective-permute-start(f32[16,128]{1,0:T(8,128)S(1)} %add.12), channel_id=1, source_target_pairs={{0,2},{2,0},{1,3},{3,1},{4,6},{6,4},{5,7},{7,5},{8,10},{10,8},{9,1... | collective-permute-start | bytes 24584 | tf_op jit(solution)/shard_map/ppermute | solution.py:415
  30.9 3.7 %collective-permute-start.6 = (f32[16,128]{1,0:T(8,128)S(1)}, f32[16,128]{1,0:T(8,128)S(1)}, u32[]{:S(2)}, u32[]{:S(2)}) collective-permute-start(f32[16,128]{1,0:T(8,128)S(1)} %add.13), channel_id=1, source_target_pairs={{0,4},{4,0},{8,12},{12,8},{1,5},{5,1},{9,13},{13,9},{2,6},{6,2},{1... | collective-permute-start | bytes 24584 | tf_op jit(solution)/shard_map/ppermute | solution.py:415
  34.5 4.5 %collective-permute-start.7 = (f32[16,128]{1,0:T(8,128)S(1)}, f32[16,128]{1,0:T(8,128)S(1)}, u32[]{:S(2)}, u32[]{:S(2)}) collective-permute-start(f32[16,128]{1,0:T(8,128)S(1)} %add.14), channel_id=1, source_target_pairs={{0,8},{4,12},{8,0},{12,4},{1,9},{5,13},{9,1},{13,5},{2,10},{6,14},... | collective-permute-start | bytes 24584 | tf_op jit(solution)/shard_map/ppermute | solution.py:415
  39.1 5.8 %copy-start.2 = (f32[20,1,8192]{2,1,0:T(1,128)S(1)}, f32[20,1,8192]{2,1,0:T(1,128)}, u32[]{:S(2)}) copy-start(f32[20,1,8192]{2,1,0:T(1,128)} %param.17) | copy-start | bytes 1966084
  39.1 5.8 %copy-start.3 = (f32[20,1,8192]{2,1,0:T(1,128)S(1)}, f32[20,1,8192]{2,1,0:T(1,128)}, u32[]{:S(2)}) copy-start(f32[20,1,8192]{2,1,0:T(1,128)} %param.19) | copy-start | bytes 1966084
  40.9 4.0 %copy-start.6 = (f32[1,8192]{1,0:T(1,128)S(1)}, f32[1,8192]{1,0:T(1,128)}, u32[]{:S(2)}) copy-start(f32[1,8192]{1,0:T(1,128)} %param.16) | copy-start | bytes 98308
  40.9 4.0 %copy-start.11 = (f32[20]{0:T(128)S(1)}, f32[20]{0:T(128)}, u32[]{:S(2)}) copy-start(f32[20]{0:T(128)} %tau_ref.1) | copy-start | bytes 244
  40.9 9.9 %all-to-all-start = ((f32[4,64,128]{2,1,0:T(8,128)}), f32[4,64,128]{2,1,0:T(8,128)S(1)}, u32[]{:S(2)}, u32[]{:S(2)}) async-start(f32[4,64,128]{2,1,0:T(8,128)} %bitcast.8), calls=%async_computation | async-start | bytes 262144 | tf_op jit(solution)/shard_map/all_to_all | solution.py:484
  44.9 0.7 %copy-start.8 = (f32[20]{0:T(128)S(1)}, f32[20]{0:T(128)}, u32[]{:S(2)}) copy-start(f32[20]{0:T(128)} %cond_ref.3) | copy-start | bytes 244
  44.9 0.7 %copy-start.9 = (f32[20]{0:T(128)S(1)}, f32[20]{0:T(128)}, u32[]{:S(2)}) copy-start(f32[20]{0:T(128)} %half_ref.1) | copy-start | bytes 244
  44.9 0.7 %copy-start.10 = (f32[20]{0:T(128)S(1)}, f32[20]{0:T(128)}, u32[]{:S(2)}) copy-start(f32[20]{0:T(128)} %slope_ref.1) | copy-start | bytes 244
  45.6 5.2 %copy-start.7 = (f32[1,8192]{1,0:T(1,128)S(1)}, f32[1,8192]{1,0:T(1,128)}, u32[]{:S(2)}) copy-start(f32[1,8192]{1,0:T(1,128)} %param.18) | copy-start | bytes 98308
  50.8 0.7 %copy-start.12 = (f32[20]{0:T(128)S(1)}, f32[20]{0:T(128)}, u32[]{:S(2)}) copy-start(f32[20]{0:T(128)} %rev_ref.1) | copy-start | bytes 244

commit v3 on v2

--- a/solution.py
+++ b/solution.py
@@ -15,6 +15,7 @@
 
 VMEM = pl.BlockSpec(memory_space=pltpu.VMEM)
 SMEM = pl.BlockSpec(memory_space=pltpu.SMEM)
+HBM = pl.BlockSpec(memory_space=pltpu.HBM)
 
 
 def shape_of(*dims):
@@ -41,8 +42,20 @@
     return lax.broadcasted_iota(jnp.int32, shape, len(shape) - 2)
 
 
-def start_kernel(right_ref, damping_ref, label_ref, w0_ref, inv_ref, pack_ref, stat_ref):
+def start_kernel(
+    right_hbm, damping_hbm, label_hbm, w0_ref, inv_ref, pack_ref, stat_ref, right_ref, damping_ref, label_ref, sems
+):
     nx, ny, nz = right_ref.shape
+    parts = sems.shape[1]
+    size = nx // parts
+    copies = []
+    for part in range(parts):
+        here = pl.ds(part * size, size)
+        for k, (source, target) in enumerate(
+            ((right_hbm, right_ref), (damping_hbm, damping_ref), (label_hbm, label_ref))
+        ):
+            copies.append(pltpu.make_async_copy(source.at[here], target.at[here], sems.at[k, part]))
+            copies[-1].start()
     gz = lax.axis_index("gz")
     lane = lanes_of((ny, nz))
     packed_w = jnp.zeros((ny, nz), F32)
@@ -50,6 +63,9 @@
     energy = jnp.zeros((ny, nz), F32)
     cells = jnp.zeros((ny, nz), F32)
     for x in range(nx):
+        if x % size == 0:
+            for k in range(3):
+                copies[3 * (x // size) + k].wait()
         label = label_ref[x].astype(F32)
         right = right_ref[x]
         inv = 1.0 / (12.0 + damping_ref[x] * (1.0 + 3.0 * label))
@@ -104,9 +120,9 @@
 
 def x_faces_kernel(one, w0_ref, inv_ref, slab_ref, *refs):
     if one:
-        got_ref, w_ref, i_ref, ring_ref, up_ref, down_ref = refs
+        got_ref, w_ref, i_ref, ring_ref, first_ref, second_ref = refs
     else:
-        low_ref, high_ref, w_ref, i_ref, ring_ref, up_ref, down_ref = refs
+        low_ref, high_ref, w_ref, i_ref, ring_ref, first_ref, second_ref = refs
     nx, ny, nz = w0_ref.shape
     sub = subs_of((SUB, nz))
     lane = lanes_of((ny + SUB, nz))
@@ -138,15 +154,16 @@
             ring_ref[0, ny:] = w_halo
             ring_ref[1, :ny] = slab_ref[1]
             ring_ref[1, ny:] = i_halo
-    for k in range(3):
-        up_ref[k] = w_ref[nx - 3 + k]
-        down_ref[k] = w_ref[k]
-    for k in range(2):
-        up_ref[3 + k] = i_ref[nx - 2 + k]
-        down_ref[3 + k] = i_ref[k]
+    odd = lax.rem(lax.axis_index("gx"), 2)
     half = pltpu.roll(ring_ref[1], nz // 2, 1)
-    up_ref[5] = jnp.where(lane >= nz - 3 * PACK, ring_ref[0], half)
-    down_ref[5] = jnp.where(lane < 3 * PACK, ring_ref[0], half)
+    up = jnp.where(lane >= nz - 3 * PACK, ring_ref[0], half)
+    down = jnp.where(lane < 3 * PACK, ring_ref[0], half)
+    for face_ref, lower in ((first_ref, odd), (second_ref, 1 - odd)):
+        for k in range(3):
+            face_ref[k] = w_ref[(1 - lower) * (nx - 3) + k]
+        for k in range(2):
+            face_ref[3 + k] = i_ref[(1 - lower) * (nx - 2) + k]
+        face_ref[5] = jnp.where(lower == 1, down, up)
 
 
 def around(v):
@@ -155,7 +172,7 @@
 
 
 def stencil_kernel(
-    w_ref, i_ref, ring_ref, low_ref, high_ref, stat_ref,
+    w_ref, i_ref, ring_ref, first_ref, second_ref, stat_ref,
     w1_ref, w2_ref, f0_ref, f1_ref, f2_ref, total_ref,
     a_ref, b_ref, sw_ref,
 ):
@@ -168,21 +185,29 @@
     lane_first = lane == 0
     lane_last = lane == nz - 1
 
+    odd = lax.rem(lax.axis_index("gx"), 2) == 1
+
+    def low(k):
+        return jnp.where(odd, first_ref[k], second_ref[k])
+
+    def high(k):
+        return jnp.where(odd, second_ref[k], first_ref[k])
+
     def w0_plane(x):
         if x < 0:
-            return low_ref[3 + x]
+            return low(3 + x)
         if x >= nx:
-            return high_ref[x - nx]
+            return high(x - nx)
         return w_ref[x]
 
     def inv_plane(x):
         if x < 0:
-            return low_ref[5 + x]
+            return low(5 + x)
         if x >= nx:
-            return high_ref[3 + x - nx]
+            return high(3 + x - nx)
         return i_ref[x]
 
-    lo5, hi5 = low_ref[5], high_ref[5]
+    lo5, hi5 = low(5), high(5)
     slab_w = jnp.where(lane < 3 * PACK, hi5, 0.0) + jnp.where(lane >= nz - 3 * PACK, lo5, 0.0)
     lo5, hi5 = pltpu.roll(lo5, nz // 2, 1), pltpu.roll(hi5, nz // 2, 1)
     slab_i = jnp.where(lane < 2 * PACK, hi5, 0.0) + jnp.where(lane >= nz - 2 * PACK, lo5, 0.0)
@@ -320,7 +345,7 @@
 
 
 def combine_kernel(
-    slot_rows, total_ref, w0_ref, w1_ref, w2_ref, f0_ref, f1_ref, f2_ref, plan_ref, x_ref, out_ref, buf_ref
+    slot_rows, total_ref, w0_ref, w1_ref, w2_ref, f0_ref, f1_ref, f2_ref, plan_ref, x_ref, *out_refs
 ):
     rows = w0_ref.shape[0]
     lane = lanes_of((rows, LANES))
@@ -352,13 +377,17 @@
     turned = pltpu.roll(slots, inner, 1)
     above = pltpu.roll(turned, 1, 0)
     moved = jnp.where(lane[: slot_rows + SUB] >= inner, turned, above)
+    *out_refs, buf_ref = out_refs
     buf_ref[...] = jnp.zeros_like(buf_ref)
     buf_ref[pl.ds(offset // LANES, slot_rows + SUB), :] = moved
-    out_ref[...] = buf_ref[: out_ref.shape[0]]
+    for k, out_ref in enumerate(out_refs):
+        size = out_ref.shape[0]
+        out_ref[...] = buf_ref[pl.ds(pl.multiple_of((gx ^ k) * size, SUB), size), :]
 
 
 def membrane_kernel(
-    half_ref, slope_ref, tau_ref, cond_ref, v_ref, gates_ref, cot_ref, base_ref, sum_ref, factor_ref
+    half_ref, slope_ref, tau_ref, cond_ref, rev_ref, v_ref, gates_ref, cot_ref,
+    base_ref, sum_ref, factor_ref, coef_ref,
 ):
     n_states = gates_ref.shape[0]
     v = v_ref[...]
@@ -379,6 +408,8 @@
         decay_slope = decay * rate * rate * ((tau_base / TIME_STEP) * bell * (-2.0 * scaled))
         change = (steady_slope * (1.0 - decay) + (gate - steady) * decay_slope) * inv_slope
         base_ref[g] = cot * decay
+        coef_ref[0, pl.ds(g, 1)] = jnp.full((1, LANES), TIME_STEP * cond_ref[g])
+        coef_ref[1, pl.ds(g, 1)] = jnp.full((1, LANES), rev_ref[g])
         return total + cot * change, current + cond_ref[g] * gate
 
     zero = jnp.zeros((rows, LANES), F32)
@@ -387,18 +418,16 @@
     factor_ref[...] = 1.0 - TIME_STEP * current
 
 
-def finish_kernel(
-    cond_ref, rev_ref, landed_ref, vcot_ref, v_ref, sum_ref, factor_ref, base_ref, volt_ref, gate_ref
-):
-    landed = landed_ref[0]
-    for k in range(1, landed_ref.shape[0]):
-        landed = landed + landed_ref[k]
+def finish_kernel(coef_ref, vcot_ref, v_ref, sum_ref, factor_ref, base_ref, *refs):
+    *landed_refs, volt_ref, gate_ref = refs
+    landed = landed_refs[0][...]
+    for ref in landed_refs[1:]:
+        landed = landed + ref[...]
     cot = vcot_ref[...] + landed
     v = v_ref[...]
     volt_ref[...] = cot * factor_ref[...] + sum_ref[...]
-    half = TIME_STEP * cot
     for g in range(base_ref.shape[0]):
-        gate_ref[g] = base_ref[g] - (cond_ref[g] * half) * (v - rev_ref[g])
+        gate_ref[g] = base_ref[g] - (coef_ref[0, g : g + 1] * cot) * (v - coef_ref[1, g : g + 1])
 
 
 def both_ways(up, down, axis):
@@ -406,6 +435,14 @@
     low = lax.ppermute(up, axis, [(i, i + 1) for i in range(count - 1)])
     high = lax.ppermute(down, axis, [(i + 1, i) for i in range(count - 1)])
     return low, high
+
+
+def pair_swaps(first, second, axis):
+    count = lax.axis_size(axis)
+    even = [(i, i ^ 1) for i in range(count)]
+    between = [(i, i + 1) for i in range(1, count - 1, 2)]
+    between = between + [(j, i) for i, j in between]
+    return lax.ppermute(first, axis, even), lax.ppermute(second, axis, between)
 
 
 def reduce_over(value, axis):
@@ -434,17 +471,25 @@
     states = lambda a: a.reshape(n_states, block_rows, LANES)
 
     w0, inv, packed, stat = call(
-        start_kernel, (block, block, shape_of(2, ny, nz), shape_of(2, SUB, nz)), 3
-    )(potential_cot, damping, tissue_label)
+        start_kernel, (block, block, shape_of(2, ny, nz), shape_of(2, SUB, nz)), 3,
+        specs=[HBM] * 3,
+        scratch=[
+            pltpu.VMEM((nx, ny, nz), F32), pltpu.VMEM((nx, ny, nz), F32), pltpu.VMEM((nx, ny, nz), jnp.int32),
+            pltpu.SemaphoreType.DMA((3, 4)),
+        ],
+    )(*[pltpu.with_memory_space_constraint(a, pltpu.HBM) for a in (potential_cot, damping, tissue_label)])
 
     got = lax.ppermute(packed, "gz", [(0, 1), (1, 0)])
-    base, total_change, factor = call(
+    base, total_change, factor, coefs = call(
         membrane_kernel,
-        (shape_of(n_states, block_rows, LANES), shape_of(block_rows, LANES), shape_of(block_rows, LANES)),
-        7,
-        specs=[SMEM] * 4 + [VMEM] * 3,
+        (
+            shape_of(n_states, block_rows, LANES), shape_of(block_rows, LANES), shape_of(block_rows, LANES),
+            shape_of(2, n_states, LANES),
+        ),
+        8,
+        specs=[SMEM] * 5 + [VMEM] * 3,
         cost=6_000_000,
-    )(half_voltage, gate_slope, tau_base, conductance, cells(voltage), states(gates), states(gates_cot))
+    )(half_voltage, gate_slope, tau_base, conductance, reversal, cells(voltage), states(gates), states(gates_cot))
     plan = call(plan_kernel, jax.ShapeDtypeStruct((rows, LANES), jnp.int32), 1, cost=6_000_000)(flat(tissue_label))
 
     face = shape_of(nx + 1, SUB, nz)
@@ -457,10 +502,10 @@
     else:
         slab, up, down = call(y_faces_kernel, (slab_shape, face, face), 4)(w0, inv, packed, got)
         halo = both_ways(up, down, "gy")
-    wide, wide_inv, ring_slab, up, down = call(
+    wide, wide_inv, ring_slab, first, second = call(
         functools.partial(x_faces_kernel, n_gy == 2), x_shapes, 3 + len(halo)
     )(w0, inv, slab, *halo)
-    low, high = both_ways(up, down, "gx")
+    first, second = pair_swaps(first, second, "gx")
 
     w1, w2, f0, f1, f2, sums = call(
         stencil_kernel,
@@ -471,24 +516,25 @@
             pltpu.VMEM((nx + 2, ring, nz), F32),
             pltpu.VMEM((ring, 2 * nz), F32),
         ],
-    )(wide, wide_inv, ring_slab, low, high, stat)
+    )(wide, wide_inv, ring_slab, first, second, stat)
     for axis in ("gz", "gy", "gx"):
         sums = reduce_over(sums, axis)
 
-    solution, placed = call(
+    solution, *blocks = call(
         functools.partial(combine_kernel, slot_rows),
-        (shape_of(rows, LANES), shape_of(n_gx * block_rows, LANES)),
+        (shape_of(rows, LANES),) + (shape_of(block_rows, LANES),) * n_gx,
         8,
         scratch=[pltpu.VMEM((n_gx * block_rows + slot_rows + SUB, LANES), F32)],
     )(sums, flat(w0), flat(w1), flat(w2), flat(f0), flat(f1), flat(f2), plan)
-    landed = lax.all_to_all(placed.reshape(n_gx, block_rows, LANES), "gx", 0, 0, tiled=True)
+    landed = blocks[:1] + [
+        lax.ppermute(blocks[k], "gx", [(i, i ^ k) for i in range(n_gx)]) for k in range(1, n_gx)
+    ]
 
     volt_grad, gate_grad = call(
         finish_kernel,
         (shape_of(block_rows, LANES), shape_of(n_states, block_rows, LANES)),
-        8,
-        specs=[SMEM] * 2 + [VMEM] * 6,
-    )(conductance, reversal, landed, cells(voltage_cot), cells(voltage), total_change, factor, base)
+        6 + n_gx,
+    )(coefs, cells(voltage_cot), cells(voltage), total_change, factor, base, *landed)
     return solution.reshape(nx, ny, nz), volt_grad.reshape(voltage.shape), gate_grad.reshape(gates.shape)
 
 

time: 53.4 us -> 46.6 us (0.87)
  waiting for transfers between devices: 17.8 us -> 11.5 us
  local copies, waits for them, and re-layouts: 4.16 us -> 0.68 us
  starting transfers between devices: 18.2 us -> 20.7 us
  Pallas kernels: 12.1 us -> 12.7 us
    ppermute x4, starting transfers between devices: 5.72 us -> 10.3 us  [reduce_over(): lax.ppermute(value, axis, [(i, i ^ step) for i in range(count)])]
    all_to_all x1 -> x0, starting transfers between devices: 3.99 us -> none  [local(): lax.all_to_all(placed.reshape(n_gx, block_rows, LANES), 'gx', 0, 0, tiled...]
    unnamed x26 -> x20, local copies, waits for them, and re-layouts: 4.16 us -> 0.68 us
    all_to_all x1 -> x0, waiting for transfers between devices: 3.32 us -> none  [local(): lax.all_to_all(placed.reshape(n_gx, block_rows, LANES), 'gx', 0, 0, tiled...]
    ppermute x2 -> x5, waiting for transfers between devices: 5.47 us -> 3.48 us  [the longest x1 2.33 us: pair_swaps(): lax.ppermute(first, axis, even)]
    ppermute x2 -> x5, starting transfers between devices: 5.08 us -> 6.98 us  [the longest x3 4.39 us: local(): lax.ppermute(blocks[k], 'gx', [(i, i ^ k) for i in range(n_gx)])]
    pallas_call x1, Pallas kernels: 0.21 us -> 1.47 us  [local(): call(start_kernel, (block, block, shape_of(2, ny, nz), shape_of(2, SUB, n...]
    ppermute x4, waiting for transfers between devices: 5.63 us -> 4.64 us  [reduce_over(): lax.ppermute(value, axis, [(i, i ^ step) for i in range(count)])]
  transfers between devices with their start and end apart: 9 -> 11, of which waited for: 9 -> 7; matrix products, arithmetic and copies ran while one was open for 0% -> 0% of each run, Pallas kernels for 7% -> 8%
where the time goes in v3:
time: 46.6 us; the launch traced here: 46.4 us
  starting transfers between devices  20.7 us (44%)
  Pallas kernels  12.7 us (27%)
  waiting for transfers between devices  11.5 us (25%)
  between operations  0.79 us (2%)
  local copies, waits for them, and re-layouts  0.68 us (1%)
    ppermute x4, starting transfers between devices, reduce_over(): lax.ppermute(value, axis, [(i, i ^ step) for i in range(count)])  10.3 us
    pallas_call x1, Pallas kernels, local(): call(stencil_kernel, (block,) * 5 + (shape_of(16, nz),), 6, scratch=[pltp...  4.77 us
    ppermute x4, waiting for transfers between devices, reduce_over(): lax.ppermute(value, axis, [(i, i ^ step) for i in range(count)])  4.64 us
    ppermute x3, starting transfers between devices, local(): lax.ppermute(blocks[k], 'gx', [(i, i ^ k) for i in range(n_gx)])  4.39 us
    ppermute x1, starting transfers between devices, local(): halo = (lax.ppermute(mine, 'gy', [(0, 1), (1, 0)]),)  2.9 us
    ppermute x1, waiting for transfers between devices, local(): halo = (lax.ppermute(mine, 'gy', [(0, 1), (1, 0)]),)  2.51 us
    ppermute x1, waiting for transfers between devices, pair_swaps(): lax.ppermute(first, axis, even)  2.33 us
    ppermute x1, starting transfers between devices, pair_swaps(): lax.ppermute(first, axis, even)  1.94 us
  transfers between devices with their start and end apart: 11, of which 7 were waited for; matrix products, arithmetic and copies ran while one was open for 0% of the time, Pallas kernels for 8%

profile of v3, /device:TPU:0, one launch (start us, length us, event | category | flops | bytes accessed | tf_op | source)
XLA Modules:
  0.0 46.4 jit_solution(5122169458041052510)
XLA Ops:
  0.6 1.5 %shard_map.139 = (f32[16,32,128]{2,1,0:T(8,128)S(1)}, f32[16,32,128]{2,1,0:T(8,128)S(1)}, f32[2,32,128]{2,1,0:T(8,128)S(1)}, f32[2,8,128]{2,1,0:T(8,128)S(1)}) custom-call(f32[16,32,128]{2,1,0:T(8,128)} %right_hbm.1, f32[16,32,128]{2,1,0:T(8,128)} %damping_hbm.1, s32[16,32,128]{2,1,0:T(8,128)} %label_hbm.1), custom_call_target="tpu_custom_call" | custom-call | flops 2000000 | bytes 2000000 | tf_op jit(solution)/shard_map/pallas_call | solution.py:473
  2.1 0.5 %collective-permute-start = (f32[2,32,128]{2,1,0:T(8,128)S(1)}, f32[2,32,128]{2,1,0:T(8,128)S(1)}, u32[]{:S(2)}, u32[]{:S(2)}) collective-permute-start(f32[2,32,128]{2,1,0:T(8,128)S(1)} %get-tuple-element.33.own_ref), channel_id=1, source_target_pairs={{0,1},{1,0},{2,3},{3,2},{4,5},{5,4},{6,7},{7,6},{8,9},{9,8},{10,11... | collective-permute-start | bytes 98312 | tf_op jit(solution)/shard_map/ppermute | solution.py:482
  2.6 0.9 %collective-permute-done.got_ref = f32[2,32,128]{2,1,0:T(8,128)S(1)} collective-permute-done((f32[2,32,128]{2,1,0:T(8,128)S(1)}, f32[2,32,128]{2,1,0:T(8,128)S(1)}, u32[]{:S(2)}, u32[]{:S(2)}) %collective-permute-start) | collective-permute-done | bytes 32800 | tf_op jit(solution)/shard_map/ppermute | solution.py:482
  3.5 2.9 %collective-permute-start.1 = (f32[17,8,128]{2,1,0:T(8,128)S(1)}, f32[17,8,128]{2,1,0:T(8,128)S(1)}, u32[]{:S(2)}, u32[]{:S(2)}) collective-permute-start(f32[17,8,128]{2,1,0:T(8,128)S(1)} %get-tuple-element.35), channel_id=1, source_target_pairs={{0,2},{2,0},{1,3},{3,1},{4,6},{6,4},{5,7},{7,5},{8,10},{10,8},{9,1... | collective-permute-start | bytes 208904 | tf_op jit(solution)/shard_map/ppermute | solution.py:501
  6.4 2.5 %collective-permute-done.1.refs_0_ = f32[17,8,128]{2,1,0:T(8,128)S(1)} collective-permute-done((f32[17,8,128]{2,1,0:T(8,128)S(1)}, f32[17,8,128]{2,1,0:T(8,128)S(1)}, u32[]{:S(2)}, u32[]{:S(2)}) %collective-permute-start.1) | collective-permute-done | bytes 69664 | tf_op jit(solution)/shard_map/ppermute | solution.py:501
  9.0 1.9 %collective-permute-start.2 = (f32[6,40,128]{2,1,0:T(8,128)S(1)}, f32[6,40,128]{2,1,0:T(8,128)S(1)}, u32[]{:S(2)}, u32[]{:S(2)}) collective-permute-start(f32[6,40,128]{2,1,0:T(8,128)S(1)} %get-tuple-element.39), channel_id=1, source_target_pairs={{0,4},{4,0},{8,12},{12,8},{1,5},{5,1},{9,13},{13,9},{2,6},{6,2},{1... | collective-permute-start | bytes 368648 | tf_op jit(solution)/shard_map/ppermute | solution.py:445
  11.0 0.7 %collective-permute-start.3 = (f32[6,40,128]{2,1,0:T(8,128)S(1)}, f32[6,40,128]{2,1,0:T(8,128)S(1)}, u32[]{:S(2)}, u32[]{:S(2)}) collective-permute-start(f32[6,40,128]{2,1,0:T(8,128)S(1)} %get-tuple-element.40), channel_id=1, source_target_pairs={{4,8},{8,4},{5,9},{9,5},{6,10},{10,6},{7,11},{11,7},{20,24},{24,20... | collective-permute-start | bytes 368648 | tf_op jit(solution)/shard_map/ppermute | solution.py:445
  11.6 2.3 %collective-permute-done.2.first_ref = f32[6,40,128]{2,1,0:T(8,128)S(1)} collective-permute-done((f32[6,40,128]{2,1,0:T(8,128)S(1)}, f32[6,40,128]{2,1,0:T(8,128)S(1)}, u32[]{:S(2)}, u32[]{:S(2)}) %collective-permute-start.2) | collective-permute-done | bytes 122912 | tf_op jit(solution)/shard_map/ppermute | solution.py:445
  14.0 4.8 %shard_map.142 = (f32[16,32,128]{2,1,0:T(8,128)S(1)}, f32[16,32,128]{2,1,0:T(8,128)S(1)}, f32[16,32,128]{2,1,0:T(8,128)S(1)}, f32[16,32,128]{2,1,0:T(8,128)S(1)}...) custom-call(f32[16,40,128]{2,1,0:T(8,128)S(1)} %get-tuple-element.36.w_ref, ...), custom_call_target="tpu_custom_call" | custom-call | flops 2000000 | bytes 2000000 | tf_op jit(solution)/shard_map/pallas_call | solution.py:510
  18.8 1.2 %collective-permute-done.4 = f32[16,128]{1,0:T(8,128)S(1)} collective-permute-done((f32[16,128]{1,0:T(8,128)S(1)}, f32[16,128]{1,0:T(8,128)S(1)}, u32[]{:S(2)}, u32[]{:S(2)}) %collective-permute-start.4) | collective-permute-done | bytes 8224 | tf_op jit(solution)/shard_map/ppermute | solution.py:452
  20.0 1.8 %collective-permute-start.5 = (f32[16,128]{1,0:T(8,128)S(1)}, f32[16,128]{1,0:T(8,128)S(1)}, u32[]{:S(2)}, u32[]{:S(2)}) collective-permute-start(f32[16,128]{1,0:T(8,128)S(1)} %add.12), channel_id=1, source_target_pairs={{0,2},{2,0},{1,3},{3,1},{4,6},{6,4},{5,7},{7,5},{8,10},{10,8},{9,1... | collective-permute-start | bytes 24584 | tf_op jit(solution)/shard_map/ppermute | solution.py:452
  21.8 1.8 %collective-permute-done.5 = f32[16,128]{1,0:T(8,128)S(1)} collective-permute-done((f32[16,128]{1,0:T(8,128)S(1)}, f32[16,128]{1,0:T(8,128)S(1)}, u32[]{:S(2)}, u32[]{:S(2)}) %collective-permute-start.5) | collective-permute-done | bytes 8224 | tf_op jit(solution)/shard_map/ppermute | solution.py:452
  23.6 4.9 %collective-permute-start.6 = (f32[16,128]{1,0:T(8,128)S(1)}, f32[16,128]{1,0:T(8,128)S(1)}, u32[]{:S(2)}, u32[]{:S(2)}) collective-permute-start(f32[16,128]{1,0:T(8,128)S(1)} %add.13), channel_id=1, source_target_pairs={{0,4},{4,0},{8,12},{12,8},{1,5},{5,1},{9,13},{13,9},{2,6},{6,2},{1... | collective-permute-start | bytes 24584 | tf_op jit(solution)/shard_map/ppermute | solution.py:452
  28.5 1.6 %collective-permute-done.6 = f32[16,128]{1,0:T(8,128)S(1)} collective-permute-done((f32[16,128]{1,0:T(8,128)S(1)}, f32[16,128]{1,0:T(8,128)S(1)}, u32[]{:S(2)}, u32[]{:S(2)}) %collective-permute-start.6) | collective-permute-done | bytes 8224 | tf_op jit(solution)/shard_map/ppermute | solution.py:452
  30.2 3.6 %collective-permute-start.7 = (f32[16,128]{1,0:T(8,128)S(1)}, f32[16,128]{1,0:T(8,128)S(1)}, u32[]{:S(2)}, u32[]{:S(2)}) collective-permute-start(f32[16,128]{1,0:T(8,128)S(1)} %add.14), channel_id=1, source_target_pairs={{0,8},{4,12},{8,0},{12,4},{1,9},{5,13},{9,1},{13,5},{2,10},{6,14},... | collective-permute-start | bytes 24584 | tf_op jit(solution)/shard_map/ppermute | solution.py:452
  33.7 1.7 %shard_map.143.plan_ref = s32[512,128]{1,0:T(8,128)S(1)} custom-call(s32[512,128]{1,0:T(8,128)S(1)} %bitcast.15), custom_call_target="tpu_custom_call" | custom-call | flops 6000000 | bytes 6000000 | tf_op jit(solution)/shard_map/pallas_call | solution.py:493
  35.5 1.8 %shard_map.144 = (f32[512,128]{1,0:T(8,128)}, f32[64,128]{1,0:T(8,128)S(1)}, f32[64,128]{1,0:T(8,128)S(1)}, f32[64,128]{1,0:T(8,128)S(1)}, f32[64,128]{1,0:T(8,128)S(1)}) custom-call(f32[16,128]{1,0:T(8,128)S(1)} %add.15.total_ref, f32[512,128]{1,0:T(8,128)S(1)} %bitcast.14, f32[512,128]{1,0:T(8,128)S(1)} %bitcast.18, f32[512,128]{1,0:T(8,128)S(1)} %bitcast.19, ...), custom_call_target="tpu_custom_call" | custom-call | flops 2000000 | bytes 2000000 | tf_op jit(solution)/shard_map/pallas_call | solution.py:523
  37.3 2.1 %collective-permute-start.10 = (f32[64,128]{1,0:T(8,128)S(1)}, f32[64,128]{1,0:T(8,128)S(1)}, u32[]{:S(2)}, u32[]{:S(2)}) collective-permute-start(f32[64,128]{1,0:T(8,128)S(1)} %get-tuple-element.56), channel_id=1, source_target_pairs={{0,12},{4,8},{8,4},{12,0},{1,13},{5,9},{9,5},{13,1},{2,14},{6,10},... | collective-permute-start | bytes 98312 | tf_op jit(solution)/shard_map/ppermute | solution.py:530
  39.4 1.2 %collective-permute-start.8 = (f32[64,128]{1,0:T(8,128)S(1)}, f32[64,128]{1,0:T(8,128)S(1)}, u32[]{:S(2)}, u32[]{:S(2)}) collective-permute-start(f32[64,128]{1,0:T(8,128)S(1)} %get-tuple-element.54), channel_id=1, source_target_pairs={{0,4},{4,0},{8,12},{12,8},{1,5},{5,1},{9,13},{13,9},{2,6},{6,2},{1... | collective-permute-start | bytes 98312 | tf_op jit(solution)/shard_map/ppermute | solution.py:530
  40.6 1.0 %collective-permute-start.9 = (f32[64,128]{1,0:T(8,128)S(1)}, f32[64,128]{1,0:T(8,128)S(1)}, u32[]{:S(2)}, u32[]{:S(2)}) collective-permute-start(f32[64,128]{1,0:T(8,128)S(1)} %get-tuple-element.55), channel_id=1, source_target_pairs={{0,8},{4,12},{8,0},{12,4},{1,9},{5,13},{9,1},{13,5},{2,10},{6,14},... | collective-permute-start | bytes 98312 | tf_op jit(solution)/shard_map/ppermute | solution.py:530
  41.7 0.6 %copy-done.5 = f32[20]{0:T(128)S(1)} copy-done((f32[20]{0:T(128)S(1)}, f32[20]{0:T(128)}, u32[]{:S(2)}) %copy-start.5) | copy-done | bytes 104
  42.4 1.9 %shard_map.145 = (f32[20,64,128]{2,1,0:T(8,128)S(1)}, f32[64,128]{1,0:T(8,128)S(1)}, f32[64,128]{1,0:T(8,128)S(1)}, f32[2,20,128]{2,1,0:T(8,128)S(1)}) custom-call(f32[20]{0:T(128)S(1)} %copy-done.5, f32[20]{0:T(128)S(1)} %copy-done.6, f32[20]{0:T(128)S(1)} %copy-done.7, f32[20]{0:T(128)S(1)} %copy-done.8, f32[20]{0:T(128)S(1)} %copy-done.9, ...), custom_call_target="tpu_custom_call" | custom-call | flops 6000000 | bytes 6000000 | tf_op jit(solution)/shard_map/pallas_call | solution.py:483
  44.3 1.1 %collective-permute-done.9.refs_2_ = f32[64,128]{1,0:T(8,128)S(1)} collective-permute-done((f32[64,128]{1,0:T(8,128)S(1)}, f32[64,128]{1,0:T(8,128)S(1)}, u32[]{:S(2)}, u32[]{:S(2)}) %collective-permute-start.9) | collective-permute-done | bytes 32800 | tf_op jit(solution)/shard_map/ppermute | solution.py:530
  45.5 0.9 %shard_map.146 = (f32[64,128]{1,0:T(8,128)}, f32[20,64,128]{2,1,0:T(8,128)}) custom-call(f32[2,20,128]{2,1,0:T(8,128)S(1)} %get-tuple-element.49.coef_ref, f32[64,128]{1,0:T(8,128)S(1)} %bitcast.25, f32[64,128]{1,0:T(8,128)S(1)} %bitcast.24, f32[64,128]{1,0:T(8,128)S(1)} %get-tuple-element.50.sum_ref, f32[64,128]{1,0:T(8,128)S(1)} %get-tuple-element.51.factor_ref, ...), custom_call_target="tpu_custom_call" | custom-call | flops 2000000 | bytes 2000000 | tf_op jit(solution)/shard_map/pallas_call | solution.py:533
  (30 shorter events, 0.3 us)
Async XLA Ops:
  2.1 1.4 %collective-permute-start = (f32[2,32,128]{2,1,0:T(8,128)S(1)}, f32[2,32,128]{2,1,0:T(8,128)S(1)}, u32[]{:S(2)}, u32[]{:S(2)}) collective-permute-start(f32[2,32,128]{2,1,0:T(8,128)S(1)} %get-tuple-element.33.own_ref), channel_id=1, source_target_pairs={{0,1},{1,0},{2,3},{3,2},{4,5},{5,4},{6,7},{7,6},{8,9},{9,8},{10,11... | collective-permute-start | bytes 98312 | tf_op jit(solution)/shard_map/ppermute | solution.py:482
  3.5 5.4 %collective-permute-start.1 = (f32[17,8,128]{2,1,0:T(8,128)S(1)}, f32[17,8,128]{2,1,0:T(8,128)S(1)}, u32[]{:S(2)}, u32[]{:S(2)}) collective-permute-start(f32[17,8,128]{2,1,0:T(8,128)S(1)} %get-tuple-element.35), channel_id=1, source_target_pairs={{0,2},{2,0},{1,3},{3,1},{4,6},{6,4},{5,7},{7,5},{8,10},{10,8},{9,1... | collective-permute-start | bytes 208904 | tf_op jit(solution)/shard_map/ppermute | solution.py:501
  9.0 4.9 %collective-permute-start.2 = (f32[6,40,128]{2,1,0:T(8,128)S(1)}, f32[6,40,128]{2,1,0:T(8,128)S(1)}, u32[]{:S(2)}, u32[]{:S(2)}) collective-permute-start(f32[6,40,128]{2,1,0:T(8,128)S(1)} %get-tuple-element.39), channel_id=1, source_target_pairs={{0,4},{4,0},{8,12},{12,8},{1,5},{5,1},{9,13},{13,9},{2,6},{6,2},{1... | collective-permute-start | bytes 368648 | tf_op jit(solution)/shard_map/ppermute | solution.py:445
  11.0 3.0 %collective-permute-start.3 = (f32[6,40,128]{2,1,0:T(8,128)S(1)}, f32[6,40,128]{2,1,0:T(8,128)S(1)}, u32[]{:S(2)}, u32[]{:S(2)}) collective-permute-start(f32[6,40,128]{2,1,0:T(8,128)S(1)} %get-tuple-element.40), channel_id=1, source_target_pairs={{4,8},{8,4},{5,9},{9,5},{6,10},{10,6},{7,11},{11,7},{20,24},{24,20... | collective-permute-start | bytes 368648 | tf_op jit(solution)/shard_map/ppermute | solution.py:445
  14.0 19.8 %copy-start = (s32[16,32,128]{2,1,0:T(8,128)S(1)}, s32[16,32,128]{2,1,0:T(8,128)}, u32[]{:S(2)}) copy-start(s32[16,32,128]{2,1,0:T(8,128)} %label_hbm.1) | copy-start | bytes 786436
  18.7 1.2 %collective-permute-start.4 = (f32[16,128]{1,0:T(8,128)S(1)}, f32[16,128]{1,0:T(8,128)S(1)}, u32[]{:S(2)}, u32[]{:S(2)}) collective-permute-start(f32[16,128]{1,0:T(8,128)S(1)} %get-tuple-element.42), channel_id=1, source_target_pairs={{0,1},{1,0},{2,3},{3,2},{4,5},{5,4},{6,7},{7,6},{8,9},{9,8},{10,11... | collective-permute-start | bytes 24584 | tf_op jit(solution)/shard_map/ppermute | solution.py:452
  20.0 3.7 %collective-permute-start.5 = (f32[16,128]{1,0:T(8,128)S(1)}, f32[16,128]{1,0:T(8,128)S(1)}, u32[]{:S(2)}, u32[]{:S(2)}) collective-permute-start(f32[16,128]{1,0:T(8,128)S(1)} %add.12), channel_id=1, source_target_pairs={{0,2},{2,0},{1,3},{3,1},{4,6},{6,4},{5,7},{7,5},{8,10},{10,8},{9,1... | collective-permute-start | bytes 24584 | tf_op jit(solution)/shard_map/ppermute | solution.py:452
  23.6 6.5 %collective-permute-start.6 = (f32[16,128]{1,0:T(8,128)S(1)}, f32[16,128]{1,0:T(8,128)S(1)}, u32[]{:S(2)}, u32[]{:S(2)}) collective-permute-start(f32[16,128]{1,0:T(8,128)S(1)} %add.13), channel_id=1, source_target_pairs={{0,4},{4,0},{8,12},{12,8},{1,5},{5,1},{9,13},{13,9},{2,6},{6,2},{1... | collective-permute-start | bytes 24584 | tf_op jit(solution)/shard_map/ppermute | solution.py:452
  30.2 5.3 %collective-permute-start.7 = (f32[16,128]{1,0:T(8,128)S(1)}, f32[16,128]{1,0:T(8,128)S(1)}, u32[]{:S(2)}, u32[]{:S(2)}) collective-permute-start(f32[16,128]{1,0:T(8,128)S(1)} %add.14), channel_id=1, source_target_pairs={{0,8},{4,12},{8,0},{12,4},{1,9},{5,13},{9,1},{13,5},{2,10},{6,14},... | collective-permute-start | bytes 24584 | tf_op jit(solution)/shard_map/ppermute | solution.py:452
  35.5 6.2 %copy-start.1 = (f32[20,1,8192]{2,1,0:T(1,128)S(1)}, f32[20,1,8192]{2,1,0:T(1,128)}, u32[]{:S(2)}) copy-start(f32[20,1,8192]{2,1,0:T(1,128)} %param.17) | copy-start | bytes 1966084
  35.5 6.2 %copy-start.2 = (f32[20,1,8192]{2,1,0:T(1,128)S(1)}, f32[20,1,8192]{2,1,0:T(1,128)}, u32[]{:S(2)}) copy-start(f32[20,1,8192]{2,1,0:T(1,128)} %param.19) | copy-start | bytes 1966084
  35.5 6.2 %copy-start.3 = (f32[1,8192]{1,0:T(1,128)S(1)}, f32[1,8192]{1,0:T(1,128)}, u32[]{:S(2)}) copy-start(f32[1,8192]{1,0:T(1,128)} %param.16) | copy-start | bytes 98308
  35.5 6.2 %copy-start.8 = (f32[20]{0:T(128)S(1)}, f32[20]{0:T(128)}, u32[]{:S(2)}) copy-start(f32[20]{0:T(128)} %cond_ref.1) | copy-start | bytes 244
  35.5 6.2 %copy-start.9 = (f32[20]{0:T(128)S(1)}, f32[20]{0:T(128)}, u32[]{:S(2)}) copy-start(f32[20]{0:T(128)} %rev_ref.1) | copy-start | bytes 244
  37.3 7.0 %collective-permute-start.10 = (f32[64,128]{1,0:T(8,128)S(1)}, f32[64,128]{1,0:T(8,128)S(1)}, u32[]{:S(2)}, u32[]{:S(2)}) collective-permute-start(f32[64,128]{1,0:T(8,128)S(1)} %get-tuple-element.56), channel_id=1, source_target_pairs={{0,12},{4,8},{8,4},{12,0},{1,13},{5,9},{9,5},{13,1},{2,14},{6,10},... | collective-permute-start | bytes 98312 | tf_op jit(solution)/shard_map/ppermute | solution.py:530
  39.4 4.9 %collective-permute-start.8 = (f32[64,128]{1,0:T(8,128)S(1)}, f32[64,128]{1,0:T(8,128)S(1)}, u32[]{:S(2)}, u32[]{:S(2)}) collective-permute-start(f32[64,128]{1,0:T(8,128)S(1)} %get-tuple-element.54), channel_id=1, source_target_pairs={{0,4},{4,0},{8,12},{12,8},{1,5},{5,1},{9,13},{13,9},{2,6},{6,2},{1... | collective-permute-start | bytes 98312 | tf_op jit(solution)/shard_map/ppermute | solution.py:530
  40.6 4.8 %collective-permute-start.9 = (f32[64,128]{1,0:T(8,128)S(1)}, f32[64,128]{1,0:T(8,128)S(1)}, u32[]{:S(2)}, u32[]{:S(2)}) collective-permute-start(f32[64,128]{1,0:T(8,128)S(1)} %get-tuple-element.55), channel_id=1, source_target_pairs={{0,8},{4,12},{8,0},{12,4},{1,9},{5,13},{9,1},{13,5},{2,10},{6,14},... | collective-permute-start | bytes 98312 | tf_op jit(solution)/shard_map/ppermute | solution.py:530
  41.7 0.7 %copy-start.5 = (f32[20]{0:T(128)S(1)}, f32[20]{0:T(128)}, u32[]{:S(2)}) copy-start(f32[20]{0:T(128)} %half_ref.1) | copy-start | bytes 244
  41.7 0.7 %copy-start.6 = (f32[20]{0:T(128)S(1)}, f32[20]{0:T(128)}, u32[]{:S(2)}) copy-start(f32[20]{0:T(128)} %slope_ref.1) | copy-start | bytes 244
  41.7 0.7 %copy-start.7 = (f32[20]{0:T(128)S(1)}, f32[20]{0:T(128)}, u32[]{:S(2)}) copy-start(f32[20]{0:T(128)} %tau_ref.1) | copy-start | bytes 244
  42.4 3.1 %copy-start.4 = (f32[1,8192]{1,0:T(1,128)S(1)}, f32[1,8192]{1,0:T(1,128)}, u32[]{:S(2)}) copy-start(f32[1,8192]{1,0:T(1,128)} %param.18) | copy-start | bytes 98308

commit v4 on v3

--- a/solution.py
+++ b/solution.py
@@ -22,16 +22,20 @@
     return jax.ShapeDtypeStruct(dims, F32)
 
 
-def call(kernel, out_shape, n_in, specs=None, scratch=(), cost=2_000_000, limit=32):
+def call(kernel, out_shape, n_in, specs=None, outs=None, scratch=(), cost=2_000_000, limit=32):
     return pl.pallas_call(
         kernel,
         out_shape=out_shape,
         in_specs=specs if specs is not None else [VMEM] * n_in,
-        out_specs=jax.tree.map(lambda _: VMEM, out_shape),
+        out_specs=outs if outs is not None else jax.tree.map(lambda _: VMEM, out_shape),
         scratch_shapes=list(scratch),
         compiler_params=pltpu.CompilerParams(vmem_limit_bytes=limit * 1024 * 1024),
         cost_estimate=pl.CostEstimate(flops=cost, bytes_accessed=cost, transcendentals=0),
     )
+
+
+def in_hbm(array):
+    return pltpu.with_memory_space_constraint(array, pltpu.HBM)
 
 
 def lanes_of(shape):
@@ -120,71 +124,50 @@
 
 def x_faces_kernel(one, w0_ref, inv_ref, slab_ref, *refs):
     if one:
-        got_ref, w_ref, i_ref, ring_ref, first_ref, second_ref = refs
+        got_ref, halo_ref, first_ref, second_ref = refs
     else:
-        low_ref, high_ref, w_ref, i_ref, ring_ref, first_ref, second_ref = refs
+        low_ref, high_ref, halo_ref, first_ref, second_ref = refs
     nx, ny, nz = w0_ref.shape
     sub = subs_of((SUB, nz))
     lane = lanes_of((ny + SUB, nz))
     if one:
         gy = lax.axis_index("gy")
-        from_low = (gy == 1) & (sub >= 5)
-        from_high = (gy == 0) & (sub <= 2)
-        inv_low = (gy == 1) & (sub >= 6)
-        inv_high = (gy == 0) & (sub <= 1)
+        w_rows = ((gy == 1) & (sub >= 5)) | ((gy == 0) & (sub <= 2))
+        i_rows = ((gy == 1) & (sub >= 6)) | ((gy == 0) & (sub <= 1))
     for x in range(nx + 1):
         if one:
             got = got_ref[x]
-            turned = pltpu.roll(got, 4, 0)
-            w_halo = jnp.where(from_low | from_high, got, 0.0)
-            i_halo = jnp.where(inv_low | inv_high, turned, 0.0)
+            halo_ref[0, x] = jnp.where(w_rows, got, 0.0)
+            halo_ref[1, x] = jnp.where(i_rows, pltpu.roll(got, 4, 0), 0.0)
         else:
             low, high = low_ref[x], high_ref[x]
-            w_halo = jnp.where(sub >= 5, low, jnp.where(sub <= 2, high, 0.0))
-            i_halo = jnp.where(
+            halo_ref[0, x] = jnp.where(sub >= 5, low, jnp.where(sub <= 2, high, 0.0))
+            halo_ref[1, x] = jnp.where(
                 sub >= 6, pltpu.roll(low, 4, 0), jnp.where(sub <= 1, pltpu.roll(high, 4, 0), 0.0)
             )
-        if x < nx:
-            w_ref[x, :ny] = w0_ref[x]
-            w_ref[x, ny:] = w_halo
-            i_ref[x, :ny] = inv_ref[x]
-            i_ref[x, ny:] = i_halo
-        else:
-            ring_ref[0, :ny] = slab_ref[0]
-            ring_ref[0, ny:] = w_halo
-            ring_ref[1, :ny] = slab_ref[1]
-            ring_ref[1, ny:] = i_halo
     odd = lax.rem(lax.axis_index("gx"), 2)
-    half = pltpu.roll(ring_ref[1], nz // 2, 1)
-    up = jnp.where(lane >= nz - 3 * PACK, ring_ref[0], half)
-    down = jnp.where(lane < 3 * PACK, ring_ref[0], half)
+    slab_w = jnp.concatenate([slab_ref[0], halo_ref[0, nx]], axis=0)
+    slab_i = jnp.concatenate([slab_ref[1], halo_ref[1, nx]], axis=0)
+    half = pltpu.roll(slab_i, nz // 2, 1)
+    up = jnp.where(lane >= nz - 3 * PACK, slab_w, half)
+    down = jnp.where(lane < 3 * PACK, slab_w, half)
     for face_ref, lower in ((first_ref, odd), (second_ref, 1 - odd)):
-        for k in range(3):
-            face_ref[k] = w_ref[(1 - lower) * (nx - 3) + k]
-        for k in range(2):
-            face_ref[3 + k] = i_ref[(1 - lower) * (nx - 2) + k]
+        for k in range(5):
+            field, source = (0, w0_ref) if k < 3 else (1, inv_ref)
+            place = (1 - lower) * (nx - 3 + field) + k - 3 * field
+            face_ref[k, :ny] = source[place]
+            face_ref[k, ny:] = halo_ref[field, place]
         face_ref[5] = jnp.where(lower == 1, down, up)
 
 
-def around(v):
-    rows = v.shape[0]
-    return pltpu.roll(v, 1, 0) + pltpu.roll(v, rows - 1, 0)
-
-
 def stencil_kernel(
-    w_ref, i_ref, ring_ref, first_ref, second_ref, stat_ref,
-    w1_ref, w2_ref, f0_ref, f1_ref, f2_ref, total_ref,
-    a_ref, b_ref, sw_ref,
+    w0_ref, inv_ref, slab_ref, halo_ref, first_ref, second_ref, stat_ref,
+    a_ref, b_ref, c_ref, slabs_ref, total_ref,
+    i_ref, si_ref,
 ):
-    nx, ring, nz = w_ref.shape
-    ny = ring - SUB
+    nx, ny, nz = w0_ref.shape
+    ring = ny + SUB
     gz = lax.axis_index("gz")
-    lane = lanes_of((ring, nz))
-    entry = (nz - 1) * gz
-    at_entry = lane == entry
-    lane_first = lane == 0
-    lane_last = lane == nz - 1
-
     odd = lax.rem(lax.axis_index("gx"), 2) == 1
 
     def low(k):
@@ -193,94 +176,93 @@
     def high(k):
         return jnp.where(odd, second_ref[k], first_ref[k])
 
-    def w0_plane(x):
-        if x < 0:
-            return low(3 + x)
-        if x >= nx:
-            return high(x - nx)
-        return w_ref[x]
-
-    def inv_plane(x):
-        if x < 0:
-            return low(5 + x)
-        if x >= nx:
-            return high(3 + x - nx)
-        return i_ref[x]
-
+    def place(ref, x, own, halo):
+        ref[x, SUB : SUB + ny] = own
+        ref[x, :SUB] = halo
+        ref[x, SUB + ny :] = halo
+
+    for x in range(nx):
+        place(a_ref, 3 + x, w0_ref[x], halo_ref[0, x])
+        place(i_ref, 2 + x, inv_ref[x], halo_ref[1, x])
+    for k in range(3):
+        for x, plane in ((k, low(k)), (nx + 3 + k, high(k))):
+            place(a_ref, x, plane[:ny], plane[ny:])
+    for k in range(2):
+        for x, plane in ((k, low(3 + k)), (nx + 2 + k, high(3 + k))):
+            place(i_ref, x, plane[:ny], plane[ny:])
+
+    lane = lanes_of((ring, nz))
     lo5, hi5 = low(5), high(5)
     slab_w = jnp.where(lane < 3 * PACK, hi5, 0.0) + jnp.where(lane >= nz - 3 * PACK, lo5, 0.0)
     lo5, hi5 = pltpu.roll(lo5, nz // 2, 1), pltpu.roll(hi5, nz // 2, 1)
     slab_i = jnp.where(lane < 2 * PACK, hi5, 0.0) + jnp.where(lane >= nz - 2 * PACK, lo5, 0.0)
-    slab = jnp.concatenate([ring_ref[0], slab_w], axis=1)
-    slab_inv = jnp.concatenate([ring_ref[1], slab_i], axis=1)
-
-    def slab_step(s):
-        width = s.shape[1]
-        along = pltpu.roll(s, 1, 1) + pltpu.roll(s, width - 1, 1)
-        both = s + 0.5 * along
-        wing = both + 0.5 * around(s)
-        total = along + around(both) + pltpu.roll(wing, PACK, 1) + pltpu.roll(wing, width - PACK, 1)
-        return total * slab_inv
-
-    def sweep(source, margin, face_ref, store):
-        wing_before = wing_here = rest_here = None
-        v_before = v_here = face_here = None
-        for x in range(-margin - 1, nx + margin + 1):
-            v = source(x)
-            place = (PACK * x) % (2 * nz)
-            half = sw_ref[:, nz * (place // nz) : nz * (place // nz) + nz]
-            turn = lax.rem(entry - (place % nz + 3 - gz) + 2 * nz, nz)
+    for ref, at, k, beyond in ((slabs_ref, 0, 0, slab_w), (si_ref, 0, 1, slab_i)):
+        ref[at, SUB : SUB + ny, :nz] = slab_ref[k]
+        ref[at, SUB : SUB + ny, nz:] = beyond[:ny]
+        for rows in (slice(0, SUB), slice(SUB + ny, SUB + ring)):
+            ref[at, rows, :nz] = halo_ref[k, nx]
+            ref[at, rows, nz:] = beyond[ny:]
+
+    sums = {}
+
+    def add(name, value, skip):
+        value = value[skip : skip + ny]
+        part = value[:SUB]
+        for k in range(SUB, ny, SUB):
+            part = part + value[k : k + SUB]
+        sums[name] = part if name not in sums else sums[name] + part
+
+    def rows_of(ref, x, start, size):
+        return ref[x, start : start + size]
+
+    for stage in range(3):
+        source = (a_ref, b_ref, c_ref)[stage]
+        target = (b_ref, c_ref, None)[stage]
+        margin = 2 - stage
+        start = SUB - margin
+        size = ny if margin == 0 else ring
+        lane = lanes_of((size, nz))
+        entry = (nz - 1) * gz
+        at_entry, lane_first, lane_last = lane == entry, lane == 0, lane == nz - 1
+
+        width = 2 * nz
+        v = slabs_ref[stage, start : start + size]
+        s = slabs_ref[stage, start - 1 : start - 1 + size] + slabs_ref[stage, start + 1 : start + 1 + size]
+        across = pltpu.roll(v, PACK, 1) + pltpu.roll(v, width - PACK, 1)
+        slab_q = v + 0.5 * (s + across)
+        if stage < 2:
+            total = (
+                pltpu.roll(slab_q, 1, 1) + pltpu.roll(slab_q, width - 1, 1) + s + across
+                + 0.5 * (pltpu.roll(s, PACK, 1) + pltpu.roll(s, width - PACK, 1))
+            )
+            slabs_ref[stage + 1, start : start + size] = total * si_ref[0, start : start + size]
+
+        def beside(x):
+            return rows_of(source, x, start - 1, size) + rows_of(source, x, start + 1, size)
+
+        s_low, s_mid = beside(0), beside(1)
+        v_low, v_mid = rows_of(source, 0, start, size), rows_of(source, 1, start, size)
+        for x in range(-margin, nx + margin):
+            at = x + margin + 1
+            v_high, s_high = rows_of(source, at + 1, start, size), beside(at + 1)
+            across = v_low + v_high
+            q = v_mid + 0.5 * (s_mid + across)
+            column = (PACK * x) % width
+            half = slab_q[:, column // nz * nz : column // nz * nz + nz]
+            turn = lax.rem(entry - (column % nz + 3 - gz) + 2 * nz, nz)
             edge = jnp.where(at_entry, pltpu.roll(half, turn, 1), 0.0)
-            along = pltpu.roll(jnp.where(lane_first, edge, v), nz - 1, 1) + pltpu.roll(
-                jnp.where(lane_last, edge, v), 1, 1
+            along = pltpu.roll(jnp.where(lane_first, edge, q), nz - 1, 1) + pltpu.roll(
+                jnp.where(lane_last, edge, q), 1, 1
             )
-            both = v + 0.5 * along
-            beside = around(v)
-            wing = both + 0.5 * beside
-            rest = along + around(both)
-            done = x - 1
-            if done >= -margin:
-                store(done, rest_here + wing_before + wing, v_here)
-                if 0 <= done < nx:
-                    face_ref[done] = face_here + (v_before + v)[:ny]
-            wing_before, wing_here, rest_here = wing_here, wing, rest
-            v_before, v_here = v_here, v
+            total = along + s_mid + across + 0.5 * (s_low + s_high)
+            if target is not None:
+                after = total * rows_of(i_ref, x + 2, start, size)
+                target[x + margin, start : start + size] = after
             if 0 <= x < nx:
-                face_here = (along + beside - 6.0 * v)[:ny]
-
-    sums = {}
-
-    def add(name, value):
-        part = jnp.sum(value[:ny].reshape(ny // SUB, SUB, nz), axis=0)
-        sums[name] = part if name not in sums else sums[name] + part
-
-    def store0(x, total, v):
-        w1 = total * inv_plane(x)
-        a_ref[x + 2] = w1
-        if 0 <= x < nx:
-            w1_ref[x] = w1[:ny]
-            add(1, v * total)
-            add(2, w1 * total)
-
-    def store1(x, total, v):
-        w2 = total * inv_plane(x)
-        b_ref[x + 1] = w2
-        if 0 <= x < nx:
-            w2_ref[x] = w2[:ny]
-            add(3, v * total)
-            add(4, w2 * total)
-
-    def store2(x, total, v):
-        add(5, v * total)
-
-    sw_ref[...] = slab
-    sweep(w0_plane, 2, f0_ref, store0)
-    slab = slab_step(slab)
-    sw_ref[...] = slab
-    sweep(lambda x: a_ref[x + 2], 1, f1_ref, store1)
-    slab = slab_step(slab)
-    sw_ref[...] = slab
-    sweep(lambda x: b_ref[x + 1], 0, f2_ref, store2)
+                add(2 * stage + 1, v_mid * total, margin)
+                if target is not None:
+                    add(2 * stage + 2, after * total, margin)
+            v_low, v_mid, s_low, s_mid = v_mid, v_high, s_mid, s_high
 
     total_ref[0:1] = stat_ref[0, 0:1]
     for k in range(1, 6):
@@ -344,31 +326,53 @@
     return c0, c1, c2
 
 
-def combine_kernel(
-    slot_rows, total_ref, w0_ref, w1_ref, w2_ref, f0_ref, f1_ref, f2_ref, plan_ref, x_ref, *out_refs
-):
-    rows = w0_ref.shape[0]
+def combine_kernel(slot_rows, total_ref, w0_ref, w1_ref, w2_ref, slabs_ref, plan_ref, x_hbm, *refs):
+    *out_refs, wide_ref, x_ref, value_ref, buf_ref, sem = refs
+    nx, ny, nz = x_ref.shape
+    rows = nx * ny
     lane = lanes_of((rows, LANES))
     row = subs_of((rows, LANES))
     sums = jnp.sum(total_ref[0:8], axis=1, keepdims=True)
     t = [jnp.broadcast_to(sums[k : k + 1], (1, LANES)) for k in range(6)]
     c0, c1, c2 = galerkin(t)
-    x_ref[...] = c0 * w0_ref[...] + c1 * w1_ref[...] + c2 * w2_ref[...]
-    value = c0 * f0_ref[...] + c1 * f1_ref[...] + c2 * f2_ref[...]
+    for x in range(nx + 2):
+        wide_ref[x] = c0 * w0_ref[x + 2] + c1 * w1_ref[x + 1] + c2 * w2_ref[x]
+    for x in range(nx):
+        x_ref[x] = wide_ref[x + 1, SUB : SUB + ny]
+    leave = pltpu.make_async_copy(x_ref, x_hbm, sem)
+    leave.start()
+
+    gz = lax.axis_index("gz")
+    own = slice(SUB, SUB + ny)
+    slab = c0 * slabs_ref[0, own, :nz] + c1 * slabs_ref[1, own, :nz] + c2 * slabs_ref[2, own, :nz]
+    column = lanes_of((ny, nz))
+    entry = (nz - 1) * gz
+    at_entry, lane_first, lane_last = column == entry, column == 0, column == nz - 1
+    for x in range(nx):
+        v = wide_ref[x + 1, own]
+        turn = lax.rem(entry - (PACK * x + 3 - gz) + 2 * nz, nz)
+        edge = jnp.where(at_entry, pltpu.roll(slab, turn, 1), 0.0)
+        along = pltpu.roll(jnp.where(lane_first, edge, v), nz - 1, 1) + pltpu.roll(
+            jnp.where(lane_last, edge, v), 1, 1
+        )
+        beside = wide_ref[x + 1, SUB - 1 : SUB - 1 + ny] + wide_ref[x + 1, SUB + 1 : SUB + 1 + ny]
+        across = wide_ref[x, own] + wide_ref[x + 2, own]
+        value_ref[ny * x : ny * x + ny] = along + beside + across - 6.0 * v
+
+    value = value_ref[...]
     plan = plan_ref[...]
     step = 1
     while step < rows * LANES:
         value = jnp.where((plan & step) != 0, shift_left(value, step, lane), value)
         step *= 2
-    ny, nz = lax.axis_size("gy"), lax.axis_size("gz")
+    n_y, n_z = lax.axis_size("gy"), lax.axis_size("gz")
     counts = total_ref[8:16]
     dev = lanes_of((SUB, LANES))
-    column = lax.axis_index("gy") * nz + lax.axis_index("gz")
-    mine = lax.rem(dev, ny * nz) == column
+    mine = lax.rem(dev, n_y * n_z) == lax.axis_index("gy") * n_z + gz
     gx = lax.axis_index("gx")
     first = subs_of((SUB, LANES)) == 0
-    offset = jnp.sum(jnp.where(first & mine & (dev < gx * ny * nz), counts, 0.0)).astype(jnp.int32)
-    count = jnp.sum(jnp.where(first & mine & (dev // (ny * nz) == gx), counts, 0.0)).astype(jnp.int32)
+    offset = jnp.sum(jnp.where(first & mine & (dev < gx * n_y * n_z), counts, 0.0)).astype(jnp.int32)
+    count = jnp.sum(jnp.where(first & mine & (dev // (n_y * n_z) == gx), counts, 0.0)).astype(jnp.int32)
     slots = value[:slot_rows]
     index = (row * LANES + lane)[:slot_rows]
     slots = jnp.where(index < count, slots, 0.0)
@@ -377,21 +381,33 @@
     turned = pltpu.roll(slots, inner, 1)
     above = pltpu.roll(turned, 1, 0)
     moved = jnp.where(lane[: slot_rows + SUB] >= inner, turned, above)
-    *out_refs, buf_ref = out_refs
     buf_ref[...] = jnp.zeros_like(buf_ref)
     buf_ref[pl.ds(offset // LANES, slot_rows + SUB), :] = moved
     for k, out_ref in enumerate(out_refs):
         size = out_ref.shape[0]
         out_ref[...] = buf_ref[pl.ds(pl.multiple_of((gx ^ k) * size, SUB), size), :]
+    leave.wait()
+
+
+def chunks_of(n_states, parts):
+    size = -(-n_states // parts)
+    return [(k, min(size, n_states - k)) for k in range(0, n_states, size)]
 
 
 def membrane_kernel(
-    half_ref, slope_ref, tau_ref, cond_ref, rev_ref, v_ref, gates_ref, cot_ref,
+    half_ref, slope_ref, tau_ref, cond_ref, rev_ref, v_ref, gates_hbm, cot_hbm,
     base_ref, sum_ref, factor_ref, coef_ref,
+    gates_ref, cot_ref, sems,
 ):
-    n_states = gates_ref.shape[0]
+    n_states, rows = gates_ref.shape[:2]
+    chunks = chunks_of(n_states, sems.shape[1])
+    copies = []
+    for part, (begin, size) in enumerate(chunks):
+        for k, (source, target) in enumerate(((gates_hbm, gates_ref), (cot_hbm, cot_ref))):
+            here = pl.ds(begin, size)
+            copies.append(pltpu.make_async_copy(source.at[here], target.at[here], sems.at[k, part]))
+            copies[-1].start()
     v = v_ref[...]
-    rows = v.shape[0]
 
     def state(g, carry):
         total, current = carry
@@ -412,22 +428,32 @@
         coef_ref[1, pl.ds(g, 1)] = jnp.full((1, LANES), rev_ref[g])
         return total + cot * change, current + cond_ref[g] * gate
 
-    zero = jnp.zeros((rows, LANES), F32)
-    total, current = lax.fori_loop(0, n_states, state, (zero, zero), unroll=2)
-    sum_ref[...] = total
-    factor_ref[...] = 1.0 - TIME_STEP * current
+    carry = (jnp.zeros((rows, LANES), F32),) * 2
+    for part, (begin, size) in enumerate(chunks):
+        copies[2 * part].wait()
+        copies[2 * part + 1].wait()
+        carry = lax.fori_loop(begin, begin + size, state, carry, unroll=True)
+    sum_ref[...] = carry[0]
+    factor_ref[...] = 1.0 - TIME_STEP * carry[1]
 
 
 def finish_kernel(coef_ref, vcot_ref, v_ref, sum_ref, factor_ref, base_ref, *refs):
-    *landed_refs, volt_ref, gate_ref = refs
+    *landed_refs, volt_ref, gate_hbm, gate_ref, sems = refs
     landed = landed_refs[0][...]
     for ref in landed_refs[1:]:
         landed = landed + ref[...]
     cot = vcot_ref[...] + landed
     v = v_ref[...]
+    copies = []
+    for part, (begin, size) in enumerate(chunks_of(base_ref.shape[0], sems.shape[0])):
+        for g in range(begin, begin + size):
+            gate_ref[g] = base_ref[g] - (coef_ref[0, g : g + 1] * cot) * (v - coef_ref[1, g : g + 1])
+        here = pl.ds(begin, size)
+        copies.append(pltpu.make_async_copy(gate_ref.at[here], gate_hbm.at[here], sems.at[part]))
+        copies[-1].start()
     volt_ref[...] = cot * factor_ref[...] + sum_ref[...]
-    for g in range(base_ref.shape[0]):
-        gate_ref[g] = base_ref[g] - (coef_ref[0, g : g + 1] * cot) * (v - coef_ref[1, g : g + 1])
+    for copy in copies:
+        copy.wait()
 
 
 def both_ways(up, down, axis):
@@ -477,7 +503,7 @@
             pltpu.VMEM((nx, ny, nz), F32), pltpu.VMEM((nx, ny, nz), F32), pltpu.VMEM((nx, ny, nz), jnp.int32),
             pltpu.SemaphoreType.DMA((3, 4)),
         ],
-    )(*[pltpu.with_memory_space_constraint(a, pltpu.HBM) for a in (potential_cot, damping, tissue_label)])
+    )(in_hbm(potential_cot), in_hbm(damping), in_hbm(tissue_label))
 
     got = lax.ppermute(packed, "gz", [(0, 1), (1, 0)])
     base, total_change, factor, coefs = call(
@@ -487,45 +513,53 @@
             shape_of(2, n_states, LANES),
         ),
         8,
-        specs=[SMEM] * 5 + [VMEM] * 3,
+        specs=[SMEM] * 5 + [VMEM] + [HBM] * 2,
+        scratch=[pltpu.VMEM((n_states, block_rows, LANES), F32)] * 2 + [pltpu.SemaphoreType.DMA((2, 4))],
         cost=6_000_000,
-    )(half_voltage, gate_slope, tau_base, conductance, reversal, cells(voltage), states(gates), states(gates_cot))
+    )(
+        half_voltage, gate_slope, tau_base, conductance, reversal,
+        cells(voltage), in_hbm(states(gates)), in_hbm(states(gates_cot)),
+    )
     plan = call(plan_kernel, jax.ShapeDtypeStruct((rows, LANES), jnp.int32), 1, cost=6_000_000)(flat(tissue_label))
 
     face = shape_of(nx + 1, SUB, nz)
     slab_shape = shape_of(2, ny, nz)
-    ring_shapes = (shape_of(nx, ring, nz), shape_of(nx, ring, nz), shape_of(2, ring, nz))
-    x_shapes = ring_shapes + (shape_of(6, ring, nz), shape_of(6, ring, nz))
+    x_shapes = (shape_of(2, nx + 1, SUB, nz), shape_of(6, ring, nz), shape_of(6, ring, nz))
     if n_gy == 2:
         slab, mine = call(y_face_one_kernel, (slab_shape, face), 4)(w0, inv, packed, got)
         halo = (lax.ppermute(mine, "gy", [(0, 1), (1, 0)]),)
     else:
         slab, up, down = call(y_faces_kernel, (slab_shape, face, face), 4)(w0, inv, packed, got)
         halo = both_ways(up, down, "gy")
-    wide, wide_inv, ring_slab, first, second = call(
+    edge_rows, first, second = call(
         functools.partial(x_faces_kernel, n_gy == 2), x_shapes, 3 + len(halo)
     )(w0, inv, slab, *halo)
     first, second = pair_swaps(first, second, "gx")
 
-    w1, w2, f0, f1, f2, sums = call(
+    tall = ring + SUB
+    basis = [shape_of(nx + 2 * k, tall, nz) for k in (3, 2, 1)]
+    wide0, wide1, wide2, slabs, sums = call(
         stencil_kernel,
-        (block,) * 5 + (shape_of(16, nz),),
-        6,
-        scratch=[
-            pltpu.VMEM((nx + 4, ring, nz), F32),
-            pltpu.VMEM((nx + 2, ring, nz), F32),
-            pltpu.VMEM((ring, 2 * nz), F32),
-        ],
-    )(wide, wide_inv, ring_slab, first, second, stat)
+        (*basis, shape_of(3, tall, 2 * nz), shape_of(16, nz)),
+        7,
+        scratch=[pltpu.VMEM((nx + 4, tall, nz), F32), pltpu.VMEM((1, tall, 2 * nz), F32)],
+    )(w0, inv, slab, edge_rows, first, second, stat)
     for axis in ("gz", "gy", "gx"):
         sums = reduce_over(sums, axis)
 
     solution, *blocks = call(
         functools.partial(combine_kernel, slot_rows),
-        (shape_of(rows, LANES),) + (shape_of(block_rows, LANES),) * n_gx,
-        8,
-        scratch=[pltpu.VMEM((n_gx * block_rows + slot_rows + SUB, LANES), F32)],
-    )(sums, flat(w0), flat(w1), flat(w2), flat(f0), flat(f1), flat(f2), plan)
+        (block,) + (shape_of(block_rows, LANES),) * n_gx,
+        6,
+        outs=(HBM,) + (VMEM,) * n_gx,
+        scratch=[
+            pltpu.VMEM((nx + 2, tall, nz), F32),
+            pltpu.VMEM((nx, ny, nz), F32),
+            pltpu.VMEM((rows, LANES), F32),
+            pltpu.VMEM((n_gx * block_rows + slot_rows + SUB, LANES), F32),
+            pltpu.SemaphoreType.DMA(()),
+        ],
+    )(sums, wide0, wide1, wide2, slabs, plan)
     landed = blocks[:1] + [
         lax.ppermute(blocks[k], "gx", [(i, i ^ k) for i in range(n_gx)]) for k in range(1, n_gx)
     ]
@@ -534,8 +568,10 @@
         finish_kernel,
         (shape_of(block_rows, LANES), shape_of(n_states, block_rows, LANES)),
         6 + n_gx,
+        outs=(VMEM, HBM),
+        scratch=[pltpu.VMEM((n_states, block_rows, LANES), F32), pltpu.SemaphoreType.DMA((4,))],
     )(coefs, cells(voltage_cot), cells(voltage), total_change, factor, base, *landed)
-    return solution.reshape(nx, ny, nz), volt_grad.reshape(voltage.shape), gate_grad.reshape(gates.shape)
+    return solution, volt_grad.reshape(voltage.shape), gate_grad.reshape(gates.shape)
 
 
 def solution(mesh):

time: 46.6 us -> 46.8 us (level)
  Pallas kernels: 12.7 us -> 13.6 us
  waiting for transfers between devices: 11.5 us -> 10.8 us
    ppermute x3, waiting for transfers between devices: 1.15 us -> 0.42 us  [local(): lax.ppermute(blocks[k], 'gx', [(i, i ^ k) for i in range(n_gx)])]
    pallas_call x1, Pallas kernels: 1.92 us -> 2.64 us  [local(): call(membrane_kernel, (shape_of(n_states, block_rows, LANES), shape_of(bl...]
    pallas_call x1, Pallas kernels: 0.94 us -> 1.52 us  [local(): call(finish_kernel, (shape_of(block_rows, LANES), shape_of(n_states, bloc...]
  transfers between devices with their start and end apart: 11 -> 11, of which waited for: 7 -> 7; matrix products, arithmetic and copies ran while one was open for 0% -> 0% of each run, Pallas kernels for 8% -> 9%
where the time goes in v4:
time: 46.8 us; the launch traced here: 46.6 us
  starting transfers between devices  20.8 us (44%)
  Pallas kernels  13.6 us (29%)
  waiting for transfers between devices  10.8 us (23%)
  between operations  0.77 us (2%)
  local copies, waits for them, and re-layouts  0.69 us (1%)
    ppermute x4, starting transfers between devices, reduce_over(): lax.ppermute(value, axis, [(i, i ^ step) for i in range(count)])  10.3 us
    ppermute x4, waiting for transfers between devices, reduce_over(): lax.ppermute(value, axis, [(i, i ^ step) for i in range(count)])  4.64 us
    ppermute x3, starting transfers between devices, local(): lax.ppermute(blocks[k], 'gx', [(i, i ^ k) for i in range(n_gx)])  4.45 us
    pallas_call x1, Pallas kernels, local(): call(stencil_kernel, (*basis, shape_of(3, tall, 2 * nz), shape_of(16, nz)...  4.08 us
    ppermute x1, starting transfers between devices, local(): halo = (lax.ppermute(mine, 'gy', [(0, 1), (1, 0)]),)  2.9 us
    pallas_call x1, Pallas kernels, local(): call(membrane_kernel, (shape_of(n_states, block_rows, LANES), shape_of(bl...  2.64 us
    ppermute x1, waiting for transfers between devices, local(): halo = (lax.ppermute(mine, 'gy', [(0, 1), (1, 0)]),)  2.51 us
    ppermute x1, waiting for transfers between devices, pair_swaps(): lax.ppermute(first, axis, even)  2.33 us
  transfers between devices with their start and end apart: 11, of which 7 were waited for; matrix products, arithmetic and copies ran while one was open for 0% of the time, Pallas kernels for 9%

profile of v4, /device:TPU:0, one launch (start us, length us, event | category | flops | bytes accessed | tf_op | source)
XLA Modules:
  0.0 46.6 jit_solution(805631394613298038)
XLA Ops:
  0.6 1.5 %shard_map.139 = (f32[16,32,128]{2,1,0:T(8,128)S(1)}, f32[16,32,128]{2,1,0:T(8,128)S(1)}, f32[2,32,128]{2,1,0:T(8,128)S(1)}, f32[2,8,128]{2,1,0:T(8,128)S(1)}) custom-call(f32[16,32,128]{2,1,0:T(8,128)} %right_hbm.1, f32[16,32,128]{2,1,0:T(8,128)} %damping_hbm.1, s32[16,32,128]{2,1,0:T(8,128)} %label_hbm.1), custom_call_target="tpu_custom_call" | custom-call | flops 2000000 | bytes 2000000 | tf_op jit(solution)/shard_map/pallas_call | solution.py:499
  2.1 0.5 %collective-permute-start = (f32[2,32,128]{2,1,0:T(8,128)S(1)}, f32[2,32,128]{2,1,0:T(8,128)S(1)}, u32[]{:S(2)}, u32[]{:S(2)}) collective-permute-start(f32[2,32,128]{2,1,0:T(8,128)S(1)} %get-tuple-element.30.own_ref), channel_id=1, source_target_pairs={{0,1},{1,0},{2,3},{3,2},{4,5},{5,4},{6,7},{7,6},{8,9},{9,8},{10,11... | collective-permute-start | bytes 98312 | tf_op jit(solution)/shard_map/ppermute | solution.py:508
  2.6 0.9 %collective-permute-done.got_ref = f32[2,32,128]{2,1,0:T(8,128)S(1)} collective-permute-done((f32[2,32,128]{2,1,0:T(8,128)S(1)}, f32[2,32,128]{2,1,0:T(8,128)S(1)}, u32[]{:S(2)}, u32[]{:S(2)}) %collective-permute-start) | collective-permute-done | bytes 32800 | tf_op jit(solution)/shard_map/ppermute | solution.py:508
  3.5 2.9 %collective-permute-start.1 = (f32[17,8,128]{2,1,0:T(8,128)S(1)}, f32[17,8,128]{2,1,0:T(8,128)S(1)}, u32[]{:S(2)}, u32[]{:S(2)}) collective-permute-start(f32[17,8,128]{2,1,0:T(8,128)S(1)} %get-tuple-element.32), channel_id=1, source_target_pairs={{0,2},{2,0},{1,3},{3,1},{4,6},{6,4},{5,7},{7,5},{8,10},{10,8},{9,1... | collective-permute-start | bytes 208904 | tf_op jit(solution)/shard_map/ppermute | solution.py:530
  6.4 2.5 %collective-permute-done.1.refs_0_ = f32[17,8,128]{2,1,0:T(8,128)S(1)} collective-permute-done((f32[17,8,128]{2,1,0:T(8,128)S(1)}, f32[17,8,128]{2,1,0:T(8,128)S(1)}, u32[]{:S(2)}, u32[]{:S(2)}) %collective-permute-start.1) | collective-permute-done | bytes 69664 | tf_op jit(solution)/shard_map/ppermute | solution.py:530
  9.0 1.9 %collective-permute-start.2 = (f32[6,40,128]{2,1,0:T(8,128)S(1)}, f32[6,40,128]{2,1,0:T(8,128)S(1)}, u32[]{:S(2)}, u32[]{:S(2)}) collective-permute-start(f32[6,40,128]{2,1,0:T(8,128)S(1)} %get-tuple-element.34), channel_id=1, source_target_pairs={{0,4},{4,0},{8,12},{12,8},{1,5},{5,1},{9,13},{13,9},{2,6},{6,2},{1... | collective-permute-start | bytes 368648 | tf_op jit(solution)/shard_map/ppermute | solution.py:471
  10.9 0.7 %collective-permute-start.3 = (f32[6,40,128]{2,1,0:T(8,128)S(1)}, f32[6,40,128]{2,1,0:T(8,128)S(1)}, u32[]{:S(2)}, u32[]{:S(2)}) collective-permute-start(f32[6,40,128]{2,1,0:T(8,128)S(1)} %get-tuple-element.35), channel_id=1, source_target_pairs={{4,8},{8,4},{5,9},{9,5},{6,10},{10,6},{7,11},{11,7},{20,24},{24,20... | collective-permute-start | bytes 368648 | tf_op jit(solution)/shard_map/ppermute | solution.py:471
  11.6 2.3 %collective-permute-done.2.first_ref = f32[6,40,128]{2,1,0:T(8,128)S(1)} collective-permute-done((f32[6,40,128]{2,1,0:T(8,128)S(1)}, f32[6,40,128]{2,1,0:T(8,128)S(1)}, u32[]{:S(2)}, u32[]{:S(2)}) %collective-permute-start.2) | collective-permute-done | bytes 122912 | tf_op jit(solution)/shard_map/ppermute | solution.py:471
  13.9 4.1 %shard_map.142 = (f32[22,48,128]{2,1,0:T(8,128)S(1)}, f32[20,48,128]{2,1,0:T(8,128)S(1)}, f32[18,48,128]{2,1,0:T(8,128)S(1)}, f32[3,48,256]{2,1,0:T(8,128)S(1)}, f32[16,128]{1,0:T(8,128)S(1)}) custom-call(f32[16,32,128]{2,1,0:T(8,128)S(1)} %get-tuple-element.28.w0_ref, f32[16,32,128]{2,1,0:T(8,128)S(1)} %get-tuple-element.29.inv_ref, ...), custom_call_target="tpu_custom_call" | custom-call | flops 2000000 | bytes 2000000 | tf_op jit(solution)/shard_map/pallas_call | solution.py:541
  18.1 1.2 %collective-permute-done.4 = f32[16,128]{1,0:T(8,128)S(1)} collective-permute-done((f32[16,128]{1,0:T(8,128)S(1)}, f32[16,128]{1,0:T(8,128)S(1)}, u32[]{:S(2)}, u32[]{:S(2)}) %collective-permute-start.4) | collective-permute-done | bytes 8224 | tf_op jit(solution)/shard_map/ppermute | solution.py:478
  19.2 1.8 %collective-permute-start.5 = (f32[16,128]{1,0:T(8,128)S(1)}, f32[16,128]{1,0:T(8,128)S(1)}, u32[]{:S(2)}, u32[]{:S(2)}) collective-permute-start(f32[16,128]{1,0:T(8,128)S(1)} %add.12), channel_id=1, source_target_pairs={{0,2},{2,0},{1,3},{3,1},{4,6},{6,4},{5,7},{7,5},{8,10},{10,8},{9,1... | collective-permute-start | bytes 24584 | tf_op jit(solution)/shard_map/ppermute | solution.py:478
  21.0 1.8 %collective-permute-done.5 = f32[16,128]{1,0:T(8,128)S(1)} collective-permute-done((f32[16,128]{1,0:T(8,128)S(1)}, f32[16,128]{1,0:T(8,128)S(1)}, u32[]{:S(2)}, u32[]{:S(2)}) %collective-permute-start.5) | collective-permute-done | bytes 8224 | tf_op jit(solution)/shard_map/ppermute | solution.py:478
  22.9 4.9 %collective-permute-start.6 = (f32[16,128]{1,0:T(8,128)S(1)}, f32[16,128]{1,0:T(8,128)S(1)}, u32[]{:S(2)}, u32[]{:S(2)}) collective-permute-start(f32[16,128]{1,0:T(8,128)S(1)} %add.13), channel_id=1, source_target_pairs={{0,4},{4,0},{8,12},{12,8},{1,5},{5,1},{9,13},{13,9},{2,6},{6,2},{1... | collective-permute-start | bytes 24584 | tf_op jit(solution)/shard_map/ppermute | solution.py:478
  27.8 1.6 %collective-permute-done.6 = f32[16,128]{1,0:T(8,128)S(1)} collective-permute-done((f32[16,128]{1,0:T(8,128)S(1)}, f32[16,128]{1,0:T(8,128)S(1)}, u32[]{:S(2)}, u32[]{:S(2)}) %collective-permute-start.6) | collective-permute-done | bytes 8224 | tf_op jit(solution)/shard_map/ppermute | solution.py:478
  29.4 3.6 %collective-permute-start.7 = (f32[16,128]{1,0:T(8,128)S(1)}, f32[16,128]{1,0:T(8,128)S(1)}, u32[]{:S(2)}, u32[]{:S(2)}) collective-permute-start(f32[16,128]{1,0:T(8,128)S(1)} %add.14), channel_id=1, source_target_pairs={{0,8},{4,12},{8,0},{12,4},{1,9},{5,13},{9,1},{13,5},{2,10},{6,14},... | collective-permute-start | bytes 24584 | tf_op jit(solution)/shard_map/ppermute | solution.py:478
  33.0 1.7 %shard_map.143.plan_ref = s32[512,128]{1,0:T(8,128)S(1)} custom-call(s32[512,128]{1,0:T(8,128)S(1)} %bitcast.7), custom_call_target="tpu_custom_call" | custom-call | flops 6000000 | bytes 6000000 | tf_op jit(solution)/shard_map/pallas_call | solution.py:523
  34.8 2.1 %shard_map.144 = (f32[16,32,128]{2,1,0:T(8,128)}, f32[64,128]{1,0:T(8,128)S(1)}, f32[64,128]{1,0:T(8,128)S(1)}, f32[64,128]{1,0:T(8,128)S(1)}, f32[64,128]{1,0:T(8,128)S(1)}) custom-call(f32[16,128]{1,0:T(8,128)S(1)} %add.15.total_ref, f32[22,48,128]{2,1,0:T(8,128)S(1)} %get-tuple-element.38.w0_ref, f32[20,48,128]{2,1,0:T(8,128)S(1)} %get-tuple-element.39.w1_ref, ...), custom_call_target="tpu_custom_call" | custom-call | flops 2000000 | bytes 2000000 | tf_op jit(solution)/shard_map/pallas_call | solution.py:550
  36.8 2.2 %collective-permute-start.10 = (f32[64,128]{1,0:T(8,128)S(1)}, f32[64,128]{1,0:T(8,128)S(1)}, u32[]{:S(2)}, u32[]{:S(2)}) collective-permute-start(f32[64,128]{1,0:T(8,128)S(1)} %get-tuple-element.50), channel_id=1, source_target_pairs={{0,12},{4,8},{8,4},{12,0},{1,13},{5,9},{9,5},{13,1},{2,14},{6,10},... | collective-permute-start | bytes 98312 | tf_op jit(solution)/shard_map/ppermute | solution.py:564
  39.0 1.2 %collective-permute-start.8 = (f32[64,128]{1,0:T(8,128)S(1)}, f32[64,128]{1,0:T(8,128)S(1)}, u32[]{:S(2)}, u32[]{:S(2)}) collective-permute-start(f32[64,128]{1,0:T(8,128)S(1)} %get-tuple-element.48), channel_id=1, source_target_pairs={{0,4},{4,0},{8,12},{12,8},{1,5},{5,1},{9,13},{13,9},{2,6},{6,2},{1... | collective-permute-start | bytes 98312 | tf_op jit(solution)/shard_map/ppermute | solution.py:564
  40.3 1.0 %collective-permute-start.9 = (f32[64,128]{1,0:T(8,128)S(1)}, f32[64,128]{1,0:T(8,128)S(1)}, u32[]{:S(2)}, u32[]{:S(2)}) collective-permute-start(f32[64,128]{1,0:T(8,128)S(1)} %get-tuple-element.49), channel_id=1, source_target_pairs={{0,8},{4,12},{8,0},{12,4},{1,9},{5,13},{9,1},{13,5},{2,10},{6,14},... | collective-permute-start | bytes 98312 | tf_op jit(solution)/shard_map/ppermute | solution.py:564
  41.3 0.6 %copy-done.3 = f32[20]{0:T(128)S(1)} copy-done((f32[20]{0:T(128)S(1)}, f32[20]{0:T(128)}, u32[]{:S(2)}) %copy-start.3) | copy-done | bytes 104
  42.0 2.6 %shard_map.145 = (f32[20,64,128]{2,1,0:T(8,128)S(1)}, f32[64,128]{1,0:T(8,128)S(1)}, f32[64,128]{1,0:T(8,128)S(1)}, f32[2,20,128]{2,1,0:T(8,128)S(1)}) custom-call(f32[20]{0:T(128)S(1)} %copy-done.3, f32[20]{0:T(128)S(1)} %copy-done.4, f32[20]{0:T(128)S(1)} %copy-done.5, f32[20]{0:T(128)S(1)} %copy-done.6, f32[20]{0:T(128)S(1)} %copy-done.7, ...), custom_call_target="tpu_custom_call" | custom-call | flops 6000000 | bytes 6000000 | tf_op jit(solution)/shard_map/pallas_call | solution.py:509
  44.7 0.4 collective-permute-done.9.refs_2_
  45.1 1.5 %shard_map.146 = (f32[64,128]{1,0:T(8,128)}, f32[20,64,128]{2,1,0:T(8,128)}) custom-call(f32[2,20,128]{2,1,0:T(8,128)S(1)} %get-tuple-element.43.coef_ref, f32[64,128]{1,0:T(8,128)S(1)} %bitcast.10, f32[64,128]{1,0:T(8,128)S(1)} %bitcast.9, f32[64,128]{1,0:T(8,128)S(1)} %get-tuple-element.44.sum_ref, f32[64,128]{1,0:T(8,128)S(1)} %get-tuple-element.45.factor_ref, ...), custom_call_target="tpu_custom_call" | custom-call | flops 2000000 | bytes 2000000 | tf_op jit(solution)/shard_map/pallas_call | solution.py:567
  (26 shorter events, 0.3 us)
Async XLA Ops:
  2.1 1.4 %collective-permute-start = (f32[2,32,128]{2,1,0:T(8,128)S(1)}, f32[2,32,128]{2,1,0:T(8,128)S(1)}, u32[]{:S(2)}, u32[]{:S(2)}) collective-permute-start(f32[2,32,128]{2,1,0:T(8,128)S(1)} %get-tuple-element.30.own_ref), channel_id=1, source_target_pairs={{0,1},{1,0},{2,3},{3,2},{4,5},{5,4},{6,7},{7,6},{8,9},{9,8},{10,11... | collective-permute-start | bytes 98312 | tf_op jit(solution)/shard_map/ppermute | solution.py:508
  3.5 5.4 %collective-permute-start.1 = (f32[17,8,128]{2,1,0:T(8,128)S(1)}, f32[17,8,128]{2,1,0:T(8,128)S(1)}, u32[]{:S(2)}, u32[]{:S(2)}) collective-permute-start(f32[17,8,128]{2,1,0:T(8,128)S(1)} %get-tuple-element.32), channel_id=1, source_target_pairs={{0,2},{2,0},{1,3},{3,1},{4,6},{6,4},{5,7},{7,5},{8,10},{10,8},{9,1... | collective-permute-start | bytes 208904 | tf_op jit(solution)/shard_map/ppermute | solution.py:530
  9.0 4.9 %collective-permute-start.2 = (f32[6,40,128]{2,1,0:T(8,128)S(1)}, f32[6,40,128]{2,1,0:T(8,128)S(1)}, u32[]{:S(2)}, u32[]{:S(2)}) collective-permute-start(f32[6,40,128]{2,1,0:T(8,128)S(1)} %get-tuple-element.34), channel_id=1, source_target_pairs={{0,4},{4,0},{8,12},{12,8},{1,5},{5,1},{9,13},{13,9},{2,6},{6,2},{1... | collective-permute-start | bytes 368648 | tf_op jit(solution)/shard_map/ppermute | solution.py:471
  10.9 3.0 %collective-permute-start.3 = (f32[6,40,128]{2,1,0:T(8,128)S(1)}, f32[6,40,128]{2,1,0:T(8,128)S(1)}, u32[]{:S(2)}, u32[]{:S(2)}) collective-permute-start(f32[6,40,128]{2,1,0:T(8,128)S(1)} %get-tuple-element.35), channel_id=1, source_target_pairs={{4,8},{8,4},{5,9},{9,5},{6,10},{10,6},{7,11},{11,7},{20,24},{24,20... | collective-permute-start | bytes 368648 | tf_op jit(solution)/shard_map/ppermute | solution.py:471
  13.9 19.1 %copy-start = (s32[16,32,128]{2,1,0:T(8,128)S(1)}, s32[16,32,128]{2,1,0:T(8,128)}, u32[]{:S(2)}) copy-start(s32[16,32,128]{2,1,0:T(8,128)} %label_hbm.1) | copy-start | bytes 786436
  18.0 1.2 %collective-permute-start.4 = (f32[16,128]{1,0:T(8,128)S(1)}, f32[16,128]{1,0:T(8,128)S(1)}, u32[]{:S(2)}, u32[]{:S(2)}) collective-permute-start(f32[16,128]{1,0:T(8,128)S(1)} %get-tuple-element.37), channel_id=1, source_target_pairs={{0,1},{1,0},{2,3},{3,2},{4,5},{5,4},{6,7},{7,6},{8,9},{9,8},{10,11... | collective-permute-start | bytes 24584 | tf_op jit(solution)/shard_map/ppermute | solution.py:478
  19.2 3.7 %collective-permute-start.5 = (f32[16,128]{1,0:T(8,128)S(1)}, f32[16,128]{1,0:T(8,128)S(1)}, u32[]{:S(2)}, u32[]{:S(2)}) collective-permute-start(f32[16,128]{1,0:T(8,128)S(1)} %add.12), channel_id=1, source_target_pairs={{0,2},{2,0},{1,3},{3,1},{4,6},{6,4},{5,7},{7,5},{8,10},{10,8},{9,1... | collective-permute-start | bytes 24584 | tf_op jit(solution)/shard_map/ppermute | solution.py:478
  22.9 6.5 %collective-permute-start.6 = (f32[16,128]{1,0:T(8,128)S(1)}, f32[16,128]{1,0:T(8,128)S(1)}, u32[]{:S(2)}, u32[]{:S(2)}) collective-permute-start(f32[16,128]{1,0:T(8,128)S(1)} %add.13), channel_id=1, source_target_pairs={{0,4},{4,0},{8,12},{12,8},{1,5},{5,1},{9,13},{13,9},{2,6},{6,2},{1... | collective-permute-start | bytes 24584 | tf_op jit(solution)/shard_map/ppermute | solution.py:478
  29.4 5.3 %collective-permute-start.7 = (f32[16,128]{1,0:T(8,128)S(1)}, f32[16,128]{1,0:T(8,128)S(1)}, u32[]{:S(2)}, u32[]{:S(2)}) collective-permute-start(f32[16,128]{1,0:T(8,128)S(1)} %add.14), channel_id=1, source_target_pairs={{0,8},{4,12},{8,0},{12,4},{1,9},{5,13},{9,1},{13,5},{2,10},{6,14},... | collective-permute-start | bytes 24584 | tf_op jit(solution)/shard_map/ppermute | solution.py:478
  34.7 6.6 %copy-start.1 = (f32[1,8192]{1,0:T(1,128)S(1)}, f32[1,8192]{1,0:T(1,128)}, u32[]{:S(2)}) copy-start(f32[1,8192]{1,0:T(1,128)} %param.16) | copy-start | bytes 98308
  34.7 6.6 %copy-start.6 = (f32[20]{0:T(128)S(1)}, f32[20]{0:T(128)}, u32[]{:S(2)}) copy-start(f32[20]{0:T(128)} %cond_ref.1) | copy-start | bytes 244
  34.8 6.6 %copy-start.7 = (f32[20]{0:T(128)S(1)}, f32[20]{0:T(128)}, u32[]{:S(2)}) copy-start(f32[20]{0:T(128)} %rev_ref.1) | copy-start | bytes 244
  36.8 7.8 %collective-permute-start.10 = (f32[64,128]{1,0:T(8,128)S(1)}, f32[64,128]{1,0:T(8,128)S(1)}, u32[]{:S(2)}, u32[]{:S(2)}) collective-permute-start(f32[64,128]{1,0:T(8,128)S(1)} %get-tuple-element.50), channel_id=1, source_target_pairs={{0,12},{4,8},{8,4},{12,0},{1,13},{5,9},{9,5},{13,1},{2,14},{6,10},... | collective-permute-start | bytes 98312 | tf_op jit(solution)/shard_map/ppermute | solution.py:564
  39.0 5.6 %collective-permute-start.8 = (f32[64,128]{1,0:T(8,128)S(1)}, f32[64,128]{1,0:T(8,128)S(1)}, u32[]{:S(2)}, u32[]{:S(2)}) collective-permute-start(f32[64,128]{1,0:T(8,128)S(1)} %get-tuple-element.48), channel_id=1, source_target_pairs={{0,4},{4,0},{8,12},{12,8},{1,5},{5,1},{9,13},{13,9},{2,6},{6,2},{1... | collective-permute-start | bytes 98312 | tf_op jit(solution)/shard_map/ppermute | solution.py:564
  40.3 4.8 %collective-permute-start.9 = (f32[64,128]{1,0:T(8,128)S(1)}, f32[64,128]{1,0:T(8,128)S(1)}, u32[]{:S(2)}, u32[]{:S(2)}) collective-permute-start(f32[64,128]{1,0:T(8,128)S(1)} %get-tuple-element.49), channel_id=1, source_target_pairs={{0,8},{4,12},{8,0},{12,4},{1,9},{5,13},{9,1},{13,5},{2,10},{6,14},... | collective-permute-start | bytes 98312 | tf_op jit(solution)/shard_map/ppermute | solution.py:564
  41.3 0.7 %copy-start.3 = (f32[20]{0:T(128)S(1)}, f32[20]{0:T(128)}, u32[]{:S(2)}) copy-start(f32[20]{0:T(128)} %half_ref.1) | copy-start | bytes 244
  41.3 0.7 %copy-start.4 = (f32[20]{0:T(128)S(1)}, f32[20]{0:T(128)}, u32[]{:S(2)}) copy-start(f32[20]{0:T(128)} %slope_ref.1) | copy-start | bytes 244
  41.3 0.7 %copy-start.5 = (f32[20]{0:T(128)S(1)}, f32[20]{0:T(128)}, u32[]{:S(2)}) copy-start(f32[20]{0:T(128)} %tau_ref.1) | copy-start | bytes 244
  42.0 3.1 %copy-start.2 = (f32[1,8192]{1,0:T(1,128)S(1)}, f32[1,8192]{1,0:T(1,128)}, u32[]{:S(2)}) copy-start(f32[1,8192]{1,0:T(1,128)} %param.18) | copy-start | bytes 98308

commit v5 on v4

--- a/solution.py
+++ b/solution.py
@@ -122,7 +122,7 @@
         face_ref[x] = jnp.where(keep_w, w_face, pltpu.roll(i_face, 4, 0))
 
 
-def x_faces_kernel(one, w0_ref, inv_ref, slab_ref, *refs):
+def x_faces_kernel(one, after_ref, w0_ref, inv_ref, slab_ref, *refs):
     if one:
         got_ref, halo_ref, first_ref, second_ref = refs
     else:
@@ -389,24 +389,11 @@
     leave.wait()
 
 
-def chunks_of(n_states, parts):
-    size = -(-n_states // parts)
-    return [(k, min(size, n_states - k)) for k in range(0, n_states, size)]
-
-
 def membrane_kernel(
-    half_ref, slope_ref, tau_ref, cond_ref, rev_ref, v_ref, gates_hbm, cot_hbm,
+    half_ref, slope_ref, tau_ref, cond_ref, rev_ref, after_ref, v_ref, gates_ref, cot_ref,
     base_ref, sum_ref, factor_ref, coef_ref,
-    gates_ref, cot_ref, sems,
 ):
     n_states, rows = gates_ref.shape[:2]
-    chunks = chunks_of(n_states, sems.shape[1])
-    copies = []
-    for part, (begin, size) in enumerate(chunks):
-        for k, (source, target) in enumerate(((gates_hbm, gates_ref), (cot_hbm, cot_ref))):
-            here = pl.ds(begin, size)
-            copies.append(pltpu.make_async_copy(source.at[here], target.at[here], sems.at[k, part]))
-            copies[-1].start()
     v = v_ref[...]
 
     def state(g, carry):
@@ -428,32 +415,22 @@
         coef_ref[1, pl.ds(g, 1)] = jnp.full((1, LANES), rev_ref[g])
         return total + cot * change, current + cond_ref[g] * gate
 
-    carry = (jnp.zeros((rows, LANES), F32),) * 2
-    for part, (begin, size) in enumerate(chunks):
-        copies[2 * part].wait()
-        copies[2 * part + 1].wait()
-        carry = lax.fori_loop(begin, begin + size, state, carry, unroll=True)
-    sum_ref[...] = carry[0]
-    factor_ref[...] = 1.0 - TIME_STEP * carry[1]
+    zero = jnp.zeros((rows, LANES), F32)
+    total, current = lax.fori_loop(0, n_states, state, (zero, zero), unroll=2)
+    sum_ref[...] = total
+    factor_ref[...] = 1.0 - TIME_STEP * current
 
 
 def finish_kernel(coef_ref, vcot_ref, v_ref, sum_ref, factor_ref, base_ref, *refs):
-    *landed_refs, volt_ref, gate_hbm, gate_ref, sems = refs
+    *landed_refs, volt_ref, gate_ref = refs
     landed = landed_refs[0][...]
     for ref in landed_refs[1:]:
         landed = landed + ref[...]
     cot = vcot_ref[...] + landed
     v = v_ref[...]
-    copies = []
-    for part, (begin, size) in enumerate(chunks_of(base_ref.shape[0], sems.shape[0])):
-        for g in range(begin, begin + size):
-            gate_ref[g] = base_ref[g] - (coef_ref[0, g : g + 1] * cot) * (v - coef_ref[1, g : g + 1])
-        here = pl.ds(begin, size)
-        copies.append(pltpu.make_async_copy(gate_ref.at[here], gate_hbm.at[here], sems.at[part]))
-        copies[-1].start()
     volt_ref[...] = cot * factor_ref[...] + sum_ref[...]
-    for copy in copies:
-        copy.wait()
+    for g in range(base_ref.shape[0]):
+        gate_ref[g] = base_ref[g] - (coef_ref[0, g : g + 1] * cot) * (v - coef_ref[1, g : g + 1])
 
 
 def both_ways(up, down, axis):
@@ -512,13 +489,12 @@
             shape_of(n_states, block_rows, LANES), shape_of(block_rows, LANES), shape_of(block_rows, LANES),
             shape_of(2, n_states, LANES),
         ),
-        8,
-        specs=[SMEM] * 5 + [VMEM] + [HBM] * 2,
-        scratch=[pltpu.VMEM((n_states, block_rows, LANES), F32)] * 2 + [pltpu.SemaphoreType.DMA((2, 4))],
+        9,
+        specs=[SMEM] * 5 + [VMEM] * 4,
         cost=6_000_000,
     )(
         half_voltage, gate_slope, tau_base, conductance, reversal,
-        cells(voltage), in_hbm(states(gates)), in_hbm(states(gates_cot)),
+        stat, cells(voltage), states(gates), states(gates_cot),
     )
     plan = call(plan_kernel, jax.ShapeDtypeStruct((rows, LANES), jnp.int32), 1, cost=6_000_000)(flat(tissue_label))
 
@@ -532,8 +508,8 @@
         slab, up, down = call(y_faces_kernel, (slab_shape, face, face), 4)(w0, inv, packed, got)
         halo = both_ways(up, down, "gy")
     edge_rows, first, second = call(
-        functools.partial(x_faces_kernel, n_gy == 2), x_shapes, 3 + len(halo)
-    )(w0, inv, slab, *halo)
+        functools.partial(x_faces_kernel, n_gy == 2), x_shapes, 4 + len(halo)
+    )(coefs, w0, inv, slab, *halo)
     first, second = pair_swaps(first, second, "gx")
 
     tall = ring + SUB
@@ -544,8 +520,9 @@
         7,
         scratch=[pltpu.VMEM((nx + 4, tall, nz), F32), pltpu.VMEM((1, tall, 2 * nz), F32)],
     )(w0, inv, slab, edge_rows, first, second, stat)
-    for axis in ("gz", "gy", "gx"):
+    for axis in ("gz", "gy"):
         sums = reduce_over(sums, axis)
+    sums = lax.psum(sums, "gx")
 
     solution, *blocks = call(
         functools.partial(combine_kernel, slot_rows),
@@ -568,8 +545,6 @@
         finish_kernel,
         (shape_of(block_rows, LANES), shape_of(n_states, block_rows, LANES)),
         6 + n_gx,
-        outs=(VMEM, HBM),
-        scratch=[pltpu.VMEM((n_states, block_rows, LANES), F32), pltpu.SemaphoreType.DMA((4,))],
     )(coefs, cells(voltage_cot), cells(voltage), total_change, factor, base, *landed)
     return solution, volt_grad.reshape(voltage.shape), gate_grad.reshape(gates.shape)
 

time: 46.8 us -> 47.1 us (level)
  blocking collectives: 0 us -> 13.2 us
  starting transfers between devices: 20.8 us -> 11.8 us
  waiting for transfers between devices: 10.8 us -> 8.07 us
  Pallas kernels: 13.6 us -> 12.4 us
    psum x0 -> x1, blocking collectives: none -> 13.2 us  [local(): sums = lax.psum(sums, 'gx')]
    ppermute x4 -> x2, starting transfers between devices: 10.3 us -> 1.5 us  [reduce_over(): lax.ppermute(value, axis, [(i, i ^ step) for i in range(count)])]
    ppermute x4 -> x2, waiting for transfers between devices: 4.64 us -> 1.65 us  [reduce_over(): lax.ppermute(value, axis, [(i, i ^ step) for i in range(count)])]
    ppermute x1, waiting for transfers between devices: 2.51 us -> 0.01 us  [local(): halo = (lax.ppermute(mine, 'gy', [(0, 1), (1, 0)]),)]
    ppermute x3, waiting for transfers between devices: 0.42 us -> 2.87 us  [local(): lax.ppermute(blocks[k], 'gx', [(i, i ^ k) for i in range(n_gx)])]
    pallas_call x1, Pallas kernels: 2.64 us -> 1.93 us  [local(): call(membrane_kernel, (shape_of(n_states, block_rows, LANES), shape_of(bl...]
    pallas_call x1, Pallas kernels: 1.52 us -> 0.94 us  [local(): call(finish_kernel, (shape_of(block_rows, LANES), shape_of(n_states, bloc...]
  transfers between devices with their start and end apart: 11 -> 9, of which waited for: 7 -> 6; matrix products, arithmetic and copies ran while one was open for 0% -> 0% of each run, Pallas kernels for 9% -> 8%
where the time goes in v5:
time: 47.1 us; the launch traced here: 46.9 us
  blocking collectives  13.2 us (28%)
  Pallas kernels  12.4 us (26%)
  starting transfers between devices  11.8 us (25%)
  waiting for transfers between devices  8.07 us (17%)
  between operations  0.77 us (2%)
  local copies, waits for them, and re-layouts  0.67 us (1%)
    psum x1, blocking collectives, local(): sums = lax.psum(sums, 'gx')  13.2 us
    ppermute x3, starting transfers between devices, local(): lax.ppermute(blocks[k], 'gx', [(i, i ^ k) for i in range(n_gx)])  4.45 us
    pallas_call x1, Pallas kernels, local(): call(stencil_kernel, (*basis, shape_of(3, tall, 2 * nz), shape_of(16, nz)...  4.07 us
    ppermute x1, starting transfers between devices, local(): halo = (lax.ppermute(mine, 'gy', [(0, 1), (1, 0)]),)  2.9 us
    ppermute x3, waiting for transfers between devices, local(): lax.ppermute(blocks[k], 'gx', [(i, i ^ k) for i in range(n_gx)])  2.87 us
    ppermute x1, waiting for transfers between devices, pair_swaps(): lax.ppermute(first, axis, even)  2.69 us
    pallas_call x1, Pallas kernels, local(): call(functools.partial(combine_kernel, slot_rows), (block,) + (shape_of(b...  2.06 us
    pallas_call x1, Pallas kernels, local(): call(membrane_kernel, (shape_of(n_states, block_rows, LANES), shape_of(bl...  1.93 us
  transfers between devices with their start and end apart: 9, of which 6 were waited for; matrix products, arithmetic and copies ran while one was open for 0% of the time, Pallas kernels for 8%

profile of v5, /device:TPU:0, one launch (start us, length us, event | category | flops | bytes accessed | tf_op | source)
XLA Modules:
  0.0 46.9 jit_solution(7544258786087321382)
XLA Ops:
  0.7 1.6 %shard_map.139 = (f32[16,32,128]{2,1,0:T(8,128)S(1)}, f32[16,32,128]{2,1,0:T(8,128)S(1)}, f32[2,32,128]{2,1,0:T(8,128)S(1)}, f32[2,8,128]{2,1,0:T(8,128)S(1)}) custom-call(f32[16,32,128]{2,1,0:T(8,128)} %right_hbm.1, f32[16,32,128]{2,1,0:T(8,128)} %damping_hbm.1, s32[16,32,128]{2,1,0:T(8,128)} %label_hbm.1), custom_call_target="tpu_custom_call" | custom-call | flops 2000000 | bytes 2000000 | tf_op jit(solution)/shard_map/pallas_call | solution.py:476
  2.2 0.5 %collective-permute-start = (f32[2,32,128]{2,1,0:T(8,128)S(1)}, f32[2,32,128]{2,1,0:T(8,128)S(1)}, u32[]{:S(2)}, u32[]{:S(2)}) collective-permute-start(f32[2,32,128]{2,1,0:T(8,128)S(1)} %get-tuple-element.30.own_ref), channel_id=1, source_target_pairs={{0,1},{1,0},{2,3},{3,2},{4,5},{5,4},{6,7},{7,6},{8,9},{9,8},{10,11... | collective-permute-start | bytes 98312 | tf_op jit(solution)/shard_map/ppermute | solution.py:485
  2.7 0.9 %collective-permute-done.got_ref = f32[2,32,128]{2,1,0:T(8,128)S(1)} collective-permute-done((f32[2,32,128]{2,1,0:T(8,128)S(1)}, f32[2,32,128]{2,1,0:T(8,128)S(1)}, u32[]{:S(2)}, u32[]{:S(2)}) %collective-permute-start) | collective-permute-done | bytes 32800 | tf_op jit(solution)/shard_map/ppermute | solution.py:485
  3.6 2.9 %collective-permute-start.1 = (f32[17,8,128]{2,1,0:T(8,128)S(1)}, f32[17,8,128]{2,1,0:T(8,128)S(1)}, u32[]{:S(2)}, u32[]{:S(2)}) collective-permute-start(f32[17,8,128]{2,1,0:T(8,128)S(1)} %get-tuple-element.34), channel_id=1, source_target_pairs={{0,2},{2,0},{1,3},{3,1},{4,6},{6,4},{5,7},{7,5},{8,10},{10,8},{9,1... | collective-permute-start | bytes 208904 | tf_op jit(solution)/shard_map/ppermute | solution.py:506
  6.6 0.6 %copy-done.5 = f32[20]{0:T(128)S(1)} copy-done((f32[20]{0:T(128)S(1)}, f32[20]{0:T(128)}, u32[]{:S(2)}) %copy-start.5) | copy-done | bytes 104
  7.2 1.9 %shard_map.141 = (f32[20,64,128]{2,1,0:T(8,128)S(1)}, f32[64,128]{1,0:T(8,128)S(1)}, f32[64,128]{1,0:T(8,128)S(1)}, f32[2,20,128]{2,1,0:T(8,128)S(1)}) custom-call(f32[20]{0:T(128)S(1)} %copy-done.5, f32[20]{0:T(128)S(1)} %copy-done.6, f32[20]{0:T(128)S(1)} %copy-done.7, f32[20]{0:T(128)S(1)} %copy-done.8, f32[20]{0:T(128)S(1)} %copy-done.9, ...), custom_call_target="tpu_custom_call" | custom-call | flops 6000000 | bytes 6000000 | tf_op jit(solution)/shard_map/pallas_call | solution.py:486
  9.2 0.1 shard_map.142
  9.3 1.8 %collective-permute-start.2 = (f32[6,40,128]{2,1,0:T(8,128)S(1)}, f32[6,40,128]{2,1,0:T(8,128)S(1)}, u32[]{:S(2)}, u32[]{:S(2)}) collective-permute-start(f32[6,40,128]{2,1,0:T(8,128)S(1)} %get-tuple-element.36), channel_id=1, source_target_pairs={{0,4},{4,0},{8,12},{12,8},{1,5},{5,1},{9,13},{13,9},{2,6},{6,2},{1... | collective-permute-start | bytes 368648 | tf_op jit(solution)/shard_map/ppermute | solution.py:448
  11.0 0.7 %collective-permute-start.3 = (f32[6,40,128]{2,1,0:T(8,128)S(1)}, f32[6,40,128]{2,1,0:T(8,128)S(1)}, u32[]{:S(2)}, u32[]{:S(2)}) collective-permute-start(f32[6,40,128]{2,1,0:T(8,128)S(1)} %get-tuple-element.37), channel_id=1, source_target_pairs={{4,8},{8,4},{5,9},{9,5},{6,10},{10,6},{7,11},{11,7},{20,24},{24,20... | collective-permute-start | bytes 368648 | tf_op jit(solution)/shard_map/ppermute | solution.py:448
  11.7 2.7 %collective-permute-done.2.first_ref = f32[6,40,128]{2,1,0:T(8,128)S(1)} collective-permute-done((f32[6,40,128]{2,1,0:T(8,128)S(1)}, f32[6,40,128]{2,1,0:T(8,128)S(1)}, u32[]{:S(2)}, u32[]{:S(2)}) %collective-permute-start.2) | collective-permute-done | bytes 122912 | tf_op jit(solution)/shard_map/ppermute | solution.py:448
  14.4 4.1 %shard_map.143 = (f32[22,48,128]{2,1,0:T(8,128)S(1)}, f32[20,48,128]{2,1,0:T(8,128)S(1)}, f32[18,48,128]{2,1,0:T(8,128)S(1)}, f32[3,48,256]{2,1,0:T(8,128)S(1)}, f32[16,128]{1,0:T(8,128)S(1)}) custom-call(f32[16,32,128]{2,1,0:T(8,128)S(1)} %get-tuple-element.28.w0_ref, f32[16,32,128]{2,1,0:T(8,128)S(1)} %get-tuple-element.29.inv_ref, ...), custom_call_target="tpu_custom_call" | custom-call | flops 2000000 | bytes 2000000 | tf_op jit(solution)/shard_map/pallas_call | solution.py:517
  18.5 0.1 collective-permute-start.4
  18.6 1.2 %collective-permute-done.4 = f32[16,128]{1,0:T(8,128)S(1)} collective-permute-done((f32[16,128]{1,0:T(8,128)S(1)}, f32[16,128]{1,0:T(8,128)S(1)}, u32[]{:S(2)}, u32[]{:S(2)}) %collective-permute-start.4) | collective-permute-done | bytes 8224 | tf_op jit(solution)/shard_map/ppermute | solution.py:455
  19.7 1.4 %collective-permute-start.5 = (f32[16,128]{1,0:T(8,128)S(1)}, f32[16,128]{1,0:T(8,128)S(1)}, u32[]{:S(2)}, u32[]{:S(2)}) collective-permute-start(f32[16,128]{1,0:T(8,128)S(1)} %add.8), channel_id=1, source_target_pairs={{0,2},{2,0},{1,3},{3,1},{4,6},{6,4},{5,7},{7,5},{8,10},{10,8},{9,1... | collective-permute-start | bytes 24584 | tf_op jit(solution)/shard_map/ppermute | solution.py:455
  21.2 1.7 %shard_map.144.plan_ref = s32[512,128]{1,0:T(8,128)S(1)} custom-call(s32[512,128]{1,0:T(8,128)S(1)} %bitcast.7), custom_call_target="tpu_custom_call" | custom-call | flops 6000000 | bytes 6000000 | tf_op jit(solution)/shard_map/pallas_call | solution.py:499
  22.9 0.5 %collective-permute-done.5 = f32[16,128]{1,0:T(8,128)S(1)} collective-permute-done((f32[16,128]{1,0:T(8,128)S(1)}, f32[16,128]{1,0:T(8,128)S(1)}, u32[]{:S(2)}, u32[]{:S(2)}) %collective-permute-start.5) | collective-permute-done | bytes 8224 | tf_op jit(solution)/shard_map/ppermute | solution.py:455
  23.4 13.2 %psum.7.total_ref = f32[16,128]{1,0:T(8,128)S(1)} all-reduce(f32[16,128]{1,0:T(8,128)S(1)} %add.9), channel_id=1, replica_groups=mesh['groups'=2,'gx'=4,'gy'=2,'gz'=2] {'gx'}, use_global_device_ids=true, to_apply=%region_0.0 | all-reduce | flops 2048 | bytes 16384 | tf_op jit(solution)/shard_map/psum | solution.py:525
  36.6 2.1 %shard_map.145 = (f32[16,32,128]{2,1,0:T(8,128)}, f32[64,128]{1,0:T(8,128)S(1)}, f32[64,128]{1,0:T(8,128)S(1)}, f32[64,128]{1,0:T(8,128)S(1)}, f32[64,128]{1,0:T(8,128)S(1)}) custom-call(f32[16,128]{1,0:T(8,128)S(1)} %psum.7.total_ref, f32[22,48,128]{2,1,0:T(8,128)S(1)} %get-tuple-element.39.w0_ref, f32[20,48,128]{2,1,0:T(8,128)S(1)} %get-tuple-element.40.w1_ref, ...), custom_call_target="tpu_custom_call" | custom-call | flops 2000000 | bytes 2000000 | tf_op jit(solution)/shard_map/pallas_call | solution.py:527
  38.6 1.0 %collective-permute-start.6 = (f32[64,128]{1,0:T(8,128)S(1)}, f32[64,128]{1,0:T(8,128)S(1)}, u32[]{:S(2)}, u32[]{:S(2)}) collective-permute-start(f32[64,128]{1,0:T(8,128)S(1)} %get-tuple-element.48), channel_id=1, source_target_pairs={{0,4},{4,0},{8,12},{12,8},{1,5},{5,1},{9,13},{13,9},{2,6},{6,2},{1... | collective-permute-start | bytes 98312 | tf_op jit(solution)/shard_map/ppermute | solution.py:541
  39.6 0.7 %collective-permute-start.7 = (f32[64,128]{1,0:T(8,128)S(1)}, f32[64,128]{1,0:T(8,128)S(1)}, u32[]{:S(2)}, u32[]{:S(2)}) collective-permute-start(f32[64,128]{1,0:T(8,128)S(1)} %get-tuple-element.49), channel_id=1, source_target_pairs={{0,8},{4,12},{8,0},{12,4},{1,9},{5,13},{9,1},{13,5},{2,10},{6,14},... | collective-permute-start | bytes 98312 | tf_op jit(solution)/shard_map/ppermute | solution.py:541
  40.2 2.8 %collective-permute-start.8 = (f32[64,128]{1,0:T(8,128)S(1)}, f32[64,128]{1,0:T(8,128)S(1)}, u32[]{:S(2)}, u32[]{:S(2)}) collective-permute-start(f32[64,128]{1,0:T(8,128)S(1)} %get-tuple-element.50), channel_id=1, source_target_pairs={{0,12},{4,8},{8,4},{12,0},{1,13},{5,9},{9,5},{13,1},{2,14},{6,10},... | collective-permute-start | bytes 98312 | tf_op jit(solution)/shard_map/ppermute | solution.py:541
  43.1 1.3 %collective-permute-done.7.refs_2_ = f32[64,128]{1,0:T(8,128)S(1)} collective-permute-done((f32[64,128]{1,0:T(8,128)S(1)}, f32[64,128]{1,0:T(8,128)S(1)}, u32[]{:S(2)}, u32[]{:S(2)}) %collective-permute-start.7) | collective-permute-done | bytes 32800 | tf_op jit(solution)/shard_map/ppermute | solution.py:541
  44.4 1.6 %collective-permute-done.8.refs_3_ = f32[64,128]{1,0:T(8,128)S(1)} collective-permute-done((f32[64,128]{1,0:T(8,128)S(1)}, f32[64,128]{1,0:T(8,128)S(1)}, u32[]{:S(2)}, u32[]{:S(2)}) %collective-permute-start.8) | collective-permute-done | bytes 32800 | tf_op jit(solution)/shard_map/ppermute | solution.py:541
  45.9 0.9 %shard_map.146 = (f32[64,128]{1,0:T(8,128)}, f32[20,64,128]{2,1,0:T(8,128)}) custom-call(f32[2,20,128]{2,1,0:T(8,128)S(1)} %get-tuple-element.33.after_ref.coef_ref, f32[64,128]{1,0:T(8,128)S(1)} %bitcast.12, f32[64,128]{1,0:T(8,128)S(1)} %bitcast.11, f32[64,128]{1,0:T(8,128)S(1)} %get-tuple-element.44.sum_ref, f32[64,128]{1,0:T(8,128)S(1)} %get-tuple-element.45.factor_ref, ...), custom_call_target="tpu_custom_call" | custom-call | flops 2000000 | bytes 2000000 | tf_op jit(solution)/shard_map/pallas_call | solution.py:544
  (25 shorter events, 0.1 us)
Async XLA Ops:
  0.6 5.9 %copy-start.1 = (f32[20,1,8192]{2,1,0:T(1,128)S(1)}, f32[20,1,8192]{2,1,0:T(1,128)}, u32[]{:S(2)}) copy-start(f32[20,1,8192]{2,1,0:T(1,128)} %param.17) | copy-start | bytes 1966084
  0.6 5.9 %copy-start.2 = (f32[20,1,8192]{2,1,0:T(1,128)S(1)}, f32[20,1,8192]{2,1,0:T(1,128)}, u32[]{:S(2)}) copy-start(f32[20,1,8192]{2,1,0:T(1,128)} %param.19) | copy-start | bytes 1966084
  2.2 1.4 %collective-permute-start = (f32[2,32,128]{2,1,0:T(8,128)S(1)}, f32[2,32,128]{2,1,0:T(8,128)S(1)}, u32[]{:S(2)}, u32[]{:S(2)}) collective-permute-start(f32[2,32,128]{2,1,0:T(8,128)S(1)} %get-tuple-element.30.own_ref), channel_id=1, source_target_pairs={{0,1},{1,0},{2,3},{3,2},{4,5},{5,4},{6,7},{7,6},{8,9},{9,8},{10,11... | collective-permute-start | bytes 98312 | tf_op jit(solution)/shard_map/ppermute | solution.py:485
  3.6 3.0 %copy-start.3 = (f32[1,8192]{1,0:T(1,128)S(1)}, f32[1,8192]{1,0:T(1,128)}, u32[]{:S(2)}) copy-start(f32[1,8192]{1,0:T(1,128)} %param.16) | copy-start | bytes 98308
  3.6 3.0 %copy-start.8 = (f32[20]{0:T(128)S(1)}, f32[20]{0:T(128)}, u32[]{:S(2)}) copy-start(f32[20]{0:T(128)} %cond_ref.1) | copy-start | bytes 244
  3.6 3.0 %copy-start.9 = (f32[20]{0:T(128)S(1)}, f32[20]{0:T(128)}, u32[]{:S(2)}) copy-start(f32[20]{0:T(128)} %rev_ref.1) | copy-start | bytes 244
  3.6 5.5 %collective-permute-start.1 = (f32[17,8,128]{2,1,0:T(8,128)S(1)}, f32[17,8,128]{2,1,0:T(8,128)S(1)}, u32[]{:S(2)}, u32[]{:S(2)}) collective-permute-start(f32[17,8,128]{2,1,0:T(8,128)S(1)} %get-tuple-element.34), channel_id=1, source_target_pairs={{0,2},{2,0},{1,3},{3,1},{4,6},{6,4},{5,7},{7,5},{8,10},{10,8},{9,1... | collective-permute-start | bytes 208904 | tf_op jit(solution)/shard_map/ppermute | solution.py:506
  6.5 0.7 %copy-start.5 = (f32[20]{0:T(128)S(1)}, f32[20]{0:T(128)}, u32[]{:S(2)}) copy-start(f32[20]{0:T(128)} %half_ref.1) | copy-start | bytes 244
  6.5 0.7 %copy-start.6 = (f32[20]{0:T(128)S(1)}, f32[20]{0:T(128)}, u32[]{:S(2)}) copy-start(f32[20]{0:T(128)} %slope_ref.1) | copy-start | bytes 244
  6.5 0.7 %copy-start.7 = (f32[20]{0:T(128)S(1)}, f32[20]{0:T(128)}, u32[]{:S(2)}) copy-start(f32[20]{0:T(128)} %tau_ref.1) | copy-start | bytes 244
  9.3 5.1 %collective-permute-start.2 = (f32[6,40,128]{2,1,0:T(8,128)S(1)}, f32[6,40,128]{2,1,0:T(8,128)S(1)}, u32[]{:S(2)}, u32[]{:S(2)}) collective-permute-start(f32[6,40,128]{2,1,0:T(8,128)S(1)} %get-tuple-element.36), channel_id=1, source_target_pairs={{0,4},{4,0},{8,12},{12,8},{1,5},{5,1},{9,13},{13,9},{2,6},{6,2},{1... | collective-permute-start | bytes 368648 | tf_op jit(solution)/shard_map/ppermute | solution.py:448
  11.0 3.4 %collective-permute-start.3 = (f32[6,40,128]{2,1,0:T(8,128)S(1)}, f32[6,40,128]{2,1,0:T(8,128)S(1)}, u32[]{:S(2)}, u32[]{:S(2)}) collective-permute-start(f32[6,40,128]{2,1,0:T(8,128)S(1)} %get-tuple-element.37), channel_id=1, source_target_pairs={{4,8},{8,4},{5,9},{9,5},{6,10},{10,6},{7,11},{11,7},{20,24},{24,20... | collective-permute-start | bytes 368648 | tf_op jit(solution)/shard_map/ppermute | solution.py:448
  14.4 6.7 %copy-start = (s32[16,32,128]{2,1,0:T(8,128)S(1)}, s32[16,32,128]{2,1,0:T(8,128)}, u32[]{:S(2)}) copy-start(s32[16,32,128]{2,1,0:T(8,128)} %label_hbm.1) | copy-start | bytes 786436
  18.5 1.2 %collective-permute-start.4 = (f32[16,128]{1,0:T(8,128)S(1)}, f32[16,128]{1,0:T(8,128)S(1)}, u32[]{:S(2)}, u32[]{:S(2)}) collective-permute-start(f32[16,128]{1,0:T(8,128)S(1)} %get-tuple-element.38), channel_id=1, source_target_pairs={{0,1},{1,0},{2,3},{3,2},{4,5},{5,4},{6,7},{7,6},{8,9},{9,8},{10,11... | collective-permute-start | bytes 24584 | tf_op jit(solution)/shard_map/ppermute | solution.py:455
  19.7 3.7 %collective-permute-start.5 = (f32[16,128]{1,0:T(8,128)S(1)}, f32[16,128]{1,0:T(8,128)S(1)}, u32[]{:S(2)}, u32[]{:S(2)}) collective-permute-start(f32[16,128]{1,0:T(8,128)S(1)} %add.8), channel_id=1, source_target_pairs={{0,2},{2,0},{1,3},{3,1},{4,6},{6,4},{5,7},{7,5},{8,10},{10,8},{9,1... | collective-permute-start | bytes 24584 | tf_op jit(solution)/shard_map/ppermute | solution.py:455
  36.5 9.4 %copy-start.4 = (f32[1,8192]{1,0:T(1,128)S(1)}, f32[1,8192]{1,0:T(1,128)}, u32[]{:S(2)}) copy-start(f32[1,8192]{1,0:T(1,128)} %param.18) | copy-start | bytes 98308
  38.6 4.5 %collective-permute-start.6 = (f32[64,128]{1,0:T(8,128)S(1)}, f32[64,128]{1,0:T(8,128)S(1)}, u32[]{:S(2)}, u32[]{:S(2)}) collective-permute-start(f32[64,128]{1,0:T(8,128)S(1)} %get-tuple-element.48), channel_id=1, source_target_pairs={{0,4},{4,0},{8,12},{12,8},{1,5},{5,1},{9,13},{13,9},{2,6},{6,2},{1... | collective-permute-start | bytes 98312 | tf_op jit(solution)/shard_map/ppermute | solution.py:541
  39.6 4.8 %collective-permute-start.7 = (f32[64,128]{1,0:T(8,128)S(1)}, f32[64,128]{1,0:T(8,128)S(1)}, u32[]{:S(2)}, u32[]{:S(2)}) collective-permute-start(f32[64,128]{1,0:T(8,128)S(1)} %get-tuple-element.49), channel_id=1, source_target_pairs={{0,8},{4,12},{8,0},{12,4},{1,9},{5,13},{9,1},{13,5},{2,10},{6,14},... | collective-permute-start | bytes 98312 | tf_op jit(solution)/shard_map/ppermute | solution.py:541
  40.2 5.7 %collective-permute-start.8 = (f32[64,128]{1,0:T(8,128)S(1)}, f32[64,128]{1,0:T(8,128)S(1)}, u32[]{:S(2)}, u32[]{:S(2)}) collective-permute-start(f32[64,128]{1,0:T(8,128)S(1)} %get-tuple-element.50), channel_id=1, source_target_pairs={{0,12},{4,8},{8,4},{12,0},{1,13},{5,9},{9,5},{13,1},{2,14},{6,10},... | collective-permute-start | bytes 98312 | tf_op jit(solution)/shard_map/ppermute | solution.py:541

commit v6 on v5

--- a/solution.py
+++ b/solution.py
@@ -160,12 +160,113 @@
         face_ref[5] = jnp.where(lower == 1, down, up)
 
 
-def stencil_kernel(
-    w0_ref, inv_ref, slab_ref, halo_ref, first_ref, second_ref, stat_ref,
-    a_ref, b_ref, c_ref, slabs_ref, total_ref,
-    i_ref, si_ref,
+def slab_step(v, s, inv):
+    width = v.shape[1]
+    across = pltpu.roll(v, PACK, 1) + pltpu.roll(v, width - PACK, 1)
+    q = v + 0.5 * (s + across)
+    if inv is None:
+        return q, None
+    total = (
+        pltpu.roll(q, 1, 1) + pltpu.roll(q, width - 1, 1) + s + across
+        + 0.5 * (pltpu.roll(s, PACK, 1) + pltpu.roll(s, width - PACK, 1))
+    )
+    return q, total * inv
+
+
+def along_z(q, half, column, gz):
+    nz = q.shape[1]
+    lane = lanes_of(q.shape)
+    entry = (nz - 1) * (1 - gz)
+    turn = lax.rem(entry - (column + 3 - gz) + 2 * nz, nz)
+    up = jnp.where(lane == nz - 1, 0.0, pltpu.roll(q, nz - 1, 1))
+    down = jnp.where(lane == 0, 0.0, pltpu.roll(q, 1, 1))
+    return up + down + jnp.where(lane == entry, pltpu.roll(half, turn, 1), 0.0)
+
+
+def sweep(stage, spans, nx, ny, nz, gz, get, get_inv, put, slab_q, sums):
+    margin = 2 - stage
+    start = SUB - margin
+    tiles = ny // SUB + (margin > 0)
+    own = subs_of((SUB, nz)) >= margin
+    parts = [[], []]
+    for tile in range(tiles):
+        row = start + SUB * tile
+        q_rows = slab_q[SUB * tile : SUB * tile + SUB]
+        acc = [jnp.zeros((SUB, nz), F32) for _ in range(2)]
+
+        def beside(x):
+            return get(x, row - 1) + get(x, row + 1)
+
+        for first, last in spans:
+            s_low, s_mid = beside(first - 1), beside(first)
+            v_low, v_mid = get(first - 1, row), get(first, row)
+            for x in range(first, last):
+                v_high, s_high = get(x + 1, row), beside(x + 1)
+                across = v_low + v_high
+                column = (PACK * x) % (2 * nz)
+                half = q_rows[:, column // nz * nz : column // nz * nz + nz]
+                rest = s_mid + across
+                total = along_z(v_mid + 0.5 * rest, half, column % nz, gz) + rest + 0.5 * (s_low + s_high)
+                if stage < 2:
+                    after = total * get_inv(x, row)
+                    put(x, row, after)
+                if 0 <= x < nx:
+                    acc[0] = acc[0] + v_mid * total
+                    if stage < 2:
+                        acc[1] = acc[1] + after * total
+                v_low, v_mid, s_low, s_mid = v_mid, v_high, s_mid, s_high
+        for k in range(2):
+            parts[k].append(acc[k])
+    for k in range(2 if stage < 2 else 1):
+        part = parts[k]
+        total = part[1]
+        for other in part[2 : ny // SUB]:
+            total = total + other
+        total = total + (jnp.where(own, part[0], part[-1]) if margin else part[0])
+        sums[2 * stage + k] = total
+
+
+def inner_kernel(
+    w0_ref, inv_ref, slab_ref, halo_ref, a_ref, i_ref, b_ref, c_ref, sum_ref, slabs_ref,
 ):
     nx, ny, nz = w0_ref.shape
+    gz = lax.axis_index("gz")
+    for x in range(nx):
+        for ref, own, halo in ((a_ref, w0_ref[x], halo_ref[0, x]), (i_ref, inv_ref[x], halo_ref[1, x])):
+            ref[x, :SUB] = halo
+            ref[x, SUB : SUB + ny] = own
+            ref[x, SUB + ny :] = halo
+    for k in range(2):
+        slabs_ref[3 * k, :SUB] = halo_ref[k, nx]
+        slabs_ref[3 * k, SUB : SUB + ny] = slab_ref[k]
+        slabs_ref[3 * k, SUB + ny :] = halo_ref[k, nx]
+    sums = {}
+    for stage in range(3):
+        source, target = (a_ref, b_ref, c_ref)[stage], (b_ref, c_ref, None)[stage]
+        start, size = SUB - 2 + stage, ny if stage == 2 else ny + SUB
+        v = slabs_ref[stage, start : start + size]
+        s = slabs_ref[stage, start - 1 : start - 1 + size] + slabs_ref[stage, start + 1 : start + 1 + size]
+        q, after = slab_step(v, s, slabs_ref[3, start : start + size] if stage < 2 else None)
+        if stage < 2:
+            slabs_ref[stage + 1, start : start + size] = after
+
+        def put(x, row, value):
+            target[x, row : row + SUB] = value
+
+        sweep(
+            stage, [(1 + stage, nx - 1 - stage)], nx, ny, nz, gz,
+            lambda x, row: source[x, row : row + SUB], lambda x, row: i_ref[x, row : row + SUB],
+            put, q, sums,
+        )
+    for k in range(5):
+        sum_ref[k] = sums[k]
+
+
+def outer_kernel(
+    a_ref, i_ref, b_ref, c_ref, slab_ref, halo_ref, sum_ref, first_ref, second_ref, stat_ref,
+    ea_ref, eb_ref, ec_ref, slabs_ref, total_ref, ei_ref, si_ref,
+):
+    nx, ny, nz = a_ref.shape[0], a_ref.shape[1] - 2 * SUB, a_ref.shape[2]
     ring = ny + SUB
     gz = lax.axis_index("gz")
     odd = lax.rem(lax.axis_index("gx"), 2) == 1
@@ -176,97 +277,58 @@
     def high(k):
         return jnp.where(odd, second_ref[k], first_ref[k])
 
-    def place(ref, x, own, halo):
-        ref[x, SUB : SUB + ny] = own
-        ref[x, :SUB] = halo
-        ref[x, SUB + ny :] = halo
-
-    for x in range(nx):
-        place(a_ref, 3 + x, w0_ref[x], halo_ref[0, x])
-        place(i_ref, 2 + x, inv_ref[x], halo_ref[1, x])
-    for k in range(3):
-        for x, plane in ((k, low(k)), (nx + 3 + k, high(k))):
-            place(a_ref, x, plane[:ny], plane[ny:])
-    for k in range(2):
-        for x, plane in ((k, low(3 + k)), (nx + 2 + k, high(3 + k))):
-            place(i_ref, x, plane[:ny], plane[ny:])
+    for ref, at, plane in (
+        [(ea_ref, k, low(k)) for k in range(3)] + [(ea_ref, 3 + k, high(k)) for k in range(3)]
+        + [(ei_ref, k, low(3 + k)) for k in range(2)] + [(ei_ref, 2 + k, high(3 + k)) for k in range(2)]
+    ):
+        ref[at, :SUB] = plane[ny:]
+        ref[at, SUB : SUB + ny] = plane[:ny]
+        ref[at, SUB + ny :] = plane[ny:]
 
     lane = lanes_of((ring, nz))
     lo5, hi5 = low(5), high(5)
     slab_w = jnp.where(lane < 3 * PACK, hi5, 0.0) + jnp.where(lane >= nz - 3 * PACK, lo5, 0.0)
     lo5, hi5 = pltpu.roll(lo5, nz // 2, 1), pltpu.roll(hi5, nz // 2, 1)
     slab_i = jnp.where(lane < 2 * PACK, hi5, 0.0) + jnp.where(lane >= nz - 2 * PACK, lo5, 0.0)
-    for ref, at, k, beyond in ((slabs_ref, 0, 0, slab_w), (si_ref, 0, 1, slab_i)):
-        ref[at, SUB : SUB + ny, :nz] = slab_ref[k]
-        ref[at, SUB : SUB + ny, nz:] = beyond[:ny]
+    for ref, k, beyond in ((slabs_ref, 0, slab_w), (si_ref, 1, slab_i)):
+        ref[0, SUB : SUB + ny, :nz] = slab_ref[k]
+        ref[0, SUB : SUB + ny, nz:] = beyond[:ny]
         for rows in (slice(0, SUB), slice(SUB + ny, SUB + ring)):
-            ref[at, rows, :nz] = halo_ref[k, nx]
-            ref[at, rows, nz:] = beyond[ny:]
+            ref[0, rows, :nz] = halo_ref[k, nx]
+            ref[0, rows, nz:] = beyond[ny:]
+
+    def reader(inside_ref, edge_ref, first, count):
+        def get(x, row):
+            if first <= x < nx - first:
+                return inside_ref[x, row : row + SUB]
+            at = x - (first - count) if x < first else x - (nx - first) + count
+            return edge_ref[at, row : row + SUB]
+
+        return get
 
     sums = {}
-
-    def add(name, value, skip):
-        value = value[skip : skip + ny]
-        part = value[:SUB]
-        for k in range(SUB, ny, SUB):
-            part = part + value[k : k + SUB]
-        sums[name] = part if name not in sums else sums[name] + part
-
-    def rows_of(ref, x, start, size):
-        return ref[x, start : start + size]
-
     for stage in range(3):
-        source = (a_ref, b_ref, c_ref)[stage]
-        target = (b_ref, c_ref, None)[stage]
-        margin = 2 - stage
-        start = SUB - margin
-        size = ny if margin == 0 else ring
-        lane = lanes_of((size, nz))
-        entry = (nz - 1) * gz
-        at_entry, lane_first, lane_last = lane == entry, lane == 0, lane == nz - 1
-
-        width = 2 * nz
+        get = reader((a_ref, b_ref, c_ref)[stage], (ea_ref, eb_ref, ec_ref)[stage], stage, 3)
+        start, size = SUB - 2 + stage, ny if stage == 2 else ring
         v = slabs_ref[stage, start : start + size]
         s = slabs_ref[stage, start - 1 : start - 1 + size] + slabs_ref[stage, start + 1 : start + 1 + size]
-        across = pltpu.roll(v, PACK, 1) + pltpu.roll(v, width - PACK, 1)
-        slab_q = v + 0.5 * (s + across)
+        q, after = slab_step(v, s, si_ref[0, start : start + size] if stage < 2 else None)
         if stage < 2:
-            total = (
-                pltpu.roll(slab_q, 1, 1) + pltpu.roll(slab_q, width - 1, 1) + s + across
-                + 0.5 * (pltpu.roll(s, PACK, 1) + pltpu.roll(s, width - PACK, 1))
-            )
-            slabs_ref[stage + 1, start : start + size] = total * si_ref[0, start : start + size]
-
-        def beside(x):
-            return rows_of(source, x, start - 1, size) + rows_of(source, x, start + 1, size)
-
-        s_low, s_mid = beside(0), beside(1)
-        v_low, v_mid = rows_of(source, 0, start, size), rows_of(source, 1, start, size)
-        for x in range(-margin, nx + margin):
-            at = x + margin + 1
-            v_high, s_high = rows_of(source, at + 1, start, size), beside(at + 1)
-            across = v_low + v_high
-            q = v_mid + 0.5 * (s_mid + across)
-            column = (PACK * x) % width
-            half = slab_q[:, column // nz * nz : column // nz * nz + nz]
-            turn = lax.rem(entry - (column % nz + 3 - gz) + 2 * nz, nz)
-            edge = jnp.where(at_entry, pltpu.roll(half, turn, 1), 0.0)
-            along = pltpu.roll(jnp.where(lane_first, edge, q), nz - 1, 1) + pltpu.roll(
-                jnp.where(lane_last, edge, q), 1, 1
-            )
-            total = along + s_mid + across + 0.5 * (s_low + s_high)
-            if target is not None:
-                after = total * rows_of(i_ref, x + 2, start, size)
-                target[x + margin, start : start + size] = after
-            if 0 <= x < nx:
-                add(2 * stage + 1, v_mid * total, margin)
-                if target is not None:
-                    add(2 * stage + 2, after * total, margin)
-            v_low, v_mid, s_low, s_mid = v_mid, v_high, s_mid, s_high
+            slabs_ref[stage + 1, start : start + size] = after
+
+        def put(x, row, value):
+            edge_ref = (eb_ref, ec_ref)[stage]
+            at = x - (stage - 2) if x < nx // 2 else x - (nx - 1 - stage) + 3
+            edge_ref[at, row : row + SUB] = value
+
+        sweep(
+            stage, [(stage - 2, stage + 1), (nx - 1 - stage, nx + 2 - stage)], nx, ny, nz, gz,
+            get, reader(i_ref, ei_ref, 0, 2), put, q, sums,
+        )
 
     total_ref[0:1] = stat_ref[0, 0:1]
-    for k in range(1, 6):
-        total_ref[k : k + 1] = jnp.sum(sums[k], axis=0, keepdims=True)
+    for k in range(5):
+        total_ref[k + 1 : k + 2] = jnp.sum(sums[k] + sum_ref[k], axis=0, keepdims=True)
     total_ref[6:8] = jnp.zeros((2, nz), F32)
     here = (lax.axis_index("gx") * lax.axis_size("gy") + lax.axis_index("gy")) * lax.axis_size("gz") + gz
     count = jnp.sum(stat_ref[1], axis=1, keepdims=True)
@@ -282,7 +344,7 @@
     return jnp.concatenate([v[amount // LANES :], v[: amount // LANES]], axis=0)
 
 
-def plan_kernel(label_ref, plan_ref):
+def plan_kernel(after_ref, label_ref, plan_ref):
     rows = label_ref.shape[0]
     lane = lanes_of((rows, LANES))
     row = subs_of((rows, LANES))
@@ -326,67 +388,87 @@
     return c0, c1, c2
 
 
-def combine_kernel(slot_rows, total_ref, w0_ref, w1_ref, w2_ref, slabs_ref, plan_ref, x_hbm, *refs):
-    *out_refs, wide_ref, x_ref, value_ref, buf_ref, sem = refs
-    nx, ny, nz = x_ref.shape
+def couple_kernel(stage, slot_rows, after_ref, inside_ref, edge_ref, slabs_ref, plan_ref, list_ref, value_ref):
+    nx, nz = inside_ref.shape[0], inside_ref.shape[2]
+    ny = inside_ref.shape[1] - 2 * SUB
     rows = nx * ny
+    gz = lax.axis_index("gz")
+
+    def get(x, row):
+        if stage <= x < nx - stage:
+            return inside_ref[x, row : row + SUB]
+        return edge_ref[x - (stage - 3) if x < stage else x - (nx - stage) + 3, row : row + SUB]
+
+    for tile in range(ny // SUB):
+        row = SUB + SUB * tile
+        slab = slabs_ref[stage, row : row + SUB, :nz]
+        v_low, v_mid = get(-1, row), get(0, row)
+        for x in range(nx):
+            v_high = get(x + 1, row)
+            beside = get(x, row - 1) + get(x, row + 1)
+            at = ny * x + SUB * tile
+            value_ref[at : at + SUB] = (
+                along_z(v_mid, slab, PACK * x, gz) + beside + (v_low + v_high) - 6.0 * v_mid
+            )
+            v_low, v_mid = v_mid, v_high
     lane = lanes_of((rows, LANES))
-    row = subs_of((rows, LANES))
-    sums = jnp.sum(total_ref[0:8], axis=1, keepdims=True)
-    t = [jnp.broadcast_to(sums[k : k + 1], (1, LANES)) for k in range(6)]
-    c0, c1, c2 = galerkin(t)
-    for x in range(nx + 2):
-        wide_ref[x] = c0 * w0_ref[x + 2] + c1 * w1_ref[x + 1] + c2 * w2_ref[x]
-    for x in range(nx):
-        x_ref[x] = wide_ref[x + 1, SUB : SUB + ny]
-    leave = pltpu.make_async_copy(x_ref, x_hbm, sem)
-    leave.start()
-
-    gz = lax.axis_index("gz")
-    own = slice(SUB, SUB + ny)
-    slab = c0 * slabs_ref[0, own, :nz] + c1 * slabs_ref[1, own, :nz] + c2 * slabs_ref[2, own, :nz]
-    column = lanes_of((ny, nz))
-    entry = (nz - 1) * gz
-    at_entry, lane_first, lane_last = column == entry, column == 0, column == nz - 1
-    for x in range(nx):
-        v = wide_ref[x + 1, own]
-        turn = lax.rem(entry - (PACK * x + 3 - gz) + 2 * nz, nz)
-        edge = jnp.where(at_entry, pltpu.roll(slab, turn, 1), 0.0)
-        along = pltpu.roll(jnp.where(lane_first, edge, v), nz - 1, 1) + pltpu.roll(
-            jnp.where(lane_last, edge, v), 1, 1
-        )
-        beside = wide_ref[x + 1, SUB - 1 : SUB - 1 + ny] + wide_ref[x + 1, SUB + 1 : SUB + 1 + ny]
-        across = wide_ref[x, own] + wide_ref[x + 2, own]
-        value_ref[ny * x : ny * x + ny] = along + beside + across - 6.0 * v
-
     value = value_ref[...]
     plan = plan_ref[...]
     step = 1
     while step < rows * LANES:
         value = jnp.where((plan & step) != 0, shift_left(value, step, lane), value)
         step *= 2
+    list_ref[...] = value[:slot_rows]
+
+
+def add_kernel(a_ref, b_ref, after_ref, out_ref):
+    out_ref[...] = a_ref[...] + b_ref[...]
+
+
+def place_kernel(n_sums, *refs):
+    sum_refs, refs = refs[:n_sums], refs[n_sums:]
+    list_refs, refs = refs[:3], refs[3:]
+    coef_ref, *out_refs, buf_ref = refs
+    total = sum_refs[0][...]
+    for ref in sum_refs[1:]:
+        total = total + ref[...]
+    sums = jnp.sum(total[0:8], axis=1, keepdims=True)
+    t = [jnp.broadcast_to(sums[k : k + 1], (1, LANES)) for k in range(6)]
+    coefs = galerkin(t)
+    for k in range(3):
+        coef_ref[k : k + 1] = coefs[k]
+    value = coefs[0] * list_refs[0][...] + coefs[1] * list_refs[1][...] + coefs[2] * list_refs[2][...]
+    slot_rows = value.shape[0]
     n_y, n_z = lax.axis_size("gy"), lax.axis_size("gz")
-    counts = total_ref[8:16]
+    counts = total[8:16]
     dev = lanes_of((SUB, LANES))
-    mine = lax.rem(dev, n_y * n_z) == lax.axis_index("gy") * n_z + gz
+    mine = lax.rem(dev, n_y * n_z) == lax.axis_index("gy") * n_z + lax.axis_index("gz")
     gx = lax.axis_index("gx")
     first = subs_of((SUB, LANES)) == 0
     offset = jnp.sum(jnp.where(first & mine & (dev < gx * n_y * n_z), counts, 0.0)).astype(jnp.int32)
     count = jnp.sum(jnp.where(first & mine & (dev // (n_y * n_z) == gx), counts, 0.0)).astype(jnp.int32)
-    slots = value[:slot_rows]
-    index = (row * LANES + lane)[:slot_rows]
-    slots = jnp.where(index < count, slots, 0.0)
+    shape = (slot_rows, LANES)
+    slots = jnp.where(subs_of(shape) * LANES + lanes_of(shape) < count, value, 0.0)
     slots = jnp.concatenate([slots, jnp.zeros((SUB, LANES), F32)], axis=0)
     inner = lax.rem(offset, LANES)
     turned = pltpu.roll(slots, inner, 1)
     above = pltpu.roll(turned, 1, 0)
-    moved = jnp.where(lane[: slot_rows + SUB] >= inner, turned, above)
+    moved = jnp.where(lanes_of((slot_rows + SUB, LANES)) >= inner, turned, above)
     buf_ref[...] = jnp.zeros_like(buf_ref)
     buf_ref[pl.ds(offset // LANES, slot_rows + SUB), :] = moved
     for k, out_ref in enumerate(out_refs):
         size = out_ref.shape[0]
         out_ref[...] = buf_ref[pl.ds(pl.multiple_of((gx ^ k) * size, SUB), size), :]
-    leave.wait()
+
+
+def potential_kernel(coef_ref, a_ref, b_ref, c_ref, eb_ref, ec_ref, x_ref):
+    nx, ny, nz = x_ref.shape
+    own = slice(SUB, SUB + ny)
+    c0, c1, c2 = [coef_ref[k : k + 1] for k in range(3)]
+    for x in range(nx):
+        w1 = b_ref[x, own] if 1 <= x < nx - 1 else eb_ref[2 if x == 0 else 3, own]
+        w2 = c_ref[x, own] if 2 <= x < nx - 2 else ec_ref[x + 1 if x < 2 else x - (nx - 2) + 3, own]
+        x_ref[x] = c0 * a_ref[x, own] + c1 * w1 + c2 * w2
 
 
 def membrane_kernel(
@@ -483,20 +565,9 @@
     )(in_hbm(potential_cot), in_hbm(damping), in_hbm(tissue_label))
 
     got = lax.ppermute(packed, "gz", [(0, 1), (1, 0)])
-    base, total_change, factor, coefs = call(
-        membrane_kernel,
-        (
-            shape_of(n_states, block_rows, LANES), shape_of(block_rows, LANES), shape_of(block_rows, LANES),
-            shape_of(2, n_states, LANES),
-        ),
-        9,
-        specs=[SMEM] * 5 + [VMEM] * 4,
-        cost=6_000_000,
-    )(
-        half_voltage, gate_slope, tau_base, conductance, reversal,
-        stat, cells(voltage), states(gates), states(gates_cot),
+    plan = call(plan_kernel, jax.ShapeDtypeStruct((rows, LANES), jnp.int32), 2, cost=6_000_000)(
+        stat, flat(tissue_label)
     )
-    plan = call(plan_kernel, jax.ShapeDtypeStruct((rows, LANES), jnp.int32), 1, cost=6_000_000)(flat(tissue_label))
 
     face = shape_of(nx + 1, SUB, nz)
     slab_shape = shape_of(2, ny, nz)
@@ -509,43 +580,80 @@
         halo = both_ways(up, down, "gy")
     edge_rows, first, second = call(
         functools.partial(x_faces_kernel, n_gy == 2), x_shapes, 4 + len(halo)
-    )(coefs, w0, inv, slab, *halo)
+    )(plan, w0, inv, slab, *halo)
     first, second = pair_swaps(first, second, "gx")
 
     tall = ring + SUB
-    basis = [shape_of(nx + 2 * k, tall, nz) for k in (3, 2, 1)]
-    wide0, wide1, wide2, slabs, sums = call(
-        stencil_kernel,
-        (*basis, shape_of(3, tall, 2 * nz), shape_of(16, nz)),
-        7,
-        scratch=[pltpu.VMEM((nx + 4, tall, nz), F32), pltpu.VMEM((1, tall, 2 * nz), F32)],
-    )(w0, inv, slab, edge_rows, first, second, stat)
-    for axis in ("gz", "gy"):
-        sums = reduce_over(sums, axis)
-    sums = lax.psum(sums, "gx")
-
-    solution, *blocks = call(
-        functools.partial(combine_kernel, slot_rows),
-        (block,) + (shape_of(block_rows, LANES),) * n_gx,
-        6,
-        outs=(HBM,) + (VMEM,) * n_gx,
-        scratch=[
-            pltpu.VMEM((nx + 2, tall, nz), F32),
-            pltpu.VMEM((nx, ny, nz), F32),
-            pltpu.VMEM((rows, LANES), F32),
-            pltpu.VMEM((n_gx * block_rows + slot_rows + SUB, LANES), F32),
-            pltpu.SemaphoreType.DMA(()),
-        ],
-    )(sums, wide0, wide1, wide2, slabs, plan)
+    planes = shape_of(nx, tall, nz)
+    edges = shape_of(6, tall, nz)
+    in0, in_inv, in1, in2, in_sums = call(
+        inner_kernel,
+        (planes,) * 4 + (shape_of(5, SUB, nz),),
+        4,
+        scratch=[pltpu.VMEM((4, tall, nz), F32)],
+        cost=6_000_000,
+    )(w0, inv, slab, edge_rows)
+    ends0, ends1, ends2, slabs, sums = call(
+        outer_kernel,
+        (edges,) * 3 + (shape_of(3, tall, 2 * nz), shape_of(16, nz)),
+        10,
+        scratch=[pltpu.VMEM((4, tall, nz), F32), pltpu.VMEM((1, tall, 2 * nz), F32)],
+    )(in0, in_inv, in1, in2, slab, edge_rows, in_sums, first, second, stat)
+
+    def couple(stage, after, inside, ends):
+        return call(
+            functools.partial(couple_kernel, stage, slot_rows),
+            shape_of(slot_rows, LANES),
+            5,
+            scratch=[pltpu.VMEM((rows, LANES), F32)],
+            cost=6_000_000,
+        )(after, inside, ends, slabs, plan)
+
+    def add(value, axis, step, after):
+        got = lax.ppermute(value, axis, [(i, i ^ step) for i in range(lax.axis_size(axis))])
+        return call(add_kernel, shape_of(16, nz), 3)(value, got, after)
+
+    list0 = couple(0, sums, in0, ends0)
+    sums = add(sums, "gz", 1, list0)
+    list1 = couple(1, sums, in1, ends1)
+    sums = add(sums, "gy", 1, list1)
+    for step in [2**k for k in range(1, n_gy.bit_length() - 1)]:
+        sums = add(sums, "gy", step, list1)
+    list2 = couple(2, sums, in2, ends2)
+    if n_gx <= 4:
+        sums = [sums] + [lax.ppermute(sums, "gx", [(i, i ^ k) for i in range(n_gx)]) for k in range(1, n_gx)]
+    else:
+        sums = [reduce_over(sums, "gx")]
+
+    coefs, *blocks = call(
+        functools.partial(place_kernel, len(sums)),
+        (shape_of(SUB, LANES),) + (shape_of(block_rows, LANES),) * n_gx,
+        len(sums) + 3,
+        scratch=[pltpu.VMEM((n_gx * block_rows + slot_rows + SUB, LANES), F32)],
+    )(*sums, list0, list1, list2)
     landed = blocks[:1] + [
         lax.ppermute(blocks[k], "gx", [(i, i ^ k) for i in range(n_gx)]) for k in range(1, n_gx)
     ]
 
+    solution = call(potential_kernel, block, 6)(coefs, in0, in1, in2, ends1, ends2)
+    base, total_change, factor, state_coefs = call(
+        membrane_kernel,
+        (
+            shape_of(n_states, block_rows, LANES), shape_of(block_rows, LANES), shape_of(block_rows, LANES),
+            shape_of(2, n_states, LANES),
+        ),
+        9,
+        specs=[SMEM] * 5 + [VMEM] * 4,
+        cost=6_000_000,
+    )(
+        half_voltage, gate_slope, tau_base, conductance, reversal,
+        coefs, cells(voltage), states(gates), states(gates_cot),
+    )
     volt_grad, gate_grad = call(
         finish_kernel,
         (shape_of(block_rows, LANES), shape_of(n_states, block_rows, LANES)),
         6 + n_gx,
-    )(coefs, cells(voltage_cot), cells(voltage), total_change, factor, base, *landed)
+    )(state_coefs, cells(voltage_cot), cells(voltage), total_change, factor, base, *landed)
     return solution, volt_grad.reshape(voltage.shape), gate_grad.reshape(gates.shape)
 
 

time: 47.1 us -> 40.3 us (0.86)
  blocking collectives: 13.2 us -> 0 us
  starting transfers between devices: 11.8 us -> 19.3 us
  waiting for transfers between devices: 8.07 us -> 6.85 us
    psum x1 -> x0, blocking collectives: 13.2 us -> none  [local(): sums = lax.psum(sums, 'gx')]
    ppermute x2 -> x5, starting transfers between devices: 1.5 us -> 8.86 us  [the longest x3 6.92 us: local(): lax.ppermute(sums, 'gx', [(i, i ^ k) for i in range(n_gx)])]
    ppermute x3, waiting for transfers between devices: 2.87 us -> 1.29 us  [local(): lax.ppermute(blocks[k], 'gx', [(i, i ^ k) for i in range(n_gx)])]
    ppermute x1, waiting for transfers between devices: 2.69 us -> 1.38 us  [pair_swaps(): lax.ppermute(first, axis, even)]
    ppermute x2 -> x5, waiting for transfers between devices: 1.65 us -> 2.54 us  [the longest x3 1.89 us: local(): lax.ppermute(sums, 'gx', [(i, i ^ k) for i in range(n_gx)])]
    ppermute x1, waiting for transfers between devices: 0.01 us -> 0.78 us  [local(): halo = (lax.ppermute(mine, 'gy', [(0, 1), (1, 0)]),)]
    pallas_call x3 -> x10, Pallas kernels: 7.84 us -> 7.92 us  [the longest x3 3.57 us: couple(): call(functools.partial(couple_kernel, stage, slot_rows), shape_of(slot_ro...]
  transfers between devices with their start and end apart: 9 -> 12, of which waited for: 6 -> 7; matrix products, arithmetic and copies ran while one was open for 0% -> 0% of each run, Pallas kernels for 8% -> 22%
where the time goes in v6:
time: 40.3 us; the launch traced here: 40.1 us
  starting transfers between devices  19.3 us (48%)
  Pallas kernels  12.4 us (31%)
  waiting for transfers between devices  6.85 us (17%)
  local copies, waits for them, and re-layouts  0.8 us (2%)
  between operations  0.77 us (2%)
    ppermute x3, starting transfers between devices, local(): lax.ppermute(sums, 'gx', [(i, i ^ k) for i in range(n_gx)])  6.92 us
    ppermute x3, starting transfers between devices, local(): lax.ppermute(blocks[k], 'gx', [(i, i ^ k) for i in range(n_gx)])  4.45 us
    pallas_call x3, Pallas kernels, couple(): call(functools.partial(couple_kernel, stage, slot_rows), shape_of(slot_ro...  3.57 us
    ppermute x1, starting transfers between devices, local(): halo = (lax.ppermute(mine, 'gy', [(0, 1), (1, 0)]),)  2.9 us
    ppermute x2, starting transfers between devices, add(): lax.ppermute(value, axis, [(i, i ^ step) for i in range(lax.axis_size(axi...  1.94 us
    pallas_call x1, Pallas kernels, local(): call(membrane_kernel, (shape_of(n_states, block_rows, LANES), shape_of(bl...  1.92 us
    ppermute x1, starting transfers between devices, pair_swaps(): lax.ppermute(first, axis, even)  1.92 us
    ppermute x3, waiting for transfers between devices, local(): lax.ppermute(sums, 'gx', [(i, i ^ k) for i in range(n_gx)])  1.89 us
  transfers between devices with their start and end apart: 12, of which 7 were waited for; matrix products, arithmetic and copies ran while one was open for 0% of the time, Pallas kernels for 22%

profile of v6, /device:TPU:0, one launch (start us, length us, event | category | flops | bytes accessed | tf_op | source)
XLA Modules:
  0.0 40.1 jit_solution(18346626561564745339)
XLA Ops:
  0.6 1.5 %shard_map.139 = (f32[16,32,128]{2,1,0:T(8,128)S(1)}, f32[16,32,128]{2,1,0:T(8,128)S(1)}, f32[2,32,128]{2,1,0:T(8,128)S(1)}, f32[2,8,128]{2,1,0:T(8,128)S(1)}) custom-call(f32[16,32,128]{2,1,0:T(8,128)} %right_hbm.1, f32[16,32,128]{2,1,0:T(8,128)} %damping_hbm.1, s32[16,32,128]{2,1,0:T(8,128)} %label_hbm.1), custom_call_target="tpu_custom_call" | custom-call | flops 2000000 | bytes 2000000 | tf_op jit(solution)/shard_map/pallas_call | solution.py:558
  2.6 0.9 %collective-permute-done.got_ref = f32[2,32,128]{2,1,0:T(8,128)S(1)} collective-permute-done((f32[2,32,128]{2,1,0:T(8,128)S(1)}, f32[2,32,128]{2,1,0:T(8,128)S(1)}, u32[]{:S(2)}, u32[]{:S(2)}) %collective-permute-start) | collective-permute-done | bytes 32800 | tf_op jit(solution)/shard_map/ppermute | solution.py:567
  3.5 2.9 %collective-permute-start.1 = (f32[17,8,128]{2,1,0:T(8,128)S(1)}, f32[17,8,128]{2,1,0:T(8,128)S(1)}, u32[]{:S(2)}, u32[]{:S(2)}) collective-permute-start(f32[17,8,128]{2,1,0:T(8,128)S(1)} %get-tuple-element.38), channel_id=1, source_target_pairs={{0,2},{2,0},{1,3},{3,1},{4,6},{6,4},{5,7},{7,5},{8,10},{10,8},{9,1... | collective-permute-start | bytes 208904 | tf_op jit(solution)/shard_map/ppermute | solution.py:577
  6.4 1.7 %shard_map.141.after_ref.plan_ref = s32[512,128]{1,0:T(8,128)S(1)} custom-call(f32[2,8,128]{2,1,0:T(8,128)S(1)} %get-tuple-element.37.after_ref.stat_ref, s32[512,128]{1,0:T(8,128)S(1)} %bitcast.7), custom_call_target="tpu_custom_call" | custom-call | flops 6000000 | bytes 6000000 | tf_op jit(solution)/shard_map/pallas_call | solution.py:568
  8.1 0.8 %collective-permute-done.1.refs_0_ = f32[17,8,128]{2,1,0:T(8,128)S(1)} collective-permute-done((f32[17,8,128]{2,1,0:T(8,128)S(1)}, f32[17,8,128]{2,1,0:T(8,128)S(1)}, u32[]{:S(2)}, u32[]{:S(2)}) %collective-permute-start.1) | collective-permute-done | bytes 69664 | tf_op jit(solution)/shard_map/ppermute | solution.py:577
  9.0 1.9 %collective-permute-start.2 = (f32[6,40,128]{2,1,0:T(8,128)S(1)}, f32[6,40,128]{2,1,0:T(8,128)S(1)}, u32[]{:S(2)}, u32[]{:S(2)}) collective-permute-start(f32[6,40,128]{2,1,0:T(8,128)S(1)} %get-tuple-element.45), channel_id=1, source_target_pairs={{0,4},{4,0},{8,12},{12,8},{1,5},{5,1},{9,13},{13,9},{2,6},{6,2},{1... | collective-permute-start | bytes 368648 | tf_op jit(solution)/shard_map/ppermute | solution.py:530
  10.9 0.7 %collective-permute-start.3 = (f32[6,40,128]{2,1,0:T(8,128)S(1)}, f32[6,40,128]{2,1,0:T(8,128)S(1)}, u32[]{:S(2)}, u32[]{:S(2)}) collective-permute-start(f32[6,40,128]{2,1,0:T(8,128)S(1)} %get-tuple-element.46), channel_id=1, source_target_pairs={{4,8},{8,4},{5,9},{9,5},{6,10},{10,6},{7,11},{11,7},{20,24},{24,20... | collective-permute-start | bytes 368648 | tf_op jit(solution)/shard_map/ppermute | solution.py:530
  11.6 0.9 %shard_map.143 = (f32[16,48,128]{2,1,0:T(8,128)S(1)}, f32[16,48,128]{2,1,0:T(8,128)S(1)}, f32[16,48,128]{2,1,0:T(8,128)S(1)}, f32[16,48,128]{2,1,0:T(8,128)S(1)}, f32[5,8,128]{2,1,0:T(8,128)S(1)}) custom-call(f32[16,32,128]{2,1,0:T(8,128)S(1)} %get-tuple-element.33.w0_ref, f32[16,32,128]{2,1,0:T(8,128)S(1)} %get-tuple-element.34.inv_ref, ...), custom_call_target="tpu_custom_call" | custom-call | flops 6000000 | bytes 6000000 | tf_op jit(solution)/shard_map/pallas_call | solution.py:589
  12.5 1.4 %collective-permute-done.2.first_ref = f32[6,40,128]{2,1,0:T(8,128)S(1)} collective-permute-done((f32[6,40,128]{2,1,0:T(8,128)S(1)}, f32[6,40,128]{2,1,0:T(8,128)S(1)}, u32[]{:S(2)}, u32[]{:S(2)}) %collective-permute-start.2) | collective-permute-done | bytes 122912 | tf_op jit(solution)/shard_map/ppermute | solution.py:530
  13.9 0.7 %shard_map.144 = (f32[6,48,128]{2,1,0:T(8,128)S(1)}, f32[6,48,128]{2,1,0:T(8,128)S(1)}, f32[6,48,128]{2,1,0:T(8,128)S(1)}, f32[3,48,256]{2,1,0:T(8,128)S(1)}, f32[16,128]{1,0:T(8,128)S(1)}) custom-call(f32[16,48,128]{2,1,0:T(8,128)S(1)} %get-tuple-element.40.a_ref.inside_ref, f32[16,48,128]{2,1,0:T(8,128)S(1)} %get-tuple-element.41.i_ref, ...), custom_call_target="tpu_custom_call" | custom-call | flops 2000000 | bytes 2000000 | tf_op jit(solution)/shard_map/pallas_call | solution.py:596
  14.7 1.2 %shard_map.145.after_ref.refs_4_ = f32[160,128]{1,0:T(8,128)S(1)} custom-call(f32[16,128]{1,0:T(8,128)S(1)} %get-tuple-element.47.after_ref.a_ref, f32[16,48,128]{2,1,0:T(8,128)S(1)} %get-tuple-element.40.a_ref.inside_ref, f32[6,48,128]{2,1,0:T(8,128)S(1)} %get-tuple-element.48.edge_ref, f32[3,48,256]{2,1,0:T(8,128)S(1)} %get-tuple-element.49.slabs_ref, ...), custom_call_target="tpu_custom_call" | custom-call | flops 6000000 | bytes 6000000 | tf_op jit(solution)/shard_map/pallas_call | solution.py:604
  15.9 1.9 %collective-permute-start.5 = (f32[16,128]{1,0:T(8,128)S(1)}, f32[16,128]{1,0:T(8,128)S(1)}, u32[]{:S(2)}, u32[]{:S(2)}) collective-permute-start(f32[16,128]{1,0:T(8,128)S(1)} %shard_map.146.after_ref.a_ref), channel_id=1, source_target_pairs={{0,2},{2,0},{1,3},{3,1},{4,6},{6,4},{5,7},{7,5},{8,10},{10,8},{9,1... | collective-permute-start | bytes 24584 | tf_op jit(solution)/shard_map/ppermute | solution.py:613
  17.8 1.2 %shard_map.147.after_ref.refs_5_ = f32[160,128]{1,0:T(8,128)S(1)} custom-call(f32[16,128]{1,0:T(8,128)S(1)} %shard_map.146.after_ref.a_ref, f32[16,48,128]{2,1,0:T(8,128)S(1)} %get-tuple-element.42.b_ref.inside_ref, f32[6,48,128]{2,1,0:T(8,128)S(1)} %get-tuple-element.50.edge_ref.eb_ref, f32[3,48,256]{2,1,0:T(8,128)S(1)} %get-tuple-element.49.slabs_ref, ...), custom_call_target="tpu_custom_call" | custom-call | flops 6000000 | bytes 6000000 | tf_op jit(solution)/shard_map/pallas_call | solution.py:604
  19.6 3.9 %collective-permute-start.8 = (f32[16,128]{1,0:T(8,128)S(1)}, f32[16,128]{1,0:T(8,128)S(1)}, u32[]{:S(2)}, u32[]{:S(2)}) collective-permute-start(f32[16,128]{1,0:T(8,128)S(1)} %shard_map.148.after_ref.refs_0_), channel_id=1, source_target_pairs={{0,12},{4,8},{8,4},{12,0},{1,13},{5,9},{9,5},{13,1},{2,14},{6,10},... | collective-permute-start | bytes 24584 | tf_op jit(solution)/shard_map/ppermute | solution.py:624
  23.5 2.5 %collective-permute-start.7 = (f32[16,128]{1,0:T(8,128)S(1)}, f32[16,128]{1,0:T(8,128)S(1)}, u32[]{:S(2)}, u32[]{:S(2)}) collective-permute-start(f32[16,128]{1,0:T(8,128)S(1)} %shard_map.148.after_ref.refs_0_), channel_id=1, source_target_pairs={{0,8},{4,12},{8,0},{12,4},{1,9},{5,13},{9,1},{13,5},{2,10},{6,14},... | collective-permute-start | bytes 24584 | tf_op jit(solution)/shard_map/ppermute | solution.py:624
  26.5 1.2 %shard_map.149.refs_6_ = f32[160,128]{1,0:T(8,128)S(1)} custom-call(f32[16,128]{1,0:T(8,128)S(1)} %shard_map.148.after_ref.refs_0_, f32[16,48,128]{2,1,0:T(8,128)S(1)} %get-tuple-element.43.c_ref.inside_ref, f32[6,48,128]{2,1,0:T(8,128)S(1)} %get-tuple-element.51.edge_ref.ec_ref, f32[3,48,256]{2,1,0:T(8,128)S(1)} %get-tuple-element.49.slabs_ref, ...), custom_call_target="tpu_custom_call" | custom-call | flops 6000000 | bytes 6000000 | tf_op jit(solution)/shard_map/pallas_call | solution.py:604
  28.1 1.6 %collective-permute-done.6.refs_1_ = f32[16,128]{1,0:T(8,128)S(1)} collective-permute-done((f32[16,128]{1,0:T(8,128)S(1)}, f32[16,128]{1,0:T(8,128)S(1)}, u32[]{:S(2)}, u32[]{:S(2)}) %collective-permute-start.6) | collective-permute-done | bytes 8224 | tf_op jit(solution)/shard_map/ppermute | solution.py:624
  29.9 1.5 %collective-permute-start.9 = (f32[64,128]{1,0:T(8,128)S(1)}, f32[64,128]{1,0:T(8,128)S(1)}, u32[]{:S(2)}, u32[]{:S(2)}) collective-permute-start(f32[64,128]{1,0:T(8,128)S(1)} %get-tuple-element.58), channel_id=1, source_target_pairs={{0,4},{4,0},{8,12},{12,8},{1,5},{5,1},{9,13},{13,9},{2,6},{6,2},{1... | collective-permute-start | bytes 98312 | tf_op jit(solution)/shard_map/ppermute | solution.py:635
  31.4 2.0 %collective-permute-start.10 = (f32[64,128]{1,0:T(8,128)S(1)}, f32[64,128]{1,0:T(8,128)S(1)}, u32[]{:S(2)}, u32[]{:S(2)}) collective-permute-start(f32[64,128]{1,0:T(8,128)S(1)} %get-tuple-element.59), channel_id=1, source_target_pairs={{0,8},{4,12},{8,0},{12,4},{1,9},{5,13},{9,1},{13,5},{2,10},{6,14},... | collective-permute-start | bytes 98312 | tf_op jit(solution)/shard_map/ppermute | solution.py:635
  33.4 0.9 %collective-permute-start.11 = (f32[64,128]{1,0:T(8,128)S(1)}, f32[64,128]{1,0:T(8,128)S(1)}, u32[]{:S(2)}, u32[]{:S(2)}) collective-permute-start(f32[64,128]{1,0:T(8,128)S(1)} %get-tuple-element.60), channel_id=1, source_target_pairs={{0,12},{4,8},{8,4},{12,0},{1,13},{5,9},{9,5},{13,1},{2,14},{6,10},... | collective-permute-start | bytes 98312 | tf_op jit(solution)/shard_map/ppermute | solution.py:635
  34.4 0.8 %shard_map.151 = f32[16,32,128]{2,1,0:T(8,128)} custom-call(f32[8,128]{1,0:T(8,128)S(1)} %get-tuple-element.52.coef_ref.after_ref, f32[16,48,128]{2,1,0:T(8,128)S(1)} %get-tuple-element.40.a_ref.inside_ref, f32[16,48,128]{2,1,0:T(8,128)S(1)} %get-tuple-element.42.b_ref.inside_ref, f32[16,48,128]{2,1,0:T(8,128)S(1)} %get-tuple-element.43.c_ref.inside_ref, ...), custom_call_target="tpu_custom_call" | custom-call | flops 2000000 | bytes 2000000 | tf_op jit(solution)/shard_map/pallas_call | solution.py:638
  35.9 1.9 %shard_map.152 = (f32[20,64,128]{2,1,0:T(8,128)S(1)}, f32[64,128]{1,0:T(8,128)S(1)}, f32[64,128]{1,0:T(8,128)S(1)}, f32[2,20,128]{2,1,0:T(8,128)S(1)}) custom-call(f32[20]{0:T(128)S(1)} %copy-done.5, f32[20]{0:T(128)S(1)} %copy-done.6, f32[20]{0:T(128)S(1)} %copy-done.7, f32[20]{0:T(128)S(1)} %copy-done.8, f32[20]{0:T(128)S(1)} %copy-done.9, ...), custom_call_target="tpu_custom_call" | custom-call | flops 6000000 | bytes 6000000 | tf_op jit(solution)/shard_map/pallas_call | solution.py:639
  37.9 1.3 %collective-permute-done.11.refs_3_ = f32[64,128]{1,0:T(8,128)S(1)} collective-permute-done((f32[64,128]{1,0:T(8,128)S(1)}, f32[64,128]{1,0:T(8,128)S(1)}, u32[]{:S(2)}, u32[]{:S(2)}) %collective-permute-start.11) | collective-permute-done | bytes 32800 | tf_op jit(solution)/shard_map/ppermute | solution.py:635
  39.1 0.9 %shard_map.153 = (f32[64,128]{1,0:T(8,128)}, f32[20,64,128]{2,1,0:T(8,128)}) custom-call(f32[2,20,128]{2,1,0:T(8,128)S(1)} %get-tuple-element.53.coef_ref, f32[64,128]{1,0:T(8,128)S(1)} %bitcast.12, f32[64,128]{1,0:T(8,128)S(1)} %bitcast.11, f32[64,128]{1,0:T(8,128)S(1)} %get-tuple-element.54.sum_ref, f32[64,128]{1,0:T(8,128)S(1)} %get-tuple-element.55.factor_ref, ...), custom_call_target="tpu_custom_call" | custom-call | flops 2000000 | bytes 2000000 | tf_op jit(solution)/shard_map/pallas_call | solution.py:652
  (35 shorter events, 3.3 us)
Async XLA Ops:
  2.1 1.4 %collective-permute-start = (f32[2,32,128]{2,1,0:T(8,128)S(1)}, f32[2,32,128]{2,1,0:T(8,128)S(1)}, u32[]{:S(2)}, u32[]{:S(2)}) collective-permute-start(f32[2,32,128]{2,1,0:T(8,128)S(1)} %get-tuple-element.35.own_ref), channel_id=1, source_target_pairs={{0,1},{1,0},{2,3},{3,2},{4,5},{5,4},{6,7},{7,6},{8,9},{9,8},{10,11... | collective-permute-start | bytes 98312 | tf_op jit(solution)/shard_map/ppermute | solution.py:567
  3.5 2.9 %copy-start = (s32[16,32,128]{2,1,0:T(8,128)S(1)}, s32[16,32,128]{2,1,0:T(8,128)}, u32[]{:S(2)}) copy-start(s32[16,32,128]{2,1,0:T(8,128)} %label_hbm.1) | copy-start | bytes 786436
  3.5 5.4 %collective-permute-start.1 = (f32[17,8,128]{2,1,0:T(8,128)S(1)}, f32[17,8,128]{2,1,0:T(8,128)S(1)}, u32[]{:S(2)}, u32[]{:S(2)}) collective-permute-start(f32[17,8,128]{2,1,0:T(8,128)S(1)} %get-tuple-element.38), channel_id=1, source_target_pairs={{0,2},{2,0},{1,3},{3,1},{4,6},{6,4},{5,7},{7,5},{8,10},{10,8},{9,1... | collective-permute-start | bytes 208904 | tf_op jit(solution)/shard_map/ppermute | solution.py:577
  9.0 4.9 %collective-permute-start.2 = (f32[6,40,128]{2,1,0:T(8,128)S(1)}, f32[6,40,128]{2,1,0:T(8,128)S(1)}, u32[]{:S(2)}, u32[]{:S(2)}) collective-permute-start(f32[6,40,128]{2,1,0:T(8,128)S(1)} %get-tuple-element.45), channel_id=1, source_target_pairs={{0,4},{4,0},{8,12},{12,8},{1,5},{5,1},{9,13},{13,9},{2,6},{6,2},{1... | collective-permute-start | bytes 368648 | tf_op jit(solution)/shard_map/ppermute | solution.py:530
  10.9 3.0 %collective-permute-start.3 = (f32[6,40,128]{2,1,0:T(8,128)S(1)}, f32[6,40,128]{2,1,0:T(8,128)S(1)}, u32[]{:S(2)}, u32[]{:S(2)}) collective-permute-start(f32[6,40,128]{2,1,0:T(8,128)S(1)} %get-tuple-element.46), channel_id=1, source_target_pairs={{4,8},{8,4},{5,9},{9,5},{6,10},{10,6},{7,11},{11,7},{20,24},{24,20... | collective-permute-start | bytes 368648 | tf_op jit(solution)/shard_map/ppermute | solution.py:530
  14.6 1.3 %collective-permute-start.4 = (f32[16,128]{1,0:T(8,128)S(1)}, f32[16,128]{1,0:T(8,128)S(1)}, u32[]{:S(2)}, u32[]{:S(2)}) collective-permute-start(f32[16,128]{1,0:T(8,128)S(1)} %get-tuple-element.47.after_ref.a_ref), channel_id=1, source_target_pairs={{0,1},{1,0},{2,3},{3,2},{4,5},{5,4},{6,7},{7,6},{8,9},{9,8},{10,11... | collective-permute-start | bytes 24584 | tf_op jit(solution)/shard_map/ppermute | solution.py:613
  15.9 3.7 %collective-permute-start.5 = (f32[16,128]{1,0:T(8,128)S(1)}, f32[16,128]{1,0:T(8,128)S(1)}, u32[]{:S(2)}, u32[]{:S(2)}) collective-permute-start(f32[16,128]{1,0:T(8,128)S(1)} %shard_map.146.after_ref.a_ref), channel_id=1, source_target_pairs={{0,2},{2,0},{1,3},{3,1},{4,6},{6,4},{5,7},{7,5},{8,10},{10,8},{9,1... | collective-permute-start | bytes 24584 | tf_op jit(solution)/shard_map/ppermute | solution.py:613
  19.6 8.1 %collective-permute-start.8 = (f32[16,128]{1,0:T(8,128)S(1)}, f32[16,128]{1,0:T(8,128)S(1)}, u32[]{:S(2)}, u32[]{:S(2)}) collective-permute-start(f32[16,128]{1,0:T(8,128)S(1)} %shard_map.148.after_ref.refs_0_), channel_id=1, source_target_pairs={{0,12},{4,8},{8,4},{12,0},{1,13},{5,9},{9,5},{13,1},{2,14},{6,10},... | collective-permute-start | bytes 24584 | tf_op jit(solution)/shard_map/ppermute | solution.py:624
  23.5 4.5 %collective-permute-start.7 = (f32[16,128]{1,0:T(8,128)S(1)}, f32[16,128]{1,0:T(8,128)S(1)}, u32[]{:S(2)}, u32[]{:S(2)}) collective-permute-start(f32[16,128]{1,0:T(8,128)S(1)} %shard_map.148.after_ref.refs_0_), channel_id=1, source_target_pairs={{0,8},{4,12},{8,0},{12,4},{1,9},{5,13},{9,1},{13,5},{2,10},{6,14},... | collective-permute-start | bytes 24584 | tf_op jit(solution)/shard_map/ppermute | solution.py:624
  26.0 3.7 %collective-permute-start.6 = (f32[16,128]{1,0:T(8,128)S(1)}, f32[16,128]{1,0:T(8,128)S(1)}, u32[]{:S(2)}, u32[]{:S(2)}) collective-permute-start(f32[16,128]{1,0:T(8,128)S(1)} %shard_map.148.after_ref.refs_0_), channel_id=1, source_target_pairs={{0,4},{4,0},{8,12},{12,8},{1,5},{5,1},{9,13},{13,9},{2,6},{6,2},{1... | collective-permute-start | bytes 24584 | tf_op jit(solution)/shard_map/ppermute | solution.py:624
  29.9 8.0 %collective-permute-start.9 = (f32[64,128]{1,0:T(8,128)S(1)}, f32[64,128]{1,0:T(8,128)S(1)}, u32[]{:S(2)}, u32[]{:S(2)}) collective-permute-start(f32[64,128]{1,0:T(8,128)S(1)} %get-tuple-element.58), channel_id=1, source_target_pairs={{0,4},{4,0},{8,12},{12,8},{1,5},{5,1},{9,13},{13,9},{2,6},{6,2},{1... | collective-permute-start | bytes 98312 | tf_op jit(solution)/shard_map/ppermute | solution.py:635
  31.4 6.4 %collective-permute-start.10 = (f32[64,128]{1,0:T(8,128)S(1)}, f32[64,128]{1,0:T(8,128)S(1)}, u32[]{:S(2)}, u32[]{:S(2)}) collective-permute-start(f32[64,128]{1,0:T(8,128)S(1)} %get-tuple-element.59), channel_id=1, source_target_pairs={{0,8},{4,12},{8,0},{12,4},{1,9},{5,13},{9,1},{13,5},{2,10},{6,14},... | collective-permute-start | bytes 98312 | tf_op jit(solution)/shard_map/ppermute | solution.py:635
  33.4 5.7 %collective-permute-start.11 = (f32[64,128]{1,0:T(8,128)S(1)}, f32[64,128]{1,0:T(8,128)S(1)}, u32[]{:S(2)}, u32[]{:S(2)}) collective-permute-start(f32[64,128]{1,0:T(8,128)S(1)} %get-tuple-element.60), channel_id=1, source_target_pairs={{0,12},{4,8},{8,4},{12,0},{1,13},{5,9},{9,5},{13,1},{2,14},{6,10},... | collective-permute-start | bytes 98312 | tf_op jit(solution)/shard_map/ppermute | solution.py:635
  34.3 1.2 %copy-start.1 = (f32[20,1,8192]{2,1,0:T(1,128)S(1)}, f32[20,1,8192]{2,1,0:T(1,128)}, u32[]{:S(2)}) copy-start(f32[20,1,8192]{2,1,0:T(1,128)} %param.17) | copy-start | bytes 1966084
  34.3 1.4 %copy-start.2 = (f32[20,1,8192]{2,1,0:T(1,128)S(1)}, f32[20,1,8192]{2,1,0:T(1,128)}, u32[]{:S(2)}) copy-start(f32[20,1,8192]{2,1,0:T(1,128)} %param.19) | copy-start | bytes 1966084
  34.3 1.4 %copy-start.3 = (f32[1,8192]{1,0:T(1,128)S(1)}, f32[1,8192]{1,0:T(1,128)}, u32[]{:S(2)}) copy-start(f32[1,8192]{1,0:T(1,128)} %param.16) | copy-start | bytes 98308
  34.3 1.4 %copy-start.8 = (f32[20]{0:T(128)S(1)}, f32[20]{0:T(128)}, u32[]{:S(2)}) copy-start(f32[20]{0:T(128)} %cond_ref.1) | copy-start | bytes 244
  34.3 1.4 %copy-start.9 = (f32[20]{0:T(128)S(1)}, f32[20]{0:T(128)}, u32[]{:S(2)}) copy-start(f32[20]{0:T(128)} %rev_ref.1) | copy-start | bytes 244
  35.1 0.8 %copy-start.5 = (f32[20]{0:T(128)S(1)}, f32[20]{0:T(128)}, u32[]{:S(2)}) copy-start(f32[20]{0:T(128)} %half_ref.1) | copy-start | bytes 244
  35.1 0.8 %copy-start.6 = (f32[20]{0:T(128)S(1)}, f32[20]{0:T(128)}, u32[]{:S(2)}) copy-start(f32[20]{0:T(128)} %slope_ref.1) | copy-start | bytes 244
  35.1 0.8 %copy-start.7 = (f32[20]{0:T(128)S(1)}, f32[20]{0:T(128)}, u32[]{:S(2)}) copy-start(f32[20]{0:T(128)} %tau_ref.1) | copy-start | bytes 244
  35.9 3.2 %copy-start.4 = (f32[1,8192]{1,0:T(1,128)S(1)}, f32[1,8192]{1,0:T(1,128)}, u32[]{:S(2)}) copy-start(f32[1,8192]{1,0:T(1,128)} %param.18) | copy-start | bytes 98308

commit v7 on v6

--- a/solution.py
+++ b/solution.py
@@ -263,19 +263,21 @@
 
 
 def outer_kernel(
-    a_ref, i_ref, b_ref, c_ref, slab_ref, halo_ref, sum_ref, first_ref, second_ref, stat_ref,
+    after_ref, a_ref, i_ref, b_ref, c_ref, slab_ref, halo_ref, sum_ref, first_ref, second_ref, stat_ref,
     ea_ref, eb_ref, ec_ref, slabs_ref, total_ref, ei_ref, si_ref,
 ):
     nx, ny, nz = a_ref.shape[0], a_ref.shape[1] - 2 * SUB, a_ref.shape[2]
     ring = ny + SUB
     gz = lax.axis_index("gz")
-    odd = lax.rem(lax.axis_index("gx"), 2) == 1
+    gx = lax.axis_index("gx")
+    odd = lax.rem(gx, 2) == 1
+    inside = jnp.where((gx > 0) & (gx < lax.axis_size("gx") - 1), 1.0, 0.0).astype(F32)
 
     def low(k):
-        return jnp.where(odd, first_ref[k], second_ref[k])
+        return jnp.where(odd, first_ref[k], second_ref[k] * inside)
 
     def high(k):
-        return jnp.where(odd, second_ref[k], first_ref[k])
+        return jnp.where(odd, second_ref[k] * inside, first_ref[k])
 
     for ref, at, plane in (
         [(ea_ref, k, low(k)) for k in range(3)] + [(ea_ref, 3 + k, high(k)) for k in range(3)]
@@ -525,9 +527,17 @@
 def pair_swaps(first, second, axis):
     count = lax.axis_size(axis)
     even = [(i, i ^ 1) for i in range(count)]
-    between = [(i, i + 1) for i in range(1, count - 1, 2)]
-    between = between + [(j, i) for i, j in between]
+    between = [(0, 0), (count - 1, count - 1)]
+    for i in range(1, count - 1, 2):
+        between += [(i, i + 1), (i + 1, i)]
     return lax.ppermute(first, axis, even), lax.ppermute(second, axis, between)
+
+
+def block_pairs(count, k, slots, block):
+    def apart(tile, owner):
+        return owner * block >= (tile + 1) * slots or (owner + 1) * block <= count * block - (count - tile) * slots
+
+    return [(i, i if apart(i, i ^ k) and apart(i ^ k, i) else i ^ k) for i in range(count)]
 
 
 def reduce_over(value, axis):
@@ -593,12 +603,25 @@
         scratch=[pltpu.VMEM((4, tall, nz), F32)],
         cost=6_000_000,
     )(w0, inv, slab, edge_rows)
+    base, total_change, factor, state_coefs = call(
+        membrane_kernel,
+        (
+            shape_of(n_states, block_rows, LANES), shape_of(block_rows, LANES), shape_of(block_rows, LANES),
+            shape_of(2, n_states, LANES),
+        ),
+        9,
+        specs=[SMEM] * 5 + [VMEM] * 4,
+        cost=6_000_000,
+    )(
+        half_voltage, gate_slope, tau_base, conductance, reversal,
+        in_sums, cells(voltage), states(gates), states(gates_cot),
+    )
     ends0, ends1, ends2, slabs, sums = call(
         outer_kernel,
         (edges,) * 3 + (shape_of(3, tall, 2 * nz), shape_of(16, nz)),
-        10,
+        11,
         scratch=[pltpu.VMEM((4, tall, nz), F32), pltpu.VMEM((1, tall, 2 * nz), F32)],
-    )(in0, in_inv, in1, in2, slab, edge_rows, in_sums, first, second, stat)
+    )(state_coefs, in0, in_inv, in1, in2, slab, edge_rows, in_sums, first, second, stat)
 
     def couple(stage, after, inside, ends):
         return call(
@@ -632,23 +655,10 @@
         scratch=[pltpu.VMEM((n_gx * block_rows + slot_rows + SUB, LANES), F32)],
     )(*sums, list0, list1, list2)
     landed = blocks[:1] + [
-        lax.ppermute(blocks[k], "gx", [(i, i ^ k) for i in range(n_gx)]) for k in range(1, n_gx)
+        lax.ppermute(blocks[k], "gx", block_pairs(n_gx, k, slot_rows, block_rows)) for k in range(1, n_gx)
     ]
 
     solution = call(potential_kernel, block, 6)(coefs, in0, in1, in2, ends1, ends2)
-    base, total_change, factor, state_coefs = call(
-        membrane_kernel,
-        (
-            shape_of(n_states, block_rows, LANES), shape_of(block_rows, LANES), shape_of(block_rows, LANES),
-            shape_of(2, n_states, LANES),
-        ),
-        9,
-        specs=[SMEM] * 5 + [VMEM] * 4,
-        cost=6_000_000,
-    )(
-        half_voltage, gate_slope, tau_base, conductance, reversal,
-        coefs, cells(voltage), states(gates), states(gates_cot),
-    )
     volt_grad, gate_grad = call(
         finish_kernel,
         (shape_of(block_rows, LANES), shape_of(n_states, block_rows, LANES)),

time: 40.3 us -> 37.6 us (0.933)
  starting transfers between devices: 19.3 us -> 16.9 us
  waiting for transfers between devices: 6.85 us -> 6.42 us
    ppermute x1, waiting for transfers between devices: 1.38 us -> 0.01 us  [pair_swaps(): lax.ppermute(first, axis, even)]
    ppermute x3, starting transfers between devices: 6.92 us -> 5.86 us  [local(): lax.ppermute(sums, 'gx', [(i, i ^ k) for i in range(n_gx)])]
    ppermute x3, starting transfers between devices: 4.45 us -> 3.39 us  [local(): lax.ppermute(blocks[k], 'gx', block_pairs(n_gx, k, slot_rows, block_rows))]
    ppermute x3, waiting for transfers between devices: 1.89 us -> 2.44 us  [local(): lax.ppermute(sums, 'gx', [(i, i ^ k) for i in range(n_gx)])]
  transfers between devices with their start and end apart: 12 -> 12, of which waited for: 7 -> 6; matrix products, arithmetic and copies ran while one was open for 0% -> 0% of each run, Pallas kernels for 22% -> 24%
where the time goes in v7:
time: 37.6 us; the launch traced here: 37.2 us
  starting transfers between devices  16.9 us (45%)
  Pallas kernels  12.4 us (33%)
  waiting for transfers between devices  6.42 us (17%)
  between operations  0.86 us (2%)
  local copies, waits for them, and re-layouts  0.65 us (2%)
    ppermute x3, starting transfers between devices, local(): lax.ppermute(sums, 'gx', [(i, i ^ k) for i in range(n_gx)])  5.86 us
    pallas_call x3, Pallas kernels, couple(): call(functools.partial(couple_kernel, stage, slot_rows), shape_of(slot_ro...  3.57 us
    ppermute x3, starting transfers between devices, local(): lax.ppermute(blocks[k], 'gx', block_pairs(n_gx, k, slot_rows, block_rows))  3.39 us
    ppermute x1, starting transfers between devices, local(): halo = (lax.ppermute(mine, 'gy', [(0, 1), (1, 0)]),)  2.9 us
    ppermute x3, waiting for transfers between devices, local(): lax.ppermute(sums, 'gx', [(i, i ^ k) for i in range(n_gx)])  2.44 us
    pallas_call x1, Pallas kernels, local(): call(membrane_kernel, (shape_of(n_states, block_rows, LANES), shape_of(bl...  1.93 us
    ppermute x1, starting transfers between devices, pair_swaps(): lax.ppermute(first, axis, even)  1.92 us
    pallas_call x1, Pallas kernels, local(): call(plan_kernel, jax.ShapeDtypeStruct((rows, LANES), jnp.int32), 2, cost...  1.72 us
  transfers between devices with their start and end apart: 12, of which 6 were waited for; matrix products, arithmetic and copies ran while one was open for 0% of the time, Pallas kernels for 24%

profile of v7, /device:TPU:0, one launch (start us, length us, event | category | flops | bytes accessed | tf_op | source)
XLA Modules:
  0.0 37.2 jit_solution(11926123840400265668)
XLA Ops:
  0.6 1.5 %shard_map.139 = (f32[16,32,128]{2,1,0:T(8,128)S(1)}, f32[16,32,128]{2,1,0:T(8,128)S(1)}, f32[2,32,128]{2,1,0:T(8,128)S(1)}, f32[2,8,128]{2,1,0:T(8,128)S(1)}) custom-call(f32[16,32,128]{2,1,0:T(8,128)} %right_hbm.1, f32[16,32,128]{2,1,0:T(8,128)} %damping_hbm.1, s32[16,32,128]{2,1,0:T(8,128)} %label_hbm.1), custom_call_target="tpu_custom_call" | custom-call | flops 2000000 | bytes 2000000 | tf_op jit(solution)/shard_map/pallas_call | solution.py:568
  2.6 0.9 %collective-permute-done.got_ref = f32[2,32,128]{2,1,0:T(8,128)S(1)} collective-permute-done((f32[2,32,128]{2,1,0:T(8,128)S(1)}, f32[2,32,128]{2,1,0:T(8,128)S(1)}, u32[]{:S(2)}, u32[]{:S(2)}) %collective-permute-start) | collective-permute-done | bytes 32800 | tf_op jit(solution)/shard_map/ppermute | solution.py:577
  3.5 2.9 %collective-permute-start.1 = (f32[17,8,128]{2,1,0:T(8,128)S(1)}, f32[17,8,128]{2,1,0:T(8,128)S(1)}, u32[]{:S(2)}, u32[]{:S(2)}) collective-permute-start(f32[17,8,128]{2,1,0:T(8,128)S(1)} %get-tuple-element.38), channel_id=1, source_target_pairs={{0,2},{2,0},{1,3},{3,1},{4,6},{6,4},{5,7},{7,5},{8,10},{10,8},{9,1... | collective-permute-start | bytes 208904 | tf_op jit(solution)/shard_map/ppermute | solution.py:587
  6.4 1.7 %shard_map.141.after_ref.plan_ref = s32[512,128]{1,0:T(8,128)S(1)} custom-call(f32[2,8,128]{2,1,0:T(8,128)S(1)} %get-tuple-element.37.after_ref.stat_ref, s32[512,128]{1,0:T(8,128)S(1)} %bitcast.7), custom_call_target="tpu_custom_call" | custom-call | flops 6000000 | bytes 6000000 | tf_op jit(solution)/shard_map/pallas_call | solution.py:578
  8.1 0.8 %collective-permute-done.1.refs_0_ = f32[17,8,128]{2,1,0:T(8,128)S(1)} collective-permute-done((f32[17,8,128]{2,1,0:T(8,128)S(1)}, f32[17,8,128]{2,1,0:T(8,128)S(1)}, u32[]{:S(2)}, u32[]{:S(2)}) %collective-permute-start.1) | collective-permute-done | bytes 69664 | tf_op jit(solution)/shard_map/ppermute | solution.py:587
  9.0 1.9 %collective-permute-start.2 = (f32[6,40,128]{2,1,0:T(8,128)S(1)}, f32[6,40,128]{2,1,0:T(8,128)S(1)}, u32[]{:S(2)}, u32[]{:S(2)}) collective-permute-start(f32[6,40,128]{2,1,0:T(8,128)S(1)} %get-tuple-element.46), channel_id=1, source_target_pairs={{0,4},{4,0},{8,12},{12,8},{1,5},{5,1},{9,13},{13,9},{2,6},{6,2},{1... | collective-permute-start | bytes 368648 | tf_op jit(solution)/shard_map/ppermute | solution.py:533
  10.9 0.7 %collective-permute-start.3 = (f32[6,40,128]{2,1,0:T(8,128)S(1)}, f32[6,40,128]{2,1,0:T(8,128)S(1)}, u32[]{:S(2)}, u32[]{:S(2)}) collective-permute-start(f32[6,40,128]{2,1,0:T(8,128)S(1)} %get-tuple-element.47), channel_id=1, source_target_pairs={{0,0},{12,12},{4,8},{8,4},{1,1},{13,13},{5,9},{9,5},{2,2},{14,14},... | collective-permute-start | bytes 368648 | tf_op jit(solution)/shard_map/ppermute | solution.py:533
  11.6 0.9 %shard_map.143 = (f32[16,48,128]{2,1,0:T(8,128)S(1)}, f32[16,48,128]{2,1,0:T(8,128)S(1)}, f32[16,48,128]{2,1,0:T(8,128)S(1)}, f32[16,48,128]{2,1,0:T(8,128)S(1)}, f32[5,8,128]{2,1,0:T(8,128)S(1)}) custom-call(f32[16,32,128]{2,1,0:T(8,128)S(1)} %get-tuple-element.33.w0_ref, f32[16,32,128]{2,1,0:T(8,128)S(1)} %get-tuple-element.34.inv_ref, ...), custom_call_target="tpu_custom_call" | custom-call | flops 6000000 | bytes 6000000 | tf_op jit(solution)/shard_map/pallas_call | solution.py:599
  13.3 1.9 %shard_map.144 = (f32[20,64,128]{2,1,0:T(8,128)S(1)}, f32[64,128]{1,0:T(8,128)S(1)}, f32[64,128]{1,0:T(8,128)S(1)}, f32[2,20,128]{2,1,0:T(8,128)S(1)}) custom-call(f32[20]{0:T(128)S(1)} %copy-done.5, f32[20]{0:T(128)S(1)} %copy-done.6, f32[20]{0:T(128)S(1)} %copy-done.7, f32[20]{0:T(128)S(1)} %copy-done.8, f32[20]{0:T(128)S(1)} %copy-done.9, ...), custom_call_target="tpu_custom_call" | custom-call | flops 6000000 | bytes 6000000 | tf_op jit(solution)/shard_map/pallas_call | solution.py:606
  15.2 0.7 %shard_map.145 = (f32[6,48,128]{2,1,0:T(8,128)S(1)}, f32[6,48,128]{2,1,0:T(8,128)S(1)}, f32[6,48,128]{2,1,0:T(8,128)S(1)}, f32[3,48,256]{2,1,0:T(8,128)S(1)}, f32[16,128]{1,0:T(8,128)S(1)}) custom-call(f32[2,20,128]{2,1,0:T(8,128)S(1)} %get-tuple-element.41.after_ref.coef_ref, f32[16,48,128]{2,1,0:T(8,128)S(1)} %get-tuple-element.42.a_ref.inside_ref, ...), custom_call_target="tpu_custom_call" | custom-call | flops 2000000 | bytes 2000000 | tf_op jit(solution)/shard_map/pallas_call | solution.py:619
  16.0 1.2 %shard_map.146.after_ref.refs_4_ = f32[160,128]{1,0:T(8,128)S(1)} custom-call(f32[16,128]{1,0:T(8,128)S(1)} %get-tuple-element.48.after_ref.a_ref, f32[16,48,128]{2,1,0:T(8,128)S(1)} %get-tuple-element.42.a_ref.inside_ref, f32[6,48,128]{2,1,0:T(8,128)S(1)} %get-tuple-element.49.edge_ref, f32[3,48,256]{2,1,0:T(8,128)S(1)} %get-tuple-element.50.slabs_ref, ...), custom_call_target="tpu_custom_call" | custom-call | flops 6000000 | bytes 6000000 | tf_op jit(solution)/shard_map/pallas_call | solution.py:627
  17.2 1.6 %collective-permute-start.5 = (f32[16,128]{1,0:T(8,128)S(1)}, f32[16,128]{1,0:T(8,128)S(1)}, u32[]{:S(2)}, u32[]{:S(2)}) collective-permute-start(f32[16,128]{1,0:T(8,128)S(1)} %shard_map.147.after_ref.a_ref), channel_id=1, source_target_pairs={{0,2},{2,0},{1,3},{3,1},{4,6},{6,4},{5,7},{7,5},{8,10},{10,8},{9,1... | collective-permute-start | bytes 24584 | tf_op jit(solution)/shard_map/ppermute | solution.py:636
  18.8 1.2 %shard_map.148.after_ref.refs_5_ = f32[160,128]{1,0:T(8,128)S(1)} custom-call(f32[16,128]{1,0:T(8,128)S(1)} %shard_map.147.after_ref.a_ref, f32[16,48,128]{2,1,0:T(8,128)S(1)} %get-tuple-element.44.b_ref.inside_ref, f32[6,48,128]{2,1,0:T(8,128)S(1)} %get-tuple-element.51.edge_ref.eb_ref, f32[3,48,256]{2,1,0:T(8,128)S(1)} %get-tuple-element.50.slabs_ref, ...), custom_call_target="tpu_custom_call" | custom-call | flops 6000000 | bytes 6000000 | tf_op jit(solution)/shard_map/pallas_call | solution.py:627
  20.0 1.0 %collective-permute-done.5.b_ref = f32[16,128]{1,0:T(8,128)S(1)} collective-permute-done((f32[16,128]{1,0:T(8,128)S(1)}, f32[16,128]{1,0:T(8,128)S(1)}, u32[]{:S(2)}, u32[]{:S(2)}) %collective-permute-start.5) | collective-permute-done | bytes 8224 | tf_op jit(solution)/shard_map/ppermute | solution.py:636
  20.9 2.6 %collective-permute-start.8 = (f32[16,128]{1,0:T(8,128)S(1)}, f32[16,128]{1,0:T(8,128)S(1)}, u32[]{:S(2)}, u32[]{:S(2)}) collective-permute-start(f32[16,128]{1,0:T(8,128)S(1)} %shard_map.149.after_ref.refs_0_), channel_id=1, source_target_pairs={{0,12},{4,8},{8,4},{12,0},{1,13},{5,9},{9,5},{13,1},{2,14},{6,10},... | collective-permute-start | bytes 24584 | tf_op jit(solution)/shard_map/ppermute | solution.py:647
  23.5 3.2 %collective-permute-start.7 = (f32[16,128]{1,0:T(8,128)S(1)}, f32[16,128]{1,0:T(8,128)S(1)}, u32[]{:S(2)}, u32[]{:S(2)}) collective-permute-start(f32[16,128]{1,0:T(8,128)S(1)} %shard_map.149.after_ref.refs_0_), channel_id=1, source_target_pairs={{0,8},{4,12},{8,0},{12,4},{1,9},{5,13},{9,1},{13,5},{2,10},{6,14},... | collective-permute-start | bytes 24584 | tf_op jit(solution)/shard_map/ppermute | solution.py:647
  26.8 1.2 %shard_map.150.refs_6_ = f32[160,128]{1,0:T(8,128)S(1)} custom-call(f32[16,128]{1,0:T(8,128)S(1)} %shard_map.149.after_ref.refs_0_, f32[16,48,128]{2,1,0:T(8,128)S(1)} %get-tuple-element.45.c_ref.inside_ref, f32[6,48,128]{2,1,0:T(8,128)S(1)} %get-tuple-element.52.edge_ref.ec_ref, f32[3,48,256]{2,1,0:T(8,128)S(1)} %get-tuple-element.50.slabs_ref, ...), custom_call_target="tpu_custom_call" | custom-call | flops 6000000 | bytes 6000000 | tf_op jit(solution)/shard_map/pallas_call | solution.py:627
  28.5 1.9 %collective-permute-done.6.refs_1_ = f32[16,128]{1,0:T(8,128)S(1)} collective-permute-done((f32[16,128]{1,0:T(8,128)S(1)}, f32[16,128]{1,0:T(8,128)S(1)}, u32[]{:S(2)}, u32[]{:S(2)}) %collective-permute-start.6) | collective-permute-done | bytes 8224 | tf_op jit(solution)/shard_map/ppermute | solution.py:647
  30.7 0.7 %collective-permute-start.9 = (f32[64,128]{1,0:T(8,128)S(1)}, f32[64,128]{1,0:T(8,128)S(1)}, u32[]{:S(2)}, u32[]{:S(2)}) collective-permute-start(f32[64,128]{1,0:T(8,128)S(1)} %get-tuple-element.58), channel_id=1, source_target_pairs={{0,4},{4,0},{8,12},{12,8},{1,5},{5,1},{9,13},{13,9},{2,6},{6,2},{1... | collective-permute-start | bytes 98312 | tf_op jit(solution)/shard_map/ppermute | solution.py:658
  31.4 2.0 %collective-permute-start.10 = (f32[64,128]{1,0:T(8,128)S(1)}, f32[64,128]{1,0:T(8,128)S(1)}, u32[]{:S(2)}, u32[]{:S(2)}) collective-permute-start(f32[64,128]{1,0:T(8,128)S(1)} %get-tuple-element.59), channel_id=1, source_target_pairs={{0,8},{4,12},{8,0},{12,4},{1,9},{5,13},{9,1},{13,5},{2,10},{6,14},... | collective-permute-start | bytes 98312 | tf_op jit(solution)/shard_map/ppermute | solution.py:658
  33.4 0.7 %collective-permute-start.11 = (f32[64,128]{1,0:T(8,128)S(1)}, f32[64,128]{1,0:T(8,128)S(1)}, u32[]{:S(2)}, u32[]{:S(2)}) collective-permute-start(f32[64,128]{1,0:T(8,128)S(1)} %get-tuple-element.60), channel_id=1, source_target_pairs={{0,0},{4,8},{8,4},{12,12},{1,1},{5,9},{9,5},{13,13},{2,2},{6,10},{... | collective-permute-start | bytes 98312 | tf_op jit(solution)/shard_map/ppermute | solution.py:658
  34.1 0.8 %shard_map.152 = f32[16,32,128]{2,1,0:T(8,128)} custom-call(f32[8,128]{1,0:T(8,128)S(1)} %get-tuple-element.53.coef_ref, f32[16,48,128]{2,1,0:T(8,128)S(1)} %get-tuple-element.42.a_ref.inside_ref, f32[16,48,128]{2,1,0:T(8,128)S(1)} %get-tuple-element.44.b_ref.inside_ref, f32[16,48,128]{2,1,0:T(8,128)S(1)} %get-tuple-element.45.c_ref.inside_ref, ...), custom_call_target="tpu_custom_call" | custom-call | flops 2000000 | bytes 2000000 | tf_op jit(solution)/shard_map/pallas_call | solution.py:661
  34.9 1.4 %collective-permute-done.10.refs_2_ = f32[64,128]{1,0:T(8,128)S(1)} collective-permute-done((f32[64,128]{1,0:T(8,128)S(1)}, f32[64,128]{1,0:T(8,128)S(1)}, u32[]{:S(2)}, u32[]{:S(2)}) %collective-permute-start.10) | collective-permute-done | bytes 32800 | tf_op jit(solution)/shard_map/ppermute | solution.py:658
  36.2 0.9 %shard_map.153 = (f32[64,128]{1,0:T(8,128)}, f32[20,64,128]{2,1,0:T(8,128)}) custom-call(f32[2,20,128]{2,1,0:T(8,128)S(1)} %get-tuple-element.41.after_ref.coef_ref, f32[64,128]{1,0:T(8,128)S(1)} %bitcast.12, f32[64,128]{1,0:T(8,128)S(1)} %bitcast.11, f32[64,128]{1,0:T(8,128)S(1)} %get-tuple-element.54.sum_ref, f32[64,128]{1,0:T(8,128)S(1)} %get-tuple-element.55.factor_ref, ...), custom_call_target="tpu_custom_call" | custom-call | flops 2000000 | bytes 2000000 | tf_op jit(solution)/shard_map/pallas_call | solution.py:662
  (35 shorter events, 2.1 us)
Async XLA Ops:
  2.1 1.4 %collective-permute-start = (f32[2,32,128]{2,1,0:T(8,128)S(1)}, f32[2,32,128]{2,1,0:T(8,128)S(1)}, u32[]{:S(2)}, u32[]{:S(2)}) collective-permute-start(f32[2,32,128]{2,1,0:T(8,128)S(1)} %get-tuple-element.35.own_ref), channel_id=1, source_target_pairs={{0,1},{1,0},{2,3},{3,2},{4,5},{5,4},{6,7},{7,6},{8,9},{9,8},{10,11... | collective-permute-start | bytes 98312 | tf_op jit(solution)/shard_map/ppermute | solution.py:577
  3.5 2.9 %copy-start = (s32[16,32,128]{2,1,0:T(8,128)S(1)}, s32[16,32,128]{2,1,0:T(8,128)}, u32[]{:S(2)}) copy-start(s32[16,32,128]{2,1,0:T(8,128)} %label_hbm.1) | copy-start | bytes 786436
  3.5 5.4 %collective-permute-start.1 = (f32[17,8,128]{2,1,0:T(8,128)S(1)}, f32[17,8,128]{2,1,0:T(8,128)S(1)}, u32[]{:S(2)}, u32[]{:S(2)}) collective-permute-start(f32[17,8,128]{2,1,0:T(8,128)S(1)} %get-tuple-element.38), channel_id=1, source_target_pairs={{0,2},{2,0},{1,3},{3,1},{4,6},{6,4},{5,7},{7,5},{8,10},{10,8},{9,1... | collective-permute-start | bytes 208904 | tf_op jit(solution)/shard_map/ppermute | solution.py:587
  8.9 3.7 %copy-start.1 = (f32[20,1,8192]{2,1,0:T(1,128)S(1)}, f32[20,1,8192]{2,1,0:T(1,128)}, u32[]{:S(2)}) copy-start(f32[20,1,8192]{2,1,0:T(1,128)} %param.17) | copy-start | bytes 1966084
  8.9 3.7 %copy-start.2 = (f32[20,1,8192]{2,1,0:T(1,128)S(1)}, f32[20,1,8192]{2,1,0:T(1,128)}, u32[]{:S(2)}) copy-start(f32[20,1,8192]{2,1,0:T(1,128)} %param.19) | copy-start | bytes 1966084
  9.0 6.2 %collective-permute-start.2 = (f32[6,40,128]{2,1,0:T(8,128)S(1)}, f32[6,40,128]{2,1,0:T(8,128)S(1)}, u32[]{:S(2)}, u32[]{:S(2)}) collective-permute-start(f32[6,40,128]{2,1,0:T(8,128)S(1)} %get-tuple-element.46), channel_id=1, source_target_pairs={{0,4},{4,0},{8,12},{12,8},{1,5},{5,1},{9,13},{13,9},{2,6},{6,2},{1... | collective-permute-start | bytes 368648 | tf_op jit(solution)/shard_map/ppermute | solution.py:533
  10.9 4.3 %collective-permute-start.3 = (f32[6,40,128]{2,1,0:T(8,128)S(1)}, f32[6,40,128]{2,1,0:T(8,128)S(1)}, u32[]{:S(2)}, u32[]{:S(2)}) collective-permute-start(f32[6,40,128]{2,1,0:T(8,128)S(1)} %get-tuple-element.47), channel_id=1, source_target_pairs={{0,0},{12,12},{4,8},{8,4},{1,1},{13,13},{5,9},{9,5},{2,2},{14,14},... | collective-permute-start | bytes 368648 | tf_op jit(solution)/shard_map/ppermute | solution.py:533
  11.6 1.0 %copy-start.3 = (f32[1,8192]{1,0:T(1,128)S(1)}, f32[1,8192]{1,0:T(1,128)}, u32[]{:S(2)}) copy-start(f32[1,8192]{1,0:T(1,128)} %param.16) | copy-start | bytes 98308
  11.6 1.0 %copy-start.8 = (f32[20]{0:T(128)S(1)}, f32[20]{0:T(128)}, u32[]{:S(2)}) copy-start(f32[20]{0:T(128)} %cond_ref.1) | copy-start | bytes 244
  11.6 1.0 %copy-start.9 = (f32[20]{0:T(128)S(1)}, f32[20]{0:T(128)}, u32[]{:S(2)}) copy-start(f32[20]{0:T(128)} %rev_ref.1) | copy-start | bytes 244
  12.6 0.7 %copy-start.5 = (f32[20]{0:T(128)S(1)}, f32[20]{0:T(128)}, u32[]{:S(2)}) copy-start(f32[20]{0:T(128)} %half_ref.1) | copy-start | bytes 244
  12.6 0.7 %copy-start.6 = (f32[20]{0:T(128)S(1)}, f32[20]{0:T(128)}, u32[]{:S(2)}) copy-start(f32[20]{0:T(128)} %slope_ref.1) | copy-start | bytes 244
  12.6 0.7 %copy-start.7 = (f32[20]{0:T(128)S(1)}, f32[20]{0:T(128)}, u32[]{:S(2)}) copy-start(f32[20]{0:T(128)} %tau_ref.1) | copy-start | bytes 244
  15.9 1.3 %collective-permute-start.4 = (f32[16,128]{1,0:T(8,128)S(1)}, f32[16,128]{1,0:T(8,128)S(1)}, u32[]{:S(2)}, u32[]{:S(2)}) collective-permute-start(f32[16,128]{1,0:T(8,128)S(1)} %get-tuple-element.48.after_ref.a_ref), channel_id=1, source_target_pairs={{0,1},{1,0},{2,3},{3,2},{4,5},{5,4},{6,7},{7,6},{8,9},{9,8},{10,11... | collective-permute-start | bytes 24584 | tf_op jit(solution)/shard_map/ppermute | solution.py:636
  17.2 3.7 %collective-permute-start.5 = (f32[16,128]{1,0:T(8,128)S(1)}, f32[16,128]{1,0:T(8,128)S(1)}, u32[]{:S(2)}, u32[]{:S(2)}) collective-permute-start(f32[16,128]{1,0:T(8,128)S(1)} %shard_map.147.after_ref.a_ref), channel_id=1, source_target_pairs={{0,2},{2,0},{1,3},{3,1},{4,6},{6,4},{5,7},{7,5},{8,10},{10,8},{9,1... | collective-permute-start | bytes 24584 | tf_op jit(solution)/shard_map/ppermute | solution.py:636
  20.9 7.1 %collective-permute-start.8 = (f32[16,128]{1,0:T(8,128)S(1)}, f32[16,128]{1,0:T(8,128)S(1)}, u32[]{:S(2)}, u32[]{:S(2)}) collective-permute-start(f32[16,128]{1,0:T(8,128)S(1)} %shard_map.149.after_ref.refs_0_), channel_id=1, source_target_pairs={{0,12},{4,8},{8,4},{12,0},{1,13},{5,9},{9,5},{13,1},{2,14},{6,10},... | collective-permute-start | bytes 24584 | tf_op jit(solution)/shard_map/ppermute | solution.py:647
  23.5 5.0 %collective-permute-start.7 = (f32[16,128]{1,0:T(8,128)S(1)}, f32[16,128]{1,0:T(8,128)S(1)}, u32[]{:S(2)}, u32[]{:S(2)}) collective-permute-start(f32[16,128]{1,0:T(8,128)S(1)} %shard_map.149.after_ref.refs_0_), channel_id=1, source_target_pairs={{0,8},{4,12},{8,0},{12,4},{1,9},{5,13},{9,1},{13,5},{2,10},{6,14},... | collective-permute-start | bytes 24584 | tf_op jit(solution)/shard_map/ppermute | solution.py:647
  26.8 3.7 %collective-permute-start.6 = (f32[16,128]{1,0:T(8,128)S(1)}, f32[16,128]{1,0:T(8,128)S(1)}, u32[]{:S(2)}, u32[]{:S(2)}) collective-permute-start(f32[16,128]{1,0:T(8,128)S(1)} %shard_map.149.after_ref.refs_0_), channel_id=1, source_target_pairs={{0,4},{4,0},{8,12},{12,8},{1,5},{5,1},{9,13},{13,9},{2,6},{6,2},{1... | collective-permute-start | bytes 24584 | tf_op jit(solution)/shard_map/ppermute | solution.py:647
  30.7 4.2 %collective-permute-start.9 = (f32[64,128]{1,0:T(8,128)S(1)}, f32[64,128]{1,0:T(8,128)S(1)}, u32[]{:S(2)}, u32[]{:S(2)}) collective-permute-start(f32[64,128]{1,0:T(8,128)S(1)} %get-tuple-element.58), channel_id=1, source_target_pairs={{0,4},{4,0},{8,12},{12,8},{1,5},{5,1},{9,13},{13,9},{2,6},{6,2},{1... | collective-permute-start | bytes 98312 | tf_op jit(solution)/shard_map/ppermute | solution.py:658
  31.4 4.8 %collective-permute-start.10 = (f32[64,128]{1,0:T(8,128)S(1)}, f32[64,128]{1,0:T(8,128)S(1)}, u32[]{:S(2)}, u32[]{:S(2)}) collective-permute-start(f32[64,128]{1,0:T(8,128)S(1)} %get-tuple-element.59), channel_id=1, source_target_pairs={{0,8},{4,12},{8,0},{12,4},{1,9},{5,13},{9,1},{13,5},{2,10},{6,14},... | collective-permute-start | bytes 98312 | tf_op jit(solution)/shard_map/ppermute | solution.py:658
  33.4 2.8 %collective-permute-start.11 = (f32[64,128]{1,0:T(8,128)S(1)}, f32[64,128]{1,0:T(8,128)S(1)}, u32[]{:S(2)}, u32[]{:S(2)}) collective-permute-start(f32[64,128]{1,0:T(8,128)S(1)} %get-tuple-element.60), channel_id=1, source_target_pairs={{0,0},{4,8},{8,4},{12,12},{1,1},{5,9},{9,5},{13,13},{2,2},{6,10},{... | collective-permute-start | bytes 98312 | tf_op jit(solution)/shard_map/ppermute | solution.py:658
  34.1 2.1 %copy-start.4 = (f32[1,8192]{1,0:T(1,128)S(1)}, f32[1,8192]{1,0:T(1,128)}, u32[]{:S(2)}) copy-start(f32[1,8192]{1,0:T(1,128)} %param.18) | copy-start | bytes 98308

commit v8 on v7

--- a/solution.py
+++ b/solution.py
@@ -145,7 +145,7 @@
             halo_ref[1, x] = jnp.where(
                 sub >= 6, pltpu.roll(low, 4, 0), jnp.where(sub <= 1, pltpu.roll(high, 4, 0), 0.0)
             )
-    odd = lax.rem(lax.axis_index("gx"), 2)
+    odd = lax.rem(lax.axis_index("gx") + lax.axis_index("gz"), 2)
     slab_w = jnp.concatenate([slab_ref[0], halo_ref[0, nx]], axis=0)
     slab_i = jnp.concatenate([slab_ref[1], halo_ref[1, nx]], axis=0)
     half = pltpu.roll(slab_i, nz // 2, 1)
@@ -270,14 +270,14 @@
     ring = ny + SUB
     gz = lax.axis_index("gz")
     gx = lax.axis_index("gx")
-    odd = lax.rem(gx, 2) == 1
-    inside = jnp.where((gx > 0) & (gx < lax.axis_size("gx") - 1), 1.0, 0.0).astype(F32)
+    odd = lax.rem(gx + gz, 2) == 1
+    has_low, has_high = gx > 0, gx < lax.axis_size("gx") - 1
 
     def low(k):
-        return jnp.where(odd, first_ref[k], second_ref[k] * inside)
+        return jnp.where(has_low, jnp.where(odd, first_ref[k], second_ref[k]), 0.0)
 
     def high(k):
-        return jnp.where(odd, second_ref[k] * inside, first_ref[k])
+        return jnp.where(has_high, jnp.where(odd, second_ref[k], first_ref[k]), 0.0)
 
     for ref, at, plane in (
         [(ea_ref, k, low(k)) for k in range(3)] + [(ea_ref, 3 + k, high(k)) for k in range(3)]
@@ -524,13 +524,18 @@
     return low, high
 
 
-def pair_swaps(first, second, axis):
-    count = lax.axis_size(axis)
-    even = [(i, i ^ 1) for i in range(count)]
-    between = [(0, 0), (count - 1, count - 1)]
-    for i in range(1, count - 1, 2):
-        between += [(i, i + 1), (i + 1, i)]
-    return lax.ppermute(first, axis, even), lax.ppermute(second, axis, between)
+def pair_swaps(first, second):
+    n_gx, n_gz = lax.axis_size("gx"), lax.axis_size("gz")
+    even = [i ^ 1 for i in range(n_gx)]
+    between = [0] + [i + 1 if i % 2 else i - 1 for i in range(1, n_gx - 1)] + [n_gx - 1]
+
+    def pairs(orders):
+        return [(x * n_gz + z, orders[z % 2][x] * n_gz + z) for x in range(n_gx) for z in range(n_gz)]
+
+    return (
+        lax.ppermute(first, ("gx", "gz"), pairs((even, between))),
+        lax.ppermute(second, ("gx", "gz"), pairs((between, even))),
+    )
 
 
 def block_pairs(count, k, slots, block):
@@ -570,7 +575,7 @@
         specs=[HBM] * 3,
         scratch=[
             pltpu.VMEM((nx, ny, nz), F32), pltpu.VMEM((nx, ny, nz), F32), pltpu.VMEM((nx, ny, nz), jnp.int32),
-            pltpu.SemaphoreType.DMA((3, 4)),
+            pltpu.SemaphoreType.DMA((3, 8)),
         ],
     )(in_hbm(potential_cot), in_hbm(damping), in_hbm(tissue_label))
 
@@ -591,7 +596,7 @@
     edge_rows, first, second = call(
         functools.partial(x_faces_kernel, n_gy == 2), x_shapes, 4 + len(halo)
     )(plan, w0, inv, slab, *halo)
-    first, second = pair_swaps(first, second, "gx")
+    first, second = pair_swaps(first, second)
 
     tall = ring + SUB
     planes = shape_of(nx, tall, nz)
@@ -655,7 +660,7 @@
         scratch=[pltpu.VMEM((n_gx * block_rows + slot_rows + SUB, LANES), F32)],
     )(*sums, list0, list1, list2)
     landed = blocks[:1] + [
-        lax.ppermute(blocks[k], "gx", block_pairs(n_gx, k, slot_rows, block_rows)) for k in range(1, n_gx)
+        lax.ppermute(blocks[k], "gx", block_pairs(n_gx, k, slot_rows, block_rows)) for k in range(n_gx - 1, 0, -1)
     ]
 
     solution = call(potential_kernel, block, 6)(coefs, in0, in1, in2, ends1, ends2)

time: 37.6 us -> 42.3 us (1.12)
  starting transfers between devices: 16.9 us -> 19.6 us
  waiting for transfers between devices: 6.42 us -> 8.2 us
    ppermute x2, starting transfers between devices: 2.57 us -> 4.58 us  [the longest x1 3.92 us: pair_swaps(): lax.ppermute(first, ('gx', 'gz'), pairs((even, between)))]
    ppermute x3, waiting for transfers between devices: 1.36 us -> 3.15 us  [local(): lax.ppermute(blocks[k], 'gx', block_pairs(n_gx, k, slot_rows, block_rows))]
    ppermute x2, starting transfers between devices: 1.63 us -> 2.89 us  [add(): lax.ppermute(value, axis, [(i, i ^ step) for i in range(lax.axis_size(axi...]
    ppermute x3, starting transfers between devices: 5.86 us -> 4.6 us  [local(): lax.ppermute(sums, 'gx', [(i, i ^ k) for i in range(n_gx)])]
    ppermute x3, starting transfers between devices: 3.39 us -> 4.09 us  [local(): lax.ppermute(blocks[k], 'gx', block_pairs(n_gx, k, slot_rows, block_rows))]
  transfers between devices with their start and end apart: 12 -> 12, of which waited for: 6 -> 7; matrix products, arithmetic and copies ran while one was open for 0% -> 0% of each run, Pallas kernels for 24% -> 21%
where the time goes in v8:
time: 42.3 us; the launch traced here: 42 us
  starting transfers between devices  19.6 us (46%)
  Pallas kernels  12.7 us (30%)
  waiting for transfers between devices  8.2 us (19%)
  between operations  0.85 us (2%)
  local copies, waits for them, and re-layouts  0.65 us (2%)
    ppermute x3, starting transfers between devices, local(): lax.ppermute(sums, 'gx', [(i, i ^ k) for i in range(n_gx)])  4.6 us
    ppermute x3, starting transfers between devices, local(): lax.ppermute(blocks[k], 'gx', block_pairs(n_gx, k, slot_rows, block_rows))  4.09 us
    ppermute x1, starting transfers between devices, pair_swaps(): lax.ppermute(first, ('gx', 'gz'), pairs((even, between)))  3.92 us
    pallas_call x3, Pallas kernels, couple(): call(functools.partial(couple_kernel, stage, slot_rows), shape_of(slot_ro...  3.56 us
    ppermute x3, waiting for transfers between devices, local(): lax.ppermute(blocks[k], 'gx', block_pairs(n_gx, k, slot_rows, block_rows))  3.15 us
    ppermute x1, starting transfers between devices, local(): halo = (lax.ppermute(mine, 'gy', [(0, 1), (1, 0)]),)  2.9 us
    ppermute x2, starting transfers between devices, add(): lax.ppermute(value, axis, [(i, i ^ step) for i in range(lax.axis_size(axi...  2.89 us
    ppermute x3, waiting for transfers between devices, local(): lax.ppermute(sums, 'gx', [(i, i ^ k) for i in range(n_gx)])  2.44 us
  transfers between devices with their start and end apart: 12, of which 7 were waited for; matrix products, arithmetic and copies ran while one was open for 0% of the time, Pallas kernels for 21%

profile of v8, /device:TPU:0, one launch (start us, length us, event | category | flops | bytes accessed | tf_op | source)
XLA Modules:
  0.0 42.0 jit_solution(14402933818553283345)
XLA Ops:
  0.6 1.8 %shard_map.139 = (f32[16,32,128]{2,1,0:T(8,128)S(1)}, f32[16,32,128]{2,1,0:T(8,128)S(1)}, f32[2,32,128]{2,1,0:T(8,128)S(1)}, f32[2,8,128]{2,1,0:T(8,128)S(1)}) custom-call(f32[16,32,128]{2,1,0:T(8,128)} %right_hbm.1, f32[16,32,128]{2,1,0:T(8,128)} %damping_hbm.1, s32[16,32,128]{2,1,0:T(8,128)} %label_hbm.1), custom_call_target="tpu_custom_call" | custom-call | flops 2000000 | bytes 2000000 | tf_op jit(solution)/shard_map/pallas_call | solution.py:573
  2.9 0.9 %collective-permute-done.got_ref = f32[2,32,128]{2,1,0:T(8,128)S(1)} collective-permute-done((f32[2,32,128]{2,1,0:T(8,128)S(1)}, f32[2,32,128]{2,1,0:T(8,128)S(1)}, u32[]{:S(2)}, u32[]{:S(2)}) %collective-permute-start) | collective-permute-done | bytes 32800 | tf_op jit(solution)/shard_map/ppermute | solution.py:582
  3.8 2.9 %collective-permute-start.1 = (f32[17,8,128]{2,1,0:T(8,128)S(1)}, f32[17,8,128]{2,1,0:T(8,128)S(1)}, u32[]{:S(2)}, u32[]{:S(2)}) collective-permute-start(f32[17,8,128]{2,1,0:T(8,128)S(1)} %get-tuple-element.38), channel_id=1, source_target_pairs={{0,2},{2,0},{1,3},{3,1},{4,6},{6,4},{5,7},{7,5},{8,10},{10,8},{9,1... | collective-permute-start | bytes 208904 | tf_op jit(solution)/shard_map/ppermute | solution.py:592
  6.7 1.7 %shard_map.141.after_ref.plan_ref = s32[512,128]{1,0:T(8,128)S(1)} custom-call(f32[2,8,128]{2,1,0:T(8,128)S(1)} %get-tuple-element.37.after_ref.stat_ref, s32[512,128]{1,0:T(8,128)S(1)} %bitcast.7), custom_call_target="tpu_custom_call" | custom-call | flops 6000000 | bytes 6000000 | tf_op jit(solution)/shard_map/pallas_call | solution.py:583
  8.5 0.8 %collective-permute-done.1.refs_0_ = f32[17,8,128]{2,1,0:T(8,128)S(1)} collective-permute-done((f32[17,8,128]{2,1,0:T(8,128)S(1)}, f32[17,8,128]{2,1,0:T(8,128)S(1)}, u32[]{:S(2)}, u32[]{:S(2)}) %collective-permute-start.1) | collective-permute-done | bytes 69664 | tf_op jit(solution)/shard_map/ppermute | solution.py:592
  9.3 3.9 %collective-permute-start.2 = (f32[6,40,128]{2,1,0:T(8,128)S(1)}, f32[6,40,128]{2,1,0:T(8,128)S(1)}, u32[]{:S(2)}, u32[]{:S(2)}) collective-permute-start(f32[6,40,128]{2,1,0:T(8,128)S(1)} %get-tuple-element.46), channel_id=1, source_target_pairs={{0,4},{1,1},{4,0},{5,9},{8,12},{9,5},{12,8},{13,13},{2,6},{3,3},{6... | collective-permute-start | bytes 368648 | tf_op jit(solution)/shard_map/ppermute | solution.py:536
  13.3 0.7 %collective-permute-start.3 = (f32[6,40,128]{2,1,0:T(8,128)S(1)}, f32[6,40,128]{2,1,0:T(8,128)S(1)}, u32[]{:S(2)}, u32[]{:S(2)}) collective-permute-start(f32[6,40,128]{2,1,0:T(8,128)S(1)} %get-tuple-element.47), channel_id=1, source_target_pairs={{0,0},{1,5},{4,8},{5,1},{8,4},{9,13},{12,12},{13,9},{2,2},{3,7},{6... | collective-permute-start | bytes 368648 | tf_op jit(solution)/shard_map/ppermute | solution.py:537
  14.0 0.9 %shard_map.143 = (f32[16,48,128]{2,1,0:T(8,128)S(1)}, f32[16,48,128]{2,1,0:T(8,128)S(1)}, f32[16,48,128]{2,1,0:T(8,128)S(1)}, f32[16,48,128]{2,1,0:T(8,128)S(1)}, f32[5,8,128]{2,1,0:T(8,128)S(1)}) custom-call(f32[16,32,128]{2,1,0:T(8,128)S(1)} %get-tuple-element.33.w0_ref, f32[16,32,128]{2,1,0:T(8,128)S(1)} %get-tuple-element.34.inv_ref, ...), custom_call_target="tpu_custom_call" | custom-call | flops 6000000 | bytes 6000000 | tf_op jit(solution)/shard_map/pallas_call | solution.py:604
  15.6 1.9 %shard_map.144 = (f32[20,64,128]{2,1,0:T(8,128)S(1)}, f32[64,128]{1,0:T(8,128)S(1)}, f32[64,128]{1,0:T(8,128)S(1)}, f32[2,20,128]{2,1,0:T(8,128)S(1)}) custom-call(f32[20]{0:T(128)S(1)} %copy-done.5, f32[20]{0:T(128)S(1)} %copy-done.6, f32[20]{0:T(128)S(1)} %copy-done.7, f32[20]{0:T(128)S(1)} %copy-done.8, f32[20]{0:T(128)S(1)} %copy-done.9, ...), custom_call_target="tpu_custom_call" | custom-call | flops 6000000 | bytes 6000000 | tf_op jit(solution)/shard_map/pallas_call | solution.py:611
  17.6 0.7 %shard_map.145 = (f32[6,48,128]{2,1,0:T(8,128)S(1)}, f32[6,48,128]{2,1,0:T(8,128)S(1)}, f32[6,48,128]{2,1,0:T(8,128)S(1)}, f32[3,48,256]{2,1,0:T(8,128)S(1)}, f32[16,128]{1,0:T(8,128)S(1)}) custom-call(f32[2,20,128]{2,1,0:T(8,128)S(1)} %get-tuple-element.41.after_ref.coef_ref, f32[16,48,128]{2,1,0:T(8,128)S(1)} %get-tuple-element.42.a_ref.inside_ref, ...), custom_call_target="tpu_custom_call" | custom-call | flops 2000000 | bytes 2000000 | tf_op jit(solution)/shard_map/pallas_call | solution.py:624
  18.3 1.3 %collective-permute-start.4 = (f32[16,128]{1,0:T(8,128)S(1)}, f32[16,128]{1,0:T(8,128)S(1)}, u32[]{:S(2)}, u32[]{:S(2)}) collective-permute-start(f32[16,128]{1,0:T(8,128)S(1)} %get-tuple-element.48.after_ref.a_ref), channel_id=1, source_target_pairs={{0,1},{1,0},{2,3},{3,2},{4,5},{5,4},{6,7},{7,6},{8,9},{9,8},{10,11... | collective-permute-start | bytes 24584 | tf_op jit(solution)/shard_map/ppermute | solution.py:641
  19.6 1.2 %shard_map.146.after_ref.refs_4_ = f32[160,128]{1,0:T(8,128)S(1)} custom-call(f32[16,128]{1,0:T(8,128)S(1)} %get-tuple-element.48.after_ref.a_ref, f32[16,48,128]{2,1,0:T(8,128)S(1)} %get-tuple-element.42.a_ref.inside_ref, f32[6,48,128]{2,1,0:T(8,128)S(1)} %get-tuple-element.49.edge_ref, f32[3,48,256]{2,1,0:T(8,128)S(1)} %get-tuple-element.50.slabs_ref, ...), custom_call_target="tpu_custom_call" | custom-call | flops 6000000 | bytes 6000000 | tf_op jit(solution)/shard_map/pallas_call | solution.py:632
  20.8 1.6 %collective-permute-start.5 = (f32[16,128]{1,0:T(8,128)S(1)}, f32[16,128]{1,0:T(8,128)S(1)}, u32[]{:S(2)}, u32[]{:S(2)}) collective-permute-start(f32[16,128]{1,0:T(8,128)S(1)} %shard_map.147.after_ref.a_ref), channel_id=1, source_target_pairs={{0,2},{2,0},{1,3},{3,1},{4,6},{6,4},{5,7},{7,5},{8,10},{10,8},{9,1... | collective-permute-start | bytes 24584 | tf_op jit(solution)/shard_map/ppermute | solution.py:641
  22.4 1.2 %shard_map.148.after_ref.refs_5_ = f32[160,128]{1,0:T(8,128)S(1)} custom-call(f32[16,128]{1,0:T(8,128)S(1)} %shard_map.147.after_ref.a_ref, f32[16,48,128]{2,1,0:T(8,128)S(1)} %get-tuple-element.44.b_ref.inside_ref, f32[6,48,128]{2,1,0:T(8,128)S(1)} %get-tuple-element.51.edge_ref.eb_ref, f32[3,48,256]{2,1,0:T(8,128)S(1)} %get-tuple-element.50.slabs_ref, ...), custom_call_target="tpu_custom_call" | custom-call | flops 6000000 | bytes 6000000 | tf_op jit(solution)/shard_map/pallas_call | solution.py:632
  23.6 1.0 %collective-permute-done.5.b_ref = f32[16,128]{1,0:T(8,128)S(1)} collective-permute-done((f32[16,128]{1,0:T(8,128)S(1)}, f32[16,128]{1,0:T(8,128)S(1)}, u32[]{:S(2)}, u32[]{:S(2)}) %collective-permute-start.5) | collective-permute-done | bytes 8224 | tf_op jit(solution)/shard_map/ppermute | solution.py:641
  24.5 1.5 %collective-permute-start.8 = (f32[16,128]{1,0:T(8,128)S(1)}, f32[16,128]{1,0:T(8,128)S(1)}, u32[]{:S(2)}, u32[]{:S(2)}) collective-permute-start(f32[16,128]{1,0:T(8,128)S(1)} %shard_map.149.after_ref.refs_0_), channel_id=1, source_target_pairs={{0,12},{4,8},{8,4},{12,0},{1,13},{5,9},{9,5},{13,1},{2,14},{6,10},... | collective-permute-start | bytes 24584 | tf_op jit(solution)/shard_map/ppermute | solution.py:652
  26.0 3.1 %collective-permute-start.7 = (f32[16,128]{1,0:T(8,128)S(1)}, f32[16,128]{1,0:T(8,128)S(1)}, u32[]{:S(2)}, u32[]{:S(2)}) collective-permute-start(f32[16,128]{1,0:T(8,128)S(1)} %shard_map.149.after_ref.refs_0_), channel_id=1, source_target_pairs={{0,8},{4,12},{8,0},{12,4},{1,9},{5,13},{9,1},{13,5},{2,10},{6,14},... | collective-permute-start | bytes 24584 | tf_op jit(solution)/shard_map/ppermute | solution.py:652
  29.1 1.2 %shard_map.150.refs_6_ = f32[160,128]{1,0:T(8,128)S(1)} custom-call(f32[16,128]{1,0:T(8,128)S(1)} %shard_map.149.after_ref.refs_0_, f32[16,48,128]{2,1,0:T(8,128)S(1)} %get-tuple-element.45.c_ref.inside_ref, f32[6,48,128]{2,1,0:T(8,128)S(1)} %get-tuple-element.52.edge_ref.ec_ref, f32[3,48,256]{2,1,0:T(8,128)S(1)} %get-tuple-element.50.slabs_ref, ...), custom_call_target="tpu_custom_call" | custom-call | flops 6000000 | bytes 6000000 | tf_op jit(solution)/shard_map/pallas_call | solution.py:632
  30.8 1.9 %collective-permute-done.6.refs_1_ = f32[16,128]{1,0:T(8,128)S(1)} collective-permute-done((f32[16,128]{1,0:T(8,128)S(1)}, f32[16,128]{1,0:T(8,128)S(1)}, u32[]{:S(2)}, u32[]{:S(2)}) %collective-permute-start.6) | collective-permute-done | bytes 8224 | tf_op jit(solution)/shard_map/ppermute | solution.py:652
  33.7 3.4 %collective-permute-start.10 = (f32[64,128]{1,0:T(8,128)S(1)}, f32[64,128]{1,0:T(8,128)S(1)}, u32[]{:S(2)}, u32[]{:S(2)}) collective-permute-start(f32[64,128]{1,0:T(8,128)S(1)} %get-tuple-element.59), channel_id=1, source_target_pairs={{0,8},{4,12},{8,0},{12,4},{1,9},{5,13},{9,1},{13,5},{2,10},{6,14},... | collective-permute-start | bytes 98312 | tf_op jit(solution)/shard_map/ppermute | solution.py:663
  37.1 0.8 %shard_map.152 = f32[16,32,128]{2,1,0:T(8,128)} custom-call(f32[8,128]{1,0:T(8,128)S(1)} %get-tuple-element.53.coef_ref, f32[16,48,128]{2,1,0:T(8,128)S(1)} %get-tuple-element.42.a_ref.inside_ref, f32[16,48,128]{2,1,0:T(8,128)S(1)} %get-tuple-element.44.b_ref.inside_ref, f32[16,48,128]{2,1,0:T(8,128)S(1)} %get-tuple-element.45.c_ref.inside_ref, ...), custom_call_target="tpu_custom_call" | custom-call | flops 2000000 | bytes 2000000 | tf_op jit(solution)/shard_map/pallas_call | solution.py:666
  37.9 1.4 %collective-permute-done.10.refs_2_ = f32[64,128]{1,0:T(8,128)S(1)} collective-permute-done((f32[64,128]{1,0:T(8,128)S(1)}, f32[64,128]{1,0:T(8,128)S(1)}, u32[]{:S(2)}, u32[]{:S(2)}) %collective-permute-start.10) | collective-permute-done | bytes 32800 | tf_op jit(solution)/shard_map/ppermute | solution.py:663
  39.3 1.8 %collective-permute-done.11.refs_3_ = f32[64,128]{1,0:T(8,128)S(1)} collective-permute-done((f32[64,128]{1,0:T(8,128)S(1)}, f32[64,128]{1,0:T(8,128)S(1)}, u32[]{:S(2)}, u32[]{:S(2)}) %collective-permute-start.11) | collective-permute-done | bytes 32800 | tf_op jit(solution)/shard_map/ppermute | solution.py:663
  41.0 0.9 %shard_map.153 = (f32[64,128]{1,0:T(8,128)}, f32[20,64,128]{2,1,0:T(8,128)}) custom-call(f32[2,20,128]{2,1,0:T(8,128)S(1)} %get-tuple-element.41.after_ref.coef_ref, f32[64,128]{1,0:T(8,128)S(1)} %bitcast.12, f32[64,128]{1,0:T(8,128)S(1)} %bitcast.11, f32[64,128]{1,0:T(8,128)S(1)} %get-tuple-element.54.sum_ref, f32[64,128]{1,0:T(8,128)S(1)} %get-tuple-element.55.factor_ref, ...), custom_call_target="tpu_custom_call" | custom-call | flops 2000000 | bytes 2000000 | tf_op jit(solution)/shard_map/pallas_call | solution.py:667
  (35 shorter events, 2.7 us)
Async XLA Ops:
  2.4 1.4 %collective-permute-start = (f32[2,32,128]{2,1,0:T(8,128)S(1)}, f32[2,32,128]{2,1,0:T(8,128)S(1)}, u32[]{:S(2)}, u32[]{:S(2)}) collective-permute-start(f32[2,32,128]{2,1,0:T(8,128)S(1)} %get-tuple-element.35.own_ref), channel_id=1, source_target_pairs={{0,1},{1,0},{2,3},{3,2},{4,5},{5,4},{6,7},{7,6},{8,9},{9,8},{10,11... | collective-permute-start | bytes 98312 | tf_op jit(solution)/shard_map/ppermute | solution.py:582
  3.8 2.9 %copy-start = (s32[16,32,128]{2,1,0:T(8,128)S(1)}, s32[16,32,128]{2,1,0:T(8,128)}, u32[]{:S(2)}) copy-start(s32[16,32,128]{2,1,0:T(8,128)} %label_hbm.1) | copy-start | bytes 786436
  3.8 5.4 %collective-permute-start.1 = (f32[17,8,128]{2,1,0:T(8,128)S(1)}, f32[17,8,128]{2,1,0:T(8,128)S(1)}, u32[]{:S(2)}, u32[]{:S(2)}) collective-permute-start(f32[17,8,128]{2,1,0:T(8,128)S(1)} %get-tuple-element.38), channel_id=1, source_target_pairs={{0,2},{2,0},{1,3},{3,1},{4,6},{6,4},{5,7},{7,5},{8,10},{10,8},{9,1... | collective-permute-start | bytes 208904 | tf_op jit(solution)/shard_map/ppermute | solution.py:592
  9.3 5.7 %copy-start.1 = (f32[20,1,8192]{2,1,0:T(1,128)S(1)}, f32[20,1,8192]{2,1,0:T(1,128)}, u32[]{:S(2)}) copy-start(f32[20,1,8192]{2,1,0:T(1,128)} %param.17) | copy-start | bytes 1966084
  9.3 5.7 %copy-start.2 = (f32[20,1,8192]{2,1,0:T(1,128)S(1)}, f32[20,1,8192]{2,1,0:T(1,128)}, u32[]{:S(2)}) copy-start(f32[20,1,8192]{2,1,0:T(1,128)} %param.19) | copy-start | bytes 1966084
  9.3 8.2 %collective-permute-start.2 = (f32[6,40,128]{2,1,0:T(8,128)S(1)}, f32[6,40,128]{2,1,0:T(8,128)S(1)}, u32[]{:S(2)}, u32[]{:S(2)}) collective-permute-start(f32[6,40,128]{2,1,0:T(8,128)S(1)} %get-tuple-element.46), channel_id=1, source_target_pairs={{0,4},{1,1},{4,0},{5,9},{8,12},{9,5},{12,8},{13,13},{2,6},{3,3},{6... | collective-permute-start | bytes 368648 | tf_op jit(solution)/shard_map/ppermute | solution.py:536
  13.3 4.3 %collective-permute-start.3 = (f32[6,40,128]{2,1,0:T(8,128)S(1)}, f32[6,40,128]{2,1,0:T(8,128)S(1)}, u32[]{:S(2)}, u32[]{:S(2)}) collective-permute-start(f32[6,40,128]{2,1,0:T(8,128)S(1)} %get-tuple-element.47), channel_id=1, source_target_pairs={{0,0},{1,5},{4,8},{5,1},{8,4},{9,13},{12,12},{13,9},{2,2},{3,7},{6... | collective-permute-start | bytes 368648 | tf_op jit(solution)/shard_map/ppermute | solution.py:537
  13.9 1.0 %copy-start.3 = (f32[1,8192]{1,0:T(1,128)S(1)}, f32[1,8192]{1,0:T(1,128)}, u32[]{:S(2)}) copy-start(f32[1,8192]{1,0:T(1,128)} %param.16) | copy-start | bytes 98308
  14.0 1.0 %copy-start.8 = (f32[20]{0:T(128)S(1)}, f32[20]{0:T(128)}, u32[]{:S(2)}) copy-start(f32[20]{0:T(128)} %cond_ref.1) | copy-start | bytes 244
  14.0 1.0 %copy-start.9 = (f32[20]{0:T(128)S(1)}, f32[20]{0:T(128)}, u32[]{:S(2)}) copy-start(f32[20]{0:T(128)} %rev_ref.1) | copy-start | bytes 244
  14.9 0.7 %copy-start.5 = (f32[20]{0:T(128)S(1)}, f32[20]{0:T(128)}, u32[]{:S(2)}) copy-start(f32[20]{0:T(128)} %half_ref.1) | copy-start | bytes 244
  14.9 0.7 %copy-start.6 = (f32[20]{0:T(128)S(1)}, f32[20]{0:T(128)}, u32[]{:S(2)}) copy-start(f32[20]{0:T(128)} %slope_ref.1) | copy-start | bytes 244
  15.0 0.7 %copy-start.7 = (f32[20]{0:T(128)S(1)}, f32[20]{0:T(128)}, u32[]{:S(2)}) copy-start(f32[20]{0:T(128)} %tau_ref.1) | copy-start | bytes 244
  18.3 2.5 %collective-permute-start.4 = (f32[16,128]{1,0:T(8,128)S(1)}, f32[16,128]{1,0:T(8,128)S(1)}, u32[]{:S(2)}, u32[]{:S(2)}) collective-permute-start(f32[16,128]{1,0:T(8,128)S(1)} %get-tuple-element.48.after_ref.a_ref), channel_id=1, source_target_pairs={{0,1},{1,0},{2,3},{3,2},{4,5},{5,4},{6,7},{7,6},{8,9},{9,8},{10,11... | collective-permute-start | bytes 24584 | tf_op jit(solution)/shard_map/ppermute | solution.py:641
  20.8 3.7 %collective-permute-start.5 = (f32[16,128]{1,0:T(8,128)S(1)}, f32[16,128]{1,0:T(8,128)S(1)}, u32[]{:S(2)}, u32[]{:S(2)}) collective-permute-start(f32[16,128]{1,0:T(8,128)S(1)} %shard_map.147.after_ref.a_ref), channel_id=1, source_target_pairs={{0,2},{2,0},{1,3},{3,1},{4,6},{6,4},{5,7},{7,5},{8,10},{10,8},{9,1... | collective-permute-start | bytes 24584 | tf_op jit(solution)/shard_map/ppermute | solution.py:641
  24.5 5.8 %collective-permute-start.8 = (f32[16,128]{1,0:T(8,128)S(1)}, f32[16,128]{1,0:T(8,128)S(1)}, u32[]{:S(2)}, u32[]{:S(2)}) collective-permute-start(f32[16,128]{1,0:T(8,128)S(1)} %shard_map.149.after_ref.refs_0_), channel_id=1, source_target_pairs={{0,12},{4,8},{8,4},{12,0},{1,13},{5,9},{9,5},{13,1},{2,14},{6,10},... | collective-permute-start | bytes 24584 | tf_op jit(solution)/shard_map/ppermute | solution.py:652
  26.0 4.8 %collective-permute-start.7 = (f32[16,128]{1,0:T(8,128)S(1)}, f32[16,128]{1,0:T(8,128)S(1)}, u32[]{:S(2)}, u32[]{:S(2)}) collective-permute-start(f32[16,128]{1,0:T(8,128)S(1)} %shard_map.149.after_ref.refs_0_), channel_id=1, source_target_pairs={{0,8},{4,12},{8,0},{12,4},{1,9},{5,13},{9,1},{13,5},{2,10},{6,14},... | collective-permute-start | bytes 24584 | tf_op jit(solution)/shard_map/ppermute | solution.py:652
  29.1 3.7 %collective-permute-start.6 = (f32[16,128]{1,0:T(8,128)S(1)}, f32[16,128]{1,0:T(8,128)S(1)}, u32[]{:S(2)}, u32[]{:S(2)}) collective-permute-start(f32[16,128]{1,0:T(8,128)S(1)} %shard_map.149.after_ref.refs_0_), channel_id=1, source_target_pairs={{0,4},{4,0},{8,12},{12,8},{1,5},{5,1},{9,13},{13,9},{2,6},{6,2},{1... | collective-permute-start | bytes 24584 | tf_op jit(solution)/shard_map/ppermute | solution.py:652
  33.0 4.9 %collective-permute-start.9 = (f32[64,128]{1,0:T(8,128)S(1)}, f32[64,128]{1,0:T(8,128)S(1)}, u32[]{:S(2)}, u32[]{:S(2)}) collective-permute-start(f32[64,128]{1,0:T(8,128)S(1)} %get-tuple-element.58), channel_id=1, source_target_pairs={{0,0},{4,8},{8,4},{12,12},{1,1},{5,9},{9,5},{13,13},{2,2},{6,10},{... | collective-permute-start | bytes 98312 | tf_op jit(solution)/shard_map/ppermute | solution.py:663
  33.7 5.6 %collective-permute-start.10 = (f32[64,128]{1,0:T(8,128)S(1)}, f32[64,128]{1,0:T(8,128)S(1)}, u32[]{:S(2)}, u32[]{:S(2)}) collective-permute-start(f32[64,128]{1,0:T(8,128)S(1)} %get-tuple-element.59), channel_id=1, source_target_pairs={{0,8},{4,12},{8,0},{12,4},{1,9},{5,13},{9,1},{13,5},{2,10},{6,14},... | collective-permute-start | bytes 98312 | tf_op jit(solution)/shard_map/ppermute | solution.py:663
  37.1 3.9 %collective-permute-start.11 = (f32[64,128]{1,0:T(8,128)S(1)}, f32[64,128]{1,0:T(8,128)S(1)}, u32[]{:S(2)}, u32[]{:S(2)}) collective-permute-start(f32[64,128]{1,0:T(8,128)S(1)} %get-tuple-element.60), channel_id=1, source_target_pairs={{0,4},{4,0},{8,12},{12,8},{1,5},{5,1},{9,13},{13,9},{2,6},{6,2},{1... | collective-permute-start | bytes 98312 | tf_op jit(solution)/shard_map/ppermute | solution.py:663
  37.1 3.9 %copy-start.4 = (f32[1,8192]{1,0:T(1,128)S(1)}, f32[1,8192]{1,0:T(1,128)}, u32[]{:S(2)}) copy-start(f32[1,8192]{1,0:T(1,128)} %param.18) | copy-start | bytes 98308

commit v9 on v8

--- a/solution.py
+++ b/solution.py
@@ -145,7 +145,7 @@
             halo_ref[1, x] = jnp.where(
                 sub >= 6, pltpu.roll(low, 4, 0), jnp.where(sub <= 1, pltpu.roll(high, 4, 0), 0.0)
             )
-    odd = lax.rem(lax.axis_index("gx") + lax.axis_index("gz"), 2)
+    odd = lax.rem(lax.axis_index("gx"), 2)
     slab_w = jnp.concatenate([slab_ref[0], halo_ref[0, nx]], axis=0)
     slab_i = jnp.concatenate([slab_ref[1], halo_ref[1, nx]], axis=0)
     half = pltpu.roll(slab_i, nz // 2, 1)
@@ -270,7 +270,7 @@
     ring = ny + SUB
     gz = lax.axis_index("gz")
     gx = lax.axis_index("gx")
-    odd = lax.rem(gx + gz, 2) == 1
+    odd = lax.rem(gx, 2) == 1
     has_low, has_high = gx > 0, gx < lax.axis_size("gx") - 1
 
     def low(k):
@@ -524,25 +524,26 @@
     return low, high
 
 
+def swap(value, partner):
+    n_gz = lax.axis_size("gz")
+    pairs = [
+        (x * n_gz + z, to * n_gz + z if to != x else x * n_gz + (z ^ 1))
+        for x, to in enumerate(partner) for z in range(n_gz)
+    ]
+    return lax.ppermute(value, ("gx", "gz"), pairs)
+
+
 def pair_swaps(first, second):
-    n_gx, n_gz = lax.axis_size("gx"), lax.axis_size("gz")
-    even = [i ^ 1 for i in range(n_gx)]
-    between = [0] + [i + 1 if i % 2 else i - 1 for i in range(1, n_gx - 1)] + [n_gx - 1]
-
-    def pairs(orders):
-        return [(x * n_gz + z, orders[z % 2][x] * n_gz + z) for x in range(n_gx) for z in range(n_gz)]
-
-    return (
-        lax.ppermute(first, ("gx", "gz"), pairs((even, between))),
-        lax.ppermute(second, ("gx", "gz"), pairs((between, even))),
-    )
-
-
-def block_pairs(count, k, slots, block):
+    count = lax.axis_size("gx")
+    between = [0] + [i + 1 if i % 2 else i - 1 for i in range(1, count - 1)] + [count - 1]
+    return swap(first, [i ^ 1 for i in range(count)]), swap(second, between)
+
+
+def block_partners(count, k, slots, block):
     def apart(tile, owner):
         return owner * block >= (tile + 1) * slots or (owner + 1) * block <= count * block - (count - tile) * slots
 
-    return [(i, i if apart(i, i ^ k) and apart(i ^ k, i) else i ^ k) for i in range(count)]
+    return [i if apart(i, i ^ k) and apart(i ^ k, i) else i ^ k for i in range(count)]
 
 
 def reduce_over(value, axis):
@@ -575,7 +576,7 @@
         specs=[HBM] * 3,
         scratch=[
             pltpu.VMEM((nx, ny, nz), F32), pltpu.VMEM((nx, ny, nz), F32), pltpu.VMEM((nx, ny, nz), jnp.int32),
-            pltpu.SemaphoreType.DMA((3, 8)),
+            pltpu.SemaphoreType.DMA((3, 2)),
         ],
     )(in_hbm(potential_cot), in_hbm(damping), in_hbm(tissue_label))
 
@@ -660,7 +661,7 @@
         scratch=[pltpu.VMEM((n_gx * block_rows + slot_rows + SUB, LANES), F32)],
     )(*sums, list0, list1, list2)
     landed = blocks[:1] + [
-        lax.ppermute(blocks[k], "gx", block_pairs(n_gx, k, slot_rows, block_rows)) for k in range(n_gx - 1, 0, -1)
+        swap(blocks[k], block_partners(n_gx, k, slot_rows, block_rows)) for k in range(1, n_gx)
     ]
 
     solution = call(potential_kernel, block, 6)(coefs, in0, in1, in2, ends1, ends2)

time: 42.3 us -> 35.4 us (0.84)
  starting transfers between devices: 19.6 us -> 14.6 us
  waiting for transfers between devices: 8.2 us -> 6.82 us
    ppermute x5, starting transfers between devices: 8.68 us -> 4.72 us  [swap(): return lax.ppermute(value, ('gx', 'gz'), pairs)]
    ppermute x5, waiting for transfers between devices: 3.16 us -> 2.04 us  [swap(): return lax.ppermute(value, ('gx', 'gz'), pairs)]
    ppermute x2, starting transfers between devices: 2.89 us -> 2.12 us  [add(): lax.ppermute(value, axis, [(i, i ^ step) for i in range(lax.axis_size(axi...]
  transfers between devices with their start and end apart: 12 -> 12, of which waited for: 7 -> 7; matrix products, arithmetic and copies ran while one was open for 0% -> 0% of each run, Pallas kernels for 21% -> 25%
where the time goes in v9:
time: 35.4 us; the launch traced here: 35.2 us
  starting transfers between devices  14.6 us (41%)
  Pallas kernels  12.3 us (35%)
  waiting for transfers between devices  6.82 us (19%)
  between operations  0.81 us (2%)
  local copies, waits for them, and re-layouts  0.64 us (2%)
    ppermute x5, starting transfers between devices, swap(): return lax.ppermute(value, ('gx', 'gz'), pairs)  4.72 us
    ppermute x3, starting transfers between devices, local(): lax.ppermute(sums, 'gx', [(i, i ^ k) for i in range(n_gx)])  4.39 us
    pallas_call x3, Pallas kernels, couple(): call(functools.partial(couple_kernel, stage, slot_rows), shape_of(slot_ro...  3.56 us
    ppermute x1, starting transfers between devices, local(): halo = (lax.ppermute(mine, 'gy', [(0, 1), (1, 0)]),)  2.9 us
    ppermute x3, waiting for transfers between devices, local(): lax.ppermute(sums, 'gx', [(i, i ^ k) for i in range(n_gx)])  2.18 us
    ppermute x2, starting transfers between devices, add(): lax.ppermute(value, axis, [(i, i ^ step) for i in range(lax.axis_size(axi...  2.12 us
    ppermute x5, waiting for transfers between devices, swap(): return lax.ppermute(value, ('gx', 'gz'), pairs)  2.04 us
    pallas_call x1, Pallas kernels, local(): call(membrane_kernel, (shape_of(n_states, block_rows, LANES), shape_of(bl...  1.93 us
  transfers between devices with their start and end apart: 12, of which 7 were waited for; matrix products, arithmetic and copies ran while one was open for 0% of the time, Pallas kernels for 25%

profile of v9, /device:TPU:0, one launch (start us, length us, event | category | flops | bytes accessed | tf_op | source)
XLA Modules:
  0.0 35.2 jit_solution(16689634584823939942)
XLA Ops:
  0.6 1.4 %shard_map.139 = (f32[16,32,128]{2,1,0:T(8,128)S(1)}, f32[16,32,128]{2,1,0:T(8,128)S(1)}, f32[2,32,128]{2,1,0:T(8,128)S(1)}, f32[2,8,128]{2,1,0:T(8,128)S(1)}) custom-call(f32[16,32,128]{2,1,0:T(8,128)} %right_hbm.1, f32[16,32,128]{2,1,0:T(8,128)} %damping_hbm.1, s32[16,32,128]{2,1,0:T(8,128)} %label_hbm.1), custom_call_target="tpu_custom_call" | custom-call | flops 2000000 | bytes 2000000 | tf_op jit(solution)/shard_map/pallas_call | solution.py:574
  2.6 0.9 %collective-permute-done.got_ref = f32[2,32,128]{2,1,0:T(8,128)S(1)} collective-permute-done((f32[2,32,128]{2,1,0:T(8,128)S(1)}, f32[2,32,128]{2,1,0:T(8,128)S(1)}, u32[]{:S(2)}, u32[]{:S(2)}) %collective-permute-start) | collective-permute-done | bytes 32800 | tf_op jit(solution)/shard_map/ppermute | solution.py:583
  3.5 2.9 %collective-permute-start.1 = (f32[17,8,128]{2,1,0:T(8,128)S(1)}, f32[17,8,128]{2,1,0:T(8,128)S(1)}, u32[]{:S(2)}, u32[]{:S(2)}) collective-permute-start(f32[17,8,128]{2,1,0:T(8,128)S(1)} %get-tuple-element.38), channel_id=1, source_target_pairs={{0,2},{2,0},{1,3},{3,1},{4,6},{6,4},{5,7},{7,5},{8,10},{10,8},{9,1... | collective-permute-start | bytes 208904 | tf_op jit(solution)/shard_map/ppermute | solution.py:593
  6.4 1.7 %shard_map.141.after_ref.plan_ref = s32[512,128]{1,0:T(8,128)S(1)} custom-call(f32[2,8,128]{2,1,0:T(8,128)S(1)} %get-tuple-element.37.after_ref.stat_ref, s32[512,128]{1,0:T(8,128)S(1)} %bitcast.7), custom_call_target="tpu_custom_call" | custom-call | flops 6000000 | bytes 6000000 | tf_op jit(solution)/shard_map/pallas_call | solution.py:584
  8.1 0.8 %collective-permute-done.1.refs_0_ = f32[17,8,128]{2,1,0:T(8,128)S(1)} collective-permute-done((f32[17,8,128]{2,1,0:T(8,128)S(1)}, f32[17,8,128]{2,1,0:T(8,128)S(1)}, u32[]{:S(2)}, u32[]{:S(2)}) %collective-permute-start.1) | collective-permute-done | bytes 69664 | tf_op jit(solution)/shard_map/ppermute | solution.py:593
  8.9 1.9 %collective-permute-start.2 = (f32[6,40,128]{2,1,0:T(8,128)S(1)}, f32[6,40,128]{2,1,0:T(8,128)S(1)}, u32[]{:S(2)}, u32[]{:S(2)}) collective-permute-start(f32[6,40,128]{2,1,0:T(8,128)S(1)} %get-tuple-element.46), channel_id=1, source_target_pairs={{0,4},{1,5},{4,0},{5,1},{8,12},{9,13},{12,8},{13,9},{2,6},{3,7},{6... | collective-permute-start | bytes 368648 | tf_op jit(solution)/shard_map/ppermute | solution.py:533
  10.9 0.9 %shard_map.143 = (f32[16,48,128]{2,1,0:T(8,128)S(1)}, f32[16,48,128]{2,1,0:T(8,128)S(1)}, f32[16,48,128]{2,1,0:T(8,128)S(1)}, f32[16,48,128]{2,1,0:T(8,128)S(1)}, f32[5,8,128]{2,1,0:T(8,128)S(1)}) custom-call(f32[16,32,128]{2,1,0:T(8,128)S(1)} %get-tuple-element.33.w0_ref, f32[16,32,128]{2,1,0:T(8,128)S(1)} %get-tuple-element.34.inv_ref, ...), custom_call_target="tpu_custom_call" | custom-call | flops 6000000 | bytes 6000000 | tf_op jit(solution)/shard_map/pallas_call | solution.py:605
  11.9 0.6 %copy-done.5 = f32[20]{0:T(128)S(1)} copy-done((f32[20]{0:T(128)S(1)}, f32[20]{0:T(128)}, u32[]{:S(2)}) %copy-start.5) | copy-done | bytes 104
  12.5 1.9 %shard_map.144 = (f32[20,64,128]{2,1,0:T(8,128)S(1)}, f32[64,128]{1,0:T(8,128)S(1)}, f32[64,128]{1,0:T(8,128)S(1)}, f32[2,20,128]{2,1,0:T(8,128)S(1)}) custom-call(f32[20]{0:T(128)S(1)} %copy-done.5, f32[20]{0:T(128)S(1)} %copy-done.6, f32[20]{0:T(128)S(1)} %copy-done.7, f32[20]{0:T(128)S(1)} %copy-done.8, f32[20]{0:T(128)S(1)} %copy-done.9, ...), custom_call_target="tpu_custom_call" | custom-call | flops 6000000 | bytes 6000000 | tf_op jit(solution)/shard_map/pallas_call | solution.py:612
  14.5 0.7 %shard_map.145 = (f32[6,48,128]{2,1,0:T(8,128)S(1)}, f32[6,48,128]{2,1,0:T(8,128)S(1)}, f32[6,48,128]{2,1,0:T(8,128)S(1)}, f32[3,48,256]{2,1,0:T(8,128)S(1)}, f32[16,128]{1,0:T(8,128)S(1)}) custom-call(f32[2,20,128]{2,1,0:T(8,128)S(1)} %get-tuple-element.41.after_ref.coef_ref, f32[16,48,128]{2,1,0:T(8,128)S(1)} %get-tuple-element.42.a_ref.inside_ref, ...), custom_call_target="tpu_custom_call" | custom-call | flops 2000000 | bytes 2000000 | tf_op jit(solution)/shard_map/pallas_call | solution.py:625
  15.2 0.6 %collective-permute-start.4 = (f32[16,128]{1,0:T(8,128)S(1)}, f32[16,128]{1,0:T(8,128)S(1)}, u32[]{:S(2)}, u32[]{:S(2)}) collective-permute-start(f32[16,128]{1,0:T(8,128)S(1)} %get-tuple-element.48.after_ref.a_ref), channel_id=1, source_target_pairs={{0,1},{1,0},{2,3},{3,2},{4,5},{5,4},{6,7},{7,6},{8,9},{9,8},{10,11... | collective-permute-start | bytes 24584 | tf_op jit(solution)/shard_map/ppermute | solution.py:642
  15.7 1.2 %shard_map.146.after_ref.refs_4_ = f32[160,128]{1,0:T(8,128)S(1)} custom-call(f32[16,128]{1,0:T(8,128)S(1)} %get-tuple-element.48.after_ref.a_ref, f32[16,48,128]{2,1,0:T(8,128)S(1)} %get-tuple-element.42.a_ref.inside_ref, f32[6,48,128]{2,1,0:T(8,128)S(1)} %get-tuple-element.49.edge_ref, f32[3,48,256]{2,1,0:T(8,128)S(1)} %get-tuple-element.50.slabs_ref, ...), custom_call_target="tpu_custom_call" | custom-call | flops 6000000 | bytes 6000000 | tf_op jit(solution)/shard_map/pallas_call | solution.py:633
  16.9 1.6 %collective-permute-start.5 = (f32[16,128]{1,0:T(8,128)S(1)}, f32[16,128]{1,0:T(8,128)S(1)}, u32[]{:S(2)}, u32[]{:S(2)}) collective-permute-start(f32[16,128]{1,0:T(8,128)S(1)} %shard_map.147.after_ref.a_ref), channel_id=1, source_target_pairs={{0,2},{2,0},{1,3},{3,1},{4,6},{6,4},{5,7},{7,5},{8,10},{10,8},{9,1... | collective-permute-start | bytes 24584 | tf_op jit(solution)/shard_map/ppermute | solution.py:642
  18.5 1.2 %shard_map.148.after_ref.refs_5_ = f32[160,128]{1,0:T(8,128)S(1)} custom-call(f32[16,128]{1,0:T(8,128)S(1)} %shard_map.147.after_ref.a_ref, f32[16,48,128]{2,1,0:T(8,128)S(1)} %get-tuple-element.44.b_ref.inside_ref, f32[6,48,128]{2,1,0:T(8,128)S(1)} %get-tuple-element.51.edge_ref.eb_ref, f32[3,48,256]{2,1,0:T(8,128)S(1)} %get-tuple-element.50.slabs_ref, ...), custom_call_target="tpu_custom_call" | custom-call | flops 6000000 | bytes 6000000 | tf_op jit(solution)/shard_map/pallas_call | solution.py:633
  19.7 1.0 %collective-permute-done.5.b_ref = f32[16,128]{1,0:T(8,128)S(1)} collective-permute-done((f32[16,128]{1,0:T(8,128)S(1)}, f32[16,128]{1,0:T(8,128)S(1)}, u32[]{:S(2)}, u32[]{:S(2)}) %collective-permute-start.5) | collective-permute-done | bytes 8224 | tf_op jit(solution)/shard_map/ppermute | solution.py:642
  20.7 2.8 %collective-permute-start.8 = (f32[16,128]{1,0:T(8,128)S(1)}, f32[16,128]{1,0:T(8,128)S(1)}, u32[]{:S(2)}, u32[]{:S(2)}) collective-permute-start(f32[16,128]{1,0:T(8,128)S(1)} %shard_map.149.after_ref.refs_0_), channel_id=1, source_target_pairs={{0,12},{4,8},{8,4},{12,0},{1,13},{5,9},{9,5},{13,1},{2,14},{6,10},... | collective-permute-start | bytes 24584 | tf_op jit(solution)/shard_map/ppermute | solution.py:653
  23.5 1.3 %collective-permute-start.7 = (f32[16,128]{1,0:T(8,128)S(1)}, f32[16,128]{1,0:T(8,128)S(1)}, u32[]{:S(2)}, u32[]{:S(2)}) collective-permute-start(f32[16,128]{1,0:T(8,128)S(1)} %shard_map.149.after_ref.refs_0_), channel_id=1, source_target_pairs={{0,8},{4,12},{8,0},{12,4},{1,9},{5,13},{9,1},{13,5},{2,10},{6,14},... | collective-permute-start | bytes 24584 | tf_op jit(solution)/shard_map/ppermute | solution.py:653
  25.0 1.2 %shard_map.150.refs_6_ = f32[160,128]{1,0:T(8,128)S(1)} custom-call(f32[16,128]{1,0:T(8,128)S(1)} %shard_map.149.after_ref.refs_0_, f32[16,48,128]{2,1,0:T(8,128)S(1)} %get-tuple-element.45.c_ref.inside_ref, f32[6,48,128]{2,1,0:T(8,128)S(1)} %get-tuple-element.52.edge_ref.ec_ref, f32[3,48,256]{2,1,0:T(8,128)S(1)} %get-tuple-element.50.slabs_ref, ...), custom_call_target="tpu_custom_call" | custom-call | flops 6000000 | bytes 6000000 | tf_op jit(solution)/shard_map/pallas_call | solution.py:633
  26.2 1.8 %collective-permute-done.7.refs_2_ = f32[16,128]{1,0:T(8,128)S(1)} collective-permute-done((f32[16,128]{1,0:T(8,128)S(1)}, f32[16,128]{1,0:T(8,128)S(1)}, u32[]{:S(2)}, u32[]{:S(2)}) %collective-permute-start.7) | collective-permute-done | bytes 8224 | tf_op jit(solution)/shard_map/ppermute | solution.py:653
  28.7 0.8 %collective-permute-start.9 = (f32[64,128]{1,0:T(8,128)S(1)}, f32[64,128]{1,0:T(8,128)S(1)}, u32[]{:S(2)}, u32[]{:S(2)}) collective-permute-start(f32[64,128]{1,0:T(8,128)S(1)} %get-tuple-element.58), channel_id=1, source_target_pairs={{0,4},{1,5},{4,0},{5,1},{8,12},{9,13},{12,8},{13,9},{2,6},{3,7},{6... | collective-permute-start | bytes 98312 | tf_op jit(solution)/shard_map/ppermute | solution.py:533
  29.5 2.0 %collective-permute-start.10 = (f32[64,128]{1,0:T(8,128)S(1)}, f32[64,128]{1,0:T(8,128)S(1)}, u32[]{:S(2)}, u32[]{:S(2)}) collective-permute-start(f32[64,128]{1,0:T(8,128)S(1)} %get-tuple-element.59), channel_id=1, source_target_pairs={{0,8},{1,9},{4,12},{5,13},{8,0},{9,1},{12,4},{13,5},{2,10},{3,11},... | collective-permute-start | bytes 98312 | tf_op jit(solution)/shard_map/ppermute | solution.py:533
  31.5 0.8 %shard_map.152 = f32[16,32,128]{2,1,0:T(8,128)} custom-call(f32[8,128]{1,0:T(8,128)S(1)} %get-tuple-element.53.coef_ref, f32[16,48,128]{2,1,0:T(8,128)S(1)} %get-tuple-element.42.a_ref.inside_ref, f32[16,48,128]{2,1,0:T(8,128)S(1)} %get-tuple-element.44.b_ref.inside_ref, f32[16,48,128]{2,1,0:T(8,128)S(1)} %get-tuple-element.45.c_ref.inside_ref, ...), custom_call_target="tpu_custom_call" | custom-call | flops 2000000 | bytes 2000000 | tf_op jit(solution)/shard_map/pallas_call | solution.py:667
  32.7 1.6 %collective-permute-done.10.refs_2_ = f32[64,128]{1,0:T(8,128)S(1)} collective-permute-done((f32[64,128]{1,0:T(8,128)S(1)}, f32[64,128]{1,0:T(8,128)S(1)}, u32[]{:S(2)}, u32[]{:S(2)}) %collective-permute-start.10) | collective-permute-done | bytes 32800 | tf_op jit(solution)/shard_map/ppermute | solution.py:533
  34.3 0.9 %shard_map.153 = (f32[64,128]{1,0:T(8,128)}, f32[20,64,128]{2,1,0:T(8,128)}) custom-call(f32[2,20,128]{2,1,0:T(8,128)S(1)} %get-tuple-element.41.after_ref.coef_ref, f32[64,128]{1,0:T(8,128)S(1)} %bitcast.12, f32[64,128]{1,0:T(8,128)S(1)} %bitcast.11, f32[64,128]{1,0:T(8,128)S(1)} %get-tuple-element.54.sum_ref, f32[64,128]{1,0:T(8,128)S(1)} %get-tuple-element.55.factor_ref, ...), custom_call_target="tpu_custom_call" | custom-call | flops 2000000 | bytes 2000000 | tf_op jit(solution)/shard_map/pallas_call | solution.py:668
  (35 shorter events, 2.1 us)
Async XLA Ops:
  2.0 1.4 %collective-permute-start = (f32[2,32,128]{2,1,0:T(8,128)S(1)}, f32[2,32,128]{2,1,0:T(8,128)S(1)}, u32[]{:S(2)}, u32[]{:S(2)}) collective-permute-start(f32[2,32,128]{2,1,0:T(8,128)S(1)} %get-tuple-element.35.own_ref), channel_id=1, source_target_pairs={{0,1},{1,0},{2,3},{3,2},{4,5},{5,4},{6,7},{7,6},{8,9},{9,8},{10,11... | collective-permute-start | bytes 98312 | tf_op jit(solution)/shard_map/ppermute | solution.py:583
  3.4 2.9 %copy-start = (s32[16,32,128]{2,1,0:T(8,128)S(1)}, s32[16,32,128]{2,1,0:T(8,128)}, u32[]{:S(2)}) copy-start(s32[16,32,128]{2,1,0:T(8,128)} %label_hbm.1) | copy-start | bytes 786436
  3.5 5.4 %collective-permute-start.1 = (f32[17,8,128]{2,1,0:T(8,128)S(1)}, f32[17,8,128]{2,1,0:T(8,128)S(1)}, u32[]{:S(2)}, u32[]{:S(2)}) collective-permute-start(f32[17,8,128]{2,1,0:T(8,128)S(1)} %get-tuple-element.38), channel_id=1, source_target_pairs={{0,2},{2,0},{1,3},{3,1},{4,6},{6,4},{5,7},{7,5},{8,10},{10,8},{9,1... | collective-permute-start | bytes 208904 | tf_op jit(solution)/shard_map/ppermute | solution.py:593
  8.9 3.0 %copy-start.1 = (f32[20,1,8192]{2,1,0:T(1,128)S(1)}, f32[20,1,8192]{2,1,0:T(1,128)}, u32[]{:S(2)}) copy-start(f32[20,1,8192]{2,1,0:T(1,128)} %param.17) | copy-start | bytes 1966084
  8.9 3.0 %copy-start.2 = (f32[20,1,8192]{2,1,0:T(1,128)S(1)}, f32[20,1,8192]{2,1,0:T(1,128)}, u32[]{:S(2)}) copy-start(f32[20,1,8192]{2,1,0:T(1,128)} %param.19) | copy-start | bytes 1966084
  8.9 5.5 %collective-permute-start.2 = (f32[6,40,128]{2,1,0:T(8,128)S(1)}, f32[6,40,128]{2,1,0:T(8,128)S(1)}, u32[]{:S(2)}, u32[]{:S(2)}) collective-permute-start(f32[6,40,128]{2,1,0:T(8,128)S(1)} %get-tuple-element.46), channel_id=1, source_target_pairs={{0,4},{1,5},{4,0},{5,1},{8,12},{9,13},{12,8},{13,9},{2,6},{3,7},{6... | collective-permute-start | bytes 368648 | tf_op jit(solution)/shard_map/ppermute | solution.py:533
  10.9 3.6 %collective-permute-start.3 = (f32[6,40,128]{2,1,0:T(8,128)S(1)}, f32[6,40,128]{2,1,0:T(8,128)S(1)}, u32[]{:S(2)}, u32[]{:S(2)}) collective-permute-start(f32[6,40,128]{2,1,0:T(8,128)S(1)} %get-tuple-element.47), channel_id=1, source_target_pairs={{0,1},{1,0},{4,8},{5,9},{8,4},{9,5},{12,13},{13,12},{2,3},{3,2},{6... | collective-permute-start | bytes 368648 | tf_op jit(solution)/shard_map/ppermute | solution.py:533
  10.9 1.0 %copy-start.3 = (f32[1,8192]{1,0:T(1,128)S(1)}, f32[1,8192]{1,0:T(1,128)}, u32[]{:S(2)}) copy-start(f32[1,8192]{1,0:T(1,128)} %param.16) | copy-start | bytes 98308
  10.9 1.0 %copy-start.8 = (f32[20]{0:T(128)S(1)}, f32[20]{0:T(128)}, u32[]{:S(2)}) copy-start(f32[20]{0:T(128)} %cond_ref.1) | copy-start | bytes 244
  10.9 1.0 %copy-start.9 = (f32[20]{0:T(128)S(1)}, f32[20]{0:T(128)}, u32[]{:S(2)}) copy-start(f32[20]{0:T(128)} %rev_ref.1) | copy-start | bytes 244
  11.8 0.7 %copy-start.5 = (f32[20]{0:T(128)S(1)}, f32[20]{0:T(128)}, u32[]{:S(2)}) copy-start(f32[20]{0:T(128)} %half_ref.1) | copy-start | bytes 244
  11.8 0.7 %copy-start.6 = (f32[20]{0:T(128)S(1)}, f32[20]{0:T(128)}, u32[]{:S(2)}) copy-start(f32[20]{0:T(128)} %slope_ref.1) | copy-start | bytes 244
  11.9 0.7 %copy-start.7 = (f32[20]{0:T(128)S(1)}, f32[20]{0:T(128)}, u32[]{:S(2)}) copy-start(f32[20]{0:T(128)} %tau_ref.1) | copy-start | bytes 244
  15.2 1.8 %collective-permute-start.4 = (f32[16,128]{1,0:T(8,128)S(1)}, f32[16,128]{1,0:T(8,128)S(1)}, u32[]{:S(2)}, u32[]{:S(2)}) collective-permute-start(f32[16,128]{1,0:T(8,128)S(1)} %get-tuple-element.48.after_ref.a_ref), channel_id=1, source_target_pairs={{0,1},{1,0},{2,3},{3,2},{4,5},{5,4},{6,7},{7,6},{8,9},{9,8},{10,11... | collective-permute-start | bytes 24584 | tf_op jit(solution)/shard_map/ppermute | solution.py:642
  16.9 3.7 %collective-permute-start.5 = (f32[16,128]{1,0:T(8,128)S(1)}, f32[16,128]{1,0:T(8,128)S(1)}, u32[]{:S(2)}, u32[]{:S(2)}) collective-permute-start(f32[16,128]{1,0:T(8,128)S(1)} %shard_map.147.after_ref.a_ref), channel_id=1, source_target_pairs={{0,2},{2,0},{1,3},{3,1},{4,6},{6,4},{5,7},{7,5},{8,10},{10,8},{9,1... | collective-permute-start | bytes 24584 | tf_op jit(solution)/shard_map/ppermute | solution.py:642
  20.7 5.6 %collective-permute-start.8 = (f32[16,128]{1,0:T(8,128)S(1)}, f32[16,128]{1,0:T(8,128)S(1)}, u32[]{:S(2)}, u32[]{:S(2)}) collective-permute-start(f32[16,128]{1,0:T(8,128)S(1)} %shard_map.149.after_ref.refs_0_), channel_id=1, source_target_pairs={{0,12},{4,8},{8,4},{12,0},{1,13},{5,9},{9,5},{13,1},{2,14},{6,10},... | collective-permute-start | bytes 24584 | tf_op jit(solution)/shard_map/ppermute | solution.py:653
  23.5 4.5 %collective-permute-start.7 = (f32[16,128]{1,0:T(8,128)S(1)}, f32[16,128]{1,0:T(8,128)S(1)}, u32[]{:S(2)}, u32[]{:S(2)}) collective-permute-start(f32[16,128]{1,0:T(8,128)S(1)} %shard_map.149.after_ref.refs_0_), channel_id=1, source_target_pairs={{0,8},{4,12},{8,0},{12,4},{1,9},{5,13},{9,1},{13,5},{2,10},{6,14},... | collective-permute-start | bytes 24584 | tf_op jit(solution)/shard_map/ppermute | solution.py:653
  24.8 3.7 %collective-permute-start.6 = (f32[16,128]{1,0:T(8,128)S(1)}, f32[16,128]{1,0:T(8,128)S(1)}, u32[]{:S(2)}, u32[]{:S(2)}) collective-permute-start(f32[16,128]{1,0:T(8,128)S(1)} %shard_map.149.after_ref.refs_0_), channel_id=1, source_target_pairs={{0,4},{4,0},{8,12},{12,8},{1,5},{5,1},{9,13},{13,9},{2,6},{6,2},{1... | collective-permute-start | bytes 24584 | tf_op jit(solution)/shard_map/ppermute | solution.py:653
  28.7 4.0 %collective-permute-start.9 = (f32[64,128]{1,0:T(8,128)S(1)}, f32[64,128]{1,0:T(8,128)S(1)}, u32[]{:S(2)}, u32[]{:S(2)}) collective-permute-start(f32[64,128]{1,0:T(8,128)S(1)} %get-tuple-element.58), channel_id=1, source_target_pairs={{0,4},{1,5},{4,0},{5,1},{8,12},{9,13},{12,8},{13,9},{2,6},{3,7},{6... | collective-permute-start | bytes 98312 | tf_op jit(solution)/shard_map/ppermute | solution.py:533
  29.5 4.8 %collective-permute-start.10 = (f32[64,128]{1,0:T(8,128)S(1)}, f32[64,128]{1,0:T(8,128)S(1)}, u32[]{:S(2)}, u32[]{:S(2)}) collective-permute-start(f32[64,128]{1,0:T(8,128)S(1)} %get-tuple-element.59), channel_id=1, source_target_pairs={{0,8},{1,9},{4,12},{5,13},{8,0},{9,1},{12,4},{13,5},{2,10},{3,11},... | collective-permute-start | bytes 98312 | tf_op jit(solution)/shard_map/ppermute | solution.py:533
  31.5 2.8 %collective-permute-start.11 = (f32[64,128]{1,0:T(8,128)S(1)}, f32[64,128]{1,0:T(8,128)S(1)}, u32[]{:S(2)}, u32[]{:S(2)}) collective-permute-start(f32[64,128]{1,0:T(8,128)S(1)} %get-tuple-element.60), channel_id=1, source_target_pairs={{0,1},{1,0},{4,8},{5,9},{8,4},{9,5},{12,13},{13,12},{2,3},{3,2},{6... | collective-permute-start | bytes 98312 | tf_op jit(solution)/shard_map/ppermute | solution.py:533
  31.5 2.8 %copy-start.4 = (f32[1,8192]{1,0:T(1,128)S(1)}, f32[1,8192]{1,0:T(1,128)}, u32[]{:S(2)}) copy-start(f32[1,8192]{1,0:T(1,128)} %param.18) | copy-start | bytes 98308

commit v10 on v6

--- a/solution.py
+++ b/solution.py
@@ -89,75 +89,65 @@
     stat_ref[1] = jnp.broadcast_to(jnp.sum(cells, axis=0, keepdims=True), (SUB, nz))
 
 
-def y_faces_kernel(w0_ref, inv_ref, own_ref, got_ref, slab_ref, up_ref, down_ref):
+def steps_of(axis):
+    return 1 if lax.axis_size(axis) == 2 else 2
+
+
+def upper_in(axis, step):
+    return lax.rem(lax.axis_index(axis), 2) == step
+
+
+def has_partner(axis, step):
+    here = lax.axis_index(axis)
+    return jnp.where(upper_in(axis, step), here < lax.axis_size(axis) - 1, here > 0)
+
+
+def unpack_rows(tile, step):
+    sub = subs_of(tile.shape)
+    up, there = upper_in("gy", step), has_partner("gy", step)
+    depth = jnp.where(there, jnp.where(up, SUB - 1 - sub, sub), -1)
+    return jnp.where(depth >= 5, tile, 0.0), jnp.where(depth >= 6, pltpu.roll(tile, 4, 0), 0.0)
+
+
+def halo_rows(tiles):
+    w_tile, i_tile = unpack_rows(tiles[0], 0)
+    for step, tile in enumerate(tiles[1:], 1):
+        w_more, i_more = unpack_rows(tile, step)
+        w_tile, i_tile = w_tile + w_more, i_tile + i_more
+    return w_tile, i_tile
+
+
+def faces_kernel(n_y, w0_ref, inv_ref, own_ref, got_ref, slab_ref, *refs):
+    y_refs, x_refs, edge_refs = refs[:n_y], refs[n_y : n_y + 2], refs[n_y + 2 :]
     nx, ny, nz = w0_ref.shape
     sub = subs_of((SUB, nz))
+    lane = lanes_of((ny, nz))
     slab_ref[...] = own_ref[...] + got_ref[...]
-    for x in range(nx + 1):
-        if x < nx:
-            w_last, w_first = w0_ref[x, ny - SUB :], w0_ref[x, :SUB]
-            i_last, i_first = inv_ref[x, ny - SUB :], inv_ref[x, :SUB]
-        else:
-            w_last, w_first = slab_ref[0, ny - SUB :], slab_ref[0, :SUB]
-            i_last, i_first = slab_ref[1, ny - SUB :], slab_ref[1, :SUB]
-        up_ref[x] = jnp.where(sub >= 5, w_last, pltpu.roll(i_last, 4, 0))
-        down_ref[x] = jnp.where(sub <= 2, w_first, pltpu.roll(i_first, 4, 0))
-
-
-def y_face_one_kernel(w0_ref, inv_ref, own_ref, got_ref, slab_ref, face_ref):
-    nx, ny, nz = w0_ref.shape
-    sub = subs_of((SUB, nz))
-    up = lax.axis_index("gy") == 0
-    keep_w = jnp.where(up, sub, SUB - 1 - sub) >= 5
-    slab_ref[...] = own_ref[...] + got_ref[...]
-    for x in range(nx + 1):
-        if x < nx:
-            w_last, w_first = w0_ref[x, ny - SUB :], w0_ref[x, :SUB]
-            i_last, i_first = inv_ref[x, ny - SUB :], inv_ref[x, :SUB]
-        else:
-            w_last, w_first = slab_ref[0, ny - SUB :], slab_ref[0, :SUB]
-            i_last, i_first = slab_ref[1, ny - SUB :], slab_ref[1, :SUB]
-        w_face = jnp.where(up, w_last, w_first)
-        i_face = jnp.where(up, i_last, i_first)
-        face_ref[x] = jnp.where(keep_w, w_face, pltpu.roll(i_face, 4, 0))
-
-
-def x_faces_kernel(one, after_ref, w0_ref, inv_ref, slab_ref, *refs):
-    if one:
-        got_ref, halo_ref, first_ref, second_ref = refs
-    else:
-        low_ref, high_ref, halo_ref, first_ref, second_ref = refs
-    nx, ny, nz = w0_ref.shape
-    sub = subs_of((SUB, nz))
-    lane = lanes_of((ny + SUB, nz))
-    if one:
-        gy = lax.axis_index("gy")
-        w_rows = ((gy == 1) & (sub >= 5)) | ((gy == 0) & (sub <= 2))
-        i_rows = ((gy == 1) & (sub >= 6)) | ((gy == 0) & (sub <= 1))
-    for x in range(nx + 1):
-        if one:
-            got = got_ref[x]
-            halo_ref[0, x] = jnp.where(w_rows, got, 0.0)
-            halo_ref[1, x] = jnp.where(i_rows, pltpu.roll(got, 4, 0), 0.0)
-        else:
-            low, high = low_ref[x], high_ref[x]
-            halo_ref[0, x] = jnp.where(sub >= 5, low, jnp.where(sub <= 2, high, 0.0))
-            halo_ref[1, x] = jnp.where(
-                sub >= 6, pltpu.roll(low, 4, 0), jnp.where(sub <= 1, pltpu.roll(high, 4, 0), 0.0)
-            )
-    odd = lax.rem(lax.axis_index("gx"), 2)
-    slab_w = jnp.concatenate([slab_ref[0], halo_ref[0, nx]], axis=0)
-    slab_i = jnp.concatenate([slab_ref[1], halo_ref[1, nx]], axis=0)
-    half = pltpu.roll(slab_i, nz // 2, 1)
-    up = jnp.where(lane >= nz - 3 * PACK, slab_w, half)
-    down = jnp.where(lane < 3 * PACK, slab_w, half)
-    for face_ref, lower in ((first_ref, odd), (second_ref, 1 - odd)):
-        for k in range(5):
-            field, source = (0, w0_ref) if k < 3 else (1, inv_ref)
-            place = (1 - lower) * (nx - 3 + field) + k - 3 * field
-            face_ref[k, :ny] = source[place]
-            face_ref[k, ny:] = halo_ref[field, place]
-        face_ref[5] = jnp.where(lower == 1, down, up)
+    for step, face_ref in enumerate(y_refs):
+        up = upper_in("gy", step)
+        keep_w = jnp.where(up, sub, SUB - 1 - sub) >= 5
+        for x in range(nx + 1):
+            w_rows, i_rows = (w0_ref.at[x], inv_ref.at[x]) if x < nx else (slab_ref.at[0], slab_ref.at[1])
+            w_face = jnp.where(up, w_rows[ny - SUB :], w_rows[:SUB])
+            i_face = jnp.where(up, i_rows[ny - SUB :], i_rows[:SUB])
+            face_ref[x] = jnp.where(keep_w, w_face, pltpu.roll(i_face, 4, 0))
+    slab_w = slab_ref[0]
+    half = pltpu.roll(slab_ref[1], nz // 2, 1)
+    up_slab = jnp.where(lane >= nz - 3 * PACK, slab_w, half)
+    down_slab = jnp.where(lane < 3 * PACK, slab_w, half)
+    for step, face_ref in enumerate(x_refs):
+        up = upper_in("gx", step)
+        first = jnp.where(up, nx - 3, 0)
+        for k in range(3):
+            face_ref[k] = w0_ref[first + k]
+        for k in range(2):
+            face_ref[3 + k] = inv_ref[jnp.where(up, nx - 2, 0) + k]
+        face_ref[5] = jnp.where(up, up_slab, down_slab)
+        for y_step, y_ref in enumerate(y_refs):
+            edge_ref = edge_refs[step * n_y + y_step]
+            for k in range(3):
+                edge_ref[k] = y_ref[first + k]
+            edge_ref[3] = y_ref[nx]
 
 
 def slab_step(v, s, inv):
@@ -226,20 +216,22 @@
         sums[2 * stage + k] = total
 
 
-def inner_kernel(
-    w0_ref, inv_ref, slab_ref, halo_ref, a_ref, i_ref, b_ref, c_ref, sum_ref, slabs_ref,
-):
+def inner_kernel(n_y, w0_ref, inv_ref, slab_ref, *refs):
+    y_refs, (a_ref, i_ref, b_ref, c_ref, sum_ref, own_slab_ref, slabs_ref) = refs[:n_y], refs[n_y:]
     nx, ny, nz = w0_ref.shape
     gz = lax.axis_index("gz")
-    for x in range(nx):
-        for ref, own, halo in ((a_ref, w0_ref[x], halo_ref[0, x]), (i_ref, inv_ref[x], halo_ref[1, x])):
-            ref[x, :SUB] = halo
-            ref[x, SUB : SUB + ny] = own
-            ref[x, SUB + ny :] = halo
+    for x in range(nx + 1):
+        halos = halo_rows([ref[x] for ref in y_refs])
+        for k in range(2):
+            if x < nx:
+                ref, own = (a_ref, i_ref)[k].at[x], (w0_ref, inv_ref)[k][x]
+            else:
+                ref, own = own_slab_ref.at[k], slab_ref[k]
+            ref[:SUB] = halos[k]
+            ref[SUB : SUB + ny] = own
+            ref[SUB + ny :] = halos[k]
     for k in range(2):
-        slabs_ref[3 * k, :SUB] = halo_ref[k, nx]
-        slabs_ref[3 * k, SUB : SUB + ny] = slab_ref[k]
-        slabs_ref[3 * k, SUB + ny :] = halo_ref[k, nx]
+        slabs_ref[3 * k] = own_slab_ref[k]
     sums = {}
     for stage in range(3):
         source, target = (a_ref, b_ref, c_ref)[stage], (b_ref, c_ref, None)[stage]
@@ -263,39 +255,56 @@
 
 
 def outer_kernel(
-    a_ref, i_ref, b_ref, c_ref, slab_ref, halo_ref, sum_ref, first_ref, second_ref, stat_ref,
-    ea_ref, eb_ref, ec_ref, slabs_ref, total_ref, ei_ref, si_ref,
+    n_y, after_ref, a_ref, i_ref, b_ref, c_ref, slab_ref, sum_ref, stat_ref, *refs
 ):
+    x_refs, corner_refs = refs[:2], refs[2 : 2 + 2 * n_y]
+    ea_ref, eb_ref, ec_ref, slabs_ref, total_ref, ei_ref, si_ref = refs[2 + 2 * n_y :]
     nx, ny, nz = a_ref.shape[0], a_ref.shape[1] - 2 * SUB, a_ref.shape[2]
     ring = ny + SUB
     gz = lax.axis_index("gz")
     odd = lax.rem(lax.axis_index("gx"), 2) == 1
 
-    def low(k):
-        return jnp.where(odd, first_ref[k], second_ref[k])
-
-    def high(k):
-        return jnp.where(odd, second_ref[k], first_ref[k])
-
-    for ref, at, plane in (
-        [(ea_ref, k, low(k)) for k in range(3)] + [(ea_ref, 3 + k, high(k)) for k in range(3)]
-        + [(ei_ref, k, low(3 + k)) for k in range(2)] + [(ei_ref, 2 + k, high(3 + k)) for k in range(2)]
-    ):
-        ref[at, :SUB] = plane[ny:]
-        ref[at, SUB : SUB + ny] = plane[:ny]
-        ref[at, SUB + ny :] = plane[ny:]
-
-    lane = lanes_of((ring, nz))
-    lo5, hi5 = low(5), high(5)
-    slab_w = jnp.where(lane < 3 * PACK, hi5, 0.0) + jnp.where(lane >= nz - 3 * PACK, lo5, 0.0)
-    lo5, hi5 = pltpu.roll(lo5, nz // 2, 1), pltpu.roll(hi5, nz // 2, 1)
-    slab_i = jnp.where(lane < 2 * PACK, hi5, 0.0) + jnp.where(lane >= nz - 2 * PACK, lo5, 0.0)
-    for ref, k, beyond in ((slabs_ref, 0, slab_w), (si_ref, 1, slab_i)):
-        ref[0, SUB : SUB + ny, :nz] = slab_ref[k]
-        ref[0, SUB : SUB + ny, nz:] = beyond[:ny]
-        for rows in (slice(0, SUB), slice(SUB + ny, SUB + ring)):
-            ref[0, rows, :nz] = halo_ref[k, nx]
-            ref[0, rows, nz:] = beyond[ny:]
+    def beyond(upper, read):
+        there = has_partner("gx", 0) if upper else has_partner("gx", 1)
+        swapped = has_partner("gx", 1) if upper else has_partner("gx", 0)
+        first, second = read(0), read(1)
+        if upper:
+            return jnp.where(jnp.where(odd, swapped, there), jnp.where(odd, second, first), 0.0)
+        return jnp.where(jnp.where(odd, swapped, there), jnp.where(odd, first, second), 0.0)
+
+    def write(ref, at, own, halo):
+        ref[at, :SUB] = halo
+        ref[at, SUB : SUB + ny] = own
+        ref[at, SUB + ny :] = halo
+
+    lane_tile, lane = lanes_of((SUB, nz)), lanes_of((ny, nz))
+    slab_parts = []
+    for side, upper in enumerate((False, True)):
+        tiles = [
+            halo_rows([beyond(upper, lambda step: corner_refs[step * n_y + j][k]) for j in range(n_y)])
+            for k in range(4)
+        ]
+        for k in range(3):
+            write(ea_ref, 3 * side + k, beyond(upper, lambda step: x_refs[step][k]), tiles[k][0])
+        for k in range(2):
+            own = beyond(upper, lambda step: x_refs[step][3 + k])
+            write(ei_ref, 2 * side + k, own, tiles[k if upper else k + 1][1])
+        own = beyond(upper, lambda step: x_refs[step][5])
+
+        def near(value, lanes, planes):
+            return jnp.where(lanes < planes * PACK if upper else lanes >= nz - planes * PACK, value, 0.0)
+
+        slab_parts.append((
+            near(own, lane, 3), near(tiles[3][0], lane_tile, 3),
+            near(pltpu.roll(own, nz // 2, 1), lane, 2), near(tiles[3][1], lane_tile, 2),
+        ))
+
+    low, high = slab_parts
+    for ref, k in ((slabs_ref, 0), (si_ref, 1)):
+        ref[0, :, :nz] = slab_ref[k]
+        ref[0, SUB : SUB + ny, nz:] = low[2 * k] + high[2 * k]
+        ref[0, :SUB, nz:] = low[2 * k + 1] + high[2 * k + 1]
+        ref[0, SUB + ny :, nz:] = low[2 * k + 1] + high[2 * k + 1]
 
     def reader(inside_ref, edge_ref, first, count):
         def get(x, row):
@@ -515,19 +524,31 @@
         gate_ref[g] = base_ref[g] - (coef_ref[0, g : g + 1] * cot) * (v - coef_ref[1, g : g + 1])
 
 
-def both_ways(up, down, axis):
+def partners(axis, step):
     count = lax.axis_size(axis)
-    low = lax.ppermute(up, axis, [(i, i + 1) for i in range(count - 1)])
-    high = lax.ppermute(down, axis, [(i + 1, i) for i in range(count - 1)])
-    return low, high
-
-
-def pair_swaps(first, second, axis):
-    count = lax.axis_size(axis)
-    even = [(i, i ^ 1) for i in range(count)]
-    between = [(i, i + 1) for i in range(1, count - 1, 2)]
-    between = between + [(j, i) for i, j in between]
-    return lax.ppermute(first, axis, even), lax.ppermute(second, axis, between)
+    if step == 0:
+        return [i ^ 1 for i in range(count)]
+    return [0] + [i + 1 if i % 2 else i - 1 for i in range(1, count - 1)] + [count - 1]
+
+
+def swap(value, x_to=None, y_to=None):
+    n_x, n_y, n_z = [lax.axis_size(axis) for axis in ("gx", "gy", "gz")]
+    pairs = []
+    for x in range(n_x):
+        for y in range(n_y):
+            to_x, to_y = x_to[x] if x_to else x, y_to[y] if y_to else y
+            alone = (x_to and to_x == x) or (y_to and to_y == y)
+            for z in range(n_z):
+                to = (x, y, z ^ 1) if alone else (to_x, to_y, z)
+                pairs.append(((x * n_y + y) * n_z + z, (to[0] * n_y + to[1]) * n_z + to[2]))
+    return lax.ppermute(value, ("gx", "gy", "gz"), pairs)
+
+
+def block_partners(count, k, slots, block):
+    def apart(tile, owner):
+        return owner * block >= (tile + 1) * slots or (owner + 1) * block <= count * block - (count - tile) * slots
+
+    return [i if apart(i, i ^ k) and apart(i ^ k, i) else i ^ k for i in range(count)]
 
 
 def reduce_over(value, axis):
@@ -560,7 +581,7 @@
         specs=[HBM] * 3,
         scratch=[
             pltpu.VMEM((nx, ny, nz), F32), pltpu.VMEM((nx, ny, nz), F32), pltpu.VMEM((nx, ny, nz), jnp.int32),
-            pltpu.SemaphoreType.DMA((3, 4)),
+            pltpu.SemaphoreType.DMA((3, 2)),
         ],
     )(in_hbm(potential_cot), in_hbm(damping), in_hbm(tissue_label))
 
@@ -569,36 +590,35 @@
         stat, flat(tissue_label)
     )
 
-    face = shape_of(nx + 1, SUB, nz)
-    slab_shape = shape_of(2, ny, nz)
-    x_shapes = (shape_of(2, nx + 1, SUB, nz), shape_of(6, ring, nz), shape_of(6, ring, nz))
-    if n_gy == 2:
-        slab, mine = call(y_face_one_kernel, (slab_shape, face), 4)(w0, inv, packed, got)
-        halo = (lax.ppermute(mine, "gy", [(0, 1), (1, 0)]),)
-    else:
-        slab, up, down = call(y_faces_kernel, (slab_shape, face, face), 4)(w0, inv, packed, got)
-        halo = both_ways(up, down, "gy")
-    edge_rows, first, second = call(
-        functools.partial(x_faces_kernel, n_gy == 2), x_shapes, 4 + len(halo)
-    )(plan, w0, inv, slab, *halo)
-    first, second = pair_swaps(first, second, "gx")
+    n_y = steps_of("gy")
+    shapes = (
+        (shape_of(2, ny, nz),) + (shape_of(nx + 1, SUB, nz),) * n_y + (shape_of(6, ny, nz),) * 2
+        + (shape_of(4, SUB, nz),) * (2 * n_y)
+    )
+    slab, *faces = call(functools.partial(faces_kernel, n_y), shapes, 4)(w0, inv, packed, got)
+    along_y, along_x, across = faces[:n_y], faces[n_y : n_y + 2], faces[n_y + 2 :]
+    y_to = [partners("gy", step) for step in range(n_y)]
+    x_to = [partners("gx", step) for step in range(2)]
+    along_y = [swap(face, y_to=y_to[j]) for j, face in enumerate(along_y)]
+    along_x = [swap(face, x_to=x_to[i]) for i, face in enumerate(along_x)]
+    across = [swap(face, x_to=x_to[k // n_y], y_to=y_to[k % n_y]) for k, face in enumerate(across)]
 
     tall = ring + SUB
     planes = shape_of(nx, tall, nz)
     edges = shape_of(6, tall, nz)
-    in0, in_inv, in1, in2, in_sums = call(
-        inner_kernel,
-        (planes,) * 4 + (shape_of(5, SUB, nz),),
-        4,
+    in0, in_inv, in1, in2, in_sums, own_slab = call(
+        functools.partial(inner_kernel, n_y),
+        (planes,) * 4 + (shape_of(5, SUB, nz), shape_of(2, tall, nz)),
+        3 + n_y,
         scratch=[pltpu.VMEM((4, tall, nz), F32)],
         cost=6_000_000,
-    )(w0, inv, slab, edge_rows)
+    )(w0, inv, slab, *along_y)
     ends0, ends1, ends2, slabs, sums = call(
-        outer_kernel,
+        functools.partial(outer_kernel, n_y),
         (edges,) * 3 + (shape_of(3, tall, 2 * nz), shape_of(16, nz)),
-        10,
+        10 + 2 * n_y,
         scratch=[pltpu.VMEM((4, tall, nz), F32), pltpu.VMEM((1, tall, 2 * nz), F32)],
-    )(in0, in_inv, in1, in2, slab, edge_rows, in_sums, first, second, stat)
+    )(plan, in0, in_inv, in1, in2, own_slab, in_sums, stat, *along_x, *across)
 
     def couple(stage, after, inside, ends):
         return call(
@@ -632,7 +652,7 @@
         scratch=[pltpu.VMEM((n_gx * block_rows + slot_rows + SUB, LANES), F32)],
     )(*sums, list0, list1, list2)
     landed = blocks[:1] + [
-        lax.ppermute(blocks[k], "gx", [(i, i ^ k) for i in range(n_gx)]) for k in range(1, n_gx)
+        swap(blocks[k], x_to=block_partners(n_gx, k, slot_rows, block_rows)) for k in [2, 1] + list(range(3, n_gx))
     ]
 
     solution = call(potential_kernel, block, 6)(coefs, in0, in1, in2, ends1, ends2)

time: 40.3 us -> 33.9 us (0.84)
  waiting for transfers between devices: 6.85 us -> 3 us
  starting transfers between devices: 19.3 us -> 16.9 us
    ppermute x6 -> x8, waiting for transfers between devices: 3.45 us -> 0.02 us  [swap(): return lax.ppermute(value, ('gx', 'gy', 'gz'), pairs)]
    ppermute x3, starting transfers between devices: 6.92 us -> 4.39 us  [local(): lax.ppermute(sums, 'gx', [(i, i ^ k) for i in range(n_gx)])]
    ppermute x3, waiting for transfers between devices: 1.89 us -> 1.15 us  [local(): lax.ppermute(sums, 'gx', [(i, i ^ k) for i in range(n_gx)])]
    ppermute x6 -> x8, starting transfers between devices: 9.92 us -> 9.83 us  [swap(): return lax.ppermute(value, ('gx', 'gy', 'gz'), pairs)]
    pallas_call x4 -> x3, Pallas kernels: 1.74 us -> 1.68 us  [the longest x1 0.94 us: local(): call(functools.partial(inner_kernel, n_y), (planes,) * 4 + (shape_of(5, S...]
  transfers between devices with their start and end apart: 12 -> 14, of which waited for: 7 -> 3; matrix products, arithmetic and copies ran while one was open for 0% -> 0% of each run, Pallas kernels for 22% -> 26%
where the time goes in v10:
time: 33.9 us; the launch traced here: 33.7 us
  starting transfers between devices  16.9 us (50%)
  Pallas kernels  12.2 us (36%)
  waiting for transfers between devices  3 us (9%)
  between operations  0.83 us (2%)
  local copies, waits for them, and re-layouts  0.8 us (2%)
    ppermute x8, starting transfers between devices, swap(): return lax.ppermute(value, ('gx', 'gy', 'gz'), pairs)  9.83 us
    ppermute x3, starting transfers between devices, local(): lax.ppermute(sums, 'gx', [(i, i ^ k) for i in range(n_gx)])  4.39 us
    pallas_call x3, Pallas kernels, couple(): call(functools.partial(couple_kernel, stage, slot_rows), shape_of(slot_ro...  3.55 us
    ppermute x2, starting transfers between devices, add(): lax.ppermute(value, axis, [(i, i ^ step) for i in range(lax.axis_size(axi...  2.13 us
    pallas_call x1, Pallas kernels, local(): call(membrane_kernel, (shape_of(n_states, block_rows, LANES), shape_of(bl...  1.92 us
    pallas_call x1, Pallas kernels, local(): call(plan_kernel, jax.ShapeDtypeStruct((rows, LANES), jnp.int32), 2, cost...  1.72 us
    pallas_call x1, Pallas kernels, local(): call(start_kernel, (block, block, shape_of(2, ny, nz), shape_of(2, SUB, n...  1.4 us
    ppermute x3, waiting for transfers between devices, local(): lax.ppermute(sums, 'gx', [(i, i ^ k) for i in range(n_gx)])  1.15 us
  transfers between devices with their start and end apart: 14, of which 3 were waited for; matrix products, arithmetic and copies ran while one was open for 0% of the time, Pallas kernels for 26%

profile of v10, /device:TPU:0, one launch (start us, length us, event | category | flops | bytes accessed | tf_op | source)
XLA Modules:
  0.0 33.7 jit_solution(14770751417041465047)
XLA Ops:
  0.6 1.4 %shard_map.139 = (f32[16,32,128]{2,1,0:T(8,128)S(1)}, f32[16,32,128]{2,1,0:T(8,128)S(1)}, f32[2,32,128]{2,1,0:T(8,128)S(1)}, f32[2,8,128]{2,1,0:T(8,128)S(1)}) custom-call(f32[16,32,128]{2,1,0:T(8,128)} %right_hbm.1, f32[16,32,128]{2,1,0:T(8,128)} %damping_hbm.1, s32[16,32,128]{2,1,0:T(8,128)} %label_hbm.1), custom_call_target="tpu_custom_call" | custom-call | flops 2000000 | bytes 2000000 | tf_op jit(solution)/shard_map/pallas_call | solution.py:579
  2.0 0.5 %collective-permute-start = (f32[2,32,128]{2,1,0:T(8,128)S(1)}, f32[2,32,128]{2,1,0:T(8,128)S(1)}, u32[]{:S(2)}, u32[]{:S(2)}) collective-permute-start(f32[2,32,128]{2,1,0:T(8,128)S(1)} %get-tuple-element.38.own_ref), channel_id=1, source_target_pairs={{0,1},{1,0},{2,3},{3,2},{4,5},{5,4},{6,7},{7,6},{8,9},{9,8},{10,11... | collective-permute-start | bytes 98312 | tf_op jit(solution)/shard_map/ppermute | solution.py:588
  2.6 0.9 %collective-permute-done.got_ref = f32[2,32,128]{2,1,0:T(8,128)S(1)} collective-permute-done((f32[2,32,128]{2,1,0:T(8,128)S(1)}, f32[2,32,128]{2,1,0:T(8,128)S(1)}, u32[]{:S(2)}, u32[]{:S(2)}) %collective-permute-start) | collective-permute-done | bytes 32800 | tf_op jit(solution)/shard_map/ppermute | solution.py:588
  3.5 3.0 %collective-permute-start.2 = (f32[6,32,128]{2,1,0:T(8,128)S(1)}, f32[6,32,128]{2,1,0:T(8,128)S(1)}, u32[]{:S(2)}, u32[]{:S(2)}) collective-permute-start(f32[6,32,128]{2,1,0:T(8,128)S(1)} %get-tuple-element.47), channel_id=1, source_target_pairs={{0,4},{1,5},{2,6},{3,7},{4,0},{5,1},{6,2},{7,3},{8,12},{9,13},{10,... | collective-permute-start | bytes 294920 | tf_op jit(solution)/shard_map/ppermute | solution.py:544
  6.5 1.5 %collective-permute-start.1 = (f32[17,8,128]{2,1,0:T(8,128)S(1)}, f32[17,8,128]{2,1,0:T(8,128)S(1)}, u32[]{:S(2)}, u32[]{:S(2)}) collective-permute-start(f32[17,8,128]{2,1,0:T(8,128)S(1)} %get-tuple-element.40), channel_id=1, source_target_pairs={{0,2},{1,3},{2,0},{3,1},{4,6},{5,7},{6,4},{7,5},{8,10},{9,11},{10,... | collective-permute-start | bytes 208904 | tf_op jit(solution)/shard_map/ppermute | solution.py:544
  7.9 3.1 %collective-permute-start.4 = (f32[4,8,128]{2,1,0:T(8,128)S(1)}, f32[4,8,128]{2,1,0:T(8,128)S(1)}, u32[]{:S(2)}, u32[]{:S(2)}) collective-permute-start(f32[4,8,128]{2,1,0:T(8,128)S(1)} %get-tuple-element.49), channel_id=1, source_target_pairs={{0,6},{1,7},{2,4},{3,5},{4,2},{5,3},{6,0},{7,1},{8,14},{9,15},{10,... | collective-permute-start | bytes 49160 | tf_op jit(solution)/shard_map/ppermute | solution.py:544
  11.1 1.7 %shard_map.140.after_ref.plan_ref = s32[512,128]{1,0:T(8,128)S(1)} custom-call(f32[2,8,128]{2,1,0:T(8,128)S(1)} %get-tuple-element.35.after_ref.stat_ref, s32[512,128]{1,0:T(8,128)S(1)} %bitcast.7), custom_call_target="tpu_custom_call" | custom-call | flops 6000000 | bytes 6000000 | tf_op jit(solution)/shard_map/pallas_call | solution.py:589
  12.8 0.9 %shard_map.142 = (f32[16,48,128]{2,1,0:T(8,128)S(1)}, f32[16,48,128]{2,1,0:T(8,128)S(1)}, f32[16,48,128]{2,1,0:T(8,128)S(1)}, f32[16,48,128]{2,1,0:T(8,128)S(1)}...) custom-call(f32[16,32,128]{2,1,0:T(8,128)S(1)} %get-tuple-element.36.w0_ref, ...), custom_call_target="tpu_custom_call" | custom-call | flops 6000000 | bytes 6000000 | tf_op jit(solution)/shard_map/pallas_call | solution.py:609
  13.8 0.7 %shard_map.143 = (f32[6,48,128]{2,1,0:T(8,128)S(1)}, f32[6,48,128]{2,1,0:T(8,128)S(1)}, f32[6,48,128]{2,1,0:T(8,128)S(1)}, f32[3,48,256]{2,1,0:T(8,128)S(1)}, f32[16,128]{1,0:T(8,128)S(1)}) custom-call(s32[512,128]{1,0:T(8,128)S(1)} %shard_map.140.after_ref.plan_ref, f32[16,48,128]{2,1,0:T(8,128)S(1)} %get-tuple-element.41.a_ref.inside_ref, ...), custom_call_target="tpu_custom_call" | custom-call | flops 2000000 | bytes 2000000 | tf_op jit(solution)/shard_map/pallas_call | solution.py:616
  14.5 0.6 %collective-permute-start.6 = (f32[16,128]{1,0:T(8,128)S(1)}, f32[16,128]{1,0:T(8,128)S(1)}, u32[]{:S(2)}, u32[]{:S(2)}) collective-permute-start(f32[16,128]{1,0:T(8,128)S(1)} %get-tuple-element.51.after_ref.a_ref), channel_id=1, source_target_pairs={{0,1},{1,0},{2,3},{3,2},{4,5},{5,4},{6,7},{7,6},{8,9},{9,8},{10,11... | collective-permute-start | bytes 24584 | tf_op jit(solution)/shard_map/ppermute | solution.py:633
  15.0 1.2 %shard_map.144.after_ref.refs_4_ = f32[160,128]{1,0:T(8,128)S(1)} custom-call(f32[16,128]{1,0:T(8,128)S(1)} %get-tuple-element.51.after_ref.a_ref, f32[16,48,128]{2,1,0:T(8,128)S(1)} %get-tuple-element.41.a_ref.inside_ref, f32[6,48,128]{2,1,0:T(8,128)S(1)} %get-tuple-element.52.edge_ref, f32[3,48,256]{2,1,0:T(8,128)S(1)} %get-tuple-element.53.slabs_ref, ...), custom_call_target="tpu_custom_call" | custom-call | flops 6000000 | bytes 6000000 | tf_op jit(solution)/shard_map/pallas_call | solution.py:624
  16.2 1.6 %collective-permute-start.7 = (f32[16,128]{1,0:T(8,128)S(1)}, f32[16,128]{1,0:T(8,128)S(1)}, u32[]{:S(2)}, u32[]{:S(2)}) collective-permute-start(f32[16,128]{1,0:T(8,128)S(1)} %shard_map.145.after_ref.a_ref), channel_id=1, source_target_pairs={{0,2},{2,0},{1,3},{3,1},{4,6},{6,4},{5,7},{7,5},{8,10},{10,8},{9,1... | collective-permute-start | bytes 24584 | tf_op jit(solution)/shard_map/ppermute | solution.py:633
  17.8 1.2 %shard_map.146.after_ref.refs_5_ = f32[160,128]{1,0:T(8,128)S(1)} custom-call(f32[16,128]{1,0:T(8,128)S(1)} %shard_map.145.after_ref.a_ref, f32[16,48,128]{2,1,0:T(8,128)S(1)} %get-tuple-element.43.b_ref.inside_ref, f32[6,48,128]{2,1,0:T(8,128)S(1)} %get-tuple-element.54.edge_ref.eb_ref, f32[3,48,256]{2,1,0:T(8,128)S(1)} %get-tuple-element.53.slabs_ref, ...), custom_call_target="tpu_custom_call" | custom-call | flops 6000000 | bytes 6000000 | tf_op jit(solution)/shard_map/pallas_call | solution.py:624
  19.0 1.0 %collective-permute-done.7.b_ref = f32[16,128]{1,0:T(8,128)S(1)} collective-permute-done((f32[16,128]{1,0:T(8,128)S(1)}, f32[16,128]{1,0:T(8,128)S(1)}, u32[]{:S(2)}, u32[]{:S(2)}) %collective-permute-start.7) | collective-permute-done | bytes 8224 | tf_op jit(solution)/shard_map/ppermute | solution.py:633
  20.0 0.9 %collective-permute-start.10 = (f32[16,128]{1,0:T(8,128)S(1)}, f32[16,128]{1,0:T(8,128)S(1)}, u32[]{:S(2)}, u32[]{:S(2)}) collective-permute-start(f32[16,128]{1,0:T(8,128)S(1)} %shard_map.147.after_ref.refs_0_), channel_id=1, source_target_pairs={{0,12},{4,8},{8,4},{12,0},{1,13},{5,9},{9,5},{13,1},{2,14},{6,10},... | collective-permute-start | bytes 24584 | tf_op jit(solution)/shard_map/ppermute | solution.py:644
  20.9 2.2 %collective-permute-start.9 = (f32[16,128]{1,0:T(8,128)S(1)}, f32[16,128]{1,0:T(8,128)S(1)}, u32[]{:S(2)}, u32[]{:S(2)}) collective-permute-start(f32[16,128]{1,0:T(8,128)S(1)} %shard_map.147.after_ref.refs_0_), channel_id=1, source_target_pairs={{0,8},{4,12},{8,0},{12,4},{1,9},{5,13},{9,1},{13,5},{2,10},{6,14},... | collective-permute-start | bytes 24584 | tf_op jit(solution)/shard_map/ppermute | solution.py:644
  23.1 1.3 %collective-permute-start.8 = (f32[16,128]{1,0:T(8,128)S(1)}, f32[16,128]{1,0:T(8,128)S(1)}, u32[]{:S(2)}, u32[]{:S(2)}) collective-permute-start(f32[16,128]{1,0:T(8,128)S(1)} %shard_map.147.after_ref.refs_0_), channel_id=1, source_target_pairs={{0,4},{4,0},{8,12},{12,8},{1,5},{5,1},{9,13},{13,9},{2,6},{6,2},{1... | collective-permute-start | bytes 24584 | tf_op jit(solution)/shard_map/ppermute | solution.py:644
  24.3 1.2 %shard_map.148.refs_6_ = f32[160,128]{1,0:T(8,128)S(1)} custom-call(f32[16,128]{1,0:T(8,128)S(1)} %shard_map.147.after_ref.refs_0_, f32[16,48,128]{2,1,0:T(8,128)S(1)} %get-tuple-element.44.c_ref.inside_ref, f32[6,48,128]{2,1,0:T(8,128)S(1)} %get-tuple-element.55.edge_ref.ec_ref, f32[3,48,256]{2,1,0:T(8,128)S(1)} %get-tuple-element.53.slabs_ref, ...), custom_call_target="tpu_custom_call" | custom-call | flops 6000000 | bytes 6000000 | tf_op jit(solution)/shard_map/pallas_call | solution.py:624
  25.6 1.1 %collective-permute-done.8.refs_1_ = f32[16,128]{1,0:T(8,128)S(1)} collective-permute-done((f32[16,128]{1,0:T(8,128)S(1)}, f32[16,128]{1,0:T(8,128)S(1)}, u32[]{:S(2)}, u32[]{:S(2)}) %collective-permute-start.8) | collective-permute-done | bytes 8224 | tf_op jit(solution)/shard_map/ppermute | solution.py:644
  27.0 1.0 %collective-permute-start.11 = (f32[64,128]{1,0:T(8,128)S(1)}, f32[64,128]{1,0:T(8,128)S(1)}, u32[]{:S(2)}, u32[]{:S(2)}) collective-permute-start(f32[64,128]{1,0:T(8,128)S(1)} %get-tuple-element.62), channel_id=1, source_target_pairs={{0,8},{1,9},{2,10},{3,11},{4,12},{5,13},{6,14},{7,15},{8,0},{9,1},... | collective-permute-start | bytes 98312 | tf_op jit(solution)/shard_map/ppermute | solution.py:544
  27.9 1.3 %collective-permute-start.12 = (f32[64,128]{1,0:T(8,128)S(1)}, f32[64,128]{1,0:T(8,128)S(1)}, u32[]{:S(2)}, u32[]{:S(2)}) collective-permute-start(f32[64,128]{1,0:T(8,128)S(1)} %get-tuple-element.63), channel_id=1, source_target_pairs={{0,4},{1,5},{2,6},{3,7},{4,0},{5,1},{6,2},{7,3},{8,12},{9,13},{10,... | collective-permute-start | bytes 98312 | tf_op jit(solution)/shard_map/ppermute | solution.py:544
  29.3 0.8 %shard_map.150 = f32[16,32,128]{2,1,0:T(8,128)} custom-call(f32[8,128]{1,0:T(8,128)S(1)} %get-tuple-element.56.coef_ref.after_ref, f32[16,48,128]{2,1,0:T(8,128)S(1)} %get-tuple-element.41.a_ref.inside_ref, f32[16,48,128]{2,1,0:T(8,128)S(1)} %get-tuple-element.43.b_ref.inside_ref, f32[16,48,128]{2,1,0:T(8,128)S(1)} %get-tuple-element.44.c_ref.inside_ref, ...), custom_call_target="tpu_custom_call" | custom-call | flops 2000000 | bytes 2000000 | tf_op jit(solution)/shard_map/pallas_call | solution.py:658
  30.8 1.9 %shard_map.151 = (f32[20,64,128]{2,1,0:T(8,128)S(1)}, f32[64,128]{1,0:T(8,128)S(1)}, f32[64,128]{1,0:T(8,128)S(1)}, f32[2,20,128]{2,1,0:T(8,128)S(1)}) custom-call(f32[20]{0:T(128)S(1)} %copy-done.5, f32[20]{0:T(128)S(1)} %copy-done.6, f32[20]{0:T(128)S(1)} %copy-done.7, f32[20]{0:T(128)S(1)} %copy-done.8, f32[20]{0:T(128)S(1)} %copy-done.9, ...), custom_call_target="tpu_custom_call" | custom-call | flops 6000000 | bytes 6000000 | tf_op jit(solution)/shard_map/pallas_call | solution.py:659
  32.8 0.9 %shard_map.152 = (f32[64,128]{1,0:T(8,128)}, f32[20,64,128]{2,1,0:T(8,128)}) custom-call(f32[2,20,128]{2,1,0:T(8,128)S(1)} %get-tuple-element.57.coef_ref, f32[64,128]{1,0:T(8,128)S(1)} %bitcast.12, f32[64,128]{1,0:T(8,128)S(1)} %bitcast.11, f32[64,128]{1,0:T(8,128)S(1)} %get-tuple-element.58.sum_ref, f32[64,128]{1,0:T(8,128)S(1)} %get-tuple-element.59.factor_ref, ...), custom_call_target="tpu_custom_call" | custom-call | flops 2000000 | bytes 2000000 | tf_op jit(solution)/shard_map/pallas_call | solution.py:672
  (38 shorter events, 1.2 us)
Async XLA Ops:
  2.0 1.4 %collective-permute-start = (f32[2,32,128]{2,1,0:T(8,128)S(1)}, f32[2,32,128]{2,1,0:T(8,128)S(1)}, u32[]{:S(2)}, u32[]{:S(2)}) collective-permute-start(f32[2,32,128]{2,1,0:T(8,128)S(1)} %get-tuple-element.38.own_ref), channel_id=1, source_target_pairs={{0,1},{1,0},{2,3},{3,2},{4,5},{5,4},{6,7},{7,6},{8,9},{9,8},{10,11... | collective-permute-start | bytes 98312 | tf_op jit(solution)/shard_map/ppermute | solution.py:588
  3.4 7.7 %copy-start = (s32[16,32,128]{2,1,0:T(8,128)S(1)}, s32[16,32,128]{2,1,0:T(8,128)}, u32[]{:S(2)}) copy-start(s32[16,32,128]{2,1,0:T(8,128)} %label_hbm.1) | copy-start | bytes 786436
  3.5 10.3 %collective-permute-start.2 = (f32[6,32,128]{2,1,0:T(8,128)S(1)}, f32[6,32,128]{2,1,0:T(8,128)S(1)}, u32[]{:S(2)}, u32[]{:S(2)}) collective-permute-start(f32[6,32,128]{2,1,0:T(8,128)S(1)} %get-tuple-element.47), channel_id=1, source_target_pairs={{0,4},{1,5},{2,6},{3,7},{4,0},{5,1},{6,2},{7,3},{8,12},{9,13},{10,... | collective-permute-start | bytes 294920 | tf_op jit(solution)/shard_map/ppermute | solution.py:544
  6.4 7.3 %collective-permute-start.3 = (f32[6,32,128]{2,1,0:T(8,128)S(1)}, f32[6,32,128]{2,1,0:T(8,128)S(1)}, u32[]{:S(2)}, u32[]{:S(2)}) collective-permute-start(f32[6,32,128]{2,1,0:T(8,128)S(1)} %get-tuple-element.48), channel_id=1, source_target_pairs={{0,1},{1,0},{2,3},{3,2},{4,8},{5,9},{6,10},{7,11},{8,4},{9,5},{10,... | collective-permute-start | bytes 294920 | tf_op jit(solution)/shard_map/ppermute | solution.py:544
  6.5 6.3 %collective-permute-start.1 = (f32[17,8,128]{2,1,0:T(8,128)S(1)}, f32[17,8,128]{2,1,0:T(8,128)S(1)}, u32[]{:S(2)}, u32[]{:S(2)}) collective-permute-start(f32[17,8,128]{2,1,0:T(8,128)S(1)} %get-tuple-element.40), channel_id=1, source_target_pairs={{0,2},{1,3},{2,0},{3,1},{4,6},{5,7},{6,4},{7,5},{8,10},{9,11},{10,... | collective-permute-start | bytes 208904 | tf_op jit(solution)/shard_map/ppermute | solution.py:544
  7.9 5.8 %collective-permute-start.4 = (f32[4,8,128]{2,1,0:T(8,128)S(1)}, f32[4,8,128]{2,1,0:T(8,128)S(1)}, u32[]{:S(2)}, u32[]{:S(2)}) collective-permute-start(f32[4,8,128]{2,1,0:T(8,128)S(1)} %get-tuple-element.49), channel_id=1, source_target_pairs={{0,6},{1,7},{2,4},{3,5},{4,2},{5,3},{6,0},{7,1},{8,14},{9,15},{10,... | collective-permute-start | bytes 49160 | tf_op jit(solution)/shard_map/ppermute | solution.py:544
  11.1 2.7 %collective-permute-start.5 = (f32[4,8,128]{2,1,0:T(8,128)S(1)}, f32[4,8,128]{2,1,0:T(8,128)S(1)}, u32[]{:S(2)}, u32[]{:S(2)}) collective-permute-start(f32[4,8,128]{2,1,0:T(8,128)S(1)} %get-tuple-element.50), channel_id=1, source_target_pairs={{0,1},{1,0},{2,3},{3,2},{4,10},{5,11},{6,8},{7,9},{8,6},{9,7},{10,... | collective-permute-start | bytes 49160 | tf_op jit(solution)/shard_map/ppermute | solution.py:544
  14.5 1.8 %collective-permute-start.6 = (f32[16,128]{1,0:T(8,128)S(1)}, f32[16,128]{1,0:T(8,128)S(1)}, u32[]{:S(2)}, u32[]{:S(2)}) collective-permute-start(f32[16,128]{1,0:T(8,128)S(1)} %get-tuple-element.51.after_ref.a_ref), channel_id=1, source_target_pairs={{0,1},{1,0},{2,3},{3,2},{4,5},{5,4},{6,7},{7,6},{8,9},{9,8},{10,11... | collective-permute-start | bytes 24584 | tf_op jit(solution)/shard_map/ppermute | solution.py:633
  16.2 3.7 %collective-permute-start.7 = (f32[16,128]{1,0:T(8,128)S(1)}, f32[16,128]{1,0:T(8,128)S(1)}, u32[]{:S(2)}, u32[]{:S(2)}) collective-permute-start(f32[16,128]{1,0:T(8,128)S(1)} %shard_map.145.after_ref.a_ref), channel_id=1, source_target_pairs={{0,2},{2,0},{1,3},{3,1},{4,6},{6,4},{5,7},{7,5},{8,10},{10,8},{9,1... | collective-permute-start | bytes 24584 | tf_op jit(solution)/shard_map/ppermute | solution.py:633
  20.0 5.6 %collective-permute-start.10 = (f32[16,128]{1,0:T(8,128)S(1)}, f32[16,128]{1,0:T(8,128)S(1)}, u32[]{:S(2)}, u32[]{:S(2)}) collective-permute-start(f32[16,128]{1,0:T(8,128)S(1)} %shard_map.147.after_ref.refs_0_), channel_id=1, source_target_pairs={{0,12},{4,8},{8,4},{12,0},{1,13},{5,9},{9,5},{13,1},{2,14},{6,10},... | collective-permute-start | bytes 24584 | tf_op jit(solution)/shard_map/ppermute | solution.py:644
  20.9 4.7 %collective-permute-start.9 = (f32[16,128]{1,0:T(8,128)S(1)}, f32[16,128]{1,0:T(8,128)S(1)}, u32[]{:S(2)}, u32[]{:S(2)}) collective-permute-start(f32[16,128]{1,0:T(8,128)S(1)} %shard_map.147.after_ref.refs_0_), channel_id=1, source_target_pairs={{0,8},{4,12},{8,0},{12,4},{1,9},{5,13},{9,1},{13,5},{2,10},{6,14},... | collective-permute-start | bytes 24584 | tf_op jit(solution)/shard_map/ppermute | solution.py:644
  23.1 3.7 %collective-permute-start.8 = (f32[16,128]{1,0:T(8,128)S(1)}, f32[16,128]{1,0:T(8,128)S(1)}, u32[]{:S(2)}, u32[]{:S(2)}) collective-permute-start(f32[16,128]{1,0:T(8,128)S(1)} %shard_map.147.after_ref.refs_0_), channel_id=1, source_target_pairs={{0,4},{4,0},{8,12},{12,8},{1,5},{5,1},{9,13},{13,9},{2,6},{6,2},{1... | collective-permute-start | bytes 24584 | tf_op jit(solution)/shard_map/ppermute | solution.py:644
  27.0 5.8 %collective-permute-start.11 = (f32[64,128]{1,0:T(8,128)S(1)}, f32[64,128]{1,0:T(8,128)S(1)}, u32[]{:S(2)}, u32[]{:S(2)}) collective-permute-start(f32[64,128]{1,0:T(8,128)S(1)} %get-tuple-element.62), channel_id=1, source_target_pairs={{0,8},{1,9},{2,10},{3,11},{4,12},{5,13},{6,14},{7,15},{8,0},{9,1},... | collective-permute-start | bytes 98312 | tf_op jit(solution)/shard_map/ppermute | solution.py:544
  27.9 4.8 %collective-permute-start.12 = (f32[64,128]{1,0:T(8,128)S(1)}, f32[64,128]{1,0:T(8,128)S(1)}, u32[]{:S(2)}, u32[]{:S(2)}) collective-permute-start(f32[64,128]{1,0:T(8,128)S(1)} %get-tuple-element.63), channel_id=1, source_target_pairs={{0,4},{1,5},{2,6},{3,7},{4,0},{5,1},{6,2},{7,3},{8,12},{9,13},{10,... | collective-permute-start | bytes 98312 | tf_op jit(solution)/shard_map/ppermute | solution.py:544
  29.2 3.5 %collective-permute-start.13 = (f32[64,128]{1,0:T(8,128)S(1)}, f32[64,128]{1,0:T(8,128)S(1)}, u32[]{:S(2)}, u32[]{:S(2)}) collective-permute-start(f32[64,128]{1,0:T(8,128)S(1)} %get-tuple-element.64), channel_id=1, source_target_pairs={{0,1},{1,0},{2,3},{3,2},{4,8},{5,9},{6,10},{7,11},{8,4},{9,5},{10,... | collective-permute-start | bytes 98312 | tf_op jit(solution)/shard_map/ppermute | solution.py:544
  29.2 1.2 %copy-start.1 = (f32[20,1,8192]{2,1,0:T(1,128)S(1)}, f32[20,1,8192]{2,1,0:T(1,128)}, u32[]{:S(2)}) copy-start(f32[20,1,8192]{2,1,0:T(1,128)} %param.17) | copy-start | bytes 1966084
  29.2 1.4 %copy-start.2 = (f32[20,1,8192]{2,1,0:T(1,128)S(1)}, f32[20,1,8192]{2,1,0:T(1,128)}, u32[]{:S(2)}) copy-start(f32[20,1,8192]{2,1,0:T(1,128)} %param.19) | copy-start | bytes 1966084
  29.2 1.4 %copy-start.3 = (f32[1,8192]{1,0:T(1,128)S(1)}, f32[1,8192]{1,0:T(1,128)}, u32[]{:S(2)}) copy-start(f32[1,8192]{1,0:T(1,128)} %param.16) | copy-start | bytes 98308
  29.2 1.4 %copy-start.8 = (f32[20]{0:T(128)S(1)}, f32[20]{0:T(128)}, u32[]{:S(2)}) copy-start(f32[20]{0:T(128)} %cond_ref.1) | copy-start | bytes 244
  29.2 1.4 %copy-start.9 = (f32[20]{0:T(128)S(1)}, f32[20]{0:T(128)}, u32[]{:S(2)}) copy-start(f32[20]{0:T(128)} %rev_ref.1) | copy-start | bytes 244
  30.0 0.8 %copy-start.5 = (f32[20]{0:T(128)S(1)}, f32[20]{0:T(128)}, u32[]{:S(2)}) copy-start(f32[20]{0:T(128)} %half_ref.1) | copy-start | bytes 244
  30.0 0.8 %copy-start.6 = (f32[20]{0:T(128)S(1)}, f32[20]{0:T(128)}, u32[]{:S(2)}) copy-start(f32[20]{0:T(128)} %slope_ref.1) | copy-start | bytes 244
  30.0 0.8 %copy-start.7 = (f32[20]{0:T(128)S(1)}, f32[20]{0:T(128)}, u32[]{:S(2)}) copy-start(f32[20]{0:T(128)} %tau_ref.1) | copy-start | bytes 244
  30.8 2.0 %copy-start.4 = (f32[1,8192]{1,0:T(1,128)S(1)}, f32[1,8192]{1,0:T(1,128)}, u32[]{:S(2)}) copy-start(f32[1,8192]{1,0:T(1,128)} %param.18) | copy-start | bytes 98308

commit v11 on v10

--- a/solution.py
+++ b/solution.py
@@ -11,6 +11,7 @@
 LANES = 128
 SUB = 8
 PACK = 8
+COUNT_LANE = 4 * PACK
 F32 = jnp.float32
 
 VMEM = pl.BlockSpec(memory_space=pltpu.VMEM)
@@ -117,7 +118,7 @@
     return w_tile, i_tile
 
 
-def faces_kernel(n_y, w0_ref, inv_ref, own_ref, got_ref, slab_ref, *refs):
+def faces_kernel(n_y, w0_ref, inv_ref, own_ref, got_ref, stat_ref, slab_ref, *refs):
     y_refs, x_refs, edge_refs = refs[:n_y], refs[n_y : n_y + 2], refs[n_y + 2 :]
     nx, ny, nz = w0_ref.shape
     sub = subs_of((SUB, nz))
@@ -131,6 +132,7 @@
             w_face = jnp.where(up, w_rows[ny - SUB :], w_rows[:SUB])
             i_face = jnp.where(up, i_rows[ny - SUB :], i_rows[:SUB])
             face_ref[x] = jnp.where(keep_w, w_face, pltpu.roll(i_face, 4, 0))
+    cells = jnp.sum(stat_ref[1, 0:1], axis=1, keepdims=True)
     slab_w = slab_ref[0]
     half = pltpu.roll(slab_ref[1], nz // 2, 1)
     up_slab = jnp.where(lane >= nz - 3 * PACK, slab_w, half)
@@ -142,7 +144,7 @@
             face_ref[k] = w0_ref[first + k]
         for k in range(2):
             face_ref[3 + k] = inv_ref[jnp.where(up, nx - 2, 0) + k]
-        face_ref[5] = jnp.where(up, up_slab, down_slab)
+        face_ref[5] = jnp.where(lane == COUNT_LANE, cells, jnp.where(up, up_slab, down_slab))
         for y_step, y_ref in enumerate(y_refs):
             edge_ref = edge_refs[step * n_y + y_step]
             for k in range(3):
@@ -255,10 +257,10 @@
 
 
 def outer_kernel(
-    n_y, after_ref, a_ref, i_ref, b_ref, c_ref, slab_ref, sum_ref, stat_ref, *refs
+    n_y, column_total, after_ref, a_ref, i_ref, b_ref, c_ref, slab_ref, sum_ref, stat_ref, *refs
 ):
     x_refs, corner_refs = refs[:2], refs[2 : 2 + 2 * n_y]
-    ea_ref, eb_ref, ec_ref, slabs_ref, total_ref, ei_ref, si_ref = refs[2 + 2 * n_y :]
+    ea_ref, eb_ref, ec_ref, slabs_ref, total_ref, where_ref, ei_ref, si_ref = refs[2 + 2 * n_y :]
     nx, ny, nz = a_ref.shape[0], a_ref.shape[1] - 2 * SUB, a_ref.shape[2]
     ring = ny + SUB
     gz = lax.axis_index("gz")
@@ -297,6 +299,7 @@
         slab_parts.append((
             near(own, lane, 3), near(tiles[3][0], lane_tile, 3),
             near(pltpu.roll(own, nz // 2, 1), lane, 2), near(tiles[3][1], lane_tile, 2),
+            own[0:1, COUNT_LANE : COUNT_LANE + 1],
         ))
 
     low, high = slab_parts
@@ -339,9 +342,16 @@
     for k in range(5):
         total_ref[k + 1 : k + 2] = jnp.sum(sums[k] + sum_ref[k], axis=0, keepdims=True)
     total_ref[6:8] = jnp.zeros((2, nz), F32)
-    here = (lax.axis_index("gx") * lax.axis_size("gy") + lax.axis_index("gy")) * lax.axis_size("gz") + gz
-    count = jnp.sum(stat_ref[1], axis=1, keepdims=True)
-    total_ref[8:16] = jnp.where(lanes_of((SUB, nz)) == here, count, 0.0)
+    gx, n_x = lax.axis_index("gx"), lax.axis_size("gx")
+    count = jnp.sum(stat_ref[1, 0:1], axis=1, keepdims=True)
+    below, above = [part[4] for part in slab_parts]
+    begin = jnp.where(
+        gx == 0, 0.0,
+        jnp.where(gx == 1, below, jnp.where(gx == n_x - 1, column_total - count, column_total - count - above)),
+    )
+    where_ref[0:1] = jnp.broadcast_to(begin, (1, nz))
+    where_ref[1:2] = jnp.broadcast_to(count, (1, nz))
+    where_ref[2:8] = jnp.zeros((6, nz), F32)
 
 
 def shift_left(v, amount, lane):
@@ -434,50 +444,28 @@
     out_ref[...] = a_ref[...] + b_ref[...]
 
 
-def place_kernel(n_sums, *refs):
-    sum_refs, refs = refs[:n_sums], refs[n_sums:]
-    list_refs, refs = refs[:3], refs[3:]
-    coef_ref, *out_refs, buf_ref = refs
-    total = sum_refs[0][...]
-    for ref in sum_refs[1:]:
-        total = total + ref[...]
-    sums = jnp.sum(total[0:8], axis=1, keepdims=True)
-    t = [jnp.broadcast_to(sums[k : k + 1], (1, LANES)) for k in range(6)]
-    coefs = galerkin(t)
-    for k in range(3):
-        coef_ref[k : k + 1] = coefs[k]
-    value = coefs[0] * list_refs[0][...] + coefs[1] * list_refs[1][...] + coefs[2] * list_refs[2][...]
-    slot_rows = value.shape[0]
-    n_y, n_z = lax.axis_size("gy"), lax.axis_size("gz")
-    counts = total[8:16]
-    dev = lanes_of((SUB, LANES))
-    mine = lax.rem(dev, n_y * n_z) == lax.axis_index("gy") * n_z + lax.axis_index("gz")
+def place_kernel(where_ref, total_ref, *refs):
+    list_refs, out_refs, buf_ref = refs[:3], refs[3:-1], refs[-1]
+    slot_rows = list_refs[0].shape[0]
+    size = (out_refs[0].shape[0] - SUB) // 3
     gx = lax.axis_index("gx")
-    first = subs_of((SUB, LANES)) == 0
-    offset = jnp.sum(jnp.where(first & mine & (dev < gx * n_y * n_z), counts, 0.0)).astype(jnp.int32)
-    count = jnp.sum(jnp.where(first & mine & (dev // (n_y * n_z) == gx), counts, 0.0)).astype(jnp.int32)
+    offset = jnp.max(where_ref[0:1]).astype(jnp.int32)
+    count = jnp.max(where_ref[1:2]).astype(jnp.int32)
     shape = (slot_rows, LANES)
-    slots = jnp.where(subs_of(shape) * LANES + lanes_of(shape) < count, value, 0.0)
-    slots = jnp.concatenate([slots, jnp.zeros((SUB, LANES), F32)], axis=0)
+    listed = subs_of(shape) * LANES + lanes_of(shape) < count
     inner = lax.rem(offset, LANES)
-    turned = pltpu.roll(slots, inner, 1)
-    above = pltpu.roll(turned, 1, 0)
-    moved = jnp.where(lanes_of((slot_rows + SUB, LANES)) >= inner, turned, above)
+    kept = lanes_of((slot_rows + SUB, LANES)) >= inner
     buf_ref[...] = jnp.zeros_like(buf_ref)
-    buf_ref[pl.ds(offset // LANES, slot_rows + SUB), :] = moved
-    for k, out_ref in enumerate(out_refs):
-        size = out_ref.shape[0]
-        out_ref[...] = buf_ref[pl.ds(pl.multiple_of((gx ^ k) * size, SUB), size), :]
-
-
-def potential_kernel(coef_ref, a_ref, b_ref, c_ref, eb_ref, ec_ref, x_ref):
-    nx, ny, nz = x_ref.shape
-    own = slice(SUB, SUB + ny)
-    c0, c1, c2 = [coef_ref[k : k + 1] for k in range(3)]
-    for x in range(nx):
-        w1 = b_ref[x, own] if 1 <= x < nx - 1 else eb_ref[2 if x == 0 else 3, own]
-        w2 = c_ref[x, own] if 2 <= x < nx - 2 else ec_ref[x + 1 if x < 2 else x - (nx - 2) + 3, own]
-        x_ref[x] = c0 * a_ref[x, own] + c1 * w1 + c2 * w2
+    for k, list_ref in enumerate(list_refs):
+        slots = jnp.where(listed, list_ref[...], 0.0)
+        slots = jnp.concatenate([slots, jnp.zeros((SUB, LANES), F32)], axis=0)
+        turned = pltpu.roll(slots, inner, 1)
+        buf_ref[k, pl.ds(offset // LANES, slot_rows + SUB), :] = jnp.where(kept, turned, pltpu.roll(turned, 1, 0))
+    for block, out_ref in enumerate(out_refs):
+        begin = pl.multiple_of((gx ^ block) * size, SUB)
+        for k in range(3):
+            out_ref[k * size : k * size + size] = buf_ref[k, pl.ds(begin, size), :]
+        out_ref[3 * size :] = total_ref[...]
 
 
 def membrane_kernel(
@@ -512,16 +500,33 @@
     factor_ref[...] = 1.0 - TIME_STEP * current
 
 
-def finish_kernel(coef_ref, vcot_ref, v_ref, sum_ref, factor_ref, base_ref, *refs):
-    *landed_refs, volt_ref, gate_ref = refs
-    landed = landed_refs[0][...]
-    for ref in landed_refs[1:]:
-        landed = landed + ref[...]
+def finish_kernel(
+    n_blocks, coef_ref, vcot_ref, v_ref, sum_ref, factor_ref, base_ref, a_ref, b_ref, c_ref, eb_ref, ec_ref, *refs
+):
+    block_refs, (x_ref, volt_ref, gate_ref) = refs[:n_blocks], refs[n_blocks:]
+    size = (block_refs[0].shape[0] - SUB) // 3
+    total = block_refs[0][3 * size :]
+    for ref in block_refs[1:]:
+        total = total + ref[3 * size :]
+    sums = jnp.sum(total, axis=1, keepdims=True)
+    c0, c1, c2 = galerkin([jnp.broadcast_to(sums[k : k + 1], (1, LANES)) for k in range(6)])
+    landed = jnp.zeros((size, LANES), F32)
+    for k, c in enumerate((c0, c1, c2)):
+        part = block_refs[0][k * size : k * size + size]
+        for ref in block_refs[1:]:
+            part = part + ref[k * size : k * size + size]
+        landed = landed + c * part
     cot = vcot_ref[...] + landed
     v = v_ref[...]
     volt_ref[...] = cot * factor_ref[...] + sum_ref[...]
     for g in range(base_ref.shape[0]):
         gate_ref[g] = base_ref[g] - (coef_ref[0, g : g + 1] * cot) * (v - coef_ref[1, g : g + 1])
+    nx, ny, nz = x_ref.shape
+    own = slice(SUB, SUB + ny)
+    for x in range(nx):
+        w1 = b_ref[x, own] if 1 <= x < nx - 1 else eb_ref[2 if x == 0 else 3, own]
+        w2 = c_ref[x, own] if 2 <= x < nx - 2 else ec_ref[x + 1 if x < 2 else x - (nx - 2) + 3, own]
+        x_ref[x] = c0 * a_ref[x, own] + c1 * w1 + c2 * w2
 
 
 def partners(axis, step):
@@ -542,22 +547,6 @@
                 to = (x, y, z ^ 1) if alone else (to_x, to_y, z)
                 pairs.append(((x * n_y + y) * n_z + z, (to[0] * n_y + to[1]) * n_z + to[2]))
     return lax.ppermute(value, ("gx", "gy", "gz"), pairs)
-
-
-def block_partners(count, k, slots, block):
-    def apart(tile, owner):
-        return owner * block >= (tile + 1) * slots or (owner + 1) * block <= count * block - (count - tile) * slots
-
-    return [i if apart(i, i ^ k) and apart(i ^ k, i) else i ^ k for i in range(count)]
-
-
-def reduce_over(value, axis):
-    count = lax.axis_size(axis)
-    step = 1
-    while step < count:
-        value = value + lax.ppermute(value, axis, [(i, i ^ step) for i in range(count)])
-        step *= 2
-    return value
 
 
 def local(
@@ -595,7 +584,7 @@
         (shape_of(2, ny, nz),) + (shape_of(nx + 1, SUB, nz),) * n_y + (shape_of(6, ny, nz),) * 2
         + (shape_of(4, SUB, nz),) * (2 * n_y)
     )
-    slab, *faces = call(functools.partial(faces_kernel, n_y), shapes, 4)(w0, inv, packed, got)
+    slab, *faces = call(functools.partial(faces_kernel, n_y), shapes, 5)(w0, inv, packed, got, stat)
     along_y, along_x, across = faces[:n_y], faces[n_y : n_y + 2], faces[n_y + 2 :]
     y_to = [partners("gy", step) for step in range(n_y)]
     x_to = [partners("gx", step) for step in range(2)]
@@ -613,9 +602,9 @@
         scratch=[pltpu.VMEM((4, tall, nz), F32)],
         cost=6_000_000,
     )(w0, inv, slab, *along_y)
-    ends0, ends1, ends2, slabs, sums = call(
-        functools.partial(outer_kernel, n_y),
-        (edges,) * 3 + (shape_of(3, tall, 2 * nz), shape_of(16, nz)),
+    ends0, ends1, ends2, slabs, sums, where = call(
+        functools.partial(outer_kernel, n_y, float(n_gx * voltage.shape[1])),
+        (edges,) * 3 + (shape_of(3, tall, 2 * nz), shape_of(SUB, nz), shape_of(SUB, nz)),
         10 + 2 * n_y,
         scratch=[pltpu.VMEM((4, tall, nz), F32), pltpu.VMEM((1, tall, 2 * nz), F32)],
     )(plan, in0, in_inv, in1, in2, own_slab, in_sums, stat, *along_x, *across)
@@ -631,31 +620,28 @@
 
     def add(value, axis, step, after):
         got = lax.ppermute(value, axis, [(i, i ^ step) for i in range(lax.axis_size(axis))])
-        return call(add_kernel, shape_of(16, nz), 3)(value, got, after)
+        return call(add_kernel, shape_of(SUB, nz), 3)(value, got, after)
 
     list0 = couple(0, sums, in0, ends0)
     sums = add(sums, "gz", 1, list0)
     list1 = couple(1, sums, in1, ends1)
-    sums = add(sums, "gy", 1, list1)
-    for step in [2**k for k in range(1, n_gy.bit_length() - 1)]:
-        sums = add(sums, "gy", step, list1)
-    list2 = couple(2, sums, in2, ends2)
-    if n_gx <= 4:
-        sums = [sums] + [lax.ppermute(sums, "gx", [(i, i ^ k) for i in range(n_gx)]) for k in range(1, n_gx)]
-    else:
-        sums = [reduce_over(sums, "gx")]
-
-    coefs, *blocks = call(
-        functools.partial(place_kernel, len(sums)),
-        (shape_of(SUB, LANES),) + (shape_of(block_rows, LANES),) * n_gx,
-        len(sums) + 3,
-        scratch=[pltpu.VMEM((n_gx * block_rows + slot_rows + SUB, LANES), F32)],
-    )(*sums, list0, list1, list2)
-    landed = blocks[:1] + [
-        swap(blocks[k], x_to=block_partners(n_gx, k, slot_rows, block_rows)) for k in [2, 1] + list(range(3, n_gx))
+    list2 = couple(2, list1, in2, ends2)
+    for step in [2**k for k in range(n_gy.bit_length() - 1)]:
+        sums = add(sums, "gy", step, list2)
+    if n_gx > 4:
+        counts = lax.all_gather(jnp.sum(stat[1, 0]), "gx")
+        begin = jnp.sum(jnp.where(jnp.arange(n_gx) < lax.axis_index("gx"), counts, 0.0))
+        where = where.at[0].set(begin)
+    blocks = call(
+        place_kernel,
+        (shape_of(3 * block_rows + SUB, LANES),) * n_gx,
+        5,
+        scratch=[pltpu.VMEM((3, n_gx * block_rows + slot_rows + SUB, LANES), F32)],
+    )(where, sums, list0, list1, list2)
+    got = [
+        lax.ppermute(blocks[k], "gx", [(i, i ^ k) for i in range(n_gx)]) for k in [2, 1] + list(range(3, n_gx))
     ]
 
-    solution = call(potential_kernel, block, 6)(coefs, in0, in1, in2, ends1, ends2)
     base, total_change, factor, state_coefs = call(
         membrane_kernel,
         (
@@ -667,13 +653,16 @@
         cost=6_000_000,
     )(
         half_voltage, gate_slope, tau_base, conductance, reversal,
-        coefs, cells(voltage), states(gates), states(gates_cot),
-    )
-    volt_grad, gate_grad = call(
-        finish_kernel,
-        (shape_of(block_rows, LANES), shape_of(n_states, block_rows, LANES)),
-        6 + n_gx,
-    )(state_coefs, cells(voltage_cot), cells(voltage), total_change, factor, base, *landed)
+        blocks[0], cells(voltage), states(gates), states(gates_cot),
+    )
+    solution, volt_grad, gate_grad = call(
+        functools.partial(finish_kernel, n_gx),
+        (block, shape_of(block_rows, LANES), shape_of(n_states, block_rows, LANES)),
+        11 + n_gx,
+    )(
+        state_coefs, cells(voltage_cot), cells(voltage), total_change, factor, base,
+        in0, in1, in2, ends1, ends2, blocks[0], *got,
+    )
     return solution, volt_grad.reshape(voltage.shape), gate_grad.reshape(gates.shape)
 
 

time: 33.9 us -> 32.7 us (0.965)
  starting transfers between devices: 16.9 us -> 14.7 us
  waiting for transfers between devices: 3 us -> 4.52 us
  Pallas kernels: 12.2 us -> 11.8 us
    ppermute x3, waiting for transfers between devices: 1.15 us -> 3.64 us  [local(): lax.ppermute(blocks[k], 'gx', [(i, i ^ k) for i in range(n_gx)])]
    ppermute x8 -> x5, starting transfers between devices: 9.83 us -> 7.6 us  [swap(): return lax.ppermute(value, ('gx', 'gy', 'gz'), pairs)]
    ppermute x2, waiting for transfers between devices: 0.97 us -> 0.01 us  [add(): lax.ppermute(value, axis, [(i, i ^ step) for i in range(lax.axis_size(axi...]
    pallas_call x7 -> x6, Pallas kernels: 2.7 us -> 2.22 us  [the longest x1 1.17 us: local(): call(functools.partial(finish_kernel, n_gx), (block, shape_of(block_rows,...]
  transfers between devices with their start and end apart: 14 -> 11, of which waited for: 3 -> 2; matrix products, arithmetic and copies ran while one was open for 0% -> 0% of each run, Pallas kernels for 26% -> 25%
where the time goes in v11:
time: 32.7 us; the launch traced here: 32.5 us
  starting transfers between devices  14.7 us (45%)
  Pallas kernels  11.8 us (36%)
  waiting for transfers between devices  4.52 us (14%)
  between operations  0.85 us (3%)
  local copies, waits for them, and re-layouts  0.68 us (2%)
    ppermute x5, starting transfers between devices, swap(): return lax.ppermute(value, ('gx', 'gy', 'gz'), pairs)  7.6 us
    ppermute x3, starting transfers between devices, local(): lax.ppermute(blocks[k], 'gx', [(i, i ^ k) for i in range(n_gx)])  4.45 us
    ppermute x3, waiting for transfers between devices, local(): lax.ppermute(blocks[k], 'gx', [(i, i ^ k) for i in range(n_gx)])  3.64 us
    pallas_call x3, Pallas kernels, couple(): call(functools.partial(couple_kernel, stage, slot_rows), shape_of(slot_ro...  3.56 us
    ppermute x2, starting transfers between devices, add(): lax.ppermute(value, axis, [(i, i ^ step) for i in range(lax.axis_size(axi...  2.13 us
    pallas_call x1, Pallas kernels, local(): call(membrane_kernel, (shape_of(n_states, block_rows, LANES), shape_of(bl...  1.93 us
    pallas_call x1, Pallas kernels, local(): call(plan_kernel, jax.ShapeDtypeStruct((rows, LANES), jnp.int32), 2, cost...  1.72 us
    pallas_call x1, Pallas kernels, local(): call(start_kernel, (block, block, shape_of(2, ny, nz), shape_of(2, SUB, n...  1.4 us
  transfers between devices with their start and end apart: 11, of which 2 were waited for; matrix products, arithmetic and copies ran while one was open for 0% of the time, Pallas kernels for 25%

profile of v11, /device:TPU:0, one launch (start us, length us, event | category | flops | bytes accessed | tf_op | source)
XLA Modules:
  0.0 32.5 jit_solution(13092691583879933912)
XLA Ops:
  0.6 1.4 %shard_map.139 = (f32[16,32,128]{2,1,0:T(8,128)S(1)}, f32[16,32,128]{2,1,0:T(8,128)S(1)}, f32[2,32,128]{2,1,0:T(8,128)S(1)}, f32[2,8,128]{2,1,0:T(8,128)S(1)}) custom-call(f32[16,32,128]{2,1,0:T(8,128)} %right_hbm.1, f32[16,32,128]{2,1,0:T(8,128)} %damping_hbm.1, s32[16,32,128]{2,1,0:T(8,128)} %label_hbm.1), custom_call_target="tpu_custom_call" | custom-call | flops 2000000 | bytes 2000000 | tf_op jit(solution)/shard_map/pallas_call | solution.py:568
  2.0 0.5 %collective-permute-start = (f32[2,32,128]{2,1,0:T(8,128)S(1)}, f32[2,32,128]{2,1,0:T(8,128)S(1)}, u32[]{:S(2)}, u32[]{:S(2)}) collective-permute-start(f32[2,32,128]{2,1,0:T(8,128)S(1)} %get-tuple-element.39.own_ref), channel_id=1, source_target_pairs={{0,1},{1,0},{2,3},{3,2},{4,5},{5,4},{6,7},{7,6},{8,9},{9,8},{10,11... | collective-permute-start | bytes 98312 | tf_op jit(solution)/shard_map/ppermute | solution.py:577
  2.6 0.9 %collective-permute-done.got_ref = f32[2,32,128]{2,1,0:T(8,128)S(1)} collective-permute-done((f32[2,32,128]{2,1,0:T(8,128)S(1)}, f32[2,32,128]{2,1,0:T(8,128)S(1)}, u32[]{:S(2)}, u32[]{:S(2)}) %collective-permute-start) | collective-permute-done | bytes 32800 | tf_op jit(solution)/shard_map/ppermute | solution.py:577
  3.4 0.1 shard_map.141
  3.5 3.0 %collective-permute-start.2 = (f32[6,32,128]{2,1,0:T(8,128)S(1)}, f32[6,32,128]{2,1,0:T(8,128)S(1)}, u32[]{:S(2)}, u32[]{:S(2)}) collective-permute-start(f32[6,32,128]{2,1,0:T(8,128)S(1)} %get-tuple-element.48), channel_id=1, source_target_pairs={{0,4},{1,5},{2,6},{3,7},{4,0},{5,1},{6,2},{7,3},{8,12},{9,13},{10,... | collective-permute-start | bytes 294920 | tf_op jit(solution)/shard_map/ppermute | solution.py:549
  6.5 1.5 %collective-permute-start.1 = (f32[17,8,128]{2,1,0:T(8,128)S(1)}, f32[17,8,128]{2,1,0:T(8,128)S(1)}, u32[]{:S(2)}, u32[]{:S(2)}) collective-permute-start(f32[17,8,128]{2,1,0:T(8,128)S(1)} %get-tuple-element.41), channel_id=1, source_target_pairs={{0,2},{1,3},{2,0},{3,1},{4,6},{5,7},{6,4},{7,5},{8,10},{9,11},{10,... | collective-permute-start | bytes 208904 | tf_op jit(solution)/shard_map/ppermute | solution.py:549
  8.0 3.1 %collective-permute-start.4 = (f32[4,8,128]{2,1,0:T(8,128)S(1)}, f32[4,8,128]{2,1,0:T(8,128)S(1)}, u32[]{:S(2)}, u32[]{:S(2)}) collective-permute-start(f32[4,8,128]{2,1,0:T(8,128)S(1)} %get-tuple-element.50), channel_id=1, source_target_pairs={{0,6},{1,7},{2,4},{3,5},{4,2},{5,3},{6,0},{7,1},{8,14},{9,15},{10,... | collective-permute-start | bytes 49160 | tf_op jit(solution)/shard_map/ppermute | solution.py:549
  11.1 1.7 %shard_map.140.after_ref.plan_ref = s32[512,128]{1,0:T(8,128)S(1)} custom-call(f32[2,8,128]{2,1,0:T(8,128)S(1)} %get-tuple-element.36.after_ref.stat_ref, s32[512,128]{1,0:T(8,128)S(1)} %bitcast.7), custom_call_target="tpu_custom_call" | custom-call | flops 6000000 | bytes 6000000 | tf_op jit(solution)/shard_map/pallas_call | solution.py:578
  12.8 0.9 %shard_map.142 = (f32[16,48,128]{2,1,0:T(8,128)S(1)}, f32[16,48,128]{2,1,0:T(8,128)S(1)}, f32[16,48,128]{2,1,0:T(8,128)S(1)}, f32[16,48,128]{2,1,0:T(8,128)S(1)}...) custom-call(f32[16,32,128]{2,1,0:T(8,128)S(1)} %get-tuple-element.37.w0_ref, ...), custom_call_target="tpu_custom_call" | custom-call | flops 6000000 | bytes 6000000 | tf_op jit(solution)/shard_map/pallas_call | solution.py:598
  13.8 0.7 %shard_map.143 = (f32[6,48,128]{2,1,0:T(8,128)S(1)}, f32[6,48,128]{2,1,0:T(8,128)S(1)}, f32[6,48,128]{2,1,0:T(8,128)S(1)}, f32[3,48,256]{2,1,0:T(8,128)S(1)}, f3...) custom-call(s32[512,128]{1,0:T(8,128)S(1)} %shard_map.140.after_ref.plan_ref, ...), custom_call_target="tpu_custom_call" | custom-call | flops 2000000 | bytes 2000000 | tf_op jit(solution)/shard_map/pallas_call | solution.py:605
  14.5 0.6 %collective-permute-start.6 = (f32[8,128]{1,0:T(8,128)S(1)}, f32[8,128]{1,0:T(8,128)S(1)}, u32[]{:S(2)}, u32[]{:S(2)}) collective-permute-start(f32[8,128]{1,0:T(8,128)S(1)} %get-tuple-element.53.after_ref.a_ref), channel_id=1, source_target_pairs={{0,1},{1,0},{2,3},{3,2},{4,5},{5,4},{6,7},{7,6},{8,9},{9,8},{10,11... | collective-permute-start | bytes 12296 | tf_op jit(solution)/shard_map/ppermute | solution.py:622
  15.1 1.2 %shard_map.144.after_ref.refs_0_ = f32[160,128]{1,0:T(8,128)S(1)} custom-call(f32[8,128]{1,0:T(8,128)S(1)} %get-tuple-element.53.after_ref.a_ref, f32[16,48,128]{2,1,0:T(8,128)S(1)} %get-tuple-element.42.a_ref.inside_ref, f32[6,48,128]{2,1,0:T(8,128)S(1)} %get-tuple-element.54.edge_ref, f32[3,48,256]{2,1,0:T(8,128)S(1)} %get-tuple-element.55.slabs_ref, ...), custom_call_target="tpu_custom_call" | custom-call | flops 6000000 | bytes 6000000 | tf_op jit(solution)/shard_map/pallas_call | solution.py:613
  16.3 1.6 %collective-permute-start.7 = (f32[8,128]{1,0:T(8,128)S(1)}, f32[8,128]{1,0:T(8,128)S(1)}, u32[]{:S(2)}, u32[]{:S(2)}) collective-permute-start(f32[8,128]{1,0:T(8,128)S(1)} %shard_map.145.after_ref.a_ref), channel_id=1, source_target_pairs={{0,2},{2,0},{1,3},{3,1},{4,6},{6,4},{5,7},{7,5},{8,10},{10,8},{9,1... | collective-permute-start | bytes 12296 | tf_op jit(solution)/shard_map/ppermute | solution.py:622
  17.8 1.2 %shard_map.146.after_ref.refs_1_ = f32[160,128]{1,0:T(8,128)S(1)} custom-call(f32[8,128]{1,0:T(8,128)S(1)} %shard_map.145.after_ref.a_ref, f32[16,48,128]{2,1,0:T(8,128)S(1)} %get-tuple-element.44.b_ref.inside_ref, f32[6,48,128]{2,1,0:T(8,128)S(1)} %get-tuple-element.56.edge_ref.eb_ref, f32[3,48,256]{2,1,0:T(8,128)S(1)} %get-tuple-element.55.slabs_ref, ...), custom_call_target="tpu_custom_call" | custom-call | flops 6000000 | bytes 6000000 | tf_op jit(solution)/shard_map/pallas_call | solution.py:613
  19.1 1.2 %shard_map.147.after_ref.refs_2_ = f32[160,128]{1,0:T(8,128)S(1)} custom-call(f32[160,128]{1,0:T(8,128)S(1)} %shard_map.146.after_ref.refs_1_, f32[16,48,128]{2,1,0:T(8,128)S(1)} %get-tuple-element.45.c_ref.inside_ref, f32[6,48,128]{2,1,0:T(8,128)S(1)} %get-tuple-element.57.edge_ref.ec_ref, f32[3,48,256]{2,1,0:T(8,128)S(1)} %get-tuple-element.55.slabs_ref, ...), custom_call_target="tpu_custom_call" | custom-call | flops 6000000 | bytes 6000000 | tf_op jit(solution)/shard_map/pallas_call | solution.py:613
  20.3 0.3 shard_map.149
  20.6 1.4 %collective-permute-start.8 = (f32[200,128]{1,0:T(8,128)S(1)}, f32[200,128]{1,0:T(8,128)S(1)}, u32[]{:S(2)}, u32[]{:S(2)}) collective-permute-start(f32[200,128]{1,0:T(8,128)S(1)} %get-tuple-element.63), channel_id=1, source_target_pairs={{0,8},{4,12},{8,0},{12,4},{1,9},{5,13},{9,1},{13,5},{2,10},{6,14},... | collective-permute-start | bytes 307208 | tf_op jit(solution)/shard_map/ppermute | solution.py:642
  22.0 0.1 collective-permute-start.9
  22.1 2.9 %collective-permute-start.10 = (f32[200,128]{1,0:T(8,128)S(1)}, f32[200,128]{1,0:T(8,128)S(1)}, u32[]{:S(2)}, u32[]{:S(2)}) collective-permute-start(f32[200,128]{1,0:T(8,128)S(1)} %get-tuple-element.65), channel_id=1, source_target_pairs={{0,12},{4,8},{8,4},{12,0},{1,13},{5,9},{9,5},{13,1},{2,14},{6,10},... | collective-permute-start | bytes 307208 | tf_op jit(solution)/shard_map/ppermute | solution.py:642
  25.1 0.6 %copy-done.5 = f32[20]{0:T(128)S(1)} copy-done((f32[20]{0:T(128)S(1)}, f32[20]{0:T(128)}, u32[]{:S(2)}) %copy-start.5) | copy-done | bytes 104
  25.7 0.0 copy-done.6
  25.8 1.9 %shard_map.150 = (f32[20,64,128]{2,1,0:T(8,128)S(1)}, f32[64,128]{1,0:T(8,128)S(1)}, f32[64,128]{1,0:T(8,128)S(1)}, f32[2,20,128]{2,1,0:T(8,128)S(1)}) custom-call(f32[20]{0:T(128)S(1)} %copy-done.5, f32[20]{0:T(128)S(1)} %copy-done.6, f32[20]{0:T(128)S(1)} %copy-done.7, f32[20]{0:T(128)S(1)} %copy-done.8, f32[20]{0:T(128)S(1)} %copy-done.9, ...), custom_call_target="tpu_custom_call" | custom-call | flops 6000000 | bytes 6000000 | tf_op jit(solution)/shard_map/pallas_call | solution.py:645
  27.7 3.6 %collective-permute-done.8.refs_1_ = f32[200,128]{1,0:T(8,128)S(1)} collective-permute-done((f32[200,128]{1,0:T(8,128)S(1)}, f32[200,128]{1,0:T(8,128)S(1)}, u32[]{:S(2)}, u32[]{:S(2)}) %collective-permute-start.8) | collective-permute-done | bytes 102432 | tf_op jit(solution)/shard_map/ppermute | solution.py:642
  31.3 1.2 %shard_map.151 = (f32[16,32,128]{2,1,0:T(8,128)}, f32[64,128]{1,0:T(8,128)}, f32[20,64,128]{2,1,0:T(8,128)}) custom-call(f32[2,20,128]{2,1,0:T(8,128)S(1)} %get-tuple-element.59.coef_ref, f32[64,128]{1,0:T(8,128)S(1)} %bitcast.12, f32[64,128]{1,0:T(8,128)S(1)} %bitcast.11, f32[64,128]{1,0:T(8,128)S(1)} %get-tuple-element.60.sum_ref, ...), custom_call_target="tpu_custom_call" | custom-call | flops 2000000 | bytes 2000000 | tf_op jit(solution)/shard_map/pallas_call | solution.py:658
  (31 shorter events, 0.1 us)
Async XLA Ops:
  2.0 1.4 %collective-permute-start = (f32[2,32,128]{2,1,0:T(8,128)S(1)}, f32[2,32,128]{2,1,0:T(8,128)S(1)}, u32[]{:S(2)}, u32[]{:S(2)}) collective-permute-start(f32[2,32,128]{2,1,0:T(8,128)S(1)} %get-tuple-element.39.own_ref), channel_id=1, source_target_pairs={{0,1},{1,0},{2,3},{3,2},{4,5},{5,4},{6,7},{7,6},{8,9},{9,8},{10,11... | collective-permute-start | bytes 98312 | tf_op jit(solution)/shard_map/ppermute | solution.py:577
  3.4 7.7 %copy-start = (s32[16,32,128]{2,1,0:T(8,128)S(1)}, s32[16,32,128]{2,1,0:T(8,128)}, u32[]{:S(2)}) copy-start(s32[16,32,128]{2,1,0:T(8,128)} %label_hbm.1) | copy-start | bytes 786436
  3.5 10.3 %collective-permute-start.2 = (f32[6,32,128]{2,1,0:T(8,128)S(1)}, f32[6,32,128]{2,1,0:T(8,128)S(1)}, u32[]{:S(2)}, u32[]{:S(2)}) collective-permute-start(f32[6,32,128]{2,1,0:T(8,128)S(1)} %get-tuple-element.48), channel_id=1, source_target_pairs={{0,4},{1,5},{2,6},{3,7},{4,0},{5,1},{6,2},{7,3},{8,12},{9,13},{10,... | collective-permute-start | bytes 294920 | tf_op jit(solution)/shard_map/ppermute | solution.py:549
  6.5 7.3 %collective-permute-start.3 = (f32[6,32,128]{2,1,0:T(8,128)S(1)}, f32[6,32,128]{2,1,0:T(8,128)S(1)}, u32[]{:S(2)}, u32[]{:S(2)}) collective-permute-start(f32[6,32,128]{2,1,0:T(8,128)S(1)} %get-tuple-element.49), channel_id=1, source_target_pairs={{0,1},{1,0},{2,3},{3,2},{4,8},{5,9},{6,10},{7,11},{8,4},{9,5},{10,... | collective-permute-start | bytes 294920 | tf_op jit(solution)/shard_map/ppermute | solution.py:549
  6.5 6.3 %collective-permute-start.1 = (f32[17,8,128]{2,1,0:T(8,128)S(1)}, f32[17,8,128]{2,1,0:T(8,128)S(1)}, u32[]{:S(2)}, u32[]{:S(2)}) collective-permute-start(f32[17,8,128]{2,1,0:T(8,128)S(1)} %get-tuple-element.41), channel_id=1, source_target_pairs={{0,2},{1,3},{2,0},{3,1},{4,6},{5,7},{6,4},{7,5},{8,10},{9,11},{10,... | collective-permute-start | bytes 208904 | tf_op jit(solution)/shard_map/ppermute | solution.py:549
  8.0 5.8 %collective-permute-start.4 = (f32[4,8,128]{2,1,0:T(8,128)S(1)}, f32[4,8,128]{2,1,0:T(8,128)S(1)}, u32[]{:S(2)}, u32[]{:S(2)}) collective-permute-start(f32[4,8,128]{2,1,0:T(8,128)S(1)} %get-tuple-element.50), channel_id=1, source_target_pairs={{0,6},{1,7},{2,4},{3,5},{4,2},{5,3},{6,0},{7,1},{8,14},{9,15},{10,... | collective-permute-start | bytes 49160 | tf_op jit(solution)/shard_map/ppermute | solution.py:549
  11.1 2.7 %collective-permute-start.5 = (f32[4,8,128]{2,1,0:T(8,128)S(1)}, f32[4,8,128]{2,1,0:T(8,128)S(1)}, u32[]{:S(2)}, u32[]{:S(2)}) collective-permute-start(f32[4,8,128]{2,1,0:T(8,128)S(1)} %get-tuple-element.51), channel_id=1, source_target_pairs={{0,1},{1,0},{2,3},{3,2},{4,10},{5,11},{6,8},{7,9},{8,6},{9,7},{10,... | collective-permute-start | bytes 49160 | tf_op jit(solution)/shard_map/ppermute | solution.py:549
  14.5 1.8 %collective-permute-start.6 = (f32[8,128]{1,0:T(8,128)S(1)}, f32[8,128]{1,0:T(8,128)S(1)}, u32[]{:S(2)}, u32[]{:S(2)}) collective-permute-start(f32[8,128]{1,0:T(8,128)S(1)} %get-tuple-element.53.after_ref.a_ref), channel_id=1, source_target_pairs={{0,1},{1,0},{2,3},{3,2},{4,5},{5,4},{6,7},{7,6},{8,9},{9,8},{10,11... | collective-permute-start | bytes 12296 | tf_op jit(solution)/shard_map/ppermute | solution.py:622
  16.3 4.0 %collective-permute-start.7 = (f32[8,128]{1,0:T(8,128)S(1)}, f32[8,128]{1,0:T(8,128)S(1)}, u32[]{:S(2)}, u32[]{:S(2)}) collective-permute-start(f32[8,128]{1,0:T(8,128)S(1)} %shard_map.145.after_ref.a_ref), channel_id=1, source_target_pairs={{0,2},{2,0},{1,3},{3,1},{4,6},{6,4},{5,7},{7,5},{8,10},{10,8},{9,1... | collective-permute-start | bytes 12296 | tf_op jit(solution)/shard_map/ppermute | solution.py:622
  19.0 6.0 %copy-start.1 = (f32[20,1,8192]{2,1,0:T(1,128)S(1)}, f32[20,1,8192]{2,1,0:T(1,128)}, u32[]{:S(2)}) copy-start(f32[20,1,8192]{2,1,0:T(1,128)} %param.17) | copy-start | bytes 1966084
  19.1 6.0 %copy-start.2 = (f32[20,1,8192]{2,1,0:T(1,128)S(1)}, f32[20,1,8192]{2,1,0:T(1,128)}, u32[]{:S(2)}) copy-start(f32[20,1,8192]{2,1,0:T(1,128)} %param.19) | copy-start | bytes 1966084
  20.3 4.8 %copy-start.3 = (f32[1,8192]{1,0:T(1,128)S(1)}, f32[1,8192]{1,0:T(1,128)}, u32[]{:S(2)}) copy-start(f32[1,8192]{1,0:T(1,128)} %param.16) | copy-start | bytes 98308
  20.3 4.8 %copy-start.8 = (f32[20]{0:T(128)S(1)}, f32[20]{0:T(128)}, u32[]{:S(2)}) copy-start(f32[20]{0:T(128)} %cond_ref.1) | copy-start | bytes 244
  20.3 4.8 %copy-start.9 = (f32[20]{0:T(128)S(1)}, f32[20]{0:T(128)}, u32[]{:S(2)}) copy-start(f32[20]{0:T(128)} %rev_ref.1) | copy-start | bytes 244
  20.6 10.7 %collective-permute-start.8 = (f32[200,128]{1,0:T(8,128)S(1)}, f32[200,128]{1,0:T(8,128)S(1)}, u32[]{:S(2)}, u32[]{:S(2)}) collective-permute-start(f32[200,128]{1,0:T(8,128)S(1)} %get-tuple-element.63), channel_id=1, source_target_pairs={{0,8},{4,12},{8,0},{12,4},{1,9},{5,13},{9,1},{13,5},{2,10},{6,14},... | collective-permute-start | bytes 307208 | tf_op jit(solution)/shard_map/ppermute | solution.py:642
  22.0 9.3 %collective-permute-start.9 = (f32[200,128]{1,0:T(8,128)S(1)}, f32[200,128]{1,0:T(8,128)S(1)}, u32[]{:S(2)}, u32[]{:S(2)}) collective-permute-start(f32[200,128]{1,0:T(8,128)S(1)} %get-tuple-element.64), channel_id=1, source_target_pairs={{0,4},{4,0},{8,12},{12,8},{1,5},{5,1},{9,13},{13,9},{2,6},{6,2},{1... | collective-permute-start | bytes 307208 | tf_op jit(solution)/shard_map/ppermute | solution.py:642
  22.1 9.2 %collective-permute-start.10 = (f32[200,128]{1,0:T(8,128)S(1)}, f32[200,128]{1,0:T(8,128)S(1)}, u32[]{:S(2)}, u32[]{:S(2)}) collective-permute-start(f32[200,128]{1,0:T(8,128)S(1)} %get-tuple-element.65), channel_id=1, source_target_pairs={{0,12},{4,8},{8,4},{12,0},{1,13},{5,9},{9,5},{13,1},{2,14},{6,10},... | collective-permute-start | bytes 307208 | tf_op jit(solution)/shard_map/ppermute | solution.py:642
  25.1 0.7 %copy-start.5 = (f32[20]{0:T(128)S(1)}, f32[20]{0:T(128)}, u32[]{:S(2)}) copy-start(f32[20]{0:T(128)} %half_ref.1) | copy-start | bytes 244
  25.1 0.7 %copy-start.6 = (f32[20]{0:T(128)S(1)}, f32[20]{0:T(128)}, u32[]{:S(2)}) copy-start(f32[20]{0:T(128)} %slope_ref.1) | copy-start | bytes 244
  25.1 0.7 %copy-start.7 = (f32[20]{0:T(128)S(1)}, f32[20]{0:T(128)}, u32[]{:S(2)}) copy-start(f32[20]{0:T(128)} %tau_ref.1) | copy-start | bytes 244
  25.8 5.6 %copy-start.4 = (f32[1,8192]{1,0:T(1,128)S(1)}, f32[1,8192]{1,0:T(1,128)}, u32[]{:S(2)}) copy-start(f32[1,8192]{1,0:T(1,128)} %param.18) | copy-start | bytes 98308

commit v12 on v11

--- a/solution.py
+++ b/solution.py
@@ -501,19 +501,32 @@
 
 
 def finish_kernel(
-    n_blocks, coef_ref, vcot_ref, v_ref, sum_ref, factor_ref, base_ref, a_ref, b_ref, c_ref, eb_ref, ec_ref, *refs
+    alone, coef_ref, vcot_ref, v_ref, sum_ref, factor_ref, base_ref, a_ref, b_ref, c_ref, eb_ref, ec_ref, *refs
 ):
-    block_refs, (x_ref, volt_ref, gate_ref) = refs[:n_blocks], refs[n_blocks:]
-    size = (block_refs[0].shape[0] - SUB) // 3
-    total = block_refs[0][3 * size :]
-    for ref in block_refs[1:]:
-        total = total + ref[3 * size :]
+    n_small, n_large = len(alone[0]), len(alone[1])
+    own_ref, small_refs, large_refs = refs[0], refs[1 : 1 + n_small], refs[1 + n_small : 1 + n_small + n_large]
+    x_ref, volt_ref, gate_ref = refs[1 + n_small + n_large :]
+    size = (own_ref.shape[0] - SUB) // 3
+    gx = lax.axis_index("gx")
+
+    def is_one(flags):
+        found = gx < 0
+        for place, flag in enumerate(flags):
+            if flag:
+                found = found | (gx == place)
+        return found
+
+    total = own_ref[3 * size :]
+    for flags, ref in zip(alone[0], small_refs):
+        total = total + jnp.where(is_one(flags), ref[...], 0.0)
+    for flags, ref in zip(alone[1], large_refs):
+        total = total + jnp.where(is_one(flags), 0.0, ref[3 * size :])
     sums = jnp.sum(total, axis=1, keepdims=True)
     c0, c1, c2 = galerkin([jnp.broadcast_to(sums[k : k + 1], (1, LANES)) for k in range(6)])
     landed = jnp.zeros((size, LANES), F32)
     for k, c in enumerate((c0, c1, c2)):
-        part = block_refs[0][k * size : k * size + size]
-        for ref in block_refs[1:]:
+        part = own_ref[k * size : k * size + size]
+        for ref in large_refs:
             part = part + ref[k * size : k * size + size]
         landed = landed + c * part
     cot = vcot_ref[...] + landed
@@ -547,6 +560,13 @@
                 to = (x, y, z ^ 1) if alone else (to_x, to_y, z)
                 pairs.append(((x * n_y + y) * n_z + z, (to[0] * n_y + to[1]) * n_z + to[2]))
     return lax.ppermute(value, ("gx", "gy", "gz"), pairs)
+
+
+def never_meet(count, k, slots, block):
+    def apart(tile, owner):
+        return owner * block >= (tile + 1) * slots or (owner + 1) * block <= count * block - (count - tile) * slots
+
+    return [apart(i, i ^ k) and apart(i ^ k, i) for i in range(count)]
 
 
 def local(
@@ -638,9 +658,15 @@
         5,
         scratch=[pltpu.VMEM((3, n_gx * block_rows + slot_rows + SUB, LANES), F32)],
     )(where, sums, list0, list1, list2)
-    got = [
-        lax.ppermute(blocks[k], "gx", [(i, i ^ k) for i in range(n_gx)]) for k in [2, 1] + list(range(3, n_gx))
-    ]
+    apart = {k: never_meet(n_gx, k, slot_rows, block_rows) for k in range(1, n_gx)}
+    small, meets = [], []
+    for k in range(1, n_gx):
+        if any(apart[k]):
+            small.append(swap(sums, x_to=[i ^ k if apart[k][i] else i for i in range(n_gx)]))
+        meets.append(not all(apart[k]))
+    order = [k for k in [2, 3, 1] + list(range(4, n_gx)) if k < n_gx and meets[k - 1]]
+    large = [swap(blocks[k], x_to=[i if apart[k][i] else i ^ k for i in range(n_gx)]) for k in order]
+    alone = [[apart[k] for k in range(1, n_gx) if any(apart[k])], [apart[k] for k in order]]
 
     base, total_change, factor, state_coefs = call(
         membrane_kernel,
@@ -656,12 +682,12 @@
         blocks[0], cells(voltage), states(gates), states(gates_cot),
     )
     solution, volt_grad, gate_grad = call(
-        functools.partial(finish_kernel, n_gx),
+        functools.partial(finish_kernel, alone),
         (block, shape_of(block_rows, LANES), shape_of(n_states, block_rows, LANES)),
-        11 + n_gx,
+        12 + len(small) + len(large),
     )(
         state_coefs, cells(voltage_cot), cells(voltage), total_change, factor, base,
-        in0, in1, in2, ends1, ends2, blocks[0], *got,
+        in0, in1, in2, ends1, ends2, blocks[0], *small, *large,
     )
     return solution, volt_grad.reshape(voltage.shape), gate_grad.reshape(gates.shape)
 

time: 32.7 us -> 31 us (0.948)
  waiting for transfers between devices: 4.52 us -> 2.87 us
    ppermute x5 -> x9, starting transfers between devices: 7.6 us -> 12.1 us  [swap(): return lax.ppermute(value, ('gx', 'gy', 'gz'), pairs)]
    ppermute x3 -> x0, starting transfers between devices: 4.45 us -> none  [local(): lax.ppermute(blocks[k], 'gx', [(i, i ^ k) for i in range(n_gx)])]
    ppermute x3 -> x0, waiting for transfers between devices: 3.64 us -> none  [local(): lax.ppermute(blocks[k], 'gx', [(i, i ^ k) for i in range(n_gx)])]
    ppermute x5 -> x9, waiting for transfers between devices: 0.01 us -> 2.01 us  [swap(): return lax.ppermute(value, ('gx', 'gy', 'gz'), pairs)]
  transfers between devices with their start and end apart: 11 -> 12, of which waited for: 2 -> 2; matrix products, arithmetic and copies ran while one was open for 0% -> 0% of each run, Pallas kernels for 25% -> 26%
where the time goes in v12:
time: 31 us; the launch traced here: 30.9 us
  starting transfers between devices  14.7 us (47%)
  Pallas kernels  11.8 us (38%)
  waiting for transfers between devices  2.87 us (9%)
  between operations  0.85 us (3%)
  local copies, waits for them, and re-layouts  0.68 us (2%)
    ppermute x9, starting transfers between devices, swap(): return lax.ppermute(value, ('gx', 'gy', 'gz'), pairs)  12.1 us
    pallas_call x3, Pallas kernels, couple(): call(functools.partial(couple_kernel, stage, slot_rows), shape_of(slot_ro...  3.56 us
    ppermute x2, starting transfers between devices, add(): lax.ppermute(value, axis, [(i, i ^ step) for i in range(lax.axis_size(axi...  2.13 us
    ppermute x9, waiting for transfers between devices, swap(): return lax.ppermute(value, ('gx', 'gy', 'gz'), pairs)  2.01 us
    pallas_call x1, Pallas kernels, local(): call(membrane_kernel, (shape_of(n_states, block_rows, LANES), shape_of(bl...  1.93 us
    pallas_call x1, Pallas kernels, local(): call(plan_kernel, jax.ShapeDtypeStruct((rows, LANES), jnp.int32), 2, cost...  1.72 us
    pallas_call x1, Pallas kernels, local(): call(start_kernel, (block, block, shape_of(2, ny, nz), shape_of(2, SUB, n...  1.4 us
    pallas_call x1, Pallas kernels, local(): call(functools.partial(finish_kernel, alone), (block, shape_of(block_rows...  1.18 us
  transfers between devices with their start and end apart: 12, of which 2 were waited for; matrix products, arithmetic and copies ran while one was open for 0% of the time, Pallas kernels for 26%

profile of v12, /device:TPU:0, one launch (start us, length us, event | category | flops | bytes accessed | tf_op | source)
XLA Modules:
  0.0 30.9 jit_solution(2834455816773694801)
XLA Ops:
  0.6 1.4 %shard_map.139 = (f32[16,32,128]{2,1,0:T(8,128)S(1)}, f32[16,32,128]{2,1,0:T(8,128)S(1)}, f32[2,32,128]{2,1,0:T(8,128)S(1)}, f32[2,8,128]{2,1,0:T(8,128)S(1)}) custom-call(f32[16,32,128]{2,1,0:T(8,128)} %right_hbm.1, f32[16,32,128]{2,1,0:T(8,128)} %damping_hbm.1, s32[16,32,128]{2,1,0:T(8,128)} %label_hbm.1), custom_call_target="tpu_custom_call" | custom-call | flops 2000000 | bytes 2000000 | tf_op jit(solution)/shard_map/pallas_call | solution.py:588
  2.0 0.5 %collective-permute-start = (f32[2,32,128]{2,1,0:T(8,128)S(1)}, f32[2,32,128]{2,1,0:T(8,128)S(1)}, u32[]{:S(2)}, u32[]{:S(2)}) collective-permute-start(f32[2,32,128]{2,1,0:T(8,128)S(1)} %get-tuple-element.39.own_ref), channel_id=1, source_target_pairs={{0,1},{1,0},{2,3},{3,2},{4,5},{5,4},{6,7},{7,6},{8,9},{9,8},{10,11... | collective-permute-start | bytes 98312 | tf_op jit(solution)/shard_map/ppermute | solution.py:597
  2.6 0.9 %collective-permute-done.got_ref = f32[2,32,128]{2,1,0:T(8,128)S(1)} collective-permute-done((f32[2,32,128]{2,1,0:T(8,128)S(1)}, f32[2,32,128]{2,1,0:T(8,128)S(1)}, u32[]{:S(2)}, u32[]{:S(2)}) %collective-permute-start) | collective-permute-done | bytes 32800 | tf_op jit(solution)/shard_map/ppermute | solution.py:597
  3.4 0.1 shard_map.141
  3.5 3.0 %collective-permute-start.2 = (f32[6,32,128]{2,1,0:T(8,128)S(1)}, f32[6,32,128]{2,1,0:T(8,128)S(1)}, u32[]{:S(2)}, u32[]{:S(2)}) collective-permute-start(f32[6,32,128]{2,1,0:T(8,128)S(1)} %get-tuple-element.48), channel_id=1, source_target_pairs={{0,4},{1,5},{2,6},{3,7},{4,0},{5,1},{6,2},{7,3},{8,12},{9,13},{10,... | collective-permute-start | bytes 294920 | tf_op jit(solution)/shard_map/ppermute | solution.py:562
  6.5 1.5 %collective-permute-start.1 = (f32[17,8,128]{2,1,0:T(8,128)S(1)}, f32[17,8,128]{2,1,0:T(8,128)S(1)}, u32[]{:S(2)}, u32[]{:S(2)}) collective-permute-start(f32[17,8,128]{2,1,0:T(8,128)S(1)} %get-tuple-element.41), channel_id=1, source_target_pairs={{0,2},{1,3},{2,0},{3,1},{4,6},{5,7},{6,4},{7,5},{8,10},{9,11},{10,... | collective-permute-start | bytes 208904 | tf_op jit(solution)/shard_map/ppermute | solution.py:562
  8.0 3.1 %collective-permute-start.4 = (f32[4,8,128]{2,1,0:T(8,128)S(1)}, f32[4,8,128]{2,1,0:T(8,128)S(1)}, u32[]{:S(2)}, u32[]{:S(2)}) collective-permute-start(f32[4,8,128]{2,1,0:T(8,128)S(1)} %get-tuple-element.50), channel_id=1, source_target_pairs={{0,6},{1,7},{2,4},{3,5},{4,2},{5,3},{6,0},{7,1},{8,14},{9,15},{10,... | collective-permute-start | bytes 49160 | tf_op jit(solution)/shard_map/ppermute | solution.py:562
  11.1 1.7 %shard_map.140.after_ref.plan_ref = s32[512,128]{1,0:T(8,128)S(1)} custom-call(f32[2,8,128]{2,1,0:T(8,128)S(1)} %get-tuple-element.36.after_ref.stat_ref, s32[512,128]{1,0:T(8,128)S(1)} %bitcast.7), custom_call_target="tpu_custom_call" | custom-call | flops 6000000 | bytes 6000000 | tf_op jit(solution)/shard_map/pallas_call | solution.py:598
  12.8 0.9 %shard_map.142 = (f32[16,48,128]{2,1,0:T(8,128)S(1)}, f32[16,48,128]{2,1,0:T(8,128)S(1)}, f32[16,48,128]{2,1,0:T(8,128)S(1)}, f32[16,48,128]{2,1,0:T(8,128)S(1)}...) custom-call(f32[16,32,128]{2,1,0:T(8,128)S(1)} %get-tuple-element.37.w0_ref, ...), custom_call_target="tpu_custom_call" | custom-call | flops 6000000 | bytes 6000000 | tf_op jit(solution)/shard_map/pallas_call | solution.py:618
  13.8 0.7 %shard_map.143 = (f32[6,48,128]{2,1,0:T(8,128)S(1)}, f32[6,48,128]{2,1,0:T(8,128)S(1)}, f32[6,48,128]{2,1,0:T(8,128)S(1)}, f32[3,48,256]{2,1,0:T(8,128)S(1)}, f3...) custom-call(s32[512,128]{1,0:T(8,128)S(1)} %shard_map.140.after_ref.plan_ref, ...), custom_call_target="tpu_custom_call" | custom-call | flops 2000000 | bytes 2000000 | tf_op jit(solution)/shard_map/pallas_call | solution.py:625
  14.5 0.6 %collective-permute-start.6 = (f32[8,128]{1,0:T(8,128)S(1)}, f32[8,128]{1,0:T(8,128)S(1)}, u32[]{:S(2)}, u32[]{:S(2)}) collective-permute-start(f32[8,128]{1,0:T(8,128)S(1)} %get-tuple-element.53.after_ref.a_ref), channel_id=1, source_target_pairs={{0,1},{1,0},{2,3},{3,2},{4,5},{5,4},{6,7},{7,6},{8,9},{9,8},{10,11... | collective-permute-start | bytes 12296 | tf_op jit(solution)/shard_map/ppermute | solution.py:642
  15.1 1.2 %shard_map.144.after_ref.refs_0_ = f32[160,128]{1,0:T(8,128)S(1)} custom-call(f32[8,128]{1,0:T(8,128)S(1)} %get-tuple-element.53.after_ref.a_ref, f32[16,48,128]{2,1,0:T(8,128)S(1)} %get-tuple-element.42.a_ref.inside_ref, f32[6,48,128]{2,1,0:T(8,128)S(1)} %get-tuple-element.54.edge_ref, f32[3,48,256]{2,1,0:T(8,128)S(1)} %get-tuple-element.55.slabs_ref, ...), custom_call_target="tpu_custom_call" | custom-call | flops 6000000 | bytes 6000000 | tf_op jit(solution)/shard_map/pallas_call | solution.py:633
  16.3 1.6 %collective-permute-start.7 = (f32[8,128]{1,0:T(8,128)S(1)}, f32[8,128]{1,0:T(8,128)S(1)}, u32[]{:S(2)}, u32[]{:S(2)}) collective-permute-start(f32[8,128]{1,0:T(8,128)S(1)} %shard_map.145.after_ref.a_ref), channel_id=1, source_target_pairs={{0,2},{2,0},{1,3},{3,1},{4,6},{6,4},{5,7},{7,5},{8,10},{10,8},{9,1... | collective-permute-start | bytes 12296 | tf_op jit(solution)/shard_map/ppermute | solution.py:642
  17.8 1.2 %shard_map.146.after_ref.refs_1_ = f32[160,128]{1,0:T(8,128)S(1)} custom-call(f32[8,128]{1,0:T(8,128)S(1)} %shard_map.145.after_ref.a_ref, f32[16,48,128]{2,1,0:T(8,128)S(1)} %get-tuple-element.44.b_ref.inside_ref, f32[6,48,128]{2,1,0:T(8,128)S(1)} %get-tuple-element.56.edge_ref.eb_ref, f32[3,48,256]{2,1,0:T(8,128)S(1)} %get-tuple-element.55.slabs_ref, ...), custom_call_target="tpu_custom_call" | custom-call | flops 6000000 | bytes 6000000 | tf_op jit(solution)/shard_map/pallas_call | solution.py:633
  19.1 1.2 %shard_map.147.after_ref.refs_2_ = f32[160,128]{1,0:T(8,128)S(1)} custom-call(f32[160,128]{1,0:T(8,128)S(1)} %shard_map.146.after_ref.refs_1_, f32[16,48,128]{2,1,0:T(8,128)S(1)} %get-tuple-element.45.c_ref.inside_ref, f32[6,48,128]{2,1,0:T(8,128)S(1)} %get-tuple-element.57.edge_ref.ec_ref, f32[3,48,256]{2,1,0:T(8,128)S(1)} %get-tuple-element.55.slabs_ref, ...), custom_call_target="tpu_custom_call" | custom-call | flops 6000000 | bytes 6000000 | tf_op jit(solution)/shard_map/pallas_call | solution.py:633
  20.3 0.3 shard_map.149
  20.6 1.4 %collective-permute-start.9 = (f32[200,128]{1,0:T(8,128)S(1)}, f32[200,128]{1,0:T(8,128)S(1)}, u32[]{:S(2)}, u32[]{:S(2)}) collective-permute-start(f32[200,128]{1,0:T(8,128)S(1)} %get-tuple-element.63), channel_id=1, source_target_pairs={{0,8},{1,9},{2,10},{3,11},{4,12},{5,13},{6,14},{7,15},{8,0},{9,1},... | collective-permute-start | bytes 307208 | tf_op jit(solution)/shard_map/ppermute | solution.py:562
  22.0 2.2 %collective-permute-start.11 = (f32[200,128]{1,0:T(8,128)S(1)}, f32[200,128]{1,0:T(8,128)S(1)}, u32[]{:S(2)}, u32[]{:S(2)}) collective-permute-start(f32[200,128]{1,0:T(8,128)S(1)} %get-tuple-element.65), channel_id=1, source_target_pairs={{0,4},{1,5},{2,6},{3,7},{4,0},{5,1},{6,2},{7,3},{8,12},{9,13},{10,... | collective-permute-start | bytes 307208 | tf_op jit(solution)/shard_map/ppermute | solution.py:562
  24.2 0.9 %collective-permute-start.8 = (f32[8,128]{1,0:T(8,128)S(1)}, f32[8,128]{1,0:T(8,128)S(1)}, u32[]{:S(2)}, u32[]{:S(2)}) collective-permute-start(f32[8,128]{1,0:T(8,128)S(1)} %shard_map.148.total_ref), channel_id=1, source_target_pairs={{0,12},{1,13},{2,14},{3,15},{4,5},{5,4},{6,7},{7,6},{8,9},{9,8},{1... | collective-permute-start | bytes 12296 | tf_op jit(solution)/shard_map/ppermute | solution.py:562
  25.1 0.6 %copy-done.5 = f32[20]{0:T(128)S(1)} copy-done((f32[20]{0:T(128)S(1)}, f32[20]{0:T(128)}, u32[]{:S(2)}) %copy-start.5) | copy-done | bytes 104
  25.7 0.0 copy-done.6
  25.8 1.9 %shard_map.150 = (f32[20,64,128]{2,1,0:T(8,128)S(1)}, f32[64,128]{1,0:T(8,128)S(1)}, f32[64,128]{1,0:T(8,128)S(1)}, f32[2,20,128]{2,1,0:T(8,128)S(1)}) custom-call(f32[20]{0:T(128)S(1)} %copy-done.5, f32[20]{0:T(128)S(1)} %copy-done.6, f32[20]{0:T(128)S(1)} %copy-done.7, f32[20]{0:T(128)S(1)} %copy-done.8, f32[20]{0:T(128)S(1)} %copy-done.9, ...), custom_call_target="tpu_custom_call" | custom-call | flops 6000000 | bytes 6000000 | tf_op jit(solution)/shard_map/pallas_call | solution.py:671
  27.7 2.0 %collective-permute-done.8.refs_1_ = f32[8,128]{1,0:T(8,128)S(1)} collective-permute-done((f32[8,128]{1,0:T(8,128)S(1)}, f32[8,128]{1,0:T(8,128)S(1)}, u32[]{:S(2)}, u32[]{:S(2)}) %collective-permute-start.8) | collective-permute-done | bytes 4128 | tf_op jit(solution)/shard_map/ppermute | solution.py:562
  29.7 1.2 %shard_map.151 = (f32[16,32,128]{2,1,0:T(8,128)}, f32[64,128]{1,0:T(8,128)}, f32[20,64,128]{2,1,0:T(8,128)}) custom-call(f32[2,20,128]{2,1,0:T(8,128)S(1)} %get-tuple-element.59.coef_ref, f32[64,128]{1,0:T(8,128)S(1)} %bitcast.12, f32[64,128]{1,0:T(8,128)S(1)} %bitcast.11, f32[64,128]{1,0:T(8,128)S(1)} %get-tuple-element.60.sum_ref, ...), custom_call_target="tpu_custom_call" | custom-call | flops 2000000 | bytes 2000000 | tf_op jit(solution)/shard_map/pallas_call | solution.py:684
  (33 shorter events, 0.1 us)
Async XLA Ops:
  2.0 1.4 %collective-permute-start = (f32[2,32,128]{2,1,0:T(8,128)S(1)}, f32[2,32,128]{2,1,0:T(8,128)S(1)}, u32[]{:S(2)}, u32[]{:S(2)}) collective-permute-start(f32[2,32,128]{2,1,0:T(8,128)S(1)} %get-tuple-element.39.own_ref), channel_id=1, source_target_pairs={{0,1},{1,0},{2,3},{3,2},{4,5},{5,4},{6,7},{7,6},{8,9},{9,8},{10,11... | collective-permute-start | bytes 98312 | tf_op jit(solution)/shard_map/ppermute | solution.py:597
  3.4 7.7 %copy-start = (s32[16,32,128]{2,1,0:T(8,128)S(1)}, s32[16,32,128]{2,1,0:T(8,128)}, u32[]{:S(2)}) copy-start(s32[16,32,128]{2,1,0:T(8,128)} %label_hbm.1) | copy-start | bytes 786436
  3.5 10.3 %collective-permute-start.2 = (f32[6,32,128]{2,1,0:T(8,128)S(1)}, f32[6,32,128]{2,1,0:T(8,128)S(1)}, u32[]{:S(2)}, u32[]{:S(2)}) collective-permute-start(f32[6,32,128]{2,1,0:T(8,128)S(1)} %get-tuple-element.48), channel_id=1, source_target_pairs={{0,4},{1,5},{2,6},{3,7},{4,0},{5,1},{6,2},{7,3},{8,12},{9,13},{10,... | collective-permute-start | bytes 294920 | tf_op jit(solution)/shard_map/ppermute | solution.py:562
  6.5 7.3 %collective-permute-start.3 = (f32[6,32,128]{2,1,0:T(8,128)S(1)}, f32[6,32,128]{2,1,0:T(8,128)S(1)}, u32[]{:S(2)}, u32[]{:S(2)}) collective-permute-start(f32[6,32,128]{2,1,0:T(8,128)S(1)} %get-tuple-element.49), channel_id=1, source_target_pairs={{0,1},{1,0},{2,3},{3,2},{4,8},{5,9},{6,10},{7,11},{8,4},{9,5},{10,... | collective-permute-start | bytes 294920 | tf_op jit(solution)/shard_map/ppermute | solution.py:562
  6.5 6.3 %collective-permute-start.1 = (f32[17,8,128]{2,1,0:T(8,128)S(1)}, f32[17,8,128]{2,1,0:T(8,128)S(1)}, u32[]{:S(2)}, u32[]{:S(2)}) collective-permute-start(f32[17,8,128]{2,1,0:T(8,128)S(1)} %get-tuple-element.41), channel_id=1, source_target_pairs={{0,2},{1,3},{2,0},{3,1},{4,6},{5,7},{6,4},{7,5},{8,10},{9,11},{10,... | collective-permute-start | bytes 208904 | tf_op jit(solution)/shard_map/ppermute | solution.py:562
  8.0 5.8 %collective-permute-start.4 = (f32[4,8,128]{2,1,0:T(8,128)S(1)}, f32[4,8,128]{2,1,0:T(8,128)S(1)}, u32[]{:S(2)}, u32[]{:S(2)}) collective-permute-start(f32[4,8,128]{2,1,0:T(8,128)S(1)} %get-tuple-element.50), channel_id=1, source_target_pairs={{0,6},{1,7},{2,4},{3,5},{4,2},{5,3},{6,0},{7,1},{8,14},{9,15},{10,... | collective-permute-start | bytes 49160 | tf_op jit(solution)/shard_map/ppermute | solution.py:562
  11.1 2.7 %collective-permute-start.5 = (f32[4,8,128]{2,1,0:T(8,128)S(1)}, f32[4,8,128]{2,1,0:T(8,128)S(1)}, u32[]{:S(2)}, u32[]{:S(2)}) collective-permute-start(f32[4,8,128]{2,1,0:T(8,128)S(1)} %get-tuple-element.51), channel_id=1, source_target_pairs={{0,1},{1,0},{2,3},{3,2},{4,10},{5,11},{6,8},{7,9},{8,6},{9,7},{10,... | collective-permute-start | bytes 49160 | tf_op jit(solution)/shard_map/ppermute | solution.py:562
  14.5 1.8 %collective-permute-start.6 = (f32[8,128]{1,0:T(8,128)S(1)}, f32[8,128]{1,0:T(8,128)S(1)}, u32[]{:S(2)}, u32[]{:S(2)}) collective-permute-start(f32[8,128]{1,0:T(8,128)S(1)} %get-tuple-element.53.after_ref.a_ref), channel_id=1, source_target_pairs={{0,1},{1,0},{2,3},{3,2},{4,5},{5,4},{6,7},{7,6},{8,9},{9,8},{10,11... | collective-permute-start | bytes 12296 | tf_op jit(solution)/shard_map/ppermute | solution.py:642
  16.3 4.0 %collective-permute-start.7 = (f32[8,128]{1,0:T(8,128)S(1)}, f32[8,128]{1,0:T(8,128)S(1)}, u32[]{:S(2)}, u32[]{:S(2)}) collective-permute-start(f32[8,128]{1,0:T(8,128)S(1)} %shard_map.145.after_ref.a_ref), channel_id=1, source_target_pairs={{0,2},{2,0},{1,3},{3,1},{4,6},{6,4},{5,7},{7,5},{8,10},{10,8},{9,1... | collective-permute-start | bytes 12296 | tf_op jit(solution)/shard_map/ppermute | solution.py:642
  19.0 6.0 %copy-start.1 = (f32[20,1,8192]{2,1,0:T(1,128)S(1)}, f32[20,1,8192]{2,1,0:T(1,128)}, u32[]{:S(2)}) copy-start(f32[20,1,8192]{2,1,0:T(1,128)} %param.17) | copy-start | bytes 1966084
  19.1 6.0 %copy-start.2 = (f32[20,1,8192]{2,1,0:T(1,128)S(1)}, f32[20,1,8192]{2,1,0:T(1,128)}, u32[]{:S(2)}) copy-start(f32[20,1,8192]{2,1,0:T(1,128)} %param.19) | copy-start | bytes 1966084
  20.3 4.8 %copy-start.3 = (f32[1,8192]{1,0:T(1,128)S(1)}, f32[1,8192]{1,0:T(1,128)}, u32[]{:S(2)}) copy-start(f32[1,8192]{1,0:T(1,128)} %param.16) | copy-start | bytes 98308
  20.3 4.8 %copy-start.8 = (f32[20]{0:T(128)S(1)}, f32[20]{0:T(128)}, u32[]{:S(2)}) copy-start(f32[20]{0:T(128)} %cond_ref.1) | copy-start | bytes 244
  20.3 4.8 %copy-start.9 = (f32[20]{0:T(128)S(1)}, f32[20]{0:T(128)}, u32[]{:S(2)}) copy-start(f32[20]{0:T(128)} %rev_ref.1) | copy-start | bytes 244
  20.6 9.1 %collective-permute-start.9 = (f32[200,128]{1,0:T(8,128)S(1)}, f32[200,128]{1,0:T(8,128)S(1)}, u32[]{:S(2)}, u32[]{:S(2)}) collective-permute-start(f32[200,128]{1,0:T(8,128)S(1)} %get-tuple-element.63), channel_id=1, source_target_pairs={{0,8},{1,9},{2,10},{3,11},{4,12},{5,13},{6,14},{7,15},{8,0},{9,1},... | collective-permute-start | bytes 307208 | tf_op jit(solution)/shard_map/ppermute | solution.py:562
  22.0 7.7 %collective-permute-start.10 = (f32[200,128]{1,0:T(8,128)S(1)}, f32[200,128]{1,0:T(8,128)S(1)}, u32[]{:S(2)}, u32[]{:S(2)}) collective-permute-start(f32[200,128]{1,0:T(8,128)S(1)} %get-tuple-element.64), channel_id=1, source_target_pairs={{0,1},{1,0},{2,3},{3,2},{4,8},{5,9},{6,10},{7,11},{8,4},{9,5},{10,... | collective-permute-start | bytes 307208 | tf_op jit(solution)/shard_map/ppermute | solution.py:562
  22.0 7.7 %collective-permute-start.11 = (f32[200,128]{1,0:T(8,128)S(1)}, f32[200,128]{1,0:T(8,128)S(1)}, u32[]{:S(2)}, u32[]{:S(2)}) collective-permute-start(f32[200,128]{1,0:T(8,128)S(1)} %get-tuple-element.65), channel_id=1, source_target_pairs={{0,4},{1,5},{2,6},{3,7},{4,0},{5,1},{6,2},{7,3},{8,12},{9,13},{10,... | collective-permute-start | bytes 307208 | tf_op jit(solution)/shard_map/ppermute | solution.py:562
  24.2 5.5 %collective-permute-start.8 = (f32[8,128]{1,0:T(8,128)S(1)}, f32[8,128]{1,0:T(8,128)S(1)}, u32[]{:S(2)}, u32[]{:S(2)}) collective-permute-start(f32[8,128]{1,0:T(8,128)S(1)} %shard_map.148.total_ref), channel_id=1, source_target_pairs={{0,12},{1,13},{2,14},{3,15},{4,5},{5,4},{6,7},{7,6},{8,9},{9,8},{1... | collective-permute-start | bytes 12296 | tf_op jit(solution)/shard_map/ppermute | solution.py:562
  25.1 0.7 %copy-start.5 = (f32[20]{0:T(128)S(1)}, f32[20]{0:T(128)}, u32[]{:S(2)}) copy-start(f32[20]{0:T(128)} %half_ref.1) | copy-start | bytes 244
  25.1 0.7 %copy-start.6 = (f32[20]{0:T(128)S(1)}, f32[20]{0:T(128)}, u32[]{:S(2)}) copy-start(f32[20]{0:T(128)} %slope_ref.1) | copy-start | bytes 244
  25.1 0.7 %copy-start.7 = (f32[20]{0:T(128)S(1)}, f32[20]{0:T(128)}, u32[]{:S(2)}) copy-start(f32[20]{0:T(128)} %tau_ref.1) | copy-start | bytes 244
  25.8 3.9 %copy-start.4 = (f32[1,8192]{1,0:T(1,128)S(1)}, f32[1,8192]{1,0:T(1,128)}, u32[]{:S(2)}) copy-start(f32[1,8192]{1,0:T(1,128)} %param.18) | copy-start | bytes 98308

commit v13 on v12

--- a/solution.py
+++ b/solution.py
@@ -609,7 +609,7 @@
     y_to = [partners("gy", step) for step in range(n_y)]
     x_to = [partners("gx", step) for step in range(2)]
     along_y = [swap(face, y_to=y_to[j]) for j, face in enumerate(along_y)]
-    along_x = [swap(face, x_to=x_to[i]) for i, face in enumerate(along_x)]
+    along_x = [swap(along_x[i], x_to=x_to[i]) for i in (1, 0)][::-1]
     across = [swap(face, x_to=x_to[k // n_y], y_to=y_to[k % n_y]) for k, face in enumerate(across)]
 
     tall = ring + SUB

time: 31 us -> 31 us (level)
  no operation moved by 1% of the time
where the time goes in v13:
time: 31 us; the launch traced here: 30.9 us
  starting transfers between devices  14.7 us (47%)
  Pallas kernels  11.8 us (38%)
  waiting for transfers between devices  2.87 us (9%)
  between operations  0.85 us (3%)
  local copies, waits for them, and re-layouts  0.68 us (2%)
    ppermute x9, starting transfers between devices, swap(): return lax.ppermute(value, ('gx', 'gy', 'gz'), pairs)  12.1 us
    pallas_call x3, Pallas kernels, couple(): call(functools.partial(couple_kernel, stage, slot_rows), shape_of(slot_ro...  3.56 us
    ppermute x2, starting transfers between devices, add(): lax.ppermute(value, axis, [(i, i ^ step) for i in range(lax.axis_size(axi...  2.13 us
    ppermute x9, waiting for transfers between devices, swap(): return lax.ppermute(value, ('gx', 'gy', 'gz'), pairs)  2.01 us
    pallas_call x1, Pallas kernels, local(): call(membrane_kernel, (shape_of(n_states, block_rows, LANES), shape_of(bl...  1.93 us
    pallas_call x1, Pallas kernels, local(): call(plan_kernel, jax.ShapeDtypeStruct((rows, LANES), jnp.int32), 2, cost...  1.72 us
    pallas_call x1, Pallas kernels, local(): call(start_kernel, (block, block, shape_of(2, ny, nz), shape_of(2, SUB, n...  1.4 us
    pallas_call x1, Pallas kernels, local(): call(functools.partial(finish_kernel, alone), (block, shape_of(block_rows...  1.18 us
  transfers between devices with their start and end apart: 12, of which 2 were waited for; matrix products, arithmetic and copies ran while one was open for 0% of the time, Pallas kernels for 26%

profile of v13, /device:TPU:0, one launch (start us, length us, event | category | flops | bytes accessed | tf_op | source)
XLA Modules:
  0.0 30.9 jit_solution(2834455816773694801)
XLA Ops:
  0.6 1.4 %shard_map.139 = (f32[16,32,128]{2,1,0:T(8,128)S(1)}, f32[16,32,128]{2,1,0:T(8,128)S(1)}, f32[2,32,128]{2,1,0:T(8,128)S(1)}, f32[2,8,128]{2,1,0:T(8,128)S(1)}) custom-call(f32[16,32,128]{2,1,0:T(8,128)} %right_hbm.1, f32[16,32,128]{2,1,0:T(8,128)} %damping_hbm.1, s32[16,32,128]{2,1,0:T(8,128)} %label_hbm.1), custom_call_target="tpu_custom_call" | custom-call | flops 2000000 | bytes 2000000 | tf_op jit(solution)/shard_map/pallas_call | solution.py:588
  2.0 0.5 %collective-permute-start = (f32[2,32,128]{2,1,0:T(8,128)S(1)}, f32[2,32,128]{2,1,0:T(8,128)S(1)}, u32[]{:S(2)}, u32[]{:S(2)}) collective-permute-start(f32[2,32,128]{2,1,0:T(8,128)S(1)} %get-tuple-element.39.own_ref), channel_id=1, source_target_pairs={{0,1},{1,0},{2,3},{3,2},{4,5},{5,4},{6,7},{7,6},{8,9},{9,8},{10,11... | collective-permute-start | bytes 98312 | tf_op jit(solution)/shard_map/ppermute | solution.py:597
  2.6 0.9 %collective-permute-done.got_ref = f32[2,32,128]{2,1,0:T(8,128)S(1)} collective-permute-done((f32[2,32,128]{2,1,0:T(8,128)S(1)}, f32[2,32,128]{2,1,0:T(8,128)S(1)}, u32[]{:S(2)}, u32[]{:S(2)}) %collective-permute-start) | collective-permute-done | bytes 32800 | tf_op jit(solution)/shard_map/ppermute | solution.py:597
  3.4 0.1 shard_map.141
  3.5 3.0 %collective-permute-start.2 = (f32[6,32,128]{2,1,0:T(8,128)S(1)}, f32[6,32,128]{2,1,0:T(8,128)S(1)}, u32[]{:S(2)}, u32[]{:S(2)}) collective-permute-start(f32[6,32,128]{2,1,0:T(8,128)S(1)} %get-tuple-element.48), channel_id=1, source_target_pairs={{0,4},{1,5},{2,6},{3,7},{4,0},{5,1},{6,2},{7,3},{8,12},{9,13},{10,... | collective-permute-start | bytes 294920 | tf_op jit(solution)/shard_map/ppermute | solution.py:562
  6.5 1.5 %collective-permute-start.1 = (f32[17,8,128]{2,1,0:T(8,128)S(1)}, f32[17,8,128]{2,1,0:T(8,128)S(1)}, u32[]{:S(2)}, u32[]{:S(2)}) collective-permute-start(f32[17,8,128]{2,1,0:T(8,128)S(1)} %get-tuple-element.41), channel_id=1, source_target_pairs={{0,2},{1,3},{2,0},{3,1},{4,6},{5,7},{6,4},{7,5},{8,10},{9,11},{10,... | collective-permute-start | bytes 208904 | tf_op jit(solution)/shard_map/ppermute | solution.py:562
  8.0 3.1 %collective-permute-start.4 = (f32[4,8,128]{2,1,0:T(8,128)S(1)}, f32[4,8,128]{2,1,0:T(8,128)S(1)}, u32[]{:S(2)}, u32[]{:S(2)}) collective-permute-start(f32[4,8,128]{2,1,0:T(8,128)S(1)} %get-tuple-element.50), channel_id=1, source_target_pairs={{0,6},{1,7},{2,4},{3,5},{4,2},{5,3},{6,0},{7,1},{8,14},{9,15},{10,... | collective-permute-start | bytes 49160 | tf_op jit(solution)/shard_map/ppermute | solution.py:562
  11.1 1.7 %shard_map.140.after_ref.plan_ref = s32[512,128]{1,0:T(8,128)S(1)} custom-call(f32[2,8,128]{2,1,0:T(8,128)S(1)} %get-tuple-element.36.after_ref.stat_ref, s32[512,128]{1,0:T(8,128)S(1)} %bitcast.7), custom_call_target="tpu_custom_call" | custom-call | flops 6000000 | bytes 6000000 | tf_op jit(solution)/shard_map/pallas_call | solution.py:598
  12.8 0.9 %shard_map.142 = (f32[16,48,128]{2,1,0:T(8,128)S(1)}, f32[16,48,128]{2,1,0:T(8,128)S(1)}, f32[16,48,128]{2,1,0:T(8,128)S(1)}, f32[16,48,128]{2,1,0:T(8,128)S(1)}...) custom-call(f32[16,32,128]{2,1,0:T(8,128)S(1)} %get-tuple-element.37.w0_ref, ...), custom_call_target="tpu_custom_call" | custom-call | flops 6000000 | bytes 6000000 | tf_op jit(solution)/shard_map/pallas_call | solution.py:618
  13.8 0.7 %shard_map.143 = (f32[6,48,128]{2,1,0:T(8,128)S(1)}, f32[6,48,128]{2,1,0:T(8,128)S(1)}, f32[6,48,128]{2,1,0:T(8,128)S(1)}, f32[3,48,256]{2,1,0:T(8,128)S(1)}, f3...) custom-call(s32[512,128]{1,0:T(8,128)S(1)} %shard_map.140.after_ref.plan_ref, ...), custom_call_target="tpu_custom_call" | custom-call | flops 2000000 | bytes 2000000 | tf_op jit(solution)/shard_map/pallas_call | solution.py:625
  14.5 0.6 %collective-permute-start.6 = (f32[8,128]{1,0:T(8,128)S(1)}, f32[8,128]{1,0:T(8,128)S(1)}, u32[]{:S(2)}, u32[]{:S(2)}) collective-permute-start(f32[8,128]{1,0:T(8,128)S(1)} %get-tuple-element.53.after_ref.a_ref), channel_id=1, source_target_pairs={{0,1},{1,0},{2,3},{3,2},{4,5},{5,4},{6,7},{7,6},{8,9},{9,8},{10,11... | collective-permute-start | bytes 12296 | tf_op jit(solution)/shard_map/ppermute | solution.py:642
  15.1 1.2 %shard_map.144.after_ref.refs_0_ = f32[160,128]{1,0:T(8,128)S(1)} custom-call(f32[8,128]{1,0:T(8,128)S(1)} %get-tuple-element.53.after_ref.a_ref, f32[16,48,128]{2,1,0:T(8,128)S(1)} %get-tuple-element.42.a_ref.inside_ref, f32[6,48,128]{2,1,0:T(8,128)S(1)} %get-tuple-element.54.edge_ref, f32[3,48,256]{2,1,0:T(8,128)S(1)} %get-tuple-element.55.slabs_ref, ...), custom_call_target="tpu_custom_call" | custom-call | flops 6000000 | bytes 6000000 | tf_op jit(solution)/shard_map/pallas_call | solution.py:633
  16.3 1.6 %collective-permute-start.7 = (f32[8,128]{1,0:T(8,128)S(1)}, f32[8,128]{1,0:T(8,128)S(1)}, u32[]{:S(2)}, u32[]{:S(2)}) collective-permute-start(f32[8,128]{1,0:T(8,128)S(1)} %shard_map.145.after_ref.a_ref), channel_id=1, source_target_pairs={{0,2},{2,0},{1,3},{3,1},{4,6},{6,4},{5,7},{7,5},{8,10},{10,8},{9,1... | collective-permute-start | bytes 12296 | tf_op jit(solution)/shard_map/ppermute | solution.py:642
  17.8 1.2 %shard_map.146.after_ref.refs_1_ = f32[160,128]{1,0:T(8,128)S(1)} custom-call(f32[8,128]{1,0:T(8,128)S(1)} %shard_map.145.after_ref.a_ref, f32[16,48,128]{2,1,0:T(8,128)S(1)} %get-tuple-element.44.b_ref.inside_ref, f32[6,48,128]{2,1,0:T(8,128)S(1)} %get-tuple-element.56.edge_ref.eb_ref, f32[3,48,256]{2,1,0:T(8,128)S(1)} %get-tuple-element.55.slabs_ref, ...), custom_call_target="tpu_custom_call" | custom-call | flops 6000000 | bytes 6000000 | tf_op jit(solution)/shard_map/pallas_call | solution.py:633
  19.1 1.2 %shard_map.147.after_ref.refs_2_ = f32[160,128]{1,0:T(8,128)S(1)} custom-call(f32[160,128]{1,0:T(8,128)S(1)} %shard_map.146.after_ref.refs_1_, f32[16,48,128]{2,1,0:T(8,128)S(1)} %get-tuple-element.45.c_ref.inside_ref, f32[6,48,128]{2,1,0:T(8,128)S(1)} %get-tuple-element.57.edge_ref.ec_ref, f32[3,48,256]{2,1,0:T(8,128)S(1)} %get-tuple-element.55.slabs_ref, ...), custom_call_target="tpu_custom_call" | custom-call | flops 6000000 | bytes 6000000 | tf_op jit(solution)/shard_map/pallas_call | solution.py:633
  20.3 0.3 shard_map.149
  20.6 1.4 %collective-permute-start.9 = (f32[200,128]{1,0:T(8,128)S(1)}, f32[200,128]{1,0:T(8,128)S(1)}, u32[]{:S(2)}, u32[]{:S(2)}) collective-permute-start(f32[200,128]{1,0:T(8,128)S(1)} %get-tuple-element.63), channel_id=1, source_target_pairs={{0,8},{1,9},{2,10},{3,11},{4,12},{5,13},{6,14},{7,15},{8,0},{9,1},... | collective-permute-start | bytes 307208 | tf_op jit(solution)/shard_map/ppermute | solution.py:562
  22.0 2.2 %collective-permute-start.11 = (f32[200,128]{1,0:T(8,128)S(1)}, f32[200,128]{1,0:T(8,128)S(1)}, u32[]{:S(2)}, u32[]{:S(2)}) collective-permute-start(f32[200,128]{1,0:T(8,128)S(1)} %get-tuple-element.65), channel_id=1, source_target_pairs={{0,4},{1,5},{2,6},{3,7},{4,0},{5,1},{6,2},{7,3},{8,12},{9,13},{10,... | collective-permute-start | bytes 307208 | tf_op jit(solution)/shard_map/ppermute | solution.py:562
  24.2 0.9 %collective-permute-start.8 = (f32[8,128]{1,0:T(8,128)S(1)}, f32[8,128]{1,0:T(8,128)S(1)}, u32[]{:S(2)}, u32[]{:S(2)}) collective-permute-start(f32[8,128]{1,0:T(8,128)S(1)} %shard_map.148.total_ref), channel_id=1, source_target_pairs={{0,12},{1,13},{2,14},{3,15},{4,5},{5,4},{6,7},{7,6},{8,9},{9,8},{1... | collective-permute-start | bytes 12296 | tf_op jit(solution)/shard_map/ppermute | solution.py:562
  25.1 0.6 %copy-done.5 = f32[20]{0:T(128)S(1)} copy-done((f32[20]{0:T(128)S(1)}, f32[20]{0:T(128)}, u32[]{:S(2)}) %copy-start.5) | copy-done | bytes 104
  25.7 0.0 copy-done.6
  25.8 1.9 %shard_map.150 = (f32[20,64,128]{2,1,0:T(8,128)S(1)}, f32[64,128]{1,0:T(8,128)S(1)}, f32[64,128]{1,0:T(8,128)S(1)}, f32[2,20,128]{2,1,0:T(8,128)S(1)}) custom-call(f32[20]{0:T(128)S(1)} %copy-done.5, f32[20]{0:T(128)S(1)} %copy-done.6, f32[20]{0:T(128)S(1)} %copy-done.7, f32[20]{0:T(128)S(1)} %copy-done.8, f32[20]{0:T(128)S(1)} %copy-done.9, ...), custom_call_target="tpu_custom_call" | custom-call | flops 6000000 | bytes 6000000 | tf_op jit(solution)/shard_map/pallas_call | solution.py:671
  27.7 2.0 %collective-permute-done.8.refs_1_ = f32[8,128]{1,0:T(8,128)S(1)} collective-permute-done((f32[8,128]{1,0:T(8,128)S(1)}, f32[8,128]{1,0:T(8,128)S(1)}, u32[]{:S(2)}, u32[]{:S(2)}) %collective-permute-start.8) | collective-permute-done | bytes 4128 | tf_op jit(solution)/shard_map/ppermute | solution.py:562
  29.7 1.2 %shard_map.151 = (f32[16,32,128]{2,1,0:T(8,128)}, f32[64,128]{1,0:T(8,128)}, f32[20,64,128]{2,1,0:T(8,128)}) custom-call(f32[2,20,128]{2,1,0:T(8,128)S(1)} %get-tuple-element.59.coef_ref, f32[64,128]{1,0:T(8,128)S(1)} %bitcast.12, f32[64,128]{1,0:T(8,128)S(1)} %bitcast.11, f32[64,128]{1,0:T(8,128)S(1)} %get-tuple-element.60.sum_ref, ...), custom_call_target="tpu_custom_call" | custom-call | flops 2000000 | bytes 2000000 | tf_op jit(solution)/shard_map/pallas_call | solution.py:684
  (33 shorter events, 0.1 us)
Async XLA Ops:
  2.0 1.4 %collective-permute-start = (f32[2,32,128]{2,1,0:T(8,128)S(1)}, f32[2,32,128]{2,1,0:T(8,128)S(1)}, u32[]{:S(2)}, u32[]{:S(2)}) collective-permute-start(f32[2,32,128]{2,1,0:T(8,128)S(1)} %get-tuple-element.39.own_ref), channel_id=1, source_target_pairs={{0,1},{1,0},{2,3},{3,2},{4,5},{5,4},{6,7},{7,6},{8,9},{9,8},{10,11... | collective-permute-start | bytes 98312 | tf_op jit(solution)/shard_map/ppermute | solution.py:597
  3.4 7.7 %copy-start = (s32[16,32,128]{2,1,0:T(8,128)S(1)}, s32[16,32,128]{2,1,0:T(8,128)}, u32[]{:S(2)}) copy-start(s32[16,32,128]{2,1,0:T(8,128)} %label_hbm.1) | copy-start | bytes 786436
  3.5 10.3 %collective-permute-start.2 = (f32[6,32,128]{2,1,0:T(8,128)S(1)}, f32[6,32,128]{2,1,0:T(8,128)S(1)}, u32[]{:S(2)}, u32[]{:S(2)}) collective-permute-start(f32[6,32,128]{2,1,0:T(8,128)S(1)} %get-tuple-element.48), channel_id=1, source_target_pairs={{0,4},{1,5},{2,6},{3,7},{4,0},{5,1},{6,2},{7,3},{8,12},{9,13},{10,... | collective-permute-start | bytes 294920 | tf_op jit(solution)/shard_map/ppermute | solution.py:562
  6.5 7.3 %collective-permute-start.3 = (f32[6,32,128]{2,1,0:T(8,128)S(1)}, f32[6,32,128]{2,1,0:T(8,128)S(1)}, u32[]{:S(2)}, u32[]{:S(2)}) collective-permute-start(f32[6,32,128]{2,1,0:T(8,128)S(1)} %get-tuple-element.49), channel_id=1, source_target_pairs={{0,1},{1,0},{2,3},{3,2},{4,8},{5,9},{6,10},{7,11},{8,4},{9,5},{10,... | collective-permute-start | bytes 294920 | tf_op jit(solution)/shard_map/ppermute | solution.py:562
  6.5 6.3 %collective-permute-start.1 = (f32[17,8,128]{2,1,0:T(8,128)S(1)}, f32[17,8,128]{2,1,0:T(8,128)S(1)}, u32[]{:S(2)}, u32[]{:S(2)}) collective-permute-start(f32[17,8,128]{2,1,0:T(8,128)S(1)} %get-tuple-element.41), channel_id=1, source_target_pairs={{0,2},{1,3},{2,0},{3,1},{4,6},{5,7},{6,4},{7,5},{8,10},{9,11},{10,... | collective-permute-start | bytes 208904 | tf_op jit(solution)/shard_map/ppermute | solution.py:562
  8.0 5.8 %collective-permute-start.4 = (f32[4,8,128]{2,1,0:T(8,128)S(1)}, f32[4,8,128]{2,1,0:T(8,128)S(1)}, u32[]{:S(2)}, u32[]{:S(2)}) collective-permute-start(f32[4,8,128]{2,1,0:T(8,128)S(1)} %get-tuple-element.50), channel_id=1, source_target_pairs={{0,6},{1,7},{2,4},{3,5},{4,2},{5,3},{6,0},{7,1},{8,14},{9,15},{10,... | collective-permute-start | bytes 49160 | tf_op jit(solution)/shard_map/ppermute | solution.py:562
  11.1 2.7 %collective-permute-start.5 = (f32[4,8,128]{2,1,0:T(8,128)S(1)}, f32[4,8,128]{2,1,0:T(8,128)S(1)}, u32[]{:S(2)}, u32[]{:S(2)}) collective-permute-start(f32[4,8,128]{2,1,0:T(8,128)S(1)} %get-tuple-element.51), channel_id=1, source_target_pairs={{0,1},{1,0},{2,3},{3,2},{4,10},{5,11},{6,8},{7,9},{8,6},{9,7},{10,... | collective-permute-start | bytes 49160 | tf_op jit(solution)/shard_map/ppermute | solution.py:562
  14.5 1.8 %collective-permute-start.6 = (f32[8,128]{1,0:T(8,128)S(1)}, f32[8,128]{1,0:T(8,128)S(1)}, u32[]{:S(2)}, u32[]{:S(2)}) collective-permute-start(f32[8,128]{1,0:T(8,128)S(1)} %get-tuple-element.53.after_ref.a_ref), channel_id=1, source_target_pairs={{0,1},{1,0},{2,3},{3,2},{4,5},{5,4},{6,7},{7,6},{8,9},{9,8},{10,11... | collective-permute-start | bytes 12296 | tf_op jit(solution)/shard_map/ppermute | solution.py:642
  16.3 4.0 %collective-permute-start.7 = (f32[8,128]{1,0:T(8,128)S(1)}, f32[8,128]{1,0:T(8,128)S(1)}, u32[]{:S(2)}, u32[]{:S(2)}) collective-permute-start(f32[8,128]{1,0:T(8,128)S(1)} %shard_map.145.after_ref.a_ref), channel_id=1, source_target_pairs={{0,2},{2,0},{1,3},{3,1},{4,6},{6,4},{5,7},{7,5},{8,10},{10,8},{9,1... | collective-permute-start | bytes 12296 | tf_op jit(solution)/shard_map/ppermute | solution.py:642
  19.0 6.0 %copy-start.1 = (f32[20,1,8192]{2,1,0:T(1,128)S(1)}, f32[20,1,8192]{2,1,0:T(1,128)}, u32[]{:S(2)}) copy-start(f32[20,1,8192]{2,1,0:T(1,128)} %param.17) | copy-start | bytes 1966084
  19.1 6.0 %copy-start.2 = (f32[20,1,8192]{2,1,0:T(1,128)S(1)}, f32[20,1,8192]{2,1,0:T(1,128)}, u32[]{:S(2)}) copy-start(f32[20,1,8192]{2,1,0:T(1,128)} %param.19) | copy-start | bytes 1966084
  20.3 4.8 %copy-start.3 = (f32[1,8192]{1,0:T(1,128)S(1)}, f32[1,8192]{1,0:T(1,128)}, u32[]{:S(2)}) copy-start(f32[1,8192]{1,0:T(1,128)} %param.16) | copy-start | bytes 98308
  20.3 4.8 %copy-start.8 = (f32[20]{0:T(128)S(1)}, f32[20]{0:T(128)}, u32[]{:S(2)}) copy-start(f32[20]{0:T(128)} %cond_ref.1) | copy-start | bytes 244
  20.3 4.8 %copy-start.9 = (f32[20]{0:T(128)S(1)}, f32[20]{0:T(128)}, u32[]{:S(2)}) copy-start(f32[20]{0:T(128)} %rev_ref.1) | copy-start | bytes 244
  20.6 9.1 %collective-permute-start.9 = (f32[200,128]{1,0:T(8,128)S(1)}, f32[200,128]{1,0:T(8,128)S(1)}, u32[]{:S(2)}, u32[]{:S(2)}) collective-permute-start(f32[200,128]{1,0:T(8,128)S(1)} %get-tuple-element.63), channel_id=1, source_target_pairs={{0,8},{1,9},{2,10},{3,11},{4,12},{5,13},{6,14},{7,15},{8,0},{9,1},... | collective-permute-start | bytes 307208 | tf_op jit(solution)/shard_map/ppermute | solution.py:562
  22.0 7.7 %collective-permute-start.10 = (f32[200,128]{1,0:T(8,128)S(1)}, f32[200,128]{1,0:T(8,128)S(1)}, u32[]{:S(2)}, u32[]{:S(2)}) collective-permute-start(f32[200,128]{1,0:T(8,128)S(1)} %get-tuple-element.64), channel_id=1, source_target_pairs={{0,1},{1,0},{2,3},{3,2},{4,8},{5,9},{6,10},{7,11},{8,4},{9,5},{10,... | collective-permute-start | bytes 307208 | tf_op jit(solution)/shard_map/ppermute | solution.py:562
  22.0 7.7 %collective-permute-start.11 = (f32[200,128]{1,0:T(8,128)S(1)}, f32[200,128]{1,0:T(8,128)S(1)}, u32[]{:S(2)}, u32[]{:S(2)}) collective-permute-start(f32[200,128]{1,0:T(8,128)S(1)} %get-tuple-element.65), channel_id=1, source_target_pairs={{0,4},{1,5},{2,6},{3,7},{4,0},{5,1},{6,2},{7,3},{8,12},{9,13},{10,... | collective-permute-start | bytes 307208 | tf_op jit(solution)/shard_map/ppermute | solution.py:562
  24.2 5.5 %collective-permute-start.8 = (f32[8,128]{1,0:T(8,128)S(1)}, f32[8,128]{1,0:T(8,128)S(1)}, u32[]{:S(2)}, u32[]{:S(2)}) collective-permute-start(f32[8,128]{1,0:T(8,128)S(1)} %shard_map.148.total_ref), channel_id=1, source_target_pairs={{0,12},{1,13},{2,14},{3,15},{4,5},{5,4},{6,7},{7,6},{8,9},{9,8},{1... | collective-permute-start | bytes 12296 | tf_op jit(solution)/shard_map/ppermute | solution.py:562
  25.1 0.7 %copy-start.5 = (f32[20]{0:T(128)S(1)}, f32[20]{0:T(128)}, u32[]{:S(2)}) copy-start(f32[20]{0:T(128)} %half_ref.1) | copy-start | bytes 244
  25.1 0.7 %copy-start.6 = (f32[20]{0:T(128)S(1)}, f32[20]{0:T(128)}, u32[]{:S(2)}) copy-start(f32[20]{0:T(128)} %slope_ref.1) | copy-start | bytes 244
  25.1 0.7 %copy-start.7 = (f32[20]{0:T(128)S(1)}, f32[20]{0:T(128)}, u32[]{:S(2)}) copy-start(f32[20]{0:T(128)} %tau_ref.1) | copy-start | bytes 244
  25.8 3.9 %copy-start.4 = (f32[1,8192]{1,0:T(1,128)S(1)}, f32[1,8192]{1,0:T(1,128)}, u32[]{:S(2)}) copy-start(f32[1,8192]{1,0:T(1,128)} %param.18) | copy-start | bytes 98308

commit v14 on v12

--- a/solution.py
+++ b/solution.py
@@ -259,7 +259,7 @@
 def outer_kernel(
     n_y, column_total, after_ref, a_ref, i_ref, b_ref, c_ref, slab_ref, sum_ref, stat_ref, *refs
 ):
-    x_refs, corner_refs = refs[:2], refs[2 : 2 + 2 * n_y]
+    x_refs, corner_refs = refs[1::-1], refs[2 : 2 + 2 * n_y]
     ea_ref, eb_ref, ec_ref, slabs_ref, total_ref, where_ref, ei_ref, si_ref = refs[2 + 2 * n_y :]
     nx, ny, nz = a_ref.shape[0], a_ref.shape[1] - 2 * SUB, a_ref.shape[2]
     ring = ny + SUB
@@ -627,7 +627,7 @@
         (edges,) * 3 + (shape_of(3, tall, 2 * nz), shape_of(SUB, nz), shape_of(SUB, nz)),
         10 + 2 * n_y,
         scratch=[pltpu.VMEM((4, tall, nz), F32), pltpu.VMEM((1, tall, 2 * nz), F32)],
-    )(plan, in0, in_inv, in1, in2, own_slab, in_sums, stat, *along_x, *across)
+    )(plan, in0, in_inv, in1, in2, own_slab, in_sums, stat, *along_x[::-1], *across)
 
     def couple(stage, after, inside, ends):
         return call(

time: 31 us -> 31.6 us (1.019)
  waiting for transfers between devices: 2.87 us -> 5.48 us
  starting transfers between devices: 14.7 us -> 12.7 us
    ppermute x9, waiting for transfers between devices: 2.01 us -> 4.06 us  [swap(): return lax.ppermute(value, ('gx', 'gy', 'gz'), pairs)]
    ppermute x2, starting transfers between devices: 2.13 us -> 0.77 us  [add(): lax.ppermute(value, axis, [(i, i ^ step) for i in range(lax.axis_size(axi...]
    ppermute x9, starting transfers between devices: 12.1 us -> 11.5 us  [swap(): return lax.ppermute(value, ('gx', 'gy', 'gz'), pairs)]
    ppermute x2, waiting for transfers between devices: 0.01 us -> 0.56 us  [add(): lax.ppermute(value, axis, [(i, i ^ step) for i in range(lax.axis_size(axi...]
  transfers between devices with their start and end apart: 12 -> 12, of which waited for: 2 -> 5; matrix products, arithmetic and copies ran while one was open for 0% -> 0% of each run, Pallas kernels for 26% -> 26%
where the time goes in v14:
time: 31.6 us; the launch traced here: 31.5 us
  starting transfers between devices  12.7 us (40%)
  Pallas kernels  11.8 us (37%)
  waiting for transfers between devices  5.48 us (17%)
  between operations  0.8 us (3%)
  local copies, waits for them, and re-layouts  0.67 us (2%)
    ppermute x9, starting transfers between devices, swap(): return lax.ppermute(value, ('gx', 'gy', 'gz'), pairs)  11.5 us
    ppermute x9, waiting for transfers between devices, swap(): return lax.ppermute(value, ('gx', 'gy', 'gz'), pairs)  4.06 us
    pallas_call x3, Pallas kernels, couple(): call(functools.partial(couple_kernel, stage, slot_rows), shape_of(slot_ro...  3.56 us
    pallas_call x1, Pallas kernels, local(): call(membrane_kernel, (shape_of(n_states, block_rows, LANES), shape_of(bl...  1.93 us
    pallas_call x1, Pallas kernels, local(): call(plan_kernel, jax.ShapeDtypeStruct((rows, LANES), jnp.int32), 2, cost...  1.72 us
    pallas_call x1, Pallas kernels, local(): call(start_kernel, (block, block, shape_of(2, ny, nz), shape_of(2, SUB, n...  1.4 us
    pallas_call x1, Pallas kernels, local(): call(functools.partial(finish_kernel, alone), (block, shape_of(block_rows...  1.18 us
    pallas_call x1, Pallas kernels, local(): call(functools.partial(inner_kernel, n_y), (planes,) * 4 + (shape_of(5, S...  0.93 us
  transfers between devices with their start and end apart: 12, of which 5 were waited for; matrix products, arithmetic and copies ran while one was open for 0% of the time, Pallas kernels for 26%

profile of v14, /device:TPU:0, one launch (start us, length us, event | category | flops | bytes accessed | tf_op | source)
XLA Modules:
  0.0 31.5 jit_solution(9030524514141202320)
XLA Ops:
  0.6 1.4 %shard_map.139 = (f32[16,32,128]{2,1,0:T(8,128)S(1)}, f32[16,32,128]{2,1,0:T(8,128)S(1)}, f32[2,32,128]{2,1,0:T(8,128)S(1)}, f32[2,8,128]{2,1,0:T(8,128)S(1)}) custom-call(f32[16,32,128]{2,1,0:T(8,128)} %right_hbm.1, f32[16,32,128]{2,1,0:T(8,128)} %damping_hbm.1, s32[16,32,128]{2,1,0:T(8,128)} %label_hbm.1), custom_call_target="tpu_custom_call" | custom-call | flops 2000000 | bytes 2000000 | tf_op jit(solution)/shard_map/pallas_call | solution.py:588
  2.0 0.5 %collective-permute-start = (f32[2,32,128]{2,1,0:T(8,128)S(1)}, f32[2,32,128]{2,1,0:T(8,128)S(1)}, u32[]{:S(2)}, u32[]{:S(2)}) collective-permute-start(f32[2,32,128]{2,1,0:T(8,128)S(1)} %get-tuple-element.39.own_ref), channel_id=1, source_target_pairs={{0,1},{1,0},{2,3},{3,2},{4,5},{5,4},{6,7},{7,6},{8,9},{9,8},{10,11... | collective-permute-start | bytes 98312 | tf_op jit(solution)/shard_map/ppermute | solution.py:597
  2.6 0.9 %collective-permute-done.got_ref = f32[2,32,128]{2,1,0:T(8,128)S(1)} collective-permute-done((f32[2,32,128]{2,1,0:T(8,128)S(1)}, f32[2,32,128]{2,1,0:T(8,128)S(1)}, u32[]{:S(2)}, u32[]{:S(2)}) %collective-permute-start) | collective-permute-done | bytes 32800 | tf_op jit(solution)/shard_map/ppermute | solution.py:597
  3.5 0.4 %collective-permute-start.2 = (f32[6,32,128]{2,1,0:T(8,128)S(1)}, f32[6,32,128]{2,1,0:T(8,128)S(1)}, u32[]{:S(2)}, u32[]{:S(2)}) collective-permute-start(f32[6,32,128]{2,1,0:T(8,128)S(1)} %get-tuple-element.48), channel_id=1, source_target_pairs={{0,1},{1,0},{2,3},{3,2},{4,8},{5,9},{6,10},{7,11},{8,4},{9,5},{10,... | collective-permute-start | bytes 294920 | tf_op jit(solution)/shard_map/ppermute | solution.py:562
  3.9 4.1 %collective-permute-start.3 = (f32[6,32,128]{2,1,0:T(8,128)S(1)}, f32[6,32,128]{2,1,0:T(8,128)S(1)}, u32[]{:S(2)}, u32[]{:S(2)}) collective-permute-start(f32[6,32,128]{2,1,0:T(8,128)S(1)} %get-tuple-element.49), channel_id=1, source_target_pairs={{0,4},{1,5},{2,6},{3,7},{4,0},{5,1},{6,2},{7,3},{8,12},{9,13},{10,... | collective-permute-start | bytes 294920 | tf_op jit(solution)/shard_map/ppermute | solution.py:562
  8.1 1.5 %collective-permute-start.1 = (f32[17,8,128]{2,1,0:T(8,128)S(1)}, f32[17,8,128]{2,1,0:T(8,128)S(1)}, u32[]{:S(2)}, u32[]{:S(2)}) collective-permute-start(f32[17,8,128]{2,1,0:T(8,128)S(1)} %get-tuple-element.41), channel_id=1, source_target_pairs={{0,2},{1,3},{2,0},{3,1},{4,6},{5,7},{6,4},{7,5},{8,10},{9,11},{10,... | collective-permute-start | bytes 208904 | tf_op jit(solution)/shard_map/ppermute | solution.py:562
  9.6 1.7 %shard_map.140.after_ref.plan_ref = s32[512,128]{1,0:T(8,128)S(1)} custom-call(f32[2,8,128]{2,1,0:T(8,128)S(1)} %get-tuple-element.36.after_ref.stat_ref, s32[512,128]{1,0:T(8,128)S(1)} %bitcast.7), custom_call_target="tpu_custom_call" | custom-call | flops 6000000 | bytes 6000000 | tf_op jit(solution)/shard_map/pallas_call | solution.py:598
  11.3 1.1 %collective-permute-done.1.refs_0_ = f32[17,8,128]{2,1,0:T(8,128)S(1)} collective-permute-done((f32[17,8,128]{2,1,0:T(8,128)S(1)}, f32[17,8,128]{2,1,0:T(8,128)S(1)}, u32[]{:S(2)}, u32[]{:S(2)}) %collective-permute-start.1) | collective-permute-done | bytes 69664 | tf_op jit(solution)/shard_map/ppermute | solution.py:562
  12.4 0.9 %shard_map.142 = (f32[16,48,128]{2,1,0:T(8,128)S(1)}, f32[16,48,128]{2,1,0:T(8,128)S(1)}, f32[16,48,128]{2,1,0:T(8,128)S(1)}, f32[16,48,128]{2,1,0:T(8,128)S(1)}...) custom-call(f32[16,32,128]{2,1,0:T(8,128)S(1)} %get-tuple-element.37.w0_ref, ...), custom_call_target="tpu_custom_call" | custom-call | flops 6000000 | bytes 6000000 | tf_op jit(solution)/shard_map/pallas_call | solution.py:618
  13.3 0.9 %collective-permute-done.4.refs_2_ = f32[4,8,128]{2,1,0:T(8,128)S(1)} collective-permute-done((f32[4,8,128]{2,1,0:T(8,128)S(1)}, f32[4,8,128]{2,1,0:T(8,128)S(1)}, u32[]{:S(2)}, u32[]{:S(2)}) %collective-permute-start.4) | collective-permute-done | bytes 16416 | tf_op jit(solution)/shard_map/ppermute | solution.py:562
  14.2 0.7 %shard_map.143 = (f32[6,48,128]{2,1,0:T(8,128)S(1)}, f32[6,48,128]{2,1,0:T(8,128)S(1)}, f32[6,48,128]{2,1,0:T(8,128)S(1)}, f32[3,48,256]{2,1,0:T(8,128)S(1)}, f3...) custom-call(s32[512,128]{1,0:T(8,128)S(1)} %shard_map.140.after_ref.plan_ref, ...), custom_call_target="tpu_custom_call" | custom-call | flops 2000000 | bytes 2000000 | tf_op jit(solution)/shard_map/pallas_call | solution.py:625
  15.0 1.2 %shard_map.144.after_ref.refs_0_ = f32[160,128]{1,0:T(8,128)S(1)} custom-call(f32[8,128]{1,0:T(8,128)S(1)} %get-tuple-element.53.after_ref.a_ref, f32[16,48,128]{2,1,0:T(8,128)S(1)} %get-tuple-element.42.a_ref.inside_ref, f32[6,48,128]{2,1,0:T(8,128)S(1)} %get-tuple-element.54.edge_ref, f32[3,48,256]{2,1,0:T(8,128)S(1)} %get-tuple-element.55.slabs_ref, ...), custom_call_target="tpu_custom_call" | custom-call | flops 6000000 | bytes 6000000 | tf_op jit(solution)/shard_map/pallas_call | solution.py:633
  16.2 0.7 %collective-permute-start.7 = (f32[8,128]{1,0:T(8,128)S(1)}, f32[8,128]{1,0:T(8,128)S(1)}, u32[]{:S(2)}, u32[]{:S(2)}) collective-permute-start(f32[8,128]{1,0:T(8,128)S(1)} %shard_map.145.after_ref.a_ref), channel_id=1, source_target_pairs={{0,2},{2,0},{1,3},{3,1},{4,6},{6,4},{5,7},{7,5},{8,10},{10,8},{9,1... | collective-permute-start | bytes 12296 | tf_op jit(solution)/shard_map/ppermute | solution.py:642
  16.9 1.2 %shard_map.146.after_ref.refs_1_ = f32[160,128]{1,0:T(8,128)S(1)} custom-call(f32[8,128]{1,0:T(8,128)S(1)} %shard_map.145.after_ref.a_ref, f32[16,48,128]{2,1,0:T(8,128)S(1)} %get-tuple-element.44.b_ref.inside_ref, f32[6,48,128]{2,1,0:T(8,128)S(1)} %get-tuple-element.56.edge_ref.eb_ref, f32[3,48,256]{2,1,0:T(8,128)S(1)} %get-tuple-element.55.slabs_ref, ...), custom_call_target="tpu_custom_call" | custom-call | flops 6000000 | bytes 6000000 | tf_op jit(solution)/shard_map/pallas_call | solution.py:633
  18.1 1.2 %shard_map.147.after_ref.refs_2_ = f32[160,128]{1,0:T(8,128)S(1)} custom-call(f32[160,128]{1,0:T(8,128)S(1)} %shard_map.146.after_ref.refs_1_, f32[16,48,128]{2,1,0:T(8,128)S(1)} %get-tuple-element.45.c_ref.inside_ref, f32[6,48,128]{2,1,0:T(8,128)S(1)} %get-tuple-element.57.edge_ref.ec_ref, f32[3,48,256]{2,1,0:T(8,128)S(1)} %get-tuple-element.55.slabs_ref, ...), custom_call_target="tpu_custom_call" | custom-call | flops 6000000 | bytes 6000000 | tf_op jit(solution)/shard_map/pallas_call | solution.py:633
  19.3 0.6 %collective-permute-done.7.b_ref = f32[8,128]{1,0:T(8,128)S(1)} collective-permute-done((f32[8,128]{1,0:T(8,128)S(1)}, f32[8,128]{1,0:T(8,128)S(1)}, u32[]{:S(2)}, u32[]{:S(2)}) %collective-permute-start.7) | collective-permute-done | bytes 4128 | tf_op jit(solution)/shard_map/ppermute | solution.py:642
  19.9 0.3 shard_map.149
  20.2 2.5 %collective-permute-start.9 = (f32[200,128]{1,0:T(8,128)S(1)}, f32[200,128]{1,0:T(8,128)S(1)}, u32[]{:S(2)}, u32[]{:S(2)}) collective-permute-start(f32[200,128]{1,0:T(8,128)S(1)} %get-tuple-element.63), channel_id=1, source_target_pairs={{0,8},{1,9},{2,10},{3,11},{4,12},{5,13},{6,14},{7,15},{8,0},{9,1},... | collective-permute-start | bytes 307208 | tf_op jit(solution)/shard_map/ppermute | solution.py:562
  22.7 1.0 %collective-permute-start.11 = (f32[200,128]{1,0:T(8,128)S(1)}, f32[200,128]{1,0:T(8,128)S(1)}, u32[]{:S(2)}, u32[]{:S(2)}) collective-permute-start(f32[200,128]{1,0:T(8,128)S(1)} %get-tuple-element.65), channel_id=1, source_target_pairs={{0,4},{1,5},{2,6},{3,7},{4,0},{5,1},{6,2},{7,3},{8,12},{9,13},{10,... | collective-permute-start | bytes 307208 | tf_op jit(solution)/shard_map/ppermute | solution.py:562
  23.7 1.8 %collective-permute-start.8 = (f32[8,128]{1,0:T(8,128)S(1)}, f32[8,128]{1,0:T(8,128)S(1)}, u32[]{:S(2)}, u32[]{:S(2)}) collective-permute-start(f32[8,128]{1,0:T(8,128)S(1)} %shard_map.148.total_ref), channel_id=1, source_target_pairs={{0,12},{1,13},{2,14},{3,15},{4,5},{5,4},{6,7},{7,6},{8,9},{9,8},{1... | collective-permute-start | bytes 12296 | tf_op jit(solution)/shard_map/ppermute | solution.py:562
  25.6 0.6 %copy-done.5 = f32[20]{0:T(128)S(1)} copy-done((f32[20]{0:T(128)S(1)}, f32[20]{0:T(128)}, u32[]{:S(2)}) %copy-start.5) | copy-done | bytes 104
  26.3 1.9 %shard_map.150 = (f32[20,64,128]{2,1,0:T(8,128)S(1)}, f32[64,128]{1,0:T(8,128)S(1)}, f32[64,128]{1,0:T(8,128)S(1)}, f32[2,20,128]{2,1,0:T(8,128)S(1)}) custom-call(f32[20]{0:T(128)S(1)} %copy-done.5, f32[20]{0:T(128)S(1)} %copy-done.6, f32[20]{0:T(128)S(1)} %copy-done.7, f32[20]{0:T(128)S(1)} %copy-done.8, f32[20]{0:T(128)S(1)} %copy-done.9, ...), custom_call_target="tpu_custom_call" | custom-call | flops 6000000 | bytes 6000000 | tf_op jit(solution)/shard_map/pallas_call | solution.py:671
  28.2 2.1 %collective-permute-done.8.refs_1_ = f32[8,128]{1,0:T(8,128)S(1)} collective-permute-done((f32[8,128]{1,0:T(8,128)S(1)}, f32[8,128]{1,0:T(8,128)S(1)}, u32[]{:S(2)}, u32[]{:S(2)}) %collective-permute-start.8) | collective-permute-done | bytes 4128 | tf_op jit(solution)/shard_map/ppermute | solution.py:562
  30.3 1.2 %shard_map.151 = (f32[16,32,128]{2,1,0:T(8,128)}, f32[64,128]{1,0:T(8,128)}, f32[20,64,128]{2,1,0:T(8,128)}) custom-call(f32[2,20,128]{2,1,0:T(8,128)S(1)} %get-tuple-element.59.coef_ref, f32[64,128]{1,0:T(8,128)S(1)} %bitcast.12, f32[64,128]{1,0:T(8,128)S(1)} %bitcast.11, f32[64,128]{1,0:T(8,128)S(1)} %get-tuple-element.60.sum_ref, ...), custom_call_target="tpu_custom_call" | custom-call | flops 2000000 | bytes 2000000 | tf_op jit(solution)/shard_map/pallas_call | solution.py:684
  (33 shorter events, 0.3 us)
Async XLA Ops:
  2.0 1.4 %collective-permute-start = (f32[2,32,128]{2,1,0:T(8,128)S(1)}, f32[2,32,128]{2,1,0:T(8,128)S(1)}, u32[]{:S(2)}, u32[]{:S(2)}) collective-permute-start(f32[2,32,128]{2,1,0:T(8,128)S(1)} %get-tuple-element.39.own_ref), channel_id=1, source_target_pairs={{0,1},{1,0},{2,3},{3,2},{4,5},{5,4},{6,7},{7,6},{8,9},{9,8},{10,11... | collective-permute-start | bytes 98312 | tf_op jit(solution)/shard_map/ppermute | solution.py:597
  3.4 6.1 %copy-start = (s32[16,32,128]{2,1,0:T(8,128)S(1)}, s32[16,32,128]{2,1,0:T(8,128)}, u32[]{:S(2)}) copy-start(s32[16,32,128]{2,1,0:T(8,128)} %label_hbm.1) | copy-start | bytes 786436
  3.5 10.7 %collective-permute-start.2 = (f32[6,32,128]{2,1,0:T(8,128)S(1)}, f32[6,32,128]{2,1,0:T(8,128)S(1)}, u32[]{:S(2)}, u32[]{:S(2)}) collective-permute-start(f32[6,32,128]{2,1,0:T(8,128)S(1)} %get-tuple-element.48), channel_id=1, source_target_pairs={{0,1},{1,0},{2,3},{3,2},{4,8},{5,9},{6,10},{7,11},{8,4},{9,5},{10,... | collective-permute-start | bytes 294920 | tf_op jit(solution)/shard_map/ppermute | solution.py:562
  3.9 10.3 %collective-permute-start.3 = (f32[6,32,128]{2,1,0:T(8,128)S(1)}, f32[6,32,128]{2,1,0:T(8,128)S(1)}, u32[]{:S(2)}, u32[]{:S(2)}) collective-permute-start(f32[6,32,128]{2,1,0:T(8,128)S(1)} %get-tuple-element.49), channel_id=1, source_target_pairs={{0,4},{1,5},{2,6},{3,7},{4,0},{5,1},{6,2},{7,3},{8,12},{9,13},{10,... | collective-permute-start | bytes 294920 | tf_op jit(solution)/shard_map/ppermute | solution.py:562
  8.1 4.3 %collective-permute-start.1 = (f32[17,8,128]{2,1,0:T(8,128)S(1)}, f32[17,8,128]{2,1,0:T(8,128)S(1)}, u32[]{:S(2)}, u32[]{:S(2)}) collective-permute-start(f32[17,8,128]{2,1,0:T(8,128)S(1)} %get-tuple-element.41), channel_id=1, source_target_pairs={{0,2},{1,3},{2,0},{3,1},{4,6},{5,7},{6,4},{7,5},{8,10},{9,11},{10,... | collective-permute-start | bytes 208904 | tf_op jit(solution)/shard_map/ppermute | solution.py:562
  9.6 4.6 %collective-permute-start.4 = (f32[4,8,128]{2,1,0:T(8,128)S(1)}, f32[4,8,128]{2,1,0:T(8,128)S(1)}, u32[]{:S(2)}, u32[]{:S(2)}) collective-permute-start(f32[4,8,128]{2,1,0:T(8,128)S(1)} %get-tuple-element.50), channel_id=1, source_target_pairs={{0,6},{1,7},{2,4},{3,5},{4,2},{5,3},{6,0},{7,1},{8,14},{9,15},{10,... | collective-permute-start | bytes 49160 | tf_op jit(solution)/shard_map/ppermute | solution.py:562
  9.6 4.6 %collective-permute-start.5 = (f32[4,8,128]{2,1,0:T(8,128)S(1)}, f32[4,8,128]{2,1,0:T(8,128)S(1)}, u32[]{:S(2)}, u32[]{:S(2)}) collective-permute-start(f32[4,8,128]{2,1,0:T(8,128)S(1)} %get-tuple-element.51), channel_id=1, source_target_pairs={{0,1},{1,0},{2,3},{3,2},{4,10},{5,11},{6,8},{7,9},{8,6},{9,7},{10,... | collective-permute-start | bytes 49160 | tf_op jit(solution)/shard_map/ppermute | solution.py:562
  14.9 1.3 %collective-permute-start.6 = (f32[8,128]{1,0:T(8,128)S(1)}, f32[8,128]{1,0:T(8,128)S(1)}, u32[]{:S(2)}, u32[]{:S(2)}) collective-permute-start(f32[8,128]{1,0:T(8,128)S(1)} %get-tuple-element.53.after_ref.a_ref), channel_id=1, source_target_pairs={{0,1},{1,0},{2,3},{3,2},{4,5},{5,4},{6,7},{7,6},{8,9},{9,8},{10,11... | collective-permute-start | bytes 12296 | tf_op jit(solution)/shard_map/ppermute | solution.py:642
  16.2 3.7 %collective-permute-start.7 = (f32[8,128]{1,0:T(8,128)S(1)}, f32[8,128]{1,0:T(8,128)S(1)}, u32[]{:S(2)}, u32[]{:S(2)}) collective-permute-start(f32[8,128]{1,0:T(8,128)S(1)} %shard_map.145.after_ref.a_ref), channel_id=1, source_target_pairs={{0,2},{2,0},{1,3},{3,1},{4,6},{6,4},{5,7},{7,5},{8,10},{10,8},{9,1... | collective-permute-start | bytes 12296 | tf_op jit(solution)/shard_map/ppermute | solution.py:642
  18.1 7.5 %copy-start.1 = (f32[20,1,8192]{2,1,0:T(1,128)S(1)}, f32[20,1,8192]{2,1,0:T(1,128)}, u32[]{:S(2)}) copy-start(f32[20,1,8192]{2,1,0:T(1,128)} %param.17) | copy-start | bytes 1966084
  18.1 7.5 %copy-start.2 = (f32[20,1,8192]{2,1,0:T(1,128)S(1)}, f32[20,1,8192]{2,1,0:T(1,128)}, u32[]{:S(2)}) copy-start(f32[20,1,8192]{2,1,0:T(1,128)} %param.19) | copy-start | bytes 1966084
  19.9 5.7 %copy-start.3 = (f32[1,8192]{1,0:T(1,128)S(1)}, f32[1,8192]{1,0:T(1,128)}, u32[]{:S(2)}) copy-start(f32[1,8192]{1,0:T(1,128)} %param.16) | copy-start | bytes 98308
  19.9 5.7 %copy-start.8 = (f32[20]{0:T(128)S(1)}, f32[20]{0:T(128)}, u32[]{:S(2)}) copy-start(f32[20]{0:T(128)} %cond_ref.1) | copy-start | bytes 244
  19.9 5.8 %copy-start.9 = (f32[20]{0:T(128)S(1)}, f32[20]{0:T(128)}, u32[]{:S(2)}) copy-start(f32[20]{0:T(128)} %rev_ref.1) | copy-start | bytes 244
  20.2 10.1 %collective-permute-start.9 = (f32[200,128]{1,0:T(8,128)S(1)}, f32[200,128]{1,0:T(8,128)S(1)}, u32[]{:S(2)}, u32[]{:S(2)}) collective-permute-start(f32[200,128]{1,0:T(8,128)S(1)} %get-tuple-element.63), channel_id=1, source_target_pairs={{0,8},{1,9},{2,10},{3,11},{4,12},{5,13},{6,14},{7,15},{8,0},{9,1},... | collective-permute-start | bytes 307208 | tf_op jit(solution)/shard_map/ppermute | solution.py:562
  22.7 7.6 %collective-permute-start.10 = (f32[200,128]{1,0:T(8,128)S(1)}, f32[200,128]{1,0:T(8,128)S(1)}, u32[]{:S(2)}, u32[]{:S(2)}) collective-permute-start(f32[200,128]{1,0:T(8,128)S(1)} %get-tuple-element.64), channel_id=1, source_target_pairs={{0,1},{1,0},{2,3},{3,2},{4,8},{5,9},{6,10},{7,11},{8,4},{9,5},{10,... | collective-permute-start | bytes 307208 | tf_op jit(solution)/shard_map/ppermute | solution.py:562
  22.7 7.6 %collective-permute-start.11 = (f32[200,128]{1,0:T(8,128)S(1)}, f32[200,128]{1,0:T(8,128)S(1)}, u32[]{:S(2)}, u32[]{:S(2)}) collective-permute-start(f32[200,128]{1,0:T(8,128)S(1)} %get-tuple-element.65), channel_id=1, source_target_pairs={{0,4},{1,5},{2,6},{3,7},{4,0},{5,1},{6,2},{7,3},{8,12},{9,13},{10,... | collective-permute-start | bytes 307208 | tf_op jit(solution)/shard_map/ppermute | solution.py:562
  23.7 6.5 %collective-permute-start.8 = (f32[8,128]{1,0:T(8,128)S(1)}, f32[8,128]{1,0:T(8,128)S(1)}, u32[]{:S(2)}, u32[]{:S(2)}) collective-permute-start(f32[8,128]{1,0:T(8,128)S(1)} %shard_map.148.total_ref), channel_id=1, source_target_pairs={{0,12},{1,13},{2,14},{3,15},{4,5},{5,4},{6,7},{7,6},{8,9},{9,8},{1... | collective-permute-start | bytes 12296 | tf_op jit(solution)/shard_map/ppermute | solution.py:562
  25.6 0.7 %copy-start.5 = (f32[20]{0:T(128)S(1)}, f32[20]{0:T(128)}, u32[]{:S(2)}) copy-start(f32[20]{0:T(128)} %half_ref.1) | copy-start | bytes 244
  25.6 0.7 %copy-start.6 = (f32[20]{0:T(128)S(1)}, f32[20]{0:T(128)}, u32[]{:S(2)}) copy-start(f32[20]{0:T(128)} %slope_ref.1) | copy-start | bytes 244
  25.6 0.7 %copy-start.7 = (f32[20]{0:T(128)S(1)}, f32[20]{0:T(128)}, u32[]{:S(2)}) copy-start(f32[20]{0:T(128)} %tau_ref.1) | copy-start | bytes 244
  26.3 4.0 %copy-start.4 = (f32[1,8192]{1,0:T(1,128)S(1)}, f32[1,8192]{1,0:T(1,128)}, u32[]{:S(2)}) copy-start(f32[1,8192]{1,0:T(1,128)} %param.18) | copy-start | bytes 98308

commit v15 on v12

--- a/solution.py
+++ b/solution.py
@@ -354,33 +354,38 @@
     where_ref[2:8] = jnp.zeros((6, nz), F32)
 
 
-def shift_left(v, amount, lane):
-    rows = v.shape[0]
-    if amount < LANES:
-        turned = pltpu.roll(v, LANES - amount, 1)
-        below = pltpu.roll(turned, rows - 1, 0)
-        return jnp.where(lane < LANES - amount, turned, below)
-    return jnp.concatenate([v[amount // LANES :], v[: amount // LANES]], axis=0)
-
-
-def plan_kernel(after_ref, label_ref, plan_ref):
-    rows = label_ref.shape[0]
-    lane = lanes_of((rows, LANES))
-    row = subs_of((rows, LANES))
-    heart = label_ref[...] == 1
-    ones = heart.astype(jnp.bfloat16)
-    upper = (subs_of((LANES, LANES)) < lanes_of((LANES, LANES))).astype(jnp.bfloat16)
-    in_row = jnp.dot(ones, upper, preferred_element_type=F32)
+def shift_up(v, amount):
+    if amount < SUB:
+        return pltpu.roll(v, v.shape[0] - amount, 0)
+    return jnp.concatenate([v[amount:], v[:amount]], axis=0)
+
+
+def plan_kernel(after_ref, label_ref, index_ref, plan_ref, lane_ref):
+    rows, slot_rows = label_ref.shape[0], index_ref.shape[0]
+    wide = -(-(slot_rows + 1) // LANES) * LANES
+    shape = (rows, LANES)
+    lane, row = lanes_of(shape), subs_of(shape)
+    ones = (label_ref[...] == 1).astype(jnp.bfloat16)
     totals = jnp.dot(ones, jnp.ones((LANES, LANES), jnp.bfloat16), preferred_element_type=F32)
     lower = (subs_of((rows, rows)) > lanes_of((rows, rows))).astype(jnp.bfloat16)
-    before = jnp.dot(lower, totals.astype(jnp.bfloat16), preferred_element_type=F32)
-    rank = (in_row + before).astype(jnp.int32)
-    way = jnp.where(heart, row * LANES + lane - rank, 0)
-    plan = jnp.zeros((rows, LANES), jnp.int32)
+    before = jnp.dot(lower, totals.astype(jnp.bfloat16), preferred_element_type=F32).astype(jnp.int32)
+    target, first = lax.div(before, LANES), lax.rem(before, LANES)
+    listed = jnp.concatenate(
+        [lax.rem(index_ref[...], LANES).astype(F32), jnp.zeros((wide - slot_rows, LANES), F32)], axis=0
+    ).astype(jnp.bfloat16)
+    spread = jnp.concatenate([target] * (wide // LANES), axis=1)
+    place = lanes_of((rows, wide))
+    here = jnp.dot((spread == place).astype(jnp.bfloat16), listed, preferred_element_type=F32)
+    after = jnp.dot((spread + 1 == place).astype(jnp.bfloat16), listed, preferred_element_type=F32)
+    lane_ref[...] = jnp.where(lane >= first, here, after).astype(jnp.int32)
+    wrapped = (lane < first).astype(jnp.int32)
+    filled = lane - first + LANES * wrapped < totals.astype(jnp.int32)
+    way = jnp.where(filled, row - target - wrapped, 0)
+    plan = jnp.zeros(shape, jnp.int32)
     step = 1
-    while step < rows * LANES:
+    while step < rows:
         moving = jnp.where((way & step) != 0, way, 0)
-        arriving = shift_left(moving, step, lane)
+        arriving = shift_up(moving, step)
         plan = plan | (arriving & step)
         way = (way - moving) | arriving
         step *= 2
@@ -407,7 +412,9 @@
     return c0, c1, c2
 
 
-def couple_kernel(stage, slot_rows, after_ref, inside_ref, edge_ref, slabs_ref, plan_ref, list_ref, value_ref):
+def couple_kernel(
+    stage, slot_rows, after_ref, inside_ref, edge_ref, slabs_ref, plan_ref, lane_ref, list_ref, value_ref
+):
     nx, nz = inside_ref.shape[0], inside_ref.shape[2]
     ny = inside_ref.shape[1] - 2 * SUB
     rows = nx * ny
@@ -430,12 +437,11 @@
                 along_z(v_mid, slab, PACK * x, gz) + beside + (v_low + v_high) - 6.0 * v_mid
             )
             v_low, v_mid = v_mid, v_high
-    lane = lanes_of((rows, LANES))
-    value = value_ref[...]
+    value = jnp.take_along_axis(value_ref[...], lane_ref[...], axis=1)
     plan = plan_ref[...]
     step = 1
-    while step < rows * LANES:
-        value = jnp.where((plan & step) != 0, shift_left(value, step, lane), value)
+    while step < rows:
+        value = jnp.where((plan & step) != 0, shift_up(value, step), value)
         step *= 2
     list_ref[...] = value[:slot_rows]
 
@@ -595,8 +601,9 @@
     )(in_hbm(potential_cot), in_hbm(damping), in_hbm(tissue_label))
 
     got = lax.ppermute(packed, "gz", [(0, 1), (1, 0)])
-    plan = call(plan_kernel, jax.ShapeDtypeStruct((rows, LANES), jnp.int32), 2, cost=6_000_000)(
-        stat, flat(tissue_label)
+    cells_shape = jax.ShapeDtypeStruct((rows, LANES), jnp.int32)
+    plan, lanes = call(plan_kernel, (cells_shape, cells_shape), 3, cost=6_000_000)(
+        stat, flat(tissue_label), heart_index.reshape(slot_rows, LANES)
     )
 
     n_y = steps_of("gy")
@@ -633,10 +640,10 @@
         return call(
             functools.partial(couple_kernel, stage, slot_rows),
             shape_of(slot_rows, LANES),
-            5,
+            6,
             scratch=[pltpu.VMEM((rows, LANES), F32)],
             cost=6_000_000,
-        )(after, inside, ends, slabs, plan)
+        )(after, inside, ends, slabs, plan, lanes)
 
     def add(value, axis, step, after):
         got = lax.ppermute(value, axis, [(i, i ^ step) for i in range(lax.axis_size(axis))])

time: 31 us -> 30.4 us (0.981)
  Pallas kernels: 11.8 us -> 9.99 us
  starting transfers between devices: 14.7 us -> 15.4 us
  waiting for transfers between devices: 2.87 us -> 3.36 us
    pallas_call x3, Pallas kernels: 3.56 us -> 1.99 us  [couple(): call(functools.partial(couple_kernel, stage, slot_rows), shape_of(slot_ro...]
    ppermute x2, waiting for transfers between devices: 0.01 us -> 0.9 us  [add(): lax.ppermute(value, axis, [(i, i ^ step) for i in range(lax.axis_size(axi...]
    ppermute x9, starting transfers between devices: 12.1 us -> 12.8 us  [swap(): return lax.ppermute(value, ('gx', 'gy', 'gz'), pairs)]
    ppermute x9, waiting for transfers between devices: 2.01 us -> 1.6 us  [swap(): return lax.ppermute(value, ('gx', 'gy', 'gz'), pairs)]
    unnamed x20 -> x22, local copies, waits for them, and re-layouts: 0.68 us -> 0.67 us
  transfers between devices with their start and end apart: 12 -> 12, of which waited for: 2 -> 4; matrix products, arithmetic and copies ran while one was open for 0% -> 0% of each run, Pallas kernels for 26% -> 21%
where the time goes in v15:
time: 30.4 us; the launch traced here: 30.3 us
  starting transfers between devices  15.4 us (51%)
  Pallas kernels  9.99 us (33%)
  waiting for transfers between devices  3.36 us (11%)
  between operations  0.81 us (3%)
  local copies, waits for them, and re-layouts  0.67 us (2%)
    ppermute x9, starting transfers between devices, swap(): return lax.ppermute(value, ('gx', 'gy', 'gz'), pairs)  12.8 us
    ppermute x2, starting transfers between devices, add(): lax.ppermute(value, axis, [(i, i ^ step) for i in range(lax.axis_size(axi...  2.06 us
    pallas_call x3, Pallas kernels, couple(): call(functools.partial(couple_kernel, stage, slot_rows), shape_of(slot_ro...  1.99 us
    pallas_call x1, Pallas kernels, local(): call(membrane_kernel, (shape_of(n_states, block_rows, LANES), shape_of(bl...  1.93 us
    ppermute x9, waiting for transfers between devices, swap(): return lax.ppermute(value, ('gx', 'gy', 'gz'), pairs)  1.6 us
    pallas_call x1, Pallas kernels, local(): call(plan_kernel, (cells_shape, cells_shape), 3, cost=6000000)  1.51 us
    pallas_call x1, Pallas kernels, local(): call(start_kernel, (block, block, shape_of(2, ny, nz), shape_of(2, SUB, n...  1.4 us
    pallas_call x1, Pallas kernels, local(): call(functools.partial(finish_kernel, alone), (block, shape_of(block_rows...  1.18 us
  transfers between devices with their start and end apart: 12, of which 4 were waited for; matrix products, arithmetic and copies ran while one was open for 0% of the time, Pallas kernels for 21%

profile of v15, /device:TPU:0, one launch (start us, length us, event | category | flops | bytes accessed | tf_op | source)
XLA Modules:
  0.0 30.3 jit_solution(11174153875877277299)
XLA Ops:
  0.6 1.4 %shard_map.148 = (f32[16,32,128]{2,1,0:T(8,128)S(1)}, f32[16,32,128]{2,1,0:T(8,128)S(1)}, f32[2,32,128]{2,1,0:T(8,128)S(1)}, f32[2,8,128]{2,1,0:T(8,128)S(1)}) custom-call(f32[16,32,128]{2,1,0:T(8,128)} %right_hbm.1, f32[16,32,128]{2,1,0:T(8,128)} %damping_hbm.1, s32[16,32,128]{2,1,0:T(8,128)} %label_hbm.1), custom_call_target="tpu_custom_call" | custom-call | flops 2000000 | bytes 2000000 | tf_op jit(solution)/shard_map/pallas_call | solution.py:594
  2.0 0.5 %collective-permute-start = (f32[2,32,128]{2,1,0:T(8,128)S(1)}, f32[2,32,128]{2,1,0:T(8,128)S(1)}, u32[]{:S(2)}, u32[]{:S(2)}) collective-permute-start(f32[2,32,128]{2,1,0:T(8,128)S(1)} %get-tuple-element.42.own_ref), channel_id=1, source_target_pairs={{0,1},{1,0},{2,3},{3,2},{4,5},{5,4},{6,7},{7,6},{8,9},{9,8},{10,11... | collective-permute-start | bytes 98312 | tf_op jit(solution)/shard_map/ppermute | solution.py:603
  2.6 0.9 %collective-permute-done.got_ref = f32[2,32,128]{2,1,0:T(8,128)S(1)} collective-permute-done((f32[2,32,128]{2,1,0:T(8,128)S(1)}, f32[2,32,128]{2,1,0:T(8,128)S(1)}, u32[]{:S(2)}, u32[]{:S(2)}) %collective-permute-start) | collective-permute-done | bytes 32800 | tf_op jit(solution)/shard_map/ppermute | solution.py:603
  3.5 3.0 %collective-permute-start.2 = (f32[6,32,128]{2,1,0:T(8,128)S(1)}, f32[6,32,128]{2,1,0:T(8,128)S(1)}, u32[]{:S(2)}, u32[]{:S(2)}) collective-permute-start(f32[6,32,128]{2,1,0:T(8,128)S(1)} %get-tuple-element.51), channel_id=1, source_target_pairs={{0,4},{1,5},{2,6},{3,7},{4,0},{5,1},{6,2},{7,3},{8,12},{9,13},{10,... | collective-permute-start | bytes 294920 | tf_op jit(solution)/shard_map/ppermute | solution.py:568
  6.5 1.5 %collective-permute-start.1 = (f32[17,8,128]{2,1,0:T(8,128)S(1)}, f32[17,8,128]{2,1,0:T(8,128)S(1)}, u32[]{:S(2)}, u32[]{:S(2)}) collective-permute-start(f32[17,8,128]{2,1,0:T(8,128)S(1)} %get-tuple-element.44), channel_id=1, source_target_pairs={{0,2},{1,3},{2,0},{3,1},{4,6},{5,7},{6,4},{7,5},{8,10},{9,11},{10,... | collective-permute-start | bytes 208904 | tf_op jit(solution)/shard_map/ppermute | solution.py:568
  8.0 3.1 %collective-permute-start.4 = (f32[4,8,128]{2,1,0:T(8,128)S(1)}, f32[4,8,128]{2,1,0:T(8,128)S(1)}, u32[]{:S(2)}, u32[]{:S(2)}) collective-permute-start(f32[4,8,128]{2,1,0:T(8,128)S(1)} %get-tuple-element.53), channel_id=1, source_target_pairs={{0,6},{1,7},{2,4},{3,5},{4,2},{5,3},{6,0},{7,1},{8,14},{9,15},{10,... | collective-permute-start | bytes 49160 | tf_op jit(solution)/shard_map/ppermute | solution.py:568
  11.1 1.5 %shard_map.149 = (s32[512,128]{1,0:T(8,128)S(1)}, s32[512,128]{1,0:T(8,128)S(1)}) custom-call(f32[2,8,128]{2,1,0:T(8,128)S(1)} %get-tuple-element.38.after_ref.stat_ref, s32[512,128]{1,0:T(8,128)S(1)} %bitcast.8, s32[160,128]{1,0:T(8,128)S(1)} %bitcast.13), custom_call_target="tpu_custom_call" | custom-call | flops 6000000 | bytes 6000000 | tf_op jit(solution)/shard_map/pallas_call | solution.py:605
  12.6 0.9 %shard_map.151 = (f32[16,48,128]{2,1,0:T(8,128)S(1)}, f32[16,48,128]{2,1,0:T(8,128)S(1)}, f32[16,48,128]{2,1,0:T(8,128)S(1)}, f32[16,48,128]{2,1,0:T(8,128)S(1)}...) custom-call(f32[16,32,128]{2,1,0:T(8,128)S(1)} %get-tuple-element.40.w0_ref, ...), custom_call_target="tpu_custom_call" | custom-call | flops 6000000 | bytes 6000000 | tf_op jit(solution)/shard_map/pallas_call | solution.py:625
  13.6 0.7 %shard_map.152 = (f32[6,48,128]{2,1,0:T(8,128)S(1)}, f32[6,48,128]{2,1,0:T(8,128)S(1)}, f32[6,48,128]{2,1,0:T(8,128)S(1)}, f32[3,48,256]{2,1,0:T(8,128)S(1)}, f3...) custom-call(s32[512,128]{1,0:T(8,128)S(1)} %get-tuple-element.39.after_ref.plan_ref, ...), custom_call_target="tpu_custom_call" | custom-call | flops 2000000 | bytes 2000000 | tf_op jit(solution)/shard_map/pallas_call | solution.py:632
  14.3 0.6 %collective-permute-start.6 = (f32[8,128]{1,0:T(8,128)S(1)}, f32[8,128]{1,0:T(8,128)S(1)}, u32[]{:S(2)}, u32[]{:S(2)}) collective-permute-start(f32[8,128]{1,0:T(8,128)S(1)} %get-tuple-element.56.after_ref.a_ref), channel_id=1, source_target_pairs={{0,1},{1,0},{2,3},{3,2},{4,5},{5,4},{6,7},{7,6},{8,9},{9,8},{10,11... | collective-permute-start | bytes 12296 | tf_op jit(solution)/shard_map/ppermute | solution.py:649
  14.9 0.7 %shard_map.153.after_ref.refs_0_ = f32[160,128]{1,0:T(8,128)S(1)} custom-call(f32[8,128]{1,0:T(8,128)S(1)} %get-tuple-element.56.after_ref.a_ref, f32[16,48,128]{2,1,0:T(8,128)S(1)} %get-tuple-element.45.a_ref.inside_ref, f32[6,48,128]{2,1,0:T(8,128)S(1)} %get-tuple-element.57.edge_ref, f32[3,48,256]{2,1,0:T(8,128)S(1)} %get-tuple-element.58.slabs_ref, ...), custom_call_target="tpu_custom_call" | custom-call | flops 6000000 | bytes 6000000 | tf_op jit(solution)/shard_map/pallas_call | solution.py:640
  15.5 0.1 collective-permute-done.6.b_ref
  15.7 1.5 %collective-permute-start.7 = (f32[8,128]{1,0:T(8,128)S(1)}, f32[8,128]{1,0:T(8,128)S(1)}, u32[]{:S(2)}, u32[]{:S(2)}) collective-permute-start(f32[8,128]{1,0:T(8,128)S(1)} %shard_map.154.after_ref.a_ref), channel_id=1, source_target_pairs={{0,2},{2,0},{1,3},{3,1},{4,6},{6,4},{5,7},{7,5},{8,10},{10,8},{9,1... | collective-permute-start | bytes 12296 | tf_op jit(solution)/shard_map/ppermute | solution.py:649
  17.2 0.7 %shard_map.155.after_ref.refs_1_ = f32[160,128]{1,0:T(8,128)S(1)} custom-call(f32[8,128]{1,0:T(8,128)S(1)} %shard_map.154.after_ref.a_ref, f32[16,48,128]{2,1,0:T(8,128)S(1)} %get-tuple-element.47.b_ref.inside_ref, f32[6,48,128]{2,1,0:T(8,128)S(1)} %get-tuple-element.60.edge_ref.eb_ref, f32[3,48,256]{2,1,0:T(8,128)S(1)} %get-tuple-element.58.slabs_ref, ...), custom_call_target="tpu_custom_call" | custom-call | flops 6000000 | bytes 6000000 | tf_op jit(solution)/shard_map/pallas_call | solution.py:640
  17.9 0.7 %shard_map.156.after_ref.refs_2_ = f32[160,128]{1,0:T(8,128)S(1)} custom-call(f32[160,128]{1,0:T(8,128)S(1)} %shard_map.155.after_ref.refs_1_, f32[16,48,128]{2,1,0:T(8,128)S(1)} %get-tuple-element.48.c_ref.inside_ref, f32[6,48,128]{2,1,0:T(8,128)S(1)} %get-tuple-element.61.edge_ref.ec_ref, f32[3,48,256]{2,1,0:T(8,128)S(1)} %get-tuple-element.58.slabs_ref, ...), custom_call_target="tpu_custom_call" | custom-call | flops 6000000 | bytes 6000000 | tf_op jit(solution)/shard_map/pallas_call | solution.py:640
  18.5 0.7 %collective-permute-done.7.b_ref = f32[8,128]{1,0:T(8,128)S(1)} collective-permute-done((f32[8,128]{1,0:T(8,128)S(1)}, f32[8,128]{1,0:T(8,128)S(1)}, u32[]{:S(2)}, u32[]{:S(2)}) %collective-permute-start.7) | collective-permute-done | bytes 4128 | tf_op jit(solution)/shard_map/ppermute | solution.py:649
  19.3 0.3 shard_map.158
  19.6 1.9 %collective-permute-start.9 = (f32[200,128]{1,0:T(8,128)S(1)}, f32[200,128]{1,0:T(8,128)S(1)}, u32[]{:S(2)}, u32[]{:S(2)}) collective-permute-start(f32[200,128]{1,0:T(8,128)S(1)} %get-tuple-element.67), channel_id=1, source_target_pairs={{0,8},{1,9},{2,10},{3,11},{4,12},{5,13},{6,14},{7,15},{8,0},{9,1},... | collective-permute-start | bytes 307208 | tf_op jit(solution)/shard_map/ppermute | solution.py:568
  21.5 1.6 %collective-permute-start.11 = (f32[200,128]{1,0:T(8,128)S(1)}, f32[200,128]{1,0:T(8,128)S(1)}, u32[]{:S(2)}, u32[]{:S(2)}) collective-permute-start(f32[200,128]{1,0:T(8,128)S(1)} %get-tuple-element.69), channel_id=1, source_target_pairs={{0,4},{1,5},{2,6},{3,7},{4,0},{5,1},{6,2},{7,3},{8,12},{9,13},{10,... | collective-permute-start | bytes 307208 | tf_op jit(solution)/shard_map/ppermute | solution.py:568
  23.2 1.7 %collective-permute-start.8 = (f32[8,128]{1,0:T(8,128)S(1)}, f32[8,128]{1,0:T(8,128)S(1)}, u32[]{:S(2)}, u32[]{:S(2)}) collective-permute-start(f32[8,128]{1,0:T(8,128)S(1)} %shard_map.157.total_ref), channel_id=1, source_target_pairs={{0,12},{1,13},{2,14},{3,15},{4,5},{5,4},{6,7},{7,6},{8,9},{9,8},{1... | collective-permute-start | bytes 12296 | tf_op jit(solution)/shard_map/ppermute | solution.py:568
  24.9 0.6 %copy-done.6 = f32[20]{0:T(128)S(1)} copy-done((f32[20]{0:T(128)S(1)}, f32[20]{0:T(128)}, u32[]{:S(2)}) %copy-start.6) | copy-done | bytes 104
  25.5 1.9 %shard_map.159 = (f32[20,64,128]{2,1,0:T(8,128)S(1)}, f32[64,128]{1,0:T(8,128)S(1)}, f32[64,128]{1,0:T(8,128)S(1)}, f32[2,20,128]{2,1,0:T(8,128)S(1)}) custom-call(f32[20]{0:T(128)S(1)} %copy-done.6, f32[20]{0:T(128)S(1)} %copy-done.7, f32[20]{0:T(128)S(1)} %copy-done.8, f32[20]{0:T(128)S(1)} %copy-done.9, f32[20]{0:T(128)S(1)} %copy-done.10, ...), custom_call_target="tpu_custom_call" | custom-call | flops 6000000 | bytes 6000000 | tf_op jit(solution)/shard_map/pallas_call | solution.py:678
  27.5 1.6 %collective-permute-done.8.refs_1_ = f32[8,128]{1,0:T(8,128)S(1)} collective-permute-done((f32[8,128]{1,0:T(8,128)S(1)}, f32[8,128]{1,0:T(8,128)S(1)}, u32[]{:S(2)}, u32[]{:S(2)}) %collective-permute-start.8) | collective-permute-done | bytes 4128 | tf_op jit(solution)/shard_map/ppermute | solution.py:568
  29.1 1.2 %shard_map.160 = (f32[16,32,128]{2,1,0:T(8,128)}, f32[64,128]{1,0:T(8,128)}, f32[20,64,128]{2,1,0:T(8,128)}) custom-call(f32[2,20,128]{2,1,0:T(8,128)S(1)} %get-tuple-element.63.coef_ref, f32[64,128]{1,0:T(8,128)S(1)} %bitcast.14, f32[64,128]{1,0:T(8,128)S(1)} %bitcast.12, f32[64,128]{1,0:T(8,128)S(1)} %get-tuple-element.64.sum_ref, ...), custom_call_target="tpu_custom_call" | custom-call | flops 2000000 | bytes 2000000 | tf_op jit(solution)/shard_map/pallas_call | solution.py:691
  (35 shorter events, 0.2 us)
Async XLA Ops:
  2.0 1.4 %collective-permute-start = (f32[2,32,128]{2,1,0:T(8,128)S(1)}, f32[2,32,128]{2,1,0:T(8,128)S(1)}, u32[]{:S(2)}, u32[]{:S(2)}) collective-permute-start(f32[2,32,128]{2,1,0:T(8,128)S(1)} %get-tuple-element.42.own_ref), channel_id=1, source_target_pairs={{0,1},{1,0},{2,3},{3,2},{4,5},{5,4},{6,7},{7,6},{8,9},{9,8},{10,11... | collective-permute-start | bytes 98312 | tf_op jit(solution)/shard_map/ppermute | solution.py:603
  3.4 7.7 %copy-start = (s32[16,32,128]{2,1,0:T(8,128)S(1)}, s32[16,32,128]{2,1,0:T(8,128)}, u32[]{:S(2)}) copy-start(s32[16,32,128]{2,1,0:T(8,128)} %label_hbm.1) | copy-start | bytes 786436
  3.4 7.7 %copy-start.4 = (s32[1,1,1,20480]{3,2,1,0:T(1,128)S(1)}, s32[1,1,1,20480]{3,2,1,0:T(1,128)}, u32[]{:S(2)}) copy-start(s32[1,1,1,20480]{3,2,1,0:T(1,128)} %param.16) | copy-start | bytes 245764
  3.5 10.1 %collective-permute-start.2 = (f32[6,32,128]{2,1,0:T(8,128)S(1)}, f32[6,32,128]{2,1,0:T(8,128)S(1)}, u32[]{:S(2)}, u32[]{:S(2)}) collective-permute-start(f32[6,32,128]{2,1,0:T(8,128)S(1)} %get-tuple-element.51), channel_id=1, source_target_pairs={{0,4},{1,5},{2,6},{3,7},{4,0},{5,1},{6,2},{7,3},{8,12},{9,13},{10,... | collective-permute-start | bytes 294920 | tf_op jit(solution)/shard_map/ppermute | solution.py:568
  6.5 7.1 %collective-permute-start.3 = (f32[6,32,128]{2,1,0:T(8,128)S(1)}, f32[6,32,128]{2,1,0:T(8,128)S(1)}, u32[]{:S(2)}, u32[]{:S(2)}) collective-permute-start(f32[6,32,128]{2,1,0:T(8,128)S(1)} %get-tuple-element.52), channel_id=1, source_target_pairs={{0,1},{1,0},{2,3},{3,2},{4,8},{5,9},{6,10},{7,11},{8,4},{9,5},{10,... | collective-permute-start | bytes 294920 | tf_op jit(solution)/shard_map/ppermute | solution.py:568
  6.5 6.1 %collective-permute-start.1 = (f32[17,8,128]{2,1,0:T(8,128)S(1)}, f32[17,8,128]{2,1,0:T(8,128)S(1)}, u32[]{:S(2)}, u32[]{:S(2)}) collective-permute-start(f32[17,8,128]{2,1,0:T(8,128)S(1)} %get-tuple-element.44), channel_id=1, source_target_pairs={{0,2},{1,3},{2,0},{3,1},{4,6},{5,7},{6,4},{7,5},{8,10},{9,11},{10,... | collective-permute-start | bytes 208904 | tf_op jit(solution)/shard_map/ppermute | solution.py:568
  8.0 5.6 %collective-permute-start.4 = (f32[4,8,128]{2,1,0:T(8,128)S(1)}, f32[4,8,128]{2,1,0:T(8,128)S(1)}, u32[]{:S(2)}, u32[]{:S(2)}) collective-permute-start(f32[4,8,128]{2,1,0:T(8,128)S(1)} %get-tuple-element.53), channel_id=1, source_target_pairs={{0,6},{1,7},{2,4},{3,5},{4,2},{5,3},{6,0},{7,1},{8,14},{9,15},{10,... | collective-permute-start | bytes 49160 | tf_op jit(solution)/shard_map/ppermute | solution.py:568
  11.1 2.5 %collective-permute-start.5 = (f32[4,8,128]{2,1,0:T(8,128)S(1)}, f32[4,8,128]{2,1,0:T(8,128)S(1)}, u32[]{:S(2)}, u32[]{:S(2)}) collective-permute-start(f32[4,8,128]{2,1,0:T(8,128)S(1)} %get-tuple-element.54), channel_id=1, source_target_pairs={{0,1},{1,0},{2,3},{3,2},{4,10},{5,11},{6,8},{7,9},{8,6},{9,7},{10,... | collective-permute-start | bytes 49160 | tf_op jit(solution)/shard_map/ppermute | solution.py:568
  14.3 1.4 %collective-permute-start.6 = (f32[8,128]{1,0:T(8,128)S(1)}, f32[8,128]{1,0:T(8,128)S(1)}, u32[]{:S(2)}, u32[]{:S(2)}) collective-permute-start(f32[8,128]{1,0:T(8,128)S(1)} %get-tuple-element.56.after_ref.a_ref), channel_id=1, source_target_pairs={{0,1},{1,0},{2,3},{3,2},{4,5},{5,4},{6,7},{7,6},{8,9},{9,8},{10,11... | collective-permute-start | bytes 12296 | tf_op jit(solution)/shard_map/ppermute | solution.py:649
  15.7 3.6 %collective-permute-start.7 = (f32[8,128]{1,0:T(8,128)S(1)}, f32[8,128]{1,0:T(8,128)S(1)}, u32[]{:S(2)}, u32[]{:S(2)}) collective-permute-start(f32[8,128]{1,0:T(8,128)S(1)} %shard_map.154.after_ref.a_ref), channel_id=1, source_target_pairs={{0,2},{2,0},{1,3},{3,1},{4,6},{6,4},{5,7},{7,5},{8,10},{10,8},{9,1... | collective-permute-start | bytes 12296 | tf_op jit(solution)/shard_map/ppermute | solution.py:649
  17.9 7.0 %copy-start.1 = (f32[20,1,8192]{2,1,0:T(1,128)S(1)}, f32[20,1,8192]{2,1,0:T(1,128)}, u32[]{:S(2)}) copy-start(f32[20,1,8192]{2,1,0:T(1,128)} %param.18) | copy-start | bytes 1966084
  17.9 7.0 %copy-start.2 = (f32[20,1,8192]{2,1,0:T(1,128)S(1)}, f32[20,1,8192]{2,1,0:T(1,128)}, u32[]{:S(2)}) copy-start(f32[20,1,8192]{2,1,0:T(1,128)} %param.20) | copy-start | bytes 1966084
  19.3 5.6 %copy-start.3 = (f32[1,8192]{1,0:T(1,128)S(1)}, f32[1,8192]{1,0:T(1,128)}, u32[]{:S(2)}) copy-start(f32[1,8192]{1,0:T(1,128)} %param.17) | copy-start | bytes 98308
  19.3 5.6 %copy-start.9 = (f32[20]{0:T(128)S(1)}, f32[20]{0:T(128)}, u32[]{:S(2)}) copy-start(f32[20]{0:T(128)} %cond_ref.1) | copy-start | bytes 244
  19.3 5.6 %copy-start.10 = (f32[20]{0:T(128)S(1)}, f32[20]{0:T(128)}, u32[]{:S(2)}) copy-start(f32[20]{0:T(128)} %rev_ref.1) | copy-start | bytes 244
  19.6 9.4 %collective-permute-start.9 = (f32[200,128]{1,0:T(8,128)S(1)}, f32[200,128]{1,0:T(8,128)S(1)}, u32[]{:S(2)}, u32[]{:S(2)}) collective-permute-start(f32[200,128]{1,0:T(8,128)S(1)} %get-tuple-element.67), channel_id=1, source_target_pairs={{0,8},{1,9},{2,10},{3,11},{4,12},{5,13},{6,14},{7,15},{8,0},{9,1},... | collective-permute-start | bytes 307208 | tf_op jit(solution)/shard_map/ppermute | solution.py:568
  21.5 7.5 %collective-permute-start.10 = (f32[200,128]{1,0:T(8,128)S(1)}, f32[200,128]{1,0:T(8,128)S(1)}, u32[]{:S(2)}, u32[]{:S(2)}) collective-permute-start(f32[200,128]{1,0:T(8,128)S(1)} %get-tuple-element.68), channel_id=1, source_target_pairs={{0,1},{1,0},{2,3},{3,2},{4,8},{5,9},{6,10},{7,11},{8,4},{9,5},{10,... | collective-permute-start | bytes 307208 | tf_op jit(solution)/shard_map/ppermute | solution.py:568
  21.5 7.5 %collective-permute-start.11 = (f32[200,128]{1,0:T(8,128)S(1)}, f32[200,128]{1,0:T(8,128)S(1)}, u32[]{:S(2)}, u32[]{:S(2)}) collective-permute-start(f32[200,128]{1,0:T(8,128)S(1)} %get-tuple-element.69), channel_id=1, source_target_pairs={{0,4},{1,5},{2,6},{3,7},{4,0},{5,1},{6,2},{7,3},{8,12},{9,13},{10,... | collective-permute-start | bytes 307208 | tf_op jit(solution)/shard_map/ppermute | solution.py:568
  23.2 5.9 %collective-permute-start.8 = (f32[8,128]{1,0:T(8,128)S(1)}, f32[8,128]{1,0:T(8,128)S(1)}, u32[]{:S(2)}, u32[]{:S(2)}) collective-permute-start(f32[8,128]{1,0:T(8,128)S(1)} %shard_map.157.total_ref), channel_id=1, source_target_pairs={{0,12},{1,13},{2,14},{3,15},{4,5},{5,4},{6,7},{7,6},{8,9},{9,8},{1... | collective-permute-start | bytes 12296 | tf_op jit(solution)/shard_map/ppermute | solution.py:568
  24.9 0.7 %copy-start.6 = (f32[20]{0:T(128)S(1)}, f32[20]{0:T(128)}, u32[]{:S(2)}) copy-start(f32[20]{0:T(128)} %half_ref.1) | copy-start | bytes 244
  24.9 0.7 %copy-start.7 = (f32[20]{0:T(128)S(1)}, f32[20]{0:T(128)}, u32[]{:S(2)}) copy-start(f32[20]{0:T(128)} %slope_ref.1) | copy-start | bytes 244
  24.9 0.7 %copy-start.8 = (f32[20]{0:T(128)S(1)}, f32[20]{0:T(128)}, u32[]{:S(2)}) copy-start(f32[20]{0:T(128)} %tau_ref.1) | copy-start | bytes 244
  25.5 3.5 %copy-start.5 = (f32[1,8192]{1,0:T(1,128)S(1)}, f32[1,8192]{1,0:T(1,128)}, u32[]{:S(2)}) copy-start(f32[1,8192]{1,0:T(1,128)} %param.19) | copy-start | bytes 98308

commit v16 on v15

--- a/solution.py
+++ b/solution.py
@@ -413,7 +413,8 @@
 
 
 def couple_kernel(
-    stage, slot_rows, after_ref, inside_ref, edge_ref, slabs_ref, plan_ref, lane_ref, list_ref, value_ref
+    stage, slot_rows, after_ref, where_ref, inside_ref, edge_ref, slabs_ref, plan_ref, lane_ref, blocks_ref,
+    value_ref, buf_ref,
 ):
     nx, nz = inside_ref.shape[0], inside_ref.shape[2]
     ny = inside_ref.shape[1] - 2 * SUB
@@ -443,34 +444,34 @@
     while step < rows:
         value = jnp.where((plan & step) != 0, shift_up(value, step), value)
         step *= 2
-    list_ref[...] = value[:slot_rows]
-
-
-def add_kernel(a_ref, b_ref, after_ref, out_ref):
-    out_ref[...] = a_ref[...] + b_ref[...]
-
-
-def place_kernel(where_ref, total_ref, *refs):
-    list_refs, out_refs, buf_ref = refs[:3], refs[3:-1], refs[-1]
-    slot_rows = list_refs[0].shape[0]
-    size = (out_refs[0].shape[0] - SUB) // 3
-    gx = lax.axis_index("gx")
     offset = jnp.max(where_ref[0:1]).astype(jnp.int32)
     count = jnp.max(where_ref[1:2]).astype(jnp.int32)
     shape = (slot_rows, LANES)
-    listed = subs_of(shape) * LANES + lanes_of(shape) < count
+    slots = jnp.where(subs_of(shape) * LANES + lanes_of(shape) < count, value[:slot_rows], 0.0)
+    slots = jnp.concatenate([slots, jnp.zeros((SUB, LANES), F32)], axis=0)
     inner = lax.rem(offset, LANES)
-    kept = lanes_of((slot_rows + SUB, LANES)) >= inner
+    turned = pltpu.roll(slots, inner, 1)
+    moved = jnp.where(lanes_of((slot_rows + SUB, LANES)) >= inner, turned, pltpu.roll(turned, 1, 0))
     buf_ref[...] = jnp.zeros_like(buf_ref)
-    for k, list_ref in enumerate(list_refs):
-        slots = jnp.where(listed, list_ref[...], 0.0)
-        slots = jnp.concatenate([slots, jnp.zeros((SUB, LANES), F32)], axis=0)
-        turned = pltpu.roll(slots, inner, 1)
-        buf_ref[k, pl.ds(offset // LANES, slot_rows + SUB), :] = jnp.where(kept, turned, pltpu.roll(turned, 1, 0))
+    buf_ref[pl.ds(offset // LANES, slot_rows + SUB), :] = moved
+    gx = lax.axis_index("gx")
+    n_gx = lax.axis_size("gx")
+    size = blocks_ref.shape[0] // n_gx
+    for block in range(n_gx):
+        begin = pl.multiple_of((gx ^ block) * size, SUB)
+        blocks_ref[block * size : block * size + size] = buf_ref[pl.ds(begin, size), :]
+
+
+def add_kernel(a_ref, b_ref, after_ref, out_ref):
+    out_ref[...] = a_ref[...] + b_ref[...]
+
+
+def pack_kernel(total_ref, *refs):
+    list_refs, out_refs = refs[:3], refs[3:]
+    size = (out_refs[0].shape[0] - SUB) // 3
     for block, out_ref in enumerate(out_refs):
-        begin = pl.multiple_of((gx ^ block) * size, SUB)
-        for k in range(3):
-            out_ref[k * size : k * size + size] = buf_ref[k, pl.ds(begin, size), :]
+        for k, list_ref in enumerate(list_refs):
+            out_ref[k * size : k * size + size] = list_ref[block * size : block * size + size]
         out_ref[3 * size :] = total_ref[...]
 
 
@@ -511,7 +512,7 @@
 ):
     n_small, n_large = len(alone[0]), len(alone[1])
     own_ref, small_refs, large_refs = refs[0], refs[1 : 1 + n_small], refs[1 + n_small : 1 + n_small + n_large]
-    x_ref, volt_ref, gate_ref = refs[1 + n_small + n_large :]
+    x_hbm, volt_ref, gate_hbm, x_ref, gate_ref, sems = refs[1 + n_small + n_large :]
     size = (own_ref.shape[0] - SUB) // 3
     gx = lax.axis_index("gx")
 
@@ -529,6 +530,14 @@
         total = total + jnp.where(is_one(flags), 0.0, ref[3 * size :])
     sums = jnp.sum(total, axis=1, keepdims=True)
     c0, c1, c2 = galerkin([jnp.broadcast_to(sums[k : k + 1], (1, LANES)) for k in range(6)])
+    nx, ny, nz = x_ref.shape
+    own = slice(SUB, SUB + ny)
+    for x in range(nx):
+        w1 = b_ref[x, own] if 1 <= x < nx - 1 else eb_ref[2 if x == 0 else 3, own]
+        w2 = c_ref[x, own] if 2 <= x < nx - 2 else ec_ref[x + 1 if x < 2 else x - (nx - 2) + 3, own]
+        x_ref[x] = c0 * a_ref[x, own] + c1 * w1 + c2 * w2
+    copies = [pltpu.make_async_copy(x_ref, x_hbm, sems.at[0])]
+    copies[0].start()
     landed = jnp.zeros((size, LANES), F32)
     for k, c in enumerate((c0, c1, c2)):
         part = own_ref[k * size : k * size + size]
@@ -538,14 +547,16 @@
     cot = vcot_ref[...] + landed
     v = v_ref[...]
     volt_ref[...] = cot * factor_ref[...] + sum_ref[...]
-    for g in range(base_ref.shape[0]):
-        gate_ref[g] = base_ref[g] - (coef_ref[0, g : g + 1] * cot) * (v - coef_ref[1, g : g + 1])
-    nx, ny, nz = x_ref.shape
-    own = slice(SUB, SUB + ny)
-    for x in range(nx):
-        w1 = b_ref[x, own] if 1 <= x < nx - 1 else eb_ref[2 if x == 0 else 3, own]
-        w2 = c_ref[x, own] if 2 <= x < nx - 2 else ec_ref[x + 1 if x < 2 else x - (nx - 2) + 3, own]
-        x_ref[x] = c0 * a_ref[x, own] + c1 * w1 + c2 * w2
+    n_states = base_ref.shape[0]
+    half = n_states // 2
+    for part, (begin, end) in enumerate(((0, half), (half, n_states))):
+        for g in range(begin, end):
+            gate_ref[g] = base_ref[g] - (coef_ref[0, g : g + 1] * cot) * (v - coef_ref[1, g : g + 1])
+        here = pl.ds(begin, end - begin)
+        copies.append(pltpu.make_async_copy(gate_ref.at[here], gate_hbm.at[here], sems.at[1 + part]))
+        copies[-1].start()
+    for copy in copies:
+        copy.wait()
 
 
 def partners(axis, step):
@@ -636,14 +647,21 @@
         scratch=[pltpu.VMEM((4, tall, nz), F32), pltpu.VMEM((1, tall, 2 * nz), F32)],
     )(plan, in0, in_inv, in1, in2, own_slab, in_sums, stat, *along_x, *across)
 
+    if n_gx > 4:
+        counts = lax.all_gather(jnp.sum(stat[1, 0]), "gx")
+        begin = jnp.sum(jnp.where(jnp.arange(n_gx) < lax.axis_index("gx"), counts, 0.0))
+        where = where.at[0].set(begin)
+
     def couple(stage, after, inside, ends):
         return call(
             functools.partial(couple_kernel, stage, slot_rows),
-            shape_of(slot_rows, LANES),
-            6,
-            scratch=[pltpu.VMEM((rows, LANES), F32)],
+            shape_of(n_gx * block_rows, LANES),
+            7,
+            scratch=[
+                pltpu.VMEM((rows, LANES), F32), pltpu.VMEM((n_gx * block_rows + slot_rows + SUB, LANES), F32),
+            ],
             cost=6_000_000,
-        )(after, inside, ends, slabs, plan, lanes)
+        )(after, where, inside, ends, slabs, plan, lanes)
 
     def add(value, axis, step, after):
         got = lax.ppermute(value, axis, [(i, i ^ step) for i in range(lax.axis_size(axis))])
@@ -655,16 +673,7 @@
     list2 = couple(2, list1, in2, ends2)
     for step in [2**k for k in range(n_gy.bit_length() - 1)]:
         sums = add(sums, "gy", step, list2)
-    if n_gx > 4:
-        counts = lax.all_gather(jnp.sum(stat[1, 0]), "gx")
-        begin = jnp.sum(jnp.where(jnp.arange(n_gx) < lax.axis_index("gx"), counts, 0.0))
-        where = where.at[0].set(begin)
-    blocks = call(
-        place_kernel,
-        (shape_of(3 * block_rows + SUB, LANES),) * n_gx,
-        5,
-        scratch=[pltpu.VMEM((3, n_gx * block_rows + slot_rows + SUB, LANES), F32)],
-    )(where, sums, list0, list1, list2)
+    blocks = call(pack_kernel, (shape_of(3 * block_rows + SUB, LANES),) * n_gx, 4)(sums, list0, list1, list2)
     apart = {k: never_meet(n_gx, k, slot_rows, block_rows) for k in range(1, n_gx)}
     small, meets = [], []
     for k in range(1, n_gx):
@@ -692,6 +701,11 @@
         functools.partial(finish_kernel, alone),
         (block, shape_of(block_rows, LANES), shape_of(n_states, block_rows, LANES)),
         12 + len(small) + len(large),
+        outs=(HBM, VMEM, HBM),
+        scratch=[
+            pltpu.VMEM((nx, ny, nz), F32), pltpu.VMEM((n_states, block_rows, LANES), F32),
+            pltpu.SemaphoreType.DMA((3,)),
+        ],
     )(
         state_coefs, cells(voltage_cot), cells(voltage), total_change, factor, base,
         in0, in1, in2, ends1, ends2, blocks[0], *small, *large,

time: 30.4 us -> 30.7 us (level)
  Pallas kernels: 9.99 us -> 10.6 us
    pallas_call x1, Pallas kernels: 1.18 us -> 1.75 us  [local(): call(functools.partial(finish_kernel, alone), (block, shape_of(block_rows...]
  transfers between devices with their start and end apart: 12 -> 12, of which waited for: 4 -> 4; matrix products, arithmetic and copies ran while one was open for 0% -> 0% of each run, Pallas kernels for 21% -> 22%
where the time goes in v16:
time: 30.7 us; the launch traced here: 30.6 us
  starting transfers between devices  15.4 us (50%)
  Pallas kernels  10.6 us (35%)
  waiting for transfers between devices  3.1 us (10%)
  between operations  0.8 us (3%)
  local copies, waits for them, and re-layouts  0.67 us (2%)
    ppermute x9, starting transfers between devices, swap(): return lax.ppermute(value, ('gx', 'gy', 'gz'), pairs)  12.8 us
    pallas_call x3, Pallas kernels, couple(): call(functools.partial(couple_kernel, stage, slot_rows), shape_of(n_gx *...  2.25 us
    ppermute x2, starting transfers between devices, add(): lax.ppermute(value, axis, [(i, i ^ step) for i in range(lax.axis_size(axi...  2.07 us
    pallas_call x1, Pallas kernels, local(): call(membrane_kernel, (shape_of(n_states, block_rows, LANES), shape_of(bl...  1.93 us
    pallas_call x1, Pallas kernels, local(): call(functools.partial(finish_kernel, alone), (block, shape_of(block_rows...  1.75 us
    ppermute x9, waiting for transfers between devices, swap(): return lax.ppermute(value, ('gx', 'gy', 'gz'), pairs)  1.6 us
    pallas_call x1, Pallas kernels, local(): call(plan_kernel, (cells_shape, cells_shape), 3, cost=6000000)  1.51 us
    pallas_call x1, Pallas kernels, local(): call(start_kernel, (block, block, shape_of(2, ny, nz), shape_of(2, SUB, n...  1.4 us
  transfers between devices with their start and end apart: 12, of which 4 were waited for; matrix products, arithmetic and copies ran while one was open for 0% of the time, Pallas kernels for 22%

profile of v16, /device:TPU:0, one launch (start us, length us, event | category | flops | bytes accessed | tf_op | source)
XLA Modules:
  0.0 30.6 jit_solution(11567153188863860803)
XLA Ops:
  0.6 1.4 %shard_map.148 = (f32[16,32,128]{2,1,0:T(8,128)S(1)}, f32[16,32,128]{2,1,0:T(8,128)S(1)}, f32[2,32,128]{2,1,0:T(8,128)S(1)}, f32[2,8,128]{2,1,0:T(8,128)S(1)}) custom-call(f32[16,32,128]{2,1,0:T(8,128)} %right_hbm.1, f32[16,32,128]{2,1,0:T(8,128)} %damping_hbm.1, s32[16,32,128]{2,1,0:T(8,128)} %label_hbm.1), custom_call_target="tpu_custom_call" | custom-call | flops 2000000 | bytes 2000000 | tf_op jit(solution)/shard_map/pallas_call | solution.py:605
  2.0 0.5 %collective-permute-start = (f32[2,32,128]{2,1,0:T(8,128)S(1)}, f32[2,32,128]{2,1,0:T(8,128)S(1)}, u32[]{:S(2)}, u32[]{:S(2)}) collective-permute-start(f32[2,32,128]{2,1,0:T(8,128)S(1)} %get-tuple-element.42.own_ref), channel_id=1, source_target_pairs={{0,1},{1,0},{2,3},{3,2},{4,5},{5,4},{6,7},{7,6},{8,9},{9,8},{10,11... | collective-permute-start | bytes 98312 | tf_op jit(solution)/shard_map/ppermute | solution.py:614
  2.6 0.9 %collective-permute-done.got_ref = f32[2,32,128]{2,1,0:T(8,128)S(1)} collective-permute-done((f32[2,32,128]{2,1,0:T(8,128)S(1)}, f32[2,32,128]{2,1,0:T(8,128)S(1)}, u32[]{:S(2)}, u32[]{:S(2)}) %collective-permute-start) | collective-permute-done | bytes 32800 | tf_op jit(solution)/shard_map/ppermute | solution.py:614
  3.4 0.1 shard_map.150
  3.5 3.0 %collective-permute-start.2 = (f32[6,32,128]{2,1,0:T(8,128)S(1)}, f32[6,32,128]{2,1,0:T(8,128)S(1)}, u32[]{:S(2)}, u32[]{:S(2)}) collective-permute-start(f32[6,32,128]{2,1,0:T(8,128)S(1)} %get-tuple-element.51), channel_id=1, source_target_pairs={{0,4},{1,5},{2,6},{3,7},{4,0},{5,1},{6,2},{7,3},{8,12},{9,13},{10,... | collective-permute-start | bytes 294920 | tf_op jit(solution)/shard_map/ppermute | solution.py:579
  6.5 1.5 %collective-permute-start.1 = (f32[17,8,128]{2,1,0:T(8,128)S(1)}, f32[17,8,128]{2,1,0:T(8,128)S(1)}, u32[]{:S(2)}, u32[]{:S(2)}) collective-permute-start(f32[17,8,128]{2,1,0:T(8,128)S(1)} %get-tuple-element.44), channel_id=1, source_target_pairs={{0,2},{1,3},{2,0},{3,1},{4,6},{5,7},{6,4},{7,5},{8,10},{9,11},{10,... | collective-permute-start | bytes 208904 | tf_op jit(solution)/shard_map/ppermute | solution.py:579
  8.0 3.1 %collective-permute-start.4 = (f32[4,8,128]{2,1,0:T(8,128)S(1)}, f32[4,8,128]{2,1,0:T(8,128)S(1)}, u32[]{:S(2)}, u32[]{:S(2)}) collective-permute-start(f32[4,8,128]{2,1,0:T(8,128)S(1)} %get-tuple-element.53), channel_id=1, source_target_pairs={{0,6},{1,7},{2,4},{3,5},{4,2},{5,3},{6,0},{7,1},{8,14},{9,15},{10,... | collective-permute-start | bytes 49160 | tf_op jit(solution)/shard_map/ppermute | solution.py:579
  11.1 1.5 %shard_map.149 = (s32[512,128]{1,0:T(8,128)S(1)}, s32[512,128]{1,0:T(8,128)S(1)}) custom-call(f32[2,8,128]{2,1,0:T(8,128)S(1)} %get-tuple-element.38.after_ref.stat_ref, s32[512,128]{1,0:T(8,128)S(1)} %bitcast.8, s32[160,128]{1,0:T(8,128)S(1)} %bitcast.13), custom_call_target="tpu_custom_call" | custom-call | flops 6000000 | bytes 6000000 | tf_op jit(solution)/shard_map/pallas_call | solution.py:616
  12.6 0.9 %shard_map.151 = (f32[16,48,128]{2,1,0:T(8,128)S(1)}, f32[16,48,128]{2,1,0:T(8,128)S(1)}, f32[16,48,128]{2,1,0:T(8,128)S(1)}, f32[16,48,128]{2,1,0:T(8,128)S(1)}...) custom-call(f32[16,32,128]{2,1,0:T(8,128)S(1)} %get-tuple-element.40.w0_ref, ...), custom_call_target="tpu_custom_call" | custom-call | flops 6000000 | bytes 6000000 | tf_op jit(solution)/shard_map/pallas_call | solution.py:636
  13.6 0.7 %shard_map.152 = (f32[6,48,128]{2,1,0:T(8,128)S(1)}, f32[6,48,128]{2,1,0:T(8,128)S(1)}, f32[6,48,128]{2,1,0:T(8,128)S(1)}, f32[3,48,256]{2,1,0:T(8,128)S(1)}, f3...) custom-call(s32[512,128]{1,0:T(8,128)S(1)} %get-tuple-element.39.after_ref.plan_ref, ...), custom_call_target="tpu_custom_call" | custom-call | flops 2000000 | bytes 2000000 | tf_op jit(solution)/shard_map/pallas_call | solution.py:643
  14.3 0.6 %collective-permute-start.6 = (f32[8,128]{1,0:T(8,128)S(1)}, f32[8,128]{1,0:T(8,128)S(1)}, u32[]{:S(2)}, u32[]{:S(2)}) collective-permute-start(f32[8,128]{1,0:T(8,128)S(1)} %get-tuple-element.55.after_ref.a_ref), channel_id=1, source_target_pairs={{0,1},{1,0},{2,3},{3,2},{4,5},{5,4},{6,7},{7,6},{8,9},{9,8},{10,11... | collective-permute-start | bytes 12296 | tf_op jit(solution)/shard_map/ppermute | solution.py:667
  14.9 0.7 %shard_map.153.after_ref.refs_0_ = f32[256,128]{1,0:T(8,128)S(1)} custom-call(f32[8,128]{1,0:T(8,128)S(1)} %get-tuple-element.55.after_ref.a_ref, f32[8,128]{1,0:T(8,128)S(1)} %get-tuple-element.56.where_ref, f32[16,48,128]{2,1,0:T(8,128)S(1)} %get-tuple-element.45.a_ref.inside_ref, f32[6,48,128]{2,1,0:T(8,128)S(1)} %get-tuple-element.57.edge_ref, ...), custom_call_target="tpu_custom_call" | custom-call | flops 6000000 | bytes 6000000 | tf_op jit(solution)/shard_map/pallas_call | solution.py:656
  15.6 0.1 collective-permute-done.6.b_ref
  15.7 1.5 %collective-permute-start.7 = (f32[8,128]{1,0:T(8,128)S(1)}, f32[8,128]{1,0:T(8,128)S(1)}, u32[]{:S(2)}, u32[]{:S(2)}) collective-permute-start(f32[8,128]{1,0:T(8,128)S(1)} %shard_map.154.after_ref.a_ref), channel_id=1, source_target_pairs={{0,2},{2,0},{1,3},{3,1},{4,6},{6,4},{5,7},{7,5},{8,10},{10,8},{9,1... | collective-permute-start | bytes 12296 | tf_op jit(solution)/shard_map/ppermute | solution.py:667
  17.2 0.7 %shard_map.155.after_ref.refs_1_ = f32[256,128]{1,0:T(8,128)S(1)} custom-call(f32[8,128]{1,0:T(8,128)S(1)} %shard_map.154.after_ref.a_ref, f32[8,128]{1,0:T(8,128)S(1)} %get-tuple-element.56.where_ref, f32[16,48,128]{2,1,0:T(8,128)S(1)} %get-tuple-element.47.b_ref.inside_ref, f32[6,48,128]{2,1,0:T(8,128)S(1)} %get-tuple-element.60.edge_ref.eb_ref, ...), custom_call_target="tpu_custom_call" | custom-call | flops 6000000 | bytes 6000000 | tf_op jit(solution)/shard_map/pallas_call | solution.py:656
  18.0 0.8 %shard_map.156.after_ref.refs_2_ = f32[256,128]{1,0:T(8,128)S(1)} custom-call(f32[256,128]{1,0:T(8,128)S(1)} %shard_map.155.after_ref.refs_1_, f32[8,128]{1,0:T(8,128)S(1)} %get-tuple-element.56.where_ref, f32[16,48,128]{2,1,0:T(8,128)S(1)} %get-tuple-element.48.c_ref.inside_ref, f32[6,48,128]{2,1,0:T(8,128)S(1)} %get-tuple-element.61.edge_ref.ec_ref, ...), custom_call_target="tpu_custom_call" | custom-call | flops 6000000 | bytes 6000000 | tf_op jit(solution)/shard_map/pallas_call | solution.py:656
  18.7 0.6 %collective-permute-done.7.b_ref = f32[8,128]{1,0:T(8,128)S(1)} collective-permute-done((f32[8,128]{1,0:T(8,128)S(1)}, f32[8,128]{1,0:T(8,128)S(1)}, u32[]{:S(2)}, u32[]{:S(2)}) %collective-permute-start.7) | collective-permute-done | bytes 4128 | tf_op jit(solution)/shard_map/ppermute | solution.py:667
  19.4 1.9 %collective-permute-start.9 = (f32[200,128]{1,0:T(8,128)S(1)}, f32[200,128]{1,0:T(8,128)S(1)}, u32[]{:S(2)}, u32[]{:S(2)}) collective-permute-start(f32[200,128]{1,0:T(8,128)S(1)} %get-tuple-element.67), channel_id=1, source_target_pairs={{0,8},{1,9},{2,10},{3,11},{4,12},{5,13},{6,14},{7,15},{8,0},{9,1},... | collective-permute-start | bytes 307208 | tf_op jit(solution)/shard_map/ppermute | solution.py:579
  21.3 1.6 %collective-permute-start.11 = (f32[200,128]{1,0:T(8,128)S(1)}, f32[200,128]{1,0:T(8,128)S(1)}, u32[]{:S(2)}, u32[]{:S(2)}) collective-permute-start(f32[200,128]{1,0:T(8,128)S(1)} %get-tuple-element.69), channel_id=1, source_target_pairs={{0,4},{1,5},{2,6},{3,7},{4,0},{5,1},{6,2},{7,3},{8,12},{9,13},{10,... | collective-permute-start | bytes 307208 | tf_op jit(solution)/shard_map/ppermute | solution.py:579
  22.9 1.7 %collective-permute-start.8 = (f32[8,128]{1,0:T(8,128)S(1)}, f32[8,128]{1,0:T(8,128)S(1)}, u32[]{:S(2)}, u32[]{:S(2)}) collective-permute-start(f32[8,128]{1,0:T(8,128)S(1)} %shard_map.157.total_ref), channel_id=1, source_target_pairs={{0,12},{1,13},{2,14},{3,15},{4,5},{5,4},{6,7},{7,6},{8,9},{9,8},{1... | collective-permute-start | bytes 12296 | tf_op jit(solution)/shard_map/ppermute | solution.py:579
  24.6 0.6 %copy-done.6 = f32[20]{0:T(128)S(1)} copy-done((f32[20]{0:T(128)S(1)}, f32[20]{0:T(128)}, u32[]{:S(2)}) %copy-start.6) | copy-done | bytes 104
  25.3 1.9 %shard_map.159 = (f32[20,64,128]{2,1,0:T(8,128)S(1)}, f32[64,128]{1,0:T(8,128)S(1)}, f32[64,128]{1,0:T(8,128)S(1)}, f32[2,20,128]{2,1,0:T(8,128)S(1)}) custom-call(f32[20]{0:T(128)S(1)} %copy-done.6, f32[20]{0:T(128)S(1)} %copy-done.7, f32[20]{0:T(128)S(1)} %copy-done.8, f32[20]{0:T(128)S(1)} %copy-done.9, f32[20]{0:T(128)S(1)} %copy-done.10, ...), custom_call_target="tpu_custom_call" | custom-call | flops 6000000 | bytes 6000000 | tf_op jit(solution)/shard_map/pallas_call | solution.py:687
  27.2 1.6 %collective-permute-done.8.refs_1_ = f32[8,128]{1,0:T(8,128)S(1)} collective-permute-done((f32[8,128]{1,0:T(8,128)S(1)}, f32[8,128]{1,0:T(8,128)S(1)}, u32[]{:S(2)}, u32[]{:S(2)}) %collective-permute-start.8) | collective-permute-done | bytes 4128 | tf_op jit(solution)/shard_map/ppermute | solution.py:579
  28.8 1.8 %shard_map.160 = (f32[16,32,128]{2,1,0:T(8,128)}, f32[64,128]{1,0:T(8,128)}, f32[20,64,128]{2,1,0:T(8,128)}) custom-call(f32[2,20,128]{2,1,0:T(8,128)S(1)} %get-tuple-element.63.coef_ref, f32[64,128]{1,0:T(8,128)S(1)} %bitcast.14, f32[64,128]{1,0:T(8,128)S(1)} %bitcast.12, f32[64,128]{1,0:T(8,128)S(1)} %get-tuple-element.64.sum_ref, ...), custom_call_target="tpu_custom_call" | custom-call | flops 2000000 | bytes 2000000 | tf_op jit(solution)/shard_map/pallas_call | solution.py:700
  (35 shorter events, 0.1 us)
Async XLA Ops:
  2.0 1.4 %collective-permute-start = (f32[2,32,128]{2,1,0:T(8,128)S(1)}, f32[2,32,128]{2,1,0:T(8,128)S(1)}, u32[]{:S(2)}, u32[]{:S(2)}) collective-permute-start(f32[2,32,128]{2,1,0:T(8,128)S(1)} %get-tuple-element.42.own_ref), channel_id=1, source_target_pairs={{0,1},{1,0},{2,3},{3,2},{4,5},{5,4},{6,7},{7,6},{8,9},{9,8},{10,11... | collective-permute-start | bytes 98312 | tf_op jit(solution)/shard_map/ppermute | solution.py:614
  3.4 7.7 %copy-start = (s32[16,32,128]{2,1,0:T(8,128)S(1)}, s32[16,32,128]{2,1,0:T(8,128)}, u32[]{:S(2)}) copy-start(s32[16,32,128]{2,1,0:T(8,128)} %label_hbm.1) | copy-start | bytes 786436
  3.4 7.7 %copy-start.4 = (s32[1,1,1,20480]{3,2,1,0:T(1,128)S(1)}, s32[1,1,1,20480]{3,2,1,0:T(1,128)}, u32[]{:S(2)}) copy-start(s32[1,1,1,20480]{3,2,1,0:T(1,128)} %param.16) | copy-start | bytes 245764
  3.5 10.1 %collective-permute-start.2 = (f32[6,32,128]{2,1,0:T(8,128)S(1)}, f32[6,32,128]{2,1,0:T(8,128)S(1)}, u32[]{:S(2)}, u32[]{:S(2)}) collective-permute-start(f32[6,32,128]{2,1,0:T(8,128)S(1)} %get-tuple-element.51), channel_id=1, source_target_pairs={{0,4},{1,5},{2,6},{3,7},{4,0},{5,1},{6,2},{7,3},{8,12},{9,13},{10,... | collective-permute-start | bytes 294920 | tf_op jit(solution)/shard_map/ppermute | solution.py:579
  6.5 7.1 %collective-permute-start.3 = (f32[6,32,128]{2,1,0:T(8,128)S(1)}, f32[6,32,128]{2,1,0:T(8,128)S(1)}, u32[]{:S(2)}, u32[]{:S(2)}) collective-permute-start(f32[6,32,128]{2,1,0:T(8,128)S(1)} %get-tuple-element.52), channel_id=1, source_target_pairs={{0,1},{1,0},{2,3},{3,2},{4,8},{5,9},{6,10},{7,11},{8,4},{9,5},{10,... | collective-permute-start | bytes 294920 | tf_op jit(solution)/shard_map/ppermute | solution.py:579
  6.5 6.1 %collective-permute-start.1 = (f32[17,8,128]{2,1,0:T(8,128)S(1)}, f32[17,8,128]{2,1,0:T(8,128)S(1)}, u32[]{:S(2)}, u32[]{:S(2)}) collective-permute-start(f32[17,8,128]{2,1,0:T(8,128)S(1)} %get-tuple-element.44), channel_id=1, source_target_pairs={{0,2},{1,3},{2,0},{3,1},{4,6},{5,7},{6,4},{7,5},{8,10},{9,11},{10,... | collective-permute-start | bytes 208904 | tf_op jit(solution)/shard_map/ppermute | solution.py:579
  8.0 5.6 %collective-permute-start.4 = (f32[4,8,128]{2,1,0:T(8,128)S(1)}, f32[4,8,128]{2,1,0:T(8,128)S(1)}, u32[]{:S(2)}, u32[]{:S(2)}) collective-permute-start(f32[4,8,128]{2,1,0:T(8,128)S(1)} %get-tuple-element.53), channel_id=1, source_target_pairs={{0,6},{1,7},{2,4},{3,5},{4,2},{5,3},{6,0},{7,1},{8,14},{9,15},{10,... | collective-permute-start | bytes 49160 | tf_op jit(solution)/shard_map/ppermute | solution.py:579
  11.1 2.5 %collective-permute-start.5 = (f32[4,8,128]{2,1,0:T(8,128)S(1)}, f32[4,8,128]{2,1,0:T(8,128)S(1)}, u32[]{:S(2)}, u32[]{:S(2)}) collective-permute-start(f32[4,8,128]{2,1,0:T(8,128)S(1)} %get-tuple-element.54), channel_id=1, source_target_pairs={{0,1},{1,0},{2,3},{3,2},{4,10},{5,11},{6,8},{7,9},{8,6},{9,7},{10,... | collective-permute-start | bytes 49160 | tf_op jit(solution)/shard_map/ppermute | solution.py:579
  14.3 1.4 %collective-permute-start.6 = (f32[8,128]{1,0:T(8,128)S(1)}, f32[8,128]{1,0:T(8,128)S(1)}, u32[]{:S(2)}, u32[]{:S(2)}) collective-permute-start(f32[8,128]{1,0:T(8,128)S(1)} %get-tuple-element.55.after_ref.a_ref), channel_id=1, source_target_pairs={{0,1},{1,0},{2,3},{3,2},{4,5},{5,4},{6,7},{7,6},{8,9},{9,8},{10,11... | collective-permute-start | bytes 12296 | tf_op jit(solution)/shard_map/ppermute | solution.py:667
  15.7 3.6 %collective-permute-start.7 = (f32[8,128]{1,0:T(8,128)S(1)}, f32[8,128]{1,0:T(8,128)S(1)}, u32[]{:S(2)}, u32[]{:S(2)}) collective-permute-start(f32[8,128]{1,0:T(8,128)S(1)} %shard_map.154.after_ref.a_ref), channel_id=1, source_target_pairs={{0,2},{2,0},{1,3},{3,1},{4,6},{6,4},{5,7},{7,5},{8,10},{10,8},{9,1... | collective-permute-start | bytes 12296 | tf_op jit(solution)/shard_map/ppermute | solution.py:667
  18.0 6.7 %copy-start.1 = (f32[20,1,8192]{2,1,0:T(1,128)S(1)}, f32[20,1,8192]{2,1,0:T(1,128)}, u32[]{:S(2)}) copy-start(f32[20,1,8192]{2,1,0:T(1,128)} %param.18) | copy-start | bytes 1966084
  18.0 6.6 %copy-start.2 = (f32[20,1,8192]{2,1,0:T(1,128)S(1)}, f32[20,1,8192]{2,1,0:T(1,128)}, u32[]{:S(2)}) copy-start(f32[20,1,8192]{2,1,0:T(1,128)} %param.20) | copy-start | bytes 1966084
  19.3 5.3 %copy-start.3 = (f32[1,8192]{1,0:T(1,128)S(1)}, f32[1,8192]{1,0:T(1,128)}, u32[]{:S(2)}) copy-start(f32[1,8192]{1,0:T(1,128)} %param.17) | copy-start | bytes 98308
  19.3 5.3 %copy-start.9 = (f32[20]{0:T(128)S(1)}, f32[20]{0:T(128)}, u32[]{:S(2)}) copy-start(f32[20]{0:T(128)} %cond_ref.1) | copy-start | bytes 244
  19.3 5.3 %copy-start.10 = (f32[20]{0:T(128)S(1)}, f32[20]{0:T(128)}, u32[]{:S(2)}) copy-start(f32[20]{0:T(128)} %rev_ref.1) | copy-start | bytes 244
  19.4 9.4 %collective-permute-start.9 = (f32[200,128]{1,0:T(8,128)S(1)}, f32[200,128]{1,0:T(8,128)S(1)}, u32[]{:S(2)}, u32[]{:S(2)}) collective-permute-start(f32[200,128]{1,0:T(8,128)S(1)} %get-tuple-element.67), channel_id=1, source_target_pairs={{0,8},{1,9},{2,10},{3,11},{4,12},{5,13},{6,14},{7,15},{8,0},{9,1},... | collective-permute-start | bytes 307208 | tf_op jit(solution)/shard_map/ppermute | solution.py:579
  21.3 7.5 %collective-permute-start.10 = (f32[200,128]{1,0:T(8,128)S(1)}, f32[200,128]{1,0:T(8,128)S(1)}, u32[]{:S(2)}, u32[]{:S(2)}) collective-permute-start(f32[200,128]{1,0:T(8,128)S(1)} %get-tuple-element.68), channel_id=1, source_target_pairs={{0,1},{1,0},{2,3},{3,2},{4,8},{5,9},{6,10},{7,11},{8,4},{9,5},{10,... | collective-permute-start | bytes 307208 | tf_op jit(solution)/shard_map/ppermute | solution.py:579
  21.3 7.5 %collective-permute-start.11 = (f32[200,128]{1,0:T(8,128)S(1)}, f32[200,128]{1,0:T(8,128)S(1)}, u32[]{:S(2)}, u32[]{:S(2)}) collective-permute-start(f32[200,128]{1,0:T(8,128)S(1)} %get-tuple-element.69), channel_id=1, source_target_pairs={{0,4},{1,5},{2,6},{3,7},{4,0},{5,1},{6,2},{7,3},{8,12},{9,13},{10,... | collective-permute-start | bytes 307208 | tf_op jit(solution)/shard_map/ppermute | solution.py:579
  22.9 5.9 %collective-permute-start.8 = (f32[8,128]{1,0:T(8,128)S(1)}, f32[8,128]{1,0:T(8,128)S(1)}, u32[]{:S(2)}, u32[]{:S(2)}) collective-permute-start(f32[8,128]{1,0:T(8,128)S(1)} %shard_map.157.total_ref), channel_id=1, source_target_pairs={{0,12},{1,13},{2,14},{3,15},{4,5},{5,4},{6,7},{7,6},{8,9},{9,8},{1... | collective-permute-start | bytes 12296 | tf_op jit(solution)/shard_map/ppermute | solution.py:579
  24.6 0.7 %copy-start.6 = (f32[20]{0:T(128)S(1)}, f32[20]{0:T(128)}, u32[]{:S(2)}) copy-start(f32[20]{0:T(128)} %half_ref.1) | copy-start | bytes 244
  24.6 0.7 %copy-start.7 = (f32[20]{0:T(128)S(1)}, f32[20]{0:T(128)}, u32[]{:S(2)}) copy-start(f32[20]{0:T(128)} %slope_ref.1) | copy-start | bytes 244
  24.6 0.7 %copy-start.8 = (f32[20]{0:T(128)S(1)}, f32[20]{0:T(128)}, u32[]{:S(2)}) copy-start(f32[20]{0:T(128)} %tau_ref.1) | copy-start | bytes 244
  25.3 3.5 %copy-start.5 = (f32[1,8192]{1,0:T(1,128)S(1)}, f32[1,8192]{1,0:T(1,128)}, u32[]{:S(2)}) copy-start(f32[1,8192]{1,0:T(1,128)} %param.19) | copy-start | bytes 98308

commit v17 on v16

--- a/solution.py
+++ b/solution.py
@@ -47,20 +47,8 @@
     return lax.broadcasted_iota(jnp.int32, shape, len(shape) - 2)
 
 
-def start_kernel(
-    right_hbm, damping_hbm, label_hbm, w0_ref, inv_ref, pack_ref, stat_ref, right_ref, damping_ref, label_ref, sems
-):
+def start_kernel(right_ref, damping_ref, label_ref, w0_ref, inv_ref, pack_ref, stat_ref):
     nx, ny, nz = right_ref.shape
-    parts = sems.shape[1]
-    size = nx // parts
-    copies = []
-    for part in range(parts):
-        here = pl.ds(part * size, size)
-        for k, (source, target) in enumerate(
-            ((right_hbm, right_ref), (damping_hbm, damping_ref), (label_hbm, label_ref))
-        ):
-            copies.append(pltpu.make_async_copy(source.at[here], target.at[here], sems.at[k, part]))
-            copies[-1].start()
     gz = lax.axis_index("gz")
     lane = lanes_of((ny, nz))
     packed_w = jnp.zeros((ny, nz), F32)
@@ -68,9 +56,6 @@
     energy = jnp.zeros((ny, nz), F32)
     cells = jnp.zeros((ny, nz), F32)
     for x in range(nx):
-        if x % size == 0:
-            for k in range(3):
-                copies[3 * (x // size) + k].wait()
         label = label_ref[x].astype(F32)
         right = right_ref[x]
         inv = 1.0 / (12.0 + damping_ref[x] * (1.0 + 3.0 * label))
@@ -512,7 +497,7 @@
 ):
     n_small, n_large = len(alone[0]), len(alone[1])
     own_ref, small_refs, large_refs = refs[0], refs[1 : 1 + n_small], refs[1 + n_small : 1 + n_small + n_large]
-    x_hbm, volt_ref, gate_hbm, x_ref, gate_ref, sems = refs[1 + n_small + n_large :]
+    x_ref, volt_ref, gate_ref = refs[1 + n_small + n_large :]
     size = (own_ref.shape[0] - SUB) // 3
     gx = lax.axis_index("gx")
 
@@ -530,14 +515,6 @@
         total = total + jnp.where(is_one(flags), 0.0, ref[3 * size :])
     sums = jnp.sum(total, axis=1, keepdims=True)
     c0, c1, c2 = galerkin([jnp.broadcast_to(sums[k : k + 1], (1, LANES)) for k in range(6)])
-    nx, ny, nz = x_ref.shape
-    own = slice(SUB, SUB + ny)
-    for x in range(nx):
-        w1 = b_ref[x, own] if 1 <= x < nx - 1 else eb_ref[2 if x == 0 else 3, own]
-        w2 = c_ref[x, own] if 2 <= x < nx - 2 else ec_ref[x + 1 if x < 2 else x - (nx - 2) + 3, own]
-        x_ref[x] = c0 * a_ref[x, own] + c1 * w1 + c2 * w2
-    copies = [pltpu.make_async_copy(x_ref, x_hbm, sems.at[0])]
-    copies[0].start()
     landed = jnp.zeros((size, LANES), F32)
     for k, c in enumerate((c0, c1, c2)):
         part = own_ref[k * size : k * size + size]
@@ -547,16 +524,14 @@
     cot = vcot_ref[...] + landed
     v = v_ref[...]
     volt_ref[...] = cot * factor_ref[...] + sum_ref[...]
-    n_states = base_ref.shape[0]
-    half = n_states // 2
-    for part, (begin, end) in enumerate(((0, half), (half, n_states))):
-        for g in range(begin, end):
-            gate_ref[g] = base_ref[g] - (coef_ref[0, g : g + 1] * cot) * (v - coef_ref[1, g : g + 1])
-        here = pl.ds(begin, end - begin)
-        copies.append(pltpu.make_async_copy(gate_ref.at[here], gate_hbm.at[here], sems.at[1 + part]))
-        copies[-1].start()
-    for copy in copies:
-        copy.wait()
+    for g in range(base_ref.shape[0]):
+        gate_ref[g] = base_ref[g] - (coef_ref[0, g : g + 1] * cot) * (v - coef_ref[1, g : g + 1])
+    nx, ny, nz = x_ref.shape
+    own = slice(SUB, SUB + ny)
+    for x in range(nx):
+        w1 = b_ref[x, own] if 1 <= x < nx - 1 else eb_ref[2 if x == 0 else 3, own]
+        w2 = c_ref[x, own] if 2 <= x < nx - 2 else ec_ref[x + 1 if x < 2 else x - (nx - 2) + 3, own]
+        x_ref[x] = c0 * a_ref[x, own] + c1 * w1 + c2 * w2
 
 
 def partners(axis, step):
@@ -604,11 +579,6 @@
 
     w0, inv, packed, stat = call(
         start_kernel, (block, block, shape_of(2, ny, nz), shape_of(2, SUB, nz)), 3,
-        specs=[HBM] * 3,
-        scratch=[
-            pltpu.VMEM((nx, ny, nz), F32), pltpu.VMEM((nx, ny, nz), F32), pltpu.VMEM((nx, ny, nz), jnp.int32),
-            pltpu.SemaphoreType.DMA((3, 2)),
-        ],
     )(in_hbm(potential_cot), in_hbm(damping), in_hbm(tissue_label))
 
     got = lax.ppermute(packed, "gz", [(0, 1), (1, 0)])
@@ -701,11 +671,6 @@
         functools.partial(finish_kernel, alone),
         (block, shape_of(block_rows, LANES), shape_of(n_states, block_rows, LANES)),
         12 + len(small) + len(large),
-        outs=(HBM, VMEM, HBM),
-        scratch=[
-            pltpu.VMEM((nx, ny, nz), F32), pltpu.VMEM((n_states, block_rows, LANES), F32),
-            pltpu.SemaphoreType.DMA((3,)),
-        ],
     )(
         state_coefs, cells(voltage_cot), cells(voltage), total_change, factor, base,
         in0, in1, in2, ends1, ends2, blocks[0], *small, *large,

time: 30.7 us -> 30.1 us (0.980)
  Pallas kernels: 10.6 us -> 9.91 us
    pallas_call x1, Pallas kernels: 1.75 us -> 1.18 us  [local(): call(functools.partial(finish_kernel, alone), (block, shape_of(block_rows...]
where the time goes in v17:
time: 30.1 us; the launch traced here: 29.9 us
  starting transfers between devices  15.4 us (51%)
  Pallas kernels  9.91 us (33%)
  waiting for transfers between devices  3.11 us (10%)
  between operations  0.8 us (3%)
  local copies, waits for them, and re-layouts  0.67 us (2%)
    ppermute x9, starting transfers between devices, swap(): return lax.ppermute(value, ('gx', 'gy', 'gz'), pairs)  12.8 us
    pallas_call x3, Pallas kernels, couple(): call(functools.partial(couple_kernel, stage, slot_rows), shape_of(n_gx *...  2.25 us
    ppermute x2, starting transfers between devices, add(): lax.ppermute(value, axis, [(i, i ^ step) for i in range(lax.axis_size(axi...  2.08 us
    pallas_call x1, Pallas kernels, local(): call(membrane_kernel, (shape_of(n_states, block_rows, LANES), shape_of(bl...  1.93 us
    ppermute x9, waiting for transfers between devices, swap(): return lax.ppermute(value, ('gx', 'gy', 'gz'), pairs)  1.6 us
    pallas_call x1, Pallas kernels, local(): call(plan_kernel, (cells_shape, cells_shape), 3, cost=6000000)  1.51 us
    pallas_call x1, Pallas kernels, local(): call(start_kernel, (block, block, shape_of(2, ny, nz), shape_of(2, SUB, n...  1.32 us
    pallas_call x1, Pallas kernels, local(): call(functools.partial(finish_kernel, alone), (block, shape_of(block_rows...  1.18 us
  transfers between devices with their start and end apart: 12, of which 4 were waited for; matrix products, arithmetic and copies ran while one was open for 0% of the time, Pallas kernels for 22%

profile of v17, /device:TPU:0, one launch (start us, length us, event | category | flops | bytes accessed | tf_op | source)
XLA Modules:
  0.0 29.9 jit_solution(6782397177338474870)
XLA Ops:
  0.6 1.3 %shard_map.148 = (f32[16,32,128]{2,1,0:T(8,128)S(1)}, f32[16,32,128]{2,1,0:T(8,128)S(1)}, f32[2,32,128]{2,1,0:T(8,128)S(1)}, f32[2,8,128]{2,1,0:T(8,128)S(1)}) custom-call(f32[16,32,128]{2,1,0:T(8,128)} %right_ref.1, f32[16,32,128]{2,1,0:T(8,128)} %damping_ref.1, s32[16,32,128]{2,1,0:T(8,128)} %label_ref.1), custom_call_target="tpu_custom_call" | custom-call | flops 2000000 | bytes 2000000 | tf_op jit(solution)/shard_map/pallas_call | solution.py:580
  2.0 0.5 %collective-permute-start = (f32[2,32,128]{2,1,0:T(8,128)S(1)}, f32[2,32,128]{2,1,0:T(8,128)S(1)}, u32[]{:S(2)}, u32[]{:S(2)}) collective-permute-start(f32[2,32,128]{2,1,0:T(8,128)S(1)} %get-tuple-element.42.own_ref), channel_id=1, source_target_pairs={{0,1},{1,0},{2,3},{3,2},{4,5},{5,4},{6,7},{7,6},{8,9},{9,8},{10,11... | collective-permute-start | bytes 98312 | tf_op jit(solution)/shard_map/ppermute | solution.py:584
  2.5 0.9 %collective-permute-done.got_ref = f32[2,32,128]{2,1,0:T(8,128)S(1)} collective-permute-done((f32[2,32,128]{2,1,0:T(8,128)S(1)}, f32[2,32,128]{2,1,0:T(8,128)S(1)}, u32[]{:S(2)}, u32[]{:S(2)}) %collective-permute-start) | collective-permute-done | bytes 32800 | tf_op jit(solution)/shard_map/ppermute | solution.py:584
  3.3 0.1 shard_map.150
  3.4 3.0 %collective-permute-start.2 = (f32[6,32,128]{2,1,0:T(8,128)S(1)}, f32[6,32,128]{2,1,0:T(8,128)S(1)}, u32[]{:S(2)}, u32[]{:S(2)}) collective-permute-start(f32[6,32,128]{2,1,0:T(8,128)S(1)} %get-tuple-element.51), channel_id=1, source_target_pairs={{0,4},{1,5},{2,6},{3,7},{4,0},{5,1},{6,2},{7,3},{8,12},{9,13},{10,... | collective-permute-start | bytes 294920 | tf_op jit(solution)/shard_map/ppermute | solution.py:554
  6.4 1.5 %collective-permute-start.1 = (f32[17,8,128]{2,1,0:T(8,128)S(1)}, f32[17,8,128]{2,1,0:T(8,128)S(1)}, u32[]{:S(2)}, u32[]{:S(2)}) collective-permute-start(f32[17,8,128]{2,1,0:T(8,128)S(1)} %get-tuple-element.44), channel_id=1, source_target_pairs={{0,2},{1,3},{2,0},{3,1},{4,6},{5,7},{6,4},{7,5},{8,10},{9,11},{10,... | collective-permute-start | bytes 208904 | tf_op jit(solution)/shard_map/ppermute | solution.py:554
  7.9 3.1 %collective-permute-start.4 = (f32[4,8,128]{2,1,0:T(8,128)S(1)}, f32[4,8,128]{2,1,0:T(8,128)S(1)}, u32[]{:S(2)}, u32[]{:S(2)}) collective-permute-start(f32[4,8,128]{2,1,0:T(8,128)S(1)} %get-tuple-element.53), channel_id=1, source_target_pairs={{0,6},{1,7},{2,4},{3,5},{4,2},{5,3},{6,0},{7,1},{8,14},{9,15},{10,... | collective-permute-start | bytes 49160 | tf_op jit(solution)/shard_map/ppermute | solution.py:554
  11.0 1.5 %shard_map.149 = (s32[512,128]{1,0:T(8,128)S(1)}, s32[512,128]{1,0:T(8,128)S(1)}) custom-call(f32[2,8,128]{2,1,0:T(8,128)S(1)} %get-tuple-element.38.after_ref.stat_ref, s32[512,128]{1,0:T(8,128)S(1)} %bitcast.8, s32[160,128]{1,0:T(8,128)S(1)} %bitcast.13), custom_call_target="tpu_custom_call" | custom-call | flops 6000000 | bytes 6000000 | tf_op jit(solution)/shard_map/pallas_call | solution.py:586
  12.6 0.9 %shard_map.151 = (f32[16,48,128]{2,1,0:T(8,128)S(1)}, f32[16,48,128]{2,1,0:T(8,128)S(1)}, f32[16,48,128]{2,1,0:T(8,128)S(1)}, f32[16,48,128]{2,1,0:T(8,128)S(1)}...) custom-call(f32[16,32,128]{2,1,0:T(8,128)S(1)} %get-tuple-element.40.w0_ref, ...), custom_call_target="tpu_custom_call" | custom-call | flops 6000000 | bytes 6000000 | tf_op jit(solution)/shard_map/pallas_call | solution.py:606
  13.5 0.7 %shard_map.152 = (f32[6,48,128]{2,1,0:T(8,128)S(1)}, f32[6,48,128]{2,1,0:T(8,128)S(1)}, f32[6,48,128]{2,1,0:T(8,128)S(1)}, f32[3,48,256]{2,1,0:T(8,128)S(1)}, f3...) custom-call(s32[512,128]{1,0:T(8,128)S(1)} %get-tuple-element.39.after_ref.plan_ref, ...), custom_call_target="tpu_custom_call" | custom-call | flops 2000000 | bytes 2000000 | tf_op jit(solution)/shard_map/pallas_call | solution.py:613
  14.2 0.6 %collective-permute-start.6 = (f32[8,128]{1,0:T(8,128)S(1)}, f32[8,128]{1,0:T(8,128)S(1)}, u32[]{:S(2)}, u32[]{:S(2)}) collective-permute-start(f32[8,128]{1,0:T(8,128)S(1)} %get-tuple-element.55.after_ref.a_ref), channel_id=1, source_target_pairs={{0,1},{1,0},{2,3},{3,2},{4,5},{5,4},{6,7},{7,6},{8,9},{9,8},{10,11... | collective-permute-start | bytes 12296 | tf_op jit(solution)/shard_map/ppermute | solution.py:637
  14.8 0.7 %shard_map.153.after_ref.refs_0_ = f32[256,128]{1,0:T(8,128)S(1)} custom-call(f32[8,128]{1,0:T(8,128)S(1)} %get-tuple-element.55.after_ref.a_ref, f32[8,128]{1,0:T(8,128)S(1)} %get-tuple-element.56.where_ref, f32[16,48,128]{2,1,0:T(8,128)S(1)} %get-tuple-element.45.a_ref.inside_ref, f32[6,48,128]{2,1,0:T(8,128)S(1)} %get-tuple-element.57.edge_ref, ...), custom_call_target="tpu_custom_call" | custom-call | flops 6000000 | bytes 6000000 | tf_op jit(solution)/shard_map/pallas_call | solution.py:626
  15.5 0.1 collective-permute-done.6.b_ref
  15.6 1.5 %collective-permute-start.7 = (f32[8,128]{1,0:T(8,128)S(1)}, f32[8,128]{1,0:T(8,128)S(1)}, u32[]{:S(2)}, u32[]{:S(2)}) collective-permute-start(f32[8,128]{1,0:T(8,128)S(1)} %shard_map.154.after_ref.a_ref), channel_id=1, source_target_pairs={{0,2},{2,0},{1,3},{3,1},{4,6},{6,4},{5,7},{7,5},{8,10},{10,8},{9,1... | collective-permute-start | bytes 12296 | tf_op jit(solution)/shard_map/ppermute | solution.py:637
  17.1 0.7 %shard_map.155.after_ref.refs_1_ = f32[256,128]{1,0:T(8,128)S(1)} custom-call(f32[8,128]{1,0:T(8,128)S(1)} %shard_map.154.after_ref.a_ref, f32[8,128]{1,0:T(8,128)S(1)} %get-tuple-element.56.where_ref, f32[16,48,128]{2,1,0:T(8,128)S(1)} %get-tuple-element.47.b_ref.inside_ref, f32[6,48,128]{2,1,0:T(8,128)S(1)} %get-tuple-element.60.edge_ref.eb_ref, ...), custom_call_target="tpu_custom_call" | custom-call | flops 6000000 | bytes 6000000 | tf_op jit(solution)/shard_map/pallas_call | solution.py:626
  17.9 0.8 %shard_map.156.after_ref.refs_2_ = f32[256,128]{1,0:T(8,128)S(1)} custom-call(f32[256,128]{1,0:T(8,128)S(1)} %shard_map.155.after_ref.refs_1_, f32[8,128]{1,0:T(8,128)S(1)} %get-tuple-element.56.where_ref, f32[16,48,128]{2,1,0:T(8,128)S(1)} %get-tuple-element.48.c_ref.inside_ref, f32[6,48,128]{2,1,0:T(8,128)S(1)} %get-tuple-element.61.edge_ref.ec_ref, ...), custom_call_target="tpu_custom_call" | custom-call | flops 6000000 | bytes 6000000 | tf_op jit(solution)/shard_map/pallas_call | solution.py:626
  18.6 0.6 %collective-permute-done.7.b_ref = f32[8,128]{1,0:T(8,128)S(1)} collective-permute-done((f32[8,128]{1,0:T(8,128)S(1)}, f32[8,128]{1,0:T(8,128)S(1)}, u32[]{:S(2)}, u32[]{:S(2)}) %collective-permute-start.7) | collective-permute-done | bytes 4128 | tf_op jit(solution)/shard_map/ppermute | solution.py:637
  19.3 1.9 %collective-permute-start.9 = (f32[200,128]{1,0:T(8,128)S(1)}, f32[200,128]{1,0:T(8,128)S(1)}, u32[]{:S(2)}, u32[]{:S(2)}) collective-permute-start(f32[200,128]{1,0:T(8,128)S(1)} %get-tuple-element.67), channel_id=1, source_target_pairs={{0,8},{1,9},{2,10},{3,11},{4,12},{5,13},{6,14},{7,15},{8,0},{9,1},... | collective-permute-start | bytes 307208 | tf_op jit(solution)/shard_map/ppermute | solution.py:554
  21.2 1.6 %collective-permute-start.11 = (f32[200,128]{1,0:T(8,128)S(1)}, f32[200,128]{1,0:T(8,128)S(1)}, u32[]{:S(2)}, u32[]{:S(2)}) collective-permute-start(f32[200,128]{1,0:T(8,128)S(1)} %get-tuple-element.69), channel_id=1, source_target_pairs={{0,4},{1,5},{2,6},{3,7},{4,0},{5,1},{6,2},{7,3},{8,12},{9,13},{10,... | collective-permute-start | bytes 307208 | tf_op jit(solution)/shard_map/ppermute | solution.py:554
  22.8 1.7 %collective-permute-start.8 = (f32[8,128]{1,0:T(8,128)S(1)}, f32[8,128]{1,0:T(8,128)S(1)}, u32[]{:S(2)}, u32[]{:S(2)}) collective-permute-start(f32[8,128]{1,0:T(8,128)S(1)} %shard_map.157.total_ref), channel_id=1, source_target_pairs={{0,12},{1,13},{2,14},{3,15},{4,5},{5,4},{6,7},{7,6},{8,9},{9,8},{1... | collective-permute-start | bytes 12296 | tf_op jit(solution)/shard_map/ppermute | solution.py:554
  24.6 0.6 %copy-done.6 = f32[20]{0:T(128)S(1)} copy-done((f32[20]{0:T(128)S(1)}, f32[20]{0:T(128)}, u32[]{:S(2)}) %copy-start.6) | copy-done | bytes 104
  25.2 1.9 %shard_map.159 = (f32[20,64,128]{2,1,0:T(8,128)S(1)}, f32[64,128]{1,0:T(8,128)S(1)}, f32[64,128]{1,0:T(8,128)S(1)}, f32[2,20,128]{2,1,0:T(8,128)S(1)}) custom-call(f32[20]{0:T(128)S(1)} %copy-done.6, f32[20]{0:T(128)S(1)} %copy-done.7, f32[20]{0:T(128)S(1)} %copy-done.8, f32[20]{0:T(128)S(1)} %copy-done.9, f32[20]{0:T(128)S(1)} %copy-done.10, ...), custom_call_target="tpu_custom_call" | custom-call | flops 6000000 | bytes 6000000 | tf_op jit(solution)/shard_map/pallas_call | solution.py:657
  27.1 1.6 %collective-permute-done.8.refs_1_ = f32[8,128]{1,0:T(8,128)S(1)} collective-permute-done((f32[8,128]{1,0:T(8,128)S(1)}, f32[8,128]{1,0:T(8,128)S(1)}, u32[]{:S(2)}, u32[]{:S(2)}) %collective-permute-start.8) | collective-permute-done | bytes 4128 | tf_op jit(solution)/shard_map/ppermute | solution.py:554
  28.7 1.2 %shard_map.160 = (f32[16,32,128]{2,1,0:T(8,128)}, f32[64,128]{1,0:T(8,128)}, f32[20,64,128]{2,1,0:T(8,128)}) custom-call(f32[2,20,128]{2,1,0:T(8,128)S(1)} %get-tuple-element.63.coef_ref, f32[64,128]{1,0:T(8,128)S(1)} %bitcast.14, f32[64,128]{1,0:T(8,128)S(1)} %bitcast.12, f32[64,128]{1,0:T(8,128)S(1)} %get-tuple-element.64.sum_ref, ...), custom_call_target="tpu_custom_call" | custom-call | flops 2000000 | bytes 2000000 | tf_op jit(solution)/shard_map/pallas_call | solution.py:670
  (35 shorter events, 0.1 us)
Async XLA Ops:
  2.0 1.4 %collective-permute-start = (f32[2,32,128]{2,1,0:T(8,128)S(1)}, f32[2,32,128]{2,1,0:T(8,128)S(1)}, u32[]{:S(2)}, u32[]{:S(2)}) collective-permute-start(f32[2,32,128]{2,1,0:T(8,128)S(1)} %get-tuple-element.42.own_ref), channel_id=1, source_target_pairs={{0,1},{1,0},{2,3},{3,2},{4,5},{5,4},{6,7},{7,6},{8,9},{9,8},{10,11... | collective-permute-start | bytes 98312 | tf_op jit(solution)/shard_map/ppermute | solution.py:584
  3.3 7.7 %copy-start = (s32[16,32,128]{2,1,0:T(8,128)S(1)}, s32[16,32,128]{2,1,0:T(8,128)}, u32[]{:S(2)}) copy-start(s32[16,32,128]{2,1,0:T(8,128)} %label_ref.1) | copy-start | bytes 786436
  3.3 7.7 %copy-start.4 = (s32[1,1,1,20480]{3,2,1,0:T(1,128)S(1)}, s32[1,1,1,20480]{3,2,1,0:T(1,128)}, u32[]{:S(2)}) copy-start(s32[1,1,1,20480]{3,2,1,0:T(1,128)} %param.16) | copy-start | bytes 245764
  3.4 10.1 %collective-permute-start.2 = (f32[6,32,128]{2,1,0:T(8,128)S(1)}, f32[6,32,128]{2,1,0:T(8,128)S(1)}, u32[]{:S(2)}, u32[]{:S(2)}) collective-permute-start(f32[6,32,128]{2,1,0:T(8,128)S(1)} %get-tuple-element.51), channel_id=1, source_target_pairs={{0,4},{1,5},{2,6},{3,7},{4,0},{5,1},{6,2},{7,3},{8,12},{9,13},{10,... | collective-permute-start | bytes 294920 | tf_op jit(solution)/shard_map/ppermute | solution.py:554
  6.4 7.1 %collective-permute-start.3 = (f32[6,32,128]{2,1,0:T(8,128)S(1)}, f32[6,32,128]{2,1,0:T(8,128)S(1)}, u32[]{:S(2)}, u32[]{:S(2)}) collective-permute-start(f32[6,32,128]{2,1,0:T(8,128)S(1)} %get-tuple-element.52), channel_id=1, source_target_pairs={{0,1},{1,0},{2,3},{3,2},{4,8},{5,9},{6,10},{7,11},{8,4},{9,5},{10,... | collective-permute-start | bytes 294920 | tf_op jit(solution)/shard_map/ppermute | solution.py:554
  6.4 6.1 %collective-permute-start.1 = (f32[17,8,128]{2,1,0:T(8,128)S(1)}, f32[17,8,128]{2,1,0:T(8,128)S(1)}, u32[]{:S(2)}, u32[]{:S(2)}) collective-permute-start(f32[17,8,128]{2,1,0:T(8,128)S(1)} %get-tuple-element.44), channel_id=1, source_target_pairs={{0,2},{1,3},{2,0},{3,1},{4,6},{5,7},{6,4},{7,5},{8,10},{9,11},{10,... | collective-permute-start | bytes 208904 | tf_op jit(solution)/shard_map/ppermute | solution.py:554
  7.9 5.6 %collective-permute-start.4 = (f32[4,8,128]{2,1,0:T(8,128)S(1)}, f32[4,8,128]{2,1,0:T(8,128)S(1)}, u32[]{:S(2)}, u32[]{:S(2)}) collective-permute-start(f32[4,8,128]{2,1,0:T(8,128)S(1)} %get-tuple-element.53), channel_id=1, source_target_pairs={{0,6},{1,7},{2,4},{3,5},{4,2},{5,3},{6,0},{7,1},{8,14},{9,15},{10,... | collective-permute-start | bytes 49160 | tf_op jit(solution)/shard_map/ppermute | solution.py:554
  11.0 2.5 %collective-permute-start.5 = (f32[4,8,128]{2,1,0:T(8,128)S(1)}, f32[4,8,128]{2,1,0:T(8,128)S(1)}, u32[]{:S(2)}, u32[]{:S(2)}) collective-permute-start(f32[4,8,128]{2,1,0:T(8,128)S(1)} %get-tuple-element.54), channel_id=1, source_target_pairs={{0,1},{1,0},{2,3},{3,2},{4,10},{5,11},{6,8},{7,9},{8,6},{9,7},{10,... | collective-permute-start | bytes 49160 | tf_op jit(solution)/shard_map/ppermute | solution.py:554
  14.2 1.4 %collective-permute-start.6 = (f32[8,128]{1,0:T(8,128)S(1)}, f32[8,128]{1,0:T(8,128)S(1)}, u32[]{:S(2)}, u32[]{:S(2)}) collective-permute-start(f32[8,128]{1,0:T(8,128)S(1)} %get-tuple-element.55.after_ref.a_ref), channel_id=1, source_target_pairs={{0,1},{1,0},{2,3},{3,2},{4,5},{5,4},{6,7},{7,6},{8,9},{9,8},{10,11... | collective-permute-start | bytes 12296 | tf_op jit(solution)/shard_map/ppermute | solution.py:637
  15.6 3.6 %collective-permute-start.7 = (f32[8,128]{1,0:T(8,128)S(1)}, f32[8,128]{1,0:T(8,128)S(1)}, u32[]{:S(2)}, u32[]{:S(2)}) collective-permute-start(f32[8,128]{1,0:T(8,128)S(1)} %shard_map.154.after_ref.a_ref), channel_id=1, source_target_pairs={{0,2},{2,0},{1,3},{3,1},{4,6},{6,4},{5,7},{7,5},{8,10},{10,8},{9,1... | collective-permute-start | bytes 12296 | tf_op jit(solution)/shard_map/ppermute | solution.py:637
  17.9 6.7 %copy-start.1 = (f32[20,1,8192]{2,1,0:T(1,128)S(1)}, f32[20,1,8192]{2,1,0:T(1,128)}, u32[]{:S(2)}) copy-start(f32[20,1,8192]{2,1,0:T(1,128)} %param.18) | copy-start | bytes 1966084
  17.9 6.6 %copy-start.2 = (f32[20,1,8192]{2,1,0:T(1,128)S(1)}, f32[20,1,8192]{2,1,0:T(1,128)}, u32[]{:S(2)}) copy-start(f32[20,1,8192]{2,1,0:T(1,128)} %param.20) | copy-start | bytes 1966084
  19.2 5.3 %copy-start.3 = (f32[1,8192]{1,0:T(1,128)S(1)}, f32[1,8192]{1,0:T(1,128)}, u32[]{:S(2)}) copy-start(f32[1,8192]{1,0:T(1,128)} %param.17) | copy-start | bytes 98308
  19.2 5.3 %copy-start.9 = (f32[20]{0:T(128)S(1)}, f32[20]{0:T(128)}, u32[]{:S(2)}) copy-start(f32[20]{0:T(128)} %cond_ref.1) | copy-start | bytes 244
  19.2 5.3 %copy-start.10 = (f32[20]{0:T(128)S(1)}, f32[20]{0:T(128)}, u32[]{:S(2)}) copy-start(f32[20]{0:T(128)} %rev_ref.1) | copy-start | bytes 244
  19.3 9.4 %collective-permute-start.9 = (f32[200,128]{1,0:T(8,128)S(1)}, f32[200,128]{1,0:T(8,128)S(1)}, u32[]{:S(2)}, u32[]{:S(2)}) collective-permute-start(f32[200,128]{1,0:T(8,128)S(1)} %get-tuple-element.67), channel_id=1, source_target_pairs={{0,8},{1,9},{2,10},{3,11},{4,12},{5,13},{6,14},{7,15},{8,0},{9,1},... | collective-permute-start | bytes 307208 | tf_op jit(solution)/shard_map/ppermute | solution.py:554
  21.2 7.5 %collective-permute-start.10 = (f32[200,128]{1,0:T(8,128)S(1)}, f32[200,128]{1,0:T(8,128)S(1)}, u32[]{:S(2)}, u32[]{:S(2)}) collective-permute-start(f32[200,128]{1,0:T(8,128)S(1)} %get-tuple-element.68), channel_id=1, source_target_pairs={{0,1},{1,0},{2,3},{3,2},{4,8},{5,9},{6,10},{7,11},{8,4},{9,5},{10,... | collective-permute-start | bytes 307208 | tf_op jit(solution)/shard_map/ppermute | solution.py:554
  21.2 7.5 %collective-permute-start.11 = (f32[200,128]{1,0:T(8,128)S(1)}, f32[200,128]{1,0:T(8,128)S(1)}, u32[]{:S(2)}, u32[]{:S(2)}) collective-permute-start(f32[200,128]{1,0:T(8,128)S(1)} %get-tuple-element.69), channel_id=1, source_target_pairs={{0,4},{1,5},{2,6},{3,7},{4,0},{5,1},{6,2},{7,3},{8,12},{9,13},{10,... | collective-permute-start | bytes 307208 | tf_op jit(solution)/shard_map/ppermute | solution.py:554
  22.8 5.9 %collective-permute-start.8 = (f32[8,128]{1,0:T(8,128)S(1)}, f32[8,128]{1,0:T(8,128)S(1)}, u32[]{:S(2)}, u32[]{:S(2)}) collective-permute-start(f32[8,128]{1,0:T(8,128)S(1)} %shard_map.157.total_ref), channel_id=1, source_target_pairs={{0,12},{1,13},{2,14},{3,15},{4,5},{5,4},{6,7},{7,6},{8,9},{9,8},{1... | collective-permute-start | bytes 12296 | tf_op jit(solution)/shard_map/ppermute | solution.py:554
  24.5 0.7 %copy-start.6 = (f32[20]{0:T(128)S(1)}, f32[20]{0:T(128)}, u32[]{:S(2)}) copy-start(f32[20]{0:T(128)} %half_ref.1) | copy-start | bytes 244
  24.5 0.7 %copy-start.7 = (f32[20]{0:T(128)S(1)}, f32[20]{0:T(128)}, u32[]{:S(2)}) copy-start(f32[20]{0:T(128)} %slope_ref.1) | copy-start | bytes 244
  24.5 0.7 %copy-start.8 = (f32[20]{0:T(128)S(1)}, f32[20]{0:T(128)}, u32[]{:S(2)}) copy-start(f32[20]{0:T(128)} %tau_ref.1) | copy-start | bytes 244
  25.2 3.5 %copy-start.5 = (f32[1,8192]{1,0:T(1,128)S(1)}, f32[1,8192]{1,0:T(1,128)}, u32[]{:S(2)}) copy-start(f32[1,8192]{1,0:T(1,128)} %param.19) | copy-start | bytes 98308

commit v18 on v17

--- a/solution.py
+++ b/solution.py
@@ -137,17 +137,25 @@
             edge_ref[3] = y_ref[nx]
 
 
-def slab_step(v, s, inv):
+SUMS = (("w0 k0", "w1 k0"), ("w1 n1", "w1 k1", "w2 k1", "w0 n1"), ("w2 k2",))
+ORDER = ("w0 r", "w0 k0", "w1 k0", "w1 n1", "w1 k1", "w2 k1", "w2 k2", "w0 n1")
+
+
+def slab_step(stage, v, s, inv):
     width = v.shape[1]
     across = pltpu.roll(v, PACK, 1) + pltpu.roll(v, width - PACK, 1)
     q = v + 0.5 * (s + across)
-    if inv is None:
+    if stage == 2:
         return q, None
     total = (
         pltpu.roll(q, 1, 1) + pltpu.roll(q, width - 1, 1) + s + across
         + 0.5 * (pltpu.roll(s, PACK, 1) + pltpu.roll(s, width - PACK, 1))
     )
-    return q, total * inv
+    return q, next_vector(stage, v, total, inv)
+
+
+def next_vector(stage, v, total, inv):
+    return v - total * inv if stage == 0 else total * inv
 
 
 def along_z(q, half, column, gz):
@@ -160,19 +168,24 @@
     return up + down + jnp.where(lane == entry, pltpu.roll(half, turn, 1), 0.0)
 
 
-def sweep(stage, spans, nx, ny, nz, gz, get, get_inv, put, slab_q, sums):
+def sweep(stage, spans, nx, ny, nz, gz, get, get_inv, put, slab_q, sums, get_right, get_w0, held):
     margin = 2 - stage
     start = SUB - margin
     tiles = ny // SUB + (margin > 0)
     own = subs_of((SUB, nz)) >= margin
-    parts = [[], []]
+    names = SUMS[stage]
+    parts = {name: [] for name in names}
     for tile in range(tiles):
         row = start + SUB * tile
         q_rows = slab_q[SUB * tile : SUB * tile + SUB]
-        acc = [jnp.zeros((SUB, nz), F32) for _ in range(2)]
+        acc = {name: jnp.zeros((SUB, nz), F32) for name in names}
 
         def beside(x):
             return get(x, row - 1) + get(x, row + 1)
+
+        def rows(name, x):
+            ref, at = held[name, x]
+            return ref.at[at, row : row + SUB]
 
         for first, last in spans:
             s_low, s_mid = beside(first - 1), beside(first)
@@ -185,26 +198,35 @@
                 rest = s_mid + across
                 total = along_z(v_mid + 0.5 * rest, half, column % nz, gz) + rest + 0.5 * (s_low + s_high)
                 if stage < 2:
-                    after = total * get_inv(x, row)
+                    after = next_vector(stage, v_mid, total, get_inv(x, row))
                     put(x, row, after)
                 if 0 <= x < nx:
-                    acc[0] = acc[0] + v_mid * total
-                    if stage < 2:
-                        acc[1] = acc[1] + after * total
+                    if stage == 0:
+                        k0 = get_right(x, row) - total
+                        rows("k0", x)[...] = k0
+                        terms = (v_mid * k0, after * k0)
+                    elif stage == 1:
+                        rows("n1", x)[...] = total
+                        k1 = rows("k0", x)[...] - total
+                        terms = (v_mid * total, v_mid * k1, after * k1, get_w0(x, row) * total)
+                    else:
+                        terms = (v_mid * (rows("n1", x)[...] - total),)
+                    for name, term in zip(names, terms):
+                        acc[name] = acc[name] + term
                 v_low, v_mid, s_low, s_mid = v_mid, v_high, s_mid, s_high
-        for k in range(2):
-            parts[k].append(acc[k])
-    for k in range(2 if stage < 2 else 1):
-        part = parts[k]
+        for name in names:
+            parts[name].append(acc[name])
+    for name in names:
+        part = parts[name]
         total = part[1]
         for other in part[2 : ny // SUB]:
             total = total + other
-        total = total + (jnp.where(own, part[0], part[-1]) if margin else part[0])
-        sums[2 * stage + k] = total
-
-
-def inner_kernel(n_y, w0_ref, inv_ref, slab_ref, *refs):
-    y_refs, (a_ref, i_ref, b_ref, c_ref, sum_ref, own_slab_ref, slabs_ref) = refs[:n_y], refs[n_y:]
+        sums[name] = total + (jnp.where(own, part[0], part[-1]) if margin else part[0])
+
+
+def inner_kernel(n_y, right_ref, w0_ref, inv_ref, slab_ref, *refs):
+    y_refs, refs = refs[:n_y], refs[n_y:]
+    a_ref, i_ref, b_ref, c_ref, sum_ref, own_slab_ref, pass_ref, slabs_ref, r_ref, k_ref, n_ref = refs
     nx, ny, nz = w0_ref.shape
     gz = lax.axis_index("gz")
     for x in range(nx + 1):
@@ -219,13 +241,18 @@
             ref[SUB + ny :] = halos[k]
     for k in range(2):
         slabs_ref[3 * k] = own_slab_ref[k]
+    for x in range(nx):
+        r_ref[x, SUB : SUB + ny] = right_ref[x]
+    held = {("k0", x): (k_ref, x) for x in range(nx)} | {("n1", x): (n_ref, x) for x in range(nx)}
+    held |= {("k0", 1): (pass_ref, 0), ("k0", nx - 2): (pass_ref, 1)}
+    held |= {("n1", 2): (pass_ref, 2), ("n1", nx - 3): (pass_ref, 3)}
     sums = {}
     for stage in range(3):
         source, target = (a_ref, b_ref, c_ref)[stage], (b_ref, c_ref, None)[stage]
         start, size = SUB - 2 + stage, ny if stage == 2 else ny + SUB
         v = slabs_ref[stage, start : start + size]
         s = slabs_ref[stage, start - 1 : start - 1 + size] + slabs_ref[stage, start + 1 : start + 1 + size]
-        q, after = slab_step(v, s, slabs_ref[3, start : start + size] if stage < 2 else None)
+        q, after = slab_step(stage, v, s, slabs_ref[3, start : start + size])
         if stage < 2:
             slabs_ref[stage + 1, start : start + size] = after
 
@@ -236,16 +263,17 @@
             stage, [(1 + stage, nx - 1 - stage)], nx, ny, nz, gz,
             lambda x, row: source[x, row : row + SUB], lambda x, row: i_ref[x, row : row + SUB],
             put, q, sums,
+            lambda x, row: r_ref[x, row : row + SUB], lambda x, row: a_ref[x, row : row + SUB], held,
         )
-    for k in range(5):
-        sum_ref[k] = sums[k]
+    for k, name in enumerate(ORDER[1:]):
+        sum_ref[k] = sums[name]
 
 
 def outer_kernel(
-    n_y, column_total, after_ref, a_ref, i_ref, b_ref, c_ref, slab_ref, sum_ref, stat_ref, *refs
+    n_y, column_total, after_ref, right_ref, a_ref, i_ref, b_ref, c_ref, slab_ref, sum_ref, pass_ref, stat_ref, *refs
 ):
     x_refs, corner_refs = refs[:2], refs[2 : 2 + 2 * n_y]
-    ea_ref, eb_ref, ec_ref, slabs_ref, total_ref, where_ref, ei_ref, si_ref = refs[2 + 2 * n_y :]
+    ea_ref, eb_ref, ec_ref, slabs_ref, total_ref, where_ref, ei_ref, si_ref, r_ref, k_ref, n_ref = refs[2 + 2 * n_y :]
     nx, ny, nz = a_ref.shape[0], a_ref.shape[1] - 2 * SUB, a_ref.shape[2]
     ring = ny + SUB
     gz = lax.axis_index("gz")
@@ -303,13 +331,19 @@
 
         return get
 
+    r_ref[0, SUB : SUB + ny] = right_ref[0]
+    r_ref[1, SUB : SUB + ny] = right_ref[nx - 1]
+    held = {("k0", 0): (k_ref, 0), ("k0", nx - 1): (k_ref, 1), ("k0", 1): (pass_ref, 0), ("k0", nx - 2): (pass_ref, 1)}
+    for at, x in enumerate((0, 1, nx - 2, nx - 1)):
+        held["n1", x] = (n_ref, at)
+    held |= {("n1", 2): (pass_ref, 2), ("n1", nx - 3): (pass_ref, 3)}
     sums = {}
     for stage in range(3):
         get = reader((a_ref, b_ref, c_ref)[stage], (ea_ref, eb_ref, ec_ref)[stage], stage, 3)
         start, size = SUB - 2 + stage, ny if stage == 2 else ring
         v = slabs_ref[stage, start : start + size]
         s = slabs_ref[stage, start - 1 : start - 1 + size] + slabs_ref[stage, start + 1 : start + 1 + size]
-        q, after = slab_step(v, s, si_ref[0, start : start + size] if stage < 2 else None)
+        q, after = slab_step(stage, v, s, si_ref[0, start : start + size])
         if stage < 2:
             slabs_ref[stage + 1, start : start + size] = after
 
@@ -321,12 +355,13 @@
         sweep(
             stage, [(stage - 2, stage + 1), (nx - 1 - stage, nx + 2 - stage)], nx, ny, nz, gz,
             get, reader(i_ref, ei_ref, 0, 2), put, q, sums,
+            lambda x, row: r_ref[0 if x == 0 else 1, row : row + SUB],
+            lambda x, row: a_ref[x, row : row + SUB], held,
         )
 
     total_ref[0:1] = stat_ref[0, 0:1]
-    for k in range(5):
-        total_ref[k + 1 : k + 2] = jnp.sum(sums[k] + sum_ref[k], axis=0, keepdims=True)
-    total_ref[6:8] = jnp.zeros((2, nz), F32)
+    for k, name in enumerate(ORDER[1:]):
+        total_ref[k + 1 : k + 2] = jnp.sum(sums[name] + sum_ref[k], axis=0, keepdims=True)
     gx, n_x = lax.axis_index("gx"), lax.axis_size("gx")
     count = jnp.sum(stat_ref[1, 0:1], axis=1, keepdims=True)
     below, above = [part[4] for part in slab_parts]
@@ -377,23 +412,29 @@
     plan_ref[...] = plan
 
 
-def galerkin(t):
-    g00, g01, g02, g12, g22 = t[0] - t[1], t[1] - t[2], t[2] - t[3], t[3] - t[4], t[4] - t[5]
-    g11 = g02
-    l10, l20 = g01 / g00, g02 / g00
-    d1 = g11 - l10 * g01
-    m21 = g12 - l20 * g01
-    ok1 = d1 > 1e-6 * g11
+def galerkin(total):
+    def add_up(*rows):
+        return [jnp.broadcast_to(jnp.sum(row, axis=1, keepdims=True), row.shape) for row in rows]
+
+    row = {name: total[k : k + 1] for k, name in enumerate(ORDER)}
+    b0, b2 = row["w0 r"], row["w0 n1"]
+    g00, g01, g02 = row["w0 k0"], row["w1 k0"], row["w1 n1"]
+    g11, g12, g22 = row["w1 k1"], row["w2 k1"], row["w2 k2"]
+    s00, s01, s02, s0, s11, s22 = add_up(g00, g01, g02, b0, g11, g22)
+    l10, l20 = s01 / s00, s02 / s00
+    h11 = g11 - l10 * (2.0 * g01 - l10 * g00)
+    h12 = g12 - l10 * g02 - l20 * (g01 - l10 * g00)
+    h22 = g22 - l20 * (2.0 * g02 - l20 * g00)
+    y1, y2 = g00 - l10 * b0, b2 - l20 * b0
+    d1, s12, s1 = add_up(h11, h12, y1)
+    ok1 = d1 > 1e-7 * s11
     d1 = jnp.where(ok1, d1, 1.0)
-    l21 = jnp.where(ok1, m21 / d1, 0.0)
-    d2 = g22 - l20 * g02 - l21 * m21
-    ok2 = ok1 & (d2 > 1e-6 * g22)
-    d2 = jnp.where(ok2, d2, 1.0)
-    y1 = t[1] - l10 * t[0]
-    y2 = t[2] - l20 * t[0] - l21 * y1
-    c2 = jnp.where(ok2, y2 / d2, 0.0)
-    c1 = jnp.where(ok1, y1 / d1 - l21 * c2, 0.0)
-    c0 = t[0] / g00 - l10 * c1 - l20 * c2
+    l21 = jnp.where(ok1, s12 / d1, 0.0)
+    d2, s2 = add_up(h22 - l21 * (2.0 * h12 - l21 * h11), y2 - l21 * y1)
+    ok2 = ok1 & (d2 > 1e-7 * s22)
+    c2 = jnp.where(ok2, s2 / jnp.where(ok2, d2, 1.0), 0.0)
+    c1 = jnp.where(ok1, s1 / d1 - l21 * c2, 0.0)
+    c0 = s0 / s00 - l10 * c1 - l20 * c2
     return c0, c1, c2
 
 
@@ -513,8 +554,7 @@
         total = total + jnp.where(is_one(flags), ref[...], 0.0)
     for flags, ref in zip(alone[1], large_refs):
         total = total + jnp.where(is_one(flags), 0.0, ref[3 * size :])
-    sums = jnp.sum(total, axis=1, keepdims=True)
-    c0, c1, c2 = galerkin([jnp.broadcast_to(sums[k : k + 1], (1, LANES)) for k in range(6)])
+    c0, c1, c2 = galerkin(total)
     landed = jnp.zeros((size, LANES), F32)
     for k, c in enumerate((c0, c1, c2)):
         part = own_ref[k * size : k * size + size]
@@ -603,19 +643,22 @@
     tall = ring + SUB
     planes = shape_of(nx, tall, nz)
     edges = shape_of(6, tall, nz)
-    in0, in_inv, in1, in2, in_sums, own_slab = call(
+    in0, in_inv, in1, in2, in_sums, own_slab, passed = call(
         functools.partial(inner_kernel, n_y),
-        (planes,) * 4 + (shape_of(5, SUB, nz), shape_of(2, tall, nz)),
-        3 + n_y,
-        scratch=[pltpu.VMEM((4, tall, nz), F32)],
+        (planes,) * 4 + (shape_of(len(ORDER) - 1, SUB, nz), shape_of(2, tall, nz), shape_of(4, tall, nz)),
+        4 + n_y,
+        scratch=[pltpu.VMEM((4, tall, nz), F32)] + [pltpu.VMEM((nx, tall, nz), F32)] * 3,
         cost=6_000_000,
-    )(w0, inv, slab, *along_y)
+    )(potential_cot, w0, inv, slab, *along_y)
     ends0, ends1, ends2, slabs, sums, where = call(
         functools.partial(outer_kernel, n_y, float(n_gx * voltage.shape[1])),
         (edges,) * 3 + (shape_of(3, tall, 2 * nz), shape_of(SUB, nz), shape_of(SUB, nz)),
-        10 + 2 * n_y,
-        scratch=[pltpu.VMEM((4, tall, nz), F32), pltpu.VMEM((1, tall, 2 * nz), F32)],
-    )(plan, in0, in_inv, in1, in2, own_slab, in_sums, stat, *along_x, *across)
+        12 + 2 * n_y,
+        scratch=[
+            pltpu.VMEM((4, tall, nz), F32), pltpu.VMEM((1, tall, 2 * nz), F32),
+            pltpu.VMEM((2, tall, nz), F32), pltpu.VMEM((2, tall, nz), F32), pltpu.VMEM((4, tall, nz), F32),
+        ],
+    )(plan, potential_cot, in0, in_inv, in1, in2, own_slab, in_sums, passed, stat, *along_x, *across)
 
     if n_gx > 4:
         counts = lax.all_gather(jnp.sum(stat[1, 0]), "gx")

time: 30.1 us -> 30.3 us (level)
    unnamed x22 -> x24, local copies, waits for them, and re-layouts: 0.67 us -> 0.68 us
where the time goes in v18:
time: 30.3 us; the launch traced here: 30.1 us
  starting transfers between devices  15.4 us (51%)
  Pallas kernels  10.1 us (33%)
  waiting for transfers between devices  3.12 us (10%)
  between operations  0.82 us (3%)
  local copies, waits for them, and re-layouts  0.68 us (2%)
    ppermute x9, starting transfers between devices, swap(): return lax.ppermute(value, ('gx', 'gy', 'gz'), pairs)  12.8 us
    pallas_call x3, Pallas kernels, couple(): call(functools.partial(couple_kernel, stage, slot_rows), shape_of(n_gx *...  2.25 us
    ppermute x2, starting transfers between devices, add(): lax.ppermute(value, axis, [(i, i ^ step) for i in range(lax.axis_size(axi...  2.07 us
    pallas_call x1, Pallas kernels, local(): call(membrane_kernel, (shape_of(n_states, block_rows, LANES), shape_of(bl...  1.91 us
    ppermute x9, waiting for transfers between devices, swap(): return lax.ppermute(value, ('gx', 'gy', 'gz'), pairs)  1.61 us
    pallas_call x1, Pallas kernels, local(): call(plan_kernel, (cells_shape, cells_shape), 3, cost=6000000)  1.51 us
    pallas_call x1, Pallas kernels, local(): call(functools.partial(finish_kernel, alone), (block, shape_of(block_rows...  1.34 us
    pallas_call x1, Pallas kernels, local(): call(start_kernel, (block, block, shape_of(2, ny, nz), shape_of(2, SUB, n...  1.32 us
  transfers between devices with their start and end apart: 12, of which 4 were waited for; matrix products, arithmetic and copies ran while one was open for 0% of the time, Pallas kernels for 22%

profile of v18, /device:TPU:0, one launch (start us, length us, event | category | flops | bytes accessed | tf_op | source)
XLA Modules:
  0.0 30.1 jit_solution(15322198079528644708)
XLA Ops:
  0.6 1.3 %shard_map.148 = (f32[16,32,128]{2,1,0:T(8,128)S(1)}, f32[16,32,128]{2,1,0:T(8,128)S(1)}, f32[2,32,128]{2,1,0:T(8,128)S(1)}, f32[2,8,128]{2,1,0:T(8,128)S(1)}) custom-call(f32[16,32,128]{2,1,0:T(8,128)} %right_ref.5, f32[16,32,128]{2,1,0:T(8,128)} %damping_ref.1, s32[16,32,128]{2,1,0:T(8,128)} %label_ref.1), custom_call_target="tpu_custom_call" | custom-call | flops 2000000 | bytes 2000000 | tf_op jit(solution)/shard_map/pallas_call | solution.py:620
  2.0 0.5 %collective-permute-start = (f32[2,32,128]{2,1,0:T(8,128)S(1)}, f32[2,32,128]{2,1,0:T(8,128)S(1)}, u32[]{:S(2)}, u32[]{:S(2)}) collective-permute-start(f32[2,32,128]{2,1,0:T(8,128)S(1)} %get-tuple-element.43.own_ref), channel_id=1, source_target_pairs={{0,1},{1,0},{2,3},{3,2},{4,5},{5,4},{6,7},{7,6},{8,9},{9,8},{10,11... | collective-permute-start | bytes 98312 | tf_op jit(solution)/shard_map/ppermute | solution.py:624
  2.5 0.9 %collective-permute-done.got_ref = f32[2,32,128]{2,1,0:T(8,128)S(1)} collective-permute-done((f32[2,32,128]{2,1,0:T(8,128)S(1)}, f32[2,32,128]{2,1,0:T(8,128)S(1)}, u32[]{:S(2)}, u32[]{:S(2)}) %collective-permute-start) | collective-permute-done | bytes 32800 | tf_op jit(solution)/shard_map/ppermute | solution.py:624
  3.3 0.1 shard_map.150
  3.4 3.0 %collective-permute-start.2 = (f32[6,32,128]{2,1,0:T(8,128)S(1)}, f32[6,32,128]{2,1,0:T(8,128)S(1)}, u32[]{:S(2)}, u32[]{:S(2)}) collective-permute-start(f32[6,32,128]{2,1,0:T(8,128)S(1)} %get-tuple-element.53), channel_id=1, source_target_pairs={{0,4},{1,5},{2,6},{3,7},{4,0},{5,1},{6,2},{7,3},{8,12},{9,13},{10,... | collective-permute-start | bytes 294920 | tf_op jit(solution)/shard_map/ppermute | solution.py:594
  6.4 1.5 %collective-permute-start.1 = (f32[17,8,128]{2,1,0:T(8,128)S(1)}, f32[17,8,128]{2,1,0:T(8,128)S(1)}, u32[]{:S(2)}, u32[]{:S(2)}) collective-permute-start(f32[17,8,128]{2,1,0:T(8,128)S(1)} %get-tuple-element.45), channel_id=1, source_target_pairs={{0,2},{1,3},{2,0},{3,1},{4,6},{5,7},{6,4},{7,5},{8,10},{9,11},{10,... | collective-permute-start | bytes 208904 | tf_op jit(solution)/shard_map/ppermute | solution.py:594
  7.9 3.1 %collective-permute-start.4 = (f32[4,8,128]{2,1,0:T(8,128)S(1)}, f32[4,8,128]{2,1,0:T(8,128)S(1)}, u32[]{:S(2)}, u32[]{:S(2)}) collective-permute-start(f32[4,8,128]{2,1,0:T(8,128)S(1)} %get-tuple-element.55), channel_id=1, source_target_pairs={{0,6},{1,7},{2,4},{3,5},{4,2},{5,3},{6,0},{7,1},{8,14},{9,15},{10,... | collective-permute-start | bytes 49160 | tf_op jit(solution)/shard_map/ppermute | solution.py:594
  11.1 1.5 %shard_map.149 = (s32[512,128]{1,0:T(8,128)S(1)}, s32[512,128]{1,0:T(8,128)S(1)}) custom-call(f32[2,8,128]{2,1,0:T(8,128)S(1)} %get-tuple-element.39.after_ref.stat_ref, s32[512,128]{1,0:T(8,128)S(1)} %bitcast.8, s32[160,128]{1,0:T(8,128)S(1)} %bitcast.13), custom_call_target="tpu_custom_call" | custom-call | flops 6000000 | bytes 6000000 | tf_op jit(solution)/shard_map/pallas_call | solution.py:626
  12.6 0.9 %shard_map.151 = (f32[16,48,128]{2,1,0:T(8,128)S(1)}, f32[16,48,128]{2,1,0:T(8,128)S(1)}, f32[16,48,128]{2,1,0:T(8,128)S(1)}, f32[16,48,128]{2,1,0:T(8,128)S(1)}...) custom-call(f32[16,32,128]{2,1,0:T(8,128)S(1)} %copy-done, ...), custom_call_target="tpu_custom_call" | custom-call | flops 6000000 | bytes 6000000 | tf_op jit(solution)/shard_map/pallas_call | solution.py:646
  13.5 0.7 %shard_map.152 = (f32[6,48,128]{2,1,0:T(8,128)S(1)}, f32[6,48,128]{2,1,0:T(8,128)S(1)}, f32[6,48,128]{2,1,0:T(8,128)S(1)}, f32[3,48,256]{2,1,0:T(8,128)S(1)}, f3...) custom-call(s32[512,128]{1,0:T(8,128)S(1)} %get-tuple-element.40.after_ref.plan_ref, f32[16,32,128]{2,1,0:T(8,128)S(1)} %copy-done, ...), custom_call_target="tpu_custom_call" | custom-call | flops 2000000 | bytes 2000000 | tf_op jit(solution)/shard_map/pallas_call | solution.py:653
  14.2 0.6 %collective-permute-start.6 = (f32[8,128]{1,0:T(8,128)S(1)}, f32[8,128]{1,0:T(8,128)S(1)}, u32[]{:S(2)}, u32[]{:S(2)}) collective-permute-start(f32[8,128]{1,0:T(8,128)S(1)} %get-tuple-element.57.after_ref.a_ref), channel_id=1, source_target_pairs={{0,1},{1,0},{2,3},{3,2},{4,5},{5,4},{6,7},{7,6},{8,9},{9,8},{10,11... | collective-permute-start | bytes 12296 | tf_op jit(solution)/shard_map/ppermute | solution.py:680
  14.8 0.7 %shard_map.153.after_ref.refs_0_ = f32[256,128]{1,0:T(8,128)S(1)} custom-call(f32[8,128]{1,0:T(8,128)S(1)} %get-tuple-element.57.after_ref.a_ref, f32[8,128]{1,0:T(8,128)S(1)} %get-tuple-element.58.where_ref, f32[16,48,128]{2,1,0:T(8,128)S(1)} %get-tuple-element.46.a_ref.inside_ref, f32[6,48,128]{2,1,0:T(8,128)S(1)} %get-tuple-element.59.edge_ref, ...), custom_call_target="tpu_custom_call" | custom-call | flops 6000000 | bytes 6000000 | tf_op jit(solution)/shard_map/pallas_call | solution.py:669
  15.6 0.1 collective-permute-done.6.b_ref
  15.6 1.5 %collective-permute-start.7 = (f32[8,128]{1,0:T(8,128)S(1)}, f32[8,128]{1,0:T(8,128)S(1)}, u32[]{:S(2)}, u32[]{:S(2)}) collective-permute-start(f32[8,128]{1,0:T(8,128)S(1)} %shard_map.154.after_ref.a_ref), channel_id=1, source_target_pairs={{0,2},{2,0},{1,3},{3,1},{4,6},{6,4},{5,7},{7,5},{8,10},{10,8},{9,1... | collective-permute-start | bytes 12296 | tf_op jit(solution)/shard_map/ppermute | solution.py:680
  17.1 0.8 %shard_map.155.after_ref.refs_1_ = f32[256,128]{1,0:T(8,128)S(1)} custom-call(f32[8,128]{1,0:T(8,128)S(1)} %shard_map.154.after_ref.a_ref, f32[8,128]{1,0:T(8,128)S(1)} %get-tuple-element.58.where_ref, f32[16,48,128]{2,1,0:T(8,128)S(1)} %get-tuple-element.48.b_ref.inside_ref, f32[6,48,128]{2,1,0:T(8,128)S(1)} %get-tuple-element.62.edge_ref.eb_ref, ...), custom_call_target="tpu_custom_call" | custom-call | flops 6000000 | bytes 6000000 | tf_op jit(solution)/shard_map/pallas_call | solution.py:669
  17.9 0.8 %shard_map.156.after_ref.refs_2_ = f32[256,128]{1,0:T(8,128)S(1)} custom-call(f32[256,128]{1,0:T(8,128)S(1)} %shard_map.155.after_ref.refs_1_, f32[8,128]{1,0:T(8,128)S(1)} %get-tuple-element.58.where_ref, f32[16,48,128]{2,1,0:T(8,128)S(1)} %get-tuple-element.49.c_ref.inside_ref, f32[6,48,128]{2,1,0:T(8,128)S(1)} %get-tuple-element.63.edge_ref.ec_ref, ...), custom_call_target="tpu_custom_call" | custom-call | flops 6000000 | bytes 6000000 | tf_op jit(solution)/shard_map/pallas_call | solution.py:669
  18.7 0.6 %collective-permute-done.7.b_ref = f32[8,128]{1,0:T(8,128)S(1)} collective-permute-done((f32[8,128]{1,0:T(8,128)S(1)}, f32[8,128]{1,0:T(8,128)S(1)}, u32[]{:S(2)}, u32[]{:S(2)}) %collective-permute-start.7) | collective-permute-done | bytes 4128 | tf_op jit(solution)/shard_map/ppermute | solution.py:680
  19.3 1.9 %collective-permute-start.9 = (f32[200,128]{1,0:T(8,128)S(1)}, f32[200,128]{1,0:T(8,128)S(1)}, u32[]{:S(2)}, u32[]{:S(2)}) collective-permute-start(f32[200,128]{1,0:T(8,128)S(1)} %get-tuple-element.69), channel_id=1, source_target_pairs={{0,8},{1,9},{2,10},{3,11},{4,12},{5,13},{6,14},{7,15},{8,0},{9,1},... | collective-permute-start | bytes 307208 | tf_op jit(solution)/shard_map/ppermute | solution.py:594
  21.2 1.6 %collective-permute-start.11 = (f32[200,128]{1,0:T(8,128)S(1)}, f32[200,128]{1,0:T(8,128)S(1)}, u32[]{:S(2)}, u32[]{:S(2)}) collective-permute-start(f32[200,128]{1,0:T(8,128)S(1)} %get-tuple-element.71), channel_id=1, source_target_pairs={{0,4},{1,5},{2,6},{3,7},{4,0},{5,1},{6,2},{7,3},{8,12},{9,13},{10,... | collective-permute-start | bytes 307208 | tf_op jit(solution)/shard_map/ppermute | solution.py:594
  22.9 1.7 %collective-permute-start.8 = (f32[8,128]{1,0:T(8,128)S(1)}, f32[8,128]{1,0:T(8,128)S(1)}, u32[]{:S(2)}, u32[]{:S(2)}) collective-permute-start(f32[8,128]{1,0:T(8,128)S(1)} %shard_map.157.total_ref), channel_id=1, source_target_pairs={{0,12},{1,13},{2,14},{3,15},{4,5},{5,4},{6,7},{7,6},{8,9},{9,8},{1... | collective-permute-start | bytes 12296 | tf_op jit(solution)/shard_map/ppermute | solution.py:594
  24.6 0.6 %copy-done.7 = f32[20]{0:T(128)S(1)} copy-done((f32[20]{0:T(128)S(1)}, f32[20]{0:T(128)}, u32[]{:S(2)}) %copy-start.7) | copy-done | bytes 104
  25.2 1.9 %shard_map.159 = (f32[20,64,128]{2,1,0:T(8,128)S(1)}, f32[64,128]{1,0:T(8,128)S(1)}, f32[64,128]{1,0:T(8,128)S(1)}, f32[2,20,128]{2,1,0:T(8,128)S(1)}) custom-call(f32[20]{0:T(128)S(1)} %copy-done.7, f32[20]{0:T(128)S(1)} %copy-done.8, f32[20]{0:T(128)S(1)} %copy-done.9, f32[20]{0:T(128)S(1)} %copy-done.10, f32[20]{0:T(128)S(1)} %copy-done.11, ...), custom_call_target="tpu_custom_call" | custom-call | flops 6000000 | bytes 6000000 | tf_op jit(solution)/shard_map/pallas_call | solution.py:700
  27.2 1.6 %collective-permute-done.8.refs_1_ = f32[8,128]{1,0:T(8,128)S(1)} collective-permute-done((f32[8,128]{1,0:T(8,128)S(1)}, f32[8,128]{1,0:T(8,128)S(1)}, u32[]{:S(2)}, u32[]{:S(2)}) %collective-permute-start.8) | collective-permute-done | bytes 4128 | tf_op jit(solution)/shard_map/ppermute | solution.py:594
  28.8 1.3 %shard_map.160 = (f32[16,32,128]{2,1,0:T(8,128)}, f32[64,128]{1,0:T(8,128)}, f32[20,64,128]{2,1,0:T(8,128)}) custom-call(f32[2,20,128]{2,1,0:T(8,128)S(1)} %get-tuple-element.65.coef_ref, f32[64,128]{1,0:T(8,128)S(1)} %bitcast.14, f32[64,128]{1,0:T(8,128)S(1)} %bitcast.12, f32[64,128]{1,0:T(8,128)S(1)} %get-tuple-element.66.sum_ref, ...), custom_call_target="tpu_custom_call" | custom-call | flops 2000000 | bytes 2000000 | tf_op jit(solution)/shard_map/pallas_call | solution.py:713
  (37 shorter events, 0.1 us)
Async XLA Ops:
  2.0 1.4 %collective-permute-start = (f32[2,32,128]{2,1,0:T(8,128)S(1)}, f32[2,32,128]{2,1,0:T(8,128)S(1)}, u32[]{:S(2)}, u32[]{:S(2)}) collective-permute-start(f32[2,32,128]{2,1,0:T(8,128)S(1)} %get-tuple-element.43.own_ref), channel_id=1, source_target_pairs={{0,1},{1,0},{2,3},{3,2},{4,5},{5,4},{6,7},{7,6},{8,9},{9,8},{10,11... | collective-permute-start | bytes 98312 | tf_op jit(solution)/shard_map/ppermute | solution.py:624
  3.3 7.7 %copy-start.1 = (s32[16,32,128]{2,1,0:T(8,128)S(1)}, s32[16,32,128]{2,1,0:T(8,128)}, u32[]{:S(2)}) copy-start(s32[16,32,128]{2,1,0:T(8,128)} %label_ref.1) | copy-start | bytes 786436
  3.3 7.7 %copy-start.5 = (s32[1,1,1,20480]{3,2,1,0:T(1,128)S(1)}, s32[1,1,1,20480]{3,2,1,0:T(1,128)}, u32[]{:S(2)}) copy-start(s32[1,1,1,20480]{3,2,1,0:T(1,128)} %param.16) | copy-start | bytes 245764
  3.4 9.2 %copy-start = (f32[16,32,128]{2,1,0:T(8,128)S(1)}, f32[16,32,128]{2,1,0:T(8,128)}, u32[]{:S(2)}) copy-start(f32[16,32,128]{2,1,0:T(8,128)} %right_ref.5) | copy-start | bytes 786436
  3.4 10.1 %collective-permute-start.2 = (f32[6,32,128]{2,1,0:T(8,128)S(1)}, f32[6,32,128]{2,1,0:T(8,128)S(1)}, u32[]{:S(2)}, u32[]{:S(2)}) collective-permute-start(f32[6,32,128]{2,1,0:T(8,128)S(1)} %get-tuple-element.53), channel_id=1, source_target_pairs={{0,4},{1,5},{2,6},{3,7},{4,0},{5,1},{6,2},{7,3},{8,12},{9,13},{10,... | collective-permute-start | bytes 294920 | tf_op jit(solution)/shard_map/ppermute | solution.py:594
  6.4 7.1 %collective-permute-start.3 = (f32[6,32,128]{2,1,0:T(8,128)S(1)}, f32[6,32,128]{2,1,0:T(8,128)S(1)}, u32[]{:S(2)}, u32[]{:S(2)}) collective-permute-start(f32[6,32,128]{2,1,0:T(8,128)S(1)} %get-tuple-element.54), channel_id=1, source_target_pairs={{0,1},{1,0},{2,3},{3,2},{4,8},{5,9},{6,10},{7,11},{8,4},{9,5},{10,... | collective-permute-start | bytes 294920 | tf_op jit(solution)/shard_map/ppermute | solution.py:594
  6.4 6.1 %collective-permute-start.1 = (f32[17,8,128]{2,1,0:T(8,128)S(1)}, f32[17,8,128]{2,1,0:T(8,128)S(1)}, u32[]{:S(2)}, u32[]{:S(2)}) collective-permute-start(f32[17,8,128]{2,1,0:T(8,128)S(1)} %get-tuple-element.45), channel_id=1, source_target_pairs={{0,2},{1,3},{2,0},{3,1},{4,6},{5,7},{6,4},{7,5},{8,10},{9,11},{10,... | collective-permute-start | bytes 208904 | tf_op jit(solution)/shard_map/ppermute | solution.py:594
  7.9 5.6 %collective-permute-start.4 = (f32[4,8,128]{2,1,0:T(8,128)S(1)}, f32[4,8,128]{2,1,0:T(8,128)S(1)}, u32[]{:S(2)}, u32[]{:S(2)}) collective-permute-start(f32[4,8,128]{2,1,0:T(8,128)S(1)} %get-tuple-element.55), channel_id=1, source_target_pairs={{0,6},{1,7},{2,4},{3,5},{4,2},{5,3},{6,0},{7,1},{8,14},{9,15},{10,... | collective-permute-start | bytes 49160 | tf_op jit(solution)/shard_map/ppermute | solution.py:594
  11.0 2.5 %collective-permute-start.5 = (f32[4,8,128]{2,1,0:T(8,128)S(1)}, f32[4,8,128]{2,1,0:T(8,128)S(1)}, u32[]{:S(2)}, u32[]{:S(2)}) collective-permute-start(f32[4,8,128]{2,1,0:T(8,128)S(1)} %get-tuple-element.56), channel_id=1, source_target_pairs={{0,1},{1,0},{2,3},{3,2},{4,10},{5,11},{6,8},{7,9},{8,6},{9,7},{10,... | collective-permute-start | bytes 49160 | tf_op jit(solution)/shard_map/ppermute | solution.py:594
  14.2 1.4 %collective-permute-start.6 = (f32[8,128]{1,0:T(8,128)S(1)}, f32[8,128]{1,0:T(8,128)S(1)}, u32[]{:S(2)}, u32[]{:S(2)}) collective-permute-start(f32[8,128]{1,0:T(8,128)S(1)} %get-tuple-element.57.after_ref.a_ref), channel_id=1, source_target_pairs={{0,1},{1,0},{2,3},{3,2},{4,5},{5,4},{6,7},{7,6},{8,9},{9,8},{10,11... | collective-permute-start | bytes 12296 | tf_op jit(solution)/shard_map/ppermute | solution.py:680
  15.6 3.6 %collective-permute-start.7 = (f32[8,128]{1,0:T(8,128)S(1)}, f32[8,128]{1,0:T(8,128)S(1)}, u32[]{:S(2)}, u32[]{:S(2)}) collective-permute-start(f32[8,128]{1,0:T(8,128)S(1)} %shard_map.154.after_ref.a_ref), channel_id=1, source_target_pairs={{0,2},{2,0},{1,3},{3,1},{4,6},{6,4},{5,7},{7,5},{8,10},{10,8},{9,1... | collective-permute-start | bytes 12296 | tf_op jit(solution)/shard_map/ppermute | solution.py:680
  17.9 6.7 %copy-start.2 = (f32[20,1,8192]{2,1,0:T(1,128)S(1)}, f32[20,1,8192]{2,1,0:T(1,128)}, u32[]{:S(2)}) copy-start(f32[20,1,8192]{2,1,0:T(1,128)} %param.18) | copy-start | bytes 1966084
  17.9 6.7 %copy-start.3 = (f32[20,1,8192]{2,1,0:T(1,128)S(1)}, f32[20,1,8192]{2,1,0:T(1,128)}, u32[]{:S(2)}) copy-start(f32[20,1,8192]{2,1,0:T(1,128)} %param.20) | copy-start | bytes 1966084
  19.3 5.3 %copy-start.4 = (f32[1,8192]{1,0:T(1,128)S(1)}, f32[1,8192]{1,0:T(1,128)}, u32[]{:S(2)}) copy-start(f32[1,8192]{1,0:T(1,128)} %param.17) | copy-start | bytes 98308
  19.3 5.3 %copy-start.10 = (f32[20]{0:T(128)S(1)}, f32[20]{0:T(128)}, u32[]{:S(2)}) copy-start(f32[20]{0:T(128)} %cond_ref.1) | copy-start | bytes 244
  19.3 5.3 %copy-start.11 = (f32[20]{0:T(128)S(1)}, f32[20]{0:T(128)}, u32[]{:S(2)}) copy-start(f32[20]{0:T(128)} %rev_ref.1) | copy-start | bytes 244
  19.3 9.4 %collective-permute-start.9 = (f32[200,128]{1,0:T(8,128)S(1)}, f32[200,128]{1,0:T(8,128)S(1)}, u32[]{:S(2)}, u32[]{:S(2)}) collective-permute-start(f32[200,128]{1,0:T(8,128)S(1)} %get-tuple-element.69), channel_id=1, source_target_pairs={{0,8},{1,9},{2,10},{3,11},{4,12},{5,13},{6,14},{7,15},{8,0},{9,1},... | collective-permute-start | bytes 307208 | tf_op jit(solution)/shard_map/ppermute | solution.py:594
  21.2 7.5 %collective-permute-start.10 = (f32[200,128]{1,0:T(8,128)S(1)}, f32[200,128]{1,0:T(8,128)S(1)}, u32[]{:S(2)}, u32[]{:S(2)}) collective-permute-start(f32[200,128]{1,0:T(8,128)S(1)} %get-tuple-element.70), channel_id=1, source_target_pairs={{0,1},{1,0},{2,3},{3,2},{4,8},{5,9},{6,10},{7,11},{8,4},{9,5},{10,... | collective-permute-start | bytes 307208 | tf_op jit(solution)/shard_map/ppermute | solution.py:594
  21.2 7.5 %collective-permute-start.11 = (f32[200,128]{1,0:T(8,128)S(1)}, f32[200,128]{1,0:T(8,128)S(1)}, u32[]{:S(2)}, u32[]{:S(2)}) collective-permute-start(f32[200,128]{1,0:T(8,128)S(1)} %get-tuple-element.71), channel_id=1, source_target_pairs={{0,4},{1,5},{2,6},{3,7},{4,0},{5,1},{6,2},{7,3},{8,12},{9,13},{10,... | collective-permute-start | bytes 307208 | tf_op jit(solution)/shard_map/ppermute | solution.py:594
  22.9 5.9 %collective-permute-start.8 = (f32[8,128]{1,0:T(8,128)S(1)}, f32[8,128]{1,0:T(8,128)S(1)}, u32[]{:S(2)}, u32[]{:S(2)}) collective-permute-start(f32[8,128]{1,0:T(8,128)S(1)} %shard_map.157.total_ref), channel_id=1, source_target_pairs={{0,12},{1,13},{2,14},{3,15},{4,5},{5,4},{6,7},{7,6},{8,9},{9,8},{1... | collective-permute-start | bytes 12296 | tf_op jit(solution)/shard_map/ppermute | solution.py:594
  24.5 0.7 %copy-start.7 = (f32[20]{0:T(128)S(1)}, f32[20]{0:T(128)}, u32[]{:S(2)}) copy-start(f32[20]{0:T(128)} %half_ref.1) | copy-start | bytes 244
  24.5 0.7 %copy-start.8 = (f32[20]{0:T(128)S(1)}, f32[20]{0:T(128)}, u32[]{:S(2)}) copy-start(f32[20]{0:T(128)} %slope_ref.1) | copy-start | bytes 244
  24.6 0.7 %copy-start.9 = (f32[20]{0:T(128)S(1)}, f32[20]{0:T(128)}, u32[]{:S(2)}) copy-start(f32[20]{0:T(128)} %tau_ref.1) | copy-start | bytes 244
  25.2 3.5 %copy-start.6 = (f32[1,8192]{1,0:T(1,128)S(1)}, f32[1,8192]{1,0:T(1,128)}, u32[]{:S(2)}) copy-start(f32[1,8192]{1,0:T(1,128)} %param.19) | copy-start | bytes 98308

commit v19 on v18

--- a/solution.py
+++ b/solution.py
@@ -16,7 +16,6 @@
 
 VMEM = pl.BlockSpec(memory_space=pltpu.VMEM)
 SMEM = pl.BlockSpec(memory_space=pltpu.SMEM)
-HBM = pl.BlockSpec(memory_space=pltpu.HBM)
 
 
 def shape_of(*dims):
@@ -501,6 +500,75 @@
         out_ref[3 * size :] = total_ref[...]
 
 
+ROUND = (1, 3, 0, 2)
+BACK = (2, 0, 3, 1)
+
+
+def pack_round_kernel(total_ref, *refs):
+    list_refs, (own_ref, round_ref, middle_ref, back_ref, rest_ref) = refs[:3], refs[3:]
+    size = (own_ref.shape[0] - SUB) // 3
+    half = size // 2
+    gx = lax.axis_index("gx")
+    inside = (gx == 1) | (gx == 2)
+    ahead, behind = jnp.where(inside, 2, 1), jnp.where(inside, 1, 2)
+    upper = jnp.where(gx >= 2, half, 0)
+    for k, list_ref in enumerate(list_refs):
+        for out_ref, begin, rows in (
+            (own_ref, 0, size), (round_ref, ahead * size, size), (middle_ref, 3 * size, size),
+            (back_ref, behind * size + upper, half), (rest_ref, behind * size + (half - upper), half),
+        ):
+            if not isinstance(begin, int):
+                begin = pl.multiple_of(begin, SUB)
+            out_ref[k * rows : k * rows + rows] = list_ref[pl.ds(begin, rows), :]
+    for out_ref in (own_ref, round_ref, middle_ref, back_ref):
+        out_ref[out_ref.shape[0] - SUB :] = total_ref[...]
+
+
+def land_round(own_ref, round_ref, middle_ref, back_ref, rest_ref, edge_ref):
+    size = (own_ref.shape[0] - SUB) // 3
+    half = size // 2
+    gx = lax.axis_index("gx")
+    inside = (gx == 1) | (gx == 2)
+    last = lambda ref: ref[ref.shape[0] - SUB :]
+    total = last(own_ref) + last(round_ref) + last(back_ref) + jnp.where(inside, last(middle_ref), edge_ref[...])
+    parts = []
+    for k in range(3):
+        whole = slice(k * size, k * size + size)
+        back, rest = [ref[k * half : k * half + half] for ref in (back_ref, rest_ref)]
+        odd = lax.rem(gx, 2) == 1
+        low = jnp.where(odd, jnp.where(gx == 3, rest, 0.0), back)
+        high = jnp.where(odd, back, jnp.where(gx == 0, rest, 0.0))
+        part = own_ref[whole] + round_ref[whole] + jnp.where(inside, middle_ref[whole], 0.0)
+        parts.append(part + jnp.concatenate([low, high], axis=0))
+    return total, parts
+
+
+def land_pairs(alone, own_ref, *refs):
+    small_refs, large_refs = refs[: len(alone[0])], refs[len(alone[0]) :]
+    size = (own_ref.shape[0] - SUB) // 3
+    gx = lax.axis_index("gx")
+
+    def is_one(flags):
+        found = gx < 0
+        for place, flag in enumerate(flags):
+            if flag:
+                found = found | (gx == place)
+        return found
+
+    total = own_ref[3 * size :]
+    for flags, ref in zip(alone[0], small_refs):
+        total = total + jnp.where(is_one(flags), ref[...], 0.0)
+    for flags, ref in zip(alone[1], large_refs):
+        total = total + jnp.where(is_one(flags), 0.0, ref[3 * size :])
+    parts = []
+    for k in range(3):
+        part = own_ref[k * size : k * size + size]
+        for ref in large_refs:
+            part = part + ref[k * size : k * size + size]
+        parts.append(part)
+    return total, parts
+
+
 def membrane_kernel(
     half_ref, slope_ref, tau_ref, cond_ref, rev_ref, after_ref, v_ref, gates_ref, cot_ref,
     base_ref, sum_ref, factor_ref, coef_ref,
@@ -534,33 +602,12 @@
 
 
 def finish_kernel(
-    alone, coef_ref, vcot_ref, v_ref, sum_ref, factor_ref, base_ref, a_ref, b_ref, c_ref, eb_ref, ec_ref, *refs
+    land, coef_ref, vcot_ref, v_ref, sum_ref, factor_ref, base_ref, a_ref, b_ref, c_ref, eb_ref, ec_ref, *refs
 ):
-    n_small, n_large = len(alone[0]), len(alone[1])
-    own_ref, small_refs, large_refs = refs[0], refs[1 : 1 + n_small], refs[1 + n_small : 1 + n_small + n_large]
-    x_ref, volt_ref, gate_ref = refs[1 + n_small + n_large :]
-    size = (own_ref.shape[0] - SUB) // 3
-    gx = lax.axis_index("gx")
-
-    def is_one(flags):
-        found = gx < 0
-        for place, flag in enumerate(flags):
-            if flag:
-                found = found | (gx == place)
-        return found
-
-    total = own_ref[3 * size :]
-    for flags, ref in zip(alone[0], small_refs):
-        total = total + jnp.where(is_one(flags), ref[...], 0.0)
-    for flags, ref in zip(alone[1], large_refs):
-        total = total + jnp.where(is_one(flags), 0.0, ref[3 * size :])
+    x_ref, volt_ref, gate_ref = refs[-3:]
+    total, parts = land(*refs[:-3])
     c0, c1, c2 = galerkin(total)
-    landed = jnp.zeros((size, LANES), F32)
-    for k, c in enumerate((c0, c1, c2)):
-        part = own_ref[k * size : k * size + size]
-        for ref in large_refs:
-            part = part + ref[k * size : k * size + size]
-        landed = landed + c * part
+    landed = c0 * parts[0] + c1 * parts[1] + c2 * parts[2]
     cot = vcot_ref[...] + landed
     v = v_ref[...]
     volt_ref[...] = cot * factor_ref[...] + sum_ref[...]
@@ -686,16 +733,31 @@
     list2 = couple(2, list1, in2, ends2)
     for step in [2**k for k in range(n_gy.bit_length() - 1)]:
         sums = add(sums, "gy", step, list2)
-    blocks = call(pack_kernel, (shape_of(3 * block_rows + SUB, LANES),) * n_gx, 4)(sums, list0, list1, list2)
-    apart = {k: never_meet(n_gx, k, slot_rows, block_rows) for k in range(1, n_gx)}
-    small, meets = [], []
-    for k in range(1, n_gx):
-        if any(apart[k]):
-            small.append(swap(sums, x_to=[i ^ k if apart[k][i] else i for i in range(n_gx)]))
-        meets.append(not all(apart[k]))
-    order = [k for k in [2, 3, 1] + list(range(4, n_gx)) if k < n_gx and meets[k - 1]]
-    large = [swap(blocks[k], x_to=[i if apart[k][i] else i ^ k for i in range(n_gx)]) for k in order]
-    alone = [[apart[k] for k in range(1, n_gx) if any(apart[k])], [apart[k] for k in order]]
+    if n_gx == 4 and 2 * slot_rows == 5 * block_rows:
+        own, ahead, middle, back, rest = call(
+            pack_round_kernel,
+            (shape_of(3 * block_rows + SUB, LANES),) * 3
+            + (shape_of(3 * block_rows // 2 + SUB, LANES), shape_of(3 * block_rows // 2, LANES)),
+            4,
+        )(sums, list0, list1, list2)
+        arrived = [
+            own,
+            swap(ahead, x_to=ROUND),
+            swap(middle, x_to=partners("gx", 1)),
+            swap(back, x_to=BACK),
+            swap(rest, x_to=partners("gx", 0)),
+            swap(sums, x_to=[3, 1, 2, 0]),
+        ]
+        land = land_round
+    else:
+        blocks = call(pack_kernel, (shape_of(3 * block_rows + SUB, LANES),) * n_gx, 4)(sums, list0, list1, list2)
+        apart = {k: never_meet(n_gx, k, slot_rows, block_rows) for k in range(1, n_gx)}
+        few = [k for k in apart if any(apart[k])]
+        many = [k for k in [2, 3, 1] + list(range(4, n_gx)) if k < n_gx and not all(apart[k])]
+        arrived = [blocks[0]]
+        arrived += [swap(sums, x_to=[i ^ k if apart[k][i] else i for i in range(n_gx)]) for k in few]
+        arrived += [swap(blocks[k], x_to=[i if apart[k][i] else i ^ k for i in range(n_gx)]) for k in many]
+        land = functools.partial(land_pairs, [[apart[k] for k in few], [apart[k] for k in many]])
 
     base, total_change, factor, state_coefs = call(
         membrane_kernel,
@@ -708,15 +770,15 @@
         cost=6_000_000,
     )(
         half_voltage, gate_slope, tau_base, conductance, reversal,
-        blocks[0], cells(voltage), states(gates), states(gates_cot),
+        arrived[0], cells(voltage), states(gates), states(gates_cot),
     )
     solution, volt_grad, gate_grad = call(
-        functools.partial(finish_kernel, alone),
+        functools.partial(finish_kernel, land),
         (block, shape_of(block_rows, LANES), shape_of(n_states, block_rows, LANES)),
-        12 + len(small) + len(large),
+        11 + len(arrived),
     )(
         state_coefs, cells(voltage_cot), cells(voltage), total_change, factor, base,
-        in0, in1, in2, ends1, ends2, blocks[0], *small, *large,
+        in0, in1, in2, ends1, ends2, *arrived,
     )
     return solution, volt_grad.reshape(voltage.shape), gate_grad.reshape(gates.shape)
 

time: 30.3 us -> 30.5 us (level)
  starting transfers between devices: 15.4 us -> 16.1 us
  waiting for transfers between devices: 3.12 us -> 2.67 us
    ppermute x9 -> x10, starting transfers between devices: 12.8 us -> 13.5 us  [swap(): return lax.ppermute(value, ('gx', 'gy', 'gz'), pairs)]
    ppermute x9 -> x10, waiting for transfers between devices: 1.61 us -> 1.16 us  [swap(): return lax.ppermute(value, ('gx', 'gy', 'gz'), pairs)]
  transfers between devices with their start and end apart: 12 -> 13, of which waited for: 4 -> 4; matrix products, arithmetic and copies ran while one was open for 0% -> 0% of each run, Pallas kernels for 22% -> 22%
where the time goes in v19:
time: 30.5 us; the launch traced here: 30.3 us
  starting transfers between devices  16.1 us (53%)
  Pallas kernels  10.1 us (33%)
  waiting for transfers between devices  2.67 us (9%)
  between operations  0.83 us (3%)
  local copies, waits for them, and re-layouts  0.68 us (2%)
    ppermute x10, starting transfers between devices, swap(): return lax.ppermute(value, ('gx', 'gy', 'gz'), pairs)  13.5 us
    pallas_call x3, Pallas kernels, couple(): call(functools.partial(couple_kernel, stage, slot_rows), shape_of(n_gx *...  2.25 us
    ppermute x2, starting transfers between devices, add(): lax.ppermute(value, axis, [(i, i ^ step) for i in range(lax.axis_size(axi...  2.07 us
    pallas_call x1, Pallas kernels, local(): call(membrane_kernel, (shape_of(n_states, block_rows, LANES), shape_of(bl...  1.91 us
    pallas_call x1, Pallas kernels, local(): call(plan_kernel, (cells_shape, cells_shape), 3, cost=6000000)  1.51 us
    pallas_call x1, Pallas kernels, local(): call(functools.partial(finish_kernel, land), (block, shape_of(block_rows,...  1.33 us
    pallas_call x1, Pallas kernels, local(): call(start_kernel, (block, block, shape_of(2, ny, nz), shape_of(2, SUB, n...  1.32 us
    ppermute x10, waiting for transfers between devices, swap(): return lax.ppermute(value, ('gx', 'gy', 'gz'), pairs)  1.16 us
  transfers between devices with their start and end apart: 13, of which 4 were waited for; matrix products, arithmetic and copies ran while one was open for 0% of the time, Pallas kernels for 22%

profile of v19, /device:TPU:0, one launch (start us, length us, event | category | flops | bytes accessed | tf_op | source)
XLA Modules:
  0.0 30.3 jit_solution(17906088994634472504)
XLA Ops:
  0.6 1.3 %shard_map.148 = (f32[16,32,128]{2,1,0:T(8,128)S(1)}, f32[16,32,128]{2,1,0:T(8,128)S(1)}, f32[2,32,128]{2,1,0:T(8,128)S(1)}, f32[2,8,128]{2,1,0:T(8,128)S(1)}) custom-call(f32[16,32,128]{2,1,0:T(8,128)} %right_ref.5, f32[16,32,128]{2,1,0:T(8,128)} %damping_ref.1, s32[16,32,128]{2,1,0:T(8,128)} %label_ref.1), custom_call_target="tpu_custom_call" | custom-call | flops 2000000 | bytes 2000000 | tf_op jit(solution)/shard_map/pallas_call | solution.py:667
  2.0 0.5 %collective-permute-start = (f32[2,32,128]{2,1,0:T(8,128)S(1)}, f32[2,32,128]{2,1,0:T(8,128)S(1)}, u32[]{:S(2)}, u32[]{:S(2)}) collective-permute-start(f32[2,32,128]{2,1,0:T(8,128)S(1)} %get-tuple-element.44.own_ref), channel_id=1, source_target_pairs={{0,1},{1,0},{2,3},{3,2},{4,5},{5,4},{6,7},{7,6},{8,9},{9,8},{10,11... | collective-permute-start | bytes 98312 | tf_op jit(solution)/shard_map/ppermute | solution.py:671
  2.5 0.9 %collective-permute-done.got_ref = f32[2,32,128]{2,1,0:T(8,128)S(1)} collective-permute-done((f32[2,32,128]{2,1,0:T(8,128)S(1)}, f32[2,32,128]{2,1,0:T(8,128)S(1)}, u32[]{:S(2)}, u32[]{:S(2)}) %collective-permute-start) | collective-permute-done | bytes 32800 | tf_op jit(solution)/shard_map/ppermute | solution.py:671
  3.3 0.1 shard_map.150
  3.4 3.0 %collective-permute-start.2 = (f32[6,32,128]{2,1,0:T(8,128)S(1)}, f32[6,32,128]{2,1,0:T(8,128)S(1)}, u32[]{:S(2)}, u32[]{:S(2)}) collective-permute-start(f32[6,32,128]{2,1,0:T(8,128)S(1)} %get-tuple-element.54), channel_id=1, source_target_pairs={{0,4},{1,5},{2,6},{3,7},{4,0},{5,1},{6,2},{7,3},{8,12},{9,13},{10,... | collective-permute-start | bytes 294920 | tf_op jit(solution)/shard_map/ppermute | solution.py:641
  6.4 1.5 %collective-permute-start.1 = (f32[17,8,128]{2,1,0:T(8,128)S(1)}, f32[17,8,128]{2,1,0:T(8,128)S(1)}, u32[]{:S(2)}, u32[]{:S(2)}) collective-permute-start(f32[17,8,128]{2,1,0:T(8,128)S(1)} %get-tuple-element.46), channel_id=1, source_target_pairs={{0,2},{1,3},{2,0},{3,1},{4,6},{5,7},{6,4},{7,5},{8,10},{9,11},{10,... | collective-permute-start | bytes 208904 | tf_op jit(solution)/shard_map/ppermute | solution.py:641
  7.9 3.1 %collective-permute-start.4 = (f32[4,8,128]{2,1,0:T(8,128)S(1)}, f32[4,8,128]{2,1,0:T(8,128)S(1)}, u32[]{:S(2)}, u32[]{:S(2)}) collective-permute-start(f32[4,8,128]{2,1,0:T(8,128)S(1)} %get-tuple-element.56), channel_id=1, source_target_pairs={{0,6},{1,7},{2,4},{3,5},{4,2},{5,3},{6,0},{7,1},{8,14},{9,15},{10,... | collective-permute-start | bytes 49160 | tf_op jit(solution)/shard_map/ppermute | solution.py:641
  11.1 1.5 %shard_map.149 = (s32[512,128]{1,0:T(8,128)S(1)}, s32[512,128]{1,0:T(8,128)S(1)}) custom-call(f32[2,8,128]{2,1,0:T(8,128)S(1)} %get-tuple-element.40.after_ref.stat_ref, s32[512,128]{1,0:T(8,128)S(1)} %bitcast.8, s32[160,128]{1,0:T(8,128)S(1)} %bitcast.13), custom_call_target="tpu_custom_call" | custom-call | flops 6000000 | bytes 6000000 | tf_op jit(solution)/shard_map/pallas_call | solution.py:673
  12.6 0.9 %shard_map.151 = (f32[16,48,128]{2,1,0:T(8,128)S(1)}, f32[16,48,128]{2,1,0:T(8,128)S(1)}, f32[16,48,128]{2,1,0:T(8,128)S(1)}, f32[16,48,128]{2,1,0:T(8,128)S(1)}...) custom-call(f32[16,32,128]{2,1,0:T(8,128)S(1)} %copy-done, ...), custom_call_target="tpu_custom_call" | custom-call | flops 6000000 | bytes 6000000 | tf_op jit(solution)/shard_map/pallas_call | solution.py:693
  13.5 0.7 %shard_map.152 = (f32[6,48,128]{2,1,0:T(8,128)S(1)}, f32[6,48,128]{2,1,0:T(8,128)S(1)}, f32[6,48,128]{2,1,0:T(8,128)S(1)}, f32[3,48,256]{2,1,0:T(8,128)S(1)}, f3...) custom-call(s32[512,128]{1,0:T(8,128)S(1)} %get-tuple-element.41.after_ref.plan_ref, f32[16,32,128]{2,1,0:T(8,128)S(1)} %copy-done, ...), custom_call_target="tpu_custom_call" | custom-call | flops 2000000 | bytes 2000000 | tf_op jit(solution)/shard_map/pallas_call | solution.py:700
  14.2 0.6 %collective-permute-start.6 = (f32[8,128]{1,0:T(8,128)S(1)}, f32[8,128]{1,0:T(8,128)S(1)}, u32[]{:S(2)}, u32[]{:S(2)}) collective-permute-start(f32[8,128]{1,0:T(8,128)S(1)} %get-tuple-element.58.after_ref.a_ref), channel_id=1, source_target_pairs={{0,1},{1,0},{2,3},{3,2},{4,5},{5,4},{6,7},{7,6},{8,9},{9,8},{10,11... | collective-permute-start | bytes 12296 | tf_op jit(solution)/shard_map/ppermute | solution.py:727
  14.8 0.7 %shard_map.153.after_ref.refs_0_ = f32[256,128]{1,0:T(8,128)S(1)} custom-call(f32[8,128]{1,0:T(8,128)S(1)} %get-tuple-element.58.after_ref.a_ref, f32[8,128]{1,0:T(8,128)S(1)} %get-tuple-element.59.where_ref, f32[16,48,128]{2,1,0:T(8,128)S(1)} %get-tuple-element.47.a_ref.inside_ref, f32[6,48,128]{2,1,0:T(8,128)S(1)} %get-tuple-element.60.edge_ref, ...), custom_call_target="tpu_custom_call" | custom-call | flops 6000000 | bytes 6000000 | tf_op jit(solution)/shard_map/pallas_call | solution.py:716
  15.6 1.5 %collective-permute-start.7 = (f32[8,128]{1,0:T(8,128)S(1)}, f32[8,128]{1,0:T(8,128)S(1)}, u32[]{:S(2)}, u32[]{:S(2)}) collective-permute-start(f32[8,128]{1,0:T(8,128)S(1)} %shard_map.154.after_ref.a_ref), channel_id=1, source_target_pairs={{0,2},{2,0},{1,3},{3,1},{4,6},{6,4},{5,7},{7,5},{8,10},{10,8},{9,1... | collective-permute-start | bytes 12296 | tf_op jit(solution)/shard_map/ppermute | solution.py:727
  17.1 0.8 %shard_map.155.after_ref.refs_1_ = f32[256,128]{1,0:T(8,128)S(1)} custom-call(f32[8,128]{1,0:T(8,128)S(1)} %shard_map.154.after_ref.a_ref, f32[8,128]{1,0:T(8,128)S(1)} %get-tuple-element.59.where_ref, f32[16,48,128]{2,1,0:T(8,128)S(1)} %get-tuple-element.49.b_ref.inside_ref, f32[6,48,128]{2,1,0:T(8,128)S(1)} %get-tuple-element.63.edge_ref.eb_ref, ...), custom_call_target="tpu_custom_call" | custom-call | flops 6000000 | bytes 6000000 | tf_op jit(solution)/shard_map/pallas_call | solution.py:716
  17.9 0.8 %shard_map.156.after_ref.refs_2_ = f32[256,128]{1,0:T(8,128)S(1)} custom-call(f32[256,128]{1,0:T(8,128)S(1)} %shard_map.155.after_ref.refs_1_, f32[8,128]{1,0:T(8,128)S(1)} %get-tuple-element.59.where_ref, f32[16,48,128]{2,1,0:T(8,128)S(1)} %get-tuple-element.50.c_ref.inside_ref, f32[6,48,128]{2,1,0:T(8,128)S(1)} %get-tuple-element.64.edge_ref.ec_ref, ...), custom_call_target="tpu_custom_call" | custom-call | flops 6000000 | bytes 6000000 | tf_op jit(solution)/shard_map/pallas_call | solution.py:716
  18.7 0.6 %collective-permute-done.7.b_ref = f32[8,128]{1,0:T(8,128)S(1)} collective-permute-done((f32[8,128]{1,0:T(8,128)S(1)}, f32[8,128]{1,0:T(8,128)S(1)}, u32[]{:S(2)}, u32[]{:S(2)}) %collective-permute-start.7) | collective-permute-done | bytes 4128 | tf_op jit(solution)/shard_map/ppermute | solution.py:727
  19.3 2.2 %collective-permute-start.8 = (f32[200,128]{1,0:T(8,128)S(1)}, f32[200,128]{1,0:T(8,128)S(1)}, u32[]{:S(2)}, u32[]{:S(2)}) collective-permute-start(f32[200,128]{1,0:T(8,128)S(1)} %get-tuple-element.70), channel_id=1, source_target_pairs={{0,4},{1,5},{2,6},{3,7},{4,12},{5,13},{6,14},{7,15},{8,0},{9,1},{1... | collective-permute-start | bytes 307208 | tf_op jit(solution)/shard_map/ppermute | solution.py:641
  21.5 1.5 %collective-permute-start.10 = (f32[104,128]{1,0:T(8,128)S(1)}, f32[104,128]{1,0:T(8,128)S(1)}, u32[]{:S(2)}, u32[]{:S(2)}) collective-permute-start(f32[104,128]{1,0:T(8,128)S(1)} %get-tuple-element.72), channel_id=1, source_target_pairs={{0,8},{1,9},{2,10},{3,11},{4,0},{5,1},{6,2},{7,3},{8,12},{9,13},{1... | collective-permute-start | bytes 159752 | tf_op jit(solution)/shard_map/ppermute | solution.py:641
  23.1 0.5 %collective-permute-start.11 = (f32[96,128]{1,0:T(8,128)S(1)}, f32[96,128]{1,0:T(8,128)S(1)}, u32[]{:S(2)}, u32[]{:S(2)}) collective-permute-start(f32[96,128]{1,0:T(8,128)S(1)} %get-tuple-element.73), channel_id=1, source_target_pairs={{0,4},{1,5},{2,6},{3,7},{4,0},{5,1},{6,2},{7,3},{8,12},{9,13},{10,... | collective-permute-start | bytes 147464 | tf_op jit(solution)/shard_map/ppermute | solution.py:641
  23.6 1.7 %collective-permute-start.12 = (f32[8,128]{1,0:T(8,128)S(1)}, f32[8,128]{1,0:T(8,128)S(1)}, u32[]{:S(2)}, u32[]{:S(2)}) collective-permute-start(f32[8,128]{1,0:T(8,128)S(1)} %shard_map.157.total_ref), channel_id=1, source_target_pairs={{0,12},{1,13},{2,14},{3,15},{4,5},{5,4},{6,7},{7,6},{8,9},{9,8},{1... | collective-permute-start | bytes 12296 | tf_op jit(solution)/shard_map/ppermute | solution.py:641
  25.3 0.6 %copy-done.7 = f32[20]{0:T(128)S(1)} copy-done((f32[20]{0:T(128)S(1)}, f32[20]{0:T(128)}, u32[]{:S(2)}) %copy-start.7) | copy-done | bytes 104
  25.9 1.9 %shard_map.159 = (f32[20,64,128]{2,1,0:T(8,128)S(1)}, f32[64,128]{1,0:T(8,128)S(1)}, f32[64,128]{1,0:T(8,128)S(1)}, f32[2,20,128]{2,1,0:T(8,128)S(1)}) custom-call(f32[20]{0:T(128)S(1)} %copy-done.7, f32[20]{0:T(128)S(1)} %copy-done.8, f32[20]{0:T(128)S(1)} %copy-done.9, f32[20]{0:T(128)S(1)} %copy-done.10, f32[20]{0:T(128)S(1)} %copy-done.11, ...), custom_call_target="tpu_custom_call" | custom-call | flops 6000000 | bytes 6000000 | tf_op jit(solution)/shard_map/pallas_call | solution.py:762
  27.8 1.1 %collective-permute-done.12.refs_5_ = f32[8,128]{1,0:T(8,128)S(1)} collective-permute-done((f32[8,128]{1,0:T(8,128)S(1)}, f32[8,128]{1,0:T(8,128)S(1)}, u32[]{:S(2)}, u32[]{:S(2)}) %collective-permute-start.12) | collective-permute-done | bytes 4128 | tf_op jit(solution)/shard_map/ppermute | solution.py:641
  29.0 1.3 %shard_map.160 = (f32[16,32,128]{2,1,0:T(8,128)}, f32[64,128]{1,0:T(8,128)}, f32[20,64,128]{2,1,0:T(8,128)}) custom-call(f32[2,20,128]{2,1,0:T(8,128)S(1)} %get-tuple-element.66.coef_ref, f32[64,128]{1,0:T(8,128)S(1)} %bitcast.14, f32[64,128]{1,0:T(8,128)S(1)} %bitcast.12, f32[64,128]{1,0:T(8,128)S(1)} %get-tuple-element.67.sum_ref, ...), custom_call_target="tpu_custom_call" | custom-call | flops 2000000 | bytes 2000000 | tf_op jit(solution)/shard_map/pallas_call | solution.py:775
  (39 shorter events, 0.2 us)
Async XLA Ops:
  2.0 1.4 %collective-permute-start = (f32[2,32,128]{2,1,0:T(8,128)S(1)}, f32[2,32,128]{2,1,0:T(8,128)S(1)}, u32[]{:S(2)}, u32[]{:S(2)}) collective-permute-start(f32[2,32,128]{2,1,0:T(8,128)S(1)} %get-tuple-element.44.own_ref), channel_id=1, source_target_pairs={{0,1},{1,0},{2,3},{3,2},{4,5},{5,4},{6,7},{7,6},{8,9},{9,8},{10,11... | collective-permute-start | bytes 98312 | tf_op jit(solution)/shard_map/ppermute | solution.py:671
  3.3 7.7 %copy-start.1 = (s32[16,32,128]{2,1,0:T(8,128)S(1)}, s32[16,32,128]{2,1,0:T(8,128)}, u32[]{:S(2)}) copy-start(s32[16,32,128]{2,1,0:T(8,128)} %label_ref.1) | copy-start | bytes 786436
  3.3 7.7 %copy-start.5 = (s32[1,1,1,20480]{3,2,1,0:T(1,128)S(1)}, s32[1,1,1,20480]{3,2,1,0:T(1,128)}, u32[]{:S(2)}) copy-start(s32[1,1,1,20480]{3,2,1,0:T(1,128)} %param.16) | copy-start | bytes 245764
  3.4 9.2 %copy-start = (f32[16,32,128]{2,1,0:T(8,128)S(1)}, f32[16,32,128]{2,1,0:T(8,128)}, u32[]{:S(2)}) copy-start(f32[16,32,128]{2,1,0:T(8,128)} %right_ref.5) | copy-start | bytes 786436
  3.4 10.1 %collective-permute-start.2 = (f32[6,32,128]{2,1,0:T(8,128)S(1)}, f32[6,32,128]{2,1,0:T(8,128)S(1)}, u32[]{:S(2)}, u32[]{:S(2)}) collective-permute-start(f32[6,32,128]{2,1,0:T(8,128)S(1)} %get-tuple-element.54), channel_id=1, source_target_pairs={{0,4},{1,5},{2,6},{3,7},{4,0},{5,1},{6,2},{7,3},{8,12},{9,13},{10,... | collective-permute-start | bytes 294920 | tf_op jit(solution)/shard_map/ppermute | solution.py:641
  6.4 7.1 %collective-permute-start.3 = (f32[6,32,128]{2,1,0:T(8,128)S(1)}, f32[6,32,128]{2,1,0:T(8,128)S(1)}, u32[]{:S(2)}, u32[]{:S(2)}) collective-permute-start(f32[6,32,128]{2,1,0:T(8,128)S(1)} %get-tuple-element.55), channel_id=1, source_target_pairs={{0,1},{1,0},{2,3},{3,2},{4,8},{5,9},{6,10},{7,11},{8,4},{9,5},{10,... | collective-permute-start | bytes 294920 | tf_op jit(solution)/shard_map/ppermute | solution.py:641
  6.4 6.1 %collective-permute-start.1 = (f32[17,8,128]{2,1,0:T(8,128)S(1)}, f32[17,8,128]{2,1,0:T(8,128)S(1)}, u32[]{:S(2)}, u32[]{:S(2)}) collective-permute-start(f32[17,8,128]{2,1,0:T(8,128)S(1)} %get-tuple-element.46), channel_id=1, source_target_pairs={{0,2},{1,3},{2,0},{3,1},{4,6},{5,7},{6,4},{7,5},{8,10},{9,11},{10,... | collective-permute-start | bytes 208904 | tf_op jit(solution)/shard_map/ppermute | solution.py:641
  7.9 5.6 %collective-permute-start.4 = (f32[4,8,128]{2,1,0:T(8,128)S(1)}, f32[4,8,128]{2,1,0:T(8,128)S(1)}, u32[]{:S(2)}, u32[]{:S(2)}) collective-permute-start(f32[4,8,128]{2,1,0:T(8,128)S(1)} %get-tuple-element.56), channel_id=1, source_target_pairs={{0,6},{1,7},{2,4},{3,5},{4,2},{5,3},{6,0},{7,1},{8,14},{9,15},{10,... | collective-permute-start | bytes 49160 | tf_op jit(solution)/shard_map/ppermute | solution.py:641
  11.0 2.5 %collective-permute-start.5 = (f32[4,8,128]{2,1,0:T(8,128)S(1)}, f32[4,8,128]{2,1,0:T(8,128)S(1)}, u32[]{:S(2)}, u32[]{:S(2)}) collective-permute-start(f32[4,8,128]{2,1,0:T(8,128)S(1)} %get-tuple-element.57), channel_id=1, source_target_pairs={{0,1},{1,0},{2,3},{3,2},{4,10},{5,11},{6,8},{7,9},{8,6},{9,7},{10,... | collective-permute-start | bytes 49160 | tf_op jit(solution)/shard_map/ppermute | solution.py:641
  14.2 1.4 %collective-permute-start.6 = (f32[8,128]{1,0:T(8,128)S(1)}, f32[8,128]{1,0:T(8,128)S(1)}, u32[]{:S(2)}, u32[]{:S(2)}) collective-permute-start(f32[8,128]{1,0:T(8,128)S(1)} %get-tuple-element.58.after_ref.a_ref), channel_id=1, source_target_pairs={{0,1},{1,0},{2,3},{3,2},{4,5},{5,4},{6,7},{7,6},{8,9},{9,8},{10,11... | collective-permute-start | bytes 12296 | tf_op jit(solution)/shard_map/ppermute | solution.py:727
  15.6 3.6 %collective-permute-start.7 = (f32[8,128]{1,0:T(8,128)S(1)}, f32[8,128]{1,0:T(8,128)S(1)}, u32[]{:S(2)}, u32[]{:S(2)}) collective-permute-start(f32[8,128]{1,0:T(8,128)S(1)} %shard_map.154.after_ref.a_ref), channel_id=1, source_target_pairs={{0,2},{2,0},{1,3},{3,1},{4,6},{6,4},{5,7},{7,5},{8,10},{10,8},{9,1... | collective-permute-start | bytes 12296 | tf_op jit(solution)/shard_map/ppermute | solution.py:727
  17.9 7.3 %copy-start.2 = (f32[20,1,8192]{2,1,0:T(1,128)S(1)}, f32[20,1,8192]{2,1,0:T(1,128)}, u32[]{:S(2)}) copy-start(f32[20,1,8192]{2,1,0:T(1,128)} %param.18) | copy-start | bytes 1966084
  17.9 7.3 %copy-start.3 = (f32[20,1,8192]{2,1,0:T(1,128)S(1)}, f32[20,1,8192]{2,1,0:T(1,128)}, u32[]{:S(2)}) copy-start(f32[20,1,8192]{2,1,0:T(1,128)} %param.20) | copy-start | bytes 1966084
  19.3 6.0 %copy-start.4 = (f32[1,8192]{1,0:T(1,128)S(1)}, f32[1,8192]{1,0:T(1,128)}, u32[]{:S(2)}) copy-start(f32[1,8192]{1,0:T(1,128)} %param.17) | copy-start | bytes 98308
  19.3 6.0 %copy-start.10 = (f32[20]{0:T(128)S(1)}, f32[20]{0:T(128)}, u32[]{:S(2)}) copy-start(f32[20]{0:T(128)} %cond_ref.1) | copy-start | bytes 244
  19.3 6.0 %copy-start.11 = (f32[20]{0:T(128)S(1)}, f32[20]{0:T(128)}, u32[]{:S(2)}) copy-start(f32[20]{0:T(128)} %rev_ref.1) | copy-start | bytes 244
  19.3 9.7 %collective-permute-start.8 = (f32[200,128]{1,0:T(8,128)S(1)}, f32[200,128]{1,0:T(8,128)S(1)}, u32[]{:S(2)}, u32[]{:S(2)}) collective-permute-start(f32[200,128]{1,0:T(8,128)S(1)} %get-tuple-element.70), channel_id=1, source_target_pairs={{0,4},{1,5},{2,6},{3,7},{4,12},{5,13},{6,14},{7,15},{8,0},{9,1},{1... | collective-permute-start | bytes 307208 | tf_op jit(solution)/shard_map/ppermute | solution.py:641
  21.5 7.5 %collective-permute-start.9 = (f32[200,128]{1,0:T(8,128)S(1)}, f32[200,128]{1,0:T(8,128)S(1)}, u32[]{:S(2)}, u32[]{:S(2)}) collective-permute-start(f32[200,128]{1,0:T(8,128)S(1)} %get-tuple-element.71), channel_id=1, source_target_pairs={{0,1},{1,0},{2,3},{3,2},{4,8},{5,9},{6,10},{7,11},{8,4},{9,5},{10,... | collective-permute-start | bytes 307208 | tf_op jit(solution)/shard_map/ppermute | solution.py:641
  21.5 7.4 %collective-permute-start.10 = (f32[104,128]{1,0:T(8,128)S(1)}, f32[104,128]{1,0:T(8,128)S(1)}, u32[]{:S(2)}, u32[]{:S(2)}) collective-permute-start(f32[104,128]{1,0:T(8,128)S(1)} %get-tuple-element.72), channel_id=1, source_target_pairs={{0,8},{1,9},{2,10},{3,11},{4,0},{5,1},{6,2},{7,3},{8,12},{9,13},{1... | collective-permute-start | bytes 159752 | tf_op jit(solution)/shard_map/ppermute | solution.py:641
  23.1 5.9 %collective-permute-start.11 = (f32[96,128]{1,0:T(8,128)S(1)}, f32[96,128]{1,0:T(8,128)S(1)}, u32[]{:S(2)}, u32[]{:S(2)}) collective-permute-start(f32[96,128]{1,0:T(8,128)S(1)} %get-tuple-element.73), channel_id=1, source_target_pairs={{0,4},{1,5},{2,6},{3,7},{4,0},{5,1},{6,2},{7,3},{8,12},{9,13},{10,... | collective-permute-start | bytes 147464 | tf_op jit(solution)/shard_map/ppermute | solution.py:641
  23.6 5.4 %collective-permute-start.12 = (f32[8,128]{1,0:T(8,128)S(1)}, f32[8,128]{1,0:T(8,128)S(1)}, u32[]{:S(2)}, u32[]{:S(2)}) collective-permute-start(f32[8,128]{1,0:T(8,128)S(1)} %shard_map.157.total_ref), channel_id=1, source_target_pairs={{0,12},{1,13},{2,14},{3,15},{4,5},{5,4},{6,7},{7,6},{8,9},{9,8},{1... | collective-permute-start | bytes 12296 | tf_op jit(solution)/shard_map/ppermute | solution.py:641
  25.2 0.7 %copy-start.8 = (f32[20]{0:T(128)S(1)}, f32[20]{0:T(128)}, u32[]{:S(2)}) copy-start(f32[20]{0:T(128)} %slope_ref.1) | copy-start | bytes 244
  25.2 0.7 %copy-start.9 = (f32[20]{0:T(128)S(1)}, f32[20]{0:T(128)}, u32[]{:S(2)}) copy-start(f32[20]{0:T(128)} %tau_ref.1) | copy-start | bytes 244
  25.9 3.1 %copy-start.6 = (f32[1,8192]{1,0:T(1,128)S(1)}, f32[1,8192]{1,0:T(1,128)}, u32[]{:S(2)}) copy-start(f32[1,8192]{1,0:T(1,128)} %param.19) | copy-start | bytes 98308
  (1 other events, 0.7 us)

commit v20 on v19

--- a/solution.py
+++ b/solution.py
@@ -524,13 +524,13 @@
         out_ref[out_ref.shape[0] - SUB :] = total_ref[...]
 
 
-def land_round(own_ref, round_ref, middle_ref, back_ref, rest_ref, edge_ref):
+def land_round(own_ref, middle_ref, round_ref, back_ref, rest_ref):
     size = (own_ref.shape[0] - SUB) // 3
     half = size // 2
     gx = lax.axis_index("gx")
     inside = (gx == 1) | (gx == 2)
     last = lambda ref: ref[ref.shape[0] - SUB :]
-    total = last(own_ref) + last(round_ref) + last(back_ref) + jnp.where(inside, last(middle_ref), edge_ref[...])
+    total = last(own_ref) + last(round_ref) + last(back_ref) + last(middle_ref)
     parts = []
     for k in range(3):
         whole = slice(k * size, k * size + size)
@@ -638,6 +638,16 @@
             for z in range(n_z):
                 to = (x, y, z ^ 1) if alone else (to_x, to_y, z)
                 pairs.append(((x * n_y + y) * n_z + z, (to[0] * n_y + to[1]) * n_z + to[2]))
+    return lax.ppermute(value, ("gx", "gy", "gz"), pairs)
+
+
+def swap_by(value, to):
+    n_x, n_y, n_z = [lax.axis_size(axis) for axis in ("gx", "gy", "gz")]
+    pairs = []
+    for x in range(n_x):
+        for y in range(n_y):
+            to_x, to_y = to(x, y)
+            pairs += [((x * n_y + y) * n_z + z, (to_x * n_y + to_y) * n_z + z) for z in range(n_z)]
     return lax.ppermute(value, ("gx", "gy", "gz"), pairs)
 
 
@@ -731,9 +741,14 @@
     sums = add(sums, "gz", 1, list0)
     list1 = couple(1, sums, in1, ends1)
     list2 = couple(2, list1, in2, ends2)
-    for step in [2**k for k in range(n_gy.bit_length() - 1)]:
-        sums = add(sums, "gy", step, list2)
-    if n_gx == 4 and 2 * slot_rows == 5 * block_rows:
+    rounds = n_gx == 4 and n_gy == 2 and 2 * slot_rows == 5 * block_rows
+    if rounds:
+        other = swap_by(sums, lambda x, y: (x if x in (1, 2) else 3 - x, 1 - y))
+        sums = call(add_kernel, shape_of(SUB, nz), 3)(sums, other, list2)
+    else:
+        for step in [2**k for k in range(n_gy.bit_length() - 1)]:
+            sums = add(sums, "gy", step, list2)
+    if rounds:
         own, ahead, middle, back, rest = call(
             pack_round_kernel,
             (shape_of(3 * block_rows + SUB, LANES),) * 3
@@ -742,11 +757,10 @@
         )(sums, list0, list1, list2)
         arrived = [
             own,
+            swap_by(middle, lambda x, y: (3 - x, y) if x in (1, 2) else (x, 1 - y)),
             swap(ahead, x_to=ROUND),
-            swap(middle, x_to=partners("gx", 1)),
             swap(back, x_to=BACK),
             swap(rest, x_to=partners("gx", 0)),
-            swap(sums, x_to=[3, 1, 2, 0]),
         ]
         land = land_round
     else:

time: 30.5 us -> 32.1 us (1.052)
  waiting for transfers between devices: 2.67 us -> 5.36 us
  starting transfers between devices: 16.1 us -> 15 us
    ppermute x0 -> x2, starting transfers between devices: none -> 3.4 us  [swap_by(): return lax.ppermute(value, ('gx', 'gy', 'gz'), pairs)]
    ppermute x10 -> x8, starting transfers between devices: 13.5 us -> 10.5 us  [swap(): return lax.ppermute(value, ('gx', 'gy', 'gz'), pairs)]
    ppermute x0 -> x2, waiting for transfers between devices: none -> 2.93 us  [swap_by(): return lax.ppermute(value, ('gx', 'gy', 'gz'), pairs)]
    ppermute x2 -> x1, starting transfers between devices: 2.07 us -> 0.57 us  [add(): lax.ppermute(value, axis, [(i, i ^ step) for i in range(lax.axis_size(axi...]
    ppermute x2 -> x1, waiting for transfers between devices: 0.65 us -> 0.07 us  [add(): lax.ppermute(value, axis, [(i, i ^ step) for i in range(lax.axis_size(axi...]
    ppermute x10 -> x8, waiting for transfers between devices: 1.16 us -> 1.5 us  [swap(): return lax.ppermute(value, ('gx', 'gy', 'gz'), pairs)]
  transfers between devices with their start and end apart: 13 -> 12, of which waited for: 4 -> 4; matrix products, arithmetic and copies ran while one was open for 0% -> 0% of each run, Pallas kernels for 22% -> 21%
where the time goes in v20:
time: 32.1 us; the launch traced here: 31.9 us
  starting transfers between devices  15 us (47%)
  Pallas kernels  10.1 us (31%)
  waiting for transfers between devices  5.36 us (17%)
  between operations  0.83 us (3%)
  local copies, waits for them, and re-layouts  0.67 us (2%)
    ppermute x8, starting transfers between devices, swap(): return lax.ppermute(value, ('gx', 'gy', 'gz'), pairs)  10.5 us
    ppermute x2, starting transfers between devices, swap_by(): return lax.ppermute(value, ('gx', 'gy', 'gz'), pairs)  3.4 us
    ppermute x2, waiting for transfers between devices, swap_by(): return lax.ppermute(value, ('gx', 'gy', 'gz'), pairs)  2.93 us
    pallas_call x3, Pallas kernels, couple(): call(functools.partial(couple_kernel, stage, slot_rows), shape_of(n_gx *...  2.25 us
    pallas_call x1, Pallas kernels, local(): call(membrane_kernel, (shape_of(n_states, block_rows, LANES), shape_of(bl...  1.91 us
    pallas_call x1, Pallas kernels, local(): call(plan_kernel, (cells_shape, cells_shape), 3, cost=6000000)  1.51 us
    ppermute x8, waiting for transfers between devices, swap(): return lax.ppermute(value, ('gx', 'gy', 'gz'), pairs)  1.5 us
    pallas_call x1, Pallas kernels, local(): call(functools.partial(finish_kernel, land), (block, shape_of(block_rows,...  1.32 us
  transfers between devices with their start and end apart: 12, of which 4 were waited for; matrix products, arithmetic and copies ran while one was open for 0% of the time, Pallas kernels for 21%

profile of v20, /device:TPU:0, one launch (start us, length us, event | category | flops | bytes accessed | tf_op | source)
XLA Modules:
  0.0 31.9 jit_solution(9040327984012266416)
XLA Ops:
  0.6 1.3 %shard_map.148 = (f32[16,32,128]{2,1,0:T(8,128)S(1)}, f32[16,32,128]{2,1,0:T(8,128)S(1)}, f32[2,32,128]{2,1,0:T(8,128)S(1)}, f32[2,8,128]{2,1,0:T(8,128)S(1)}) custom-call(f32[16,32,128]{2,1,0:T(8,128)} %right_ref.5, f32[16,32,128]{2,1,0:T(8,128)} %damping_ref.1, s32[16,32,128]{2,1,0:T(8,128)} %label_ref.1), custom_call_target="tpu_custom_call" | custom-call | flops 2000000 | bytes 2000000 | tf_op jit(solution)/shard_map/pallas_call | solution.py:677
  2.0 0.5 %collective-permute-start = (f32[2,32,128]{2,1,0:T(8,128)S(1)}, f32[2,32,128]{2,1,0:T(8,128)S(1)}, u32[]{:S(2)}, u32[]{:S(2)}) collective-permute-start(f32[2,32,128]{2,1,0:T(8,128)S(1)} %get-tuple-element.44.own_ref), channel_id=1, source_target_pairs={{0,1},{1,0},{2,3},{3,2},{4,5},{5,4},{6,7},{7,6},{8,9},{9,8},{10,11... | collective-permute-start | bytes 98312 | tf_op jit(solution)/shard_map/ppermute | solution.py:681
  2.5 0.9 %collective-permute-done.got_ref = f32[2,32,128]{2,1,0:T(8,128)S(1)} collective-permute-done((f32[2,32,128]{2,1,0:T(8,128)S(1)}, f32[2,32,128]{2,1,0:T(8,128)S(1)}, u32[]{:S(2)}, u32[]{:S(2)}) %collective-permute-start) | collective-permute-done | bytes 32800 | tf_op jit(solution)/shard_map/ppermute | solution.py:681
  3.3 0.1 shard_map.150
  3.4 3.0 %collective-permute-start.2 = (f32[6,32,128]{2,1,0:T(8,128)S(1)}, f32[6,32,128]{2,1,0:T(8,128)S(1)}, u32[]{:S(2)}, u32[]{:S(2)}) collective-permute-start(f32[6,32,128]{2,1,0:T(8,128)S(1)} %get-tuple-element.54), channel_id=1, source_target_pairs={{0,4},{1,5},{2,6},{3,7},{4,0},{5,1},{6,2},{7,3},{8,12},{9,13},{10,... | collective-permute-start | bytes 294920 | tf_op jit(solution)/shard_map/ppermute | solution.py:641
  6.4 1.5 %collective-permute-start.1 = (f32[17,8,128]{2,1,0:T(8,128)S(1)}, f32[17,8,128]{2,1,0:T(8,128)S(1)}, u32[]{:S(2)}, u32[]{:S(2)}) collective-permute-start(f32[17,8,128]{2,1,0:T(8,128)S(1)} %get-tuple-element.46), channel_id=1, source_target_pairs={{0,2},{1,3},{2,0},{3,1},{4,6},{5,7},{6,4},{7,5},{8,10},{9,11},{10,... | collective-permute-start | bytes 208904 | tf_op jit(solution)/shard_map/ppermute | solution.py:641
  7.9 3.1 %collective-permute-start.4 = (f32[4,8,128]{2,1,0:T(8,128)S(1)}, f32[4,8,128]{2,1,0:T(8,128)S(1)}, u32[]{:S(2)}, u32[]{:S(2)}) collective-permute-start(f32[4,8,128]{2,1,0:T(8,128)S(1)} %get-tuple-element.56), channel_id=1, source_target_pairs={{0,6},{1,7},{2,4},{3,5},{4,2},{5,3},{6,0},{7,1},{8,14},{9,15},{10,... | collective-permute-start | bytes 49160 | tf_op jit(solution)/shard_map/ppermute | solution.py:641
  11.1 1.5 %shard_map.149 = (s32[512,128]{1,0:T(8,128)S(1)}, s32[512,128]{1,0:T(8,128)S(1)}) custom-call(f32[2,8,128]{2,1,0:T(8,128)S(1)} %get-tuple-element.40.after_ref.stat_ref, s32[512,128]{1,0:T(8,128)S(1)} %bitcast.8, s32[160,128]{1,0:T(8,128)S(1)} %bitcast.13), custom_call_target="tpu_custom_call" | custom-call | flops 6000000 | bytes 6000000 | tf_op jit(solution)/shard_map/pallas_call | solution.py:683
  12.6 0.9 %shard_map.151 = (f32[16,48,128]{2,1,0:T(8,128)S(1)}, f32[16,48,128]{2,1,0:T(8,128)S(1)}, f32[16,48,128]{2,1,0:T(8,128)S(1)}, f32[16,48,128]{2,1,0:T(8,128)S(1)}...) custom-call(f32[16,32,128]{2,1,0:T(8,128)S(1)} %copy-done, ...), custom_call_target="tpu_custom_call" | custom-call | flops 6000000 | bytes 6000000 | tf_op jit(solution)/shard_map/pallas_call | solution.py:703
  13.5 0.7 %shard_map.152 = (f32[6,48,128]{2,1,0:T(8,128)S(1)}, f32[6,48,128]{2,1,0:T(8,128)S(1)}, f32[6,48,128]{2,1,0:T(8,128)S(1)}, f32[3,48,256]{2,1,0:T(8,128)S(1)}, f3...) custom-call(s32[512,128]{1,0:T(8,128)S(1)} %get-tuple-element.41.after_ref.plan_ref, f32[16,32,128]{2,1,0:T(8,128)S(1)} %copy-done, ...), custom_call_target="tpu_custom_call" | custom-call | flops 2000000 | bytes 2000000 | tf_op jit(solution)/shard_map/pallas_call | solution.py:710
  14.2 0.6 %collective-permute-start.6 = (f32[8,128]{1,0:T(8,128)S(1)}, f32[8,128]{1,0:T(8,128)S(1)}, u32[]{:S(2)}, u32[]{:S(2)}) collective-permute-start(f32[8,128]{1,0:T(8,128)S(1)} %get-tuple-element.58.after_ref.a_ref), channel_id=1, source_target_pairs={{0,1},{1,0},{2,3},{3,2},{4,5},{5,4},{6,7},{7,6},{8,9},{9,8},{10,11... | collective-permute-start | bytes 12296 | tf_op jit(solution)/shard_map/ppermute | solution.py:737
  14.8 0.7 %shard_map.153.after_ref.refs_0_ = f32[256,128]{1,0:T(8,128)S(1)} custom-call(f32[8,128]{1,0:T(8,128)S(1)} %get-tuple-element.58.after_ref.a_ref, f32[8,128]{1,0:T(8,128)S(1)} %get-tuple-element.59.where_ref, f32[16,48,128]{2,1,0:T(8,128)S(1)} %get-tuple-element.47.a_ref.inside_ref, f32[6,48,128]{2,1,0:T(8,128)S(1)} %get-tuple-element.60.edge_ref, ...), custom_call_target="tpu_custom_call" | custom-call | flops 6000000 | bytes 6000000 | tf_op jit(solution)/shard_map/pallas_call | solution.py:726
  15.6 0.1 collective-permute-done.6.b_ref
  15.6 1.8 %collective-permute-start.7 = (f32[8,128]{1,0:T(8,128)S(1)}, f32[8,128]{1,0:T(8,128)S(1)}, u32[]{:S(2)}, u32[]{:S(2)}) collective-permute-start(f32[8,128]{1,0:T(8,128)S(1)} %shard_map.154.after_ref.a_ref), channel_id=1, source_target_pairs={{0,14},{1,15},{2,12},{3,13},{4,6},{5,7},{6,4},{7,5},{8,10},{9,11},... | collective-permute-start | bytes 12296 | tf_op jit(solution)/shard_map/ppermute | solution.py:651
  17.5 0.8 %shard_map.155.after_ref.refs_1_ = f32[256,128]{1,0:T(8,128)S(1)} custom-call(f32[8,128]{1,0:T(8,128)S(1)} %shard_map.154.after_ref.a_ref, f32[8,128]{1,0:T(8,128)S(1)} %get-tuple-element.59.where_ref, f32[16,48,128]{2,1,0:T(8,128)S(1)} %get-tuple-element.49.b_ref.inside_ref, f32[6,48,128]{2,1,0:T(8,128)S(1)} %get-tuple-element.63.edge_ref.eb_ref, ...), custom_call_target="tpu_custom_call" | custom-call | flops 6000000 | bytes 6000000 | tf_op jit(solution)/shard_map/pallas_call | solution.py:726
  18.3 0.8 %shard_map.156.after_ref.refs_2_ = f32[256,128]{1,0:T(8,128)S(1)} custom-call(f32[256,128]{1,0:T(8,128)S(1)} %shard_map.155.after_ref.refs_1_, f32[8,128]{1,0:T(8,128)S(1)} %get-tuple-element.59.where_ref, f32[16,48,128]{2,1,0:T(8,128)S(1)} %get-tuple-element.50.c_ref.inside_ref, f32[6,48,128]{2,1,0:T(8,128)S(1)} %get-tuple-element.64.edge_ref.ec_ref, ...), custom_call_target="tpu_custom_call" | custom-call | flops 6000000 | bytes 6000000 | tf_op jit(solution)/shard_map/pallas_call | solution.py:726
  19.0 2.9 %collective-permute-done.7.b_ref = f32[8,128]{1,0:T(8,128)S(1)} collective-permute-done((f32[8,128]{1,0:T(8,128)S(1)}, f32[8,128]{1,0:T(8,128)S(1)}, u32[]{:S(2)}, u32[]{:S(2)}) %collective-permute-start.7) | collective-permute-done | bytes 4128 | tf_op jit(solution)/shard_map/ppermute | solution.py:651
  22.0 1.6 %collective-permute-start.8 = (f32[200,128]{1,0:T(8,128)S(1)}, f32[200,128]{1,0:T(8,128)S(1)}, u32[]{:S(2)}, u32[]{:S(2)}) collective-permute-start(f32[200,128]{1,0:T(8,128)S(1)} %get-tuple-element.70), channel_id=1, source_target_pairs={{0,2},{1,3},{2,0},{3,1},{4,8},{5,9},{6,10},{7,11},{8,4},{9,5},{10,... | collective-permute-start | bytes 307208 | tf_op jit(solution)/shard_map/ppermute | solution.py:651
  23.6 2.9 %collective-permute-start.10 = (f32[104,128]{1,0:T(8,128)S(1)}, f32[104,128]{1,0:T(8,128)S(1)}, u32[]{:S(2)}, u32[]{:S(2)}) collective-permute-start(f32[104,128]{1,0:T(8,128)S(1)} %get-tuple-element.72), channel_id=1, source_target_pairs={{0,8},{1,9},{2,10},{3,11},{4,0},{5,1},{6,2},{7,3},{8,12},{9,13},{1... | collective-permute-start | bytes 159752 | tf_op jit(solution)/shard_map/ppermute | solution.py:641
  26.6 0.6 %copy-done.7 = f32[20]{0:T(128)S(1)} copy-done((f32[20]{0:T(128)S(1)}, f32[20]{0:T(128)}, u32[]{:S(2)}) %copy-start.7) | copy-done | bytes 104
  27.1 0.0 copy-done.8
  27.2 1.9 %shard_map.159 = (f32[20,64,128]{2,1,0:T(8,128)S(1)}, f32[64,128]{1,0:T(8,128)S(1)}, f32[64,128]{1,0:T(8,128)S(1)}, f32[2,20,128]{2,1,0:T(8,128)S(1)}) custom-call(f32[20]{0:T(128)S(1)} %copy-done.7, f32[20]{0:T(128)S(1)} %copy-done.8, f32[20]{0:T(128)S(1)} %copy-done.9, f32[20]{0:T(128)S(1)} %copy-done.10, f32[20]{0:T(128)S(1)} %copy-done.11, ...), custom_call_target="tpu_custom_call" | custom-call | flops 6000000 | bytes 6000000 | tf_op jit(solution)/shard_map/pallas_call | solution.py:776
  29.1 1.5 %collective-permute-done.11.refs_4_ = f32[96,128]{1,0:T(8,128)S(1)} collective-permute-done((f32[96,128]{1,0:T(8,128)S(1)}, f32[96,128]{1,0:T(8,128)S(1)}, u32[]{:S(2)}, u32[]{:S(2)}) %collective-permute-start.11) | collective-permute-done | bytes 49184 | tf_op jit(solution)/shard_map/ppermute | solution.py:641
  30.6 1.3 %shard_map.160 = (f32[16,32,128]{2,1,0:T(8,128)}, f32[64,128]{1,0:T(8,128)}, f32[20,64,128]{2,1,0:T(8,128)}) custom-call(f32[2,20,128]{2,1,0:T(8,128)S(1)} %get-tuple-element.66.coef_ref, f32[64,128]{1,0:T(8,128)S(1)} %bitcast.14, f32[64,128]{1,0:T(8,128)S(1)} %bitcast.12, f32[64,128]{1,0:T(8,128)S(1)} %get-tuple-element.67.sum_ref, ...), custom_call_target="tpu_custom_call" | custom-call | flops 2000000 | bytes 2000000 | tf_op jit(solution)/shard_map/pallas_call | solution.py:789
  (37 shorter events, 0.1 us)
Async XLA Ops:
  2.0 1.4 %collective-permute-start = (f32[2,32,128]{2,1,0:T(8,128)S(1)}, f32[2,32,128]{2,1,0:T(8,128)S(1)}, u32[]{:S(2)}, u32[]{:S(2)}) collective-permute-start(f32[2,32,128]{2,1,0:T(8,128)S(1)} %get-tuple-element.44.own_ref), channel_id=1, source_target_pairs={{0,1},{1,0},{2,3},{3,2},{4,5},{5,4},{6,7},{7,6},{8,9},{9,8},{10,11... | collective-permute-start | bytes 98312 | tf_op jit(solution)/shard_map/ppermute | solution.py:681
  3.3 7.7 %copy-start.1 = (s32[16,32,128]{2,1,0:T(8,128)S(1)}, s32[16,32,128]{2,1,0:T(8,128)}, u32[]{:S(2)}) copy-start(s32[16,32,128]{2,1,0:T(8,128)} %label_ref.1) | copy-start | bytes 786436
  3.3 7.7 %copy-start.5 = (s32[1,1,1,20480]{3,2,1,0:T(1,128)S(1)}, s32[1,1,1,20480]{3,2,1,0:T(1,128)}, u32[]{:S(2)}) copy-start(s32[1,1,1,20480]{3,2,1,0:T(1,128)} %param.16) | copy-start | bytes 245764
  3.4 9.2 %copy-start = (f32[16,32,128]{2,1,0:T(8,128)S(1)}, f32[16,32,128]{2,1,0:T(8,128)}, u32[]{:S(2)}) copy-start(f32[16,32,128]{2,1,0:T(8,128)} %right_ref.5) | copy-start | bytes 786436
  3.4 10.1 %collective-permute-start.2 = (f32[6,32,128]{2,1,0:T(8,128)S(1)}, f32[6,32,128]{2,1,0:T(8,128)S(1)}, u32[]{:S(2)}, u32[]{:S(2)}) collective-permute-start(f32[6,32,128]{2,1,0:T(8,128)S(1)} %get-tuple-element.54), channel_id=1, source_target_pairs={{0,4},{1,5},{2,6},{3,7},{4,0},{5,1},{6,2},{7,3},{8,12},{9,13},{10,... | collective-permute-start | bytes 294920 | tf_op jit(solution)/shard_map/ppermute | solution.py:641
  6.4 7.1 %collective-permute-start.3 = (f32[6,32,128]{2,1,0:T(8,128)S(1)}, f32[6,32,128]{2,1,0:T(8,128)S(1)}, u32[]{:S(2)}, u32[]{:S(2)}) collective-permute-start(f32[6,32,128]{2,1,0:T(8,128)S(1)} %get-tuple-element.55), channel_id=1, source_target_pairs={{0,1},{1,0},{2,3},{3,2},{4,8},{5,9},{6,10},{7,11},{8,4},{9,5},{10,... | collective-permute-start | bytes 294920 | tf_op jit(solution)/shard_map/ppermute | solution.py:641
  6.4 6.1 %collective-permute-start.1 = (f32[17,8,128]{2,1,0:T(8,128)S(1)}, f32[17,8,128]{2,1,0:T(8,128)S(1)}, u32[]{:S(2)}, u32[]{:S(2)}) collective-permute-start(f32[17,8,128]{2,1,0:T(8,128)S(1)} %get-tuple-element.46), channel_id=1, source_target_pairs={{0,2},{1,3},{2,0},{3,1},{4,6},{5,7},{6,4},{7,5},{8,10},{9,11},{10,... | collective-permute-start | bytes 208904 | tf_op jit(solution)/shard_map/ppermute | solution.py:641
  7.9 5.6 %collective-permute-start.4 = (f32[4,8,128]{2,1,0:T(8,128)S(1)}, f32[4,8,128]{2,1,0:T(8,128)S(1)}, u32[]{:S(2)}, u32[]{:S(2)}) collective-permute-start(f32[4,8,128]{2,1,0:T(8,128)S(1)} %get-tuple-element.56), channel_id=1, source_target_pairs={{0,6},{1,7},{2,4},{3,5},{4,2},{5,3},{6,0},{7,1},{8,14},{9,15},{10,... | collective-permute-start | bytes 49160 | tf_op jit(solution)/shard_map/ppermute | solution.py:641
  11.0 2.5 %collective-permute-start.5 = (f32[4,8,128]{2,1,0:T(8,128)S(1)}, f32[4,8,128]{2,1,0:T(8,128)S(1)}, u32[]{:S(2)}, u32[]{:S(2)}) collective-permute-start(f32[4,8,128]{2,1,0:T(8,128)S(1)} %get-tuple-element.57), channel_id=1, source_target_pairs={{0,1},{1,0},{2,3},{3,2},{4,10},{5,11},{6,8},{7,9},{8,6},{9,7},{10,... | collective-permute-start | bytes 49160 | tf_op jit(solution)/shard_map/ppermute | solution.py:641
  14.2 1.4 %collective-permute-start.6 = (f32[8,128]{1,0:T(8,128)S(1)}, f32[8,128]{1,0:T(8,128)S(1)}, u32[]{:S(2)}, u32[]{:S(2)}) collective-permute-start(f32[8,128]{1,0:T(8,128)S(1)} %get-tuple-element.58.after_ref.a_ref), channel_id=1, source_target_pairs={{0,1},{1,0},{2,3},{3,2},{4,5},{5,4},{6,7},{7,6},{8,9},{9,8},{10,11... | collective-permute-start | bytes 12296 | tf_op jit(solution)/shard_map/ppermute | solution.py:737
  15.6 6.3 %collective-permute-start.7 = (f32[8,128]{1,0:T(8,128)S(1)}, f32[8,128]{1,0:T(8,128)S(1)}, u32[]{:S(2)}, u32[]{:S(2)}) collective-permute-start(f32[8,128]{1,0:T(8,128)S(1)} %shard_map.154.after_ref.a_ref), channel_id=1, source_target_pairs={{0,14},{1,15},{2,12},{3,13},{4,6},{5,7},{6,4},{7,5},{8,10},{9,11},... | collective-permute-start | bytes 12296 | tf_op jit(solution)/shard_map/ppermute | solution.py:651
  18.2 8.3 %copy-start.2 = (f32[20,1,8192]{2,1,0:T(1,128)S(1)}, f32[20,1,8192]{2,1,0:T(1,128)}, u32[]{:S(2)}) copy-start(f32[20,1,8192]{2,1,0:T(1,128)} %param.18) | copy-start | bytes 1966084
  18.3 8.3 %copy-start.3 = (f32[20,1,8192]{2,1,0:T(1,128)S(1)}, f32[20,1,8192]{2,1,0:T(1,128)}, u32[]{:S(2)}) copy-start(f32[20,1,8192]{2,1,0:T(1,128)} %param.20) | copy-start | bytes 1966084
  22.0 4.6 %copy-start.4 = (f32[1,8192]{1,0:T(1,128)S(1)}, f32[1,8192]{1,0:T(1,128)}, u32[]{:S(2)}) copy-start(f32[1,8192]{1,0:T(1,128)} %param.17) | copy-start | bytes 98308
  22.0 4.6 %copy-start.10 = (f32[20]{0:T(128)S(1)}, f32[20]{0:T(128)}, u32[]{:S(2)}) copy-start(f32[20]{0:T(128)} %cond_ref.1) | copy-start | bytes 244
  22.0 4.6 %copy-start.11 = (f32[20]{0:T(128)S(1)}, f32[20]{0:T(128)}, u32[]{:S(2)}) copy-start(f32[20]{0:T(128)} %rev_ref.1) | copy-start | bytes 244
  22.0 8.6 %collective-permute-start.8 = (f32[200,128]{1,0:T(8,128)S(1)}, f32[200,128]{1,0:T(8,128)S(1)}, u32[]{:S(2)}, u32[]{:S(2)}) collective-permute-start(f32[200,128]{1,0:T(8,128)S(1)} %get-tuple-element.70), channel_id=1, source_target_pairs={{0,2},{1,3},{2,0},{3,1},{4,8},{5,9},{6,10},{7,11},{8,4},{9,5},{10,... | collective-permute-start | bytes 307208 | tf_op jit(solution)/shard_map/ppermute | solution.py:651
  23.6 7.0 %collective-permute-start.9 = (f32[200,128]{1,0:T(8,128)S(1)}, f32[200,128]{1,0:T(8,128)S(1)}, u32[]{:S(2)}, u32[]{:S(2)}) collective-permute-start(f32[200,128]{1,0:T(8,128)S(1)} %get-tuple-element.71), channel_id=1, source_target_pairs={{0,4},{1,5},{2,6},{3,7},{4,12},{5,13},{6,14},{7,15},{8,0},{9,1},{1... | collective-permute-start | bytes 307208 | tf_op jit(solution)/shard_map/ppermute | solution.py:641
  23.6 7.0 %collective-permute-start.10 = (f32[104,128]{1,0:T(8,128)S(1)}, f32[104,128]{1,0:T(8,128)S(1)}, u32[]{:S(2)}, u32[]{:S(2)}) collective-permute-start(f32[104,128]{1,0:T(8,128)S(1)} %get-tuple-element.72), channel_id=1, source_target_pairs={{0,8},{1,9},{2,10},{3,11},{4,0},{5,1},{6,2},{7,3},{8,12},{9,13},{1... | collective-permute-start | bytes 159752 | tf_op jit(solution)/shard_map/ppermute | solution.py:641
  26.5 4.1 %collective-permute-start.11 = (f32[96,128]{1,0:T(8,128)S(1)}, f32[96,128]{1,0:T(8,128)S(1)}, u32[]{:S(2)}, u32[]{:S(2)}) collective-permute-start(f32[96,128]{1,0:T(8,128)S(1)} %get-tuple-element.73), channel_id=1, source_target_pairs={{0,4},{1,5},{2,6},{3,7},{4,0},{5,1},{6,2},{7,3},{8,12},{9,13},{10,... | collective-permute-start | bytes 147464 | tf_op jit(solution)/shard_map/ppermute | solution.py:641
  26.5 0.7 %copy-start.7 = (f32[20]{0:T(128)S(1)}, f32[20]{0:T(128)}, u32[]{:S(2)}) copy-start(f32[20]{0:T(128)} %half_ref.1) | copy-start | bytes 244
  26.5 0.7 %copy-start.8 = (f32[20]{0:T(128)S(1)}, f32[20]{0:T(128)}, u32[]{:S(2)}) copy-start(f32[20]{0:T(128)} %slope_ref.1) | copy-start | bytes 244
  26.5 0.7 %copy-start.9 = (f32[20]{0:T(128)S(1)}, f32[20]{0:T(128)}, u32[]{:S(2)}) copy-start(f32[20]{0:T(128)} %tau_ref.1) | copy-start | bytes 244
  27.2 3.4 %copy-start.6 = (f32[1,8192]{1,0:T(1,128)S(1)}, f32[1,8192]{1,0:T(1,128)}, u32[]{:S(2)}) copy-start(f32[1,8192]{1,0:T(1,128)} %param.19) | copy-start | bytes 98308

commit v21 on v19

--- a/solution.py
+++ b/solution.py
@@ -11,6 +11,7 @@
 LANES = 128
 SUB = 8
 PACK = 8
+EDGE_COST = 1_000_000_000
 COUNT_LANE = 4 * PACK
 F32 = jnp.float32
 
@@ -524,13 +525,18 @@
         out_ref[out_ref.shape[0] - SUB :] = total_ref[...]
 
 
+def edge_kernel(total_ref, other_ref, after_ref, out_ref):
+    gx = lax.axis_index("gx")
+    out_ref[...] = total_ref[...] + jnp.where((gx == 1) | (gx == 2), 0.0, other_ref[...])
+
+
 def land_round(own_ref, round_ref, middle_ref, back_ref, rest_ref, edge_ref):
     size = (own_ref.shape[0] - SUB) // 3
     half = size // 2
     gx = lax.axis_index("gx")
     inside = (gx == 1) | (gx == 2)
     last = lambda ref: ref[ref.shape[0] - SUB :]
-    total = last(own_ref) + last(round_ref) + last(back_ref) + jnp.where(inside, last(middle_ref), edge_ref[...])
+    total = edge_ref[...] + last(round_ref) + last(back_ref) + jnp.where(inside, last(middle_ref), 0.0)
     parts = []
     for k in range(3):
         whole = slice(k * size, k * size + size)
@@ -746,8 +752,8 @@
             swap(middle, x_to=partners("gx", 1)),
             swap(back, x_to=BACK),
             swap(rest, x_to=partners("gx", 0)),
-            swap(sums, x_to=[3, 1, 2, 0]),
         ]
+        other = swap(sums, x_to=[3, 1, 2, 0])
         land = land_round
     else:
         blocks = call(pack_kernel, (shape_of(3 * block_rows + SUB, LANES),) * n_gx, 4)(sums, list0, list1, list2)
@@ -772,6 +778,8 @@
         half_voltage, gate_slope, tau_base, conductance, reversal,
         arrived[0], cells(voltage), states(gates), states(gates_cot),
     )
+    if land is land_round:
+        arrived.append(call(edge_kernel, shape_of(SUB, nz), 3, cost=EDGE_COST)(sums, other, factor))
     solution, volt_grad, gate_grad = call(
         functools.partial(finish_kernel, land),
         (block, shape_of(block_rows, LANES), shape_of(n_states, block_rows, LANES)),

time: 30.5 us -> 30.8 us (level)
  waiting for transfers between devices: 2.67 us -> 1.54 us
  starting transfers between devices: 16.1 us -> 16.8 us
  local copies, waits for them, and re-layouts: 0.68 us -> 1.36 us
    ppermute x10, waiting for transfers between devices: 1.16 us -> 0.03 us  [swap(): return lax.ppermute(value, ('gx', 'gy', 'gz'), pairs)]
    ppermute x10, starting transfers between devices: 13.5 us -> 14.2 us  [swap(): return lax.ppermute(value, ('gx', 'gy', 'gz'), pairs)]
    unnamed x24, local copies, waits for them, and re-layouts: 0.68 us -> 1.36 us
  transfers between devices with their start and end apart: 13 -> 13, of which waited for: 4 -> 3; matrix products, arithmetic and copies ran while one was open for 0% -> 0% of each run, Pallas kernels for 22% -> 22%
where the time goes in v21:
time: 30.8 us; the launch traced here: 30.6 us
  starting transfers between devices  16.8 us (55%)
  Pallas kernels  10.1 us (33%)
  waiting for transfers between devices  1.54 us (5%)
  local copies, waits for them, and re-layouts  1.36 us (4%)
  between operations  0.86 us (3%)
    ppermute x10, starting transfers between devices, swap(): return lax.ppermute(value, ('gx', 'gy', 'gz'), pairs)  14.2 us
    pallas_call x3, Pallas kernels, couple(): call(functools.partial(couple_kernel, stage, slot_rows), shape_of(n_gx *...  2.25 us
    ppermute x2, starting transfers between devices, add(): lax.ppermute(value, axis, [(i, i ^ step) for i in range(lax.axis_size(axi...  2.07 us
    pallas_call x1, Pallas kernels, local(): call(membrane_kernel, (shape_of(n_states, block_rows, LANES), shape_of(bl...  1.91 us
    pallas_call x1, Pallas kernels, local(): call(plan_kernel, (cells_shape, cells_shape), 3, cost=6000000)  1.51 us
    unnamed x24, local copies, waits for them, and re-layouts  1.36 us
    pallas_call x1, Pallas kernels, local(): call(start_kernel, (block, block, shape_of(2, ny, nz), shape_of(2, SUB, n...  1.32 us
    pallas_call x1, Pallas kernels, local(): call(functools.partial(finish_kernel, land), (block, shape_of(block_rows,...  1.31 us
  transfers between devices with their start and end apart: 13, of which 3 were waited for; matrix products, arithmetic and copies ran while one was open for 0% of the time, Pallas kernels for 22%

profile of v21, /device:TPU:0, one launch (start us, length us, event | category | flops | bytes accessed | tf_op | source)
XLA Modules:
  0.0 30.6 jit_solution(404325202163168314)
XLA Ops:
  0.6 1.3 %shard_map.148 = (f32[16,32,128]{2,1,0:T(8,128)S(1)}, f32[16,32,128]{2,1,0:T(8,128)S(1)}, f32[2,32,128]{2,1,0:T(8,128)S(1)}, f32[2,8,128]{2,1,0:T(8,128)S(1)}) custom-call(f32[16,32,128]{2,1,0:T(8,128)} %right_ref.5, f32[16,32,128]{2,1,0:T(8,128)} %damping_ref.1, s32[16,32,128]{2,1,0:T(8,128)} %label_ref.1), custom_call_target="tpu_custom_call" | custom-call | flops 2000000 | bytes 2000000 | tf_op jit(solution)/shard_map/pallas_call | solution.py:673
  2.0 0.5 %collective-permute-start = (f32[2,32,128]{2,1,0:T(8,128)S(1)}, f32[2,32,128]{2,1,0:T(8,128)S(1)}, u32[]{:S(2)}, u32[]{:S(2)}) collective-permute-start(f32[2,32,128]{2,1,0:T(8,128)S(1)} %get-tuple-element.44.own_ref), channel_id=1, source_target_pairs={{0,1},{1,0},{2,3},{3,2},{4,5},{5,4},{6,7},{7,6},{8,9},{9,8},{10,11... | collective-permute-start | bytes 98312 | tf_op jit(solution)/shard_map/ppermute | solution.py:677
  2.5 0.9 %collective-permute-done.got_ref = f32[2,32,128]{2,1,0:T(8,128)S(1)} collective-permute-done((f32[2,32,128]{2,1,0:T(8,128)S(1)}, f32[2,32,128]{2,1,0:T(8,128)S(1)}, u32[]{:S(2)}, u32[]{:S(2)}) %collective-permute-start) | collective-permute-done | bytes 32800 | tf_op jit(solution)/shard_map/ppermute | solution.py:677
  3.3 0.1 shard_map.150
  3.4 3.0 %collective-permute-start.2 = (f32[6,32,128]{2,1,0:T(8,128)S(1)}, f32[6,32,128]{2,1,0:T(8,128)S(1)}, u32[]{:S(2)}, u32[]{:S(2)}) collective-permute-start(f32[6,32,128]{2,1,0:T(8,128)S(1)} %get-tuple-element.54), channel_id=1, source_target_pairs={{0,4},{1,5},{2,6},{3,7},{4,0},{5,1},{6,2},{7,3},{8,12},{9,13},{10,... | collective-permute-start | bytes 294920 | tf_op jit(solution)/shard_map/ppermute | solution.py:647
  6.4 1.5 %collective-permute-start.1 = (f32[17,8,128]{2,1,0:T(8,128)S(1)}, f32[17,8,128]{2,1,0:T(8,128)S(1)}, u32[]{:S(2)}, u32[]{:S(2)}) collective-permute-start(f32[17,8,128]{2,1,0:T(8,128)S(1)} %get-tuple-element.46), channel_id=1, source_target_pairs={{0,2},{1,3},{2,0},{3,1},{4,6},{5,7},{6,4},{7,5},{8,10},{9,11},{10,... | collective-permute-start | bytes 208904 | tf_op jit(solution)/shard_map/ppermute | solution.py:647
  7.9 3.1 %collective-permute-start.4 = (f32[4,8,128]{2,1,0:T(8,128)S(1)}, f32[4,8,128]{2,1,0:T(8,128)S(1)}, u32[]{:S(2)}, u32[]{:S(2)}) collective-permute-start(f32[4,8,128]{2,1,0:T(8,128)S(1)} %get-tuple-element.56), channel_id=1, source_target_pairs={{0,6},{1,7},{2,4},{3,5},{4,2},{5,3},{6,0},{7,1},{8,14},{9,15},{10,... | collective-permute-start | bytes 49160 | tf_op jit(solution)/shard_map/ppermute | solution.py:647
  11.1 1.5 %shard_map.149 = (s32[512,128]{1,0:T(8,128)S(1)}, s32[512,128]{1,0:T(8,128)S(1)}) custom-call(f32[2,8,128]{2,1,0:T(8,128)S(1)} %get-tuple-element.40.after_ref.stat_ref, s32[512,128]{1,0:T(8,128)S(1)} %bitcast.8, s32[160,128]{1,0:T(8,128)S(1)} %bitcast.13), custom_call_target="tpu_custom_call" | custom-call | flops 6000000 | bytes 6000000 | tf_op jit(solution)/shard_map/pallas_call | solution.py:679
  12.6 0.9 %shard_map.151 = (f32[16,48,128]{2,1,0:T(8,128)S(1)}, f32[16,48,128]{2,1,0:T(8,128)S(1)}, f32[16,48,128]{2,1,0:T(8,128)S(1)}, f32[16,48,128]{2,1,0:T(8,128)S(1)}...) custom-call(f32[16,32,128]{2,1,0:T(8,128)S(1)} %copy-done, ...), custom_call_target="tpu_custom_call" | custom-call | flops 6000000 | bytes 6000000 | tf_op jit(solution)/shard_map/pallas_call | solution.py:699
  13.5 0.7 %shard_map.152 = (f32[6,48,128]{2,1,0:T(8,128)S(1)}, f32[6,48,128]{2,1,0:T(8,128)S(1)}, f32[6,48,128]{2,1,0:T(8,128)S(1)}, f32[3,48,256]{2,1,0:T(8,128)S(1)}, f3...) custom-call(s32[512,128]{1,0:T(8,128)S(1)} %get-tuple-element.41.after_ref.plan_ref, f32[16,32,128]{2,1,0:T(8,128)S(1)} %copy-done, ...), custom_call_target="tpu_custom_call" | custom-call | flops 2000000 | bytes 2000000 | tf_op jit(solution)/shard_map/pallas_call | solution.py:706
  14.2 0.6 %collective-permute-start.6 = (f32[8,128]{1,0:T(8,128)S(1)}, f32[8,128]{1,0:T(8,128)S(1)}, u32[]{:S(2)}, u32[]{:S(2)}) collective-permute-start(f32[8,128]{1,0:T(8,128)S(1)} %get-tuple-element.58.after_ref.a_ref), channel_id=1, source_target_pairs={{0,1},{1,0},{2,3},{3,2},{4,5},{5,4},{6,7},{7,6},{8,9},{9,8},{10,11... | collective-permute-start | bytes 12296 | tf_op jit(solution)/shard_map/ppermute | solution.py:733
  14.8 0.7 %shard_map.153.after_ref.refs_0_ = f32[256,128]{1,0:T(8,128)S(1)} custom-call(f32[8,128]{1,0:T(8,128)S(1)} %get-tuple-element.58.after_ref.a_ref, f32[8,128]{1,0:T(8,128)S(1)} %get-tuple-element.59.where_ref, f32[16,48,128]{2,1,0:T(8,128)S(1)} %get-tuple-element.47.a_ref.inside_ref, f32[6,48,128]{2,1,0:T(8,128)S(1)} %get-tuple-element.60.edge_ref, ...), custom_call_target="tpu_custom_call" | custom-call | flops 6000000 | bytes 6000000 | tf_op jit(solution)/shard_map/pallas_call | solution.py:722
  15.6 1.5 %collective-permute-start.7 = (f32[8,128]{1,0:T(8,128)S(1)}, f32[8,128]{1,0:T(8,128)S(1)}, u32[]{:S(2)}, u32[]{:S(2)}) collective-permute-start(f32[8,128]{1,0:T(8,128)S(1)} %shard_map.154.after_ref.a_ref), channel_id=1, source_target_pairs={{0,2},{2,0},{1,3},{3,1},{4,6},{6,4},{5,7},{7,5},{8,10},{10,8},{9,1... | collective-permute-start | bytes 12296 | tf_op jit(solution)/shard_map/ppermute | solution.py:733
  17.1 0.8 %shard_map.155.after_ref.refs_1_ = f32[256,128]{1,0:T(8,128)S(1)} custom-call(f32[8,128]{1,0:T(8,128)S(1)} %shard_map.154.after_ref.a_ref, f32[8,128]{1,0:T(8,128)S(1)} %get-tuple-element.59.where_ref, f32[16,48,128]{2,1,0:T(8,128)S(1)} %get-tuple-element.49.b_ref.inside_ref, f32[6,48,128]{2,1,0:T(8,128)S(1)} %get-tuple-element.63.edge_ref.eb_ref, ...), custom_call_target="tpu_custom_call" | custom-call | flops 6000000 | bytes 6000000 | tf_op jit(solution)/shard_map/pallas_call | solution.py:722
  17.9 0.8 %shard_map.156.after_ref.refs_2_ = f32[256,128]{1,0:T(8,128)S(1)} custom-call(f32[256,128]{1,0:T(8,128)S(1)} %shard_map.155.after_ref.refs_1_, f32[8,128]{1,0:T(8,128)S(1)} %get-tuple-element.59.where_ref, f32[16,48,128]{2,1,0:T(8,128)S(1)} %get-tuple-element.50.c_ref.inside_ref, f32[6,48,128]{2,1,0:T(8,128)S(1)} %get-tuple-element.64.edge_ref.ec_ref, ...), custom_call_target="tpu_custom_call" | custom-call | flops 6000000 | bytes 6000000 | tf_op jit(solution)/shard_map/pallas_call | solution.py:722
  18.7 0.6 %collective-permute-done.7.b_ref = f32[8,128]{1,0:T(8,128)S(1)} collective-permute-done((f32[8,128]{1,0:T(8,128)S(1)}, f32[8,128]{1,0:T(8,128)S(1)}, u32[]{:S(2)}, u32[]{:S(2)}) %collective-permute-start.7) | collective-permute-done | bytes 4128 | tf_op jit(solution)/shard_map/ppermute | solution.py:733
  19.3 2.2 %collective-permute-start.8 = (f32[200,128]{1,0:T(8,128)S(1)}, f32[200,128]{1,0:T(8,128)S(1)}, u32[]{:S(2)}, u32[]{:S(2)}) collective-permute-start(f32[200,128]{1,0:T(8,128)S(1)} %get-tuple-element.70), channel_id=1, source_target_pairs={{0,4},{1,5},{2,6},{3,7},{4,12},{5,13},{6,14},{7,15},{8,0},{9,1},{1... | collective-permute-start | bytes 307208 | tf_op jit(solution)/shard_map/ppermute | solution.py:647
  21.5 1.1 %collective-permute-start.12 = (f32[8,128]{1,0:T(8,128)S(1)}, f32[8,128]{1,0:T(8,128)S(1)}, u32[]{:S(2)}, u32[]{:S(2)}) collective-permute-start(f32[8,128]{1,0:T(8,128)S(1)} %shard_map.157.total_ref), channel_id=1, source_target_pairs={{0,12},{1,13},{2,14},{3,15},{4,5},{5,4},{6,7},{7,6},{8,9},{9,8},{1... | collective-permute-start | bytes 12296 | tf_op jit(solution)/shard_map/ppermute | solution.py:647
  22.7 0.2 collective-permute-start.11
  22.9 3.1 %collective-permute-start.10 = (f32[104,128]{1,0:T(8,128)S(1)}, f32[104,128]{1,0:T(8,128)S(1)}, u32[]{:S(2)}, u32[]{:S(2)}) collective-permute-start(f32[104,128]{1,0:T(8,128)S(1)} %get-tuple-element.72), channel_id=1, source_target_pairs={{0,8},{1,9},{2,10},{3,11},{4,0},{5,1},{6,2},{7,3},{8,12},{9,13},{1... | collective-permute-start | bytes 159752 | tf_op jit(solution)/shard_map/ppermute | solution.py:647
  26.0 0.6 %copy-done.7 = f32[20]{0:T(128)S(1)} copy-done((f32[20]{0:T(128)S(1)}, f32[20]{0:T(128)}, u32[]{:S(2)}) %copy-start.7) | copy-done | bytes 104
  26.6 1.9 %shard_map.159 = (f32[20,64,128]{2,1,0:T(8,128)S(1)}, f32[64,128]{1,0:T(8,128)S(1)}, f32[64,128]{1,0:T(8,128)S(1)}, f32[2,20,128]{2,1,0:T(8,128)S(1)}) custom-call(f32[20]{0:T(128)S(1)} %copy-done.7, f32[20]{0:T(128)S(1)} %copy-done.8, f32[20]{0:T(128)S(1)} %copy-done.9, f32[20]{0:T(128)S(1)} %copy-done.10, f32[20]{0:T(128)S(1)} %copy-done.11, ...), custom_call_target="tpu_custom_call" | custom-call | flops 6000000 | bytes 6000000 | tf_op jit(solution)/shard_map/pallas_call | solution.py:768
  28.6 0.7 %copy-done.6 = f32[1,8192]{1,0:T(1,128)S(1)} copy-done((f32[1,8192]{1,0:T(1,128)S(1)}, f32[1,8192]{1,0:T(1,128)}, u32[]{:S(2)}) %copy-start.6) | copy-done | bytes 32792
  29.3 1.3 %shard_map.161 = (f32[16,32,128]{2,1,0:T(8,128)}, f32[64,128]{1,0:T(8,128)}, f32[20,64,128]{2,1,0:T(8,128)}) custom-call(f32[2,20,128]{2,1,0:T(8,128)S(1)} %get-tuple-element.66.coef_ref, f32[64,128]{1,0:T(8,128)S(1)} %bitcast.14, f32[64,128]{1,0:T(8,128)S(1)} %bitcast.12, f32[64,128]{1,0:T(8,128)S(1)} %get-tuple-element.67.sum_ref, ...), custom_call_target="tpu_custom_call" | custom-call | flops 2000000 | bytes 2000000 | tf_op jit(solution)/shard_map/pallas_call | solution.py:783
  (40 shorter events, 0.2 us)
Async XLA Ops:
  2.0 1.4 %collective-permute-start = (f32[2,32,128]{2,1,0:T(8,128)S(1)}, f32[2,32,128]{2,1,0:T(8,128)S(1)}, u32[]{:S(2)}, u32[]{:S(2)}) collective-permute-start(f32[2,32,128]{2,1,0:T(8,128)S(1)} %get-tuple-element.44.own_ref), channel_id=1, source_target_pairs={{0,1},{1,0},{2,3},{3,2},{4,5},{5,4},{6,7},{7,6},{8,9},{9,8},{10,11... | collective-permute-start | bytes 98312 | tf_op jit(solution)/shard_map/ppermute | solution.py:677
  3.3 7.7 %copy-start.1 = (s32[16,32,128]{2,1,0:T(8,128)S(1)}, s32[16,32,128]{2,1,0:T(8,128)}, u32[]{:S(2)}) copy-start(s32[16,32,128]{2,1,0:T(8,128)} %label_ref.1) | copy-start | bytes 786436
  3.3 7.7 %copy-start.5 = (s32[1,1,1,20480]{3,2,1,0:T(1,128)S(1)}, s32[1,1,1,20480]{3,2,1,0:T(1,128)}, u32[]{:S(2)}) copy-start(s32[1,1,1,20480]{3,2,1,0:T(1,128)} %param.16) | copy-start | bytes 245764
  3.4 9.2 %copy-start = (f32[16,32,128]{2,1,0:T(8,128)S(1)}, f32[16,32,128]{2,1,0:T(8,128)}, u32[]{:S(2)}) copy-start(f32[16,32,128]{2,1,0:T(8,128)} %right_ref.5) | copy-start | bytes 786436
  3.4 10.1 %collective-permute-start.2 = (f32[6,32,128]{2,1,0:T(8,128)S(1)}, f32[6,32,128]{2,1,0:T(8,128)S(1)}, u32[]{:S(2)}, u32[]{:S(2)}) collective-permute-start(f32[6,32,128]{2,1,0:T(8,128)S(1)} %get-tuple-element.54), channel_id=1, source_target_pairs={{0,4},{1,5},{2,6},{3,7},{4,0},{5,1},{6,2},{7,3},{8,12},{9,13},{10,... | collective-permute-start | bytes 294920 | tf_op jit(solution)/shard_map/ppermute | solution.py:647
  6.4 7.1 %collective-permute-start.3 = (f32[6,32,128]{2,1,0:T(8,128)S(1)}, f32[6,32,128]{2,1,0:T(8,128)S(1)}, u32[]{:S(2)}, u32[]{:S(2)}) collective-permute-start(f32[6,32,128]{2,1,0:T(8,128)S(1)} %get-tuple-element.55), channel_id=1, source_target_pairs={{0,1},{1,0},{2,3},{3,2},{4,8},{5,9},{6,10},{7,11},{8,4},{9,5},{10,... | collective-permute-start | bytes 294920 | tf_op jit(solution)/shard_map/ppermute | solution.py:647
  6.4 6.1 %collective-permute-start.1 = (f32[17,8,128]{2,1,0:T(8,128)S(1)}, f32[17,8,128]{2,1,0:T(8,128)S(1)}, u32[]{:S(2)}, u32[]{:S(2)}) collective-permute-start(f32[17,8,128]{2,1,0:T(8,128)S(1)} %get-tuple-element.46), channel_id=1, source_target_pairs={{0,2},{1,3},{2,0},{3,1},{4,6},{5,7},{6,4},{7,5},{8,10},{9,11},{10,... | collective-permute-start | bytes 208904 | tf_op jit(solution)/shard_map/ppermute | solution.py:647
  7.9 5.6 %collective-permute-start.4 = (f32[4,8,128]{2,1,0:T(8,128)S(1)}, f32[4,8,128]{2,1,0:T(8,128)S(1)}, u32[]{:S(2)}, u32[]{:S(2)}) collective-permute-start(f32[4,8,128]{2,1,0:T(8,128)S(1)} %get-tuple-element.56), channel_id=1, source_target_pairs={{0,6},{1,7},{2,4},{3,5},{4,2},{5,3},{6,0},{7,1},{8,14},{9,15},{10,... | collective-permute-start | bytes 49160 | tf_op jit(solution)/shard_map/ppermute | solution.py:647
  11.0 2.5 %collective-permute-start.5 = (f32[4,8,128]{2,1,0:T(8,128)S(1)}, f32[4,8,128]{2,1,0:T(8,128)S(1)}, u32[]{:S(2)}, u32[]{:S(2)}) collective-permute-start(f32[4,8,128]{2,1,0:T(8,128)S(1)} %get-tuple-element.57), channel_id=1, source_target_pairs={{0,1},{1,0},{2,3},{3,2},{4,10},{5,11},{6,8},{7,9},{8,6},{9,7},{10,... | collective-permute-start | bytes 49160 | tf_op jit(solution)/shard_map/ppermute | solution.py:647
  14.2 1.4 %collective-permute-start.6 = (f32[8,128]{1,0:T(8,128)S(1)}, f32[8,128]{1,0:T(8,128)S(1)}, u32[]{:S(2)}, u32[]{:S(2)}) collective-permute-start(f32[8,128]{1,0:T(8,128)S(1)} %get-tuple-element.58.after_ref.a_ref), channel_id=1, source_target_pairs={{0,1},{1,0},{2,3},{3,2},{4,5},{5,4},{6,7},{7,6},{8,9},{9,8},{10,11... | collective-permute-start | bytes 12296 | tf_op jit(solution)/shard_map/ppermute | solution.py:733
  15.6 3.6 %collective-permute-start.7 = (f32[8,128]{1,0:T(8,128)S(1)}, f32[8,128]{1,0:T(8,128)S(1)}, u32[]{:S(2)}, u32[]{:S(2)}) collective-permute-start(f32[8,128]{1,0:T(8,128)S(1)} %shard_map.154.after_ref.a_ref), channel_id=1, source_target_pairs={{0,2},{2,0},{1,3},{3,1},{4,6},{6,4},{5,7},{7,5},{8,10},{10,8},{9,1... | collective-permute-start | bytes 12296 | tf_op jit(solution)/shard_map/ppermute | solution.py:733
  17.9 8.0 %copy-start.2 = (f32[20,1,8192]{2,1,0:T(1,128)S(1)}, f32[20,1,8192]{2,1,0:T(1,128)}, u32[]{:S(2)}) copy-start(f32[20,1,8192]{2,1,0:T(1,128)} %param.18) | copy-start | bytes 1966084
  17.9 8.0 %copy-start.3 = (f32[20,1,8192]{2,1,0:T(1,128)S(1)}, f32[20,1,8192]{2,1,0:T(1,128)}, u32[]{:S(2)}) copy-start(f32[20,1,8192]{2,1,0:T(1,128)} %param.20) | copy-start | bytes 1966084
  19.3 6.7 %copy-start.4 = (f32[1,8192]{1,0:T(1,128)S(1)}, f32[1,8192]{1,0:T(1,128)}, u32[]{:S(2)}) copy-start(f32[1,8192]{1,0:T(1,128)} %param.17) | copy-start | bytes 98308
  19.3 6.7 %copy-start.10 = (f32[20]{0:T(128)S(1)}, f32[20]{0:T(128)}, u32[]{:S(2)}) copy-start(f32[20]{0:T(128)} %cond_ref.1) | copy-start | bytes 244
  19.3 6.7 %copy-start.11 = (f32[20]{0:T(128)S(1)}, f32[20]{0:T(128)}, u32[]{:S(2)}) copy-start(f32[20]{0:T(128)} %rev_ref.1) | copy-start | bytes 244
  19.3 9.3 %collective-permute-start.8 = (f32[200,128]{1,0:T(8,128)S(1)}, f32[200,128]{1,0:T(8,128)S(1)}, u32[]{:S(2)}, u32[]{:S(2)}) collective-permute-start(f32[200,128]{1,0:T(8,128)S(1)} %get-tuple-element.70), channel_id=1, source_target_pairs={{0,4},{1,5},{2,6},{3,7},{4,12},{5,13},{6,14},{7,15},{8,0},{9,1},{1... | collective-permute-start | bytes 307208 | tf_op jit(solution)/shard_map/ppermute | solution.py:647
  21.5 7.1 %collective-permute-start.9 = (f32[200,128]{1,0:T(8,128)S(1)}, f32[200,128]{1,0:T(8,128)S(1)}, u32[]{:S(2)}, u32[]{:S(2)}) collective-permute-start(f32[200,128]{1,0:T(8,128)S(1)} %get-tuple-element.71), channel_id=1, source_target_pairs={{0,1},{1,0},{2,3},{3,2},{4,8},{5,9},{6,10},{7,11},{8,4},{9,5},{10,... | collective-permute-start | bytes 307208 | tf_op jit(solution)/shard_map/ppermute | solution.py:647
  21.5 7.0 %collective-permute-start.12 = (f32[8,128]{1,0:T(8,128)S(1)}, f32[8,128]{1,0:T(8,128)S(1)}, u32[]{:S(2)}, u32[]{:S(2)}) collective-permute-start(f32[8,128]{1,0:T(8,128)S(1)} %shard_map.157.total_ref), channel_id=1, source_target_pairs={{0,12},{1,13},{2,14},{3,15},{4,5},{5,4},{6,7},{7,6},{8,9},{9,8},{1... | collective-permute-start | bytes 12296 | tf_op jit(solution)/shard_map/ppermute | solution.py:647
  22.7 5.9 %collective-permute-start.11 = (f32[96,128]{1,0:T(8,128)S(1)}, f32[96,128]{1,0:T(8,128)S(1)}, u32[]{:S(2)}, u32[]{:S(2)}) collective-permute-start(f32[96,128]{1,0:T(8,128)S(1)} %get-tuple-element.73), channel_id=1, source_target_pairs={{0,4},{1,5},{2,6},{3,7},{4,0},{5,1},{6,2},{7,3},{8,12},{9,13},{10,... | collective-permute-start | bytes 147464 | tf_op jit(solution)/shard_map/ppermute | solution.py:647
  22.9 5.7 %collective-permute-start.10 = (f32[104,128]{1,0:T(8,128)S(1)}, f32[104,128]{1,0:T(8,128)S(1)}, u32[]{:S(2)}, u32[]{:S(2)}) collective-permute-start(f32[104,128]{1,0:T(8,128)S(1)} %get-tuple-element.72), channel_id=1, source_target_pairs={{0,8},{1,9},{2,10},{3,11},{4,0},{5,1},{6,2},{7,3},{8,12},{9,13},{1... | collective-permute-start | bytes 159752 | tf_op jit(solution)/shard_map/ppermute | solution.py:647
  25.9 0.7 %copy-start.8 = (f32[20]{0:T(128)S(1)}, f32[20]{0:T(128)}, u32[]{:S(2)}) copy-start(f32[20]{0:T(128)} %slope_ref.1) | copy-start | bytes 244
  25.9 0.7 %copy-start.9 = (f32[20]{0:T(128)S(1)}, f32[20]{0:T(128)}, u32[]{:S(2)}) copy-start(f32[20]{0:T(128)} %tau_ref.1) | copy-start | bytes 244
  28.5 0.8 %copy-start.6 = (f32[1,8192]{1,0:T(1,128)S(1)}, f32[1,8192]{1,0:T(1,128)}, u32[]{:S(2)}) copy-start(f32[1,8192]{1,0:T(1,128)} %param.19) | copy-start | bytes 98308
  (1 other events, 0.7 us)

commit v22 on v21

--- a/solution.py
+++ b/solution.py
@@ -11,7 +11,7 @@
 LANES = 128
 SUB = 8
 PACK = 8
-EDGE_COST = 1_000_000_000
+EDGE_COST = 500_000_000
 COUNT_LANE = 4 * PACK
 F32 = jnp.float32
 
@@ -576,8 +576,8 @@
 
 
 def membrane_kernel(
-    half_ref, slope_ref, tau_ref, cond_ref, rev_ref, after_ref, v_ref, gates_ref, cot_ref,
-    base_ref, sum_ref, factor_ref, coef_ref,
+    half_ref, slope_ref, tau_ref, cond_ref, rev_ref, after_ref, vcot_ref, v_ref, gates_ref, cot_ref,
+    base_ref, sum_ref, factor_ref, coef_ref, kept_ref,
 ):
     n_states, rows = gates_ref.shape[:2]
     v = v_ref[...]
@@ -605,6 +605,7 @@
     total, current = lax.fori_loop(0, n_states, state, (zero, zero), unroll=2)
     sum_ref[...] = total
     factor_ref[...] = 1.0 - TIME_STEP * current
+    kept_ref[...] = vcot_ref[...]
 
 
 def finish_kernel(
@@ -765,18 +766,18 @@
         arrived += [swap(blocks[k], x_to=[i if apart[k][i] else i ^ k for i in range(n_gx)]) for k in many]
         land = functools.partial(land_pairs, [[apart[k] for k in few], [apart[k] for k in many]])
 
-    base, total_change, factor, state_coefs = call(
+    base, total_change, factor, state_coefs, vcot = call(
         membrane_kernel,
         (
             shape_of(n_states, block_rows, LANES), shape_of(block_rows, LANES), shape_of(block_rows, LANES),
-            shape_of(2, n_states, LANES),
+            shape_of(2, n_states, LANES), shape_of(block_rows, LANES),
         ),
-        9,
-        specs=[SMEM] * 5 + [VMEM] * 4,
+        10,
+        specs=[SMEM] * 5 + [VMEM] * 5,
         cost=6_000_000,
     )(
         half_voltage, gate_slope, tau_base, conductance, reversal,
-        arrived[0], cells(voltage), states(gates), states(gates_cot),
+        arrived[0], cells(voltage_cot), cells(voltage), states(gates), states(gates_cot),
     )
     if land is land_round:
         arrived.append(call(edge_kernel, shape_of(SUB, nz), 3, cost=EDGE_COST)(sums, other, factor))
@@ -785,7 +786,7 @@
         (block, shape_of(block_rows, LANES), shape_of(n_states, block_rows, LANES)),
         11 + len(arrived),
     )(
-        state_coefs, cells(voltage_cot), cells(voltage), total_change, factor, base,
+        state_coefs, vcot, cells(voltage), total_change, factor, base,
         in0, in1, in2, ends1, ends2, *arrived,
     )
     return solution, volt_grad.reshape(voltage.shape), gate_grad.reshape(gates.shape)

time: 30.8 us -> 30.8 us (level)
  waiting for transfers between devices: 1.54 us -> 3.01 us
  local copies, waits for them, and re-layouts: 1.36 us -> 0.66 us
  starting transfers between devices: 16.8 us -> 16.1 us
    ppermute x10, waiting for transfers between devices: 0.03 us -> 1.5 us  [swap(): return lax.ppermute(value, ('gx', 'gy', 'gz'), pairs)]
    ppermute x10, starting transfers between devices: 14.2 us -> 13.5 us  [swap(): return lax.ppermute(value, ('gx', 'gy', 'gz'), pairs)]
    unnamed x24, local copies, waits for them, and re-layouts: 1.36 us -> 0.66 us
  transfers between devices with their start and end apart: 13 -> 13, of which waited for: 3 -> 5; matrix products, arithmetic and copies ran while one was open for 0% -> 0% of each run, Pallas kernels for 22% -> 21%
where the time goes in v22:
time: 30.8 us; the launch traced here: 30.7 us
  starting transfers between devices  16.1 us (52%)
  Pallas kernels  10.1 us (33%)
  waiting for transfers between devices  3.01 us (10%)
  between operations  0.84 us (3%)
  local copies, waits for them, and re-layouts  0.66 us (2%)
    ppermute x10, starting transfers between devices, swap(): return lax.ppermute(value, ('gx', 'gy', 'gz'), pairs)  13.5 us
    pallas_call x3, Pallas kernels, couple(): call(functools.partial(couple_kernel, stage, slot_rows), shape_of(n_gx *...  2.25 us
    ppermute x2, starting transfers between devices, add(): lax.ppermute(value, axis, [(i, i ^ step) for i in range(lax.axis_size(axi...  2.07 us
    pallas_call x1, Pallas kernels, local(): call(membrane_kernel, (shape_of(n_states, block_rows, LANES), shape_of(bl...  1.91 us
    pallas_call x1, Pallas kernels, local(): call(plan_kernel, (cells_shape, cells_shape), 3, cost=6000000)  1.51 us
    ppermute x10, waiting for transfers between devices, swap(): return lax.ppermute(value, ('gx', 'gy', 'gz'), pairs)  1.5 us
    pallas_call x1, Pallas kernels, local(): call(functools.partial(finish_kernel, land), (block, shape_of(block_rows,...  1.33 us
    pallas_call x1, Pallas kernels, local(): call(start_kernel, (block, block, shape_of(2, ny, nz), shape_of(2, SUB, n...  1.32 us
  transfers between devices with their start and end apart: 13, of which 5 were waited for; matrix products, arithmetic and copies ran while one was open for 0% of the time, Pallas kernels for 21%

profile of v22, /device:TPU:0, one launch (start us, length us, event | category | flops | bytes accessed | tf_op | source)
XLA Modules:
  0.0 30.7 jit_solution(1880855475834107609)
XLA Ops:
  0.6 1.3 %shard_map.148 = (f32[16,32,128]{2,1,0:T(8,128)S(1)}, f32[16,32,128]{2,1,0:T(8,128)S(1)}, f32[2,32,128]{2,1,0:T(8,128)S(1)}, f32[2,8,128]{2,1,0:T(8,128)S(1)}) custom-call(f32[16,32,128]{2,1,0:T(8,128)} %right_ref.5, f32[16,32,128]{2,1,0:T(8,128)} %damping_ref.1, s32[16,32,128]{2,1,0:T(8,128)} %label_ref.1), custom_call_target="tpu_custom_call" | custom-call | flops 2000000 | bytes 2000000 | tf_op jit(solution)/shard_map/pallas_call | solution.py:674
  2.0 0.5 %collective-permute-start = (f32[2,32,128]{2,1,0:T(8,128)S(1)}, f32[2,32,128]{2,1,0:T(8,128)S(1)}, u32[]{:S(2)}, u32[]{:S(2)}) collective-permute-start(f32[2,32,128]{2,1,0:T(8,128)S(1)} %get-tuple-element.45.own_ref), channel_id=1, source_target_pairs={{0,1},{1,0},{2,3},{3,2},{4,5},{5,4},{6,7},{7,6},{8,9},{9,8},{10,11... | collective-permute-start | bytes 98312 | tf_op jit(solution)/shard_map/ppermute | solution.py:678
  2.5 0.9 %collective-permute-done.got_ref = f32[2,32,128]{2,1,0:T(8,128)S(1)} collective-permute-done((f32[2,32,128]{2,1,0:T(8,128)S(1)}, f32[2,32,128]{2,1,0:T(8,128)S(1)}, u32[]{:S(2)}, u32[]{:S(2)}) %collective-permute-start) | collective-permute-done | bytes 32800 | tf_op jit(solution)/shard_map/ppermute | solution.py:678
  3.3 0.1 shard_map.150
  3.4 3.0 %collective-permute-start.2 = (f32[6,32,128]{2,1,0:T(8,128)S(1)}, f32[6,32,128]{2,1,0:T(8,128)S(1)}, u32[]{:S(2)}, u32[]{:S(2)}) collective-permute-start(f32[6,32,128]{2,1,0:T(8,128)S(1)} %get-tuple-element.55), channel_id=1, source_target_pairs={{0,4},{1,5},{2,6},{3,7},{4,0},{5,1},{6,2},{7,3},{8,12},{9,13},{10,... | collective-permute-start | bytes 294920 | tf_op jit(solution)/shard_map/ppermute | solution.py:648
  6.4 1.5 %collective-permute-start.1 = (f32[17,8,128]{2,1,0:T(8,128)S(1)}, f32[17,8,128]{2,1,0:T(8,128)S(1)}, u32[]{:S(2)}, u32[]{:S(2)}) collective-permute-start(f32[17,8,128]{2,1,0:T(8,128)S(1)} %get-tuple-element.47), channel_id=1, source_target_pairs={{0,2},{1,3},{2,0},{3,1},{4,6},{5,7},{6,4},{7,5},{8,10},{9,11},{10,... | collective-permute-start | bytes 208904 | tf_op jit(solution)/shard_map/ppermute | solution.py:648
  7.9 3.1 %collective-permute-start.4 = (f32[4,8,128]{2,1,0:T(8,128)S(1)}, f32[4,8,128]{2,1,0:T(8,128)S(1)}, u32[]{:S(2)}, u32[]{:S(2)}) collective-permute-start(f32[4,8,128]{2,1,0:T(8,128)S(1)} %get-tuple-element.57), channel_id=1, source_target_pairs={{0,6},{1,7},{2,4},{3,5},{4,2},{5,3},{6,0},{7,1},{8,14},{9,15},{10,... | collective-permute-start | bytes 49160 | tf_op jit(solution)/shard_map/ppermute | solution.py:648
  11.1 1.5 %shard_map.149 = (s32[512,128]{1,0:T(8,128)S(1)}, s32[512,128]{1,0:T(8,128)S(1)}) custom-call(f32[2,8,128]{2,1,0:T(8,128)S(1)} %get-tuple-element.41.after_ref.stat_ref, s32[512,128]{1,0:T(8,128)S(1)} %bitcast.8, s32[160,128]{1,0:T(8,128)S(1)} %bitcast.13), custom_call_target="tpu_custom_call" | custom-call | flops 6000000 | bytes 6000000 | tf_op jit(solution)/shard_map/pallas_call | solution.py:680
  12.6 0.9 %shard_map.151 = (f32[16,48,128]{2,1,0:T(8,128)S(1)}, f32[16,48,128]{2,1,0:T(8,128)S(1)}, f32[16,48,128]{2,1,0:T(8,128)S(1)}, f32[16,48,128]{2,1,0:T(8,128)S(1)}...) custom-call(f32[16,32,128]{2,1,0:T(8,128)S(1)} %copy-done, ...), custom_call_target="tpu_custom_call" | custom-call | flops 6000000 | bytes 6000000 | tf_op jit(solution)/shard_map/pallas_call | solution.py:700
  13.5 0.7 %shard_map.152 = (f32[6,48,128]{2,1,0:T(8,128)S(1)}, f32[6,48,128]{2,1,0:T(8,128)S(1)}, f32[6,48,128]{2,1,0:T(8,128)S(1)}, f32[3,48,256]{2,1,0:T(8,128)S(1)}, f3...) custom-call(s32[512,128]{1,0:T(8,128)S(1)} %get-tuple-element.42.after_ref.plan_ref, f32[16,32,128]{2,1,0:T(8,128)S(1)} %copy-done, ...), custom_call_target="tpu_custom_call" | custom-call | flops 2000000 | bytes 2000000 | tf_op jit(solution)/shard_map/pallas_call | solution.py:707
  14.2 0.6 %collective-permute-start.6 = (f32[8,128]{1,0:T(8,128)S(1)}, f32[8,128]{1,0:T(8,128)S(1)}, u32[]{:S(2)}, u32[]{:S(2)}) collective-permute-start(f32[8,128]{1,0:T(8,128)S(1)} %get-tuple-element.59.after_ref.a_ref), channel_id=1, source_target_pairs={{0,1},{1,0},{2,3},{3,2},{4,5},{5,4},{6,7},{7,6},{8,9},{9,8},{10,11... | collective-permute-start | bytes 12296 | tf_op jit(solution)/shard_map/ppermute | solution.py:734
  14.8 0.7 %shard_map.153.after_ref.refs_0_ = f32[256,128]{1,0:T(8,128)S(1)} custom-call(f32[8,128]{1,0:T(8,128)S(1)} %get-tuple-element.59.after_ref.a_ref, f32[8,128]{1,0:T(8,128)S(1)} %get-tuple-element.60.where_ref, f32[16,48,128]{2,1,0:T(8,128)S(1)} %get-tuple-element.48.a_ref.inside_ref, f32[6,48,128]{2,1,0:T(8,128)S(1)} %get-tuple-element.61.edge_ref, ...), custom_call_target="tpu_custom_call" | custom-call | flops 6000000 | bytes 6000000 | tf_op jit(solution)/shard_map/pallas_call | solution.py:723
  15.6 1.5 %collective-permute-start.7 = (f32[8,128]{1,0:T(8,128)S(1)}, f32[8,128]{1,0:T(8,128)S(1)}, u32[]{:S(2)}, u32[]{:S(2)}) collective-permute-start(f32[8,128]{1,0:T(8,128)S(1)} %shard_map.154.after_ref.a_ref), channel_id=1, source_target_pairs={{0,2},{2,0},{1,3},{3,1},{4,6},{6,4},{5,7},{7,5},{8,10},{10,8},{9,1... | collective-permute-start | bytes 12296 | tf_op jit(solution)/shard_map/ppermute | solution.py:734
  17.1 0.8 %shard_map.155.after_ref.refs_1_ = f32[256,128]{1,0:T(8,128)S(1)} custom-call(f32[8,128]{1,0:T(8,128)S(1)} %shard_map.154.after_ref.a_ref, f32[8,128]{1,0:T(8,128)S(1)} %get-tuple-element.60.where_ref, f32[16,48,128]{2,1,0:T(8,128)S(1)} %get-tuple-element.50.b_ref.inside_ref, f32[6,48,128]{2,1,0:T(8,128)S(1)} %get-tuple-element.64.edge_ref.eb_ref, ...), custom_call_target="tpu_custom_call" | custom-call | flops 6000000 | bytes 6000000 | tf_op jit(solution)/shard_map/pallas_call | solution.py:723
  17.9 0.8 %shard_map.156.after_ref.refs_2_ = f32[256,128]{1,0:T(8,128)S(1)} custom-call(f32[256,128]{1,0:T(8,128)S(1)} %shard_map.155.after_ref.refs_1_, f32[8,128]{1,0:T(8,128)S(1)} %get-tuple-element.60.where_ref, f32[16,48,128]{2,1,0:T(8,128)S(1)} %get-tuple-element.51.c_ref.inside_ref, f32[6,48,128]{2,1,0:T(8,128)S(1)} %get-tuple-element.65.edge_ref.ec_ref, ...), custom_call_target="tpu_custom_call" | custom-call | flops 6000000 | bytes 6000000 | tf_op jit(solution)/shard_map/pallas_call | solution.py:723
  18.7 0.6 %collective-permute-done.7.b_ref = f32[8,128]{1,0:T(8,128)S(1)} collective-permute-done((f32[8,128]{1,0:T(8,128)S(1)}, f32[8,128]{1,0:T(8,128)S(1)}, u32[]{:S(2)}, u32[]{:S(2)}) %collective-permute-start.7) | collective-permute-done | bytes 4128 | tf_op jit(solution)/shard_map/ppermute | solution.py:734
  19.3 2.2 %collective-permute-start.8 = (f32[200,128]{1,0:T(8,128)S(1)}, f32[200,128]{1,0:T(8,128)S(1)}, u32[]{:S(2)}, u32[]{:S(2)}) collective-permute-start(f32[200,128]{1,0:T(8,128)S(1)} %get-tuple-element.72), channel_id=1, source_target_pairs={{0,4},{1,5},{2,6},{3,7},{4,12},{5,13},{6,14},{7,15},{8,0},{9,1},{1... | collective-permute-start | bytes 307208 | tf_op jit(solution)/shard_map/ppermute | solution.py:648
  21.5 1.5 %collective-permute-start.10 = (f32[104,128]{1,0:T(8,128)S(1)}, f32[104,128]{1,0:T(8,128)S(1)}, u32[]{:S(2)}, u32[]{:S(2)}) collective-permute-start(f32[104,128]{1,0:T(8,128)S(1)} %get-tuple-element.74), channel_id=1, source_target_pairs={{0,8},{1,9},{2,10},{3,11},{4,0},{5,1},{6,2},{7,3},{8,12},{9,13},{1... | collective-permute-start | bytes 159752 | tf_op jit(solution)/shard_map/ppermute | solution.py:648
  23.1 2.1 %collective-permute-start.12 = (f32[8,128]{1,0:T(8,128)S(1)}, f32[8,128]{1,0:T(8,128)S(1)}, u32[]{:S(2)}, u32[]{:S(2)}) collective-permute-start(f32[8,128]{1,0:T(8,128)S(1)} %shard_map.157.total_ref), channel_id=1, source_target_pairs={{0,12},{1,13},{2,14},{3,15},{4,5},{5,4},{6,7},{7,6},{8,9},{9,8},{1... | collective-permute-start | bytes 12296 | tf_op jit(solution)/shard_map/ppermute | solution.py:648
  25.3 0.6 %copy-done.7 = f32[20]{0:T(128)S(1)} copy-done((f32[20]{0:T(128)S(1)}, f32[20]{0:T(128)}, u32[]{:S(2)}) %copy-start.7) | copy-done | bytes 104
  25.9 1.9 %shard_map.159 = (f32[20,64,128]{2,1,0:T(8,128)S(1)}, f32[64,128]{1,0:T(8,128)S(1)}, f32[64,128]{1,0:T(8,128)S(1)}, f32[2,20,128]{2,1,0:T(8,128)S(1)}, f32[64,128]{1,0:T(8,128)S(1)}) custom-call(f32[20]{0:T(128)S(1)} %copy-done.7, f32[20]{0:T(128)S(1)} %copy-done.8, f32[20]{0:T(128)S(1)} %copy-done.9, f32[20]{0:T(128)S(1)} %copy-done.10, f32[20]{0:T(128)S(1)} %copy-done.11, ...), custom_call_target="tpu_custom_call" | custom-call | flops 6000000 | bytes 6000000 | tf_op jit(solution)/shard_map/pallas_call | solution.py:769
  27.8 0.7 %collective-permute-done.12.other_ref = f32[8,128]{1,0:T(8,128)S(1)} collective-permute-done((f32[8,128]{1,0:T(8,128)S(1)}, f32[8,128]{1,0:T(8,128)S(1)}, u32[]{:S(2)}, u32[]{:S(2)}) %collective-permute-start.12) | collective-permute-done | bytes 4128 | tf_op jit(solution)/shard_map/ppermute | solution.py:648
  28.5 0.8 %collective-permute-done.11.refs_4_ = f32[96,128]{1,0:T(8,128)S(1)} collective-permute-done((f32[96,128]{1,0:T(8,128)S(1)}, f32[96,128]{1,0:T(8,128)S(1)}, u32[]{:S(2)}, u32[]{:S(2)}) %collective-permute-start.11) | collective-permute-done | bytes 49184 | tf_op jit(solution)/shard_map/ppermute | solution.py:648
  29.3 1.3 %shard_map.161 = (f32[16,32,128]{2,1,0:T(8,128)}, f32[64,128]{1,0:T(8,128)}, f32[20,64,128]{2,1,0:T(8,128)}) custom-call(f32[2,20,128]{2,1,0:T(8,128)S(1)} %get-tuple-element.67.coef_ref, f32[64,128]{1,0:T(8,128)S(1)} %get-tuple-element.68.vcot_ref, f32[64,128]{1,0:T(8,128)S(1)} %bitcast.12, f32[64,128]{1,0:T(8,128)S(1)} %get-tuple-element.69.sum_ref, ...), custom_call_target="tpu_custom_call" | custom-call | flops 2000000 | bytes 2000000 | tf_op jit(solution)/shard_map/pallas_call | solution.py:784
  (40 shorter events, 0.2 us)
Async XLA Ops:
  2.0 1.4 %collective-permute-start = (f32[2,32,128]{2,1,0:T(8,128)S(1)}, f32[2,32,128]{2,1,0:T(8,128)S(1)}, u32[]{:S(2)}, u32[]{:S(2)}) collective-permute-start(f32[2,32,128]{2,1,0:T(8,128)S(1)} %get-tuple-element.45.own_ref), channel_id=1, source_target_pairs={{0,1},{1,0},{2,3},{3,2},{4,5},{5,4},{6,7},{7,6},{8,9},{9,8},{10,11... | collective-permute-start | bytes 98312 | tf_op jit(solution)/shard_map/ppermute | solution.py:678
  3.3 7.7 %copy-start.1 = (s32[16,32,128]{2,1,0:T(8,128)S(1)}, s32[16,32,128]{2,1,0:T(8,128)}, u32[]{:S(2)}) copy-start(s32[16,32,128]{2,1,0:T(8,128)} %label_ref.1) | copy-start | bytes 786436
  3.3 7.7 %copy-start.5 = (s32[1,1,1,20480]{3,2,1,0:T(1,128)S(1)}, s32[1,1,1,20480]{3,2,1,0:T(1,128)}, u32[]{:S(2)}) copy-start(s32[1,1,1,20480]{3,2,1,0:T(1,128)} %param.16) | copy-start | bytes 245764
  3.4 9.2 %copy-start = (f32[16,32,128]{2,1,0:T(8,128)S(1)}, f32[16,32,128]{2,1,0:T(8,128)}, u32[]{:S(2)}) copy-start(f32[16,32,128]{2,1,0:T(8,128)} %right_ref.5) | copy-start | bytes 786436
  3.4 10.1 %collective-permute-start.2 = (f32[6,32,128]{2,1,0:T(8,128)S(1)}, f32[6,32,128]{2,1,0:T(8,128)S(1)}, u32[]{:S(2)}, u32[]{:S(2)}) collective-permute-start(f32[6,32,128]{2,1,0:T(8,128)S(1)} %get-tuple-element.55), channel_id=1, source_target_pairs={{0,4},{1,5},{2,6},{3,7},{4,0},{5,1},{6,2},{7,3},{8,12},{9,13},{10,... | collective-permute-start | bytes 294920 | tf_op jit(solution)/shard_map/ppermute | solution.py:648
  6.4 7.1 %collective-permute-start.3 = (f32[6,32,128]{2,1,0:T(8,128)S(1)}, f32[6,32,128]{2,1,0:T(8,128)S(1)}, u32[]{:S(2)}, u32[]{:S(2)}) collective-permute-start(f32[6,32,128]{2,1,0:T(8,128)S(1)} %get-tuple-element.56), channel_id=1, source_target_pairs={{0,1},{1,0},{2,3},{3,2},{4,8},{5,9},{6,10},{7,11},{8,4},{9,5},{10,... | collective-permute-start | bytes 294920 | tf_op jit(solution)/shard_map/ppermute | solution.py:648
  6.4 6.1 %collective-permute-start.1 = (f32[17,8,128]{2,1,0:T(8,128)S(1)}, f32[17,8,128]{2,1,0:T(8,128)S(1)}, u32[]{:S(2)}, u32[]{:S(2)}) collective-permute-start(f32[17,8,128]{2,1,0:T(8,128)S(1)} %get-tuple-element.47), channel_id=1, source_target_pairs={{0,2},{1,3},{2,0},{3,1},{4,6},{5,7},{6,4},{7,5},{8,10},{9,11},{10,... | collective-permute-start | bytes 208904 | tf_op jit(solution)/shard_map/ppermute | solution.py:648
  7.9 5.6 %collective-permute-start.4 = (f32[4,8,128]{2,1,0:T(8,128)S(1)}, f32[4,8,128]{2,1,0:T(8,128)S(1)}, u32[]{:S(2)}, u32[]{:S(2)}) collective-permute-start(f32[4,8,128]{2,1,0:T(8,128)S(1)} %get-tuple-element.57), channel_id=1, source_target_pairs={{0,6},{1,7},{2,4},{3,5},{4,2},{5,3},{6,0},{7,1},{8,14},{9,15},{10,... | collective-permute-start | bytes 49160 | tf_op jit(solution)/shard_map/ppermute | solution.py:648
  11.0 2.5 %collective-permute-start.5 = (f32[4,8,128]{2,1,0:T(8,128)S(1)}, f32[4,8,128]{2,1,0:T(8,128)S(1)}, u32[]{:S(2)}, u32[]{:S(2)}) collective-permute-start(f32[4,8,128]{2,1,0:T(8,128)S(1)} %get-tuple-element.58), channel_id=1, source_target_pairs={{0,1},{1,0},{2,3},{3,2},{4,10},{5,11},{6,8},{7,9},{8,6},{9,7},{10,... | collective-permute-start | bytes 49160 | tf_op jit(solution)/shard_map/ppermute | solution.py:648
  14.2 1.4 %collective-permute-start.6 = (f32[8,128]{1,0:T(8,128)S(1)}, f32[8,128]{1,0:T(8,128)S(1)}, u32[]{:S(2)}, u32[]{:S(2)}) collective-permute-start(f32[8,128]{1,0:T(8,128)S(1)} %get-tuple-element.59.after_ref.a_ref), channel_id=1, source_target_pairs={{0,1},{1,0},{2,3},{3,2},{4,5},{5,4},{6,7},{7,6},{8,9},{9,8},{10,11... | collective-permute-start | bytes 12296 | tf_op jit(solution)/shard_map/ppermute | solution.py:734
  15.6 3.6 %collective-permute-start.7 = (f32[8,128]{1,0:T(8,128)S(1)}, f32[8,128]{1,0:T(8,128)S(1)}, u32[]{:S(2)}, u32[]{:S(2)}) collective-permute-start(f32[8,128]{1,0:T(8,128)S(1)} %shard_map.154.after_ref.a_ref), channel_id=1, source_target_pairs={{0,2},{2,0},{1,3},{3,1},{4,6},{6,4},{5,7},{7,5},{8,10},{10,8},{9,1... | collective-permute-start | bytes 12296 | tf_op jit(solution)/shard_map/ppermute | solution.py:734
  17.9 7.3 %copy-start.2 = (f32[20,1,8192]{2,1,0:T(1,128)S(1)}, f32[20,1,8192]{2,1,0:T(1,128)}, u32[]{:S(2)}) copy-start(f32[20,1,8192]{2,1,0:T(1,128)} %param.18) | copy-start | bytes 1966084
  17.9 7.3 %copy-start.3 = (f32[20,1,8192]{2,1,0:T(1,128)S(1)}, f32[20,1,8192]{2,1,0:T(1,128)}, u32[]{:S(2)}) copy-start(f32[20,1,8192]{2,1,0:T(1,128)} %param.20) | copy-start | bytes 1966084
  19.3 6.0 %copy-start.4 = (f32[1,8192]{1,0:T(1,128)S(1)}, f32[1,8192]{1,0:T(1,128)}, u32[]{:S(2)}) copy-start(f32[1,8192]{1,0:T(1,128)} %param.17) | copy-start | bytes 98308
  19.3 6.0 %copy-start.6 = (f32[1,8192]{1,0:T(1,128)S(1)}, f32[1,8192]{1,0:T(1,128)}, u32[]{:S(2)}) copy-start(f32[1,8192]{1,0:T(1,128)} %param.19) | copy-start | bytes 98308
  19.3 6.0 %copy-start.10 = (f32[20]{0:T(128)S(1)}, f32[20]{0:T(128)}, u32[]{:S(2)}) copy-start(f32[20]{0:T(128)} %cond_ref.1) | copy-start | bytes 244
  19.3 6.0 %copy-start.11 = (f32[20]{0:T(128)S(1)}, f32[20]{0:T(128)}, u32[]{:S(2)}) copy-start(f32[20]{0:T(128)} %rev_ref.1) | copy-start | bytes 244
  19.3 10.0 %collective-permute-start.8 = (f32[200,128]{1,0:T(8,128)S(1)}, f32[200,128]{1,0:T(8,128)S(1)}, u32[]{:S(2)}, u32[]{:S(2)}) collective-permute-start(f32[200,128]{1,0:T(8,128)S(1)} %get-tuple-element.72), channel_id=1, source_target_pairs={{0,4},{1,5},{2,6},{3,7},{4,12},{5,13},{6,14},{7,15},{8,0},{9,1},{1... | collective-permute-start | bytes 307208 | tf_op jit(solution)/shard_map/ppermute | solution.py:648
  21.5 7.8 %collective-permute-start.9 = (f32[200,128]{1,0:T(8,128)S(1)}, f32[200,128]{1,0:T(8,128)S(1)}, u32[]{:S(2)}, u32[]{:S(2)}) collective-permute-start(f32[200,128]{1,0:T(8,128)S(1)} %get-tuple-element.73), channel_id=1, source_target_pairs={{0,1},{1,0},{2,3},{3,2},{4,8},{5,9},{6,10},{7,11},{8,4},{9,5},{10,... | collective-permute-start | bytes 307208 | tf_op jit(solution)/shard_map/ppermute | solution.py:648
  21.5 7.8 %collective-permute-start.10 = (f32[104,128]{1,0:T(8,128)S(1)}, f32[104,128]{1,0:T(8,128)S(1)}, u32[]{:S(2)}, u32[]{:S(2)}) collective-permute-start(f32[104,128]{1,0:T(8,128)S(1)} %get-tuple-element.74), channel_id=1, source_target_pairs={{0,8},{1,9},{2,10},{3,11},{4,0},{5,1},{6,2},{7,3},{8,12},{9,13},{1... | collective-permute-start | bytes 159752 | tf_op jit(solution)/shard_map/ppermute | solution.py:648
  23.1 5.4 %collective-permute-start.12 = (f32[8,128]{1,0:T(8,128)S(1)}, f32[8,128]{1,0:T(8,128)S(1)}, u32[]{:S(2)}, u32[]{:S(2)}) collective-permute-start(f32[8,128]{1,0:T(8,128)S(1)} %shard_map.157.total_ref), channel_id=1, source_target_pairs={{0,12},{1,13},{2,14},{3,15},{4,5},{5,4},{6,7},{7,6},{8,9},{9,8},{1... | collective-permute-start | bytes 12296 | tf_op jit(solution)/shard_map/ppermute | solution.py:648
  25.2 4.1 %collective-permute-start.11 = (f32[96,128]{1,0:T(8,128)S(1)}, f32[96,128]{1,0:T(8,128)S(1)}, u32[]{:S(2)}, u32[]{:S(2)}) collective-permute-start(f32[96,128]{1,0:T(8,128)S(1)} %get-tuple-element.75), channel_id=1, source_target_pairs={{0,4},{1,5},{2,6},{3,7},{4,0},{5,1},{6,2},{7,3},{8,12},{9,13},{10,... | collective-permute-start | bytes 147464 | tf_op jit(solution)/shard_map/ppermute | solution.py:648
  25.2 0.7 %copy-start.8 = (f32[20]{0:T(128)S(1)}, f32[20]{0:T(128)}, u32[]{:S(2)}) copy-start(f32[20]{0:T(128)} %slope_ref.1) | copy-start | bytes 244
  25.2 0.7 %copy-start.9 = (f32[20]{0:T(128)S(1)}, f32[20]{0:T(128)}, u32[]{:S(2)}) copy-start(f32[20]{0:T(128)} %tau_ref.1) | copy-start | bytes 244
  (1 other events, 0.7 us)

commit v23 on v18

--- a/solution.py
+++ b/solution.py
@@ -414,13 +414,18 @@
 
 def galerkin(total):
     def add_up(*rows):
-        return [jnp.broadcast_to(jnp.sum(row, axis=1, keepdims=True), row.shape) for row in rows]
+        sums = jnp.sum(jnp.concatenate(rows, axis=0), axis=1, keepdims=True)
+        return [jnp.broadcast_to(sums[k : k + 1], row.shape) for k, row in enumerate(rows)]
 
     row = {name: total[k : k + 1] for k, name in enumerate(ORDER)}
     b0, b2 = row["w0 r"], row["w0 n1"]
     g00, g01, g02 = row["w0 k0"], row["w1 k0"], row["w1 n1"]
     g11, g12, g22 = row["w1 k1"], row["w2 k1"], row["w2 k2"]
-    s00, s01, s02, s0, s11, s22 = add_up(g00, g01, g02, b0, g11, g22)
+    sums = jnp.sum(total, axis=1, keepdims=True)
+    s00, s01, s02, s0, s11, s22 = [
+        jnp.broadcast_to(sums[k : k + 1], b0.shape)
+        for k in map(ORDER.index, ("w0 k0", "w1 k0", "w1 n1", "w0 r", "w1 k1", "w2 k2"))
+    ]
     l10, l20 = s01 / s00, s02 / s00
     h11 = g11 - l10 * (2.0 * g01 - l10 * g00)
     h12 = g12 - l10 * g02 - l20 * (g01 - l10 * g00)

time: 30.3 us -> 30.3 us (level)
  no operation moved by 1% of the time
where the time goes in v23:
time: 30.3 us; the launch traced here: 30.1 us
  starting transfers between devices  15.4 us (51%)
  Pallas kernels  10.1 us (33%)
  waiting for transfers between devices  3.12 us (10%)
  between operations  0.82 us (3%)
  local copies, waits for them, and re-layouts  0.68 us (2%)
    ppermute x9, starting transfers between devices, swap(): return lax.ppermute(value, ('gx', 'gy', 'gz'), pairs)  12.8 us
    pallas_call x3, Pallas kernels, couple(): call(functools.partial(couple_kernel, stage, slot_rows), shape_of(n_gx *...  2.25 us
    ppermute x2, starting transfers between devices, add(): lax.ppermute(value, axis, [(i, i ^ step) for i in range(lax.axis_size(axi...  2.07 us
    pallas_call x1, Pallas kernels, local(): call(membrane_kernel, (shape_of(n_states, block_rows, LANES), shape_of(bl...  1.91 us
    ppermute x9, waiting for transfers between devices, swap(): return lax.ppermute(value, ('gx', 'gy', 'gz'), pairs)  1.61 us
    pallas_call x1, Pallas kernels, local(): call(plan_kernel, (cells_shape, cells_shape), 3, cost=6000000)  1.51 us
    pallas_call x1, Pallas kernels, local(): call(functools.partial(finish_kernel, alone), (block, shape_of(block_rows...  1.34 us
    pallas_call x1, Pallas kernels, local(): call(start_kernel, (block, block, shape_of(2, ny, nz), shape_of(2, SUB, n...  1.32 us
  transfers between devices with their start and end apart: 12, of which 4 were waited for; matrix products, arithmetic and copies ran while one was open for 0% of the time, Pallas kernels for 22%

profile of v23, /device:TPU:0, one launch (start us, length us, event | category | flops | bytes accessed | tf_op | source)
XLA Modules:
  0.0 30.1 jit_solution(4114686350206954472)
XLA Ops:
  0.6 1.3 %shard_map.148 = (f32[16,32,128]{2,1,0:T(8,128)S(1)}, f32[16,32,128]{2,1,0:T(8,128)S(1)}, f32[2,32,128]{2,1,0:T(8,128)S(1)}, f32[2,8,128]{2,1,0:T(8,128)S(1)}) custom-call(f32[16,32,128]{2,1,0:T(8,128)} %right_ref.5, f32[16,32,128]{2,1,0:T(8,128)} %damping_ref.1, s32[16,32,128]{2,1,0:T(8,128)} %label_ref.1), custom_call_target="tpu_custom_call" | custom-call | flops 2000000 | bytes 2000000 | tf_op jit(solution)/shard_map/pallas_call | solution.py:625
  2.0 0.5 %collective-permute-start = (f32[2,32,128]{2,1,0:T(8,128)S(1)}, f32[2,32,128]{2,1,0:T(8,128)S(1)}, u32[]{:S(2)}, u32[]{:S(2)}) collective-permute-start(f32[2,32,128]{2,1,0:T(8,128)S(1)} %get-tuple-element.43.own_ref), channel_id=1, source_target_pairs={{0,1},{1,0},{2,3},{3,2},{4,5},{5,4},{6,7},{7,6},{8,9},{9,8},{10,11... | collective-permute-start | bytes 98312 | tf_op jit(solution)/shard_map/ppermute | solution.py:629
  2.5 0.9 %collective-permute-done.got_ref = f32[2,32,128]{2,1,0:T(8,128)S(1)} collective-permute-done((f32[2,32,128]{2,1,0:T(8,128)S(1)}, f32[2,32,128]{2,1,0:T(8,128)S(1)}, u32[]{:S(2)}, u32[]{:S(2)}) %collective-permute-start) | collective-permute-done | bytes 32800 | tf_op jit(solution)/shard_map/ppermute | solution.py:629
  3.3 0.1 shard_map.150
  3.4 3.0 %collective-permute-start.2 = (f32[6,32,128]{2,1,0:T(8,128)S(1)}, f32[6,32,128]{2,1,0:T(8,128)S(1)}, u32[]{:S(2)}, u32[]{:S(2)}) collective-permute-start(f32[6,32,128]{2,1,0:T(8,128)S(1)} %get-tuple-element.53), channel_id=1, source_target_pairs={{0,4},{1,5},{2,6},{3,7},{4,0},{5,1},{6,2},{7,3},{8,12},{9,13},{10,... | collective-permute-start | bytes 294920 | tf_op jit(solution)/shard_map/ppermute | solution.py:599
  6.4 1.5 %collective-permute-start.1 = (f32[17,8,128]{2,1,0:T(8,128)S(1)}, f32[17,8,128]{2,1,0:T(8,128)S(1)}, u32[]{:S(2)}, u32[]{:S(2)}) collective-permute-start(f32[17,8,128]{2,1,0:T(8,128)S(1)} %get-tuple-element.45), channel_id=1, source_target_pairs={{0,2},{1,3},{2,0},{3,1},{4,6},{5,7},{6,4},{7,5},{8,10},{9,11},{10,... | collective-permute-start | bytes 208904 | tf_op jit(solution)/shard_map/ppermute | solution.py:599
  7.9 3.1 %collective-permute-start.4 = (f32[4,8,128]{2,1,0:T(8,128)S(1)}, f32[4,8,128]{2,1,0:T(8,128)S(1)}, u32[]{:S(2)}, u32[]{:S(2)}) collective-permute-start(f32[4,8,128]{2,1,0:T(8,128)S(1)} %get-tuple-element.55), channel_id=1, source_target_pairs={{0,6},{1,7},{2,4},{3,5},{4,2},{5,3},{6,0},{7,1},{8,14},{9,15},{10,... | collective-permute-start | bytes 49160 | tf_op jit(solution)/shard_map/ppermute | solution.py:599
  11.1 1.5 %shard_map.149 = (s32[512,128]{1,0:T(8,128)S(1)}, s32[512,128]{1,0:T(8,128)S(1)}) custom-call(f32[2,8,128]{2,1,0:T(8,128)S(1)} %get-tuple-element.39.after_ref.stat_ref, s32[512,128]{1,0:T(8,128)S(1)} %bitcast.8, s32[160,128]{1,0:T(8,128)S(1)} %bitcast.13), custom_call_target="tpu_custom_call" | custom-call | flops 6000000 | bytes 6000000 | tf_op jit(solution)/shard_map/pallas_call | solution.py:631
  12.6 0.9 %shard_map.151 = (f32[16,48,128]{2,1,0:T(8,128)S(1)}, f32[16,48,128]{2,1,0:T(8,128)S(1)}, f32[16,48,128]{2,1,0:T(8,128)S(1)}, f32[16,48,128]{2,1,0:T(8,128)S(1)}...) custom-call(f32[16,32,128]{2,1,0:T(8,128)S(1)} %copy-done, ...), custom_call_target="tpu_custom_call" | custom-call | flops 6000000 | bytes 6000000 | tf_op jit(solution)/shard_map/pallas_call | solution.py:651
  13.5 0.7 %shard_map.152 = (f32[6,48,128]{2,1,0:T(8,128)S(1)}, f32[6,48,128]{2,1,0:T(8,128)S(1)}, f32[6,48,128]{2,1,0:T(8,128)S(1)}, f32[3,48,256]{2,1,0:T(8,128)S(1)}, f3...) custom-call(s32[512,128]{1,0:T(8,128)S(1)} %get-tuple-element.40.after_ref.plan_ref, f32[16,32,128]{2,1,0:T(8,128)S(1)} %copy-done, ...), custom_call_target="tpu_custom_call" | custom-call | flops 2000000 | bytes 2000000 | tf_op jit(solution)/shard_map/pallas_call | solution.py:658
  14.2 0.6 %collective-permute-start.6 = (f32[8,128]{1,0:T(8,128)S(1)}, f32[8,128]{1,0:T(8,128)S(1)}, u32[]{:S(2)}, u32[]{:S(2)}) collective-permute-start(f32[8,128]{1,0:T(8,128)S(1)} %get-tuple-element.57.after_ref.a_ref), channel_id=1, source_target_pairs={{0,1},{1,0},{2,3},{3,2},{4,5},{5,4},{6,7},{7,6},{8,9},{9,8},{10,11... | collective-permute-start | bytes 12296 | tf_op jit(solution)/shard_map/ppermute | solution.py:685
  14.8 0.7 %shard_map.153.after_ref.refs_0_ = f32[256,128]{1,0:T(8,128)S(1)} custom-call(f32[8,128]{1,0:T(8,128)S(1)} %get-tuple-element.57.after_ref.a_ref, f32[8,128]{1,0:T(8,128)S(1)} %get-tuple-element.58.where_ref, f32[16,48,128]{2,1,0:T(8,128)S(1)} %get-tuple-element.46.a_ref.inside_ref, f32[6,48,128]{2,1,0:T(8,128)S(1)} %get-tuple-element.59.edge_ref, ...), custom_call_target="tpu_custom_call" | custom-call | flops 6000000 | bytes 6000000 | tf_op jit(solution)/shard_map/pallas_call | solution.py:674
  15.6 0.1 collective-permute-done.6.b_ref
  15.6 1.5 %collective-permute-start.7 = (f32[8,128]{1,0:T(8,128)S(1)}, f32[8,128]{1,0:T(8,128)S(1)}, u32[]{:S(2)}, u32[]{:S(2)}) collective-permute-start(f32[8,128]{1,0:T(8,128)S(1)} %shard_map.154.after_ref.a_ref), channel_id=1, source_target_pairs={{0,2},{2,0},{1,3},{3,1},{4,6},{6,4},{5,7},{7,5},{8,10},{10,8},{9,1... | collective-permute-start | bytes 12296 | tf_op jit(solution)/shard_map/ppermute | solution.py:685
  17.1 0.8 %shard_map.155.after_ref.refs_1_ = f32[256,128]{1,0:T(8,128)S(1)} custom-call(f32[8,128]{1,0:T(8,128)S(1)} %shard_map.154.after_ref.a_ref, f32[8,128]{1,0:T(8,128)S(1)} %get-tuple-element.58.where_ref, f32[16,48,128]{2,1,0:T(8,128)S(1)} %get-tuple-element.48.b_ref.inside_ref, f32[6,48,128]{2,1,0:T(8,128)S(1)} %get-tuple-element.62.edge_ref.eb_ref, ...), custom_call_target="tpu_custom_call" | custom-call | flops 6000000 | bytes 6000000 | tf_op jit(solution)/shard_map/pallas_call | solution.py:674
  17.9 0.8 %shard_map.156.after_ref.refs_2_ = f32[256,128]{1,0:T(8,128)S(1)} custom-call(f32[256,128]{1,0:T(8,128)S(1)} %shard_map.155.after_ref.refs_1_, f32[8,128]{1,0:T(8,128)S(1)} %get-tuple-element.58.where_ref, f32[16,48,128]{2,1,0:T(8,128)S(1)} %get-tuple-element.49.c_ref.inside_ref, f32[6,48,128]{2,1,0:T(8,128)S(1)} %get-tuple-element.63.edge_ref.ec_ref, ...), custom_call_target="tpu_custom_call" | custom-call | flops 6000000 | bytes 6000000 | tf_op jit(solution)/shard_map/pallas_call | solution.py:674
  18.7 0.6 %collective-permute-done.7.b_ref = f32[8,128]{1,0:T(8,128)S(1)} collective-permute-done((f32[8,128]{1,0:T(8,128)S(1)}, f32[8,128]{1,0:T(8,128)S(1)}, u32[]{:S(2)}, u32[]{:S(2)}) %collective-permute-start.7) | collective-permute-done | bytes 4128 | tf_op jit(solution)/shard_map/ppermute | solution.py:685
  19.3 1.9 %collective-permute-start.9 = (f32[200,128]{1,0:T(8,128)S(1)}, f32[200,128]{1,0:T(8,128)S(1)}, u32[]{:S(2)}, u32[]{:S(2)}) collective-permute-start(f32[200,128]{1,0:T(8,128)S(1)} %get-tuple-element.69), channel_id=1, source_target_pairs={{0,8},{1,9},{2,10},{3,11},{4,12},{5,13},{6,14},{7,15},{8,0},{9,1},... | collective-permute-start | bytes 307208 | tf_op jit(solution)/shard_map/ppermute | solution.py:599
  21.2 1.6 %collective-permute-start.11 = (f32[200,128]{1,0:T(8,128)S(1)}, f32[200,128]{1,0:T(8,128)S(1)}, u32[]{:S(2)}, u32[]{:S(2)}) collective-permute-start(f32[200,128]{1,0:T(8,128)S(1)} %get-tuple-element.71), channel_id=1, source_target_pairs={{0,4},{1,5},{2,6},{3,7},{4,0},{5,1},{6,2},{7,3},{8,12},{9,13},{10,... | collective-permute-start | bytes 307208 | tf_op jit(solution)/shard_map/ppermute | solution.py:599
  22.9 1.7 %collective-permute-start.8 = (f32[8,128]{1,0:T(8,128)S(1)}, f32[8,128]{1,0:T(8,128)S(1)}, u32[]{:S(2)}, u32[]{:S(2)}) collective-permute-start(f32[8,128]{1,0:T(8,128)S(1)} %shard_map.157.total_ref), channel_id=1, source_target_pairs={{0,12},{1,13},{2,14},{3,15},{4,5},{5,4},{6,7},{7,6},{8,9},{9,8},{1... | collective-permute-start | bytes 12296 | tf_op jit(solution)/shard_map/ppermute | solution.py:599
  24.6 0.6 %copy-done.7 = f32[20]{0:T(128)S(1)} copy-done((f32[20]{0:T(128)S(1)}, f32[20]{0:T(128)}, u32[]{:S(2)}) %copy-start.7) | copy-done | bytes 104
  25.2 1.9 %shard_map.159 = (f32[20,64,128]{2,1,0:T(8,128)S(1)}, f32[64,128]{1,0:T(8,128)S(1)}, f32[64,128]{1,0:T(8,128)S(1)}, f32[2,20,128]{2,1,0:T(8,128)S(1)}) custom-call(f32[20]{0:T(128)S(1)} %copy-done.7, f32[20]{0:T(128)S(1)} %copy-done.8, f32[20]{0:T(128)S(1)} %copy-done.9, f32[20]{0:T(128)S(1)} %copy-done.10, f32[20]{0:T(128)S(1)} %copy-done.11, ...), custom_call_target="tpu_custom_call" | custom-call | flops 6000000 | bytes 6000000 | tf_op jit(solution)/shard_map/pallas_call | solution.py:705
  27.2 1.6 %collective-permute-done.8.refs_1_ = f32[8,128]{1,0:T(8,128)S(1)} collective-permute-done((f32[8,128]{1,0:T(8,128)S(1)}, f32[8,128]{1,0:T(8,128)S(1)}, u32[]{:S(2)}, u32[]{:S(2)}) %collective-permute-start.8) | collective-permute-done | bytes 4128 | tf_op jit(solution)/shard_map/ppermute | solution.py:599
  28.8 1.3 %shard_map.160 = (f32[16,32,128]{2,1,0:T(8,128)}, f32[64,128]{1,0:T(8,128)}, f32[20,64,128]{2,1,0:T(8,128)}) custom-call(f32[2,20,128]{2,1,0:T(8,128)S(1)} %get-tuple-element.65.coef_ref, f32[64,128]{1,0:T(8,128)S(1)} %bitcast.14, f32[64,128]{1,0:T(8,128)S(1)} %bitcast.12, f32[64,128]{1,0:T(8,128)S(1)} %get-tuple-element.66.sum_ref, ...), custom_call_target="tpu_custom_call" | custom-call | flops 2000000 | bytes 2000000 | tf_op jit(solution)/shard_map/pallas_call | solution.py:718
  (37 shorter events, 0.1 us)
Async XLA Ops:
  2.0 1.4 %collective-permute-start = (f32[2,32,128]{2,1,0:T(8,128)S(1)}, f32[2,32,128]{2,1,0:T(8,128)S(1)}, u32[]{:S(2)}, u32[]{:S(2)}) collective-permute-start(f32[2,32,128]{2,1,0:T(8,128)S(1)} %get-tuple-element.43.own_ref), channel_id=1, source_target_pairs={{0,1},{1,0},{2,3},{3,2},{4,5},{5,4},{6,7},{7,6},{8,9},{9,8},{10,11... | collective-permute-start | bytes 98312 | tf_op jit(solution)/shard_map/ppermute | solution.py:629
  3.3 7.7 %copy-start.1 = (s32[16,32,128]{2,1,0:T(8,128)S(1)}, s32[16,32,128]{2,1,0:T(8,128)}, u32[]{:S(2)}) copy-start(s32[16,32,128]{2,1,0:T(8,128)} %label_ref.1) | copy-start | bytes 786436
  3.3 7.7 %copy-start.5 = (s32[1,1,1,20480]{3,2,1,0:T(1,128)S(1)}, s32[1,1,1,20480]{3,2,1,0:T(1,128)}, u32[]{:S(2)}) copy-start(s32[1,1,1,20480]{3,2,1,0:T(1,128)} %param.16) | copy-start | bytes 245764
  3.4 9.2 %copy-start = (f32[16,32,128]{2,1,0:T(8,128)S(1)}, f32[16,32,128]{2,1,0:T(8,128)}, u32[]{:S(2)}) copy-start(f32[16,32,128]{2,1,0:T(8,128)} %right_ref.5) | copy-start | bytes 786436
  3.4 10.1 %collective-permute-start.2 = (f32[6,32,128]{2,1,0:T(8,128)S(1)}, f32[6,32,128]{2,1,0:T(8,128)S(1)}, u32[]{:S(2)}, u32[]{:S(2)}) collective-permute-start(f32[6,32,128]{2,1,0:T(8,128)S(1)} %get-tuple-element.53), channel_id=1, source_target_pairs={{0,4},{1,5},{2,6},{3,7},{4,0},{5,1},{6,2},{7,3},{8,12},{9,13},{10,... | collective-permute-start | bytes 294920 | tf_op jit(solution)/shard_map/ppermute | solution.py:599
  6.4 7.1 %collective-permute-start.3 = (f32[6,32,128]{2,1,0:T(8,128)S(1)}, f32[6,32,128]{2,1,0:T(8,128)S(1)}, u32[]{:S(2)}, u32[]{:S(2)}) collective-permute-start(f32[6,32,128]{2,1,0:T(8,128)S(1)} %get-tuple-element.54), channel_id=1, source_target_pairs={{0,1},{1,0},{2,3},{3,2},{4,8},{5,9},{6,10},{7,11},{8,4},{9,5},{10,... | collective-permute-start | bytes 294920 | tf_op jit(solution)/shard_map/ppermute | solution.py:599
  6.4 6.1 %collective-permute-start.1 = (f32[17,8,128]{2,1,0:T(8,128)S(1)}, f32[17,8,128]{2,1,0:T(8,128)S(1)}, u32[]{:S(2)}, u32[]{:S(2)}) collective-permute-start(f32[17,8,128]{2,1,0:T(8,128)S(1)} %get-tuple-element.45), channel_id=1, source_target_pairs={{0,2},{1,3},{2,0},{3,1},{4,6},{5,7},{6,4},{7,5},{8,10},{9,11},{10,... | collective-permute-start | bytes 208904 | tf_op jit(solution)/shard_map/ppermute | solution.py:599
  7.9 5.6 %collective-permute-start.4 = (f32[4,8,128]{2,1,0:T(8,128)S(1)}, f32[4,8,128]{2,1,0:T(8,128)S(1)}, u32[]{:S(2)}, u32[]{:S(2)}) collective-permute-start(f32[4,8,128]{2,1,0:T(8,128)S(1)} %get-tuple-element.55), channel_id=1, source_target_pairs={{0,6},{1,7},{2,4},{3,5},{4,2},{5,3},{6,0},{7,1},{8,14},{9,15},{10,... | collective-permute-start | bytes 49160 | tf_op jit(solution)/shard_map/ppermute | solution.py:599
  11.0 2.5 %collective-permute-start.5 = (f32[4,8,128]{2,1,0:T(8,128)S(1)}, f32[4,8,128]{2,1,0:T(8,128)S(1)}, u32[]{:S(2)}, u32[]{:S(2)}) collective-permute-start(f32[4,8,128]{2,1,0:T(8,128)S(1)} %get-tuple-element.56), channel_id=1, source_target_pairs={{0,1},{1,0},{2,3},{3,2},{4,10},{5,11},{6,8},{7,9},{8,6},{9,7},{10,... | collective-permute-start | bytes 49160 | tf_op jit(solution)/shard_map/ppermute | solution.py:599
  14.2 1.4 %collective-permute-start.6 = (f32[8,128]{1,0:T(8,128)S(1)}, f32[8,128]{1,0:T(8,128)S(1)}, u32[]{:S(2)}, u32[]{:S(2)}) collective-permute-start(f32[8,128]{1,0:T(8,128)S(1)} %get-tuple-element.57.after_ref.a_ref), channel_id=1, source_target_pairs={{0,1},{1,0},{2,3},{3,2},{4,5},{5,4},{6,7},{7,6},{8,9},{9,8},{10,11... | collective-permute-start | bytes 12296 | tf_op jit(solution)/shard_map/ppermute | solution.py:685
  15.6 3.6 %collective-permute-start.7 = (f32[8,128]{1,0:T(8,128)S(1)}, f32[8,128]{1,0:T(8,128)S(1)}, u32[]{:S(2)}, u32[]{:S(2)}) collective-permute-start(f32[8,128]{1,0:T(8,128)S(1)} %shard_map.154.after_ref.a_ref), channel_id=1, source_target_pairs={{0,2},{2,0},{1,3},{3,1},{4,6},{6,4},{5,7},{7,5},{8,10},{10,8},{9,1... | collective-permute-start | bytes 12296 | tf_op jit(solution)/shard_map/ppermute | solution.py:685
  17.9 6.7 %copy-start.2 = (f32[20,1,8192]{2,1,0:T(1,128)S(1)}, f32[20,1,8192]{2,1,0:T(1,128)}, u32[]{:S(2)}) copy-start(f32[20,1,8192]{2,1,0:T(1,128)} %param.18) | copy-start | bytes 1966084
  17.9 6.7 %copy-start.3 = (f32[20,1,8192]{2,1,0:T(1,128)S(1)}, f32[20,1,8192]{2,1,0:T(1,128)}, u32[]{:S(2)}) copy-start(f32[20,1,8192]{2,1,0:T(1,128)} %param.20) | copy-start | bytes 1966084
  19.3 5.3 %copy-start.4 = (f32[1,8192]{1,0:T(1,128)S(1)}, f32[1,8192]{1,0:T(1,128)}, u32[]{:S(2)}) copy-start(f32[1,8192]{1,0:T(1,128)} %param.17) | copy-start | bytes 98308
  19.3 5.3 %copy-start.10 = (f32[20]{0:T(128)S(1)}, f32[20]{0:T(128)}, u32[]{:S(2)}) copy-start(f32[20]{0:T(128)} %cond_ref.1) | copy-start | bytes 244
  19.3 5.3 %copy-start.11 = (f32[20]{0:T(128)S(1)}, f32[20]{0:T(128)}, u32[]{:S(2)}) copy-start(f32[20]{0:T(128)} %rev_ref.1) | copy-start | bytes 244
  19.3 9.4 %collective-permute-start.9 = (f32[200,128]{1,0:T(8,128)S(1)}, f32[200,128]{1,0:T(8,128)S(1)}, u32[]{:S(2)}, u32[]{:S(2)}) collective-permute-start(f32[200,128]{1,0:T(8,128)S(1)} %get-tuple-element.69), channel_id=1, source_target_pairs={{0,8},{1,9},{2,10},{3,11},{4,12},{5,13},{6,14},{7,15},{8,0},{9,1},... | collective-permute-start | bytes 307208 | tf_op jit(solution)/shard_map/ppermute | solution.py:599
  21.2 7.5 %collective-permute-start.10 = (f32[200,128]{1,0:T(8,128)S(1)}, f32[200,128]{1,0:T(8,128)S(1)}, u32[]{:S(2)}, u32[]{:S(2)}) collective-permute-start(f32[200,128]{1,0:T(8,128)S(1)} %get-tuple-element.70), channel_id=1, source_target_pairs={{0,1},{1,0},{2,3},{3,2},{4,8},{5,9},{6,10},{7,11},{8,4},{9,5},{10,... | collective-permute-start | bytes 307208 | tf_op jit(solution)/shard_map/ppermute | solution.py:599
  21.2 7.5 %collective-permute-start.11 = (f32[200,128]{1,0:T(8,128)S(1)}, f32[200,128]{1,0:T(8,128)S(1)}, u32[]{:S(2)}, u32[]{:S(2)}) collective-permute-start(f32[200,128]{1,0:T(8,128)S(1)} %get-tuple-element.71), channel_id=1, source_target_pairs={{0,4},{1,5},{2,6},{3,7},{4,0},{5,1},{6,2},{7,3},{8,12},{9,13},{10,... | collective-permute-start | bytes 307208 | tf_op jit(solution)/shard_map/ppermute | solution.py:599
  22.9 5.9 %collective-permute-start.8 = (f32[8,128]{1,0:T(8,128)S(1)}, f32[8,128]{1,0:T(8,128)S(1)}, u32[]{:S(2)}, u32[]{:S(2)}) collective-permute-start(f32[8,128]{1,0:T(8,128)S(1)} %shard_map.157.total_ref), channel_id=1, source_target_pairs={{0,12},{1,13},{2,14},{3,15},{4,5},{5,4},{6,7},{7,6},{8,9},{9,8},{1... | collective-permute-start | bytes 12296 | tf_op jit(solution)/shard_map/ppermute | solution.py:599
  24.5 0.7 %copy-start.7 = (f32[20]{0:T(128)S(1)}, f32[20]{0:T(128)}, u32[]{:S(2)}) copy-start(f32[20]{0:T(128)} %half_ref.1) | copy-start | bytes 244
  24.5 0.7 %copy-start.8 = (f32[20]{0:T(128)S(1)}, f32[20]{0:T(128)}, u32[]{:S(2)}) copy-start(f32[20]{0:T(128)} %slope_ref.1) | copy-start | bytes 244
  24.6 0.7 %copy-start.9 = (f32[20]{0:T(128)S(1)}, f32[20]{0:T(128)}, u32[]{:S(2)}) copy-start(f32[20]{0:T(128)} %tau_ref.1) | copy-start | bytes 244
  25.2 3.5 %copy-start.6 = (f32[1,8192]{1,0:T(1,128)S(1)}, f32[1,8192]{1,0:T(1,128)}, u32[]{:S(2)}) copy-start(f32[1,8192]{1,0:T(1,128)} %param.19) | copy-start | bytes 98308

commit v24 on v18

--- a/solution.py
+++ b/solution.py
@@ -693,7 +693,7 @@
         if any(apart[k]):
             small.append(swap(sums, x_to=[i ^ k if apart[k][i] else i for i in range(n_gx)]))
         meets.append(not all(apart[k]))
-    order = [k for k in [2, 3, 1] + list(range(4, n_gx)) if k < n_gx and meets[k - 1]]
+    order = [k for k in [3, 2, 1] + list(range(4, n_gx)) if k < n_gx and meets[k - 1]]
     large = [swap(blocks[k], x_to=[i if apart[k][i] else i ^ k for i in range(n_gx)]) for k in order]
     alone = [[apart[k] for k in range(1, n_gx) if any(apart[k])], [apart[k] for k in order]]
 

time: 30.3 us -> 30.8 us (1.017)
  waiting for transfers between devices: 3.12 us -> 3.72 us
    ppermute x9, waiting for transfers between devices: 1.61 us -> 2.2 us  [swap(): return lax.ppermute(value, ('gx', 'gy', 'gz'), pairs)]
  transfers between devices with their start and end apart: 12 -> 12, of which waited for: 4 -> 5; matrix products, arithmetic and copies ran while one was open for 0% -> 0% of each run, Pallas kernels for 22% -> 22%
where the time goes in v24:
time: 30.8 us; the launch traced here: 30.6 us
  starting transfers between devices  15.3 us (50%)
  Pallas kernels  10.1 us (33%)
  waiting for transfers between devices  3.72 us (12%)
  between operations  0.81 us (3%)
  local copies, waits for them, and re-layouts  0.68 us (2%)
    ppermute x9, starting transfers between devices, swap(): return lax.ppermute(value, ('gx', 'gy', 'gz'), pairs)  12.8 us
    pallas_call x3, Pallas kernels, couple(): call(functools.partial(couple_kernel, stage, slot_rows), shape_of(n_gx *...  2.25 us
    ppermute x9, waiting for transfers between devices, swap(): return lax.ppermute(value, ('gx', 'gy', 'gz'), pairs)  2.2 us
    ppermute x2, starting transfers between devices, add(): lax.ppermute(value, axis, [(i, i ^ step) for i in range(lax.axis_size(axi...  2.07 us
    pallas_call x1, Pallas kernels, local(): call(membrane_kernel, (shape_of(n_states, block_rows, LANES), shape_of(bl...  1.91 us
    pallas_call x1, Pallas kernels, local(): call(plan_kernel, (cells_shape, cells_shape), 3, cost=6000000)  1.51 us
    pallas_call x1, Pallas kernels, local(): call(functools.partial(finish_kernel, alone), (block, shape_of(block_rows...  1.33 us
    pallas_call x1, Pallas kernels, local(): call(start_kernel, (block, block, shape_of(2, ny, nz), shape_of(2, SUB, n...  1.32 us
  transfers between devices with their start and end apart: 12, of which 5 were waited for; matrix products, arithmetic and copies ran while one was open for 0% of the time, Pallas kernels for 22%

profile of v24, /device:TPU:0, one launch (start us, length us, event | category | flops | bytes accessed | tf_op | source)
XLA Modules:
  0.0 30.6 jit_solution(3634145106907187239)
XLA Ops:
  0.6 1.3 %shard_map.148 = (f32[16,32,128]{2,1,0:T(8,128)S(1)}, f32[16,32,128]{2,1,0:T(8,128)S(1)}, f32[2,32,128]{2,1,0:T(8,128)S(1)}, f32[2,8,128]{2,1,0:T(8,128)S(1)}) custom-call(f32[16,32,128]{2,1,0:T(8,128)} %right_ref.5, f32[16,32,128]{2,1,0:T(8,128)} %damping_ref.1, s32[16,32,128]{2,1,0:T(8,128)} %label_ref.1), custom_call_target="tpu_custom_call" | custom-call | flops 2000000 | bytes 2000000 | tf_op jit(solution)/shard_map/pallas_call | solution.py:620
  2.0 0.5 %collective-permute-start = (f32[2,32,128]{2,1,0:T(8,128)S(1)}, f32[2,32,128]{2,1,0:T(8,128)S(1)}, u32[]{:S(2)}, u32[]{:S(2)}) collective-permute-start(f32[2,32,128]{2,1,0:T(8,128)S(1)} %get-tuple-element.43.own_ref), channel_id=1, source_target_pairs={{0,1},{1,0},{2,3},{3,2},{4,5},{5,4},{6,7},{7,6},{8,9},{9,8},{10,11... | collective-permute-start | bytes 98312 | tf_op jit(solution)/shard_map/ppermute | solution.py:624
  2.5 0.9 %collective-permute-done.got_ref = f32[2,32,128]{2,1,0:T(8,128)S(1)} collective-permute-done((f32[2,32,128]{2,1,0:T(8,128)S(1)}, f32[2,32,128]{2,1,0:T(8,128)S(1)}, u32[]{:S(2)}, u32[]{:S(2)}) %collective-permute-start) | collective-permute-done | bytes 32800 | tf_op jit(solution)/shard_map/ppermute | solution.py:624
  3.3 0.1 shard_map.150
  3.4 3.0 %collective-permute-start.2 = (f32[6,32,128]{2,1,0:T(8,128)S(1)}, f32[6,32,128]{2,1,0:T(8,128)S(1)}, u32[]{:S(2)}, u32[]{:S(2)}) collective-permute-start(f32[6,32,128]{2,1,0:T(8,128)S(1)} %get-tuple-element.53), channel_id=1, source_target_pairs={{0,4},{1,5},{2,6},{3,7},{4,0},{5,1},{6,2},{7,3},{8,12},{9,13},{10,... | collective-permute-start | bytes 294920 | tf_op jit(solution)/shard_map/ppermute | solution.py:594
  6.4 1.5 %collective-permute-start.1 = (f32[17,8,128]{2,1,0:T(8,128)S(1)}, f32[17,8,128]{2,1,0:T(8,128)S(1)}, u32[]{:S(2)}, u32[]{:S(2)}) collective-permute-start(f32[17,8,128]{2,1,0:T(8,128)S(1)} %get-tuple-element.45), channel_id=1, source_target_pairs={{0,2},{1,3},{2,0},{3,1},{4,6},{5,7},{6,4},{7,5},{8,10},{9,11},{10,... | collective-permute-start | bytes 208904 | tf_op jit(solution)/shard_map/ppermute | solution.py:594
  7.9 3.1 %collective-permute-start.4 = (f32[4,8,128]{2,1,0:T(8,128)S(1)}, f32[4,8,128]{2,1,0:T(8,128)S(1)}, u32[]{:S(2)}, u32[]{:S(2)}) collective-permute-start(f32[4,8,128]{2,1,0:T(8,128)S(1)} %get-tuple-element.55), channel_id=1, source_target_pairs={{0,6},{1,7},{2,4},{3,5},{4,2},{5,3},{6,0},{7,1},{8,14},{9,15},{10,... | collective-permute-start | bytes 49160 | tf_op jit(solution)/shard_map/ppermute | solution.py:594
  11.1 1.5 %shard_map.149 = (s32[512,128]{1,0:T(8,128)S(1)}, s32[512,128]{1,0:T(8,128)S(1)}) custom-call(f32[2,8,128]{2,1,0:T(8,128)S(1)} %get-tuple-element.39.after_ref.stat_ref, s32[512,128]{1,0:T(8,128)S(1)} %bitcast.8, s32[160,128]{1,0:T(8,128)S(1)} %bitcast.13), custom_call_target="tpu_custom_call" | custom-call | flops 6000000 | bytes 6000000 | tf_op jit(solution)/shard_map/pallas_call | solution.py:626
  12.6 0.9 %shard_map.151 = (f32[16,48,128]{2,1,0:T(8,128)S(1)}, f32[16,48,128]{2,1,0:T(8,128)S(1)}, f32[16,48,128]{2,1,0:T(8,128)S(1)}, f32[16,48,128]{2,1,0:T(8,128)S(1)}...) custom-call(f32[16,32,128]{2,1,0:T(8,128)S(1)} %copy-done, ...), custom_call_target="tpu_custom_call" | custom-call | flops 6000000 | bytes 6000000 | tf_op jit(solution)/shard_map/pallas_call | solution.py:646
  13.5 0.7 %shard_map.152 = (f32[6,48,128]{2,1,0:T(8,128)S(1)}, f32[6,48,128]{2,1,0:T(8,128)S(1)}, f32[6,48,128]{2,1,0:T(8,128)S(1)}, f32[3,48,256]{2,1,0:T(8,128)S(1)}, f3...) custom-call(s32[512,128]{1,0:T(8,128)S(1)} %get-tuple-element.40.after_ref.plan_ref, f32[16,32,128]{2,1,0:T(8,128)S(1)} %copy-done, ...), custom_call_target="tpu_custom_call" | custom-call | flops 2000000 | bytes 2000000 | tf_op jit(solution)/shard_map/pallas_call | solution.py:653
  14.2 0.6 %collective-permute-start.6 = (f32[8,128]{1,0:T(8,128)S(1)}, f32[8,128]{1,0:T(8,128)S(1)}, u32[]{:S(2)}, u32[]{:S(2)}) collective-permute-start(f32[8,128]{1,0:T(8,128)S(1)} %get-tuple-element.57.after_ref.a_ref), channel_id=1, source_target_pairs={{0,1},{1,0},{2,3},{3,2},{4,5},{5,4},{6,7},{7,6},{8,9},{9,8},{10,11... | collective-permute-start | bytes 12296 | tf_op jit(solution)/shard_map/ppermute | solution.py:680
  14.8 0.7 %shard_map.153.after_ref.refs_0_ = f32[256,128]{1,0:T(8,128)S(1)} custom-call(f32[8,128]{1,0:T(8,128)S(1)} %get-tuple-element.57.after_ref.a_ref, f32[8,128]{1,0:T(8,128)S(1)} %get-tuple-element.58.where_ref, f32[16,48,128]{2,1,0:T(8,128)S(1)} %get-tuple-element.46.a_ref.inside_ref, f32[6,48,128]{2,1,0:T(8,128)S(1)} %get-tuple-element.59.edge_ref, ...), custom_call_target="tpu_custom_call" | custom-call | flops 6000000 | bytes 6000000 | tf_op jit(solution)/shard_map/pallas_call | solution.py:669
  15.6 1.5 %collective-permute-start.7 = (f32[8,128]{1,0:T(8,128)S(1)}, f32[8,128]{1,0:T(8,128)S(1)}, u32[]{:S(2)}, u32[]{:S(2)}) collective-permute-start(f32[8,128]{1,0:T(8,128)S(1)} %shard_map.154.after_ref.a_ref), channel_id=1, source_target_pairs={{0,2},{2,0},{1,3},{3,1},{4,6},{6,4},{5,7},{7,5},{8,10},{10,8},{9,1... | collective-permute-start | bytes 12296 | tf_op jit(solution)/shard_map/ppermute | solution.py:680
  17.1 0.8 %shard_map.155.after_ref.refs_1_ = f32[256,128]{1,0:T(8,128)S(1)} custom-call(f32[8,128]{1,0:T(8,128)S(1)} %shard_map.154.after_ref.a_ref, f32[8,128]{1,0:T(8,128)S(1)} %get-tuple-element.58.where_ref, f32[16,48,128]{2,1,0:T(8,128)S(1)} %get-tuple-element.48.b_ref.inside_ref, f32[6,48,128]{2,1,0:T(8,128)S(1)} %get-tuple-element.62.edge_ref.eb_ref, ...), custom_call_target="tpu_custom_call" | custom-call | flops 6000000 | bytes 6000000 | tf_op jit(solution)/shard_map/pallas_call | solution.py:669
  17.9 0.8 %shard_map.156.after_ref.refs_2_ = f32[256,128]{1,0:T(8,128)S(1)} custom-call(f32[256,128]{1,0:T(8,128)S(1)} %shard_map.155.after_ref.refs_1_, f32[8,128]{1,0:T(8,128)S(1)} %get-tuple-element.58.where_ref, f32[16,48,128]{2,1,0:T(8,128)S(1)} %get-tuple-element.49.c_ref.inside_ref, f32[6,48,128]{2,1,0:T(8,128)S(1)} %get-tuple-element.63.edge_ref.ec_ref, ...), custom_call_target="tpu_custom_call" | custom-call | flops 6000000 | bytes 6000000 | tf_op jit(solution)/shard_map/pallas_call | solution.py:669
  18.7 0.6 %collective-permute-done.7.b_ref = f32[8,128]{1,0:T(8,128)S(1)} collective-permute-done((f32[8,128]{1,0:T(8,128)S(1)}, f32[8,128]{1,0:T(8,128)S(1)}, u32[]{:S(2)}, u32[]{:S(2)}) %collective-permute-start.7) | collective-permute-done | bytes 4128 | tf_op jit(solution)/shard_map/ppermute | solution.py:680
  19.3 0.1 collective-permute-start.9
  19.4 3.6 %collective-permute-start.10 = (f32[200,128]{1,0:T(8,128)S(1)}, f32[200,128]{1,0:T(8,128)S(1)}, u32[]{:S(2)}, u32[]{:S(2)}) collective-permute-start(f32[200,128]{1,0:T(8,128)S(1)} %get-tuple-element.70), channel_id=1, source_target_pairs={{0,8},{1,9},{2,10},{3,11},{4,12},{5,13},{6,14},{7,15},{8,0},{9,1},... | collective-permute-start | bytes 307208 | tf_op jit(solution)/shard_map/ppermute | solution.py:594
  23.0 1.5 %collective-permute-start.8 = (f32[8,128]{1,0:T(8,128)S(1)}, f32[8,128]{1,0:T(8,128)S(1)}, u32[]{:S(2)}, u32[]{:S(2)}) collective-permute-start(f32[8,128]{1,0:T(8,128)S(1)} %shard_map.157.total_ref), channel_id=1, source_target_pairs={{0,12},{1,13},{2,14},{3,15},{4,5},{5,4},{6,7},{7,6},{8,9},{9,8},{1... | collective-permute-start | bytes 12296 | tf_op jit(solution)/shard_map/ppermute | solution.py:594
  24.5 0.6 %copy-done.7 = f32[20]{0:T(128)S(1)} copy-done((f32[20]{0:T(128)S(1)}, f32[20]{0:T(128)}, u32[]{:S(2)}) %copy-start.7) | copy-done | bytes 104
  25.2 1.9 %shard_map.159 = (f32[20,64,128]{2,1,0:T(8,128)S(1)}, f32[64,128]{1,0:T(8,128)S(1)}, f32[64,128]{1,0:T(8,128)S(1)}, f32[2,20,128]{2,1,0:T(8,128)S(1)}) custom-call(f32[20]{0:T(128)S(1)} %copy-done.7, f32[20]{0:T(128)S(1)} %copy-done.8, f32[20]{0:T(128)S(1)} %copy-done.9, f32[20]{0:T(128)S(1)} %copy-done.10, f32[20]{0:T(128)S(1)} %copy-done.11, ...), custom_call_target="tpu_custom_call" | custom-call | flops 6000000 | bytes 6000000 | tf_op jit(solution)/shard_map/pallas_call | solution.py:700
  27.1 1.4 %collective-permute-done.8.refs_1_ = f32[8,128]{1,0:T(8,128)S(1)} collective-permute-done((f32[8,128]{1,0:T(8,128)S(1)}, f32[8,128]{1,0:T(8,128)S(1)}, u32[]{:S(2)}, u32[]{:S(2)}) %collective-permute-start.8) | collective-permute-done | bytes 4128 | tf_op jit(solution)/shard_map/ppermute | solution.py:594
  28.5 0.7 %collective-permute-done.10.refs_3_ = f32[200,128]{1,0:T(8,128)S(1)} collective-permute-done((f32[200,128]{1,0:T(8,128)S(1)}, f32[200,128]{1,0:T(8,128)S(1)}, u32[]{:S(2)}, u32[]{:S(2)}) %collective-permute-start.10) | collective-permute-done | bytes 102432 | tf_op jit(solution)/shard_map/ppermute | solution.py:594
  29.3 1.3 %shard_map.160 = (f32[16,32,128]{2,1,0:T(8,128)}, f32[64,128]{1,0:T(8,128)}, f32[20,64,128]{2,1,0:T(8,128)}) custom-call(f32[2,20,128]{2,1,0:T(8,128)S(1)} %get-tuple-element.65.coef_ref, f32[64,128]{1,0:T(8,128)S(1)} %bitcast.14, f32[64,128]{1,0:T(8,128)S(1)} %bitcast.12, f32[64,128]{1,0:T(8,128)S(1)} %get-tuple-element.66.sum_ref, ...), custom_call_target="tpu_custom_call" | custom-call | flops 2000000 | bytes 2000000 | tf_op jit(solution)/shard_map/pallas_call | solution.py:713
  (37 shorter events, 0.2 us)
Async XLA Ops:
  2.0 1.4 %collective-permute-start = (f32[2,32,128]{2,1,0:T(8,128)S(1)}, f32[2,32,128]{2,1,0:T(8,128)S(1)}, u32[]{:S(2)}, u32[]{:S(2)}) collective-permute-start(f32[2,32,128]{2,1,0:T(8,128)S(1)} %get-tuple-element.43.own_ref), channel_id=1, source_target_pairs={{0,1},{1,0},{2,3},{3,2},{4,5},{5,4},{6,7},{7,6},{8,9},{9,8},{10,11... | collective-permute-start | bytes 98312 | tf_op jit(solution)/shard_map/ppermute | solution.py:624
  3.3 7.7 %copy-start.1 = (s32[16,32,128]{2,1,0:T(8,128)S(1)}, s32[16,32,128]{2,1,0:T(8,128)}, u32[]{:S(2)}) copy-start(s32[16,32,128]{2,1,0:T(8,128)} %label_ref.1) | copy-start | bytes 786436
  3.3 7.7 %copy-start.5 = (s32[1,1,1,20480]{3,2,1,0:T(1,128)S(1)}, s32[1,1,1,20480]{3,2,1,0:T(1,128)}, u32[]{:S(2)}) copy-start(s32[1,1,1,20480]{3,2,1,0:T(1,128)} %param.16) | copy-start | bytes 245764
  3.4 9.2 %copy-start = (f32[16,32,128]{2,1,0:T(8,128)S(1)}, f32[16,32,128]{2,1,0:T(8,128)}, u32[]{:S(2)}) copy-start(f32[16,32,128]{2,1,0:T(8,128)} %right_ref.5) | copy-start | bytes 786436
  3.4 10.1 %collective-permute-start.2 = (f32[6,32,128]{2,1,0:T(8,128)S(1)}, f32[6,32,128]{2,1,0:T(8,128)S(1)}, u32[]{:S(2)}, u32[]{:S(2)}) collective-permute-start(f32[6,32,128]{2,1,0:T(8,128)S(1)} %get-tuple-element.53), channel_id=1, source_target_pairs={{0,4},{1,5},{2,6},{3,7},{4,0},{5,1},{6,2},{7,3},{8,12},{9,13},{10,... | collective-permute-start | bytes 294920 | tf_op jit(solution)/shard_map/ppermute | solution.py:594
  6.4 7.1 %collective-permute-start.3 = (f32[6,32,128]{2,1,0:T(8,128)S(1)}, f32[6,32,128]{2,1,0:T(8,128)S(1)}, u32[]{:S(2)}, u32[]{:S(2)}) collective-permute-start(f32[6,32,128]{2,1,0:T(8,128)S(1)} %get-tuple-element.54), channel_id=1, source_target_pairs={{0,1},{1,0},{2,3},{3,2},{4,8},{5,9},{6,10},{7,11},{8,4},{9,5},{10,... | collective-permute-start | bytes 294920 | tf_op jit(solution)/shard_map/ppermute | solution.py:594
  6.4 6.1 %collective-permute-start.1 = (f32[17,8,128]{2,1,0:T(8,128)S(1)}, f32[17,8,128]{2,1,0:T(8,128)S(1)}, u32[]{:S(2)}, u32[]{:S(2)}) collective-permute-start(f32[17,8,128]{2,1,0:T(8,128)S(1)} %get-tuple-element.45), channel_id=1, source_target_pairs={{0,2},{1,3},{2,0},{3,1},{4,6},{5,7},{6,4},{7,5},{8,10},{9,11},{10,... | collective-permute-start | bytes 208904 | tf_op jit(solution)/shard_map/ppermute | solution.py:594
  7.9 5.6 %collective-permute-start.4 = (f32[4,8,128]{2,1,0:T(8,128)S(1)}, f32[4,8,128]{2,1,0:T(8,128)S(1)}, u32[]{:S(2)}, u32[]{:S(2)}) collective-permute-start(f32[4,8,128]{2,1,0:T(8,128)S(1)} %get-tuple-element.55), channel_id=1, source_target_pairs={{0,6},{1,7},{2,4},{3,5},{4,2},{5,3},{6,0},{7,1},{8,14},{9,15},{10,... | collective-permute-start | bytes 49160 | tf_op jit(solution)/shard_map/ppermute | solution.py:594
  11.0 2.5 %collective-permute-start.5 = (f32[4,8,128]{2,1,0:T(8,128)S(1)}, f32[4,8,128]{2,1,0:T(8,128)S(1)}, u32[]{:S(2)}, u32[]{:S(2)}) collective-permute-start(f32[4,8,128]{2,1,0:T(8,128)S(1)} %get-tuple-element.56), channel_id=1, source_target_pairs={{0,1},{1,0},{2,3},{3,2},{4,10},{5,11},{6,8},{7,9},{8,6},{9,7},{10,... | collective-permute-start | bytes 49160 | tf_op jit(solution)/shard_map/ppermute | solution.py:594
  14.2 1.4 %collective-permute-start.6 = (f32[8,128]{1,0:T(8,128)S(1)}, f32[8,128]{1,0:T(8,128)S(1)}, u32[]{:S(2)}, u32[]{:S(2)}) collective-permute-start(f32[8,128]{1,0:T(8,128)S(1)} %get-tuple-element.57.after_ref.a_ref), channel_id=1, source_target_pairs={{0,1},{1,0},{2,3},{3,2},{4,5},{5,4},{6,7},{7,6},{8,9},{9,8},{10,11... | collective-permute-start | bytes 12296 | tf_op jit(solution)/shard_map/ppermute | solution.py:680
  15.6 3.6 %collective-permute-start.7 = (f32[8,128]{1,0:T(8,128)S(1)}, f32[8,128]{1,0:T(8,128)S(1)}, u32[]{:S(2)}, u32[]{:S(2)}) collective-permute-start(f32[8,128]{1,0:T(8,128)S(1)} %shard_map.154.after_ref.a_ref), channel_id=1, source_target_pairs={{0,2},{2,0},{1,3},{3,1},{4,6},{6,4},{5,7},{7,5},{8,10},{10,8},{9,1... | collective-permute-start | bytes 12296 | tf_op jit(solution)/shard_map/ppermute | solution.py:680
  17.9 6.6 %copy-start.2 = (f32[20,1,8192]{2,1,0:T(1,128)S(1)}, f32[20,1,8192]{2,1,0:T(1,128)}, u32[]{:S(2)}) copy-start(f32[20,1,8192]{2,1,0:T(1,128)} %param.18) | copy-start | bytes 1966084
  17.9 6.6 %copy-start.3 = (f32[20,1,8192]{2,1,0:T(1,128)S(1)}, f32[20,1,8192]{2,1,0:T(1,128)}, u32[]{:S(2)}) copy-start(f32[20,1,8192]{2,1,0:T(1,128)} %param.20) | copy-start | bytes 1966084
  19.3 5.2 %copy-start.4 = (f32[1,8192]{1,0:T(1,128)S(1)}, f32[1,8192]{1,0:T(1,128)}, u32[]{:S(2)}) copy-start(f32[1,8192]{1,0:T(1,128)} %param.17) | copy-start | bytes 98308
  19.3 5.2 %copy-start.10 = (f32[20]{0:T(128)S(1)}, f32[20]{0:T(128)}, u32[]{:S(2)}) copy-start(f32[20]{0:T(128)} %cond_ref.1) | copy-start | bytes 244
  19.3 5.2 %copy-start.11 = (f32[20]{0:T(128)S(1)}, f32[20]{0:T(128)}, u32[]{:S(2)}) copy-start(f32[20]{0:T(128)} %rev_ref.1) | copy-start | bytes 244
  19.3 9.2 %collective-permute-start.9 = (f32[200,128]{1,0:T(8,128)S(1)}, f32[200,128]{1,0:T(8,128)S(1)}, u32[]{:S(2)}, u32[]{:S(2)}) collective-permute-start(f32[200,128]{1,0:T(8,128)S(1)} %get-tuple-element.69), channel_id=1, source_target_pairs={{0,1},{1,0},{2,3},{3,2},{4,8},{5,9},{6,10},{7,11},{8,4},{9,5},{10,... | collective-permute-start | bytes 307208 | tf_op jit(solution)/shard_map/ppermute | solution.py:594
  19.4 9.9 %collective-permute-start.10 = (f32[200,128]{1,0:T(8,128)S(1)}, f32[200,128]{1,0:T(8,128)S(1)}, u32[]{:S(2)}, u32[]{:S(2)}) collective-permute-start(f32[200,128]{1,0:T(8,128)S(1)} %get-tuple-element.70), channel_id=1, source_target_pairs={{0,8},{1,9},{2,10},{3,11},{4,12},{5,13},{6,14},{7,15},{8,0},{9,1},... | collective-permute-start | bytes 307208 | tf_op jit(solution)/shard_map/ppermute | solution.py:594
  23.0 6.3 %collective-permute-start.11 = (f32[200,128]{1,0:T(8,128)S(1)}, f32[200,128]{1,0:T(8,128)S(1)}, u32[]{:S(2)}, u32[]{:S(2)}) collective-permute-start(f32[200,128]{1,0:T(8,128)S(1)} %get-tuple-element.71), channel_id=1, source_target_pairs={{0,4},{1,5},{2,6},{3,7},{4,0},{5,1},{6,2},{7,3},{8,12},{9,13},{10,... | collective-permute-start | bytes 307208 | tf_op jit(solution)/shard_map/ppermute | solution.py:594
  23.0 5.5 %collective-permute-start.8 = (f32[8,128]{1,0:T(8,128)S(1)}, f32[8,128]{1,0:T(8,128)S(1)}, u32[]{:S(2)}, u32[]{:S(2)}) collective-permute-start(f32[8,128]{1,0:T(8,128)S(1)} %shard_map.157.total_ref), channel_id=1, source_target_pairs={{0,12},{1,13},{2,14},{3,15},{4,5},{5,4},{6,7},{7,6},{8,9},{9,8},{1... | collective-permute-start | bytes 12296 | tf_op jit(solution)/shard_map/ppermute | solution.py:594
  24.5 0.7 %copy-start.7 = (f32[20]{0:T(128)S(1)}, f32[20]{0:T(128)}, u32[]{:S(2)}) copy-start(f32[20]{0:T(128)} %half_ref.1) | copy-start | bytes 244
  24.5 0.7 %copy-start.8 = (f32[20]{0:T(128)S(1)}, f32[20]{0:T(128)}, u32[]{:S(2)}) copy-start(f32[20]{0:T(128)} %slope_ref.1) | copy-start | bytes 244
  24.5 0.7 %copy-start.9 = (f32[20]{0:T(128)S(1)}, f32[20]{0:T(128)}, u32[]{:S(2)}) copy-start(f32[20]{0:T(128)} %tau_ref.1) | copy-start | bytes 244
  25.2 4.1 %copy-start.6 = (f32[1,8192]{1,0:T(1,128)S(1)}, f32[1,8192]{1,0:T(1,128)}, u32[]{:S(2)}) copy-start(f32[1,8192]{1,0:T(1,128)} %param.19) | copy-start | bytes 98308
